TPU v7x, 32 devices: a whole 2x2x4 slice. The times are simulated.
32 devices in a mesh: group: 2 (over x), expert: 16 (over z, y, core).
Axes of the slice: x: 2, y: 2, z: 4, core: 2. Of those that a mesh axis runs over, the one named last changes fastest.
Arguments:
- hidden: bfloat16 [3, 512, 2048], P(None, ('group', 'expert')), parts along dimension 1, may hold values from -6 to 6
- route_ids: int32 [3, 512, 8], P(None, ('group', 'expert')), parts along dimension 1, may hold values from 0 to 15, all different within a row; in each aligned block of 16 rows (0 to 15, 16 to 31, ..., all dimensions but the last counted through in order) at most 16 rows name the same one
- route_logits: float32 [3, 512, 8], P(None, ('group', 'expert')), parts along dimension 1, may hold values from -4 to 368
- placement: int32 [16], replicated, may hold values from 0 to 15, each once
- factors: bfloat16 [16, 540672], P(None, 'expert'), may hold values from -0.375 to 0.375
- w_gate: bfloat16 [16, 2048, 768], P('expert'), may hold values from -0.125 to 0.125
- w_up: bfloat16 [16, 2048, 768], P('expert'), may hold values from -0.125 to 0.125
- down_weight: bfloat16 [16, 768, 2048], P('expert'), may hold values from -0.21875 to 0.21875
Outputs:
- decoded: bfloat16 [3, 512, 2048], P(None, ('group', 'expert')), parts along dimension 1
There are 2 independent parts, one for each index of `group`. A program takes and returns all parts, laid end to end along the dimension named above; an argument that names none is the same for every part. Nothing has to cross between parts.
Inputs may be any that keep to these rules, and one draw needn't show every extreme that they name: `route_ids`: in every decode step the 16 rows of one device name each expert at most 16 times, and in every draw some device names some expert exactly 16 times; the 8 ids of a row differ. `placement`: each expert stands in exactly one slot.
All inputs are finite; a program needn't handle non-finite values.
Results may differ from a plain program's by a relative error of at most 0.0083.
Values may be sent and summed in bfloat16 or wider, within the bound.
No kernel may reach another device: no remote copies, remote signals or barrier semaphores. Data moves between devices by JAX's collectives and lax.ppermute only.
A program may use at most 128 MiB of HBM per device.

v0:
```python
import jax
import jax.numpy as jnp
from jax import lax
from jax.sharding import PartitionSpec as P

adapter_scale = 2.0


def unpack_factors(flat_factors, width, hidden_units, rank_size):
    layouts = [
        (width, rank_size),
        (rank_size, hidden_units),
        (width, rank_size),
        (rank_size, hidden_units),
        (hidden_units, rank_size),
        (rank_size, width),
    ]
    offset = 0
    segments = []
    for leading, trailing in layouts:
        segments.append(
            flat_factors[offset : offset + leading * trailing].reshape(leading, trailing)
        )
        offset = offset + leading * trailing
    return segments


def merge_weight(loaded_weights, factor_a, factor_b):
    adapter_delta = jnp.dot(factor_a, factor_b, preferred_element_type=jnp.float32)
    return (loaded_weights.astype(jnp.float32) + adapter_scale * adapter_delta).astype(jnp.bfloat16)


def apply_expert_block(inputs, merged_gate, merged_up, combined_down_weight):
    gate_part = jnp.dot(inputs, merged_gate, preferred_element_type=jnp.float32)
    up_part = jnp.dot(inputs, merged_up, preferred_element_type=jnp.float32)
    inner = (jax.nn.silu(gate_part) * up_part).astype(jnp.bfloat16)
    return jnp.dot(inner, combined_down_weight, preferred_element_type=jnp.float32).astype(
        jnp.bfloat16
    )


def route_gates(logits):
    highest = jnp.max(logits, axis=-1, keepdims=True)
    router_scores = jnp.exp(logits - highest)
    return (router_scores / jnp.sum(router_scores, axis=-1, keepdims=True)).astype(jnp.bfloat16)


def shards(hidden, route_ids, route_logits, placement, factors, w_gate, w_up, down_weight):
    owners = lax.axis_size("expert")
    experts = placement.shape[0]
    steps_count, row_count, width = hidden.shape
    top_count = route_ids.shape[2]
    hidden_units = w_gate.shape[2]
    rank_size = factors.shape[1] * owners // (3 * (width + hidden_units))
    capacity = min(row_count, 3 * max(1, row_count * top_count // experts))
    slot_of = (
        jnp.zeros((experts,), jnp.int32).at[placement].set(jnp.arange(experts, dtype=jnp.int32))
    )
    ordered = jnp.take(factors, slot_of, axis=0)
    received = lax.all_to_all(ordered, "expert", split_axis=0, concat_axis=1, tiled=True)
    segments = unpack_factors(received[0], width, hidden_units, rank_size)
    merged_gate = merge_weight(w_gate[0], segments[0], segments[1])
    merged_up = merge_weight(w_up[0], segments[2], segments[3])
    combined_down_weight = merge_weight(down_weight[0], segments[4], segments[5])

    def layout(step_index):
        ids_flat = route_ids[step_index].reshape(-1)
        onehot = (ids_flat[:, None] == jnp.arange(experts, dtype=jnp.int32)[None, :]).astype(
            jnp.int32
        )
        position = jnp.sum((jnp.cumsum(onehot, axis=0) - 1) * onehot, axis=1)
        target = ids_flat * capacity + position
        placed = (
            jnp.arange(experts * capacity, dtype=jnp.int32)[:, None] == target[None, :]
        ).astype(jnp.bfloat16)
        pair_rows = jnp.repeat(hidden[step_index], top_count, axis=0)
        outgoing = jnp.dot(placed, pair_rows, preferred_element_type=jnp.float32).astype(
            jnp.bfloat16
        )
        outgoing = outgoing.reshape(experts, 1, capacity, width)
        gates = route_gates(route_logits[step_index]).reshape(-1)
        weighted = placed * gates[None, :]
        return (outgoing, weighted)

    layouts_all = [layout(step_index) for step_index in range(steps_count)]
    results = []
    for step_index in range(steps_count):
        outgoing, weighted = layouts_all[step_index]
        arrived = lax.all_to_all(outgoing, "expert", split_axis=0, concat_axis=1, tiled=True)
        outputs = apply_expert_block(
            arrived.reshape(-1, width), merged_gate, merged_up, combined_down_weight
        )
        outputs = outputs.reshape(arrived.shape)
        returned = lax.all_to_all(outputs, "expert", split_axis=1, concat_axis=0, tiled=True)
        flat_back = returned.reshape(experts * capacity, width)
        pair_out = jnp.einsum("cp,cd->pd", weighted, flat_back, preferred_element_type=jnp.float32)
        results.append(
            pair_out.reshape(row_count, top_count, width).sum(axis=1).astype(jnp.bfloat16)
        )
    return jnp.stack(results, axis=0)


def solution(mesh):
    placed = (
        P(None, ("group", "expert"), None),
        P(None, ("group", "expert"), None),
        P(None, ("group", "expert"), None),
        P(),
        P(None, "expert"),
        P("expert", None, None),
        P("expert", None, None),
        P("expert", None, None),
    )
    return jax.shard_map(
        shards,
        mesh=mesh,
        in_specs=placed,
        out_specs=P(None, ("group", "expert"), None),
        check_vma=False,
    )
```

profile of v0, /device:TPU:0, one launch (start us, length us, event | category | flops | bytes accessed | tf_op | source)
XLA Modules:
  0.0 216.5 jit_solution(17599078058128800140)
XLA Ops:
  2.4 1.5 convolution_convert_fusion
  3.8 7.4 %all-to-all-start.5 = ((bf16[16,1,16,2048]{3,2,1,0:T(8,128)(2,1)}), bf16[16,1,16,2048]{3,2,1,0:T(8,128)(2,1)}, u32[]{:S(2)}, u32[]{:S(2)}) async-start(bf16[16,1,16,2048]{3,2,1,0:T(8,128)(2,1)} %bitcast.36), calls=%async_computation.5 | async-start | bytes 2097152 | tf_op jit(solution)/shard_map/all_to_all | solution.py:89
  13.9 1.5 reduce.6
  15.4 1.6 reshape.382
  17.0 17.2 %all-to-all-done.5 = bf16[16,1,16,2048]{3,2,1,0:T(8,128)(2,1)} async-done(((bf16[16,1,16,2048]{3,2,1,0:T(8,128)(2,1)}), bf16[16,1,16,2048]{3,2,1,0:T(8,128)(2,1)}, u32[]{:S(2)}, u32[]{:S(2)}) %all-to-all-start.5) | async-done | bytes 1048608 | tf_op jit(solution)/shard_map/all_to_all | solution.py:89
  34.3 6.9 %all-to-all-start.1 = ((bf16[16,2,16896]{2,1,0:T(2,128)(2,1)}), bf16[16,2,16896]{2,1,0:T(2,128)(2,1)S(1)}, u32[]{:S(2)}, u32[]{:S(2)}) async-start(bf16[16,2,16896]{2,1,0:T(2,128)(2,1)} %reshape.382), calls=%async_computation.1 | async-start | bytes 2162688 | tf_op jit(solution)/shard_map/all_to_all | solution.py:60
  41.9 1.5 convolution_convert_fusion.1
  43.4 21.3 %all-to-all-done.1 = bf16[16,2,16896]{2,1,0:T(2,128)(2,1)S(1)} async-done(((bf16[16,2,16896]{2,1,0:T(2,128)(2,1)}), bf16[16,2,16896]{2,1,0:T(2,128)(2,1)S(1)}, u32[]{:S(2)}, u32[]{:S(2)}) %all-to-all-start.1) | async-done | bytes 1081376 | tf_op jit(solution)/shard_map/all_to_all | solution.py:60
  64.6 7.0 %all-to-all-start.3 = ((bf16[16,1,16,2048]{3,2,1,0:T(8,128)(2,1)}), bf16[16,1,16,2048]{3,2,1,0:T(8,128)(2,1)S(1)}, u32[]{:S(2)}, u32[]{:S(2)}) async-start(bf16[16,1,16,2048]{3,2,1,0:T(8,128)(2,1)} %bitcast.23), calls=%async_computation.3 | async-start | bytes 2097152 | tf_op jit(solution)/shard_map/all_to_all | solution.py:89
  72.1 1.4 convolution_convert_fusion.2
  73.5 3.3 %reshape.383 = bf16[16,1,33792]{2,1,0:T(2,128)(2,1)} reshape(bf16[16,2,16896]{2,1,0:T(2,128)(2,1)S(1)} %all-to-all-done.1) | data formatting | bytes 2162688
  76.8 7.6 %reduce.3 = bf16[16,33792]{1,0:T(8,128)(2,1)S(1)} reduce(bf16[16,1,33792]{2,1,0:T(2,128)(2,1)} %reshape.383, bf16[]{:T(256)} %constant.55), dimensions={1}, to_apply=%all_to_all.16.reduce_sub_computation | reduce | bytes 2162690 | tf_op jit(solution)/shard_map/all_to_all | solution.py:60
  84.4 2.4 %slice.56 = bf16[8448,64]{1,0:T(8,128)(2,1)} reshape(bf16[16,33792]{1,0:T(8,128)(2,1)S(1)} %reduce.3) | data formatting | bytes 2162688 | tf_op jit(solution)/shard_map/slice | solution.py:22
  87.1 7.5 %all-to-all-done.3 = bf16[16,1,16,2048]{3,2,1,0:T(8,128)(2,1)S(1)} async-done(((bf16[16,1,16,2048]{3,2,1,0:T(8,128)(2,1)}), bf16[16,1,16,2048]{3,2,1,0:T(8,128)(2,1)S(1)}, u32[]{:S(2)}, u32[]{:S(2)}) %all-to-all-start.3) | async-done | bytes 1048608 | tf_op jit(solution)/shard_map/all_to_all | solution.py:89
  94.6 6.9 %all-to-all-start = ((bf16[16,1,16,2048]{3,2,1,0:T(8,128)(2,1)}), bf16[16,1,16,2048]{3,2,1,0:T(8,128)(2,1)}, u32[]{:S(2)}, u32[]{:S(2)}) async-start(bf16[16,1,16,2048]{3,2,1,0:T(8,128)(2,1)} %bitcast.6), calls=%async_computation | async-start | bytes 2097152 | tf_op jit(solution)/shard_map/all_to_all | solution.py:89
  101.5 4.7 %fusion.2 = bf16[2048,768]{1,0:T(8,128)(2,1)} fusion(bf16[64,768]{1,0:T(8,128)(2,1)S(1)} %reshape.339, bf16[1,2048,768]{2,1,0:T(8,128)(2,1)} %param.13, bf16[8448,64]{1,0:T(8,128)(2,1)} %slice.56), kind=kOutput, calls=%fused_computation.7 | convolution fusion | flops 207618048 | bytes 6914048 | tf_op jit(solution)/shard_map/dot_general | solution.py:29
  106.2 1.6 slice.62
  108.0 3.3 %fusion.61 = f32[256,768]{1,0:T(8,128)S(1)} fusion(bf16[256,2048]{1,0:T(8,128)(2,1)} %bitcast.37, bf16[2048,768]{1,0:T(8,128)(2,1)} %fusion.2), kind=kOutput, calls=%fused_computation.114 | convolution fusion | flops 805306368 | bytes 4980736 | tf_op jit(solution)/shard_map/dot_general | solution.py:34
  111.4 3.7 %fusion = bf16[768,2048]{1,0:T(8,128)(2,1)} fusion(bf16[1,768,2048]{2,1,0:T(8,128)(2,1)S(1)} %copy-done.1, bf16[264,2048]{1,0:T(8,128)(2,1)S(1)} %slice.62, bf16[8448,64]{1,0:T(8,128)(2,1)} %slice.56), kind=kOutput, calls=%fused_computation.3 | convolution fusion | flops 207618048 | bytes 6750208 | tf_op jit(solution)/shard_map/dot_general | solution.py:29
  115.1 3.7 %fusion.1 = bf16[2048,768]{1,0:T(8,128)(2,1)} fusion(bf16[64,768]{1,0:T(8,128)(2,1)S(1)} %reshape.340, bf16[1,2048,768]{2,1,0:T(8,128)(2,1)S(1)} %copy-done.2, bf16[8448,64]{1,0:T(8,128)(2,1)} %slice.56), kind=kOutput, calls=%fused_computation.5 | convolution fusion | flops 207618048 | bytes 6914048 | tf_op jit(solution)/shard_map/dot_general | solution.py:29
  118.8 6.3 %convolution_convert_fusion.3 = bf16[256,2048]{1,0:T(8,128)(2,1)} fusion(bf16[768,2048]{1,0:T(8,128)(2,1)} %fusion, bf16[256,2048]{1,0:T(8,128)(2,1)} %bitcast.37, bf16[2048,768]{1,0:T(8,128)(2,1)} %fusion.1, f32[256,768]{1,0:T(8,128)S(1)} %fusion.61), kind=kOutput, calls=%fused_computation.11 | convolution fusion | flops 1612316672 | bytes 9175040 | tf_op jit(solution)/shard_map/dot_general | solution.py:37
  125.1 6.2 %all-to-all-start.6 = ((bf16[1,16,16,2048]{3,2,0,1:T(8,128)(2,1)}), bf16[1,16,16,2048]{3,2,0,1:T(8,128)(2,1)S(1)}, u32[]{:S(2)}, u32[]{:S(2)}) async-start(bf16[1,16,16,2048]{3,2,0,1:T(8,128)(2,1)} %bitcast.134), calls=%async_computation.6 | async-start | bytes 2097152 | tf_op jit(solution)/shard_map/all_to_all | solution.py:94
  131.4 3.7 %fusion.60 = f32[256,768]{1,0:T(8,128)} fusion(bf16[256,2048]{1,0:T(8,128)(2,1)S(1)} %bitcast.131, bf16[2048,768]{1,0:T(8,128)(2,1)} %fusion.2), kind=kOutput, calls=%fused_computation.113 | convolution fusion | flops 805306368 | bytes 4980736 | tf_op jit(solution)/shard_map/dot_general | solution.py:34
  135.1 6.2 %convolution_convert_fusion.4 = bf16[256,2048]{1,0:T(8,128)(2,1)} fusion(bf16[768,2048]{1,0:T(8,128)(2,1)} %fusion, bf16[256,2048]{1,0:T(8,128)(2,1)S(1)} %bitcast.132, bf16[2048,768]{1,0:T(8,128)(2,1)} %fusion.1, f32[256,768]{1,0:T(8,128)} %fusion.60), kind=kOutput, calls=%fused_computation.12 | convolution fusion | flops 1612316672 | bytes 9175040 | tf_op jit(solution)/shard_map/dot_general | solution.py:37
  141.3 13.0 %all-to-all-done.6 = bf16[1,16,16,2048]{3,2,0,1:T(8,128)(2,1)S(1)} async-done(((bf16[1,16,16,2048]{3,2,0,1:T(8,128)(2,1)}), bf16[1,16,16,2048]{3,2,0,1:T(8,128)(2,1)S(1)}, u32[]{:S(2)}, u32[]{:S(2)}) %all-to-all-start.6) | async-done | bytes 1048608 | tf_op jit(solution)/shard_map/all_to_all | solution.py:94
  154.3 6.9 %all-to-all-start.4 = ((bf16[1,16,16,2048]{3,2,0,1:T(8,128)(2,1)}), bf16[1,16,16,2048]{3,2,0,1:T(8,128)(2,1)S(1)}, u32[]{:S(2)}, u32[]{:S(2)}) async-start(bf16[1,16,16,2048]{3,2,0,1:T(8,128)(2,1)} %bitcast.133), calls=%async_computation.4 | async-start | bytes 2097152 | tf_op jit(solution)/shard_map/all_to_all | solution.py:94
  161.2 4.1 %fusion.59 = f32[256,768]{1,0:T(8,128)} fusion(bf16[256,2048]{1,0:T(8,128)(2,1)} %bitcast.7, bf16[2048,768]{1,0:T(8,128)(2,1)} %fusion.2), kind=kOutput, calls=%fused_computation.112 | convolution fusion | flops 805306368 | bytes 4980736 | tf_op jit(solution)/shard_map/dot_general | solution.py:34
  165.3 6.5 %convolution_convert_fusion.5 = bf16[256,2048]{1,0:T(8,128)(2,1)} fusion(bf16[768,2048]{1,0:T(8,128)(2,1)} %fusion, bf16[256,2048]{1,0:T(8,128)(2,1)} %bitcast.7, bf16[2048,768]{1,0:T(8,128)(2,1)} %fusion.1, f32[256,768]{1,0:T(8,128)} %fusion.59), kind=kOutput, calls=%fused_computation.13 | convolution fusion | flops 1612316672 | bytes 9175040 | tf_op jit(solution)/shard_map/dot_general | solution.py:37
  171.8 12.3 %all-to-all-done.4 = bf16[1,16,16,2048]{3,2,0,1:T(8,128)(2,1)S(1)} async-done(((bf16[1,16,16,2048]{3,2,0,1:T(8,128)(2,1)}), bf16[1,16,16,2048]{3,2,0,1:T(8,128)(2,1)S(1)}, u32[]{:S(2)}, u32[]{:S(2)}) %all-to-all-start.4) | async-done | bytes 1048608 | tf_op jit(solution)/shard_map/all_to_all | solution.py:94
  184.1 6.9 %all-to-all-start.2 = ((bf16[1,16,16,2048]{3,2,0,1:T(8,128)(2,1)}), bf16[1,16,16,2048]{3,2,0,1:T(8,128)(2,1)}, u32[]{:S(2)}, u32[]{:S(2)}) async-start(bf16[1,16,16,2048]{3,2,0,1:T(8,128)(2,1)} %bitcast.130), calls=%async_computation.2 | async-start | bytes 2097152 | tf_op jit(solution)/shard_map/all_to_all | solution.py:94
  193.1 21.0 %all-to-all-done.2 = bf16[1,16,16,2048]{3,2,0,1:T(8,128)(2,1)} async-done(((bf16[1,16,16,2048]{3,2,0,1:T(8,128)(2,1)}), bf16[1,16,16,2048]{3,2,0,1:T(8,128)(2,1)}, u32[]{:S(2)}, u32[]{:S(2)}) %all-to-all-start.2) | async-done | bytes 1048608 | tf_op jit(solution)/shard_map/all_to_all | solution.py:94
  214.1 1.7 convolution_reduce_fusion.2
  (69 shorter events, 9.2 us)
Async XLA Ops:
  0.0 12.0 %copy-start = (bf16[16,33792]{1,0:T(8,128)(2,1)S(1)}, bf16[16,33792]{1,0:T(8,128)(2,1)}, u32[]{:S(2)}) copy-start(bf16[16,33792]{1,0:T(8,128)(2,1)} %param.12) | copy-start | bytes 3244036
  0.0 11.3 %copy-start.7 = (s32[16]{0:T(128)S(1)}, s32[16]{0:T(128)}, u32[]{:S(2)}) copy-start(s32[16]{0:T(128)} %param.11) | copy-start | bytes 196
  3.8 30.4 %all-to-all-start.5 = ((bf16[16,1,16,2048]{3,2,1,0:T(8,128)(2,1)}), bf16[16,1,16,2048]{3,2,1,0:T(8,128)(2,1)}, u32[]{:S(2)}, u32[]{:S(2)}) async-start(bf16[16,1,16,2048]{3,2,1,0:T(8,128)(2,1)} %bitcast.36), calls=%async_computation.5 | async-start | bytes 2097152 | tf_op jit(solution)/shard_map/all_to_all | solution.py:89
  34.3 30.4 %all-to-all-start.1 = ((bf16[16,2,16896]{2,1,0:T(2,128)(2,1)}), bf16[16,2,16896]{2,1,0:T(2,128)(2,1)S(1)}, u32[]{:S(2)}, u32[]{:S(2)}) async-start(bf16[16,2,16896]{2,1,0:T(2,128)(2,1)} %reshape.382), calls=%async_computation.1 | async-start | bytes 2162688 | tf_op jit(solution)/shard_map/all_to_all | solution.py:60
  64.6 30.0 %all-to-all-start.3 = ((bf16[16,1,16,2048]{3,2,1,0:T(8,128)(2,1)}), bf16[16,1,16,2048]{3,2,1,0:T(8,128)(2,1)S(1)}, u32[]{:S(2)}, u32[]{:S(2)}) async-start(bf16[16,1,16,2048]{3,2,1,0:T(8,128)(2,1)} %bitcast.23), calls=%async_computation.3 | async-start | bytes 2097152 | tf_op jit(solution)/shard_map/all_to_all | solution.py:89
  94.6 6.9 %copy-start.3 = (bf16[16,1,16,2048]{3,2,1,0:T(8,128)(2,1)}, bf16[16,1,16,2048]{3,2,1,0:T(8,128)(2,1)S(1)}, u32[]{:S(2)}) copy-start(bf16[16,1,16,2048]{3,2,1,0:T(8,128)(2,1)S(1)} %all-to-all-done.3) | copy-start | bytes 3145732
  94.6 30.5 %all-to-all-start = ((bf16[16,1,16,2048]{3,2,1,0:T(8,128)(2,1)}), bf16[16,1,16,2048]{3,2,1,0:T(8,128)(2,1)}, u32[]{:S(2)}, u32[]{:S(2)}) async-start(bf16[16,1,16,2048]{3,2,1,0:T(8,128)(2,1)} %bitcast.6), calls=%async_computation | async-start | bytes 2097152 | tf_op jit(solution)/shard_map/all_to_all | solution.py:89
  108.0 3.4 %copy-start.1 = (bf16[1,768,2048]{2,1,0:T(8,128)(2,1)S(1)}, bf16[1,768,2048]{2,1,0:T(8,128)(2,1)}, u32[]{:S(2)}) copy-start(bf16[1,768,2048]{2,1,0:T(8,128)(2,1)} %param.15) | copy-start | bytes 9437188
  111.4 3.7 %copy-start.2 = (bf16[1,2048,768]{2,1,0:T(8,128)(2,1)S(1)}, bf16[1,2048,768]{2,1,0:T(8,128)(2,1)}, u32[]{:S(2)}) copy-start(bf16[1,2048,768]{2,1,0:T(8,128)(2,1)} %param.14) | copy-start | bytes 9437188
  118.8 12.6 %copy-start.4 = (bf16[16,1,16,2048]{3,2,1,0:T(8,128)(2,1)S(1)}, bf16[16,1,16,2048]{3,2,1,0:T(8,128)(2,1)}, u32[]{:S(2)}) copy-start(bf16[16,1,16,2048]{3,2,1,0:T(8,128)(2,1)} %copy-done.3) | copy-start | bytes 3145732
  125.1 29.2 %all-to-all-start.6 = ((bf16[1,16,16,2048]{3,2,0,1:T(8,128)(2,1)}), bf16[1,16,16,2048]{3,2,0,1:T(8,128)(2,1)S(1)}, u32[]{:S(2)}, u32[]{:S(2)}) async-start(bf16[1,16,16,2048]{3,2,0,1:T(8,128)(2,1)} %bitcast.134), calls=%async_computation.6 | async-start | bytes 2097152 | tf_op jit(solution)/shard_map/all_to_all | solution.py:94
  154.3 29.8 %all-to-all-start.4 = ((bf16[1,16,16,2048]{3,2,0,1:T(8,128)(2,1)}), bf16[1,16,16,2048]{3,2,0,1:T(8,128)(2,1)S(1)}, u32[]{:S(2)}, u32[]{:S(2)}) async-start(bf16[1,16,16,2048]{3,2,0,1:T(8,128)(2,1)} %bitcast.133), calls=%async_computation.4 | async-start | bytes 2097152 | tf_op jit(solution)/shard_map/all_to_all | solution.py:94
  165.3 26.3 %copy-start.6 = (s32[3,16,8]{1,2,0:T(8,128)S(1)}, s32[3,16,8]{1,2,0:T(8,128)}, u32[]{:S(2)}) copy-start(s32[3,16,8]{1,2,0:T(8,128)} %param.9) | copy-start | bytes 4612
  165.3 26.3 %copy-start.5 = (f32[3,16,8]{1,2,0:T(8,128)S(1)}, f32[3,16,8]{1,2,0:T(8,128)}, u32[]{:S(2)}) copy-start(f32[3,16,8]{1,2,0:T(8,128)} %param.10) | copy-start | bytes 4612
  184.1 29.9 %all-to-all-start.2 = ((bf16[1,16,16,2048]{3,2,0,1:T(8,128)(2,1)}), bf16[1,16,16,2048]{3,2,0,1:T(8,128)(2,1)}, u32[]{:S(2)}, u32[]{:S(2)}) async-start(bf16[1,16,16,2048]{3,2,0,1:T(8,128)(2,1)} %bitcast.130), calls=%async_computation.2 | async-start | bytes 2097152 | tf_op jit(solution)/shard_map/all_to_all | solution.py:94
where the time goes:
time: 219 us; the launch traced here: 216 us
  waiting for transfers between devices  92.3 us (42%)
  matrix products  49.3 us (23%)
  starting transfers between devices  48.3 us (22%)
  local copies, waits for them, and re-layouts  15 us (7%)
  other arithmetic  11.3 us (5%)
    all_to_all x3, waiting for transfers between devices, shards(): lax.all_to_all(outputs, 'expert', split_axis=1, concat_axis=0, tiled=True)  46.3 us
    all_to_all x3, waiting for transfers between devices, shards(): lax.all_to_all(outgoing, 'expert', split_axis=0, concat_axis=1, tiled=True)  24.7 us
    all_to_all x3, starting transfers between devices, shards(): lax.all_to_all(outgoing, 'expert', split_axis=0, concat_axis=1, tiled=True)  21.4 us
    all_to_all x1, waiting for transfers between devices, shards(): lax.all_to_all(ordered, 'expert', split_axis=0, concat_axis=1, tiled=True)  21.3 us
    all_to_all x3, starting transfers between devices, shards(): lax.all_to_all(outputs, 'expert', split_axis=1, concat_axis=0, tiled=True)  20 us
    dot_general x3, matrix products, apply_expert_block(): jnp.dot(inner, combined_down_weight, preferred_element_type=jnp.float32)  19.1 us
    dot_general x3, matrix products, merge_weight(): jnp.dot(factor_a, factor_b, preferred_element_type=jnp.float32)  12.1 us
    dot_general x3, matrix products, apply_expert_block(): gate_part = jnp.dot(inputs, merged_gate, preferred_element_type=jnp.float32)  11.1 us
  transfers between devices with their start and end apart: 7, of which 6 were waited for; matrix products, arithmetic and copies ran while one was open for 32% of the time, Pallas kernels for 0%

commit v1 on v0

v1 whole, which is shorter than its diff:
```python
import jax
import jax.numpy as jnp
from jax import lax
from jax.sharding import PartitionSpec as P

adapter_scale = 2.0
LANES = 128


def route_gates(logits):
    highest = jnp.max(logits, axis=-1, keepdims=True)
    router_scores = jnp.exp(logits - highest)
    return (router_scores / jnp.sum(router_scores, axis=-1, keepdims=True)).astype(jnp.bfloat16)


def dot(a, b):
    return jnp.dot(a, b, preferred_element_type=jnp.float32)


def shards(hidden, route_ids, route_logits, placement, factors, w_gate, w_up, down_weight):
    owners = lax.axis_size("expert")
    experts = placement.shape[0]
    steps, rows, width = hidden.shape
    units = w_gate.shape[2]
    rank = factors.shape[1] * owners // (3 * (width + units))
    total = rows * owners

    gates = route_gates(route_logits)
    chosen = route_ids[..., None] == jnp.arange(experts, dtype=jnp.int32)
    dense = jnp.sum(jnp.where(chosen, gates[..., None], 0), axis=2, dtype=jnp.float32)
    dense = dense.astype(jnp.bfloat16)
    padded = -(-experts // LANES) * LANES
    dense = jnp.pad(dense, ((0, 0), (0, 0), (0, padded - experts)))
    payload = jnp.concatenate([hidden, dense], axis=-1)
    gathered = lax.all_gather(payload, "expert", axis=1, tiled=True)

    slot_of = (
        jnp.zeros((experts,), jnp.int32).at[placement].set(jnp.arange(experts, dtype=jnp.int32))
    )
    ordered = jnp.take(factors, slot_of, axis=0).reshape(experts, -1, LANES)
    received = lax.all_to_all(ordered, "expert", split_axis=0, concat_axis=0, tiled=True)
    flat = received.reshape(-1, LANES)
    shapes = [(width, rank), (rank, units)] * 2 + [(units, rank), (rank, width)]
    segments, at = [], 0
    for lead, trail in shapes:
        n = lead * trail // LANES
        segments.append(flat[at : at + n].reshape(lead, trail))
        at += n
    gate_a, gate_b, up_a, up_b, down_a, down_b = segments

    x = gathered[..., :width].reshape(steps * total, width)
    me = lax.axis_index("expert")
    mine = lax.dynamic_index_in_dim(gathered[..., width:], me, 2, keepdims=True)
    gate_part = dot(x, w_gate[0])
    up_part = dot(x, w_up[0])

    results = []
    for s in range(steps):
        cut = slice(s * total, (s + 1) * total)
        low_g = (adapter_scale * dot(x[cut], gate_a)).astype(jnp.bfloat16)
        low_u = (adapter_scale * dot(x[cut], up_a)).astype(jnp.bfloat16)
        g = gate_part[cut] + dot(low_g, gate_b)
        u = up_part[cut] + dot(low_u, up_b)
        inner = (jax.nn.silu(g) * u).astype(jnp.bfloat16)
        low_d = (adapter_scale * dot(inner, down_a)).astype(jnp.bfloat16)
        out = dot(inner, down_weight[0]) + dot(low_d, down_b)
        weighted = (out * mine[s].astype(jnp.float32)).astype(jnp.bfloat16)
        results.append(lax.psum_scatter(weighted, "expert", scatter_dimension=0, tiled=True))
    return jnp.stack(results, axis=0)


def solution(mesh):
    placed = (
        P(None, ("group", "expert"), None),
        P(None, ("group", "expert"), None),
        P(None, ("group", "expert"), None),
        P(),
        P(None, "expert"),
        P("expert", None, None),
        P("expert", None, None),
        P("expert", None, None),
    )
    return jax.shard_map(
        shards,
        mesh=mesh,
        in_specs=placed,
        out_specs=P(None, ("group", "expert"), None),
        check_vma=False,
    )
```

time: 219 us -> 292 us (1.33)
  waiting for transfers between devices: 92.3 us -> 191 us
  starting transfers between devices: 48.3 us -> 7.74 us
  between operations: 0.34 us -> 13.3 us
  local copies, waits for them, and re-layouts: 15 us -> 21.6 us
  other arithmetic: 11.3 us -> 6.42 us
    reduce_scatter x0 -> x3, waiting for transfers between devices: none -> 158 us  [shards(): lax.psum_scatter(weighted, 'expert', scatter_dimension=0, tiled=True)]
    all_to_all x7 -> x1, waiting for transfers between devices: 92.3 us -> 32.5 us  [shards(): lax.all_to_all(ordered, 'expert', split_axis=0, concat_axis=0, tiled=True)]
    all_to_all x7 -> x1, starting transfers between devices: 48.3 us -> 7.43 us  [shards(): lax.all_to_all(ordered, 'expert', split_axis=0, concat_axis=0, tiled=True)]
    all_to_all x1 -> x0, other arithmetic: 7.59 us -> none  [shards(): lax.all_to_all(ordered, 'expert', split_axis=0, concat_axis=1, tiled=True)]
    reshape x2 -> x6, local copies, waits for them, and re-layouts: 0.21 us -> 7.63 us  [shards(): segments.append(flat[at:at + n].reshape(lead, trail))]
    gather x1, local copies, waits for them, and re-layouts: 1.26 us -> 4.53 us  [shards(): ordered = jnp.take(factors, slot_of, axis=0).reshape(experts, -1, LANES)]
    dot_general x15 -> x14, matrix products: 49.3 us -> 50.6 us  [dot(): return jnp.dot(a, b, preferred_element_type=jnp.float32)]
    slice x7 -> x5, local copies, waits for them, and re-layouts: 4.98 us -> 6.17 us  [the longest x2 3.72 us: shards(): segments.append(flat[at:at + n].reshape(lead, trail))]
  transfers between devices with their start and end apart: 7 -> 5, of which waited for: 6 -> 5; matrix products, arithmetic and copies ran while one was open for 32% -> 17% of each run, Pallas kernels for 0% -> 0%
where the time goes in v1:
time: 292 us; the launch traced here: 291 us
  waiting for transfers between devices  191 us (65%)
  matrix products  50.6 us (17%)
  local copies, waits for them, and re-layouts  21.6 us (7%)
  between operations  13.3 us (5%)
  starting transfers between devices  7.74 us (3%)
  other arithmetic  6.42 us (2%)
    reduce_scatter x3, waiting for transfers between devices, shards(): lax.psum_scatter(weighted, 'expert', scatter_dimension=0, tiled=True)  158 us
    dot_general x14, matrix products, dot(): return jnp.dot(a, b, preferred_element_type=jnp.float32)  50.6 us
    all_to_all x1, waiting for transfers between devices, shards(): lax.all_to_all(ordered, 'expert', split_axis=0, concat_axis=0, tiled=True)  32.5 us
    reshape x6, local copies, waits for them, and re-layouts, shards(): segments.append(flat[at:at + n].reshape(lead, trail))  7.63 us
    all_to_all x1, starting transfers between devices, shards(): lax.all_to_all(ordered, 'expert', split_axis=0, concat_axis=0, tiled=True)  7.43 us
  transfers between devices with their start and end apart: 5, of which 5 were waited for; matrix products, arithmetic and copies ran while one was open for 17% of the time, Pallas kernels for 0%

profile of v1, /device:TPU:0, one launch (start us, length us, event | category | flops | bytes accessed | tf_op | source)
XLA Modules:
  0.0 291.0 jit_solution(6894144483432343302)
XLA Ops:
  6.5 0.9 fusion.84
  8.5 1.6 fusion.59
  11.5 4.5 %gather_fusion = bf16[16,33792]{1,0:T(8,128)(2,1)} fusion(bf16[16,33792]{1,0:T(8,128)(2,1)} %param.12, s32[1024]{0:T(1024)S(1)} %pad_clamp_fusion), kind=kCustom, calls=%fused_computation | custom fusion | bytes 2162752 | tf_op jit(solution)/shard_map/jit(_take)/gather | solution.py:40
  16.0 1.4 copy.15
  17.4 1.2 bitcast_select_fusion
  18.6 7.4 %all-to-all-start = ((bf16[16,264,128]{2,1,0:T(8,128)(2,1)}), bf16[16,264,128]{2,1,0:T(8,128)(2,1)}, u32[]{:S(2)}, u32[]{:S(2)}) async-start(bf16[16,264,128]{2,1,0:T(8,128)(2,1)} %bitcast_select_fusion), calls=%async_computation | async-start | bytes 2162688 | tf_op jit(solution)/shard_map/all_to_all | solution.py:41
  26.1 32.5 %all-to-all-done = bf16[16,264,128]{2,1,0:T(8,128)(2,1)} async-done(((bf16[16,264,128]{2,1,0:T(8,128)(2,1)}), bf16[16,264,128]{2,1,0:T(8,128)(2,1)}, u32[]{:S(2)}, u32[]{:S(2)}) %all-to-all-start) | async-done | bytes 1081376 | tf_op jit(solution)/shard_map/all_to_all | solution.py:41
  58.6 1.6 fusion.82
  60.2 1.0 reshape.76
  62.1 2.1 fusion.83
  64.2 2.0 reshape.72
  66.2 1.8 reshape.77
  68.0 2.0 reshape.74
  70.7 2.4 slice.100
  73.6 4.1 %fusion.7 = f32[768,768]{1,0:T(8,128)} fusion(bf16[768,2048]{1,0:T(8,128)(2,1)S(1)} %bitcast.86, bf16[1,2048,768]{2,1,0:T(8,128)(2,1)S(1)} %copy-done.6), kind=kOutput, calls=%fused_computation.9 | convolution fusion | flops 2415919104 | bytes 8650752 | tf_op jit(solution)/shard_map/dot_general | solution.py:17
  77.6 4.1 %fusion.9 = f32[768,768]{1,0:T(8,128)} fusion(bf16[768,2048]{1,0:T(8,128)(2,1)S(1)} %bitcast.87, bf16[1,2048,768]{2,1,0:T(8,128)(2,1)S(1)} %copy-done.7), kind=kOutput, calls=%fused_computation.11 | convolution fusion | flops 2415919104 | bytes 8650752 | tf_op jit(solution)/shard_map/dot_general | solution.py:17
  81.7 3.5 %convolution_add_fusion.3 = f32[256,768]{1,0:T(8,128)} fusion(bf16[64,768]{1,0:T(8,128)(2,1)S(1)} %reshape.73, bf16[2048,64]{1,0:T(8,128)(2,1)} %reshape.72, bf16[3,256,2176]{2,1,0:T(8,128)(2,1)} %all-gather.2.cloned.1.call-done, f32[768,768]{1,0:T(8,128)} %fusion.9), kind=kOutput, calls=%fused_computation.27 | convolution fusion | flops 92504064 | bytes 3244032 | tf_op jit(solution)/shard_map/dot_general | solution.py:17
  85.2 3.5 %fusion.42 = bf16[256,768]{1,0:T(8,128)(2,1)} fusion(bf16[64,768]{1,0:T(8,128)(2,1)S(1)} %copy-done.5, bf16[2048,64]{1,0:T(8,128)(2,1)} %reshape.74, bf16[3,256,2176]{2,1,0:T(8,128)(2,1)} %all-gather.2.cloned.1.call-done, f32[768,768]{1,0:T(8,128)} %fusion.7, f32[256,768]{1,0:T(8,128)} %convolution_add_fusion.3), kind=kOutput, calls=%fused_computation.32 | convolution fusion | flops 93683712 | bytes 3637248 | tf_op jit(solution)/shard_map/dot_general | solution.py:17
  88.8 3.4 %fusion.54 = f32[256,2048]{1,0:T(8,128)} fusion(bf16[64,2048]{1,0:T(8,128)(2,1)} %reshape.77, bf16[256,768]{1,0:T(8,128)(2,1)} %fusion.42, bf16[768,64]{1,0:T(8,128)(2,1)S(1)} %reshape.76), kind=kOutput, calls=%fused_computation.53 | convolution fusion | flops 92307456 | bytes 2850816 | tf_op jit(solution)/shard_map/dot_general | solution.py:17
  92.4 3.7 %fusion.32 = bf16[256,2048]{1,0:T(8,128)(2,1)} fusion(f32[256,2048]{1,0:T(8,128)} %fusion.54, bf16[256,768]{1,0:T(8,128)(2,1)} %fusion.42, bf16[1,768,2048]{2,1,0:T(8,128)(2,1)S(1)} %copy-done, f32[256]{0:T(256)S(1)} %get-tuple-element.6), kind=kOutput, calls=%fused_computation.20 | convolution fusion | flops 806879232 | bytes 6685696 | tf_op jit(solution)/shard_map/dot_general | solution.py:17
  96.4 3.5 %convolution_add_fusion.5 = f32[256,768]{1,0:T(8,128)} fusion(bf16[64,768]{1,0:T(8,128)(2,1)S(1)} %copy-done.4, bf16[2048,64]{1,0:T(8,128)(2,1)} %reshape.72, bf16[3,256,2176]{2,1,0:T(8,128)(2,1)} %all-gather.2.cloned.1.call-done, f32[768,768]{1,0:T(8,128)} %fusion.9), kind=kOutput, calls=%fused_computation.30 | convolution fusion | flops 92504064 | bytes 3244032 | tf_op jit(solution)/shard_map/dot_general | solution.py:17
  99.9 3.6 %fusion.41 = bf16[256,768]{1,0:T(8,128)(2,1)} fusion(bf16[64,768]{1,0:T(8,128)(2,1)} %reshape.75, bf16[2048,64]{1,0:T(8,128)(2,1)} %reshape.74, bf16[3,256,2176]{2,1,0:T(8,128)(2,1)} %all-gather.2.cloned.1.call-done, f32[768,768]{1,0:T(8,128)} %fusion.7, f32[256,768]{1,0:T(8,128)} %convolution_add_fusion.5), kind=kOutput, calls=%fused_computation.31 | convolution fusion | flops 93683712 | bytes 3637248 | tf_op jit(solution)/shard_map/dot_general | solution.py:17
  103.5 3.3 %fusion.55 = f32[256,2048]{1,0:T(8,128)} fusion(bf16[64,2048]{1,0:T(8,128)(2,1)S(1)} %copy-done.1, bf16[256,768]{1,0:T(8,128)(2,1)} %fusion.41, bf16[768,64]{1,0:T(8,128)(2,1)} %copy-done.2), kind=kOutput, calls=%fused_computation.54 | convolution fusion | flops 92307456 | bytes 2850816 | tf_op jit(solution)/shard_map/dot_general | solution.py:17
  106.8 3.7 %fusion.35 = bf16[256,2048]{1,0:T(8,128)(2,1)} fusion(f32[256,2048]{1,0:T(8,128)} %fusion.55, bf16[256,768]{1,0:T(8,128)(2,1)} %fusion.41, bf16[1,768,2048]{2,1,0:T(8,128)(2,1)S(1)} %copy-done, f32[256]{0:T(256)S(1)} %get-tuple-element.5), kind=kOutput, calls=%fused_computation.21 | convolution fusion | flops 806879232 | bytes 6685696 | tf_op jit(solution)/shard_map/dot_general | solution.py:17
  110.6 3.5 %convolution_add_fusion.1 = f32[256,768]{1,0:T(8,128)} fusion(bf16[64,768]{1,0:T(8,128)(2,1)S(1)} %copy-done.4, bf16[2048,64]{1,0:T(8,128)(2,1)} %reshape.72, bf16[3,256,2176]{2,1,0:T(8,128)(2,1)} %all-gather.2.cloned.1.call-done, f32[768,768]{1,0:T(8,128)} %fusion.9), kind=kOutput, calls=%fused_computation.24 | convolution fusion | flops 92504064 | bytes 3244032 | tf_op jit(solution)/shard_map/dot_general | solution.py:17
  114.1 3.6 %fusion.43 = bf16[256,768]{1,0:T(8,128)(2,1)} fusion(bf16[64,768]{1,0:T(8,128)(2,1)} %reshape.75, bf16[2048,64]{1,0:T(8,128)(2,1)} %reshape.74, bf16[3,256,2176]{2,1,0:T(8,128)(2,1)} %all-gather.2.cloned.1.call-done, f32[768,768]{1,0:T(8,128)} %fusion.7, f32[256,768]{1,0:T(8,128)} %convolution_add_fusion.1), kind=kOutput, calls=%fused_computation.33 | convolution fusion | flops 93683712 | bytes 3637248 | tf_op jit(solution)/shard_map/dot_general | solution.py:17
  117.7 3.3 %fusion.53 = f32[256,2048]{1,0:T(8,128)} fusion(bf16[64,2048]{1,0:T(8,128)(2,1)S(1)} %copy-done.1, bf16[256,768]{1,0:T(8,128)(2,1)} %fusion.43, bf16[768,64]{1,0:T(8,128)(2,1)} %copy-done.2), kind=kOutput, calls=%fused_computation.52 | convolution fusion | flops 92307456 | bytes 2850816 | tf_op jit(solution)/shard_map/dot_general | solution.py:17
  121.1 3.8 %fusion.29 = bf16[256,2048]{1,0:T(8,128)(2,1)} fusion(f32[256,2048]{1,0:T(8,128)} %fusion.53, bf16[256,768]{1,0:T(8,128)(2,1)} %fusion.43, bf16[1,768,2048]{2,1,0:T(8,128)(2,1)S(1)} %copy-done, f32[256]{0:T(256)S(1)} %get-tuple-element.7), kind=kOutput, calls=%fused_computation.19 | convolution fusion | flops 806879232 | bytes 6685696 | tf_op jit(solution)/shard_map/dot_general | solution.py:17
  124.8 37.5 %reduce-scatter.6.cloned.1.call-done = bf16[16,2048]{1,0:T(8,128)(2,1)} async-done(((bf16[256,2048]{1,0:T(8,128)(2,1)}), bf16[16,2048]{1,0:T(8,128)(2,1)}) %reduce-scatter.6.cloned.1.call-update) | async-done | bytes 65552 | tf_op jit(solution)/shard_map/reduce_scatter | solution.py:68
  162.4 60.5 %reduce-scatter.4.cloned.1.call-done = bf16[16,2048]{1,0:T(8,128)(2,1)} async-done(((bf16[256,2048]{1,0:T(8,128)(2,1)}), bf16[16,2048]{1,0:T(8,128)(2,1)}) %reduce-scatter.4.cloned.1.call-update) | async-done | bytes 65552 | tf_op jit(solution)/shard_map/reduce_scatter | solution.py:68
  222.9 59.9 %reduce-scatter.8.cloned.1.call-done = bf16[16,2048]{1,0:T(8,128)(2,1)} async-done(((bf16[256,2048]{1,0:T(8,128)(2,1)}), bf16[16,2048]{1,0:T(8,128)(2,1)}) %reduce-scatter.8.cloned.1.call-update) | async-done | bytes 65552 | tf_op jit(solution)/shard_map/reduce_scatter | solution.py:68
  282.8 1.6 pad_maximum_fusion
  (40 shorter events, 5.0 us)
Async XLA Ops:
  6.5 85.9 %copy-start = (bf16[1,768,2048]{2,1,0:T(8,128)(2,1)S(1)}, bf16[1,768,2048]{2,1,0:T(8,128)(2,1)}, u32[]{:S(2)}) copy-start(bf16[1,768,2048]{2,1,0:T(8,128)(2,1)} %param.15) | copy-start | bytes 9437188
  6.5 64.2 %all-gather.2.cloned.1.call-start = ((), (), s32[]{:S(2)}) async-start(), calls=%async_computation.4 | async-start | bytes 3551232 | tf_op jit(solution)/shard_map/all_gather | solution.py:35
  18.6 40.0 %all-to-all-start = ((bf16[16,264,128]{2,1,0:T(8,128)(2,1)}), bf16[16,264,128]{2,1,0:T(8,128)(2,1)}, u32[]{:S(2)}, u32[]{:S(2)}) async-start(bf16[16,264,128]{2,1,0:T(8,128)(2,1)} %bitcast_select_fusion), calls=%async_computation | async-start | bytes 2162688 | tf_op jit(solution)/shard_map/all_to_all | solution.py:41
  26.0 136.4 %reduce-scatter.6.cloned.1.call-start = ((), (), s32[]{:S(2)}) async-start(), calls=%async_computation.6 | async-start | bytes 1114112 | tf_op jit(solution)/shard_map/reduce_scatter | solution.py:68
  61.3 27.5 %copy-start.2 = (bf16[768,64]{1,0:T(8,128)(2,1)}, bf16[768,64]{1,0:T(8,128)(2,1)S(1)}, u32[]{:S(2)}) copy-start(bf16[768,64]{1,0:T(8,128)(2,1)S(1)} %reshape.76) | copy-start | bytes 294916
  62.1 19.6 %copy-start.3 = (bf16[64,768]{1,0:T(8,128)(2,1)}, bf16[64,768]{1,0:T(8,128)(2,1)S(1)}, u32[]{:S(2)}) copy-start(bf16[64,768]{1,0:T(8,128)(2,1)S(1)} %reshape.73) | copy-start | bytes 294916
  70.7 2.8 copy-start.6
  73.6 4.1 %copy-start.7 = (bf16[1,2048,768]{2,1,0:T(8,128)(2,1)S(1)}, bf16[1,2048,768]{2,1,0:T(8,128)(2,1)}, u32[]{:S(2)}) copy-start(bf16[1,2048,768]{2,1,0:T(8,128)(2,1)} %param.13) | copy-start | bytes 9437188
  81.7 3.5 %copy-start.5 = (bf16[64,768]{1,0:T(8,128)(2,1)S(1)}, bf16[64,768]{1,0:T(8,128)(2,1)}, u32[]{:S(2)}) copy-start(bf16[64,768]{1,0:T(8,128)(2,1)} %reshape.75) | copy-start | bytes 294916
  88.8 3.4 %slice-start = ((bf16[3,256,2176]{2,1,0:T(8,128)(2,1)}), bf16[3,256,128]{2,1,0:T(8,128)(2,1)S(1)}, s32[]{:S(2)}) async-start(bf16[3,256,2176]{2,1,0:T(8,128)(2,1)} %all-gather.2.cloned.1.call-done), calls=%async_computation.8 | async-start | bytes 393216 | tf_op jit(solution)/shard_map/slice | solution.py:53
  92.4 4.0 %copy-start.4 = (bf16[64,768]{1,0:T(8,128)(2,1)S(1)}, bf16[64,768]{1,0:T(8,128)(2,1)}, u32[]{:S(2)}) copy-start(bf16[64,768]{1,0:T(8,128)(2,1)} %copy-done.3) | copy-start | bytes 294916
  96.2 126.7 %reduce-scatter.4.cloned.1.call-start = ((), (), s32[]{:S(2)}) async-start(), calls=%async_computation.5 | async-start | bytes 1114112 | tf_op jit(solution)/shard_map/reduce_scatter | solution.py:68
  99.9 3.6 %copy-start.1 = (bf16[64,2048]{1,0:T(8,128)(2,1)S(1)}, bf16[64,2048]{1,0:T(8,128)(2,1)}, u32[]{:S(2)}) copy-start(bf16[64,2048]{1,0:T(8,128)(2,1)} %reshape.77) | copy-start | bytes 786436
  110.5 172.3 %reduce-scatter.8.cloned.1.call-start = ((), (), s32[]{:S(2)}) async-start(), calls=%async_computation.7 | async-start | bytes 1114112 | tf_op jit(solution)/shard_map/reduce_scatter | solution.py:68
Sparse Core Ops, SparseCore 0:
  10.3 60.3 all-gather.1
  96.3 66.0 reduce-scatter.5
  166.4 56.4 reduce-scatter.3
  226.4 56.3 reduce-scatter.7

commit v2 on v0

--- a/solution.py
+++ b/solution.py
@@ -4,6 +4,108 @@
 from jax.sharding import PartitionSpec as P
 
 adapter_scale = 2.0
+LANES = 128
+
+
+def route_gates(logits):
+    highest = jnp.max(logits, axis=-1, keepdims=True)
+    router_scores = jnp.exp(logits - highest)
+    return (router_scores / jnp.sum(router_scores, axis=-1, keepdims=True)).astype(jnp.bfloat16)
+
+
+def split_axis(n):
+    cores = 2 if n % 2 == 0 else 1
+    chips = n // cores
+    middle = 1
+    while chips % (2 * middle) == 0 and 4 * middle * middle <= chips:
+        middle *= 2
+    return chips // middle, middle, cores
+
+
+def shift(x, n, stride, size, k):
+    pairs = []
+    for i in range(n):
+        place = i // stride % size
+        pairs.append((i, i + ((place + k) % size - place) * stride))
+    return lax.ppermute(x, "expert", pairs)
+
+
+def gather_rows(x, n):
+    outer, middle, cores = split_axis(n)
+    for stride, size in ((middle * cores, outer), (cores, middle), (1, cores)):
+        x = jnp.stack([x] + [shift(x, n, stride, size, k) for k in range(1, size)])
+    return x
+
+
+def scatter_rows(x, n):
+    outer, middle, cores = split_axis(n)
+    for stride, size in ((1, cores), (cores, middle), (middle * cores, outer)):
+        kept = x[0]
+        for k in range(1, size):
+            sent = shift(x[k].astype(jnp.bfloat16), n, stride, size, size - k)
+            kept = kept + sent.astype(jnp.float32)
+        x = kept
+    return x.astype(jnp.bfloat16)
+
+
+def dot(a, b):
+    return jnp.dot(a, b, preferred_element_type=jnp.float32)
+
+
+def dense_shards(hidden, route_ids, route_logits, placement, factors, w_gate, w_up, down_weight):
+    owners = lax.axis_size("expert")
+    experts = placement.shape[0]
+    steps, rows, width = hidden.shape
+    units = w_gate.shape[2]
+    rank = factors.shape[1] * owners // (3 * (width + units))
+    total = rows * owners
+
+    gates = route_gates(route_logits)
+    chosen = route_ids[..., None] == jnp.arange(experts, dtype=jnp.int32)
+    dense = jnp.sum(jnp.where(chosen, gates[..., None], 0), axis=2, dtype=jnp.float32)
+    dense = dense.astype(jnp.bfloat16)
+    padded = -(-experts // LANES) * LANES
+    dense = jnp.pad(dense, ((0, 0), (0, 0), (0, padded - experts)))
+    payload = jnp.concatenate([hidden, dense], axis=-1)
+    gathered = [
+        gather_rows(payload[s], owners).reshape(total, width + padded) for s in range(steps)
+    ]
+
+    slot_of = (
+        jnp.zeros((experts,), jnp.int32).at[placement].set(jnp.arange(experts, dtype=jnp.int32))
+    )
+    ordered = jnp.take(factors, slot_of, axis=0).reshape(experts, -1, LANES)
+    received = lax.all_to_all(ordered, "expert", split_axis=0, concat_axis=0, tiled=True)
+    flat = received.reshape(-1, LANES)
+    shapes = [(width, rank), (rank, units)] * 2 + [(units, rank), (rank, width)]
+    segments, at = [], 0
+    for lead, trail in shapes:
+        n = lead * trail // LANES
+        segments.append(flat[at : at + n].reshape(lead, trail))
+        at += n
+    gate_a, gate_b, up_a, up_b, down_a, down_b = segments
+
+    me = lax.axis_index("expert")
+    results = []
+    for s in range(steps):
+        x = gathered[s][:, :width]
+        mine = lax.dynamic_index_in_dim(gathered[s][:, width:], me, 1, keepdims=True)
+        low_g = (adapter_scale * dot(x, gate_a)).astype(jnp.bfloat16)
+        low_u = (adapter_scale * dot(x, up_a)).astype(jnp.bfloat16)
+        g = dot(x, w_gate[0]) + dot(low_g, gate_b)
+        u = dot(x, w_up[0]) + dot(low_u, up_b)
+        inner = (jax.nn.silu(g) * u).astype(jnp.bfloat16)
+        low_d = (adapter_scale * dot(inner, down_a)).astype(jnp.bfloat16)
+        out = dot(inner, down_weight[0]) + dot(low_d, down_b)
+        weighted = out * mine.astype(jnp.float32)
+        outer, middle, cores = split_axis(owners)
+        weighted = weighted.reshape(cores, middle, outer, rows, width)
+        results.append(scatter_rows(weighted, owners))
+    return jnp.stack(results, axis=0)
+
+
+def row_capacity(rows, top, experts):
+    return min(rows, 3 * max(1, rows * top // experts))
 
 
 def unpack_factors(flat_factors, width, hidden_units, rank_size):
@@ -39,20 +141,14 @@
     )
 
 
-def route_gates(logits):
-    highest = jnp.max(logits, axis=-1, keepdims=True)
-    router_scores = jnp.exp(logits - highest)
-    return (router_scores / jnp.sum(router_scores, axis=-1, keepdims=True)).astype(jnp.bfloat16)
-
-
-def shards(hidden, route_ids, route_logits, placement, factors, w_gate, w_up, down_weight):
+def sparse_shards(hidden, route_ids, route_logits, placement, factors, w_gate, w_up, down_weight):
     owners = lax.axis_size("expert")
     experts = placement.shape[0]
     steps_count, row_count, width = hidden.shape
     top_count = route_ids.shape[2]
     hidden_units = w_gate.shape[2]
     rank_size = factors.shape[1] * owners // (3 * (width + hidden_units))
-    capacity = min(row_count, 3 * max(1, row_count * top_count // experts))
+    capacity = row_capacity(row_count, top_count, experts)
     slot_of = (
         jnp.zeros((experts,), jnp.int32).at[placement].set(jnp.arange(experts, dtype=jnp.int32))
     )
@@ -98,6 +194,13 @@
             pair_out.reshape(row_count, top_count, width).sum(axis=1).astype(jnp.bfloat16)
         )
     return jnp.stack(results, axis=0)
+
+
+def shards(hidden, route_ids, *rest):
+    rows, top = route_ids.shape[1:]
+    experts = rest[1].shape[0]
+    every = row_capacity(rows, top, experts) == rows
+    return (dense_shards if every else sparse_shards)(hidden, route_ids, *rest)
 
 
 def solution(mesh):

time: 219 us -> 187 us (0.85)
  waiting for transfers between devices: 92.3 us -> 35.6 us
  local copies, waits for them, and re-layouts: 15 us -> 31.8 us
  starting transfers between devices: 48.3 us -> 52.4 us
  matrix products: 49.3 us -> 52.4 us
    all_to_all x7 -> x1, waiting for transfers between devices: 92.3 us -> 0.01 us  [dense_shards(): lax.all_to_all(ordered, 'expert', split_axis=0, concat_axis=0, tiled=True)]
    ppermute x0 -> x30, starting transfers between devices: none -> 46.6 us  [shift(): return lax.ppermute(x, 'expert', pairs)]
    all_to_all x7 -> x1, starting transfers between devices: 48.3 us -> 5.76 us  [dense_shards(): lax.all_to_all(ordered, 'expert', split_axis=0, concat_axis=0, tiled=True)]
    ppermute x0 -> x30, waiting for transfers between devices: none -> 35.6 us  [shift(): return lax.ppermute(x, 'expert', pairs)]
    reshape x2 -> x6, local copies, waits for them, and re-layouts: 0.21 us -> 8.47 us  [dense_shards(): segments.append(flat[at:at + n].reshape(lead, trail))]
    all_to_all x1 -> x0, other arithmetic: 7.59 us -> none  [shards(): lax.all_to_all(ordered, 'expert', split_axis=0, concat_axis=1, tiled=True)]
    unnamed x19 -> x39, local copies, waits for them, and re-layouts: 5.15 us -> 12 us
    another operation x4 -> x16, other arithmetic: 1.22 us -> 7.93 us  [the longest x9 6.94 us: gather_rows(): x = jnp.stack([x] + [shift(x, n, stride, size, k) for k in range(1, size)])]
  transfers between devices with their start and end apart: 7 -> 31, of which waited for: 6 -> 7; matrix products, arithmetic and copies ran while one was open for 32% -> 31% of each run, Pallas kernels for 0% -> 0%
where the time goes in v2:
time: 187 us; the launch traced here: 186 us
  starting transfers between devices  52.4 us (28%)
  matrix products  52.4 us (28%)
  waiting for transfers between devices  35.6 us (19%)
  local copies, waits for them, and re-layouts  31.8 us (17%)
  other arithmetic  12.9 us (7%)
    dot_general x18, matrix products, dot(): return jnp.dot(a, b, preferred_element_type=jnp.float32)  52.4 us
    ppermute x30, starting transfers between devices, shift(): return lax.ppermute(x, 'expert', pairs)  46.6 us
    ppermute x30, waiting for transfers between devices, shift(): return lax.ppermute(x, 'expert', pairs)  35.6 us
    unnamed x39, local copies, waits for them, and re-layouts  12 us
    reshape x6, local copies, waits for them, and re-layouts, dense_shards(): segments.append(flat[at:at + n].reshape(lead, trail))  8.47 us
    another operation x9, other arithmetic, gather_rows(): x = jnp.stack([x] + [shift(x, n, stride, size, k) for k in range(1, size)])  6.94 us
    all_to_all x1, starting transfers between devices, dense_shards(): lax.all_to_all(ordered, 'expert', split_axis=0, concat_axis=0, tiled=True)  5.76 us
    gather x1, local copies, waits for them, and re-layouts, dense_shards(): ordered = jnp.take(factors, slot_of, axis=0).reshape(experts, -1, LANES)  4.57 us
  transfers between devices with their start and end apart: 31, of which 7 were waited for; matrix products, arithmetic and copies ran while one was open for 31% of the time, Pallas kernels for 0%

profile of v2, /device:TPU:0, one launch (start us, length us, event | category | flops | bytes accessed | tf_op | source)
XLA Modules:
  0.0 185.6 jit_solution(11761838664109901296)
XLA Ops:
  3.6 3.0 %collective-permute-start = (bf16[16,2176]{1,0:T(8,128)(2,1)}, bf16[16,2176]{1,0:T(8,128)(2,1)}, u32[]{:S(2)}, u32[]{:S(2)}) collective-permute-start(bf16[16,2176]{1,0:T(8,128)(2,1)} %get-tuple-element.39), channel_id=1, source_target_pairs={{0,4},{1,5},{2,6},{3,7},{4,8},{5,9},{6,10},{7,11},{8,12},{9,13},{1... | collective-permute-start | bytes 208904 | tf_op jit(solution)/shard_map/ppermute | solution.py:30
  6.6 2.6 %collective-permute-start.1 = (bf16[16,2176]{1,0:T(8,128)(2,1)}, bf16[16,2176]{1,0:T(8,128)(2,1)}, u32[]{:S(2)}, u32[]{:S(2)}) collective-permute-start(bf16[16,2176]{1,0:T(8,128)(2,1)} %get-tuple-element.39), channel_id=1, source_target_pairs={{0,8},{1,9},{2,10},{3,11},{4,12},{5,13},{6,14},{7,15},{8,0},{9,1},... | collective-permute-start | bytes 208904 | tf_op jit(solution)/shard_map/ppermute | solution.py:30
  12.3 4.6 %gather_fusion = bf16[16,33792]{1,0:T(8,128)(2,1)} fusion(bf16[16,33792]{1,0:T(8,128)(2,1)} %param.12, s32[1024]{0:T(1024)S(1)} %pad_clamp_fusion), kind=kCustom, calls=%fused_computation | custom fusion | bytes 2162752 | tf_op jit(solution)/shard_map/jit(_take)/gather | solution.py:77
  19.5 5.8 %all-to-all-start = ((bf16[16,264,128]{2,1,0:T(8,128)(2,1)}), bf16[16,264,128]{2,1,0:T(8,128)(2,1)}, u32[]{:S(2)}, u32[]{:S(2)}) async-start(bf16[16,264,128]{2,1,0:T(8,128)(2,1)} %bitcast_select_fusion), calls=%async_computation | async-start | bytes 2162688 | tf_op jit(solution)/shard_map/all_to_all | solution.py:78
  25.3 3.7 %collective-permute-start.12 = (bf16[16,2176]{1,0:T(8,128)(2,1)S(1)}, bf16[16,2176]{1,0:T(8,128)(2,1)S(1)}, u32[]{:S(2)}, u32[]{:S(2)}) collective-permute-start(bf16[16,2176]{1,0:T(8,128)(2,1)S(1)} %get-tuple-element.40), channel_id=1, source_target_pairs={{0,12},{1,13},{2,14},{3,15},{4,0},{5,1},{6,2},{7,3},{8,4},{9,5},{1... | collective-permute-start | bytes 208904 | tf_op jit(solution)/shard_map/ppermute | solution.py:30
  31.1 2.9 %collective-permute-start.22 = (bf16[16,2176]{1,0:T(8,128)(2,1)S(1)}, bf16[16,2176]{1,0:T(8,128)(2,1)S(1)}, u32[]{:S(2)}, u32[]{:S(2)}) collective-permute-start(bf16[16,2176]{1,0:T(8,128)(2,1)S(1)} %get-tuple-element.41), channel_id=1, source_target_pairs={{0,12},{1,13},{2,14},{3,15},{4,0},{5,1},{6,2},{7,3},{8,4},{9,5},{1... | collective-permute-start | bytes 208904 | tf_op jit(solution)/shard_map/ppermute | solution.py:30
  35.5 10.0 %collective-permute-done.12 = bf16[16,2176]{1,0:T(8,128)(2,1)S(1)} collective-permute-done((bf16[16,2176]{1,0:T(8,128)(2,1)S(1)}, bf16[16,2176]{1,0:T(8,128)(2,1)S(1)}, u32[]{:S(2)}, u32[]{:S(2)}) %collective-permute-start.12) | collective-permute-done | bytes 69664 | tf_op jit(solution)/shard_map/ppermute | solution.py:30
  48.4 2.8 %collective-permute-done.20 = bf16[16,2176]{1,0:T(8,128)(2,1)S(1)} collective-permute-done((bf16[16,2176]{1,0:T(8,128)(2,1)S(1)}, bf16[16,2176]{1,0:T(8,128)(2,1)S(1)}, u32[]{:S(2)}, u32[]{:S(2)}) %collective-permute-start.20) | collective-permute-done | bytes 69664 | tf_op jit(solution)/shard_map/ppermute | solution.py:30
  51.2 7.7 %collective-permute-done.21 = bf16[16,2176]{1,0:T(8,128)(2,1)S(1)} collective-permute-done((bf16[16,2176]{1,0:T(8,128)(2,1)S(1)}, bf16[16,2176]{1,0:T(8,128)(2,1)S(1)}, u32[]{:S(2)}, u32[]{:S(2)}) %collective-permute-start.21) | collective-permute-done | bytes 69664 | tf_op jit(solution)/shard_map/ppermute | solution.py:30
  62.3 4.5 %collective-permute-done.23 = bf16[4,16,2176]{2,1,0:T(8,128)(2,1)S(1)} collective-permute-done((bf16[4,16,2176]{2,1,0:T(8,128)(2,1)S(1)}, bf16[4,16,2176]{2,1,0:T(8,128)(2,1)S(1)}, u32[]{:S(2)}, u32[]{:S(2)}) %collective-permute-start.23) | collective-permute-done | bytes 278560 | tf_op jit(solution)/shard_map/ppermute | solution.py:30
  74.1 4.2 %fusion.17 = f32[256,768]{1,0:T(8,128)} fusion(bf16[1,2048,768]{2,1,0:T(8,128)(2,1)} %param.13, bf16[256,2176]{1,0:T(8,128)(2,1)} %bitcast.202), kind=kOutput, calls=%fused_computation.19 | convolution fusion | flops 805306368 | bytes 4980736 | tf_op jit(solution)/shard_map/dot_general | solution.py:52
  88.4 2.0 %fusion.133 = (bf16[1024,128]{1,0:T(8,128)(2,1)}, bf16[1024,128]{1,0:T(8,128)(2,1)}, bf16[1024,128]{1,0:T(8,128)(2,1)S(1)}) fusion(bf16[4224,128]{1,0:T(8,128)(2,1)} %bitcast.10), kind=kLoop, calls=%fused_computation.177 | loop fusion | bytes 1572864 | tf_op jit(solution)/shard_map/slice | solution.py:84
  92.0 2.0 %reshape.78 = bf16[2048,64]{1,0:T(8,128)(2,1)} reshape(bf16[1024,128]{1,0:T(8,128)(2,1)} %get-tuple-element.14) | data formatting | bytes 524288 | tf_op jit(solution)/shard_map/reshape | solution.py:84
  100.5 3.4 %convolution_add_fusion.5 = f32[256,768]{1,0:T(8,128)} fusion(f32[256,768]{1,0:T(8,128)} %fusion.17, bf16[64,768]{1,0:T(8,128)(2,1)S(1)} %reshape.79, bf16[2048,64]{1,0:T(8,128)(2,1)} %reshape.78, bf16[256,2176]{1,0:T(8,128)(2,1)} %bitcast.203), kind=kOutput, calls=%fused_computation.35 | convolution fusion | flops 92504064 | bytes 3244032 | tf_op jit(solution)/shard_map/dot_general | solution.py:52
  103.9 3.6 %fusion.40 = bf16[256,768]{1,0:T(8,128)(2,1)} fusion(f32[256,768]{1,0:T(8,128)} %fusion.11, bf16[64,768]{1,0:T(8,128)(2,1)} %reshape.81, bf16[2048,64]{1,0:T(8,128)(2,1)} %reshape.80, f32[256,768]{1,0:T(8,128)} %convolution_add_fusion.5, bf16[256,2176]{1,0:T(8,128)(2,1)} %bitcast.204), kind=kOutput, calls=%fused_computation.36 | convolution fusion | flops 93683712 | bytes 3637248 | tf_op jit(solution)/shard_map/dot_general | solution.py:52
  107.5 3.3 %fusion.54 = f32[256,2048]{1,0:T(8,128)} fusion(bf16[64,2048]{1,0:T(8,128)(2,1)S(1)} %reshape.83, bf16[256,768]{1,0:T(8,128)(2,1)} %fusion.40, bf16[768,64]{1,0:T(8,128)(2,1)} %reshape.82), kind=kOutput, calls=%fused_computation.62 | convolution fusion | flops 92307456 | bytes 2850816 | tf_op jit(solution)/shard_map/dot_general | solution.py:52
  110.8 2.7 %fusion.22 = f32[256,2048]{1,0:T(8,128)S(1)} fusion(f32[256,2048]{1,0:T(8,128)} %fusion.54, bf16[256,768]{1,0:T(8,128)(2,1)} %fusion.40, bf16[1,768,2048]{2,1,0:T(8,128)(2,1)S(1)} %copy-done, f32[256]{0:T(256)S(1)} %bitcast.218), kind=kOutput, calls=%fused_computation.22 | convolution fusion | flops 806354944 | bytes 7734272 | tf_op jit(solution)/shard_map/dot_general | solution.py:52
  116.3 3.4 %convolution_add_fusion.3 = f32[256,768]{1,0:T(8,128)} fusion(f32[256,768]{1,0:T(8,128)} %fusion.15, bf16[64,768]{1,0:T(8,128)(2,1)S(1)} %reshape.79, bf16[2048,64]{1,0:T(8,128)(2,1)} %reshape.78, bf16[256,2176]{1,0:T(8,128)(2,1)} %bitcast.197), kind=kOutput, calls=%fused_computation.32 | convolution fusion | flops 92504064 | bytes 3244032 | tf_op jit(solution)/shard_map/dot_general | solution.py:52
  119.7 3.6 %fusion.41 = bf16[256,768]{1,0:T(8,128)(2,1)} fusion(f32[256,768]{1,0:T(8,128)} %fusion.9, bf16[64,768]{1,0:T(8,128)(2,1)} %reshape.81, bf16[2048,64]{1,0:T(8,128)(2,1)} %reshape.80, f32[256,768]{1,0:T(8,128)} %convolution_add_fusion.3, bf16[256,2176]{1,0:T(8,128)(2,1)} %bitcast.198), kind=kOutput, calls=%fused_computation.37 | convolution fusion | flops 93683712 | bytes 3637248 | tf_op jit(solution)/shard_map/dot_general | solution.py:52
  123.3 3.3 %fusion.53 = f32[256,2048]{1,0:T(8,128)} fusion(bf16[64,2048]{1,0:T(8,128)(2,1)S(1)} %reshape.83, bf16[256,768]{1,0:T(8,128)(2,1)} %fusion.41, bf16[768,64]{1,0:T(8,128)(2,1)} %reshape.82), kind=kOutput, calls=%fused_computation.61 | convolution fusion | flops 92307456 | bytes 2850816 | tf_op jit(solution)/shard_map/dot_general | solution.py:52
  126.6 3.6 %convolution_add_fusion.1 = f32[256,768]{1,0:T(8,128)} fusion(f32[256,768]{1,0:T(8,128)} %fusion.13, bf16[64,768]{1,0:T(8,128)(2,1)S(1)} %reshape.79, bf16[2048,64]{1,0:T(8,128)(2,1)} %reshape.78, bf16[256,2176]{1,0:T(8,128)(2,1)} %bitcast.192), kind=kOutput, calls=%fused_computation.29 | convolution fusion | flops 92504064 | bytes 3244032 | tf_op jit(solution)/shard_map/dot_general | solution.py:52
  130.2 4.1 %fusion.28 = f32[256,2048]{1,0:T(8,128)} fusion(f32[256,2048]{1,0:T(8,128)} %fusion.53, bf16[256,768]{1,0:T(8,128)(2,1)} %fusion.41, bf16[1,768,2048]{2,1,0:T(8,128)(2,1)S(1)} %copy-done, f32[256]{0:T(256)S(1)} %bitcast.219), kind=kOutput, calls=%fused_computation.24 | convolution fusion | flops 806354944 | bytes 7734272 | tf_op jit(solution)/shard_map/dot_general | solution.py:52
  134.3 3.5 %fusion.42 = bf16[256,768]{1,0:T(8,128)(2,1)} fusion(f32[256,768]{1,0:T(8,128)} %fusion.7, bf16[64,768]{1,0:T(8,128)(2,1)S(1)} %copy-done.13, bf16[2048,64]{1,0:T(8,128)(2,1)} %reshape.80, f32[256,768]{1,0:T(8,128)} %convolution_add_fusion.1, bf16[256,2176]{1,0:T(8,128)(2,1)} %bitcast.193), kind=kOutput, calls=%fused_computation.38 | convolution fusion | flops 93683712 | bytes 3637248 | tf_op jit(solution)/shard_map/dot_general | solution.py:52
  137.8 3.3 %fusion.52 = f32[256,2048]{1,0:T(8,128)} fusion(bf16[64,2048]{1,0:T(8,128)(2,1)S(1)} %reshape.83, bf16[256,768]{1,0:T(8,128)(2,1)} %fusion.42, bf16[768,64]{1,0:T(8,128)(2,1)} %reshape.82), kind=kOutput, calls=%fused_computation.60 | convolution fusion | flops 92307456 | bytes 2850816 | tf_op jit(solution)/shard_map/dot_general | solution.py:52
  152.8 5.2 %collective-permute-done.6 = bf16[4,16,2048]{2,1,0:T(8,128)(2,1)S(1)} collective-permute-done((bf16[4,16,2048]{2,1,0:T(8,128)(2,1)S(1)}, bf16[4,16,2048]{2,1,0:T(8,128)(2,1)S(1)}, u32[]{:S(2)}, u32[]{:S(2)}) %collective-permute-start.6) | collective-permute-done | bytes 262176 | tf_op jit(solution)/shard_map/ppermute | solution.py:30
  158.1 3.0 %collective-permute-start.7 = (bf16[16,2048]{1,0:T(8,128)(2,1)S(1)}, bf16[16,2048]{1,0:T(8,128)(2,1)S(1)}, u32[]{:S(2)}, u32[]{:S(2)}) collective-permute-start(bf16[16,2048]{1,0:T(8,128)(2,1)S(1)} %get-tuple-element.29), channel_id=1, source_target_pairs={{0,12},{1,13},{2,14},{3,15},{4,0},{5,1},{6,2},{7,3},{8,4},{9,5},{1... | collective-permute-start | bytes 196616 | tf_op jit(solution)/shard_map/ppermute | solution.py:30
  161.1 4.5 %collective-permute-start.8 = (bf16[16,2048]{1,0:T(8,128)(2,1)S(1)}, bf16[16,2048]{1,0:T(8,128)(2,1)S(1)}, u32[]{:S(2)}, u32[]{:S(2)}) collective-permute-start(bf16[16,2048]{1,0:T(8,128)(2,1)S(1)} %get-tuple-element.31), channel_id=1, source_target_pairs={{0,8},{1,9},{2,10},{3,11},{4,12},{5,13},{6,14},{7,15},{8,0},{9,1},... | collective-permute-start | bytes 196616 | tf_op jit(solution)/shard_map/ppermute | solution.py:30
  165.7 3.9 %collective-permute-start.17 = (bf16[16,2048]{1,0:T(8,128)(2,1)S(1)}, bf16[16,2048]{1,0:T(8,128)(2,1)S(1)}, u32[]{:S(2)}, u32[]{:S(2)}) collective-permute-start(bf16[16,2048]{1,0:T(8,128)(2,1)S(1)} %get-tuple-element.32), channel_id=1, source_target_pairs={{0,12},{1,13},{2,14},{3,15},{4,0},{5,1},{6,2},{7,3},{8,4},{9,5},{1... | collective-permute-start | bytes 196616 | tf_op jit(solution)/shard_map/ppermute | solution.py:30
  169.6 3.7 %collective-permute-start.18 = (bf16[16,2048]{1,0:T(8,128)(2,1)S(1)}, bf16[16,2048]{1,0:T(8,128)(2,1)S(1)}, u32[]{:S(2)}, u32[]{:S(2)}) collective-permute-start(bf16[16,2048]{1,0:T(8,128)(2,1)S(1)} %get-tuple-element.34), channel_id=1, source_target_pairs={{0,8},{1,9},{2,10},{3,11},{4,12},{5,13},{6,14},{7,15},{8,0},{9,1},... | collective-permute-start | bytes 196616 | tf_op jit(solution)/shard_map/ppermute | solution.py:30
  174.4 2.8 %collective-permute-start.27 = (bf16[16,2048]{1,0:T(8,128)(2,1)S(1)}, bf16[16,2048]{1,0:T(8,128)(2,1)S(1)}, u32[]{:S(2)}, u32[]{:S(2)}) collective-permute-start(bf16[16,2048]{1,0:T(8,128)(2,1)S(1)} %get-tuple-element.35), channel_id=1, source_target_pairs={{0,12},{1,13},{2,14},{3,15},{4,0},{5,1},{6,2},{7,3},{8,4},{9,5},{1... | collective-permute-start | bytes 196616 | tf_op jit(solution)/shard_map/ppermute | solution.py:30
  177.5 2.0 %collective-permute-start.29 = (bf16[16,2048]{1,0:T(8,128)(2,1)S(1)}, bf16[16,2048]{1,0:T(8,128)(2,1)S(1)}, u32[]{:S(2)}, u32[]{:S(2)}) collective-permute-start(bf16[16,2048]{1,0:T(8,128)(2,1)S(1)} %get-tuple-element.36), channel_id=1, source_target_pairs={{0,4},{1,5},{2,6},{3,7},{4,8},{5,9},{6,10},{7,11},{8,12},{9,13},{1... | collective-permute-start | bytes 196616 | tf_op jit(solution)/shard_map/ppermute | solution.py:30
  181.0 3.8 %collective-permute-done.28 = bf16[16,2048]{1,0:T(8,128)(2,1)S(1)} collective-permute-done((bf16[16,2048]{1,0:T(8,128)(2,1)S(1)}, bf16[16,2048]{1,0:T(8,128)(2,1)S(1)}, u32[]{:S(2)}, u32[]{:S(2)}) %collective-permute-start.28) | collective-permute-done | bytes 65568 | tf_op jit(solution)/shard_map/ppermute | solution.py:30
  (148 shorter events, 62.7 us)
Async XLA Ops:
  0.0 110.8 %copy-start = (bf16[1,768,2048]{2,1,0:T(8,128)(2,1)S(1)}, bf16[1,768,2048]{2,1,0:T(8,128)(2,1)}, u32[]{:S(2)}) copy-start(bf16[1,768,2048]{2,1,0:T(8,128)(2,1)} %param.15) | copy-start | bytes 9437188
  3.6 21.6 %collective-permute-start = (bf16[16,2176]{1,0:T(8,128)(2,1)}, bf16[16,2176]{1,0:T(8,128)(2,1)}, u32[]{:S(2)}, u32[]{:S(2)}) collective-permute-start(bf16[16,2176]{1,0:T(8,128)(2,1)} %get-tuple-element.39), channel_id=1, source_target_pairs={{0,4},{1,5},{2,6},{3,7},{4,8},{5,9},{6,10},{7,11},{8,12},{9,13},{1... | collective-permute-start | bytes 208904 | tf_op jit(solution)/shard_map/ppermute | solution.py:30
  6.6 22.3 %collective-permute-start.1 = (bf16[16,2176]{1,0:T(8,128)(2,1)}, bf16[16,2176]{1,0:T(8,128)(2,1)}, u32[]{:S(2)}, u32[]{:S(2)}) collective-permute-start(bf16[16,2176]{1,0:T(8,128)(2,1)} %get-tuple-element.39), channel_id=1, source_target_pairs={{0,8},{1,9},{2,10},{3,11},{4,12},{5,13},{6,14},{7,15},{8,0},{9,1},... | collective-permute-start | bytes 208904 | tf_op jit(solution)/shard_map/ppermute | solution.py:30
  9.2 19.8 %collective-permute-start.2 = (bf16[16,2176]{1,0:T(8,128)(2,1)}, bf16[16,2176]{1,0:T(8,128)(2,1)}, u32[]{:S(2)}, u32[]{:S(2)}) collective-permute-start(bf16[16,2176]{1,0:T(8,128)(2,1)} %get-tuple-element.39), channel_id=1, source_target_pairs={{0,12},{1,13},{2,14},{3,15},{4,0},{5,1},{6,2},{7,3},{8,4},{9,5},{1... | collective-permute-start | bytes 208904 | tf_op jit(solution)/shard_map/ppermute | solution.py:30
  10.6 20.5 %collective-permute-start.10 = (bf16[16,2176]{1,0:T(8,128)(2,1)S(1)}, bf16[16,2176]{1,0:T(8,128)(2,1)}, u32[]{:S(2)}, u32[]{:S(2)}) collective-permute-start(bf16[16,2176]{1,0:T(8,128)(2,1)S(1)} %get-tuple-element.40), channel_id=1, source_target_pairs={{0,4},{1,5},{2,6},{3,7},{4,8},{5,9},{6,10},{7,11},{8,12},{9,13},{1... | collective-permute-start | bytes 208904 | tf_op jit(solution)/shard_map/ppermute | solution.py:30
  11.3 22.8 %collective-permute-start.11 = (bf16[16,2176]{1,0:T(8,128)(2,1)S(1)}, bf16[16,2176]{1,0:T(8,128)(2,1)}, u32[]{:S(2)}, u32[]{:S(2)}) collective-permute-start(bf16[16,2176]{1,0:T(8,128)(2,1)S(1)} %get-tuple-element.40), channel_id=1, source_target_pairs={{0,8},{1,9},{2,10},{3,11},{4,12},{5,13},{6,14},{7,15},{8,0},{9,1},... | collective-permute-start | bytes 208904 | tf_op jit(solution)/shard_map/ppermute | solution.py:30
  19.5 68.9 %all-to-all-start = ((bf16[16,264,128]{2,1,0:T(8,128)(2,1)}), bf16[16,264,128]{2,1,0:T(8,128)(2,1)}, u32[]{:S(2)}, u32[]{:S(2)}) async-start(bf16[16,264,128]{2,1,0:T(8,128)(2,1)} %bitcast_select_fusion), calls=%async_computation | async-start | bytes 2162688 | tf_op jit(solution)/shard_map/all_to_all | solution.py:78
  25.3 20.3 %collective-permute-start.12 = (bf16[16,2176]{1,0:T(8,128)(2,1)S(1)}, bf16[16,2176]{1,0:T(8,128)(2,1)S(1)}, u32[]{:S(2)}, u32[]{:S(2)}) collective-permute-start(bf16[16,2176]{1,0:T(8,128)(2,1)S(1)} %get-tuple-element.40), channel_id=1, source_target_pairs={{0,12},{1,13},{2,14},{3,15},{4,0},{5,1},{6,2},{7,3},{8,4},{9,5},{1... | collective-permute-start | bytes 208904 | tf_op jit(solution)/shard_map/ppermute | solution.py:30
  29.0 22.2 %collective-permute-start.20 = (bf16[16,2176]{1,0:T(8,128)(2,1)S(1)}, bf16[16,2176]{1,0:T(8,128)(2,1)S(1)}, u32[]{:S(2)}, u32[]{:S(2)}) collective-permute-start(bf16[16,2176]{1,0:T(8,128)(2,1)S(1)} %get-tuple-element.41), channel_id=1, source_target_pairs={{0,4},{1,5},{2,6},{3,7},{4,8},{5,9},{6,10},{7,11},{8,12},{9,13},{1... | collective-permute-start | bytes 208904 | tf_op jit(solution)/shard_map/ppermute | solution.py:30
  29.0 29.9 %collective-permute-start.21 = (bf16[16,2176]{1,0:T(8,128)(2,1)S(1)}, bf16[16,2176]{1,0:T(8,128)(2,1)S(1)}, u32[]{:S(2)}, u32[]{:S(2)}) collective-permute-start(bf16[16,2176]{1,0:T(8,128)(2,1)S(1)} %get-tuple-element.41), channel_id=1, source_target_pairs={{0,8},{1,9},{2,10},{3,11},{4,12},{5,13},{6,14},{7,15},{8,0},{9,1},... | collective-permute-start | bytes 208904 | tf_op jit(solution)/shard_map/ppermute | solution.py:30
  31.1 27.8 %collective-permute-start.22 = (bf16[16,2176]{1,0:T(8,128)(2,1)S(1)}, bf16[16,2176]{1,0:T(8,128)(2,1)S(1)}, u32[]{:S(2)}, u32[]{:S(2)}) collective-permute-start(bf16[16,2176]{1,0:T(8,128)(2,1)S(1)} %get-tuple-element.41), channel_id=1, source_target_pairs={{0,12},{1,13},{2,14},{3,15},{4,0},{5,1},{6,2},{7,3},{8,4},{9,5},{1... | collective-permute-start | bytes 208904 | tf_op jit(solution)/shard_map/ppermute | solution.py:30
  34.1 26.5 %collective-permute-start.3 = (bf16[4,16,2176]{2,1,0:T(8,128)(2,1)S(1)}, bf16[4,16,2176]{2,1,0:T(8,128)(2,1)S(1)}, u32[]{:S(2)}, u32[]{:S(2)}) collective-permute-start(bf16[4,16,2176]{2,1,0:T(8,128)(2,1)S(1)} %get-tuple-element.24), channel_id=1, source_target_pairs={{0,2},{1,3},{2,0},{3,1},{4,6},{5,7},{6,4},{7,5},{8,10},{9,11},{10,... | collective-permute-start | bytes 835592 | tf_op jit(solution)/shard_map/ppermute | solution.py:30
  46.5 14.2 %collective-permute-start.13 = (bf16[4,16,2176]{2,1,0:T(8,128)(2,1)S(1)}, bf16[4,16,2176]{2,1,0:T(8,128)(2,1)S(1)}, u32[]{:S(2)}, u32[]{:S(2)}) collective-permute-start(bf16[4,16,2176]{2,1,0:T(8,128)(2,1)S(1)} %get-tuple-element.26), channel_id=1, source_target_pairs={{0,2},{1,3},{2,0},{3,1},{4,6},{5,7},{6,4},{7,5},{8,10},{9,11},{10,... | collective-permute-start | bytes 835592 | tf_op jit(solution)/shard_map/ppermute | solution.py:30
  59.0 7.8 %collective-permute-start.23 = (bf16[4,16,2176]{2,1,0:T(8,128)(2,1)S(1)}, bf16[4,16,2176]{2,1,0:T(8,128)(2,1)S(1)}, u32[]{:S(2)}, u32[]{:S(2)}) collective-permute-start(bf16[4,16,2176]{2,1,0:T(8,128)(2,1)S(1)} %get-tuple-element.28), channel_id=1, source_target_pairs={{0,2},{1,3},{2,0},{3,1},{4,6},{5,7},{6,4},{7,5},{8,10},{9,11},{10,... | collective-permute-start | bytes 835592 | tf_op jit(solution)/shard_map/ppermute | solution.py:30
  60.7 7.2 %collective-permute-start.4 = (bf16[2,4,16,2176]{3,2,1,0:T(8,128)(2,1)S(1)}, bf16[2,4,16,2176]{3,2,1,0:T(8,128)(2,1)S(1)}, u32[]{:S(2)}, u32[]{:S(2)}) collective-permute-start(bf16[2,4,16,2176]{3,2,1,0:T(8,128)(2,1)S(1)} %get-tuple-element.18), channel_id=1, source_target_pairs={{0,1},{1,0},{2,3},{3,2},{4,5},{5,4},{6,7},{7,6},{8,9},{9,8},{10,11... | collective-permute-start | bytes 1671176 | tf_op jit(solution)/shard_map/ppermute | solution.py:30
  61.8 7.4 %collective-permute-start.14 = (bf16[2,4,16,2176]{3,2,1,0:T(8,128)(2,1)}, bf16[2,4,16,2176]{3,2,1,0:T(8,128)(2,1)}, u32[]{:S(2)}, u32[]{:S(2)}) collective-permute-start(bf16[2,4,16,2176]{3,2,1,0:T(8,128)(2,1)} %get-tuple-element.20), channel_id=1, source_target_pairs={{0,1},{1,0},{2,3},{3,2},{4,5},{5,4},{6,7},{7,6},{8,9},{9,8},{10,11... | collective-permute-start | bytes 1671176 | tf_op jit(solution)/shard_map/ppermute | solution.py:30
  67.9 2.8 %collective-permute-start.24 = (bf16[2,4,16,2176]{3,2,1,0:T(8,128)(2,1)}, bf16[2,4,16,2176]{3,2,1,0:T(8,128)(2,1)}, u32[]{:S(2)}, u32[]{:S(2)}) collective-permute-start(bf16[2,4,16,2176]{3,2,1,0:T(8,128)(2,1)} %get-tuple-element.22), channel_id=1, source_target_pairs={{0,1},{1,0},{2,3},{3,2},{4,5},{5,4},{6,7},{7,6},{8,9},{9,8},{10,11... | collective-permute-start | bytes 1671176 | tf_op jit(solution)/shard_map/ppermute | solution.py:30
  115.8 31.6 %collective-permute-start.5 = (bf16[2,4,16,2048]{3,2,1,0:T(8,128)(2,1)}, bf16[2,4,16,2048]{3,2,1,0:T(8,128)(2,1)}, u32[]{:S(2)}, u32[]{:S(2)}) collective-permute-start(bf16[2,4,16,2048]{3,2,1,0:T(8,128)(2,1)} %bitcast.15), channel_id=1, source_target_pairs={{0,1},{1,0},{2,3},{3,2},{4,5},{5,4},{6,7},{7,6},{8,9},{9,8},{10,11... | collective-permute-start | bytes 1572872 | tf_op jit(solution)/shard_map/ppermute | solution.py:30
  146.9 3.5 %collective-permute-start.15 = (bf16[2,4,16,2048]{3,2,1,0:T(8,128)(2,1)S(1)}, bf16[2,4,16,2048]{3,2,1,0:T(8,128)(2,1)S(1)}, u32[]{:S(2)}, u32[]{:S(2)}) collective-permute-start(bf16[2,4,16,2048]{3,2,1,0:T(8,128)(2,1)S(1)} %bitcast.209), channel_id=1, source_target_pairs={{0,1},{1,0},{2,3},{3,2},{4,5},{5,4},{6,7},{7,6},{8,9},{9,8},{10,11... | collective-permute-start | bytes 1572872 | tf_op jit(solution)/shard_map/ppermute | solution.py:30
  146.9 4.2 %collective-permute-start.25 = (bf16[2,4,16,2048]{3,2,1,0:T(8,128)(2,1)S(1)}, bf16[2,4,16,2048]{3,2,1,0:T(8,128)(2,1)S(1)}, u32[]{:S(2)}, u32[]{:S(2)}) collective-permute-start(bf16[2,4,16,2048]{3,2,1,0:T(8,128)(2,1)S(1)} %bitcast.208), channel_id=1, source_target_pairs={{0,1},{1,0},{2,3},{3,2},{4,5},{5,4},{6,7},{7,6},{8,9},{9,8},{10,11... | collective-permute-start | bytes 1572872 | tf_op jit(solution)/shard_map/ppermute | solution.py:30
  148.8 9.2 %collective-permute-start.6 = (bf16[4,16,2048]{2,1,0:T(8,128)(2,1)S(1)}, bf16[4,16,2048]{2,1,0:T(8,128)(2,1)S(1)}, u32[]{:S(2)}, u32[]{:S(2)}) collective-permute-start(bf16[4,16,2048]{2,1,0:T(8,128)(2,1)S(1)} %fusion.79), channel_id=1, source_target_pairs={{0,2},{1,3},{2,0},{3,1},{4,6},{5,7},{6,4},{7,5},{8,10},{9,11},{10,... | collective-permute-start | bytes 786440 | tf_op jit(solution)/shard_map/ppermute | solution.py:30
  150.5 15.1 %collective-permute-start.16 = (bf16[4,16,2048]{2,1,0:T(8,128)(2,1)S(1)}, bf16[4,16,2048]{2,1,0:T(8,128)(2,1)S(1)}, u32[]{:S(2)}, u32[]{:S(2)}) collective-permute-start(bf16[4,16,2048]{2,1,0:T(8,128)(2,1)S(1)} %fusion.80), channel_id=1, source_target_pairs={{0,2},{1,3},{2,0},{3,1},{4,6},{5,7},{6,4},{7,5},{8,10},{9,11},{10,... | collective-permute-start | bytes 786440 | tf_op jit(solution)/shard_map/ppermute | solution.py:30
  151.7 17.8 %collective-permute-start.26 = (bf16[4,16,2048]{2,1,0:T(8,128)(2,1)S(1)}, bf16[4,16,2048]{2,1,0:T(8,128)(2,1)S(1)}, u32[]{:S(2)}, u32[]{:S(2)}) collective-permute-start(bf16[4,16,2048]{2,1,0:T(8,128)(2,1)S(1)} %fusion.81), channel_id=1, source_target_pairs={{0,2},{1,3},{2,0},{3,1},{4,6},{5,7},{6,4},{7,5},{8,10},{9,11},{10,... | collective-permute-start | bytes 786440 | tf_op jit(solution)/shard_map/ppermute | solution.py:30
  158.1 15.2 %collective-permute-start.7 = (bf16[16,2048]{1,0:T(8,128)(2,1)S(1)}, bf16[16,2048]{1,0:T(8,128)(2,1)S(1)}, u32[]{:S(2)}, u32[]{:S(2)}) collective-permute-start(bf16[16,2048]{1,0:T(8,128)(2,1)S(1)} %get-tuple-element.29), channel_id=1, source_target_pairs={{0,12},{1,13},{2,14},{3,15},{4,0},{5,1},{6,2},{7,3},{8,4},{9,5},{1... | collective-permute-start | bytes 196616 | tf_op jit(solution)/shard_map/ppermute | solution.py:30
  161.1 13.3 %collective-permute-start.8 = (bf16[16,2048]{1,0:T(8,128)(2,1)S(1)}, bf16[16,2048]{1,0:T(8,128)(2,1)S(1)}, u32[]{:S(2)}, u32[]{:S(2)}) collective-permute-start(bf16[16,2048]{1,0:T(8,128)(2,1)S(1)} %get-tuple-element.31), channel_id=1, source_target_pairs={{0,8},{1,9},{2,10},{3,11},{4,12},{5,13},{6,14},{7,15},{8,0},{9,1},... | collective-permute-start | bytes 196616 | tf_op jit(solution)/shard_map/ppermute | solution.py:30
  165.6 11.6 %collective-permute-start.9 = (bf16[16,2048]{1,0:T(8,128)(2,1)S(1)}, bf16[16,2048]{1,0:T(8,128)(2,1)S(1)}, u32[]{:S(2)}, u32[]{:S(2)}) collective-permute-start(bf16[16,2048]{1,0:T(8,128)(2,1)S(1)} %get-tuple-element.30), channel_id=1, source_target_pairs={{0,4},{1,5},{2,6},{3,7},{4,8},{5,9},{6,10},{7,11},{8,12},{9,13},{1... | collective-permute-start | bytes 196616 | tf_op jit(solution)/shard_map/ppermute | solution.py:30
  165.7 11.8 %collective-permute-start.17 = (bf16[16,2048]{1,0:T(8,128)(2,1)S(1)}, bf16[16,2048]{1,0:T(8,128)(2,1)S(1)}, u32[]{:S(2)}, u32[]{:S(2)}) collective-permute-start(bf16[16,2048]{1,0:T(8,128)(2,1)S(1)} %get-tuple-element.32), channel_id=1, source_target_pairs={{0,12},{1,13},{2,14},{3,15},{4,0},{5,1},{6,2},{7,3},{8,4},{9,5},{1... | collective-permute-start | bytes 196616 | tf_op jit(solution)/shard_map/ppermute | solution.py:30
  169.6 9.9 %collective-permute-start.18 = (bf16[16,2048]{1,0:T(8,128)(2,1)S(1)}, bf16[16,2048]{1,0:T(8,128)(2,1)S(1)}, u32[]{:S(2)}, u32[]{:S(2)}) collective-permute-start(bf16[16,2048]{1,0:T(8,128)(2,1)S(1)} %get-tuple-element.34), channel_id=1, source_target_pairs={{0,8},{1,9},{2,10},{3,11},{4,12},{5,13},{6,14},{7,15},{8,0},{9,1},... | collective-permute-start | bytes 196616 | tf_op jit(solution)/shard_map/ppermute | solution.py:30
  173.3 7.6 %collective-permute-start.19 = (bf16[16,2048]{1,0:T(8,128)(2,1)S(1)}, bf16[16,2048]{1,0:T(8,128)(2,1)S(1)}, u32[]{:S(2)}, u32[]{:S(2)}) collective-permute-start(bf16[16,2048]{1,0:T(8,128)(2,1)S(1)} %get-tuple-element.33), channel_id=1, source_target_pairs={{0,4},{1,5},{2,6},{3,7},{4,8},{5,9},{6,10},{7,11},{8,12},{9,13},{1... | collective-permute-start | bytes 196616 | tf_op jit(solution)/shard_map/ppermute | solution.py:30
  174.4 6.6 %collective-permute-start.27 = (bf16[16,2048]{1,0:T(8,128)(2,1)S(1)}, bf16[16,2048]{1,0:T(8,128)(2,1)S(1)}, u32[]{:S(2)}, u32[]{:S(2)}) collective-permute-start(bf16[16,2048]{1,0:T(8,128)(2,1)S(1)} %get-tuple-element.35), channel_id=1, source_target_pairs={{0,12},{1,13},{2,14},{3,15},{4,0},{5,1},{6,2},{7,3},{8,4},{9,5},{1... | collective-permute-start | bytes 196616 | tf_op jit(solution)/shard_map/ppermute | solution.py:30
  177.2 7.6 %collective-permute-start.28 = (bf16[16,2048]{1,0:T(8,128)(2,1)S(1)}, bf16[16,2048]{1,0:T(8,128)(2,1)S(1)}, u32[]{:S(2)}, u32[]{:S(2)}) collective-permute-start(bf16[16,2048]{1,0:T(8,128)(2,1)S(1)} %get-tuple-element.37), channel_id=1, source_target_pairs={{0,8},{1,9},{2,10},{3,11},{4,12},{5,13},{6,14},{7,15},{8,0},{9,1},... | collective-permute-start | bytes 196616 | tf_op jit(solution)/shard_map/ppermute | solution.py:30
  177.5 7.4 %collective-permute-start.29 = (bf16[16,2048]{1,0:T(8,128)(2,1)S(1)}, bf16[16,2048]{1,0:T(8,128)(2,1)S(1)}, u32[]{:S(2)}, u32[]{:S(2)}) collective-permute-start(bf16[16,2048]{1,0:T(8,128)(2,1)S(1)} %get-tuple-element.36), channel_id=1, source_target_pairs={{0,4},{1,5},{2,6},{3,7},{4,8},{5,9},{6,10},{7,11},{8,12},{9,13},{1... | collective-permute-start | bytes 196616 | tf_op jit(solution)/shard_map/ppermute | solution.py:30
  (19 other events, 49.0 us)

commit v3 on v0

--- a/solution.py
+++ b/solution.py
@@ -1,9 +1,317 @@
+import functools
+
 import jax
 import jax.numpy as jnp
 from jax import lax
+from jax.experimental import pallas as pl
+from jax.experimental.pallas import tpu as pltpu
 from jax.sharding import PartitionSpec as P
 
 adapter_scale = 2.0
+LANES = 128
+
+
+def route_gates(logits):
+    highest = jnp.max(logits, axis=-1, keepdims=True)
+    router_scores = jnp.exp(logits - highest)
+    return (router_scores / jnp.sum(router_scores, axis=-1, keepdims=True)).astype(jnp.bfloat16)
+
+
+def split_axis(n):
+    cores = 2 if n % 2 == 0 else 1
+    chips = n // cores
+    middle = 1
+    while chips % (2 * middle) == 0 and 4 * middle * middle <= chips:
+        middle *= 2
+    return chips // middle, middle, cores
+
+
+def shift(x, n, stride, size, k):
+    pairs = []
+    for i in range(n):
+        place = i // stride % size
+        pairs.append((i, i + ((place + k) % size - place) * stride))
+    return lax.ppermute(x, "expert", pairs)
+
+
+def gather_rows(x, n):
+    outer, middle, cores = split_axis(n)
+    column = [x] + [shift(x, n, middle * cores, outer, k) for k in range(1, outer)]
+    column = jnp.concatenate(column, axis=0)
+    sheet = [column] + [shift(column, n, cores, middle, k) for k in range(1, middle)]
+    return sheet + [shift(p, n, 1, cores, k) for k in range(1, cores) for p in sheet]
+
+
+def scatter_rows(kept, sent, n):
+    outer, middle, cores = split_axis(n)
+    count, width = kept.shape
+    if cores > 1:
+        kept = kept + shift(sent, n, 1, cores, 1).astype(jnp.float32)
+    for stride, size in ((cores, middle), (middle * cores, outer)):
+        count //= size
+        total = kept[:count]
+        for k in range(1, size):
+            part = kept[k * count : (k + 1) * count].astype(jnp.bfloat16)
+            total = total + shift(part, n, stride, size, size - k).astype(jnp.float32)
+        kept = total
+    return kept.astype(jnp.bfloat16)
+
+
+def dot(a, b):
+    return jnp.dot(a, b, preferred_element_type=jnp.float32)
+
+
+def payload_kernel(hidden_ref, ids_ref, logits_ref, *out_refs):
+    rows, width = out_refs[0].shape[0], hidden_ref.shape[1]
+    padded = out_refs[0].shape[1] - width
+    gates = route_gates(logits_ref[...]).astype(jnp.float32)
+    ids = ids_ref[...]
+    lane = lax.broadcasted_iota(jnp.int32, (ids.shape[0], padded), 1)
+    dense = jnp.zeros(lane.shape, jnp.float32)
+    for k in range(ids.shape[1]):
+        dense += jnp.where(ids[:, k : k + 1] == lane, gates[:, k : k + 1], 0.0)
+    dense = dense.astype(jnp.bfloat16)
+    for s, out_ref in enumerate(out_refs):
+        out_ref[:, :width] = hidden_ref[s * rows : (s + 1) * rows, :]
+        out_ref[:, width:] = dense[s * rows : (s + 1) * rows, :]
+
+
+def make_payload(hidden, route_ids, route_logits, experts):
+    steps, rows, width = hidden.shape
+    padded = -(-experts // LANES) * LANES
+    shape = jax.ShapeDtypeStruct((rows, width + padded), jnp.bfloat16)
+    return pl.pallas_call(
+        payload_kernel,
+        out_shape=[shape] * steps,
+        name="payload",
+    )(
+        hidden.reshape(steps * rows, width),
+        route_ids.reshape(steps * rows, -1),
+        route_logits.reshape(steps * rows, -1),
+    )
+
+
+def order_kernel(placement_ref, factors_ref, out_ref, wide_ref):
+    slots, length, lanes = out_ref.shape
+
+    def cut(t, carry):
+        start = pl.multiple_of(t * lanes, lanes)
+        tile = factors_ref[:, pl.ds(start, lanes)].astype(jnp.float32)
+        wide_ref[pl.ds(t, slots, stride=length), :] = tile
+        return carry
+
+    lax.fori_loop(0, length, cut, 0, unroll=8)
+    for s in range(slots):
+        out_ref[placement_ref[s]] = wide_ref[s * length : (s + 1) * length, :].astype(jnp.bfloat16)
+
+
+def order_factors(placement, factors):
+    slots, entries = factors.shape
+    length = entries // LANES
+    return pl.pallas_call(
+        order_kernel,
+        out_shape=jax.ShapeDtypeStruct((slots, length, LANES), jnp.bfloat16),
+        in_specs=[
+            pl.BlockSpec(memory_space=pltpu.SMEM),
+            pl.BlockSpec(memory_space=pltpu.VMEM),
+        ],
+        scratch_shapes=[pltpu.VMEM((slots * length, LANES), jnp.float32)],
+        compiler_params=pltpu.CompilerParams(vmem_limit_bytes=12 << 20),
+        name="order_factors",
+    )(placement, factors)
+
+
+def relayout_kernel(flat_ref, a_gu_ref, gate_b_ref, up_b_ref, down_a_ref, down_b_ref, wide_ref):
+    width, units = a_gu_ref.shape[0], gate_b_ref.shape[1]
+    rank = gate_b_ref.shape[0]
+    n_wide, n_unit = width // 2, units // 2
+    at_ub = 2 * n_wide + n_unit
+    at_da = 2 * n_wide + 2 * n_unit
+    chunk = 128
+    left = lax.broadcasted_iota(jnp.int32, (chunk, LANES), 1) < rank
+
+    def load(start):
+        return flat_ref[pl.ds(pl.multiple_of(start, 128), chunk), :].astype(jnp.float32)
+
+    def gate_up(i, carry):
+        g, u = load(i * chunk), load(n_wide + n_unit + i * chunk)
+        at = 2 * i * chunk
+        wide_ref[pl.ds(at, chunk, stride=2), :] = jnp.where(left, g, pltpu.roll(u, rank, 1))
+        wide_ref[pl.ds(at + 1, chunk, stride=2), :] = jnp.where(left, pltpu.roll(g, rank, 1), u)
+        both = wide_ref[pl.ds(pl.multiple_of(at, 128), 2 * chunk), :]
+        a_gu_ref[pl.ds(pl.multiple_of(at, 128), 2 * chunk), :] = both.astype(jnp.bfloat16)
+        return carry
+
+    lax.fori_loop(0, n_wide // chunk, gate_up, 0, unroll=2)
+    for i in range(n_unit // chunk):
+        d = load(at_da + i * chunk)
+        at = 2 * i * chunk
+        wide_ref[pl.ds(at, chunk, stride=2), :] = jnp.where(left, d, 0.0)
+        wide_ref[pl.ds(at + 1, chunk, stride=2), :] = jnp.where(left, pltpu.roll(d, rank, 1), 0.0)
+        down_a_ref[at : at + 2 * chunk, :] = wide_ref[at : at + 2 * chunk, :].astype(jnp.bfloat16)
+    for start, b_ref in (
+        (n_wide, gate_b_ref),
+        (at_ub, up_b_ref),
+        (at_da + n_unit, down_b_ref),
+    ):
+        tiles = b_ref.shape[1] // LANES
+        count = rank * tiles
+        wide_ref[:count, :] = flat_ref[start : start + count, :].astype(jnp.float32)
+        for j in range(tiles):
+            row = wide_ref[pl.ds(j, rank, stride=tiles), :]
+            b_ref[:, j * LANES : (j + 1) * LANES] = row.astype(jnp.bfloat16)
+
+
+def relayout_factors(flat, width, units, rank):
+    shapes = [(width, 2 * rank), (rank, units), (rank, units), (units, 2 * rank), (rank, width)]
+    return pl.pallas_call(
+        relayout_kernel,
+        out_shape=[jax.ShapeDtypeStruct(shape, jnp.bfloat16) for shape in shapes],
+        scratch_shapes=[pltpu.VMEM((max(width, rank * width // LANES), LANES), jnp.float32)],
+        compiler_params=pltpu.CompilerParams(vmem_limit_bytes=12 << 20),
+        name="relayout_factors",
+    )(flat)
+
+
+def fill_rows(pieces, x_ref):
+    rows, width = pieces[0].shape[0], x_ref.shape[1]
+    for i, piece in enumerate(pieces):
+        x_ref[i * rows : (i + 1) * rows, :] = piece[:, :width]
+
+
+def base_kernel(count, *refs):
+    pieces = refs[:count]
+    w_gate_ref, w_up_ref, gate_ref, up_ref, x_ref = refs[count:]
+
+    @pl.when(pl.program_id(0) == 0)
+    def _():
+        fill_rows(pieces, x_ref)
+
+    gate_ref[...] = dot(x_ref[...], w_gate_ref[...])
+    up_ref[...] = dot(x_ref[...], w_up_ref[...])
+
+
+def base_products(pieces, w_gate, w_up):
+    width, units = w_gate.shape
+    total = sum(p.shape[0] for p in pieces)
+    block = 256 if units % 256 == 0 else units
+    out = jax.ShapeDtypeStruct((total, units), jnp.float32)
+    return pl.pallas_call(
+        functools.partial(base_kernel, len(pieces)),
+        grid=(units // block,),
+        out_shape=[out, out],
+        in_specs=[pl.BlockSpec(p.shape, lambda i: (0, 0)) for p in pieces]
+        + [pl.BlockSpec((width, block), lambda i: (0, i))] * 2,
+        out_specs=[pl.BlockSpec((total, block), lambda i: (0, i))] * 2,
+        scratch_shapes=[pltpu.VMEM((total, width), jnp.bfloat16)],
+        compiler_params=pltpu.CompilerParams(vmem_limit_bytes=24 << 20),
+        cost_estimate=pl.CostEstimate(
+            flops=4 * total * width * units,
+            bytes_accessed=4 * width * units + 2 * total * width + 8 * total * units,
+            transcendentals=0,
+        ),
+        name="base_products",
+    )(*pieces, w_gate, w_up)
+
+
+def finish_kernel(count, me_ref, *refs):
+    pieces = refs[:count]
+    (gate_ref, up_ref, a_gu_ref, gate_b_ref, up_b_ref, down_a_ref, down_b_ref, w_down_ref) = refs[
+        count : count + 8
+    ]
+    out_refs = refs[count + 8 : -4]
+    x_ref, inner_ref, low_ref, mine_ref = refs[-4:]
+    rank = gate_b_ref.shape[0]
+    rows, width = pieces[0].shape[0], x_ref.shape[1]
+
+    @pl.when(pl.program_id(0) == 0)
+    def _():
+        fill_rows(pieces, x_ref)
+        for i, piece in enumerate(pieces):
+            gates = piece[:, width:].astype(jnp.float32)
+            lane = lax.broadcasted_iota(jnp.int32, gates.shape, 1)
+            own = jnp.sum(jnp.where(lane == me_ref[0], gates, 0.0), axis=1, keepdims=True)
+            mine_ref[i * rows : (i + 1) * rows, :] = jnp.broadcast_to(own, (rows, LANES))
+        low = (adapter_scale * dot(x_ref[...], a_gu_ref[...])).astype(jnp.bfloat16)
+        g = gate_ref[...] + dot(low[:, :rank], gate_b_ref[...])
+        u = up_ref[...] + dot(low[:, rank:], up_b_ref[...])
+        inner = (g / (1.0 + jnp.exp(-g)) * u).astype(jnp.bfloat16)
+        inner_ref[...] = inner
+        low_ref[...] = (adapter_scale * dot(inner, down_a_ref[...])).astype(jnp.bfloat16)
+
+    out = dot(inner_ref[...], w_down_ref[...]) + dot(low_ref[:, :rank], down_b_ref[...])
+    out = out * mine_ref[:, :1]
+    at = 0
+    for out_ref in out_refs:
+        n = out_ref.shape[0]
+        out_ref[...] = out[at : at + n].astype(out_ref.dtype)
+        at += n
+
+
+def finish_step(me, pieces, gate, up, low_rank, w_down, cores):
+    units, width = w_down.shape
+    total = gate.shape[0]
+    block = 512 if width % 512 == 0 else width
+    own = total // cores
+    outs = [jax.ShapeDtypeStruct((own, width), jnp.float32)]
+    if cores > 1:
+        outs.append(jax.ShapeDtypeStruct((total - own, width), jnp.bfloat16))
+    a_gu, gate_b, up_b, down_a, down_b = low_rank
+    rank = down_b.shape[0]
+    whole = [*pieces, gate, up, a_gu, gate_b, up_b, down_a]
+    return pl.pallas_call(
+        functools.partial(finish_kernel, len(pieces)),
+        grid=(width // block,),
+        out_shape=outs,
+        in_specs=[pl.BlockSpec(memory_space=pltpu.SMEM)]
+        + [pl.BlockSpec(a.shape, lambda i: (0, 0)) for a in whole]
+        + [
+            pl.BlockSpec((rank, block), lambda i: (0, i)),
+            pl.BlockSpec((units, block), lambda i: (0, i)),
+        ],
+        out_specs=[pl.BlockSpec((o.shape[0], block), lambda i: (0, i)) for o in outs],
+        scratch_shapes=[
+            pltpu.VMEM((total, width), jnp.bfloat16),
+            pltpu.VMEM((total, units), jnp.bfloat16),
+            pltpu.VMEM((total, down_a.shape[1]), jnp.bfloat16),
+            pltpu.VMEM((total, LANES), jnp.float32),
+        ],
+        compiler_params=pltpu.CompilerParams(vmem_limit_bytes=28 << 20),
+        cost_estimate=pl.CostEstimate(
+            flops=2 * total * units * (width + 4 * rank) + 4 * total * width * rank,
+            bytes_accessed=2 * units * width + 8 * total * width + 8 * total * units,
+            transcendentals=total * units,
+        ),
+        name="finish_step",
+    )(me, *whole, down_b, w_down)
+
+
+def dense_shards(
+    hidden, route_ids, route_logits, placement, factors, w_gate, w_up, down_weight
+):
+    owners = lax.axis_size("expert")
+    experts = placement.shape[0]
+    steps, rows, width = hidden.shape
+    units = w_gate.shape[2]
+    rank = factors.shape[1] * owners // (3 * (width + units))
+    cores = split_axis(owners)[2]
+
+    payload = make_payload(hidden, route_ids, route_logits, experts)
+    gathered = [gather_rows(payload[s], owners) for s in range(steps)]
+    ordered = order_factors(placement, factors)
+    received = lax.all_to_all(ordered, "expert", split_axis=0, concat_axis=0, tiled=True)
+    base = [base_products(pieces, w_gate[0], w_up[0]) for pieces in gathered]
+    low_rank = relayout_factors(received.reshape(-1, LANES), width, units, rank)
+    me = lax.axis_index("expert").reshape(1)
+    results = []
+    for pieces, (gate, up) in zip(gathered, base):
+        parts = finish_step(me, pieces, gate, up, low_rank, down_weight[0], cores)
+        results.append(scatter_rows(parts[0], parts[-1], owners))
+    return jnp.stack(results, axis=0)
+
+
+def row_capacity(rows, top, experts):
+    return min(rows, 3 * max(1, rows * top // experts))
 
 
 def unpack_factors(flat_factors, width, hidden_units, rank_size):
@@ -39,20 +347,14 @@
     )
 
 
-def route_gates(logits):
-    highest = jnp.max(logits, axis=-1, keepdims=True)
-    router_scores = jnp.exp(logits - highest)
-    return (router_scores / jnp.sum(router_scores, axis=-1, keepdims=True)).astype(jnp.bfloat16)
-
-
-def shards(hidden, route_ids, route_logits, placement, factors, w_gate, w_up, down_weight):
+def sparse_shards(hidden, route_ids, route_logits, placement, factors, w_gate, w_up, down_weight):
     owners = lax.axis_size("expert")
     experts = placement.shape[0]
     steps_count, row_count, width = hidden.shape
     top_count = route_ids.shape[2]
     hidden_units = w_gate.shape[2]
     rank_size = factors.shape[1] * owners // (3 * (width + hidden_units))
-    capacity = min(row_count, 3 * max(1, row_count * top_count // experts))
+    capacity = row_capacity(row_count, top_count, experts)
     slot_of = (
         jnp.zeros((experts,), jnp.int32).at[placement].set(jnp.arange(experts, dtype=jnp.int32))
     )
@@ -100,6 +402,13 @@
     return jnp.stack(results, axis=0)
 
 
+def shards(hidden, route_ids, *rest):
+    rows, top = route_ids.shape[1:]
+    experts = rest[1].shape[0]
+    every = row_capacity(rows, top, experts) == rows
+    return (dense_shards if every else sparse_shards)(hidden, route_ids, *rest)
+
+
 def solution(mesh):
     placed = (
         P(None, ("group", "expert"), None),

time: 219 us -> 139 us (0.63)
  waiting for transfers between devices: 92.3 us -> 29.5 us
  matrix products: 49.3 us -> 0 us
  Pallas kernels: 0 us -> 29.7 us
  other arithmetic: 11.3 us -> 1.3 us
  local copies, waits for them, and re-layouts: 15 us -> 23.3 us
  starting transfers between devices: 48.3 us -> 54.1 us
    all_to_all x7 -> x1, waiting for transfers between devices: 92.3 us -> 0.01 us  [dense_shards(): lax.all_to_all(ordered, 'expert', split_axis=0, concat_axis=0, tiled=True)]
    dot_general x15 -> x0, matrix products: 49.3 us -> none  [the longest x3 19.1 us: apply_expert_block(): jnp.dot(inner, combined_down_weight, preferred_element_type=jnp.float32)]
    ppermute x0 -> x33, starting transfers between devices: none -> 48.4 us  [shift(): return lax.ppermute(x, 'expert', pairs)]
    all_to_all x7 -> x1, starting transfers between devices: 48.3 us -> 5.76 us  [dense_shards(): lax.all_to_all(ordered, 'expert', split_axis=0, concat_axis=0, tiled=True)]
    pallas_call x0 -> x9, Pallas kernels: none -> 29.7 us  [the longest x3 12.8 us: finish_step(): pl.pallas_call(functools.partial(finish_kernel, len(pieces)), grid=(width...]
    ppermute x0 -> x33, waiting for transfers between devices: none -> 29.5 us  [shift(): return lax.ppermute(x, 'expert', pairs)]
    unnamed x19 -> x41, local copies, waits for them, and re-layouts: 5.15 us -> 21 us
    all_to_all x1 -> x0, other arithmetic: 7.59 us -> none  [shards(): lax.all_to_all(ordered, 'expert', split_axis=0, concat_axis=1, tiled=True)]
  transfers between devices with their start and end apart: 7 -> 34, of which waited for: 6 -> 7; matrix products, arithmetic and copies ran while one was open for 32% -> 7% of each run, Pallas kernels for 0% -> 20%
where the time goes in v3:
time: 139 us; the launch traced here: 138 us
  starting transfers between devices  54.1 us (39%)
  Pallas kernels  29.7 us (21%)
  waiting for transfers between devices  29.5 us (21%)
  local copies, waits for them, and re-layouts  23.3 us (17%)
    ppermute x33, starting transfers between devices, shift(): return lax.ppermute(x, 'expert', pairs)  48.4 us
    ppermute x33, waiting for transfers between devices, shift(): return lax.ppermute(x, 'expert', pairs)  29.5 us
    unnamed x41, local copies, waits for them, and re-layouts  21 us
    pallas_call x3, Pallas kernels, finish_step(): pl.pallas_call(functools.partial(finish_kernel, len(pieces)), grid=(width...  12.8 us
    pallas_call x3, Pallas kernels, base_products(): pl.pallas_call(functools.partial(base_kernel, len(pieces)), grid=(units /...  11.6 us
    all_to_all x1, starting transfers between devices, dense_shards(): lax.all_to_all(ordered, 'expert', split_axis=0, concat_axis=0, tiled=True)  5.76 us
  transfers between devices with their start and end apart: 34, of which 7 were waited for; matrix products, arithmetic and copies ran while one was open for 7% of the time, Pallas kernels for 20%

profile of v3, /device:TPU:0, one launch (start us, length us, event | category | flops | bytes accessed | tf_op | source)
XLA Modules:
  0.0 138.3 jit_solution(4325337779870009372)
XLA Ops:
  1.4 1.5 %copy.10 = f32[3,16,8]{2,1,0:T(8,128)} copy(f32[3,16,8]{1,2,0:T(8,128)} %param.10) | data formatting | bytes 3072 | tf_op args[2]
  2.9 1.9 %payload.1 = (bf16[16,2176]{1,0:T(8,128)(2,1)}, bf16[16,2176]{1,0:T(8,128)(2,1)}, bf16[16,2176]{1,0:T(8,128)(2,1)}) custom-call(bf16[48,2048]{1,0:T(8,128)(2,1)} %bitcast.23, s32[48,8]{1,0:T(8,128)} %bitcast.24, f32[48,8]{1,0:T(8,128)} %bitcast.25), custom_call_target="tpu_custom_call" | custom-call | tf_op jit(solution)/shard_map/payload/pallas_call | solution.py:83
  4.8 3.0 %collective-permute-start = (bf16[16,2176]{1,0:T(8,128)(2,1)}, bf16[16,2176]{1,0:T(8,128)(2,1)}, u32[]{:S(2)}, u32[]{:S(2)}) collective-permute-start(bf16[16,2176]{1,0:T(8,128)(2,1)} %get-tuple-element.25), channel_id=1, source_target_pairs={{0,4},{1,5},{2,6},{3,7},{4,8},{5,9},{6,10},{7,11},{8,12},{9,13},{1... | collective-permute-start | bytes 208904 | tf_op jit(solution)/shard_map/ppermute | solution.py:34
  7.9 2.6 %collective-permute-start.1 = (bf16[16,2176]{1,0:T(8,128)(2,1)}, bf16[16,2176]{1,0:T(8,128)(2,1)}, u32[]{:S(2)}, u32[]{:S(2)}) collective-permute-start(bf16[16,2176]{1,0:T(8,128)(2,1)} %get-tuple-element.25), channel_id=1, source_target_pairs={{0,8},{1,9},{2,10},{3,11},{4,12},{5,13},{6,14},{7,15},{8,0},{9,1},... | collective-permute-start | bytes 208904 | tf_op jit(solution)/shard_map/ppermute | solution.py:34
  17.1 5.8 %all-to-all-start = ((bf16[16,264,128]{2,1,0:T(8,128)(2,1)}), bf16[16,264,128]{2,1,0:T(8,128)(2,1)}, u32[]{:S(2)}, u32[]{:S(2)}) async-start(bf16[16,264,128]{2,1,0:T(8,128)(2,1)} %copy-done.5), calls=%async_computation | async-start | bytes 2162688 | tf_op jit(solution)/shard_map/all_to_all | solution.py:302
  24.1 3.7 %collective-permute-start.13 = (bf16[16,2176]{1,0:T(8,128)(2,1)}, bf16[16,2176]{1,0:T(8,128)(2,1)S(1)}, u32[]{:S(2)}, u32[]{:S(2)}) collective-permute-start(bf16[16,2176]{1,0:T(8,128)(2,1)} %get-tuple-element.35), channel_id=1, source_target_pairs={{0,12},{1,13},{2,14},{3,15},{4,0},{5,1},{6,2},{7,3},{8,4},{9,5},{1... | collective-permute-start | bytes 208904 | tf_op jit(solution)/shard_map/ppermute | solution.py:34
  33.5 2.7 %collective-permute-start.24 = (bf16[16,2176]{1,0:T(8,128)(2,1)S(1)}, bf16[16,2176]{1,0:T(8,128)(2,1)S(1)}, u32[]{:S(2)}, u32[]{:S(2)}) collective-permute-start(bf16[16,2176]{1,0:T(8,128)(2,1)S(1)} %copy-done.12), channel_id=1, source_target_pairs={{0,12},{1,13},{2,14},{3,15},{4,0},{5,1},{6,2},{7,3},{8,4},{9,5},{1... | collective-permute-start | bytes 208904 | tf_op jit(solution)/shard_map/ppermute | solution.py:34
  39.2 1.5 %constant_dynamic-update-slice_fusion.5 = bf16[64,2176]{1,0:T(8,128)(2,1)} fusion(bf16[64,2176]{1,0:T(8,128)(2,1)} %constant_dynamic-update-slice_fusion.6, bf16[16,2176]{1,0:T(8,128)(2,1)} %collective-permute-done.12), kind=kLoop, calls=%fused_computation.30 | loop fusion | bytes 139264
  40.7 2.4 %collective-permute-done.13 = bf16[16,2176]{1,0:T(8,128)(2,1)S(1)} collective-permute-done((bf16[16,2176]{1,0:T(8,128)(2,1)}, bf16[16,2176]{1,0:T(8,128)(2,1)S(1)}, u32[]{:S(2)}, u32[]{:S(2)}) %collective-permute-start.13) | collective-permute-done | bytes 69664 | tf_op jit(solution)/shard_map/ppermute | solution.py:34
  43.8 5.0 %collective-permute-done.22 = bf16[16,2176]{1,0:T(8,128)(2,1)S(1)} collective-permute-done((bf16[16,2176]{1,0:T(8,128)(2,1)S(1)}, bf16[16,2176]{1,0:T(8,128)(2,1)S(1)}, u32[]{:S(2)}, u32[]{:S(2)}) %collective-permute-start.22) | collective-permute-done | bytes 69664 | tf_op jit(solution)/shard_map/ppermute | solution.py:34
  50.3 6.2 %collective-permute-done.23 = bf16[16,2176]{1,0:T(8,128)(2,1)S(1)} collective-permute-done((bf16[16,2176]{1,0:T(8,128)(2,1)S(1)}, bf16[16,2176]{1,0:T(8,128)(2,1)S(1)}, u32[]{:S(2)}, u32[]{:S(2)}) %collective-permute-start.23) | collective-permute-done | bytes 69664 | tf_op jit(solution)/shard_map/ppermute | solution.py:34
  56.5 1.6 %collective-permute-start.25 = (bf16[64,2176]{1,0:T(8,128)(2,1)S(1)}, bf16[64,2176]{1,0:T(8,128)(2,1)}, u32[]{:S(2)}, u32[]{:S(2)}) collective-permute-start(bf16[64,2176]{1,0:T(8,128)(2,1)S(1)} %constant_dynamic-update-slice_fusion.8.refs_0_), channel_id=1, source_target_pairs={{0,2},{1,3},{2,0},{3,1},{4,6},{5,7},{6,4},{7,5},{8,10},{9,11},{10,... | collective-permute-start | bytes 835592 | tf_op jit(solution)/shard_map/ppermute | solution.py:34
  59.2 5.3 %collective-permute-done.25.refs_1_ = bf16[64,2176]{1,0:T(8,128)(2,1)} collective-permute-done((bf16[64,2176]{1,0:T(8,128)(2,1)S(1)}, bf16[64,2176]{1,0:T(8,128)(2,1)}, u32[]{:S(2)}, u32[]{:S(2)}) %collective-permute-start.25) | collective-permute-done | bytes 278560 | tf_op jit(solution)/shard_map/ppermute | solution.py:34
  64.5 1.9 %copy-done.1 = bf16[1,2048,768]{2,1,0:T(8,128)(2,1)S(1)} copy-done((bf16[1,2048,768]{2,1,0:T(8,128)(2,1)S(1)}, bf16[1,2048,768]{2,1,0:T(8,128)(2,1)}, u32[]{:S(2)}) %copy-start.1) | copy-done | bytes 3145752
  66.3 3.8 %base_products.3 = (f32[256,768]{1,0:T(8,128)S(1)}, f32[256,768]{1,0:T(8,128)S(1)}) custom-call(bf16[64,2176]{1,0:T(8,128)(2,1)} %constant_dynamic-update-slice_fusion.refs_0_, bf16[64,2176]{1,0:T(8,128)(2,1)} %collective-permute-done.3.refs_1_, bf16[64,2176]{1,0:T(8,128)(2,1)} %collective-permute-done.4.refs_2_, ...), custom_call_target="tpu_custom_call" | custom-call | flops 1610612736 | bytes 8912896 | tf_op jit(solution)/shard_map/base_products/pallas_call | solution.py:199
  72.0 2.1 %relayout_factors.1 = (bf16[2048,128]{1,0:T(8,128)(2,1)S(1)}, bf16[64,768]{1,0:T(8,128)(2,1)S(1)}, bf16[64,768]{1,0:T(8,128)(2,1)S(1)}, bf16[768,128]{1,0:T(8,128)(2,1)S(1)}, bf16[64,2048]{1,0:T(8,128)(2,1)S(1)}) custom-call(bf16[4224,128]{1,0:T(8,128)(2,1)} %bitcast.6.flat_ref), custom_call_target="tpu_custom_call" | custom-call | tf_op jit(solution)/shard_map/relayout_factors/pallas_call | solution.py:167
  74.1 1.9 %copy-done.3 = bf16[1,768,2048]{2,1,0:T(8,128)(2,1)S(1)} copy-done((bf16[1,768,2048]{2,1,0:T(8,128)(2,1)S(1)}, bf16[1,768,2048]{2,1,0:T(8,128)(2,1)}, u32[]{:S(2)}) %copy-start.3) | copy-done | bytes 3145752
  78.2 4.4 %finish_step.3 = (f32[128,2048]{1,0:T(8,128)S(1)}, bf16[128,2048]{1,0:T(8,128)(2,1)S(1)}) custom-call(s32[1]{0:T(128)} %bitcast.me_ref, bf16[64,2176]{1,0:T(8,128)(2,1)} %constant_dynamic-update-slice_fusion.refs_0_, bf16[64,2176]{1,0:T(8,128)(2,1)} %collective-permute-done.3.refs_1_, bf16[64,2176]{1,0:T(8,128)(2,1)} %collective-permute-done.4.refs_2_, ...), custom_call_target="tpu_custom_call" | custom-call | flops 1040187392 | bytes 8912896 | tf_op jit(solution)/shard_map/finish_step/pallas_call | solution.py:262
  83.2 3.9 %base_products.4 = (f32[256,768]{1,0:T(8,128)S(1)}, f32[256,768]{1,0:T(8,128)S(1)}) custom-call(bf16[64,2176]{1,0:T(8,128)(2,1)} %constant_dynamic-update-slice_fusion.4.refs_0_, bf16[64,2176]{1,0:T(8,128)(2,1)} %collective-permute-done.14.refs_1_, bf16[64,2176]{1,0:T(8,128)(2,1)} %collective-permute-done.15.refs_2_, ...), custom_call_target="tpu_custom_call" | custom-call | flops 1610612736 | bytes 8912896 | tf_op jit(solution)/shard_map/base_products/pallas_call | solution.py:199
  87.1 3.9 %base_products.5 = (f32[256,768]{1,0:T(8,128)S(1)}, f32[256,768]{1,0:T(8,128)S(1)}) custom-call(bf16[64,2176]{1,0:T(8,128)(2,1)S(1)} %constant_dynamic-update-slice_fusion.8.refs_0_, bf16[64,2176]{1,0:T(8,128)(2,1)} %collective-permute-done.25.refs_1_, bf16[64,2176]{1,0:T(8,128)(2,1)} %collective-permute-done.26.refs_2_, ...), custom_call_target="tpu_custom_call" | custom-call | flops 1610612736 | bytes 8912896 | tf_op jit(solution)/shard_map/base_products/pallas_call | solution.py:199
  91.0 4.3 %finish_step.4 = (f32[128,2048]{1,0:T(8,128)S(1)}, bf16[128,2048]{1,0:T(8,128)(2,1)S(1)}) custom-call(s32[1]{0:T(128)} %bitcast.me_ref, bf16[64,2176]{1,0:T(8,128)(2,1)} %constant_dynamic-update-slice_fusion.4.refs_0_, bf16[64,2176]{1,0:T(8,128)(2,1)} %collective-permute-done.14.refs_1_, bf16[64,2176]{1,0:T(8,128)(2,1)} %collective-permute-done.15.refs_2_, ...), custom_call_target="tpu_custom_call" | custom-call | flops 1040187392 | bytes 8912896 | tf_op jit(solution)/shard_map/finish_step/pallas_call | solution.py:262
  95.4 4.2 %finish_step.5 = (f32[128,2048]{1,0:T(8,128)S(1)}, bf16[128,2048]{1,0:T(8,128)(2,1)S(1)}) custom-call(s32[1]{0:T(128)} %bitcast.me_ref, bf16[64,2176]{1,0:T(8,128)(2,1)S(1)} %constant_dynamic-update-slice_fusion.8.refs_0_, bf16[64,2176]{1,0:T(8,128)(2,1)} %collective-permute-done.25.refs_1_, bf16[64,2176]{1,0:T(8,128)(2,1)} %collective-permute-done.26.refs_2_, ...), custom_call_target="tpu_custom_call" | custom-call | flops 1040187392 | bytes 8912896 | tf_op jit(solution)/shard_map/finish_step/pallas_call | solution.py:262
  100.3 1.6 %collective-permute-start.7 = (bf16[64,2048]{1,0:T(8,128)(2,1)S(1)}, bf16[64,2048]{1,0:T(8,128)(2,1)S(1)}, u32[]{:S(2)}, u32[]{:S(2)}) collective-permute-start(bf16[64,2048]{1,0:T(8,128)(2,1)S(1)} %slice.137), channel_id=1, source_target_pairs={{0,2},{1,3},{2,0},{3,1},{4,6},{5,7},{6,4},{7,5},{8,10},{9,11},{10,... | collective-permute-start | bytes 786440 | tf_op jit(solution)/shard_map/ppermute | solution.py:34
  102.7 1.6 %collective-permute-start.29 = (bf16[64,2048]{1,0:T(8,128)(2,1)S(1)}, bf16[64,2048]{1,0:T(8,128)(2,1)S(1)}, u32[]{:S(2)}, u32[]{:S(2)}) collective-permute-start(bf16[64,2048]{1,0:T(8,128)(2,1)S(1)} %slice.135), channel_id=1, source_target_pairs={{0,2},{1,3},{2,0},{3,1},{4,6},{5,7},{6,4},{7,5},{8,10},{9,11},{10,... | collective-permute-start | bytes 786440 | tf_op jit(solution)/shard_map/ppermute | solution.py:34
  104.3 5.2 %collective-permute-done.7 = bf16[64,2048]{1,0:T(8,128)(2,1)S(1)} collective-permute-done((bf16[64,2048]{1,0:T(8,128)(2,1)S(1)}, bf16[64,2048]{1,0:T(8,128)(2,1)S(1)}, u32[]{:S(2)}, u32[]{:S(2)}) %collective-permute-start.7) | collective-permute-done | bytes 262176 | tf_op jit(solution)/shard_map/ppermute | solution.py:34
  109.6 7.2 %collective-permute-start.10 = (bf16[16,2048]{1,0:T(8,128)(2,1)S(1)}, bf16[16,2048]{1,0:T(8,128)(2,1)S(1)}, u32[]{:S(2)}, u32[]{:S(2)}) collective-permute-start(bf16[16,2048]{1,0:T(8,128)(2,1)S(1)} %get-tuple-element.52), channel_id=1, source_target_pairs={{0,4},{1,5},{2,6},{3,7},{4,8},{5,9},{6,10},{7,11},{8,12},{9,13},{1... | collective-permute-start | bytes 196616 | tf_op jit(solution)/shard_map/ppermute | solution.py:34
  116.8 1.6 %collective-permute-start.9 = (bf16[16,2048]{1,0:T(8,128)(2,1)S(1)}, bf16[16,2048]{1,0:T(8,128)(2,1)S(1)}, u32[]{:S(2)}, u32[]{:S(2)}) collective-permute-start(bf16[16,2048]{1,0:T(8,128)(2,1)S(1)} %get-tuple-element.53), channel_id=1, source_target_pairs={{0,8},{1,9},{2,10},{3,11},{4,12},{5,13},{6,14},{7,15},{8,0},{9,1},... | collective-permute-start | bytes 196616 | tf_op jit(solution)/shard_map/ppermute | solution.py:34
  118.5 2.8 %collective-permute-start.19 = (bf16[16,2048]{1,0:T(8,128)(2,1)S(1)}, bf16[16,2048]{1,0:T(8,128)(2,1)S(1)}, u32[]{:S(2)}, u32[]{:S(2)}) collective-permute-start(bf16[16,2048]{1,0:T(8,128)(2,1)S(1)} %get-tuple-element.54), channel_id=1, source_target_pairs={{0,12},{1,13},{2,14},{3,15},{4,0},{5,1},{6,2},{7,3},{8,4},{9,5},{1... | collective-permute-start | bytes 196616 | tf_op jit(solution)/shard_map/ppermute | solution.py:34
  121.3 5.2 %collective-permute-start.20 = (bf16[16,2048]{1,0:T(8,128)(2,1)S(1)}, bf16[16,2048]{1,0:T(8,128)(2,1)S(1)}, u32[]{:S(2)}, u32[]{:S(2)}) collective-permute-start(bf16[16,2048]{1,0:T(8,128)(2,1)S(1)} %get-tuple-element.56), channel_id=1, source_target_pairs={{0,8},{1,9},{2,10},{3,11},{4,12},{5,13},{6,14},{7,15},{8,0},{9,1},... | collective-permute-start | bytes 196616 | tf_op jit(solution)/shard_map/ppermute | solution.py:34
  127.1 3.4 %collective-permute-start.30 = (bf16[16,2048]{1,0:T(8,128)(2,1)S(1)}, bf16[16,2048]{1,0:T(8,128)(2,1)S(1)}, u32[]{:S(2)}, u32[]{:S(2)}) collective-permute-start(bf16[16,2048]{1,0:T(8,128)(2,1)S(1)} %get-tuple-element.57), channel_id=1, source_target_pairs={{0,12},{1,13},{2,14},{3,15},{4,0},{5,1},{6,2},{7,3},{8,4},{9,5},{1... | collective-permute-start | bytes 196616 | tf_op jit(solution)/shard_map/ppermute | solution.py:34
  130.6 1.6 %collective-permute-start.32 = (bf16[16,2048]{1,0:T(8,128)(2,1)S(1)}, bf16[16,2048]{1,0:T(8,128)(2,1)S(1)}, u32[]{:S(2)}, u32[]{:S(2)}) collective-permute-start(bf16[16,2048]{1,0:T(8,128)(2,1)S(1)} %get-tuple-element.58), channel_id=1, source_target_pairs={{0,4},{1,5},{2,6},{3,7},{4,8},{5,9},{6,10},{7,11},{8,12},{9,13},{1... | collective-permute-start | bytes 196616 | tf_op jit(solution)/shard_map/ppermute | solution.py:34
  133.7 3.9 %collective-permute-done.31 = bf16[16,2048]{1,0:T(8,128)(2,1)S(1)} collective-permute-done((bf16[16,2048]{1,0:T(8,128)(2,1)S(1)}, bf16[16,2048]{1,0:T(8,128)(2,1)S(1)}, u32[]{:S(2)}, u32[]{:S(2)}) %collective-permute-start.31) | collective-permute-done | bytes 65568 | tf_op jit(solution)/shard_map/ppermute | solution.py:34
  (105 shorter events, 30.4 us)
Async XLA Ops:
  4.8 19.3 %collective-permute-start = (bf16[16,2176]{1,0:T(8,128)(2,1)}, bf16[16,2176]{1,0:T(8,128)(2,1)}, u32[]{:S(2)}, u32[]{:S(2)}) collective-permute-start(bf16[16,2176]{1,0:T(8,128)(2,1)} %get-tuple-element.25), channel_id=1, source_target_pairs={{0,4},{1,5},{2,6},{3,7},{4,8},{5,9},{6,10},{7,11},{8,12},{9,13},{1... | collective-permute-start | bytes 208904 | tf_op jit(solution)/shard_map/ppermute | solution.py:34
  7.9 21.5 %collective-permute-start.1 = (bf16[16,2176]{1,0:T(8,128)(2,1)}, bf16[16,2176]{1,0:T(8,128)(2,1)}, u32[]{:S(2)}, u32[]{:S(2)}) collective-permute-start(bf16[16,2176]{1,0:T(8,128)(2,1)} %get-tuple-element.25), channel_id=1, source_target_pairs={{0,8},{1,9},{2,10},{3,11},{4,12},{5,13},{6,14},{7,15},{8,0},{9,1},... | collective-permute-start | bytes 208904 | tf_op jit(solution)/shard_map/ppermute | solution.py:34
  10.5 20.4 %collective-permute-start.2 = (bf16[16,2176]{1,0:T(8,128)(2,1)}, bf16[16,2176]{1,0:T(8,128)(2,1)}, u32[]{:S(2)}, u32[]{:S(2)}) collective-permute-start(bf16[16,2176]{1,0:T(8,128)(2,1)} %get-tuple-element.25), channel_id=1, source_target_pairs={{0,12},{1,13},{2,14},{3,15},{4,0},{5,1},{6,2},{7,3},{8,4},{9,5},{1... | collective-permute-start | bytes 208904 | tf_op jit(solution)/shard_map/ppermute | solution.py:34
  11.8 21.7 %collective-permute-start.11 = (bf16[16,2176]{1,0:T(8,128)(2,1)}, bf16[16,2176]{1,0:T(8,128)(2,1)}, u32[]{:S(2)}, u32[]{:S(2)}) collective-permute-start(bf16[16,2176]{1,0:T(8,128)(2,1)} %get-tuple-element.35), channel_id=1, source_target_pairs={{0,4},{1,5},{2,6},{3,7},{4,8},{5,9},{6,10},{7,11},{8,12},{9,13},{1... | collective-permute-start | bytes 208904 | tf_op jit(solution)/shard_map/ppermute | solution.py:34
  12.5 25.3 %collective-permute-start.12 = (bf16[16,2176]{1,0:T(8,128)(2,1)}, bf16[16,2176]{1,0:T(8,128)(2,1)}, u32[]{:S(2)}, u32[]{:S(2)}) collective-permute-start(bf16[16,2176]{1,0:T(8,128)(2,1)} %get-tuple-element.35), channel_id=1, source_target_pairs={{0,8},{1,9},{2,10},{3,11},{4,12},{5,13},{6,14},{7,15},{8,0},{9,1},... | collective-permute-start | bytes 208904 | tf_op jit(solution)/shard_map/ppermute | solution.py:34
  17.1 54.9 %all-to-all-start = ((bf16[16,264,128]{2,1,0:T(8,128)(2,1)}), bf16[16,264,128]{2,1,0:T(8,128)(2,1)}, u32[]{:S(2)}, u32[]{:S(2)}) async-start(bf16[16,264,128]{2,1,0:T(8,128)(2,1)} %copy-done.5), calls=%async_computation | async-start | bytes 2162688 | tf_op jit(solution)/shard_map/all_to_all | solution.py:302
  24.1 19.0 %collective-permute-start.13 = (bf16[16,2176]{1,0:T(8,128)(2,1)}, bf16[16,2176]{1,0:T(8,128)(2,1)S(1)}, u32[]{:S(2)}, u32[]{:S(2)}) collective-permute-start(bf16[16,2176]{1,0:T(8,128)(2,1)} %get-tuple-element.35), channel_id=1, source_target_pairs={{0,12},{1,13},{2,14},{3,15},{4,0},{5,1},{6,2},{7,3},{8,4},{9,5},{1... | collective-permute-start | bytes 208904 | tf_op jit(solution)/shard_map/ppermute | solution.py:34
  29.4 19.4 %collective-permute-start.22 = (bf16[16,2176]{1,0:T(8,128)(2,1)S(1)}, bf16[16,2176]{1,0:T(8,128)(2,1)S(1)}, u32[]{:S(2)}, u32[]{:S(2)}) collective-permute-start(bf16[16,2176]{1,0:T(8,128)(2,1)S(1)} %copy-done.12), channel_id=1, source_target_pairs={{0,4},{1,5},{2,6},{3,7},{4,8},{5,9},{6,10},{7,11},{8,12},{9,13},{1... | collective-permute-start | bytes 208904 | tf_op jit(solution)/shard_map/ppermute | solution.py:34
  30.9 25.6 %collective-permute-start.23 = (bf16[16,2176]{1,0:T(8,128)(2,1)S(1)}, bf16[16,2176]{1,0:T(8,128)(2,1)S(1)}, u32[]{:S(2)}, u32[]{:S(2)}) collective-permute-start(bf16[16,2176]{1,0:T(8,128)(2,1)S(1)} %copy-done.12), channel_id=1, source_target_pairs={{0,8},{1,9},{2,10},{3,11},{4,12},{5,13},{6,14},{7,15},{8,0},{9,1},... | collective-permute-start | bytes 208904 | tf_op jit(solution)/shard_map/ppermute | solution.py:34
  33.5 23.0 %collective-permute-start.24 = (bf16[16,2176]{1,0:T(8,128)(2,1)S(1)}, bf16[16,2176]{1,0:T(8,128)(2,1)S(1)}, u32[]{:S(2)}, u32[]{:S(2)}) collective-permute-start(bf16[16,2176]{1,0:T(8,128)(2,1)S(1)} %copy-done.12), channel_id=1, source_target_pairs={{0,12},{1,13},{2,14},{3,15},{4,0},{5,1},{6,2},{7,3},{8,4},{9,5},{1... | collective-permute-start | bytes 208904 | tf_op jit(solution)/shard_map/ppermute | solution.py:34
  37.8 20.4 %collective-permute-start.3 = (bf16[64,2176]{1,0:T(8,128)(2,1)}, bf16[64,2176]{1,0:T(8,128)(2,1)}, u32[]{:S(2)}, u32[]{:S(2)}) collective-permute-start(bf16[64,2176]{1,0:T(8,128)(2,1)} %constant_dynamic-update-slice_fusion.refs_0_), channel_id=1, source_target_pairs={{0,2},{1,3},{2,0},{3,1},{4,6},{5,7},{6,4},{7,5},{8,10},{9,11},{10,... | collective-permute-start | bytes 835592 | tf_op jit(solution)/shard_map/ppermute | solution.py:34
  43.1 15.5 %collective-permute-start.4 = (bf16[64,2176]{1,0:T(8,128)(2,1)}, bf16[64,2176]{1,0:T(8,128)(2,1)}, u32[]{:S(2)}, u32[]{:S(2)}) collective-permute-start(bf16[64,2176]{1,0:T(8,128)(2,1)} %constant_dynamic-update-slice_fusion.refs_0_), channel_id=1, source_target_pairs={{0,1},{1,0},{2,3},{3,2},{4,5},{5,4},{6,7},{7,6},{8,9},{9,8},{10,11... | collective-permute-start | bytes 835592 | tf_op jit(solution)/shard_map/ppermute | solution.py:34
  48.8 9.9 %collective-permute-start.14 = (bf16[64,2176]{1,0:T(8,128)(2,1)}, bf16[64,2176]{1,0:T(8,128)(2,1)}, u32[]{:S(2)}, u32[]{:S(2)}) collective-permute-start(bf16[64,2176]{1,0:T(8,128)(2,1)} %constant_dynamic-update-slice_fusion.4.refs_0_), channel_id=1, source_target_pairs={{0,2},{1,3},{2,0},{3,1},{4,6},{5,7},{6,4},{7,5},{8,10},{9,11},{10,... | collective-permute-start | bytes 835592 | tf_op jit(solution)/shard_map/ppermute | solution.py:34
  56.5 7.9 %collective-permute-start.25 = (bf16[64,2176]{1,0:T(8,128)(2,1)S(1)}, bf16[64,2176]{1,0:T(8,128)(2,1)}, u32[]{:S(2)}, u32[]{:S(2)}) collective-permute-start(bf16[64,2176]{1,0:T(8,128)(2,1)S(1)} %constant_dynamic-update-slice_fusion.8.refs_0_), channel_id=1, source_target_pairs={{0,2},{1,3},{2,0},{3,1},{4,6},{5,7},{6,4},{7,5},{8,10},{9,11},{10,... | collective-permute-start | bytes 835592 | tf_op jit(solution)/shard_map/ppermute | solution.py:34
  58.1 25.1 %collective-permute-start.15 = (bf16[64,2176]{1,0:T(8,128)(2,1)}, bf16[64,2176]{1,0:T(8,128)(2,1)}, u32[]{:S(2)}, u32[]{:S(2)}) collective-permute-start(bf16[64,2176]{1,0:T(8,128)(2,1)} %constant_dynamic-update-slice_fusion.4.refs_0_), channel_id=1, source_target_pairs={{0,1},{1,0},{2,3},{3,2},{4,5},{5,4},{6,7},{7,6},{8,9},{9,8},{10,11... | collective-permute-start | bytes 835592 | tf_op jit(solution)/shard_map/ppermute | solution.py:34
  58.6 24.5 %collective-permute-start.16 = (bf16[64,2176]{1,0:T(8,128)(2,1)}, bf16[64,2176]{1,0:T(8,128)(2,1)}, u32[]{:S(2)}, u32[]{:S(2)}) collective-permute-start(bf16[64,2176]{1,0:T(8,128)(2,1)} %collective-permute-done.14.refs_1_), channel_id=1, source_target_pairs={{0,1},{1,0},{2,3},{3,2},{4,5},{5,4},{6,7},{7,6},{8,9},{9,8},{10,11... | collective-permute-start | bytes 835592 | tf_op jit(solution)/shard_map/ppermute | solution.py:34
  58.6 28.4 %collective-permute-start.26 = (bf16[64,2176]{1,0:T(8,128)(2,1)S(1)}, bf16[64,2176]{1,0:T(8,128)(2,1)}, u32[]{:S(2)}, u32[]{:S(2)}) collective-permute-start(bf16[64,2176]{1,0:T(8,128)(2,1)S(1)} %constant_dynamic-update-slice_fusion.8.refs_0_), channel_id=1, source_target_pairs={{0,1},{1,0},{2,3},{3,2},{4,5},{5,4},{6,7},{7,6},{8,9},{9,8},{10,11... | collective-permute-start | bytes 835592 | tf_op jit(solution)/shard_map/ppermute | solution.py:34
  64.4 22.6 %collective-permute-start.27 = (bf16[64,2176]{1,0:T(8,128)(2,1)}, bf16[64,2176]{1,0:T(8,128)(2,1)}, u32[]{:S(2)}, u32[]{:S(2)}) collective-permute-start(bf16[64,2176]{1,0:T(8,128)(2,1)} %collective-permute-done.25.refs_1_), channel_id=1, source_target_pairs={{0,1},{1,0},{2,3},{3,2},{4,5},{5,4},{6,7},{7,6},{8,9},{9,8},{10,11... | collective-permute-start | bytes 835592 | tf_op jit(solution)/shard_map/ppermute | solution.py:34
  82.6 17.5 %collective-permute-start.6 = (bf16[128,2048]{1,0:T(8,128)(2,1)S(1)}, bf16[128,2048]{1,0:T(8,128)(2,1)S(1)}, u32[]{:S(2)}, u32[]{:S(2)}) collective-permute-start(bf16[128,2048]{1,0:T(8,128)(2,1)S(1)} %get-tuple-element.34), channel_id=1, source_target_pairs={{0,1},{1,0},{2,3},{3,2},{4,5},{5,4},{6,7},{7,6},{8,9},{9,8},{10,11... | collective-permute-start | bytes 1572872 | tf_op jit(solution)/shard_map/ppermute | solution.py:34
  95.3 6.5 %collective-permute-start.17 = (bf16[128,2048]{1,0:T(8,128)(2,1)S(1)}, bf16[128,2048]{1,0:T(8,128)(2,1)S(1)}, u32[]{:S(2)}, u32[]{:S(2)}) collective-permute-start(bf16[128,2048]{1,0:T(8,128)(2,1)S(1)} %get-tuple-element.39), channel_id=1, source_target_pairs={{0,1},{1,0},{2,3},{3,2},{4,5},{5,4},{6,7},{7,6},{8,9},{9,8},{10,11... | collective-permute-start | bytes 1572872 | tf_op jit(solution)/shard_map/ppermute | solution.py:34
  100.3 9.2 %collective-permute-start.7 = (bf16[64,2048]{1,0:T(8,128)(2,1)S(1)}, bf16[64,2048]{1,0:T(8,128)(2,1)S(1)}, u32[]{:S(2)}, u32[]{:S(2)}) collective-permute-start(bf16[64,2048]{1,0:T(8,128)(2,1)S(1)} %slice.137), channel_id=1, source_target_pairs={{0,2},{1,3},{2,0},{3,1},{4,6},{5,7},{6,4},{7,5},{8,10},{9,11},{10,... | collective-permute-start | bytes 786440 | tf_op jit(solution)/shard_map/ppermute | solution.py:34
  102.0 16.4 %collective-permute-start.18 = (bf16[64,2048]{1,0:T(8,128)(2,1)S(1)}, bf16[64,2048]{1,0:T(8,128)(2,1)S(1)}, u32[]{:S(2)}, u32[]{:S(2)}) collective-permute-start(bf16[64,2048]{1,0:T(8,128)(2,1)S(1)} %slice.136), channel_id=1, source_target_pairs={{0,2},{1,3},{2,0},{3,1},{4,6},{5,7},{6,4},{7,5},{8,10},{9,11},{10,... | collective-permute-start | bytes 786440 | tf_op jit(solution)/shard_map/ppermute | solution.py:34
  102.7 18.6 %collective-permute-start.29 = (bf16[64,2048]{1,0:T(8,128)(2,1)S(1)}, bf16[64,2048]{1,0:T(8,128)(2,1)S(1)}, u32[]{:S(2)}, u32[]{:S(2)}) collective-permute-start(bf16[64,2048]{1,0:T(8,128)(2,1)S(1)} %slice.135), channel_id=1, source_target_pairs={{0,2},{1,3},{2,0},{3,1},{4,6},{5,7},{6,4},{7,5},{8,10},{9,11},{10,... | collective-permute-start | bytes 786440 | tf_op jit(solution)/shard_map/ppermute | solution.py:34
  109.6 17.0 %collective-permute-start.10 = (bf16[16,2048]{1,0:T(8,128)(2,1)S(1)}, bf16[16,2048]{1,0:T(8,128)(2,1)S(1)}, u32[]{:S(2)}, u32[]{:S(2)}) collective-permute-start(bf16[16,2048]{1,0:T(8,128)(2,1)S(1)} %get-tuple-element.52), channel_id=1, source_target_pairs={{0,4},{1,5},{2,6},{3,7},{4,8},{5,9},{6,10},{7,11},{8,12},{9,13},{1... | collective-permute-start | bytes 196616 | tf_op jit(solution)/shard_map/ppermute | solution.py:34
  116.8 10.3 %collective-permute-start.8 = (bf16[16,2048]{1,0:T(8,128)(2,1)S(1)}, bf16[16,2048]{1,0:T(8,128)(2,1)S(1)}, u32[]{:S(2)}, u32[]{:S(2)}) collective-permute-start(bf16[16,2048]{1,0:T(8,128)(2,1)S(1)} %get-tuple-element.51), channel_id=1, source_target_pairs={{0,12},{1,13},{2,14},{3,15},{4,0},{5,1},{6,2},{7,3},{8,4},{9,5},{1... | collective-permute-start | bytes 196616 | tf_op jit(solution)/shard_map/ppermute | solution.py:34
  116.8 13.7 %collective-permute-start.9 = (bf16[16,2048]{1,0:T(8,128)(2,1)S(1)}, bf16[16,2048]{1,0:T(8,128)(2,1)S(1)}, u32[]{:S(2)}, u32[]{:S(2)}) collective-permute-start(bf16[16,2048]{1,0:T(8,128)(2,1)S(1)} %get-tuple-element.53), channel_id=1, source_target_pairs={{0,8},{1,9},{2,10},{3,11},{4,12},{5,13},{6,14},{7,15},{8,0},{9,1},... | collective-permute-start | bytes 196616 | tf_op jit(solution)/shard_map/ppermute | solution.py:34
  118.5 12.1 %collective-permute-start.19 = (bf16[16,2048]{1,0:T(8,128)(2,1)S(1)}, bf16[16,2048]{1,0:T(8,128)(2,1)S(1)}, u32[]{:S(2)}, u32[]{:S(2)}) collective-permute-start(bf16[16,2048]{1,0:T(8,128)(2,1)S(1)} %get-tuple-element.54), channel_id=1, source_target_pairs={{0,12},{1,13},{2,14},{3,15},{4,0},{5,1},{6,2},{7,3},{8,4},{9,5},{1... | collective-permute-start | bytes 196616 | tf_op jit(solution)/shard_map/ppermute | solution.py:34
  121.3 10.9 %collective-permute-start.20 = (bf16[16,2048]{1,0:T(8,128)(2,1)S(1)}, bf16[16,2048]{1,0:T(8,128)(2,1)S(1)}, u32[]{:S(2)}, u32[]{:S(2)}) collective-permute-start(bf16[16,2048]{1,0:T(8,128)(2,1)S(1)} %get-tuple-element.56), channel_id=1, source_target_pairs={{0,8},{1,9},{2,10},{3,11},{4,12},{5,13},{6,14},{7,15},{8,0},{9,1},... | collective-permute-start | bytes 196616 | tf_op jit(solution)/shard_map/ppermute | solution.py:34
  126.6 7.0 %collective-permute-start.21 = (bf16[16,2048]{1,0:T(8,128)(2,1)S(1)}, bf16[16,2048]{1,0:T(8,128)(2,1)S(1)}, u32[]{:S(2)}, u32[]{:S(2)}) collective-permute-start(bf16[16,2048]{1,0:T(8,128)(2,1)S(1)} %get-tuple-element.55), channel_id=1, source_target_pairs={{0,4},{1,5},{2,6},{3,7},{4,8},{5,9},{6,10},{7,11},{8,12},{9,13},{1... | collective-permute-start | bytes 196616 | tf_op jit(solution)/shard_map/ppermute | solution.py:34
  127.1 6.5 %collective-permute-start.30 = (bf16[16,2048]{1,0:T(8,128)(2,1)S(1)}, bf16[16,2048]{1,0:T(8,128)(2,1)S(1)}, u32[]{:S(2)}, u32[]{:S(2)}) collective-permute-start(bf16[16,2048]{1,0:T(8,128)(2,1)S(1)} %get-tuple-element.57), channel_id=1, source_target_pairs={{0,12},{1,13},{2,14},{3,15},{4,0},{5,1},{6,2},{7,3},{8,4},{9,5},{1... | collective-permute-start | bytes 196616 | tf_op jit(solution)/shard_map/ppermute | solution.py:34
  130.5 7.0 %collective-permute-start.31 = (bf16[16,2048]{1,0:T(8,128)(2,1)S(1)}, bf16[16,2048]{1,0:T(8,128)(2,1)S(1)}, u32[]{:S(2)}, u32[]{:S(2)}) collective-permute-start(bf16[16,2048]{1,0:T(8,128)(2,1)S(1)} %get-tuple-element.59), channel_id=1, source_target_pairs={{0,8},{1,9},{2,10},{3,11},{4,12},{5,13},{6,14},{7,15},{8,0},{9,1},... | collective-permute-start | bytes 196616 | tf_op jit(solution)/shard_map/ppermute | solution.py:34
  130.6 7.0 %collective-permute-start.32 = (bf16[16,2048]{1,0:T(8,128)(2,1)S(1)}, bf16[16,2048]{1,0:T(8,128)(2,1)S(1)}, u32[]{:S(2)}, u32[]{:S(2)}) collective-permute-start(bf16[16,2048]{1,0:T(8,128)(2,1)S(1)} %get-tuple-element.58), channel_id=1, source_target_pairs={{0,4},{1,5},{2,6},{3,7},{4,8},{5,9},{6,10},{7,11},{8,12},{9,13},{1... | collective-permute-start | bytes 196616 | tf_op jit(solution)/shard_map/ppermute | solution.py:34
  (17 other events, 118.3 us)

commit v4 on v3

--- a/solution.py
+++ b/solution.py
@@ -9,6 +9,7 @@
 
 adapter_scale = 2.0
 LANES = 128
+GRANT = 60 << 20
 
 
 def route_gates(logits):
@@ -37,42 +38,78 @@
 def gather_rows(x, n):
     outer, middle, cores = split_axis(n)
     column = [x] + [shift(x, n, middle * cores, outer, k) for k in range(1, outer)]
-    column = jnp.concatenate(column, axis=0)
+    column = jnp.stack(column).reshape(-1, x.shape[1])
     sheet = [column] + [shift(column, n, cores, middle, k) for k in range(1, middle)]
     return sheet + [shift(p, n, 1, cores, k) for k in range(1, cores) for p in sheet]
 
 
-def scatter_rows(kept, sent, n):
+def scatter_rows(parts, n):
     outer, middle, cores = split_axis(n)
-    count, width = kept.shape
-    if cores > 1:
+    results, before = [], None
+    for kept, sent in parts:
+        count = kept.shape[0] // middle
         kept = kept + shift(sent, n, 1, cores, 1).astype(jnp.float32)
-    for stride, size in ((cores, middle), (middle * cores, outer)):
-        count //= size
+        away = kept[count:].astype(jnp.bfloat16)
+        if before is not None:
+            away, before = lax.optimization_barrier((away, before))
+            results[-1] = before
         total = kept[:count]
-        for k in range(1, size):
+        for k in range(1, middle):
+            part = away[(k - 1) * count : k * count]
+            total = total + shift(part, n, cores, middle, middle - k).astype(jnp.float32)
+        results.append(total)
+        before = total
+    finals = []
+    for kept in results:
+        count = kept.shape[0] // outer
+        total = kept[:count]
+        for k in range(1, outer):
             part = kept[k * count : (k + 1) * count].astype(jnp.bfloat16)
-            total = total + shift(part, n, stride, size, size - k).astype(jnp.float32)
-        kept = total
-    return kept.astype(jnp.bfloat16)
+            total = total + shift(part, n, middle * cores, outer, outer - k).astype(jnp.float32)
+        finals.append(total.astype(jnp.bfloat16))
+    return finals
+
+
+def exchange_factors(blocks, n):
+    outer, middle, cores = split_axis(n)
+    stride = middle * cores
+    turned = [blocks[0]] + [shift(blocks[r], n, cores, middle, r) for r in range(1, middle)]
+    here, there = [], []
+    for q in range(outer):
+        pairs = []
+        for g in range(2):
+            for i in range(n):
+                place = i // stride
+                to = (i + ((place + q) % outer - place) * stride) ^ g
+                pairs.append((g * n + i, g * n + to))
+        part = jnp.stack([t[q] for t in turned])
+        part = lax.ppermute(part, ("group", "expert"), pairs)
+        here.append(part)
+        there.append(lax.ppermute(part, "group", [(0, 1), (1, 0)]))
+    return here, there
 
 
 def dot(a, b):
     return jnp.dot(a, b, preferred_element_type=jnp.float32)
 
 
-def payload_kernel(hidden_ref, ids_ref, logits_ref, *out_refs):
-    rows, width = out_refs[0].shape[0], hidden_ref.shape[1]
-    padded = out_refs[0].shape[1] - width
-    gates = route_gates(logits_ref[...]).astype(jnp.float32)
-    ids = ids_ref[...]
-    lane = lax.broadcasted_iota(jnp.int32, (ids.shape[0], padded), 1)
-    dense = jnp.zeros(lane.shape, jnp.float32)
-    for k in range(ids.shape[1]):
-        dense += jnp.where(ids[:, k : k + 1] == lane, gates[:, k : k + 1], 0.0)
-    dense = dense.astype(jnp.bfloat16)
+def payload_kernel(hidden_ref, ids_ref, logits_ref, *refs):
+    out_refs, turned_ref = refs[:-1], refs[-1]
+    steps, top, rows = ids_ref.shape
+    width = hidden_ref.shape[2]
+    turned_ref[...] = jnp.zeros_like(turned_ref)
+    for s in range(steps):
+        logits, ids = logits_ref[s], ids_ref[s]
+        scores = jnp.exp(logits - jnp.max(logits, axis=0, keepdims=True))
+        gates = scores / jnp.sum(scores, axis=0, keepdims=True)
+        expert = lax.broadcasted_iota(jnp.int32, (turned_ref.shape[0], rows), 0)
+        dense = jnp.zeros(expert.shape, jnp.float32)
+        for k in range(top):
+            dense += jnp.where(ids[k : k + 1, :] == expert, gates[k : k + 1, :], 0.0)
+        turned_ref[:, s * rows : (s + 1) * rows] = dense
+    dense = turned_ref[...].T.astype(jnp.bfloat16)
     for s, out_ref in enumerate(out_refs):
-        out_ref[:, :width] = hidden_ref[s * rows : (s + 1) * rows, :]
+        out_ref[:, :width] = hidden_ref[s]
         out_ref[:, width:] = dense[s * rows : (s + 1) * rows, :]
 
 
@@ -83,16 +120,17 @@
     return pl.pallas_call(
         payload_kernel,
         out_shape=[shape] * steps,
+        scratch_shapes=[pltpu.VMEM((padded, -(-steps * rows // LANES) * LANES), jnp.float32)],
+        compiler_params=pltpu.CompilerParams(vmem_limit_bytes=GRANT),
         name="payload",
-    )(
-        hidden.reshape(steps * rows, width),
-        route_ids.reshape(steps * rows, -1),
-        route_logits.reshape(steps * rows, -1),
-    )
-
-
-def order_kernel(placement_ref, factors_ref, out_ref, wide_ref):
-    slots, length, lanes = out_ref.shape
+    )(hidden, jnp.swapaxes(route_ids, 1, 2), jnp.swapaxes(route_logits, 1, 2))
+
+
+def order_kernel(outer, middle, place_ref, placement_ref, factors_ref, *refs):
+    out_refs, wide_ref = refs[:-1], refs[-1]
+    slots = factors_ref.shape[0]
+    length, lanes = out_refs[0].shape[1:]
+    group, me = place_ref[0], place_ref[1]
 
     def cut(t, carry):
         start = pl.multiple_of(t * lanes, lanes)
@@ -101,29 +139,59 @@
         return carry
 
     lax.fori_loop(0, length, cut, 0, unroll=8)
-    for s in range(slots):
-        out_ref[placement_ref[s]] = wide_ref[s * length : (s + 1) * length, :].astype(jnp.bfloat16)
-
-
-def order_factors(placement, factors):
+
+    def put(s, carry):
+        to = placement_ref[s]
+        aside = lax.rem(to // 2 + middle - lax.rem(me // 2, middle), middle)
+        ahead = lax.rem(to // (2 * middle) + outer - me // (2 * middle), outer)
+        ours = lax.rem(to + me + group, 2) == 0
+        rows = wide_ref[pl.ds(pl.multiple_of(s * length, 8), length), :].astype(jnp.bfloat16)
+        for r, out_ref in enumerate(out_refs):
+
+            @pl.when(jnp.logical_and(ours, aside == r))
+            def _():
+                out_ref[ahead] = rows
+
+        return carry
+
+    lax.fori_loop(0, slots, put, 0)
+
+
+def order_factors(place, placement, factors, n):
+    outer, middle, _ = split_axis(n)
     slots, entries = factors.shape
     length = entries // LANES
     return pl.pallas_call(
-        order_kernel,
-        out_shape=jax.ShapeDtypeStruct((slots, length, LANES), jnp.bfloat16),
+        functools.partial(order_kernel, outer, middle),
+        out_shape=[jax.ShapeDtypeStruct((outer, length, LANES), jnp.bfloat16)] * middle,
         in_specs=[
+            pl.BlockSpec(memory_space=pltpu.SMEM),
             pl.BlockSpec(memory_space=pltpu.SMEM),
             pl.BlockSpec(memory_space=pltpu.VMEM),
         ],
         scratch_shapes=[pltpu.VMEM((slots * length, LANES), jnp.float32)],
-        compiler_params=pltpu.CompilerParams(vmem_limit_bytes=12 << 20),
+        compiler_params=pltpu.CompilerParams(vmem_limit_bytes=GRANT),
         name="order_factors",
-    )(placement, factors)
-
-
-def relayout_kernel(flat_ref, a_gu_ref, gate_b_ref, up_b_ref, down_a_ref, down_b_ref, wide_ref):
+    )(place, placement, factors)
+
+
+def relayout_kernel(outer, middle, place_ref, *refs):
+    pieces = refs[: 2 * outer]
+    a_gu_ref, gate_b_ref, up_b_ref, down_a_ref, down_b_ref, flat_ref, wide_ref = refs[2 * outer :]
     width, units = a_gu_ref.shape[0], gate_b_ref.shape[1]
     rank = gate_b_ref.shape[0]
+    length = pieces[0].shape[1]
+    group, me = place_ref[0], place_ref[1]
+    for i, piece in enumerate(pieces):
+        swapped, q = i // outer, i % outer
+        core = lax.rem(me + group + swapped, 2)
+        for r in range(middle):
+            row = lax.rem(me // 2 + middle - r, middle)
+            column = lax.rem(me // (2 * middle) + outer - q, outer)
+            source = (column * middle + row) * 2 + core
+            start = pl.multiple_of(source * length, 8)
+            flat_ref[pl.ds(start, length), :] = piece[r].astype(jnp.float32)
+
     n_wide, n_unit = width // 2, units // 2
     at_ub = 2 * n_wide + n_unit
     at_da = 2 * n_wide + 2 * n_unit
@@ -131,7 +199,7 @@
     left = lax.broadcasted_iota(jnp.int32, (chunk, LANES), 1) < rank
 
     def load(start):
-        return flat_ref[pl.ds(pl.multiple_of(start, 128), chunk), :].astype(jnp.float32)
+        return flat_ref[pl.ds(pl.multiple_of(start, 128), chunk), :]
 
     def gate_up(i, carry):
         g, u = load(i * chunk), load(n_wide + n_unit + i * chunk)
@@ -155,22 +223,27 @@
         (at_da + n_unit, down_b_ref),
     ):
         tiles = b_ref.shape[1] // LANES
-        count = rank * tiles
-        wide_ref[:count, :] = flat_ref[start : start + count, :].astype(jnp.float32)
         for j in range(tiles):
-            row = wide_ref[pl.ds(j, rank, stride=tiles), :]
+            row = flat_ref[pl.ds(start + j, rank, stride=tiles), :]
             b_ref[:, j * LANES : (j + 1) * LANES] = row.astype(jnp.bfloat16)
 
 
-def relayout_factors(flat, width, units, rank):
+def relayout_factors(place, here, there, width, units, rank, n):
+    outer, middle, _ = split_axis(n)
     shapes = [(width, 2 * rank), (rank, units), (rank, units), (units, 2 * rank), (rank, width)]
+    length = here[0].shape[1]
     return pl.pallas_call(
-        relayout_kernel,
+        functools.partial(relayout_kernel, outer, middle),
         out_shape=[jax.ShapeDtypeStruct(shape, jnp.bfloat16) for shape in shapes],
-        scratch_shapes=[pltpu.VMEM((max(width, rank * width // LANES), LANES), jnp.float32)],
-        compiler_params=pltpu.CompilerParams(vmem_limit_bytes=12 << 20),
+        in_specs=[pl.BlockSpec(memory_space=pltpu.SMEM)]
+        + [pl.BlockSpec(memory_space=pltpu.VMEM)] * (2 * outer),
+        scratch_shapes=[
+            pltpu.VMEM((n * length, LANES), jnp.float32),
+            pltpu.VMEM((width, LANES), jnp.float32),
+        ],
+        compiler_params=pltpu.CompilerParams(vmem_limit_bytes=GRANT),
         name="relayout_factors",
-    )(flat)
+    )(place, *here, *there)
 
 
 def fill_rows(pieces, x_ref):
@@ -204,7 +277,7 @@
         + [pl.BlockSpec((width, block), lambda i: (0, i))] * 2,
         out_specs=[pl.BlockSpec((total, block), lambda i: (0, i))] * 2,
         scratch_shapes=[pltpu.VMEM((total, width), jnp.bfloat16)],
-        compiler_params=pltpu.CompilerParams(vmem_limit_bytes=24 << 20),
+        compiler_params=pltpu.CompilerParams(vmem_limit_bytes=GRANT),
         cost_estimate=pl.CostEstimate(
             flops=4 * total * width * units,
             bytes_accessed=4 * width * units + 2 * total * width + 8 * total * units,
@@ -214,7 +287,7 @@
     )(*pieces, w_gate, w_up)
 
 
-def finish_kernel(count, me_ref, *refs):
+def finish_kernel(count, place_ref, *refs):
     pieces = refs[:count]
     (gate_ref, up_ref, a_gu_ref, gate_b_ref, up_b_ref, down_a_ref, down_b_ref, w_down_ref) = refs[
         count : count + 8
@@ -230,7 +303,7 @@
         for i, piece in enumerate(pieces):
             gates = piece[:, width:].astype(jnp.float32)
             lane = lax.broadcasted_iota(jnp.int32, gates.shape, 1)
-            own = jnp.sum(jnp.where(lane == me_ref[0], gates, 0.0), axis=1, keepdims=True)
+            own = jnp.sum(jnp.where(lane == place_ref[1], gates, 0.0), axis=1, keepdims=True)
             mine_ref[i * rows : (i + 1) * rows, :] = jnp.broadcast_to(own, (rows, LANES))
         low = (adapter_scale * dot(x_ref[...], a_gu_ref[...])).astype(jnp.bfloat16)
         g = gate_ref[...] + dot(low[:, :rank], gate_b_ref[...])
@@ -248,7 +321,7 @@
         at += n
 
 
-def finish_step(me, pieces, gate, up, low_rank, w_down, cores):
+def finish_step(place, pieces, gate, up, low_rank, w_down, cores):
     units, width = w_down.shape
     total = gate.shape[0]
     block = 512 if width % 512 == 0 else width
@@ -276,14 +349,14 @@
             pltpu.VMEM((total, down_a.shape[1]), jnp.bfloat16),
             pltpu.VMEM((total, LANES), jnp.float32),
         ],
-        compiler_params=pltpu.CompilerParams(vmem_limit_bytes=28 << 20),
+        compiler_params=pltpu.CompilerParams(vmem_limit_bytes=GRANT),
         cost_estimate=pl.CostEstimate(
             flops=2 * total * units * (width + 4 * rank) + 4 * total * width * rank,
             bytes_accessed=2 * units * width + 8 * total * width + 8 * total * units,
             transcendentals=total * units,
         ),
         name="finish_step",
-    )(me, *whole, down_b, w_down)
+    )(place, *whole, down_b, w_down)
 
 
 def dense_shards(
@@ -295,19 +368,20 @@
     units = w_gate.shape[2]
     rank = factors.shape[1] * owners // (3 * (width + units))
     cores = split_axis(owners)[2]
+    place = jnp.stack([lax.axis_index("group"), lax.axis_index("expert")]).astype(jnp.int32)
 
     payload = make_payload(hidden, route_ids, route_logits, experts)
+    blocks = order_factors(place, placement, factors, owners)
     gathered = [gather_rows(payload[s], owners) for s in range(steps)]
-    ordered = order_factors(placement, factors)
-    received = lax.all_to_all(ordered, "expert", split_axis=0, concat_axis=0, tiled=True)
+    here, there = exchange_factors(blocks, owners)
     base = [base_products(pieces, w_gate[0], w_up[0]) for pieces in gathered]
-    low_rank = relayout_factors(received.reshape(-1, LANES), width, units, rank)
-    me = lax.axis_index("expert").reshape(1)
-    results = []
-    for pieces, (gate, up) in zip(gathered, base):
-        parts = finish_step(me, pieces, gate, up, low_rank, down_weight[0], cores)
-        results.append(scatter_rows(parts[0], parts[-1], owners))
-    return jnp.stack(results, axis=0)
+    here, there, base = lax.optimization_barrier((here, there, base))
+    low_rank = relayout_factors(place, here, there, width, units, rank, owners)
+    parts = [
+        finish_step(place, pieces, gate, up, low_rank, down_weight[0], cores)
+        for pieces, (gate, up) in zip(gathered, base)
+    ]
+    return jnp.stack(scatter_rows(parts, owners), axis=0)
 
 
 def row_capacity(rows, top, experts):
@@ -402,11 +476,18 @@
     return jnp.stack(results, axis=0)
 
 
-def shards(hidden, route_ids, *rest):
+def shards(hidden, route_ids, route_logits, placement, factors, w_gate, w_up, down_weight):
     rows, top = route_ids.shape[1:]
-    experts = rest[1].shape[0]
-    every = row_capacity(rows, top, experts) == rows
-    return (dense_shards if every else sparse_shards)(hidden, route_ids, *rest)
+    width, units = w_gate.shape[1:]
+    owners = lax.axis_size("expert")
+    rank = factors.shape[1] * owners // (3 * (width + units))
+    dense = row_capacity(rows, top, placement.shape[0]) == rows
+    dense = dense and lax.axis_size("group") == 2 and split_axis(owners)[2] == 2
+    dense = dense and 2 * rank == LANES and width % 256 == 0 and units % 256 == 0
+    dense = dense and factors.shape[1] % (8 * LANES) == 0
+    return (dense_shards if dense else sparse_shards)(
+        hidden, route_ids, route_logits, placement, factors, w_gate, w_up, down_weight
+    )
 
 
 def solution(mesh):

time: 139 us -> 145 us (1.043)
  local copies, waits for them, and re-layouts: 23.3 us -> 2.65 us
  Pallas kernels: 29.7 us -> 47.4 us
  waiting for transfers between devices: 29.5 us -> 38.4 us
  starting transfers between devices: 54.1 us -> 50.4 us
  other arithmetic: 1.3 us -> 4.82 us
    unnamed x41 -> x46, local copies, waits for them, and re-layouts: 21 us -> 1.5 us
    ppermute x0 -> x8, starting transfers between devices: none -> 11.2 us  [the longest x4 6.09 us: exchange_factors(): part = lax.ppermute(part, ('group', 'expert'), pairs)]
    ppermute x33 -> x34, starting transfers between devices: 48.4 us -> 39.1 us  [shift(): return lax.ppermute(x, 'expert', pairs)]
    pallas_call x3, Pallas kernels: 12.8 us -> 20.5 us  [finish_step(): pl.pallas_call(functools.partial(finish_kernel, len(pieces)), grid=(width...]
    pallas_call x3, Pallas kernels: 11.6 us -> 18.5 us  [base_products(): pl.pallas_call(functools.partial(base_kernel, len(pieces)), grid=(units /...]
    all_to_all x1 -> x0, starting transfers between devices: 5.76 us -> none  [dense_shards(): lax.all_to_all(ordered, 'expert', split_axis=0, concat_axis=0, tiled=True)]
    ppermute x33 -> x34, waiting for transfers between devices: 29.5 us -> 34.9 us  [shift(): return lax.ppermute(x, 'expert', pairs)]
    ppermute x0 -> x8, waiting for transfers between devices: none -> 3.52 us  [the longest x4 3.51 us: exchange_factors(): there.append(lax.ppermute(part, 'group', [(0, 1), (1, 0)]))]
  transfers between devices with their start and end apart: 34 -> 42, of which waited for: 7 -> 15; matrix products, arithmetic and copies ran while one was open for 7% -> 4% of each run, Pallas kernels for 20% -> 25%
where the time goes in v4:
time: 145 us; the launch traced here: 144 us
  starting transfers between devices  50.4 us (35%)
  Pallas kernels  47.4 us (33%)
  waiting for transfers between devices  38.4 us (26%)
  other arithmetic  4.82 us (3%)
  local copies, waits for them, and re-layouts  2.65 us (2%)
    ppermute x34, starting transfers between devices, shift(): return lax.ppermute(x, 'expert', pairs)  39.1 us
    ppermute x34, waiting for transfers between devices, shift(): return lax.ppermute(x, 'expert', pairs)  34.9 us
    pallas_call x3, Pallas kernels, finish_step(): pl.pallas_call(functools.partial(finish_kernel, len(pieces)), grid=(width...  20.5 us
    pallas_call x3, Pallas kernels, base_products(): pl.pallas_call(functools.partial(base_kernel, len(pieces)), grid=(units /...  18.5 us
    ppermute x4, starting transfers between devices, exchange_factors(): part = lax.ppermute(part, ('group', 'expert'), pairs)  6.09 us
    ppermute x4, starting transfers between devices, exchange_factors(): there.append(lax.ppermute(part, 'group', [(0, 1), (1, 0)]))  5.14 us
    ppermute x4, waiting for transfers between devices, exchange_factors(): there.append(lax.ppermute(part, 'group', [(0, 1), (1, 0)]))  3.51 us
    pallas_call x1, Pallas kernels, order_factors(): pl.pallas_call(functools.partial(order_kernel, outer, middle), out_shape=...  3.35 us
  transfers between devices with their start and end apart: 42, of which 15 were waited for; matrix products, arithmetic and copies ran while one was open for 4% of the time, Pallas kernels for 25%

profile of v4, /device:TPU:0, one launch (start us, length us, event | category | flops | bytes accessed | tf_op | source)
XLA Modules:
  0.0 144.2 jit_solution(2707895405823054484)
XLA Ops:
  0.0 2.0 %payload.1 = (bf16[16,2176]{1,0:T(8,128)(2,1)}, bf16[16,2176]{1,0:T(8,128)(2,1)}, bf16[16,2176]{1,0:T(8,128)(2,1)}) custom-call(bf16[3,16,2048]{2,1,0:T(8,128)(2,1)} %hidden_ref.1, s32[3,8,16]{2,1,0:T(8,128)} %bitcast.61, f32[3,8,16]{2,1,0:T(8,128)} %bitcast.62), custom_call_target="tpu_custom_call" | custom-call | tf_op jit(solution)/shard_map/payload/pallas_call | solution.py:120
  2.0 5.0 %collective-permute-start.2 = (bf16[16,2176]{1,0:T(8,128)(2,1)}, bf16[16,2176]{1,0:T(8,128)(2,1)S(1)}, u32[]{:S(2)}, u32[]{:S(2)}) collective-permute-start(bf16[16,2176]{1,0:T(8,128)(2,1)} %get-tuple-element.45), channel_id=1, source_target_pairs={{0,12},{1,13},{2,14},{3,15},{4,0},{5,1},{6,2},{7,3},{8,4},{9,5},{1... | collective-permute-start | bytes 208904 | tf_op jit(solution)/shard_map/ppermute | solution.py:35
  7.5 2.5 %collective-permute-start.22 = (bf16[16,2176]{1,0:T(8,128)(2,1)}, bf16[16,2176]{1,0:T(8,128)(2,1)S(1)}, u32[]{:S(2)}, u32[]{:S(2)}) collective-permute-start(bf16[16,2176]{1,0:T(8,128)(2,1)} %get-tuple-element.53), channel_id=1, source_target_pairs={{0,8},{1,9},{2,10},{3,11},{4,12},{5,13},{6,14},{7,15},{8,0},{9,1},... | collective-permute-start | bytes 208904 | tf_op jit(solution)/shard_map/ppermute | solution.py:35
  9.9 2.0 %collective-permute-start.21 = (bf16[16,2176]{1,0:T(8,128)(2,1)}, bf16[16,2176]{1,0:T(8,128)(2,1)S(1)}, u32[]{:S(2)}, u32[]{:S(2)}) collective-permute-start(bf16[16,2176]{1,0:T(8,128)(2,1)} %get-tuple-element.53), channel_id=1, source_target_pairs={{0,4},{1,5},{2,6},{3,7},{4,8},{5,9},{6,10},{7,11},{8,12},{9,13},{1... | collective-permute-start | bytes 208904 | tf_op jit(solution)/shard_map/ppermute | solution.py:35
  12.6 3.4 %order_factors.1 = (bf16[4,264,128]{2,1,0:T(8,128)(2,1)}, bf16[4,264,128]{2,1,0:T(8,128)(2,1)}) custom-call(s32[2]{0:T(128)} %pad_add_fusion.place_ref, s32[16]{0:T(128)} %placement_ref.1, bf16[16,33792]{1,0:T(8,128)(2,1)} %factors_ref.1), custom_call_target="tpu_custom_call" | custom-call | tf_op jit(solution)/shard_map/order_factors/pallas_call | solution.py:164
  18.5 2.4 %collective-permute-start.17 = (bf16[16,2176]{1,0:T(8,128)(2,1)}, bf16[16,2176]{1,0:T(8,128)(2,1)S(1)}, u32[]{:S(2)}, u32[]{:S(2)}) collective-permute-start(bf16[16,2176]{1,0:T(8,128)(2,1)} %get-tuple-element.48), channel_id=1, source_target_pairs={{0,12},{1,13},{2,14},{3,15},{4,0},{5,1},{6,2},{7,3},{8,4},{9,5},{1... | collective-permute-start | bytes 208904 | tf_op jit(solution)/shard_map/ppermute | solution.py:35
  22.5 1.5 %collective-permute-start.6 = (bf16[4,264,128]{2,1,0:T(8,128)(2,1)}, bf16[4,264,128]{2,1,0:T(8,128)(2,1)S(1)}, u32[]{:S(2)}, u32[]{:S(2)}) collective-permute-start(bf16[4,264,128]{2,1,0:T(8,128)(2,1)} %get-tuple-element.47), channel_id=1, source_target_pairs={{0,2},{1,3},{2,0},{3,1},{4,6},{5,7},{6,4},{7,5},{8,10},{9,11},{10,... | collective-permute-start | bytes 811016 | tf_op jit(solution)/shard_map/ppermute | solution.py:35
  24.9 1.6 %collective-permute-start.24 = (bf16[64,2176]{1,0:T(8,128)(2,1)S(1)}, bf16[64,2176]{1,0:T(8,128)(2,1)S(1)}, u32[]{:S(2)}, u32[]{:S(2)}) collective-permute-start(bf16[64,2176]{1,0:T(8,128)(2,1)S(1)} %bitcast.38), channel_id=1, source_target_pairs={{0,2},{1,3},{2,0},{3,1},{4,6},{5,7},{6,4},{7,5},{8,10},{9,11},{10,... | collective-permute-start | bytes 835592 | tf_op jit(solution)/shard_map/ppermute | solution.py:35
  28.2 1.5 %collective-permute-start.3 = (bf16[64,2176]{1,0:T(8,128)(2,1)S(1)}, bf16[64,2176]{1,0:T(8,128)(2,1)S(1)}, u32[]{:S(2)}, u32[]{:S(2)}) collective-permute-start(bf16[64,2176]{1,0:T(8,128)(2,1)S(1)} %bitcast.42), channel_id=1, source_target_pairs={{0,2},{1,3},{2,0},{3,1},{4,6},{5,7},{6,4},{7,5},{8,10},{9,11},{10,... | collective-permute-start | bytes 835592 | tf_op jit(solution)/shard_map/ppermute | solution.py:35
  31.7 10.4 %collective-permute-done.3.refs_1_ = bf16[64,2176]{1,0:T(8,128)(2,1)S(1)} collective-permute-done((bf16[64,2176]{1,0:T(8,128)(2,1)S(1)}, bf16[64,2176]{1,0:T(8,128)(2,1)S(1)}, u32[]{:S(2)}, u32[]{:S(2)}) %collective-permute-start.3) | collective-permute-done | bytes 278560 | tf_op jit(solution)/shard_map/ppermute | solution.py:35
  42.7 4.4 %collective-permute-done.18.refs_1_ = bf16[64,2176]{1,0:T(8,128)(2,1)S(1)} collective-permute-done((bf16[64,2176]{1,0:T(8,128)(2,1)S(1)}, bf16[64,2176]{1,0:T(8,128)(2,1)S(1)}, u32[]{:S(2)}, u32[]{:S(2)}) %collective-permute-start.18) | collective-permute-done | bytes 278560 | tf_op jit(solution)/shard_map/ppermute | solution.py:35
  48.5 6.2 %base_products.4 = (f32[256,768]{1,0:T(8,128)}, f32[256,768]{1,0:T(8,128)}) custom-call(bf16[64,2176]{1,0:T(8,128)(2,1)} %bitcast.43, bf16[64,2176]{1,0:T(8,128)(2,1)} %copy-done.6, bf16[64,2176]{1,0:T(8,128)(2,1)} %copy-done.5, bf16[64,2176]{1,0:T(8,128)(2,1)} %copy-done.8, bf16[2048,768]{1,0:T(8,128)(2,1)} %bitcast.28, bf16[2048,768]{1,0:T(8,128)(2,1)} %bitcast.31), custom_call_target="tpu_custom_call" | custom-call | flops 1610612736 | bytes 8912896 | tf_op jit(solution)/shard_map/base_products/pallas_call | solution.py:272
  54.7 2.9 %collective-permute-start.8 = (bf16[2,264,128]{2,1,0:T(8,128)(2,1)S(1)}, bf16[2,264,128]{2,1,0:T(8,128)(2,1)S(1)}, u32[]{:S(2)}, u32[]{:S(2)}) collective-permute-start(bf16[2,264,128]{2,1,0:T(8,128)(2,1)S(1)} %pad_maximum_fusion.5), channel_id=1, source_target_pairs={{0,4},{1,5},{2,6},{3,7},{4,8},{5,9},{6,10},{7,11},{8,12},{9,13},{1... | collective-permute-start | bytes 405512 | tf_op jit(solution)/shard_map/ppermute | solution.py:86
  60.2 6.2 %base_products.3 = (f32[256,768]{1,0:T(8,128)}, f32[256,768]{1,0:T(8,128)}) custom-call(bf16[64,2176]{1,0:T(8,128)(2,1)} %bitcast.47, bf16[64,2176]{1,0:T(8,128)(2,1)} %copy-done.7, bf16[64,2176]{1,0:T(8,128)(2,1)} %copy-done.9, bf16[64,2176]{1,0:T(8,128)(2,1)} %copy-done.11, bf16[2048,768]{1,0:T(8,128)(2,1)} %bitcast.29, bf16[2048,768]{1,0:T(8,128)(2,1)} %bitcast.32), custom_call_target="tpu_custom_call" | custom-call | flops 1610612736 | bytes 8912896 | tf_op jit(solution)/shard_map/base_products/pallas_call | solution.py:272
  66.4 3.0 %collective-permute-start.11 = (bf16[2,264,128]{2,1,0:T(8,128)(2,1)S(1)}, bf16[2,264,128]{2,1,0:T(8,128)(2,1)S(1)}, u32[]{:S(2)}, u32[]{:S(2)}) collective-permute-start(bf16[2,264,128]{2,1,0:T(8,128)(2,1)S(1)} %collective-permute-done.7.refs_0_), channel_id=1, source_target_pairs={{0,16},{16,0},{1,17},{17,1},{2,18},{18,2},{3,19},{19,3},{4,20},{20... | collective-permute-start | bytes 405512 | tf_op jit(solution)/shard_map/ppermute | solution.py:88
  69.4 2.0 %collective-permute-start.13 = (bf16[2,264,128]{2,1,0:T(8,128)(2,1)S(1)}, bf16[2,264,128]{2,1,0:T(8,128)(2,1)S(1)}, u32[]{:S(2)}, u32[]{:S(2)}) collective-permute-start(bf16[2,264,128]{2,1,0:T(8,128)(2,1)S(1)} %collective-permute-done.9.refs_2_), channel_id=1, source_target_pairs={{0,16},{16,0},{1,17},{17,1},{2,18},{18,2},{3,19},{19,3},{4,20},{20... | collective-permute-start | bytes 405512 | tf_op jit(solution)/shard_map/ppermute | solution.py:88
  72.2 6.2 %base_products.5 = (f32[256,768]{1,0:T(8,128)}, f32[256,768]{1,0:T(8,128)}) custom-call(bf16[64,2176]{1,0:T(8,128)(2,1)} %bitcast.39, bf16[64,2176]{1,0:T(8,128)(2,1)} %copy-done.4, bf16[64,2176]{1,0:T(8,128)(2,1)} %copy-done.3, bf16[64,2176]{1,0:T(8,128)(2,1)} %copy-done.10, bf16[2048,768]{1,0:T(8,128)(2,1)} %bitcast.30, bf16[2048,768]{1,0:T(8,128)(2,1)} %bitcast.33), custom_call_target="tpu_custom_call" | custom-call | flops 1610612736 | bytes 8912896 | tf_op jit(solution)/shard_map/base_products/pallas_call | solution.py:272
  79.5 2.5 %collective-permute-done.14.refs_7_ = bf16[2,264,128]{2,1,0:T(8,128)(2,1)S(1)} collective-permute-done((bf16[2,264,128]{2,1,0:T(8,128)(2,1)S(1)}, bf16[2,264,128]{2,1,0:T(8,128)(2,1)S(1)}, u32[]{:S(2)}, u32[]{:S(2)}) %collective-permute-start.14) | collective-permute-done | bytes 135200 | tf_op jit(solution)/shard_map/ppermute | solution.py:88
  82.6 3.1 %relayout_factors.1 = (bf16[2048,128]{1,0:T(8,128)(2,1)}, bf16[64,768]{1,0:T(8,128)(2,1)}, bf16[64,768]{1,0:T(8,128)(2,1)}, bf16[768,128]{1,0:T(8,128)(2,1)}, bf16[64,2048]{1,0:T(8,128)(2,1)}) custom-call(s32[2]{0:T(128)} %pad_add_fusion.place_ref, bf16[2,264,128]{2,1,0:T(8,128)(2,1)} %copy-done.15, bf16[2,264,128]{2,1,0:T(8,128)(2,1)} %copy-done.16, ...), custom_call_target="tpu_custom_call" | custom-call | tf_op jit(solution)/shard_map/relayout_factors/pallas_call | solution.py:235
  85.7 6.8 %finish_step.4 = (f32[128,2048]{1,0:T(8,128)}, bf16[128,2048]{1,0:T(8,128)(2,1)}) custom-call(s32[2]{0:T(128)} %pad_add_fusion.place_ref, bf16[64,2176]{1,0:T(8,128)(2,1)} %bitcast.48, bf16[64,2176]{1,0:T(8,128)(2,1)} %copy-done.7, bf16[64,2176]{1,0:T(8,128)(2,1)} %copy-done.9, bf16[64,2176]{1,0:T(8,128)(2,1)} %copy-done.11, ...), custom_call_target="tpu_custom_call" | custom-call | flops 1040187392 | bytes 8912896 | tf_op jit(solution)/shard_map/finish_step/pallas_call | solution.py:335
  92.6 6.8 %finish_step.3 = (f32[128,2048]{1,0:T(8,128)}, bf16[128,2048]{1,0:T(8,128)(2,1)}) custom-call(s32[2]{0:T(128)} %pad_add_fusion.place_ref, bf16[64,2176]{1,0:T(8,128)(2,1)} %bitcast.44, bf16[64,2176]{1,0:T(8,128)(2,1)} %copy-done.6, bf16[64,2176]{1,0:T(8,128)(2,1)} %copy-done.5, bf16[64,2176]{1,0:T(8,128)(2,1)} %copy-done.8, ...), custom_call_target="tpu_custom_call" | custom-call | flops 1040187392 | bytes 8912896 | tf_op jit(solution)/shard_map/finish_step/pallas_call | solution.py:335
  100.0 6.8 %finish_step.5 = (f32[128,2048]{1,0:T(8,128)}, bf16[128,2048]{1,0:T(8,128)(2,1)}) custom-call(s32[2]{0:T(128)} %pad_add_fusion.place_ref, bf16[64,2176]{1,0:T(8,128)(2,1)} %bitcast.40, bf16[64,2176]{1,0:T(8,128)(2,1)} %copy-done.4, bf16[64,2176]{1,0:T(8,128)(2,1)} %copy-done.3, bf16[64,2176]{1,0:T(8,128)(2,1)} %copy-done.10, ...), custom_call_target="tpu_custom_call" | custom-call | flops 1040187392 | bytes 8912896 | tf_op jit(solution)/shard_map/finish_step/pallas_call | solution.py:335
  107.2 1.6 %collective-permute-start.29 = (bf16[64,2048]{1,0:T(8,128)(2,1)S(1)}, bf16[64,2048]{1,0:T(8,128)(2,1)S(1)}, u32[]{:S(2)}, u32[]{:S(2)}) collective-permute-start(bf16[64,2048]{1,0:T(8,128)(2,1)S(1)} %slice.158), channel_id=1, source_target_pairs={{0,2},{1,3},{2,0},{3,1},{4,6},{5,7},{6,4},{7,5},{8,10},{9,11},{10,... | collective-permute-start | bytes 786440 | tf_op jit(solution)/shard_map/ppermute | solution.py:35
  108.9 7.0 %collective-permute-done.29 = bf16[64,2048]{1,0:T(8,128)(2,1)S(1)} collective-permute-done((bf16[64,2048]{1,0:T(8,128)(2,1)S(1)}, bf16[64,2048]{1,0:T(8,128)(2,1)S(1)}, u32[]{:S(2)}, u32[]{:S(2)}) %collective-permute-start.29) | collective-permute-done | bytes 262176 | tf_op jit(solution)/shard_map/ppermute | solution.py:35
  116.0 1.9 %collective-permute-start.30 = (bf16[16,2048]{1,0:T(8,128)(2,1)S(1)}, bf16[16,2048]{1,0:T(8,128)(2,1)S(1)}, u32[]{:S(2)}, u32[]{:S(2)}) collective-permute-start(bf16[16,2048]{1,0:T(8,128)(2,1)S(1)} %get-tuple-element.95), channel_id=1, source_target_pairs={{0,12},{1,13},{2,14},{3,15},{4,0},{5,1},{6,2},{7,3},{8,4},{9,5},{1... | collective-permute-start | bytes 196616 | tf_op jit(solution)/shard_map/ppermute | solution.py:35
  119.2 1.6 %collective-permute-start.34 = (bf16[64,2048]{1,0:T(8,128)(2,1)S(1)}, bf16[64,2048]{1,0:T(8,128)(2,1)S(1)}, u32[]{:S(2)}, u32[]{:S(2)}) collective-permute-start(bf16[64,2048]{1,0:T(8,128)(2,1)S(1)} %slice.159), channel_id=1, source_target_pairs={{0,2},{1,3},{2,0},{3,1},{4,6},{5,7},{6,4},{7,5},{8,10},{9,11},{10,... | collective-permute-start | bytes 786440 | tf_op jit(solution)/shard_map/ppermute | solution.py:35
  120.8 3.2 %collective-permute-done.32 = bf16[16,2048]{1,0:T(8,128)(2,1)S(1)} collective-permute-done((bf16[16,2048]{1,0:T(8,128)(2,1)S(1)}, bf16[16,2048]{1,0:T(8,128)(2,1)S(1)}, u32[]{:S(2)}, u32[]{:S(2)}) %collective-permute-start.32) | collective-permute-done | bytes 65568 | tf_op jit(solution)/shard_map/ppermute | solution.py:35
  126.4 1.6 %collective-permute-start.38 = (bf16[64,2048]{1,0:T(8,128)(2,1)S(1)}, bf16[64,2048]{1,0:T(8,128)(2,1)S(1)}, u32[]{:S(2)}, u32[]{:S(2)}) collective-permute-start(bf16[64,2048]{1,0:T(8,128)(2,1)S(1)} %slice.157), channel_id=1, source_target_pairs={{0,2},{1,3},{2,0},{3,1},{4,6},{5,7},{6,4},{7,5},{8,10},{9,11},{10,... | collective-permute-start | bytes 786440 | tf_op jit(solution)/shard_map/ppermute | solution.py:35
  128.0 3.0 %collective-permute-start.35 = (bf16[16,2048]{1,0:T(8,128)(2,1)S(1)}, bf16[16,2048]{1,0:T(8,128)(2,1)S(1)}, u32[]{:S(2)}, u32[]{:S(2)}) collective-permute-start(bf16[16,2048]{1,0:T(8,128)(2,1)S(1)} %get-tuple-element.98), channel_id=1, source_target_pairs={{0,12},{1,13},{2,14},{3,15},{4,0},{5,1},{6,2},{7,3},{8,4},{9,5},{1... | collective-permute-start | bytes 196616 | tf_op jit(solution)/shard_map/ppermute | solution.py:35
  132.9 3.0 %collective-permute-start.39 = (bf16[16,2048]{1,0:T(8,128)(2,1)S(1)}, bf16[16,2048]{1,0:T(8,128)(2,1)S(1)}, u32[]{:S(2)}, u32[]{:S(2)}) collective-permute-start(bf16[16,2048]{1,0:T(8,128)(2,1)S(1)} %get-tuple-element.101), channel_id=1, source_target_pairs={{0,12},{1,13},{2,14},{3,15},{4,0},{5,1},{6,2},{7,3},{8,4},{9,5},{1... | collective-permute-start | bytes 196616 | tf_op jit(solution)/shard_map/ppermute | solution.py:35
  137.7 2.7 %collective-permute-done.36 = bf16[16,2048]{1,0:T(8,128)(2,1)S(1)} collective-permute-done((bf16[16,2048]{1,0:T(8,128)(2,1)S(1)}, bf16[16,2048]{1,0:T(8,128)(2,1)S(1)}, u32[]{:S(2)}, u32[]{:S(2)}) %collective-permute-start.36) | collective-permute-done | bytes 65568 | tf_op jit(solution)/shard_map/ppermute | solution.py:35
  140.4 1.7 %collective-permute-done.41 = bf16[16,2048]{1,0:T(8,128)(2,1)S(1)} collective-permute-done((bf16[16,2048]{1,0:T(8,128)(2,1)S(1)}, bf16[16,2048]{1,0:T(8,128)(2,1)S(1)}, u32[]{:S(2)}, u32[]{:S(2)}) %collective-permute-start.41) | collective-permute-done | bytes 65568 | tf_op jit(solution)/shard_map/ppermute | solution.py:35
  (135 shorter events, 27.5 us)
Async XLA Ops:
  2.0 19.9 %collective-permute-start.2 = (bf16[16,2176]{1,0:T(8,128)(2,1)}, bf16[16,2176]{1,0:T(8,128)(2,1)S(1)}, u32[]{:S(2)}, u32[]{:S(2)}) collective-permute-start(bf16[16,2176]{1,0:T(8,128)(2,1)} %get-tuple-element.45), channel_id=1, source_target_pairs={{0,12},{1,13},{2,14},{3,15},{4,0},{5,1},{6,2},{7,3},{8,4},{9,5},{1... | collective-permute-start | bytes 208904 | tf_op jit(solution)/shard_map/ppermute | solution.py:35
  7.0 15.5 %collective-permute-start.1 = (bf16[16,2176]{1,0:T(8,128)(2,1)}, bf16[16,2176]{1,0:T(8,128)(2,1)S(1)}, u32[]{:S(2)}, u32[]{:S(2)}) collective-permute-start(bf16[16,2176]{1,0:T(8,128)(2,1)} %get-tuple-element.45), channel_id=1, source_target_pairs={{0,8},{1,9},{2,10},{3,11},{4,12},{5,13},{6,14},{7,15},{8,0},{9,1},... | collective-permute-start | bytes 208904 | tf_op jit(solution)/shard_map/ppermute | solution.py:35
  7.0 9.9 %collective-permute-start.23 = (bf16[16,2176]{1,0:T(8,128)(2,1)}, bf16[16,2176]{1,0:T(8,128)(2,1)S(1)}, u32[]{:S(2)}, u32[]{:S(2)}) collective-permute-start(bf16[16,2176]{1,0:T(8,128)(2,1)} %get-tuple-element.53), channel_id=1, source_target_pairs={{0,12},{1,13},{2,14},{3,15},{4,0},{5,1},{6,2},{7,3},{8,4},{9,5},{1... | collective-permute-start | bytes 208904 | tf_op jit(solution)/shard_map/ppermute | solution.py:35
  7.5 11.0 %collective-permute-start.22 = (bf16[16,2176]{1,0:T(8,128)(2,1)}, bf16[16,2176]{1,0:T(8,128)(2,1)S(1)}, u32[]{:S(2)}, u32[]{:S(2)}) collective-permute-start(bf16[16,2176]{1,0:T(8,128)(2,1)} %get-tuple-element.53), channel_id=1, source_target_pairs={{0,8},{1,9},{2,10},{3,11},{4,12},{5,13},{6,14},{7,15},{8,0},{9,1},... | collective-permute-start | bytes 208904 | tf_op jit(solution)/shard_map/ppermute | solution.py:35
  9.9 10.9 %collective-permute-start.21 = (bf16[16,2176]{1,0:T(8,128)(2,1)}, bf16[16,2176]{1,0:T(8,128)(2,1)S(1)}, u32[]{:S(2)}, u32[]{:S(2)}) collective-permute-start(bf16[16,2176]{1,0:T(8,128)(2,1)} %get-tuple-element.53), channel_id=1, source_target_pairs={{0,4},{1,5},{2,6},{3,7},{4,8},{5,9},{6,10},{7,11},{8,12},{9,13},{1... | collective-permute-start | bytes 208904 | tf_op jit(solution)/shard_map/ppermute | solution.py:35
  22.5 8.2 %collective-permute-start.6 = (bf16[4,264,128]{2,1,0:T(8,128)(2,1)}, bf16[4,264,128]{2,1,0:T(8,128)(2,1)S(1)}, u32[]{:S(2)}, u32[]{:S(2)}) collective-permute-start(bf16[4,264,128]{2,1,0:T(8,128)(2,1)} %get-tuple-element.47), channel_id=1, source_target_pairs={{0,2},{1,3},{2,0},{3,1},{4,6},{5,7},{6,4},{7,5},{8,10},{9,11},{10,... | collective-permute-start | bytes 811016 | tf_op jit(solution)/shard_map/ppermute | solution.py:35
  24.0 30.7 %collective-permute-start.25 = (bf16[64,2176]{1,0:T(8,128)(2,1)S(1)}, bf16[64,2176]{1,0:T(8,128)(2,1)S(1)}, u32[]{:S(2)}, u32[]{:S(2)}) collective-permute-start(bf16[64,2176]{1,0:T(8,128)(2,1)S(1)} %bitcast.37), channel_id=1, source_target_pairs={{0,1},{1,0},{2,3},{3,2},{4,5},{5,4},{6,7},{7,6},{8,9},{9,8},{10,11... | collective-permute-start | bytes 835592 | tf_op jit(solution)/shard_map/ppermute | solution.py:35
  24.9 17.1 %collective-permute-start.24 = (bf16[64,2176]{1,0:T(8,128)(2,1)S(1)}, bf16[64,2176]{1,0:T(8,128)(2,1)S(1)}, u32[]{:S(2)}, u32[]{:S(2)}) collective-permute-start(bf16[64,2176]{1,0:T(8,128)(2,1)S(1)} %bitcast.38), channel_id=1, source_target_pairs={{0,2},{1,3},{2,0},{3,1},{4,6},{5,7},{6,4},{7,5},{8,10},{9,11},{10,... | collective-permute-start | bytes 835592 | tf_op jit(solution)/shard_map/ppermute | solution.py:35
  27.1 20.0 %collective-permute-start.4 = (bf16[64,2176]{1,0:T(8,128)(2,1)S(1)}, bf16[64,2176]{1,0:T(8,128)(2,1)S(1)}, u32[]{:S(2)}, u32[]{:S(2)}) collective-permute-start(bf16[64,2176]{1,0:T(8,128)(2,1)S(1)} %bitcast.41), channel_id=1, source_target_pairs={{0,1},{1,0},{2,3},{3,2},{4,5},{5,4},{6,7},{7,6},{8,9},{9,8},{10,11... | collective-permute-start | bytes 835592 | tf_op jit(solution)/shard_map/ppermute | solution.py:35
  28.2 13.8 %collective-permute-start.3 = (bf16[64,2176]{1,0:T(8,128)(2,1)S(1)}, bf16[64,2176]{1,0:T(8,128)(2,1)S(1)}, u32[]{:S(2)}, u32[]{:S(2)}) collective-permute-start(bf16[64,2176]{1,0:T(8,128)(2,1)S(1)} %bitcast.42), channel_id=1, source_target_pairs={{0,2},{1,3},{2,0},{3,1},{4,6},{5,7},{6,4},{7,5},{8,10},{9,11},{10,... | collective-permute-start | bytes 835592 | tf_op jit(solution)/shard_map/ppermute | solution.py:35
  30.7 16.3 %collective-permute-start.18 = (bf16[64,2176]{1,0:T(8,128)(2,1)S(1)}, bf16[64,2176]{1,0:T(8,128)(2,1)S(1)}, u32[]{:S(2)}, u32[]{:S(2)}) collective-permute-start(bf16[64,2176]{1,0:T(8,128)(2,1)S(1)} %bitcast.45), channel_id=1, source_target_pairs={{0,2},{1,3},{2,0},{3,1},{4,6},{5,7},{6,4},{7,5},{8,10},{9,11},{10,... | collective-permute-start | bytes 835592 | tf_op jit(solution)/shard_map/ppermute | solution.py:35
  42.1 15.6 %collective-permute-start.19 = (bf16[64,2176]{1,0:T(8,128)(2,1)S(1)}, bf16[64,2176]{1,0:T(8,128)(2,1)S(1)}, u32[]{:S(2)}, u32[]{:S(2)}) collective-permute-start(bf16[64,2176]{1,0:T(8,128)(2,1)S(1)} %bitcast.46), channel_id=1, source_target_pairs={{0,1},{1,0},{2,3},{3,2},{4,5},{5,4},{6,7},{7,6},{8,9},{9,8},{10,11... | collective-permute-start | bytes 835592 | tf_op jit(solution)/shard_map/ppermute | solution.py:35
  47.0 11.7 %collective-permute-start.20 = (bf16[64,2176]{1,0:T(8,128)(2,1)S(1)}, bf16[64,2176]{1,0:T(8,128)(2,1)S(1)}, u32[]{:S(2)}, u32[]{:S(2)}) collective-permute-start(bf16[64,2176]{1,0:T(8,128)(2,1)S(1)} %collective-permute-done.18.refs_1_), channel_id=1, source_target_pairs={{0,1},{1,0},{2,3},{3,2},{4,5},{5,4},{6,7},{7,6},{8,9},{9,8},{10,11... | collective-permute-start | bytes 835592 | tf_op jit(solution)/shard_map/ppermute | solution.py:35
  47.1 19.2 %collective-permute-start.7 = (bf16[2,264,128]{2,1,0:T(8,128)(2,1)S(1)}, bf16[2,264,128]{2,1,0:T(8,128)(2,1)S(1)}, u32[]{:S(2)}, u32[]{:S(2)}) collective-permute-start(bf16[2,264,128]{2,1,0:T(8,128)(2,1)S(1)} %pad_maximum_fusion.4), channel_id=1, source_target_pairs={{0,0},{1,1},{2,2},{3,3},{4,4},{5,5},{6,6},{7,7},{8,8},{9,9},{10,10... | collective-permute-start | bytes 405512 | tf_op jit(solution)/shard_map/ppermute | solution.py:86
  47.8 23.7 %collective-permute-start.26 = (bf16[64,2176]{1,0:T(8,128)(2,1)S(1)}, bf16[64,2176]{1,0:T(8,128)(2,1)S(1)}, u32[]{:S(2)}, u32[]{:S(2)}) collective-permute-start(bf16[64,2176]{1,0:T(8,128)(2,1)S(1)} %collective-permute-done.24.refs_1_), channel_id=1, source_target_pairs={{0,1},{1,0},{2,3},{3,2},{4,5},{5,4},{6,7},{7,6},{8,9},{9,8},{10,11... | collective-permute-start | bytes 835592 | tf_op jit(solution)/shard_map/ppermute | solution.py:35
  54.7 14.6 %collective-permute-start.8 = (bf16[2,264,128]{2,1,0:T(8,128)(2,1)S(1)}, bf16[2,264,128]{2,1,0:T(8,128)(2,1)S(1)}, u32[]{:S(2)}, u32[]{:S(2)}) collective-permute-start(bf16[2,264,128]{2,1,0:T(8,128)(2,1)S(1)} %pad_maximum_fusion.5), channel_id=1, source_target_pairs={{0,4},{1,5},{2,6},{3,7},{4,8},{5,9},{6,10},{7,11},{8,12},{9,13},{1... | collective-permute-start | bytes 405512 | tf_op jit(solution)/shard_map/ppermute | solution.py:86
  57.6 11.8 %collective-permute-start.9 = (bf16[2,264,128]{2,1,0:T(8,128)(2,1)S(1)}, bf16[2,264,128]{2,1,0:T(8,128)(2,1)S(1)}, u32[]{:S(2)}, u32[]{:S(2)}) collective-permute-start(bf16[2,264,128]{2,1,0:T(8,128)(2,1)S(1)} %pad_maximum_fusion.6), channel_id=1, source_target_pairs={{0,8},{1,9},{2,10},{3,11},{4,12},{5,13},{6,14},{7,15},{8,0},{9,1},... | collective-permute-start | bytes 405512 | tf_op jit(solution)/shard_map/ppermute | solution.py:86
  58.8 12.6 %collective-permute-start.10 = (bf16[2,264,128]{2,1,0:T(8,128)(2,1)S(1)}, bf16[2,264,128]{2,1,0:T(8,128)(2,1)S(1)}, u32[]{:S(2)}, u32[]{:S(2)}) collective-permute-start(bf16[2,264,128]{2,1,0:T(8,128)(2,1)S(1)} %pad_maximum_fusion.7), channel_id=1, source_target_pairs={{0,12},{1,13},{2,14},{3,15},{4,0},{5,1},{6,2},{7,3},{8,4},{9,5},{1... | collective-permute-start | bytes 405512 | tf_op jit(solution)/shard_map/ppermute | solution.py:86
  66.4 12.0 %collective-permute-start.11 = (bf16[2,264,128]{2,1,0:T(8,128)(2,1)S(1)}, bf16[2,264,128]{2,1,0:T(8,128)(2,1)S(1)}, u32[]{:S(2)}, u32[]{:S(2)}) collective-permute-start(bf16[2,264,128]{2,1,0:T(8,128)(2,1)S(1)} %collective-permute-done.7.refs_0_), channel_id=1, source_target_pairs={{0,16},{16,0},{1,17},{17,1},{2,18},{18,2},{3,19},{19,3},{4,20},{20... | collective-permute-start | bytes 405512 | tf_op jit(solution)/shard_map/ppermute | solution.py:88
  69.3 9.1 %collective-permute-start.12 = (bf16[2,264,128]{2,1,0:T(8,128)(2,1)S(1)}, bf16[2,264,128]{2,1,0:T(8,128)(2,1)S(1)}, u32[]{:S(2)}, u32[]{:S(2)}) collective-permute-start(bf16[2,264,128]{2,1,0:T(8,128)(2,1)S(1)} %collective-permute-done.8.refs_1_), channel_id=1, source_target_pairs={{0,16},{16,0},{1,17},{17,1},{2,18},{18,2},{3,19},{19,3},{4,20},{20... | collective-permute-start | bytes 405512 | tf_op jit(solution)/shard_map/ppermute | solution.py:88
  69.4 10.1 %collective-permute-start.13 = (bf16[2,264,128]{2,1,0:T(8,128)(2,1)S(1)}, bf16[2,264,128]{2,1,0:T(8,128)(2,1)S(1)}, u32[]{:S(2)}, u32[]{:S(2)}) collective-permute-start(bf16[2,264,128]{2,1,0:T(8,128)(2,1)S(1)} %collective-permute-done.9.refs_2_), channel_id=1, source_target_pairs={{0,16},{16,0},{1,17},{17,1},{2,18},{18,2},{3,19},{19,3},{4,20},{20... | collective-permute-start | bytes 405512 | tf_op jit(solution)/shard_map/ppermute | solution.py:88
  71.4 10.5 %collective-permute-start.14 = (bf16[2,264,128]{2,1,0:T(8,128)(2,1)S(1)}, bf16[2,264,128]{2,1,0:T(8,128)(2,1)S(1)}, u32[]{:S(2)}, u32[]{:S(2)}) collective-permute-start(bf16[2,264,128]{2,1,0:T(8,128)(2,1)S(1)} %collective-permute-done.10.refs_3_), channel_id=1, source_target_pairs={{0,16},{16,0},{1,17},{17,1},{2,18},{18,2},{3,19},{19,3},{4,20},{20... | collective-permute-start | bytes 405512 | tf_op jit(solution)/shard_map/ppermute | solution.py:88
  92.5 14.5 %collective-permute-start.28 = (bf16[128,2048]{1,0:T(8,128)(2,1)}, bf16[128,2048]{1,0:T(8,128)(2,1)S(1)}, u32[]{:S(2)}, u32[]{:S(2)}) collective-permute-start(bf16[128,2048]{1,0:T(8,128)(2,1)} %get-tuple-element.76), channel_id=1, source_target_pairs={{0,1},{1,0},{2,3},{3,2},{4,5},{5,4},{6,7},{7,6},{8,9},{9,8},{10,11... | collective-permute-start | bytes 1572872 | tf_op jit(solution)/shard_map/ppermute | solution.py:35
  99.4 9.3 %collective-permute-start.27 = (bf16[128,2048]{1,0:T(8,128)(2,1)}, bf16[128,2048]{1,0:T(8,128)(2,1)S(1)}, u32[]{:S(2)}, u32[]{:S(2)}) collective-permute-start(bf16[128,2048]{1,0:T(8,128)(2,1)} %get-tuple-element.72), channel_id=1, source_target_pairs={{0,1},{1,0},{2,3},{3,2},{4,5},{5,4},{6,7},{7,6},{8,9},{9,8},{10,11... | collective-permute-start | bytes 1572872 | tf_op jit(solution)/shard_map/ppermute | solution.py:35
  106.8 12.2 %collective-permute-start.33 = (bf16[128,2048]{1,0:T(8,128)(2,1)}, bf16[128,2048]{1,0:T(8,128)(2,1)S(1)}, u32[]{:S(2)}, u32[]{:S(2)}) collective-permute-start(bf16[128,2048]{1,0:T(8,128)(2,1)} %get-tuple-element.81), channel_id=1, source_target_pairs={{0,1},{1,0},{2,3},{3,2},{4,5},{5,4},{6,7},{7,6},{8,9},{9,8},{10,11... | collective-permute-start | bytes 1572872 | tf_op jit(solution)/shard_map/ppermute | solution.py:35
  107.2 8.7 %collective-permute-start.29 = (bf16[64,2048]{1,0:T(8,128)(2,1)S(1)}, bf16[64,2048]{1,0:T(8,128)(2,1)S(1)}, u32[]{:S(2)}, u32[]{:S(2)}) collective-permute-start(bf16[64,2048]{1,0:T(8,128)(2,1)S(1)} %slice.158), channel_id=1, source_target_pairs={{0,2},{1,3},{2,0},{3,1},{4,6},{5,7},{6,4},{7,5},{8,10},{9,11},{10,... | collective-permute-start | bytes 786440 | tf_op jit(solution)/shard_map/ppermute | solution.py:35
  118.1 7.1 %collective-permute-start.31 = (bf16[16,2048]{1,0:T(8,128)(2,1)S(1)}, bf16[16,2048]{1,0:T(8,128)(2,1)S(1)}, u32[]{:S(2)}, u32[]{:S(2)}) collective-permute-start(bf16[16,2048]{1,0:T(8,128)(2,1)S(1)} %get-tuple-element.97), channel_id=1, source_target_pairs={{0,8},{1,9},{2,10},{3,11},{4,12},{5,13},{6,14},{7,15},{8,0},{9,1},... | collective-permute-start | bytes 196616 | tf_op jit(solution)/shard_map/ppermute | solution.py:35
  119.2 7.1 %collective-permute-start.34 = (bf16[64,2048]{1,0:T(8,128)(2,1)S(1)}, bf16[64,2048]{1,0:T(8,128)(2,1)S(1)}, u32[]{:S(2)}, u32[]{:S(2)}) collective-permute-start(bf16[64,2048]{1,0:T(8,128)(2,1)S(1)} %slice.159), channel_id=1, source_target_pairs={{0,2},{1,3},{2,0},{3,1},{4,6},{5,7},{6,4},{7,5},{8,10},{9,11},{10,... | collective-permute-start | bytes 786440 | tf_op jit(solution)/shard_map/ppermute | solution.py:35
  128.0 8.3 %collective-permute-start.35 = (bf16[16,2048]{1,0:T(8,128)(2,1)S(1)}, bf16[16,2048]{1,0:T(8,128)(2,1)S(1)}, u32[]{:S(2)}, u32[]{:S(2)}) collective-permute-start(bf16[16,2048]{1,0:T(8,128)(2,1)S(1)} %get-tuple-element.98), channel_id=1, source_target_pairs={{0,12},{1,13},{2,14},{3,15},{4,0},{5,1},{6,2},{7,3},{8,4},{9,5},{1... | collective-permute-start | bytes 196616 | tf_op jit(solution)/shard_map/ppermute | solution.py:35
  131.3 9.0 %collective-permute-start.36 = (bf16[16,2048]{1,0:T(8,128)(2,1)S(1)}, bf16[16,2048]{1,0:T(8,128)(2,1)S(1)}, u32[]{:S(2)}, u32[]{:S(2)}) collective-permute-start(bf16[16,2048]{1,0:T(8,128)(2,1)S(1)} %get-tuple-element.100), channel_id=1, source_target_pairs={{0,8},{1,9},{2,10},{3,11},{4,12},{5,13},{6,14},{7,15},{8,0},{9,1},... | collective-permute-start | bytes 196616 | tf_op jit(solution)/shard_map/ppermute | solution.py:35
  132.9 7.5 %collective-permute-start.39 = (bf16[16,2048]{1,0:T(8,128)(2,1)S(1)}, bf16[16,2048]{1,0:T(8,128)(2,1)S(1)}, u32[]{:S(2)}, u32[]{:S(2)}) collective-permute-start(bf16[16,2048]{1,0:T(8,128)(2,1)S(1)} %get-tuple-element.101), channel_id=1, source_target_pairs={{0,12},{1,13},{2,14},{3,15},{4,0},{5,1},{6,2},{7,3},{8,4},{9,5},{1... | collective-permute-start | bytes 196616 | tf_op jit(solution)/shard_map/ppermute | solution.py:35
  136.3 7.1 %collective-permute-start.40 = (bf16[16,2048]{1,0:T(8,128)(2,1)S(1)}, bf16[16,2048]{1,0:T(8,128)(2,1)S(1)}, u32[]{:S(2)}, u32[]{:S(2)}) collective-permute-start(bf16[16,2048]{1,0:T(8,128)(2,1)S(1)} %get-tuple-element.103), channel_id=1, source_target_pairs={{0,8},{1,9},{2,10},{3,11},{4,12},{5,13},{6,14},{7,15},{8,0},{9,1},... | collective-permute-start | bytes 196616 | tf_op jit(solution)/shard_map/ppermute | solution.py:35
  (33 other events, 275.6 us)

commit v5 on v4

--- a/solution.py
+++ b/solution.py
@@ -35,39 +35,21 @@
     return lax.ppermute(x, "expert", pairs)
 
 
-def gather_rows(x, n):
-    outer, middle, cores = split_axis(n)
-    column = [x] + [shift(x, n, middle * cores, outer, k) for k in range(1, outer)]
-    column = jnp.stack(column).reshape(-1, x.shape[1])
-    sheet = [column] + [shift(column, n, cores, middle, k) for k in range(1, middle)]
-    return sheet + [shift(p, n, 1, cores, k) for k in range(1, cores) for p in sheet]
-
-
-def scatter_rows(parts, n):
-    outer, middle, cores = split_axis(n)
-    results, before = [], None
-    for kept, sent in parts:
-        count = kept.shape[0] // middle
-        kept = kept + shift(sent, n, 1, cores, 1).astype(jnp.float32)
-        away = kept[count:].astype(jnp.bfloat16)
-        if before is not None:
-            away, before = lax.optimization_barrier((away, before))
-            results[-1] = before
-        total = kept[:count]
-        for k in range(1, middle):
-            part = away[(k - 1) * count : k * count]
-            total = total + shift(part, n, cores, middle, middle - k).astype(jnp.float32)
-        results.append(total)
-        before = total
-    finals = []
-    for kept in results:
-        count = kept.shape[0] // outer
-        total = kept[:count]
-        for k in range(1, outer):
-            part = kept[k * count : (k + 1) * count].astype(jnp.bfloat16)
-            total = total + shift(part, n, middle * cores, outer, outer - k).astype(jnp.float32)
-        finals.append(total.astype(jnp.bfloat16))
-    return finals
+def stack_rows(pieces):
+    return jnp.stack(pieces).reshape(-1, pieces[0].shape[1])
+
+
+def gather_along(x, n, stride, size):
+    return stack_rows([x] + [shift(x, n, stride, size, k) for k in range(1, size)])
+
+
+def scatter_along(total, n, stride, size):
+    count = total.shape[0] // size
+    result = total[:count]
+    for k in range(1, size):
+        part = total[k * count : (k + 1) * count].astype(jnp.bfloat16)
+        result = result + shift(part, n, stride, size, size - k).astype(jnp.float32)
+    return result
 
 
 def exchange_factors(blocks, n):
@@ -108,18 +90,23 @@
             dense += jnp.where(ids[k : k + 1, :] == expert, gates[k : k + 1, :], 0.0)
         turned_ref[:, s * rows : (s + 1) * rows] = dense
     dense = turned_ref[...].T.astype(jnp.bfloat16)
-    for s, out_ref in enumerate(out_refs):
-        out_ref[:, :width] = hidden_ref[s]
-        out_ref[:, width:] = dense[s * rows : (s + 1) * rows, :]
-
-
-def make_payload(hidden, route_ids, route_logits, experts):
+    s = 0
+    for out_ref in out_refs:
+        for at in range(0, out_ref.shape[0], rows):
+            out_ref[at : at + rows, :width] = hidden_ref[s]
+            out_ref[at : at + rows, width:] = dense[s * rows : (s + 1) * rows, :]
+            s += 1
+
+
+def make_payload(hidden, route_ids, route_logits, experts, first):
     steps, rows, width = hidden.shape
     padded = -(-experts // LANES) * LANES
-    shape = jax.ShapeDtypeStruct((rows, width + padded), jnp.bfloat16)
     return pl.pallas_call(
         payload_kernel,
-        out_shape=[shape] * steps,
+        out_shape=[
+            jax.ShapeDtypeStruct((count * rows, width + padded), jnp.bfloat16)
+            for count in (first, steps - first)
+        ],
         scratch_shapes=[pltpu.VMEM((padded, -(-steps * rows // LANES) * LANES), jnp.float32)],
         compiler_params=pltpu.CompilerParams(vmem_limit_bytes=GRANT),
         name="payload",
@@ -246,117 +233,111 @@
     )(place, *here, *there)
 
 
-def fill_rows(pieces, x_ref):
-    rows, width = pieces[0].shape[0], x_ref.shape[1]
-    for i, piece in enumerate(pieces):
-        x_ref[i * rows : (i + 1) * rows, :] = piece[:, :width]
-
-
-def base_kernel(count, *refs):
-    pieces = refs[:count]
-    w_gate_ref, w_up_ref, gate_ref, up_ref, x_ref = refs[count:]
-
-    @pl.when(pl.program_id(0) == 0)
-    def _():
-        fill_rows(pieces, x_ref)
-
-    gate_ref[...] = dot(x_ref[...], w_gate_ref[...])
-    up_ref[...] = dot(x_ref[...], w_up_ref[...])
-
-
-def base_products(pieces, w_gate, w_up):
-    width, units = w_gate.shape
+def expert_kernel(count, place_ref, *refs):
+    pieces, refs = refs[:count], refs[count:]
+    a_gu_hbm, gate_b_hbm, up_b_hbm, down_a_hbm, down_b_hbm = refs[:5]
+    w_gate_hbm, w_up_hbm, w_down_hbm, kept_hbm, sent_hbm = refs[5:10]
+    x_ref, a_gu_ref, gate_b_ref, up_b_ref, down_a_ref, down_b_ref = refs[10:16]
+    w_gate_ref, w_up_ref, w_down_ref, inner_ref, kept_ref, sent_ref, sem, out_sem = refs[16:]
+    rows = pieces[0].shape[0]
+    units, width = w_down_ref.shape
+    rank = gate_b_ref.shape[0]
+    own = kept_ref.shape[0]
+    begun = []
+
+    def begin(src, dst):
+        copy = pltpu.make_async_copy(src, dst, sem.at[len(begun)])
+        copy.start()
+        begun.append(copy)
+        return copy
+
+    def blocks(length, block):
+        return [slice(at, at + block) for at in range(0, length, block)]
+
+    x_in = [begin(p, x_ref.at[pl.ds(i * rows, rows)]) for i, p in enumerate(pieces)]
+    x_in.append(begin(a_gu_hbm, a_gu_ref))
+    b_in = [begin(gate_b_hbm, gate_b_ref), begin(up_b_hbm, up_b_ref)]
+    unit_cuts, width_cuts = blocks(units, 256), blocks(width, 512 if width % 512 == 0 else 256)
+    gu_in = [
+        (
+            begin(w_gate_hbm.at[:, cut], w_gate_ref.at[:, cut]),
+            begin(w_up_hbm.at[:, cut], w_up_ref.at[:, cut]),
+        )
+        for cut in unit_cuts
+    ]
+    d_in = [begin(down_a_hbm, down_a_ref), begin(down_b_hbm, down_b_ref)]
+    down_in = [begin(w_down_hbm.at[:, cut], w_down_ref.at[:, cut]) for cut in width_cuts]
+
+    for copy in x_in:
+        copy.wait()
+    gates = x_ref[:, width:].astype(jnp.float32)
+    lane = lax.broadcasted_iota(jnp.int32, gates.shape, 1)
+    mine = jnp.sum(jnp.where(lane == place_ref[1], gates, 0.0), axis=1, keepdims=True)
+    x = x_ref[:, :width]
+    low = (adapter_scale * dot(x, a_gu_ref[...])).astype(jnp.bfloat16)
+    for copy in b_in:
+        copy.wait()
+    for cut, (gate_in, up_in) in zip(unit_cuts, gu_in):
+        gate_in.wait()
+        g = dot(x, w_gate_ref[:, cut]) + dot(low[:, :rank], gate_b_ref[:, cut])
+        up_in.wait()
+        u = dot(x, w_up_ref[:, cut]) + dot(low[:, rank:], up_b_ref[:, cut])
+        inner_ref[:, cut] = (g / (1.0 + jnp.exp(-g)) * u).astype(jnp.bfloat16)
+    for copy in d_in:
+        copy.wait()
+    inner = inner_ref[...]
+    low = (adapter_scale * dot(inner, down_a_ref[...])).astype(jnp.bfloat16)[:, :rank]
+    out_copies = []
+    for i, (cut, copy) in enumerate(zip(width_cuts, down_in)):
+        copy.wait()
+        out = dot(inner, w_down_ref[:, cut]) + dot(low, down_b_ref[:, cut])
+        out = out * mine
+        sent_ref[:, cut] = out[own:].astype(jnp.bfloat16)
+        kept_ref[:, cut] = out[:own]
+        for j, (src, dst) in enumerate(((sent_ref, sent_hbm), (kept_ref, kept_hbm))):
+            copy = pltpu.make_async_copy(src.at[:, cut], dst.at[:, cut], out_sem.at[2 * i + j])
+            copy.start()
+            out_copies.append(copy)
+    for copy in out_copies:
+        copy.wait()
+
+
+def run_expert(place, pieces, low_rank, w_gate, w_up, w_down):
+    units, width = w_down.shape
     total = sum(p.shape[0] for p in pieces)
-    block = 256 if units % 256 == 0 else units
-    out = jax.ShapeDtypeStruct((total, units), jnp.float32)
-    return pl.pallas_call(
-        functools.partial(base_kernel, len(pieces)),
-        grid=(units // block,),
-        out_shape=[out, out],
-        in_specs=[pl.BlockSpec(p.shape, lambda i: (0, 0)) for p in pieces]
-        + [pl.BlockSpec((width, block), lambda i: (0, i))] * 2,
-        out_specs=[pl.BlockSpec((total, block), lambda i: (0, i))] * 2,
-        scratch_shapes=[pltpu.VMEM((total, width), jnp.bfloat16)],
-        compiler_params=pltpu.CompilerParams(vmem_limit_bytes=GRANT),
-        cost_estimate=pl.CostEstimate(
-            flops=4 * total * width * units,
-            bytes_accessed=4 * width * units + 2 * total * width + 8 * total * units,
-            transcendentals=0,
-        ),
-        name="base_products",
-    )(*pieces, w_gate, w_up)
-
-
-def finish_kernel(count, place_ref, *refs):
-    pieces = refs[:count]
-    (gate_ref, up_ref, a_gu_ref, gate_b_ref, up_b_ref, down_a_ref, down_b_ref, w_down_ref) = refs[
-        count : count + 8
-    ]
-    out_refs = refs[count + 8 : -4]
-    x_ref, inner_ref, low_ref, mine_ref = refs[-4:]
-    rank = gate_b_ref.shape[0]
-    rows, width = pieces[0].shape[0], x_ref.shape[1]
-
-    @pl.when(pl.program_id(0) == 0)
-    def _():
-        fill_rows(pieces, x_ref)
-        for i, piece in enumerate(pieces):
-            gates = piece[:, width:].astype(jnp.float32)
-            lane = lax.broadcasted_iota(jnp.int32, gates.shape, 1)
-            own = jnp.sum(jnp.where(lane == place_ref[1], gates, 0.0), axis=1, keepdims=True)
-            mine_ref[i * rows : (i + 1) * rows, :] = jnp.broadcast_to(own, (rows, LANES))
-        low = (adapter_scale * dot(x_ref[...], a_gu_ref[...])).astype(jnp.bfloat16)
-        g = gate_ref[...] + dot(low[:, :rank], gate_b_ref[...])
-        u = up_ref[...] + dot(low[:, rank:], up_b_ref[...])
-        inner = (g / (1.0 + jnp.exp(-g)) * u).astype(jnp.bfloat16)
-        inner_ref[...] = inner
-        low_ref[...] = (adapter_scale * dot(inner, down_a_ref[...])).astype(jnp.bfloat16)
-
-    out = dot(inner_ref[...], w_down_ref[...]) + dot(low_ref[:, :rank], down_b_ref[...])
-    out = out * mine_ref[:, :1]
-    at = 0
-    for out_ref in out_refs:
-        n = out_ref.shape[0]
-        out_ref[...] = out[at : at + n].astype(out_ref.dtype)
-        at += n
-
-
-def finish_step(place, pieces, gate, up, low_rank, w_down, cores):
-    units, width = w_down.shape
-    total = gate.shape[0]
-    block = 512 if width % 512 == 0 else width
-    own = total // cores
-    outs = [jax.ShapeDtypeStruct((own, width), jnp.float32)]
-    if cores > 1:
-        outs.append(jax.ShapeDtypeStruct((total - own, width), jnp.bfloat16))
+    own = total // 2
     a_gu, gate_b, up_b, down_a, down_b = low_rank
     rank = down_b.shape[0]
-    whole = [*pieces, gate, up, a_gu, gate_b, up_b, down_a]
+    outs = [
+        jax.ShapeDtypeStruct((own, width), jnp.float32),
+        jax.ShapeDtypeStruct((total - own, width), jnp.bfloat16),
+    ]
+    kept = [a_gu, gate_b, up_b, down_a, down_b, w_gate, w_up, w_down]
+    width_block = 512 if width % 512 == 0 else 256
+    copies = len(pieces) + 5 + 2 * (units // 256) + width // width_block
     return pl.pallas_call(
-        functools.partial(finish_kernel, len(pieces)),
-        grid=(width // block,),
+        functools.partial(expert_kernel, len(pieces)),
         out_shape=outs,
         in_specs=[pl.BlockSpec(memory_space=pltpu.SMEM)]
-        + [pl.BlockSpec(a.shape, lambda i: (0, 0)) for a in whole]
+        + [pl.BlockSpec(memory_space=pl.ANY)] * (len(pieces) + len(kept)),
+        out_specs=[pl.BlockSpec(memory_space=pl.ANY)] * 2,
+        scratch_shapes=[pltpu.VMEM((total, pieces[0].shape[1]), jnp.bfloat16)]
+        + [pltpu.VMEM(a.shape, a.dtype) for a in kept]
         + [
-            pl.BlockSpec((rank, block), lambda i: (0, i)),
-            pl.BlockSpec((units, block), lambda i: (0, i)),
-        ],
-        out_specs=[pl.BlockSpec((o.shape[0], block), lambda i: (0, i)) for o in outs],
-        scratch_shapes=[
-            pltpu.VMEM((total, width), jnp.bfloat16),
             pltpu.VMEM((total, units), jnp.bfloat16),
-            pltpu.VMEM((total, down_a.shape[1]), jnp.bfloat16),
-            pltpu.VMEM((total, LANES), jnp.float32),
+            pltpu.VMEM(outs[0].shape, outs[0].dtype),
+            pltpu.VMEM(outs[1].shape, outs[1].dtype),
+            pltpu.SemaphoreType.DMA((copies,)),
+            pltpu.SemaphoreType.DMA((2 * (width // width_block),)),
         ],
         compiler_params=pltpu.CompilerParams(vmem_limit_bytes=GRANT),
         cost_estimate=pl.CostEstimate(
-            flops=2 * total * units * (width + 4 * rank) + 4 * total * width * rank,
-            bytes_accessed=2 * units * width + 8 * total * width + 8 * total * units,
+            flops=2 * total * units * (3 * width + 4 * rank) + 8 * total * width * rank,
+            bytes_accessed=6 * units * width + 5 * total * width,
             transcendentals=total * units,
         ),
-        name="finish_step",
-    )(place, *whole, down_b, w_down)
+        name="run_expert",
+    )(place, *pieces, *kept)
 
 
 def dense_shards(
@@ -367,21 +348,32 @@
     steps, rows, width = hidden.shape
     units = w_gate.shape[2]
     rank = factors.shape[1] * owners // (3 * (width + units))
-    cores = split_axis(owners)[2]
+    outer, middle, cores = split_axis(owners)
+    along_outer, along_middle = (middle * cores, outer), (cores, middle)
     place = jnp.stack([lax.axis_index("group"), lax.axis_index("expert")]).astype(jnp.int32)
 
-    payload = make_payload(hidden, route_ids, route_logits, experts)
+    first = max(1, steps * 2 // 3)
+    head, tail = make_payload(hidden, route_ids, route_logits, experts, first)
+    tail = gather_along(tail, owners, *along_middle)
+    head = gather_along(head, owners, *along_outer)
     blocks = order_factors(place, placement, factors, owners)
-    gathered = [gather_rows(payload[s], owners) for s in range(steps)]
     here, there = exchange_factors(blocks, owners)
-    base = [base_products(pieces, w_gate[0], w_up[0]) for pieces in gathered]
-    here, there, base = lax.optimization_barrier((here, there, base))
+    heads = [head] + [shift(head, owners, *along_middle, k) for k in range(1, middle)]
+    heads += [shift(p, owners, 1, cores, 1) for p in heads]
+    tail = gather_along(tail, owners, *along_outer)
+    tails = [tail, shift(tail, owners, 1, cores, 1)]
+
     low_rank = relayout_factors(place, here, there, width, units, rank, owners)
-    parts = [
-        finish_step(place, pieces, gate, up, low_rank, down_weight[0], cores)
-        for pieces, (gate, up) in zip(gathered, base)
-    ]
-    return jnp.stack(scatter_rows(parts, owners), axis=0)
+    weights = (w_gate[0], w_up[0], down_weight[0])
+    head, head_sent = run_expert(place, heads, low_rank, *weights)
+    tail, tail_sent = run_expert(place, tails, low_rank, *weights)
+    head = head + shift(head_sent, owners, 1, cores, 1).astype(jnp.float32)
+    tail = tail + shift(tail_sent, owners, 1, cores, 1).astype(jnp.float32)
+    head = scatter_along(head, owners, *along_middle)
+    tail = scatter_along(tail, owners, *along_outer)
+    head = scatter_along(head, owners, *along_outer)
+    tail = scatter_along(tail, owners, *along_middle)
+    return jnp.concatenate([head, tail]).astype(jnp.bfloat16).reshape(steps, rows, width)
 
 
 def row_capacity(rows, top, experts):
@@ -484,7 +476,7 @@
     dense = row_capacity(rows, top, placement.shape[0]) == rows
     dense = dense and lax.axis_size("group") == 2 and split_axis(owners)[2] == 2
     dense = dense and 2 * rank == LANES and width % 256 == 0 and units % 256 == 0
-    dense = dense and factors.shape[1] % (8 * LANES) == 0
+    dense = dense and factors.shape[1] % (8 * LANES) == 0 and hidden.shape[0] > 1
     return (dense_shards if dense else sparse_shards)(
         hidden, route_ids, route_logits, placement, factors, w_gate, w_up, down_weight
     )

time: 145 us -> 128 us (0.88)
  Pallas kernels: 47.4 us -> 36.3 us
  starting transfers between devices: 50.4 us -> 40.8 us
  waiting for transfers between devices: 38.4 us -> 42.5 us
    ppermute x34 -> x22, starting transfers between devices: 39.1 us -> 27.9 us  [shift(): return lax.ppermute(x, 'expert', pairs)]
    pallas_call x7 -> x3, Pallas kernels: 41 us -> 29.8 us  [the longest x2 27.9 us: run_expert(): pl.pallas_call(functools.partial(expert_kernel, len(pieces)), out_shape=o...]
    ppermute x34 -> x22, waiting for transfers between devices: 34.9 us -> 26.3 us  [shift(): return lax.ppermute(x, 'expert', pairs)]
    ppermute x4, waiting for transfers between devices: 0.01 us -> 7.31 us  [exchange_factors(): part = lax.ppermute(part, ('group', 'expert'), pairs)]
    ppermute x4, waiting for transfers between devices: 3.51 us -> 8.96 us  [exchange_factors(): there.append(lax.ppermute(part, 'group', [(0, 1), (1, 0)]))]
    another operation x10 -> x7, other arithmetic: 3.71 us -> 2.37 us  [the longest x3 1.98 us: stack_rows(): return jnp.stack(pieces).reshape(-1, pieces[0].shape[1])]
  transfers between devices with their start and end apart: 42 -> 30, of which waited for: 15 -> 13; matrix products, arithmetic and copies ran while one was open for 4% -> 4% of each run, Pallas kernels for 25% -> 27%
where the time goes in v5:
time: 128 us
  waiting for transfers between devices  42.5 us (33%)
  starting transfers between devices  40.8 us (32%)
  Pallas kernels  36.3 us (28%)
  other arithmetic  4.19 us (3%)
  local copies, waits for them, and re-layouts  3.45 us (3%)
    ppermute x22, starting transfers between devices, shift(): return lax.ppermute(x, 'expert', pairs)  27.9 us
    pallas_call x2, Pallas kernels, run_expert(): pl.pallas_call(functools.partial(expert_kernel, len(pieces)), out_shape=o...  27.9 us
    ppermute x22, waiting for transfers between devices, shift(): return lax.ppermute(x, 'expert', pairs)  26.3 us
    ppermute x4, waiting for transfers between devices, exchange_factors(): there.append(lax.ppermute(part, 'group', [(0, 1), (1, 0)]))  8.96 us
    ppermute x4, waiting for transfers between devices, exchange_factors(): part = lax.ppermute(part, ('group', 'expert'), pairs)  7.31 us
    ppermute x4, starting transfers between devices, exchange_factors(): part = lax.ppermute(part, ('group', 'expert'), pairs)  6.5 us
    ppermute x4, starting transfers between devices, exchange_factors(): there.append(lax.ppermute(part, 'group', [(0, 1), (1, 0)]))  6.41 us
    pallas_call x1, Pallas kernels, order_factors(): pl.pallas_call(functools.partial(order_kernel, outer, middle), out_shape=...  3.35 us
  transfers between devices with their start and end apart: 30, of which 13 were waited for; matrix products, arithmetic and copies ran while one was open for 4% of the time, Pallas kernels for 27%

profile of v5, /device:TPU:0, one launch (start us, length us, event | category | flops | bytes accessed | tf_op | source)
XLA Modules:
  0.0 127.6 jit_solution(15726067437654694934)
XLA Ops:
  0.0 2.0 %payload.1 = (bf16[32,2176]{1,0:T(8,128)(2,1)}, bf16[16,2176]{1,0:T(8,128)(2,1)}) custom-call(bf16[3,16,2048]{2,1,0:T(8,128)(2,1)} %hidden_ref.1, s32[3,8,16]{2,1,0:T(8,128)} %bitcast.45, f32[3,8,16]{2,1,0:T(8,128)} %bitcast.46), custom_call_target="tpu_custom_call" | custom-call | tf_op jit(solution)/shard_map/payload/pallas_call | solution.py:104
  2.0 5.0 %collective-permute-start.2 = (bf16[32,2176]{1,0:T(8,128)(2,1)}, bf16[32,2176]{1,0:T(8,128)(2,1)S(1)}, u32[]{:S(2)}, u32[]{:S(2)}) collective-permute-start(bf16[32,2176]{1,0:T(8,128)(2,1)} %get-tuple-element.18), channel_id=1, source_target_pairs={{0,12},{1,13},{2,14},{3,15},{4,0},{5,1},{6,2},{7,3},{8,4},{9,5},{1... | collective-permute-start | bytes 417800 | tf_op jit(solution)/shard_map/ppermute | solution.py:35
  8.0 1.5 %collective-permute-start.20 = (bf16[16,2176]{1,0:T(8,128)(2,1)}, bf16[16,2176]{1,0:T(8,128)(2,1)S(1)}, u32[]{:S(2)}, u32[]{:S(2)}) collective-permute-start(bf16[16,2176]{1,0:T(8,128)(2,1)} %get-tuple-element.28), channel_id=1, source_target_pairs={{0,2},{1,3},{2,0},{3,1},{4,6},{5,7},{6,4},{7,5},{8,10},{9,11},{10,... | collective-permute-start | bytes 208904 | tf_op jit(solution)/shard_map/ppermute | solution.py:35
  10.2 3.4 %order_factors.1 = (bf16[4,264,128]{2,1,0:T(8,128)(2,1)}, bf16[4,264,128]{2,1,0:T(8,128)(2,1)}) custom-call(s32[2]{0:T(128)} %pad_add_fusion.place_ref, s32[16]{0:T(128)} %placement_ref.1, bf16[16,33792]{1,0:T(8,128)(2,1)} %factors_ref.1), custom_call_target="tpu_custom_call" | custom-call | tf_op jit(solution)/shard_map/order_factors/pallas_call | solution.py:151
  16.0 2.9 %collective-permute-start.23 = (bf16[32,2176]{1,0:T(8,128)(2,1)S(1)}, bf16[32,2176]{1,0:T(8,128)(2,1)S(1)}, u32[]{:S(2)}, u32[]{:S(2)}) collective-permute-start(bf16[32,2176]{1,0:T(8,128)(2,1)S(1)} %bitcast.29), channel_id=1, source_target_pairs={{0,12},{1,13},{2,14},{3,15},{4,0},{5,1},{6,2},{7,3},{8,4},{9,5},{1... | collective-permute-start | bytes 417800 | tf_op jit(solution)/shard_map/ppermute | solution.py:35
  18.8 1.1 collective-permute-start.22
  21.0 1.6 %collective-permute-start.3 = (bf16[128,2176]{1,0:T(8,128)(2,1)S(1)}, bf16[128,2176]{1,0:T(8,128)(2,1)S(1)}, u32[]{:S(2)}, u32[]{:S(2)}) collective-permute-start(bf16[128,2176]{1,0:T(8,128)(2,1)S(1)} %bitcast.33), channel_id=1, source_target_pairs={{0,2},{1,3},{2,0},{3,1},{4,6},{5,7},{6,4},{7,5},{8,10},{9,11},{10,... | collective-permute-start | bytes 1671176 | tf_op jit(solution)/shard_map/ppermute | solution.py:35
  23.0 8.0 %collective-permute-done.22 = bf16[32,2176]{1,0:T(8,128)(2,1)S(1)} collective-permute-done((bf16[32,2176]{1,0:T(8,128)(2,1)S(1)}, bf16[32,2176]{1,0:T(8,128)(2,1)S(1)}, u32[]{:S(2)}, u32[]{:S(2)}) %collective-permute-start.22) | collective-permute-done | bytes 139296 | tf_op jit(solution)/shard_map/ppermute | solution.py:35
  32.8 2.0 %collective-permute-start.9 = (bf16[2,264,128]{2,1,0:T(8,128)(2,1)S(1)}, bf16[2,264,128]{2,1,0:T(8,128)(2,1)S(1)}, u32[]{:S(2)}, u32[]{:S(2)}) collective-permute-start(bf16[2,264,128]{2,1,0:T(8,128)(2,1)S(1)} %pad_maximum_fusion.6), channel_id=1, source_target_pairs={{0,8},{1,9},{2,10},{3,11},{4,12},{5,13},{6,14},{7,15},{8,0},{9,1},... | collective-permute-start | bytes 405512 | tf_op jit(solution)/shard_map/ppermute | solution.py:68
  34.9 3.0 %collective-permute-start.10 = (bf16[2,264,128]{2,1,0:T(8,128)(2,1)S(1)}, bf16[2,264,128]{2,1,0:T(8,128)(2,1)S(1)}, u32[]{:S(2)}, u32[]{:S(2)}) collective-permute-start(bf16[2,264,128]{2,1,0:T(8,128)(2,1)S(1)} %pad_maximum_fusion.7), channel_id=1, source_target_pairs={{0,12},{1,13},{2,14},{3,15},{4,0},{5,1},{6,2},{7,3},{8,4},{9,5},{1... | collective-permute-start | bytes 405512 | tf_op jit(solution)/shard_map/ppermute | solution.py:68
  37.8 2.5 %collective-permute-done.8.refs_1_ = bf16[2,264,128]{2,1,0:T(8,128)(2,1)S(1)} collective-permute-done((bf16[2,264,128]{2,1,0:T(8,128)(2,1)S(1)}, bf16[2,264,128]{2,1,0:T(8,128)(2,1)S(1)}, u32[]{:S(2)}, u32[]{:S(2)}) %collective-permute-start.8) | collective-permute-done | bytes 135200 | tf_op jit(solution)/shard_map/ppermute | solution.py:68
  40.8 4.8 %collective-permute-done.9.refs_2_ = bf16[2,264,128]{2,1,0:T(8,128)(2,1)S(1)} collective-permute-done((bf16[2,264,128]{2,1,0:T(8,128)(2,1)S(1)}, bf16[2,264,128]{2,1,0:T(8,128)(2,1)S(1)}, u32[]{:S(2)}, u32[]{:S(2)}) %collective-permute-start.9) | collective-permute-done | bytes 135200 | tf_op jit(solution)/shard_map/ppermute | solution.py:68
  45.6 2.3 %collective-permute-start.11 = (bf16[2,264,128]{2,1,0:T(8,128)(2,1)S(1)}, bf16[2,264,128]{2,1,0:T(8,128)(2,1)S(1)}, u32[]{:S(2)}, u32[]{:S(2)}) collective-permute-start(bf16[2,264,128]{2,1,0:T(8,128)(2,1)S(1)} %collective-permute-done.7.refs_0_), channel_id=1, source_target_pairs={{0,16},{16,0},{1,17},{17,1},{2,18},{18,2},{3,19},{19,3},{4,20},{20... | collective-permute-start | bytes 405512 | tf_op jit(solution)/shard_map/ppermute | solution.py:70
  48.0 4.3 %collective-permute-done.11.refs_4_ = bf16[2,264,128]{2,1,0:T(8,128)(2,1)S(1)} collective-permute-done((bf16[2,264,128]{2,1,0:T(8,128)(2,1)S(1)}, bf16[2,264,128]{2,1,0:T(8,128)(2,1)S(1)}, u32[]{:S(2)}, u32[]{:S(2)}) %collective-permute-start.11) | collective-permute-done | bytes 135200 | tf_op jit(solution)/shard_map/ppermute | solution.py:70
  52.4 2.0 %collective-permute-start.13 = (bf16[2,264,128]{2,1,0:T(8,128)(2,1)S(1)}, bf16[2,264,128]{2,1,0:T(8,128)(2,1)S(1)}, u32[]{:S(2)}, u32[]{:S(2)}) collective-permute-start(bf16[2,264,128]{2,1,0:T(8,128)(2,1)S(1)} %collective-permute-done.9.refs_2_), channel_id=1, source_target_pairs={{0,16},{16,0},{1,17},{17,1},{2,18},{18,2},{3,19},{19,3},{4,20},{20... | collective-permute-start | bytes 405512 | tf_op jit(solution)/shard_map/ppermute | solution.py:70
  55.3 2.0 %collective-permute-start.14 = (bf16[2,264,128]{2,1,0:T(8,128)(2,1)S(1)}, bf16[2,264,128]{2,1,0:T(8,128)(2,1)S(1)}, u32[]{:S(2)}, u32[]{:S(2)}) collective-permute-start(bf16[2,264,128]{2,1,0:T(8,128)(2,1)S(1)} %collective-permute-done.10.refs_3_), channel_id=1, source_target_pairs={{0,16},{16,0},{1,17},{17,1},{2,18},{18,2},{3,19},{19,3},{4,20},{20... | collective-permute-start | bytes 405512 | tf_op jit(solution)/shard_map/ppermute | solution.py:70
  58.3 2.7 %collective-permute-done.14.refs_7_ = bf16[2,264,128]{2,1,0:T(8,128)(2,1)S(1)} collective-permute-done((bf16[2,264,128]{2,1,0:T(8,128)(2,1)S(1)}, bf16[2,264,128]{2,1,0:T(8,128)(2,1)S(1)}, u32[]{:S(2)}, u32[]{:S(2)}) %collective-permute-start.14) | collective-permute-done | bytes 135200 | tf_op jit(solution)/shard_map/ppermute | solution.py:70
  61.7 3.1 %relayout_factors.1 = (bf16[2048,128]{1,0:T(8,128)(2,1)}, bf16[64,768]{1,0:T(8,128)(2,1)}, bf16[64,768]{1,0:T(8,128)(2,1)}, bf16[768,128]{1,0:T(8,128)(2,1)}, bf16[64,2048]{1,0:T(8,128)(2,1)}) custom-call(s32[2]{0:T(128)} %pad_add_fusion.place_ref, bf16[2,264,128]{2,1,0:T(8,128)(2,1)} %copy-done.5, bf16[2,264,128]{2,1,0:T(8,128)(2,1)} %copy-done.6, ...), custom_call_target="tpu_custom_call" | custom-call | tf_op jit(solution)/shard_map/relayout_factors/pallas_call | solution.py:222
  65.7 9.9 %run_expert.3 = (f32[128,2048]{1,0:T(8,128)}, bf16[128,2048]{1,0:T(8,128)(2,1)}) custom-call(s32[2]{0:T(128)} %pad_add_fusion.place_ref, bf16[128,2176]{1,0:T(8,128)(2,1)} %bitcast.28, bf16[128,2176]{1,0:T(8,128)(2,1)} %copy-done.3, bf16[2048,128]{1,0:T(8,128)(2,1)} %get-tuple-element.21.refs_4_.refs_2_, bf16[64,768]{1,0:T(8,128)(2,1)} %get-tuple-element.22.refs_5_.refs_3_, ...), custom_call_target="tpu_custom_call" | custom-call | flops 2785017856 | bytes 12058624 | tf_op jit(solution)/shard_map/run_expert/pallas_call | solution.py:318
  76.6 18.0 %run_expert.2 = (f32[256,2048]{1,0:T(8,128)}, bf16[256,2048]{1,0:T(8,128)(2,1)}) custom-call(s32[2]{0:T(128)} %pad_add_fusion.place_ref, bf16[128,2176]{1,0:T(8,128)(2,1)} %bitcast.35, bf16[128,2176]{1,0:T(8,128)(2,1)} %copy-done.13, bf16[128,2176]{1,0:T(8,128)(2,1)} %copy-done.14, bf16[128,2176]{1,0:T(8,128)(2,1)} %collective-permute-done.5.refs_3_, ...), custom_call_target="tpu_custom_call" | custom-call | flops 5570035712 | bytes 14680064 | tf_op jit(solution)/shard_map/run_expert/pallas_call | solution.py:318
  95.3 2.0 %collective-permute-start.28 = (bf16[32,2048]{1,0:T(8,128)(2,1)S(1)}, bf16[32,2048]{1,0:T(8,128)(2,1)S(1)}, u32[]{:S(2)}, u32[]{:S(2)}) collective-permute-start(bf16[32,2048]{1,0:T(8,128)(2,1)S(1)} %get-tuple-element.39), channel_id=1, source_target_pairs={{0,4},{1,5},{2,6},{3,7},{4,8},{5,9},{6,10},{7,11},{8,12},{9,13},{1... | collective-permute-start | bytes 393224 | tf_op jit(solution)/shard_map/ppermute | solution.py:35
  97.2 3.4 %collective-permute-start.27 = (bf16[32,2048]{1,0:T(8,128)(2,1)S(1)}, bf16[32,2048]{1,0:T(8,128)(2,1)S(1)}, u32[]{:S(2)}, u32[]{:S(2)}) collective-permute-start(bf16[32,2048]{1,0:T(8,128)(2,1)S(1)} %get-tuple-element.40), channel_id=1, source_target_pairs={{0,8},{1,9},{2,10},{3,11},{4,12},{5,13},{6,14},{7,15},{8,0},{9,1},... | collective-permute-start | bytes 393224 | tf_op jit(solution)/shard_map/ppermute | solution.py:35
  101.1 1.6 %collective-permute-start.16 = (bf16[128,2048]{1,0:T(8,128)(2,1)S(1)}, bf16[128,2048]{1,0:T(8,128)(2,1)S(1)}, u32[]{:S(2)}, u32[]{:S(2)}) collective-permute-start(bf16[128,2048]{1,0:T(8,128)(2,1)S(1)} %slice.122), channel_id=1, source_target_pairs={{0,2},{1,3},{2,0},{3,1},{4,6},{5,7},{6,4},{7,5},{8,10},{9,11},{10,... | collective-permute-start | bytes 1572872 | tf_op jit(solution)/shard_map/ppermute | solution.py:35
  102.7 1.8 %collective-permute-done.28 = bf16[32,2048]{1,0:T(8,128)(2,1)S(1)} collective-permute-done((bf16[32,2048]{1,0:T(8,128)(2,1)S(1)}, bf16[32,2048]{1,0:T(8,128)(2,1)S(1)}, u32[]{:S(2)}, u32[]{:S(2)}) %collective-permute-start.28) | collective-permute-done | bytes 131104 | tf_op jit(solution)/shard_map/ppermute | solution.py:35
  104.5 5.0 %collective-permute-done.27 = bf16[32,2048]{1,0:T(8,128)(2,1)S(1)} collective-permute-done((bf16[32,2048]{1,0:T(8,128)(2,1)S(1)}, bf16[32,2048]{1,0:T(8,128)(2,1)S(1)}, u32[]{:S(2)}, u32[]{:S(2)}) %collective-permute-start.27) | collective-permute-done | bytes 131104 | tf_op jit(solution)/shard_map/ppermute | solution.py:35
  109.5 1.6 %collective-permute-start.29 = (bf16[16,2048]{1,0:T(8,128)(2,1)S(1)}, bf16[16,2048]{1,0:T(8,128)(2,1)S(1)}, u32[]{:S(2)}, u32[]{:S(2)}) collective-permute-start(bf16[16,2048]{1,0:T(8,128)(2,1)S(1)} %slice.123), channel_id=1, source_target_pairs={{0,2},{1,3},{2,0},{3,1},{4,6},{5,7},{6,4},{7,5},{8,10},{9,11},{10,... | collective-permute-start | bytes 196616 | tf_op jit(solution)/shard_map/ppermute | solution.py:35
  111.1 4.0 %collective-permute-done.16 = bf16[128,2048]{1,0:T(8,128)(2,1)S(1)} collective-permute-done((bf16[128,2048]{1,0:T(8,128)(2,1)S(1)}, bf16[128,2048]{1,0:T(8,128)(2,1)S(1)}, u32[]{:S(2)}, u32[]{:S(2)}) %collective-permute-start.16) | collective-permute-done | bytes 524320 | tf_op jit(solution)/shard_map/ppermute | solution.py:35
  115.3 1.7 %collective-permute-start.19 = (bf16[32,2048]{1,0:T(8,128)(2,1)S(1)}, bf16[32,2048]{1,0:T(8,128)(2,1)S(1)}, u32[]{:S(2)}, u32[]{:S(2)}) collective-permute-start(bf16[32,2048]{1,0:T(8,128)(2,1)S(1)} %get-tuple-element.36), channel_id=1, source_target_pairs={{0,4},{1,5},{2,6},{3,7},{4,8},{5,9},{6,10},{7,11},{8,12},{9,13},{1... | collective-permute-start | bytes 393224 | tf_op jit(solution)/shard_map/ppermute | solution.py:35
  117.0 1.4 %collective-permute-start.18 = (bf16[32,2048]{1,0:T(8,128)(2,1)S(1)}, bf16[32,2048]{1,0:T(8,128)(2,1)S(1)}, u32[]{:S(2)}, u32[]{:S(2)}) collective-permute-start(bf16[32,2048]{1,0:T(8,128)(2,1)S(1)} %get-tuple-element.37), channel_id=1, source_target_pairs={{0,8},{1,9},{2,10},{3,11},{4,12},{5,13},{6,14},{7,15},{8,0},{9,1},... | collective-permute-start | bytes 393224 | tf_op jit(solution)/shard_map/ppermute | solution.py:35
  118.4 1.5 %collective-permute-start.17 = (bf16[32,2048]{1,0:T(8,128)(2,1)S(1)}, bf16[32,2048]{1,0:T(8,128)(2,1)S(1)}, u32[]{:S(2)}, u32[]{:S(2)}) collective-permute-start(bf16[32,2048]{1,0:T(8,128)(2,1)S(1)} %get-tuple-element.35), channel_id=1, source_target_pairs={{0,12},{1,13},{2,14},{3,15},{4,0},{5,1},{6,2},{7,3},{8,4},{9,5},{1... | collective-permute-start | bytes 393224 | tf_op jit(solution)/shard_map/ppermute | solution.py:35
  119.9 3.5 %collective-permute-done.19 = bf16[32,2048]{1,0:T(8,128)(2,1)S(1)} collective-permute-done((bf16[32,2048]{1,0:T(8,128)(2,1)S(1)}, bf16[32,2048]{1,0:T(8,128)(2,1)S(1)}, u32[]{:S(2)}, u32[]{:S(2)}) %collective-permute-start.19) | collective-permute-done | bytes 131104 | tf_op jit(solution)/shard_map/ppermute | solution.py:35
  123.4 3.5 %collective-permute-done.18 = bf16[32,2048]{1,0:T(8,128)(2,1)S(1)} collective-permute-done((bf16[32,2048]{1,0:T(8,128)(2,1)S(1)}, bf16[32,2048]{1,0:T(8,128)(2,1)S(1)}, u32[]{:S(2)}, u32[]{:S(2)}) %collective-permute-start.18) | collective-permute-done | bytes 131104 | tf_op jit(solution)/shard_map/ppermute | solution.py:35
  (84 shorter events, 14.3 us)
Async XLA Ops:
  2.0 16.9 %collective-permute-start.2 = (bf16[32,2176]{1,0:T(8,128)(2,1)}, bf16[32,2176]{1,0:T(8,128)(2,1)S(1)}, u32[]{:S(2)}, u32[]{:S(2)}) collective-permute-start(bf16[32,2176]{1,0:T(8,128)(2,1)} %get-tuple-element.18), channel_id=1, source_target_pairs={{0,12},{1,13},{2,14},{3,15},{4,0},{5,1},{6,2},{7,3},{8,4},{9,5},{1... | collective-permute-start | bytes 417800 | tf_op jit(solution)/shard_map/ppermute | solution.py:35
  7.0 13.0 %collective-permute-start.1 = (bf16[32,2176]{1,0:T(8,128)(2,1)}, bf16[32,2176]{1,0:T(8,128)(2,1)S(1)}, u32[]{:S(2)}, u32[]{:S(2)}) collective-permute-start(bf16[32,2176]{1,0:T(8,128)(2,1)} %get-tuple-element.18), channel_id=1, source_target_pairs={{0,8},{1,9},{2,10},{3,11},{4,12},{5,13},{6,14},{7,15},{8,0},{9,1},... | collective-permute-start | bytes 417800 | tf_op jit(solution)/shard_map/ppermute | solution.py:35
  7.0 13.0 %collective-permute-start = (bf16[32,2176]{1,0:T(8,128)(2,1)}, bf16[32,2176]{1,0:T(8,128)(2,1)S(1)}, u32[]{:S(2)}, u32[]{:S(2)}) collective-permute-start(bf16[32,2176]{1,0:T(8,128)(2,1)} %get-tuple-element.18), channel_id=1, source_target_pairs={{0,4},{1,5},{2,6},{3,7},{4,8},{5,9},{6,10},{7,11},{8,12},{9,13},{1... | collective-permute-start | bytes 417800 | tf_op jit(solution)/shard_map/ppermute | solution.py:35
  8.0 7.0 %collective-permute-start.20 = (bf16[16,2176]{1,0:T(8,128)(2,1)}, bf16[16,2176]{1,0:T(8,128)(2,1)S(1)}, u32[]{:S(2)}, u32[]{:S(2)}) collective-permute-start(bf16[16,2176]{1,0:T(8,128)(2,1)} %get-tuple-element.28), channel_id=1, source_target_pairs={{0,2},{1,3},{2,0},{3,1},{4,6},{5,7},{6,4},{7,5},{8,10},{9,11},{10,... | collective-permute-start | bytes 208904 | tf_op jit(solution)/shard_map/ppermute | solution.py:35
  13.6 17.6 %collective-permute-start.6 = (bf16[4,264,128]{2,1,0:T(8,128)(2,1)}, bf16[4,264,128]{2,1,0:T(8,128)(2,1)S(1)}, u32[]{:S(2)}, u32[]{:S(2)}) collective-permute-start(bf16[4,264,128]{2,1,0:T(8,128)(2,1)} %get-tuple-element.20), channel_id=1, source_target_pairs={{0,2},{1,3},{2,0},{3,1},{4,6},{5,7},{6,4},{7,5},{8,10},{9,11},{10,... | collective-permute-start | bytes 811016 | tf_op jit(solution)/shard_map/ppermute | solution.py:35
  16.0 7.0 %collective-permute-start.23 = (bf16[32,2176]{1,0:T(8,128)(2,1)S(1)}, bf16[32,2176]{1,0:T(8,128)(2,1)S(1)}, u32[]{:S(2)}, u32[]{:S(2)}) collective-permute-start(bf16[32,2176]{1,0:T(8,128)(2,1)S(1)} %bitcast.29), channel_id=1, source_target_pairs={{0,12},{1,13},{2,14},{3,15},{4,0},{5,1},{6,2},{7,3},{8,4},{9,5},{1... | collective-permute-start | bytes 417800 | tf_op jit(solution)/shard_map/ppermute | solution.py:35
  18.8 12.1 %collective-permute-start.22 = (bf16[32,2176]{1,0:T(8,128)(2,1)S(1)}, bf16[32,2176]{1,0:T(8,128)(2,1)S(1)}, u32[]{:S(2)}, u32[]{:S(2)}) collective-permute-start(bf16[32,2176]{1,0:T(8,128)(2,1)S(1)} %bitcast.30), channel_id=1, source_target_pairs={{0,8},{1,9},{2,10},{3,11},{4,12},{5,13},{6,14},{7,15},{8,0},{9,1},... | collective-permute-start | bytes 417800 | tf_op jit(solution)/shard_map/ppermute | solution.py:35
  20.0 11.0 %collective-permute-start.21 = (bf16[32,2176]{1,0:T(8,128)(2,1)S(1)}, bf16[32,2176]{1,0:T(8,128)(2,1)S(1)}, u32[]{:S(2)}, u32[]{:S(2)}) collective-permute-start(bf16[32,2176]{1,0:T(8,128)(2,1)S(1)} %bitcast.31), channel_id=1, source_target_pairs={{0,4},{1,5},{2,6},{3,7},{4,8},{5,9},{6,10},{7,11},{8,12},{9,13},{1... | collective-permute-start | bytes 417800 | tf_op jit(solution)/shard_map/ppermute | solution.py:35
  21.0 54.6 %copy-start.4 = (bf16[4,32,2176]{2,1,0:T(8,128)(2,1)}, bf16[4,32,2176]{2,1,0:T(8,128)(2,1)S(1)}, u32[]{:S(2)}) copy-start(bf16[4,32,2176]{2,1,0:T(8,128)(2,1)S(1)} %pad_maximum_fusion) | copy-start | bytes 1671172
  21.0 19.3 %collective-permute-start.3 = (bf16[128,2176]{1,0:T(8,128)(2,1)S(1)}, bf16[128,2176]{1,0:T(8,128)(2,1)S(1)}, u32[]{:S(2)}, u32[]{:S(2)}) collective-permute-start(bf16[128,2176]{1,0:T(8,128)(2,1)S(1)} %bitcast.33), channel_id=1, source_target_pairs={{0,2},{1,3},{2,0},{3,1},{4,6},{5,7},{6,4},{7,5},{8,10},{9,11},{10,... | collective-permute-start | bytes 1671176 | tf_op jit(solution)/shard_map/ppermute | solution.py:35
  31.1 33.8 %collective-permute-start.24 = (bf16[128,2176]{1,0:T(8,128)(2,1)S(1)}, bf16[128,2176]{1,0:T(8,128)(2,1)S(1)}, u32[]{:S(2)}, u32[]{:S(2)}) collective-permute-start(bf16[128,2176]{1,0:T(8,128)(2,1)S(1)} %bitcast.27), channel_id=1, source_target_pairs={{0,1},{1,0},{2,3},{3,2},{4,5},{5,4},{6,7},{7,6},{8,9},{9,8},{10,11... | collective-permute-start | bytes 1671176 | tf_op jit(solution)/shard_map/ppermute | solution.py:35
  31.2 3.6 %collective-permute-start.7 = (bf16[2,264,128]{2,1,0:T(8,128)(2,1)S(1)}, bf16[2,264,128]{2,1,0:T(8,128)(2,1)S(1)}, u32[]{:S(2)}, u32[]{:S(2)}) collective-permute-start(bf16[2,264,128]{2,1,0:T(8,128)(2,1)S(1)} %pad_maximum_fusion.4), channel_id=1, source_target_pairs={{0,0},{1,1},{2,2},{3,3},{4,4},{5,5},{6,6},{7,7},{8,8},{9,9},{10,10... | collective-permute-start | bytes 405512 | tf_op jit(solution)/shard_map/ppermute | solution.py:68
  31.9 8.4 %collective-permute-start.8 = (bf16[2,264,128]{2,1,0:T(8,128)(2,1)S(1)}, bf16[2,264,128]{2,1,0:T(8,128)(2,1)S(1)}, u32[]{:S(2)}, u32[]{:S(2)}) collective-permute-start(bf16[2,264,128]{2,1,0:T(8,128)(2,1)S(1)} %pad_maximum_fusion.5), channel_id=1, source_target_pairs={{0,4},{1,5},{2,6},{3,7},{4,8},{5,9},{6,10},{7,11},{8,12},{9,13},{1... | collective-permute-start | bytes 405512 | tf_op jit(solution)/shard_map/ppermute | solution.py:68
  32.8 12.8 %collective-permute-start.9 = (bf16[2,264,128]{2,1,0:T(8,128)(2,1)S(1)}, bf16[2,264,128]{2,1,0:T(8,128)(2,1)S(1)}, u32[]{:S(2)}, u32[]{:S(2)}) collective-permute-start(bf16[2,264,128]{2,1,0:T(8,128)(2,1)S(1)} %pad_maximum_fusion.6), channel_id=1, source_target_pairs={{0,8},{1,9},{2,10},{3,11},{4,12},{5,13},{6,14},{7,15},{8,0},{9,1},... | collective-permute-start | bytes 405512 | tf_op jit(solution)/shard_map/ppermute | solution.py:68
  34.9 13.1 %collective-permute-start.10 = (bf16[2,264,128]{2,1,0:T(8,128)(2,1)S(1)}, bf16[2,264,128]{2,1,0:T(8,128)(2,1)S(1)}, u32[]{:S(2)}, u32[]{:S(2)}) collective-permute-start(bf16[2,264,128]{2,1,0:T(8,128)(2,1)S(1)} %pad_maximum_fusion.7), channel_id=1, source_target_pairs={{0,12},{1,13},{2,14},{3,15},{4,0},{5,1},{6,2},{7,3},{8,4},{9,5},{1... | collective-permute-start | bytes 405512 | tf_op jit(solution)/shard_map/ppermute | solution.py:68
  40.3 35.4 %collective-permute-start.4 = (bf16[128,2176]{1,0:T(8,128)(2,1)S(1)}, bf16[128,2176]{1,0:T(8,128)(2,1)S(1)}, u32[]{:S(2)}, u32[]{:S(2)}) collective-permute-start(bf16[128,2176]{1,0:T(8,128)(2,1)S(1)} %bitcast.34), channel_id=1, source_target_pairs={{0,1},{1,0},{2,3},{3,2},{4,5},{5,4},{6,7},{7,6},{8,9},{9,8},{10,11... | collective-permute-start | bytes 1671176 | tf_op jit(solution)/shard_map/ppermute | solution.py:35
  40.3 35.3 %copy-start.13 = (bf16[128,2176]{1,0:T(8,128)(2,1)}, bf16[128,2176]{1,0:T(8,128)(2,1)S(1)}, u32[]{:S(2)}) copy-start(bf16[128,2176]{1,0:T(8,128)(2,1)S(1)} %collective-permute-done.3.refs_1_) | copy-start | bytes 1671172
  40.3 35.4 %collective-permute-start.5 = (bf16[128,2176]{1,0:T(8,128)(2,1)S(1)}, bf16[128,2176]{1,0:T(8,128)(2,1)}, u32[]{:S(2)}, u32[]{:S(2)}) collective-permute-start(bf16[128,2176]{1,0:T(8,128)(2,1)S(1)} %collective-permute-done.3.refs_1_), channel_id=1, source_target_pairs={{0,1},{1,0},{2,3},{3,2},{4,5},{5,4},{6,7},{7,6},{8,9},{9,8},{10,11... | collective-permute-start | bytes 1671176 | tf_op jit(solution)/shard_map/ppermute | solution.py:35
  45.6 6.7 %collective-permute-start.11 = (bf16[2,264,128]{2,1,0:T(8,128)(2,1)S(1)}, bf16[2,264,128]{2,1,0:T(8,128)(2,1)S(1)}, u32[]{:S(2)}, u32[]{:S(2)}) collective-permute-start(bf16[2,264,128]{2,1,0:T(8,128)(2,1)S(1)} %collective-permute-done.7.refs_0_), channel_id=1, source_target_pairs={{0,16},{16,0},{1,17},{17,1},{2,18},{18,2},{3,19},{19,3},{4,20},{20... | collective-permute-start | bytes 405512 | tf_op jit(solution)/shard_map/ppermute | solution.py:70
  47.9 7.3 %collective-permute-start.12 = (bf16[2,264,128]{2,1,0:T(8,128)(2,1)S(1)}, bf16[2,264,128]{2,1,0:T(8,128)(2,1)S(1)}, u32[]{:S(2)}, u32[]{:S(2)}) collective-permute-start(bf16[2,264,128]{2,1,0:T(8,128)(2,1)S(1)} %collective-permute-done.8.refs_1_), channel_id=1, source_target_pairs={{0,16},{16,0},{1,17},{17,1},{2,18},{18,2},{3,19},{19,3},{4,20},{20... | collective-permute-start | bytes 405512 | tf_op jit(solution)/shard_map/ppermute | solution.py:70
  52.4 5.9 %collective-permute-start.13 = (bf16[2,264,128]{2,1,0:T(8,128)(2,1)S(1)}, bf16[2,264,128]{2,1,0:T(8,128)(2,1)S(1)}, u32[]{:S(2)}, u32[]{:S(2)}) collective-permute-start(bf16[2,264,128]{2,1,0:T(8,128)(2,1)S(1)} %collective-permute-done.9.refs_2_), channel_id=1, source_target_pairs={{0,16},{16,0},{1,17},{17,1},{2,18},{18,2},{3,19},{19,3},{4,20},{20... | collective-permute-start | bytes 405512 | tf_op jit(solution)/shard_map/ppermute | solution.py:70
  55.3 5.8 %collective-permute-start.14 = (bf16[2,264,128]{2,1,0:T(8,128)(2,1)S(1)}, bf16[2,264,128]{2,1,0:T(8,128)(2,1)S(1)}, u32[]{:S(2)}, u32[]{:S(2)}) collective-permute-start(bf16[2,264,128]{2,1,0:T(8,128)(2,1)S(1)} %collective-permute-done.10.refs_3_), channel_id=1, source_target_pairs={{0,16},{16,0},{1,17},{17,1},{2,18},{18,2},{3,19},{19,3},{4,20},{20... | collective-permute-start | bytes 405512 | tf_op jit(solution)/shard_map/ppermute | solution.py:70
  75.6 19.5 %collective-permute-start.25 = (bf16[128,2048]{1,0:T(8,128)(2,1)}, bf16[128,2048]{1,0:T(8,128)(2,1)S(1)}, u32[]{:S(2)}, u32[]{:S(2)}) collective-permute-start(bf16[128,2048]{1,0:T(8,128)(2,1)} %get-tuple-element.30), channel_id=1, source_target_pairs={{0,1},{1,0},{2,3},{3,2},{4,5},{5,4},{6,7},{7,6},{8,9},{9,8},{10,11... | collective-permute-start | bytes 1572872 | tf_op jit(solution)/shard_map/ppermute | solution.py:35
  94.5 6.1 %collective-permute-start.15 = (bf16[256,2048]{1,0:T(8,128)(2,1)}, bf16[256,2048]{1,0:T(8,128)(2,1)S(1)}, u32[]{:S(2)}, u32[]{:S(2)}) collective-permute-start(bf16[256,2048]{1,0:T(8,128)(2,1)} %get-tuple-element.27), channel_id=1, source_target_pairs={{0,1},{1,0},{2,3},{3,2},{4,5},{5,4},{6,7},{7,6},{8,9},{9,8},{10,11... | collective-permute-start | bytes 3145736 | tf_op jit(solution)/shard_map/ppermute | solution.py:35
  95.3 9.2 %collective-permute-start.28 = (bf16[32,2048]{1,0:T(8,128)(2,1)S(1)}, bf16[32,2048]{1,0:T(8,128)(2,1)S(1)}, u32[]{:S(2)}, u32[]{:S(2)}) collective-permute-start(bf16[32,2048]{1,0:T(8,128)(2,1)S(1)} %get-tuple-element.39), channel_id=1, source_target_pairs={{0,4},{1,5},{2,6},{3,7},{4,8},{5,9},{6,10},{7,11},{8,12},{9,13},{1... | collective-permute-start | bytes 393224 | tf_op jit(solution)/shard_map/ppermute | solution.py:35
  97.2 12.2 %collective-permute-start.27 = (bf16[32,2048]{1,0:T(8,128)(2,1)S(1)}, bf16[32,2048]{1,0:T(8,128)(2,1)S(1)}, u32[]{:S(2)}, u32[]{:S(2)}) collective-permute-start(bf16[32,2048]{1,0:T(8,128)(2,1)S(1)} %get-tuple-element.40), channel_id=1, source_target_pairs={{0,8},{1,9},{2,10},{3,11},{4,12},{5,13},{6,14},{7,15},{8,0},{9,1},... | collective-permute-start | bytes 393224 | tf_op jit(solution)/shard_map/ppermute | solution.py:35
  100.6 8.8 %collective-permute-start.26 = (bf16[32,2048]{1,0:T(8,128)(2,1)S(1)}, bf16[32,2048]{1,0:T(8,128)(2,1)S(1)}, u32[]{:S(2)}, u32[]{:S(2)}) collective-permute-start(bf16[32,2048]{1,0:T(8,128)(2,1)S(1)} %get-tuple-element.38), channel_id=1, source_target_pairs={{0,12},{1,13},{2,14},{3,15},{4,0},{5,1},{6,2},{7,3},{8,4},{9,5},{1... | collective-permute-start | bytes 393224 | tf_op jit(solution)/shard_map/ppermute | solution.py:35
  101.1 14.1 %collective-permute-start.16 = (bf16[128,2048]{1,0:T(8,128)(2,1)S(1)}, bf16[128,2048]{1,0:T(8,128)(2,1)S(1)}, u32[]{:S(2)}, u32[]{:S(2)}) collective-permute-start(bf16[128,2048]{1,0:T(8,128)(2,1)S(1)} %slice.122), channel_id=1, source_target_pairs={{0,2},{1,3},{2,0},{3,1},{4,6},{5,7},{6,4},{7,5},{8,10},{9,11},{10,... | collective-permute-start | bytes 1572872 | tf_op jit(solution)/shard_map/ppermute | solution.py:35
  109.5 10.3 %collective-permute-start.29 = (bf16[16,2048]{1,0:T(8,128)(2,1)S(1)}, bf16[16,2048]{1,0:T(8,128)(2,1)S(1)}, u32[]{:S(2)}, u32[]{:S(2)}) collective-permute-start(bf16[16,2048]{1,0:T(8,128)(2,1)S(1)} %slice.123), channel_id=1, source_target_pairs={{0,2},{1,3},{2,0},{3,1},{4,6},{5,7},{6,4},{7,5},{8,10},{9,11},{10,... | collective-permute-start | bytes 196616 | tf_op jit(solution)/shard_map/ppermute | solution.py:35
  115.3 8.1 %collective-permute-start.19 = (bf16[32,2048]{1,0:T(8,128)(2,1)S(1)}, bf16[32,2048]{1,0:T(8,128)(2,1)S(1)}, u32[]{:S(2)}, u32[]{:S(2)}) collective-permute-start(bf16[32,2048]{1,0:T(8,128)(2,1)S(1)} %get-tuple-element.36), channel_id=1, source_target_pairs={{0,4},{1,5},{2,6},{3,7},{4,8},{5,9},{6,10},{7,11},{8,12},{9,13},{1... | collective-permute-start | bytes 393224 | tf_op jit(solution)/shard_map/ppermute | solution.py:35
  117.0 9.8 %collective-permute-start.18 = (bf16[32,2048]{1,0:T(8,128)(2,1)S(1)}, bf16[32,2048]{1,0:T(8,128)(2,1)S(1)}, u32[]{:S(2)}, u32[]{:S(2)}) collective-permute-start(bf16[32,2048]{1,0:T(8,128)(2,1)S(1)} %get-tuple-element.37), channel_id=1, source_target_pairs={{0,8},{1,9},{2,10},{3,11},{4,12},{5,13},{6,14},{7,15},{8,0},{9,1},... | collective-permute-start | bytes 393224 | tf_op jit(solution)/shard_map/ppermute | solution.py:35
  118.4 8.5 %collective-permute-start.17 = (bf16[32,2048]{1,0:T(8,128)(2,1)S(1)}, bf16[32,2048]{1,0:T(8,128)(2,1)S(1)}, u32[]{:S(2)}, u32[]{:S(2)}) collective-permute-start(bf16[32,2048]{1,0:T(8,128)(2,1)S(1)} %get-tuple-element.35), channel_id=1, source_target_pairs={{0,12},{1,13},{2,14},{3,15},{4,0},{5,1},{6,2},{7,3},{8,4},{9,5},{1... | collective-permute-start | bytes 393224 | tf_op jit(solution)/shard_map/ppermute | solution.py:35
  (13 other events, 154.4 us)

commit v6 on v5

--- a/solution.py
+++ b/solution.py
@@ -9,7 +9,8 @@
 
 adapter_scale = 2.0
 LANES = 128
-GRANT = 60 << 20
+GRANT = 16 << 20
+EXPERT_GRANT = 36 << 20
 
 
 def route_gates(logits):
@@ -251,46 +252,38 @@
         begun.append(copy)
         return copy
 
-    def blocks(length, block):
-        return [slice(at, at + block) for at in range(0, length, block)]
+    def begin_rows(src, dst):
+        quarter = src.shape[0] // 4
+        cuts = [pl.ds(at, quarter) for at in range(0, src.shape[0], quarter)]
+        return [begin(src.at[cut], dst.at[cut]) for cut in cuts]
+
+    def wait(copies):
+        for copy in copies:
+            copy.wait()
 
     x_in = [begin(p, x_ref.at[pl.ds(i * rows, rows)]) for i, p in enumerate(pieces)]
     x_in.append(begin(a_gu_hbm, a_gu_ref))
-    b_in = [begin(gate_b_hbm, gate_b_ref), begin(up_b_hbm, up_b_ref)]
-    unit_cuts, width_cuts = blocks(units, 256), blocks(width, 512 if width % 512 == 0 else 256)
-    gu_in = [
-        (
-            begin(w_gate_hbm.at[:, cut], w_gate_ref.at[:, cut]),
-            begin(w_up_hbm.at[:, cut], w_up_ref.at[:, cut]),
-        )
-        for cut in unit_cuts
-    ]
-    d_in = [begin(down_a_hbm, down_a_ref), begin(down_b_hbm, down_b_ref)]
-    down_in = [begin(w_down_hbm.at[:, cut], w_down_ref.at[:, cut]) for cut in width_cuts]
-
-    for copy in x_in:
-        copy.wait()
+    gate_in = begin_rows(w_gate_hbm, w_gate_ref) + [begin(gate_b_hbm, gate_b_ref)]
+    up_in = begin_rows(w_up_hbm, w_up_ref) + [begin(up_b_hbm, up_b_ref)]
+    down_in = [begin(down_a_hbm, down_a_ref), begin(down_b_hbm, down_b_ref)]
+    down_in += begin_rows(w_down_hbm, w_down_ref)
+
+    wait(x_in)
     gates = x_ref[:, width:].astype(jnp.float32)
     lane = lax.broadcasted_iota(jnp.int32, gates.shape, 1)
     mine = jnp.sum(jnp.where(lane == place_ref[1], gates, 0.0), axis=1, keepdims=True)
-    x = x_ref[:, :width]
-    low = (adapter_scale * dot(x, a_gu_ref[...])).astype(jnp.bfloat16)
-    for copy in b_in:
-        copy.wait()
-    for cut, (gate_in, up_in) in zip(unit_cuts, gu_in):
-        gate_in.wait()
-        g = dot(x, w_gate_ref[:, cut]) + dot(low[:, :rank], gate_b_ref[:, cut])
-        up_in.wait()
-        u = dot(x, w_up_ref[:, cut]) + dot(low[:, rank:], up_b_ref[:, cut])
-        inner_ref[:, cut] = (g / (1.0 + jnp.exp(-g)) * u).astype(jnp.bfloat16)
-    for copy in d_in:
-        copy.wait()
-    inner = inner_ref[...]
-    low = (adapter_scale * dot(inner, down_a_ref[...])).astype(jnp.bfloat16)[:, :rank]
+    low = (adapter_scale * dot(x_ref[:, :width], a_gu_ref[...])).astype(jnp.bfloat16)
+    wait(gate_in)
+    g = dot(x_ref[:, :width], w_gate_ref[...]) + dot(low[:, :rank], gate_b_ref[...])
+    wait(up_in)
+    u = dot(x_ref[:, :width], w_up_ref[...]) + dot(low[:, rank:], up_b_ref[...])
+    inner_ref[...] = (g / (1.0 + jnp.exp(-g)) * u).astype(jnp.bfloat16)
+    wait(down_in)
+    low = (adapter_scale * dot(inner_ref[...], down_a_ref[...])).astype(jnp.bfloat16)[:, :rank]
     out_copies = []
-    for i, (cut, copy) in enumerate(zip(width_cuts, down_in)):
-        copy.wait()
-        out = dot(inner, w_down_ref[:, cut]) + dot(low, down_b_ref[:, cut])
+    block = width // 2
+    for i, cut in enumerate((slice(0, block), slice(block, width))):
+        out = dot(inner_ref[...], w_down_ref[:, cut]) + dot(low, down_b_ref[:, cut])
         out = out * mine
         sent_ref[:, cut] = out[own:].astype(jnp.bfloat16)
         kept_ref[:, cut] = out[:own]
@@ -313,13 +306,13 @@
         jax.ShapeDtypeStruct((total - own, width), jnp.bfloat16),
     ]
     kept = [a_gu, gate_b, up_b, down_a, down_b, w_gate, w_up, w_down]
-    width_block = 512 if width % 512 == 0 else 256
-    copies = len(pieces) + 5 + 2 * (units // 256) + width // width_block
+    copies = len(pieces) + 5 + 3 * 4
     return pl.pallas_call(
         functools.partial(expert_kernel, len(pieces)),
         out_shape=outs,
         in_specs=[pl.BlockSpec(memory_space=pltpu.SMEM)]
-        + [pl.BlockSpec(memory_space=pl.ANY)] * (len(pieces) + len(kept)),
+        + [pl.BlockSpec(memory_space=pl.ANY)] * (len(pieces) + len(low_rank))
+        + [pl.BlockSpec(memory_space=pltpu.HBM)] * 3,
         out_specs=[pl.BlockSpec(memory_space=pl.ANY)] * 2,
         scratch_shapes=[pltpu.VMEM((total, pieces[0].shape[1]), jnp.bfloat16)]
         + [pltpu.VMEM(a.shape, a.dtype) for a in kept]
@@ -328,9 +321,9 @@
             pltpu.VMEM(outs[0].shape, outs[0].dtype),
             pltpu.VMEM(outs[1].shape, outs[1].dtype),
             pltpu.SemaphoreType.DMA((copies,)),
-            pltpu.SemaphoreType.DMA((2 * (width // width_block),)),
+            pltpu.SemaphoreType.DMA((4,)),
         ],
-        compiler_params=pltpu.CompilerParams(vmem_limit_bytes=GRANT),
+        compiler_params=pltpu.CompilerParams(vmem_limit_bytes=EXPERT_GRANT),
         cost_estimate=pl.CostEstimate(
             flops=2 * total * units * (3 * width + 4 * rank) + 8 * total * width * rank,
             bytes_accessed=6 * units * width + 5 * total * width,
@@ -360,6 +353,7 @@
     here, there = exchange_factors(blocks, owners)
     heads = [head] + [shift(head, owners, *along_middle, k) for k in range(1, middle)]
     heads += [shift(p, owners, 1, cores, 1) for p in heads]
+    tail, here = lax.optimization_barrier((tail, here))
     tail = gather_along(tail, owners, *along_outer)
     tails = [tail, shift(tail, owners, 1, cores, 1)]
 

time: 128 us -> 132 us (1.031)
  waiting for transfers between devices: 42.5 us -> 54.6 us
  Pallas kernels: 36.3 us -> 28.3 us
  local copies, waits for them, and re-layouts: 3.45 us -> 6.29 us
  other arithmetic: 4.19 us -> 1.72 us
    ppermute x22, waiting for transfers between devices: 26.3 us -> 34.2 us  [shift(): return lax.ppermute(x, 'expert', pairs)]
    ppermute x4, waiting for transfers between devices: 7.31 us -> 11.4 us  [exchange_factors(): part = lax.ppermute(part, ('group', 'expert'), pairs)]
    unnamed x30 -> x16, local copies, waits for them, and re-layouts: 2.3 us -> 6.12 us
    pallas_call x2, Pallas kernels: 27.9 us -> 24.4 us  [run_expert(): pl.pallas_call(functools.partial(expert_kernel, len(pieces)), out_shape=o...]
    another operation x3, other arithmetic: 1.98 us -> 0.19 us  [stack_rows(): return jnp.stack(pieces).reshape(-1, pieces[0].shape[1])]
    pallas_call x1, Pallas kernels: 1.96 us -> 0.32 us  [make_payload(): pl.pallas_call(payload_kernel, out_shape=[jax.ShapeDtypeStruct((count * r...]
    pallas_call x1, Pallas kernels: 3.35 us -> 1.85 us  [order_factors(): pl.pallas_call(functools.partial(order_kernel, outer, middle), out_shape=...]
    pallas_call x1, Pallas kernels: 3.14 us -> 1.77 us  [relayout_factors(): pl.pallas_call(functools.partial(relayout_kernel, outer, middle), out_sha...]
  transfers between devices with their start and end apart: 30 -> 30, of which waited for: 13 -> 18; matrix products, arithmetic and copies ran while one was open for 4% -> 1% of each run, Pallas kernels for 27% -> 20%
where the time goes in v6:
time: 132 us
  waiting for transfers between devices  54.6 us (41%)
  starting transfers between devices  40.3 us (31%)
  Pallas kernels  28.3 us (21%)
  local copies, waits for them, and re-layouts  6.29 us (5%)
  other arithmetic  1.72 us (1%)
    ppermute x22, waiting for transfers between devices, shift(): return lax.ppermute(x, 'expert', pairs)  34.2 us
    ppermute x22, starting transfers between devices, shift(): return lax.ppermute(x, 'expert', pairs)  27.3 us
    pallas_call x2, Pallas kernels, run_expert(): pl.pallas_call(functools.partial(expert_kernel, len(pieces)), out_shape=o...  24.4 us
    ppermute x4, waiting for transfers between devices, exchange_factors(): part = lax.ppermute(part, ('group', 'expert'), pairs)  11.4 us
    ppermute x4, waiting for transfers between devices, exchange_factors(): there.append(lax.ppermute(part, 'group', [(0, 1), (1, 0)]))  9.01 us
    ppermute x4, starting transfers between devices, exchange_factors(): part = lax.ppermute(part, ('group', 'expert'), pairs)  6.99 us
    unnamed x16, local copies, waits for them, and re-layouts  6.12 us
    ppermute x4, starting transfers between devices, exchange_factors(): there.append(lax.ppermute(part, 'group', [(0, 1), (1, 0)]))  6.02 us
  transfers between devices with their start and end apart: 30, of which 18 were waited for; matrix products, arithmetic and copies ran while one was open for 1% of the time, Pallas kernels for 20%

profile of v6, /device:TPU:0, one launch (start us, length us, event | category | flops | bytes accessed | tf_op | source)
XLA Modules:
  0.0 131.5 jit_solution(969645040937492026)
XLA Ops:
  2.0 1.8 %order_factors.1 = (bf16[4,264,128]{2,1,0:T(8,128)(2,1)S(1)}, bf16[4,264,128]{2,1,0:T(8,128)(2,1)S(1)}) custom-call(s32[2]{0:T(128)S(1)} %pad_add_fusion.place_ref, s32[16]{0:T(128)S(1)} %copy-done.7, bf16[16,33792]{1,0:T(8,128)(2,1)S(1)} %copy-done.3), custom_call_target="tpu_custom_call" | custom-call | tf_op jit(solution)/shard_map/order_factors/pallas_call | solution.py:152
  3.8 3.0 %collective-permute-start.7 = (bf16[4,264,128]{2,1,0:T(8,128)(2,1)S(1)}, bf16[4,264,128]{2,1,0:T(8,128)(2,1)S(1)}, u32[]{:S(2)}, u32[]{:S(2)}) collective-permute-start(bf16[4,264,128]{2,1,0:T(8,128)(2,1)S(1)} %get-tuple-element.26), channel_id=1, source_target_pairs={{0,2},{1,3},{2,0},{3,1},{4,6},{5,7},{6,4},{7,5},{8,10},{9,11},{10,... | collective-permute-start | bytes 811016 | tf_op jit(solution)/shard_map/ppermute | solution.py:36
  9.5 3.7 %collective-permute-start.2 = (bf16[32,2176]{1,0:T(8,128)(2,1)S(1)}, bf16[32,2176]{1,0:T(8,128)(2,1)S(1)}, u32[]{:S(2)}, u32[]{:S(2)}) collective-permute-start(bf16[32,2176]{1,0:T(8,128)(2,1)S(1)} %get-tuple-element.23), channel_id=1, source_target_pairs={{0,12},{1,13},{2,14},{3,15},{4,0},{5,1},{6,2},{7,3},{8,4},{9,5},{1... | collective-permute-start | bytes 417800 | tf_op jit(solution)/shard_map/ppermute | solution.py:36
  14.5 1.5 %collective-permute-start.9 = (bf16[2,264,128]{2,1,0:T(8,128)(2,1)S(1)}, bf16[2,264,128]{2,1,0:T(8,128)(2,1)S(1)}, u32[]{:S(2)}, u32[]{:S(2)}) collective-permute-start(bf16[2,264,128]{2,1,0:T(8,128)(2,1)S(1)} %pad_maximum_fusion.5), channel_id=1, source_target_pairs={{0,4},{1,5},{2,6},{3,7},{4,8},{5,9},{6,10},{7,11},{8,12},{9,13},{1... | collective-permute-start | bytes 405512 | tf_op jit(solution)/shard_map/ppermute | solution.py:69
  16.0 1.5 %collective-permute-done.6 = bf16[16,2176]{1,0:T(8,128)(2,1)S(1)} collective-permute-done((bf16[16,2176]{1,0:T(8,128)(2,1)S(1)}, bf16[16,2176]{1,0:T(8,128)(2,1)S(1)}, u32[]{:S(2)}, u32[]{:S(2)}) %collective-permute-start.6) | collective-permute-done | bytes 69664 | tf_op jit(solution)/shard_map/ppermute | solution.py:36
  18.5 1.9 %collective-permute-start.10 = (bf16[2,264,128]{2,1,0:T(8,128)(2,1)S(1)}, bf16[2,264,128]{2,1,0:T(8,128)(2,1)S(1)}, u32[]{:S(2)}, u32[]{:S(2)}) collective-permute-start(bf16[2,264,128]{2,1,0:T(8,128)(2,1)S(1)} %pad_maximum_fusion.6), channel_id=1, source_target_pairs={{0,8},{1,9},{2,10},{3,11},{4,12},{5,13},{6,14},{7,15},{8,0},{9,1},... | collective-permute-start | bytes 405512 | tf_op jit(solution)/shard_map/ppermute | solution.py:69
  20.4 3.8 %collective-permute-done.9.refs_1_ = bf16[2,264,128]{2,1,0:T(8,128)(2,1)S(1)} collective-permute-done((bf16[2,264,128]{2,1,0:T(8,128)(2,1)S(1)}, bf16[2,264,128]{2,1,0:T(8,128)(2,1)S(1)}, u32[]{:S(2)}, u32[]{:S(2)}) %collective-permute-start.9) | collective-permute-done | bytes 135200 | tf_op jit(solution)/shard_map/ppermute | solution.py:69
  24.2 2.9 %collective-permute-start.11 = (bf16[2,264,128]{2,1,0:T(8,128)(2,1)S(1)}, bf16[2,264,128]{2,1,0:T(8,128)(2,1)S(1)}, u32[]{:S(2)}, u32[]{:S(2)}) collective-permute-start(bf16[2,264,128]{2,1,0:T(8,128)(2,1)S(1)} %pad_maximum_fusion.7), channel_id=1, source_target_pairs={{0,12},{1,13},{2,14},{3,15},{4,0},{5,1},{6,2},{7,3},{8,4},{9,5},{1... | collective-permute-start | bytes 405512 | tf_op jit(solution)/shard_map/ppermute | solution.py:69
  27.1 7.1 %collective-permute-done.10.refs_2_ = bf16[2,264,128]{2,1,0:T(8,128)(2,1)S(1)} collective-permute-done((bf16[2,264,128]{2,1,0:T(8,128)(2,1)S(1)}, bf16[2,264,128]{2,1,0:T(8,128)(2,1)S(1)}, u32[]{:S(2)}, u32[]{:S(2)}) %collective-permute-start.10) | collective-permute-done | bytes 135200 | tf_op jit(solution)/shard_map/ppermute | solution.py:69
  34.8 5.1 %collective-permute-start.23 = (bf16[32,2176]{1,0:T(8,128)(2,1)S(1)}, bf16[32,2176]{1,0:T(8,128)(2,1)S(1)}, u32[]{:S(2)}, u32[]{:S(2)}) collective-permute-start(bf16[32,2176]{1,0:T(8,128)(2,1)S(1)} %bitcast.36), channel_id=1, source_target_pairs={{0,12},{1,13},{2,14},{3,15},{4,0},{5,1},{6,2},{7,3},{8,4},{9,5},{1... | collective-permute-start | bytes 417800 | tf_op jit(solution)/shard_map/ppermute | solution.py:36
  41.7 2.3 %collective-permute-done.23 = bf16[32,2176]{1,0:T(8,128)(2,1)S(1)} collective-permute-done((bf16[32,2176]{1,0:T(8,128)(2,1)S(1)}, bf16[32,2176]{1,0:T(8,128)(2,1)S(1)}, u32[]{:S(2)}, u32[]{:S(2)}) %collective-permute-start.23) | collective-permute-done | bytes 139296 | tf_op jit(solution)/shard_map/ppermute | solution.py:36
  44.1 7.0 %collective-permute-done.22 = bf16[32,2176]{1,0:T(8,128)(2,1)S(1)} collective-permute-done((bf16[32,2176]{1,0:T(8,128)(2,1)S(1)}, bf16[32,2176]{1,0:T(8,128)(2,1)S(1)}, u32[]{:S(2)}, u32[]{:S(2)}) %collective-permute-start.22) | collective-permute-done | bytes 139296 | tf_op jit(solution)/shard_map/ppermute | solution.py:36
  51.7 2.2 %collective-permute-done.3.refs_1_ = bf16[128,2176]{1,0:T(8,128)(2,1)S(1)} collective-permute-done((bf16[128,2176]{1,0:T(8,128)(2,1)S(1)}, bf16[128,2176]{1,0:T(8,128)(2,1)S(1)}, u32[]{:S(2)}, u32[]{:S(2)}) %collective-permute-start.3) | collective-permute-done | bytes 557088 | tf_op jit(solution)/shard_map/ppermute | solution.py:36
  53.9 2.1 %collective-permute-start.12 = (bf16[2,264,128]{2,1,0:T(8,128)(2,1)S(1)}, bf16[2,264,128]{2,1,0:T(8,128)(2,1)S(1)}, u32[]{:S(2)}, u32[]{:S(2)}) collective-permute-start(bf16[2,264,128]{2,1,0:T(8,128)(2,1)S(1)} %collective-permute-done.8.refs_0_), channel_id=1, source_target_pairs={{0,16},{16,0},{1,17},{17,1},{2,18},{18,2},{3,19},{19,3},{4,20},{20... | collective-permute-start | bytes 405512 | tf_op jit(solution)/shard_map/ppermute | solution.py:71
  56.0 4.4 %collective-permute-done.12.refs_4_ = bf16[2,264,128]{2,1,0:T(8,128)(2,1)S(1)} collective-permute-done((bf16[2,264,128]{2,1,0:T(8,128)(2,1)S(1)}, bf16[2,264,128]{2,1,0:T(8,128)(2,1)S(1)}, u32[]{:S(2)}, u32[]{:S(2)}) %collective-permute-start.12) | collective-permute-done | bytes 135200 | tf_op jit(solution)/shard_map/ppermute | solution.py:71
  60.4 1.9 %collective-permute-start.14 = (bf16[2,264,128]{2,1,0:T(8,128)(2,1)S(1)}, bf16[2,264,128]{2,1,0:T(8,128)(2,1)S(1)}, u32[]{:S(2)}, u32[]{:S(2)}) collective-permute-start(bf16[2,264,128]{2,1,0:T(8,128)(2,1)S(1)} %collective-permute-done.10.refs_2_), channel_id=1, source_target_pairs={{0,16},{16,0},{1,17},{17,1},{2,18},{18,2},{3,19},{19,3},{4,20},{20... | collective-permute-start | bytes 405512 | tf_op jit(solution)/shard_map/ppermute | solution.py:71
  63.3 1.9 %collective-permute-start.15 = (bf16[2,264,128]{2,1,0:T(8,128)(2,1)S(1)}, bf16[2,264,128]{2,1,0:T(8,128)(2,1)S(1)}, u32[]{:S(2)}, u32[]{:S(2)}) collective-permute-start(bf16[2,264,128]{2,1,0:T(8,128)(2,1)S(1)} %collective-permute-done.11.refs_3_), channel_id=1, source_target_pairs={{0,16},{16,0},{1,17},{17,1},{2,18},{18,2},{3,19},{19,3},{4,20},{20... | collective-permute-start | bytes 405512 | tf_op jit(solution)/shard_map/ppermute | solution.py:71
  66.3 2.6 %collective-permute-done.15.refs_7_ = bf16[2,264,128]{2,1,0:T(8,128)(2,1)S(1)} collective-permute-done((bf16[2,264,128]{2,1,0:T(8,128)(2,1)S(1)}, bf16[2,264,128]{2,1,0:T(8,128)(2,1)S(1)}, u32[]{:S(2)}, u32[]{:S(2)}) %collective-permute-start.15) | collective-permute-done | bytes 135200 | tf_op jit(solution)/shard_map/ppermute | solution.py:71
  68.9 1.8 %relayout_factors.1 = (bf16[2048,128]{1,0:T(8,128)(2,1)S(1)}, bf16[64,768]{1,0:T(8,128)(2,1)S(1)}, bf16[64,768]{1,0:T(8,128)(2,1)S(1)}, bf16[768,128]{1,0:T(8,128)(2,1)S(1)}, bf16[64,2048]{1,0:T(8,128)(2,1)S(1)}) custom-call(s32[2]{0:T(128)S(1)} %pad_add_fusion.place_ref, bf16[2,264,128]{2,1,0:T(8,128)(2,1)S(1)} %collective-permute-done.8.refs_0_, ...), custom_call_target="tpu_custom_call" | custom-call | tf_op jit(solution)/shard_map/relayout_factors/pallas_call | solution.py:223
  70.7 1.9 %copy-done.2 = bf16[1,768,2048]{2,1,0:T(8,128)(2,1)S(1)} copy-done((bf16[1,768,2048]{2,1,0:T(8,128)(2,1)S(1)}, bf16[1,768,2048]{2,1,0:T(8,128)(2,1)}, u32[]{:S(2)}) %copy-start.2) | copy-done | bytes 3145752
  72.6 8.2 %run_expert.3 = (f32[128,2048]{1,0:T(8,128)S(1)}, bf16[128,2048]{1,0:T(8,128)(2,1)S(1)}) custom-call(s32[2]{0:T(128)S(1)} %pad_add_fusion.place_ref, bf16[128,2176]{1,0:T(8,128)(2,1)S(1)} %bitcast.28, bf16[128,2176]{1,0:T(8,128)(2,1)S(1)} %collective-permute-done.24.refs_1_, bf16[2048,128]{1,0:T(8,128)(2,1)S(1)} %get-tuple-element.31.refs_4_.refs_2_, ...), custom_call_target="tpu_custom_call" | custom-call | flops 2785017856 | bytes 12058624 | tf_op jit(solution)/shard_map/run_expert/pallas_call | solution.py:310
  80.9 16.2 %run_expert.2 = (f32[256,2048]{1,0:T(8,128)S(1)}, bf16[256,2048]{1,0:T(8,128)(2,1)S(1)}) custom-call(s32[2]{0:T(128)S(1)} %pad_add_fusion.place_ref, bf16[128,2176]{1,0:T(8,128)(2,1)S(1)} %bitcast.31, bf16[128,2176]{1,0:T(8,128)(2,1)S(1)} %collective-permute-done.3.refs_1_, bf16[128,2176]{1,0:T(8,128)(2,1)S(1)} %collective-permute-done.4.refs_2_, ...), custom_call_target="tpu_custom_call" | custom-call | flops 5570035712 | bytes 14680064 | tf_op jit(solution)/shard_map/run_expert/pallas_call | solution.py:310
  97.8 3.3 %collective-permute-start.26 = (bf16[32,2048]{1,0:T(8,128)(2,1)S(1)}, bf16[32,2048]{1,0:T(8,128)(2,1)S(1)}, u32[]{:S(2)}, u32[]{:S(2)}) collective-permute-start(bf16[32,2048]{1,0:T(8,128)(2,1)S(1)} %get-tuple-element.48), channel_id=1, source_target_pairs={{0,12},{1,13},{2,14},{3,15},{4,0},{5,1},{6,2},{7,3},{8,4},{9,5},{1... | collective-permute-start | bytes 393224 | tf_op jit(solution)/shard_map/ppermute | solution.py:36
  103.2 1.9 %collective-permute-done.26 = bf16[32,2048]{1,0:T(8,128)(2,1)S(1)} collective-permute-done((bf16[32,2048]{1,0:T(8,128)(2,1)S(1)}, bf16[32,2048]{1,0:T(8,128)(2,1)S(1)}, u32[]{:S(2)}, u32[]{:S(2)}) %collective-permute-start.26) | collective-permute-done | bytes 131104 | tf_op jit(solution)/shard_map/ppermute | solution.py:36
  105.1 4.3 %collective-permute-done.28 = bf16[32,2048]{1,0:T(8,128)(2,1)S(1)} collective-permute-done((bf16[32,2048]{1,0:T(8,128)(2,1)S(1)}, bf16[32,2048]{1,0:T(8,128)(2,1)S(1)}, u32[]{:S(2)}, u32[]{:S(2)}) %collective-permute-start.28) | collective-permute-done | bytes 131104 | tf_op jit(solution)/shard_map/ppermute | solution.py:36
  109.4 4.4 %collective-permute-done.27 = bf16[32,2048]{1,0:T(8,128)(2,1)S(1)} collective-permute-done((bf16[32,2048]{1,0:T(8,128)(2,1)S(1)}, bf16[32,2048]{1,0:T(8,128)(2,1)S(1)}, u32[]{:S(2)}, u32[]{:S(2)}) %collective-permute-start.27) | collective-permute-done | bytes 131104 | tf_op jit(solution)/shard_map/ppermute | solution.py:36
  114.5 1.2 collective-permute-done.17
  115.9 3.0 %collective-permute-start.18 = (bf16[32,2048]{1,0:T(8,128)(2,1)S(1)}, bf16[32,2048]{1,0:T(8,128)(2,1)S(1)}, u32[]{:S(2)}, u32[]{:S(2)}) collective-permute-start(bf16[32,2048]{1,0:T(8,128)(2,1)S(1)} %get-tuple-element.45), channel_id=1, source_target_pairs={{0,12},{1,13},{2,14},{3,15},{4,0},{5,1},{6,2},{7,3},{8,4},{9,5},{1... | collective-permute-start | bytes 393224 | tf_op jit(solution)/shard_map/ppermute | solution.py:36
  120.0 1.4 %collective-permute-start.19 = (bf16[32,2048]{1,0:T(8,128)(2,1)S(1)}, bf16[32,2048]{1,0:T(8,128)(2,1)S(1)}, u32[]{:S(2)}, u32[]{:S(2)}) collective-permute-start(bf16[32,2048]{1,0:T(8,128)(2,1)S(1)} %get-tuple-element.47), channel_id=1, source_target_pairs={{0,8},{1,9},{2,10},{3,11},{4,12},{5,13},{6,14},{7,15},{8,0},{9,1},... | collective-permute-start | bytes 393224 | tf_op jit(solution)/shard_map/ppermute | solution.py:36
  121.4 4.3 %collective-permute-done.18 = bf16[32,2048]{1,0:T(8,128)(2,1)S(1)} collective-permute-done((bf16[32,2048]{1,0:T(8,128)(2,1)S(1)}, bf16[32,2048]{1,0:T(8,128)(2,1)S(1)}, u32[]{:S(2)}, u32[]{:S(2)}) %collective-permute-start.18) | collective-permute-done | bytes 131104 | tf_op jit(solution)/shard_map/ppermute | solution.py:36
  125.7 1.6 %collective-permute-done.20 = bf16[32,2048]{1,0:T(8,128)(2,1)S(1)} collective-permute-done((bf16[32,2048]{1,0:T(8,128)(2,1)S(1)}, bf16[32,2048]{1,0:T(8,128)(2,1)S(1)}, u32[]{:S(2)}, u32[]{:S(2)}) %collective-permute-start.20) | collective-permute-done | bytes 131104 | tf_op jit(solution)/shard_map/ppermute | solution.py:36
  127.3 3.5 %collective-permute-done.19 = bf16[32,2048]{1,0:T(8,128)(2,1)S(1)} collective-permute-done((bf16[32,2048]{1,0:T(8,128)(2,1)S(1)}, bf16[32,2048]{1,0:T(8,128)(2,1)S(1)}, u32[]{:S(2)}, u32[]{:S(2)}) %collective-permute-start.19) | collective-permute-done | bytes 131104 | tf_op jit(solution)/shard_map/ppermute | solution.py:36
  (70 shorter events, 17.6 us)
Async XLA Ops:
  2.0 68.7 %copy-start.1 = (bf16[1,2048,768]{2,1,0:T(8,128)(2,1)S(1)}, bf16[1,2048,768]{2,1,0:T(8,128)(2,1)}, u32[]{:S(2)}) copy-start(bf16[1,2048,768]{2,1,0:T(8,128)(2,1)} %param.14) | copy-start | bytes 9437188
  3.8 9.9 %collective-permute-start.7 = (bf16[4,264,128]{2,1,0:T(8,128)(2,1)S(1)}, bf16[4,264,128]{2,1,0:T(8,128)(2,1)S(1)}, u32[]{:S(2)}, u32[]{:S(2)}) collective-permute-start(bf16[4,264,128]{2,1,0:T(8,128)(2,1)S(1)} %get-tuple-element.26), channel_id=1, source_target_pairs={{0,2},{1,3},{2,0},{3,1},{4,6},{5,7},{6,4},{7,5},{8,10},{9,11},{10,... | collective-permute-start | bytes 811016 | tf_op jit(solution)/shard_map/ppermute | solution.py:36
  9.5 30.4 %collective-permute-start.2 = (bf16[32,2176]{1,0:T(8,128)(2,1)S(1)}, bf16[32,2176]{1,0:T(8,128)(2,1)S(1)}, u32[]{:S(2)}, u32[]{:S(2)}) collective-permute-start(bf16[32,2176]{1,0:T(8,128)(2,1)S(1)} %get-tuple-element.23), channel_id=1, source_target_pairs={{0,12},{1,13},{2,14},{3,15},{4,0},{5,1},{6,2},{7,3},{8,4},{9,5},{1... | collective-permute-start | bytes 417800 | tf_op jit(solution)/shard_map/ppermute | solution.py:36
  13.2 27.9 %collective-permute-start.1 = (bf16[32,2176]{1,0:T(8,128)(2,1)S(1)}, bf16[32,2176]{1,0:T(8,128)(2,1)S(1)}, u32[]{:S(2)}, u32[]{:S(2)}) collective-permute-start(bf16[32,2176]{1,0:T(8,128)(2,1)S(1)} %get-tuple-element.23), channel_id=1, source_target_pairs={{0,8},{1,9},{2,10},{3,11},{4,12},{5,13},{6,14},{7,15},{8,0},{9,1},... | collective-permute-start | bytes 417800 | tf_op jit(solution)/shard_map/ppermute | solution.py:36
  13.2 4.3 %collective-permute-start.6 = (bf16[16,2176]{1,0:T(8,128)(2,1)S(1)}, bf16[16,2176]{1,0:T(8,128)(2,1)S(1)}, u32[]{:S(2)}, u32[]{:S(2)}) collective-permute-start(bf16[16,2176]{1,0:T(8,128)(2,1)S(1)} %get-tuple-element.24), channel_id=1, source_target_pairs={{0,2},{1,3},{2,0},{3,1},{4,6},{5,7},{6,4},{7,5},{8,10},{9,11},{10,... | collective-permute-start | bytes 208904 | tf_op jit(solution)/shard_map/ppermute | solution.py:36
  13.8 4.7 %collective-permute-start.8 = (bf16[2,264,128]{2,1,0:T(8,128)(2,1)S(1)}, bf16[2,264,128]{2,1,0:T(8,128)(2,1)S(1)}, u32[]{:S(2)}, u32[]{:S(2)}) collective-permute-start(bf16[2,264,128]{2,1,0:T(8,128)(2,1)S(1)} %pad_maximum_fusion.4), channel_id=1, source_target_pairs={{0,0},{1,1},{2,2},{3,3},{4,4},{5,5},{6,6},{7,7},{8,8},{9,9},{10,10... | collective-permute-start | bytes 405512 | tf_op jit(solution)/shard_map/ppermute | solution.py:69
  14.5 56.2 %copy-start = (bf16[1,2048,768]{2,1,0:T(8,128)(2,1)S(1)}, bf16[1,2048,768]{2,1,0:T(8,128)(2,1)}, u32[]{:S(2)}) copy-start(bf16[1,2048,768]{2,1,0:T(8,128)(2,1)} %param.13) | copy-start | bytes 9437188
  14.5 9.7 %collective-permute-start.9 = (bf16[2,264,128]{2,1,0:T(8,128)(2,1)S(1)}, bf16[2,264,128]{2,1,0:T(8,128)(2,1)S(1)}, u32[]{:S(2)}, u32[]{:S(2)}) collective-permute-start(bf16[2,264,128]{2,1,0:T(8,128)(2,1)S(1)} %pad_maximum_fusion.5), channel_id=1, source_target_pairs={{0,4},{1,5},{2,6},{3,7},{4,8},{5,9},{6,10},{7,11},{8,12},{9,13},{1... | collective-permute-start | bytes 405512 | tf_op jit(solution)/shard_map/ppermute | solution.py:69
  17.5 23.6 %collective-permute-start = (bf16[32,2176]{1,0:T(8,128)(2,1)S(1)}, bf16[32,2176]{1,0:T(8,128)(2,1)S(1)}, u32[]{:S(2)}, u32[]{:S(2)}) collective-permute-start(bf16[32,2176]{1,0:T(8,128)(2,1)S(1)} %get-tuple-element.23), channel_id=1, source_target_pairs={{0,4},{1,5},{2,6},{3,7},{4,8},{5,9},{6,10},{7,11},{8,12},{9,13},{1... | collective-permute-start | bytes 417800 | tf_op jit(solution)/shard_map/ppermute | solution.py:36
  18.5 15.7 %collective-permute-start.10 = (bf16[2,264,128]{2,1,0:T(8,128)(2,1)S(1)}, bf16[2,264,128]{2,1,0:T(8,128)(2,1)S(1)}, u32[]{:S(2)}, u32[]{:S(2)}) collective-permute-start(bf16[2,264,128]{2,1,0:T(8,128)(2,1)S(1)} %pad_maximum_fusion.6), channel_id=1, source_target_pairs={{0,8},{1,9},{2,10},{3,11},{4,12},{5,13},{6,14},{7,15},{8,0},{9,1},... | collective-permute-start | bytes 405512 | tf_op jit(solution)/shard_map/ppermute | solution.py:69
  24.2 10.6 %collective-permute-start.11 = (bf16[2,264,128]{2,1,0:T(8,128)(2,1)S(1)}, bf16[2,264,128]{2,1,0:T(8,128)(2,1)S(1)}, u32[]{:S(2)}, u32[]{:S(2)}) collective-permute-start(bf16[2,264,128]{2,1,0:T(8,128)(2,1)S(1)} %pad_maximum_fusion.7), channel_id=1, source_target_pairs={{0,12},{1,13},{2,14},{3,15},{4,0},{5,1},{6,2},{7,3},{8,4},{9,5},{1... | collective-permute-start | bytes 405512 | tf_op jit(solution)/shard_map/ppermute | solution.py:69
  34.8 9.2 %collective-permute-start.23 = (bf16[32,2176]{1,0:T(8,128)(2,1)S(1)}, bf16[32,2176]{1,0:T(8,128)(2,1)S(1)}, u32[]{:S(2)}, u32[]{:S(2)}) collective-permute-start(bf16[32,2176]{1,0:T(8,128)(2,1)S(1)} %bitcast.36), channel_id=1, source_target_pairs={{0,12},{1,13},{2,14},{3,15},{4,0},{5,1},{6,2},{7,3},{8,4},{9,5},{1... | collective-permute-start | bytes 417800 | tf_op jit(solution)/shard_map/ppermute | solution.py:36
  39.9 11.1 %collective-permute-start.22 = (bf16[32,2176]{1,0:T(8,128)(2,1)S(1)}, bf16[32,2176]{1,0:T(8,128)(2,1)S(1)}, u32[]{:S(2)}, u32[]{:S(2)}) collective-permute-start(bf16[32,2176]{1,0:T(8,128)(2,1)S(1)} %bitcast.37), channel_id=1, source_target_pairs={{0,8},{1,9},{2,10},{3,11},{4,12},{5,13},{6,14},{7,15},{8,0},{9,1},... | collective-permute-start | bytes 417800 | tf_op jit(solution)/shard_map/ppermute | solution.py:36
  39.9 11.1 %collective-permute-start.21 = (bf16[32,2176]{1,0:T(8,128)(2,1)S(1)}, bf16[32,2176]{1,0:T(8,128)(2,1)S(1)}, u32[]{:S(2)}, u32[]{:S(2)}) collective-permute-start(bf16[32,2176]{1,0:T(8,128)(2,1)S(1)} %bitcast.38), channel_id=1, source_target_pairs={{0,4},{1,5},{2,6},{3,7},{4,8},{5,9},{6,10},{7,11},{8,12},{9,13},{1... | collective-permute-start | bytes 417800 | tf_op jit(solution)/shard_map/ppermute | solution.py:36
  41.2 12.7 %collective-permute-start.3 = (bf16[128,2176]{1,0:T(8,128)(2,1)S(1)}, bf16[128,2176]{1,0:T(8,128)(2,1)S(1)}, u32[]{:S(2)}, u32[]{:S(2)}) collective-permute-start(bf16[128,2176]{1,0:T(8,128)(2,1)S(1)} %bitcast.29), channel_id=1, source_target_pairs={{0,2},{1,3},{2,0},{3,1},{4,6},{5,7},{6,4},{7,5},{8,10},{9,11},{10,... | collective-permute-start | bytes 1671176 | tf_op jit(solution)/shard_map/ppermute | solution.py:36
  51.1 19.5 %collective-permute-start.24 = (bf16[128,2176]{1,0:T(8,128)(2,1)S(1)}, bf16[128,2176]{1,0:T(8,128)(2,1)S(1)}, u32[]{:S(2)}, u32[]{:S(2)}) collective-permute-start(bf16[128,2176]{1,0:T(8,128)(2,1)S(1)} %bitcast.27), channel_id=1, source_target_pairs={{0,1},{1,0},{2,3},{3,2},{4,5},{5,4},{6,7},{7,6},{8,9},{9,8},{10,11... | collective-permute-start | bytes 1671176 | tf_op jit(solution)/shard_map/ppermute | solution.py:36
  51.2 29.7 %collective-permute-start.4 = (bf16[128,2176]{1,0:T(8,128)(2,1)S(1)}, bf16[128,2176]{1,0:T(8,128)(2,1)S(1)}, u32[]{:S(2)}, u32[]{:S(2)}) collective-permute-start(bf16[128,2176]{1,0:T(8,128)(2,1)S(1)} %bitcast.30), channel_id=1, source_target_pairs={{0,1},{1,0},{2,3},{3,2},{4,5},{5,4},{6,7},{7,6},{8,9},{9,8},{10,11... | collective-permute-start | bytes 1671176 | tf_op jit(solution)/shard_map/ppermute | solution.py:36
  53.8 27.0 %collective-permute-start.5 = (bf16[128,2176]{1,0:T(8,128)(2,1)S(1)}, bf16[128,2176]{1,0:T(8,128)(2,1)S(1)}, u32[]{:S(2)}, u32[]{:S(2)}) collective-permute-start(bf16[128,2176]{1,0:T(8,128)(2,1)S(1)} %collective-permute-done.3.refs_1_), channel_id=1, source_target_pairs={{0,1},{1,0},{2,3},{3,2},{4,5},{5,4},{6,7},{7,6},{8,9},{9,8},{10,11... | collective-permute-start | bytes 1671176 | tf_op jit(solution)/shard_map/ppermute | solution.py:36
  53.9 6.5 %collective-permute-start.12 = (bf16[2,264,128]{2,1,0:T(8,128)(2,1)S(1)}, bf16[2,264,128]{2,1,0:T(8,128)(2,1)S(1)}, u32[]{:S(2)}, u32[]{:S(2)}) collective-permute-start(bf16[2,264,128]{2,1,0:T(8,128)(2,1)S(1)} %collective-permute-done.8.refs_0_), channel_id=1, source_target_pairs={{0,16},{16,0},{1,17},{17,1},{2,18},{18,2},{3,19},{19,3},{4,20},{20... | collective-permute-start | bytes 405512 | tf_op jit(solution)/shard_map/ppermute | solution.py:71
  55.9 7.3 %collective-permute-start.13 = (bf16[2,264,128]{2,1,0:T(8,128)(2,1)S(1)}, bf16[2,264,128]{2,1,0:T(8,128)(2,1)S(1)}, u32[]{:S(2)}, u32[]{:S(2)}) collective-permute-start(bf16[2,264,128]{2,1,0:T(8,128)(2,1)S(1)} %collective-permute-done.9.refs_1_), channel_id=1, source_target_pairs={{0,16},{16,0},{1,17},{17,1},{2,18},{18,2},{3,19},{19,3},{4,20},{20... | collective-permute-start | bytes 405512 | tf_op jit(solution)/shard_map/ppermute | solution.py:71
  60.4 5.9 %collective-permute-start.14 = (bf16[2,264,128]{2,1,0:T(8,128)(2,1)S(1)}, bf16[2,264,128]{2,1,0:T(8,128)(2,1)S(1)}, u32[]{:S(2)}, u32[]{:S(2)}) collective-permute-start(bf16[2,264,128]{2,1,0:T(8,128)(2,1)S(1)} %collective-permute-done.10.refs_2_), channel_id=1, source_target_pairs={{0,16},{16,0},{1,17},{17,1},{2,18},{18,2},{3,19},{19,3},{4,20},{20... | collective-permute-start | bytes 405512 | tf_op jit(solution)/shard_map/ppermute | solution.py:71
  63.3 5.6 %collective-permute-start.15 = (bf16[2,264,128]{2,1,0:T(8,128)(2,1)S(1)}, bf16[2,264,128]{2,1,0:T(8,128)(2,1)S(1)}, u32[]{:S(2)}, u32[]{:S(2)}) collective-permute-start(bf16[2,264,128]{2,1,0:T(8,128)(2,1)S(1)} %collective-permute-done.11.refs_3_), channel_id=1, source_target_pairs={{0,16},{16,0},{1,17},{17,1},{2,18},{18,2},{3,19},{19,3},{4,20},{20... | collective-permute-start | bytes 405512 | tf_op jit(solution)/shard_map/ppermute | solution.py:71
  80.8 16.8 %collective-permute-start.25 = (bf16[128,2048]{1,0:T(8,128)(2,1)S(1)}, bf16[128,2048]{1,0:T(8,128)(2,1)S(1)}, u32[]{:S(2)}, u32[]{:S(2)}) collective-permute-start(bf16[128,2048]{1,0:T(8,128)(2,1)S(1)} %get-tuple-element.40), channel_id=1, source_target_pairs={{0,1},{1,0},{2,3},{3,2},{4,5},{5,4},{6,7},{7,6},{8,9},{9,8},{10,11... | collective-permute-start | bytes 1572872 | tf_op jit(solution)/shard_map/ppermute | solution.py:36
  97.1 5.2 %collective-permute-start.16 = (bf16[256,2048]{1,0:T(8,128)(2,1)S(1)}, bf16[256,2048]{1,0:T(8,128)(2,1)S(1)}, u32[]{:S(2)}, u32[]{:S(2)}) collective-permute-start(bf16[256,2048]{1,0:T(8,128)(2,1)S(1)} %get-tuple-element.37), channel_id=1, source_target_pairs={{0,1},{1,0},{2,3},{3,2},{4,5},{5,4},{6,7},{7,6},{8,9},{9,8},{10,11... | collective-permute-start | bytes 3145736 | tf_op jit(solution)/shard_map/ppermute | solution.py:36
  97.8 7.2 %collective-permute-start.26 = (bf16[32,2048]{1,0:T(8,128)(2,1)S(1)}, bf16[32,2048]{1,0:T(8,128)(2,1)S(1)}, u32[]{:S(2)}, u32[]{:S(2)}) collective-permute-start(bf16[32,2048]{1,0:T(8,128)(2,1)S(1)} %get-tuple-element.48), channel_id=1, source_target_pairs={{0,12},{1,13},{2,14},{3,15},{4,0},{5,1},{6,2},{7,3},{8,4},{9,5},{1... | collective-permute-start | bytes 393224 | tf_op jit(solution)/shard_map/ppermute | solution.py:36
  101.1 8.3 %collective-permute-start.28 = (bf16[32,2048]{1,0:T(8,128)(2,1)S(1)}, bf16[32,2048]{1,0:T(8,128)(2,1)S(1)}, u32[]{:S(2)}, u32[]{:S(2)}) collective-permute-start(bf16[32,2048]{1,0:T(8,128)(2,1)S(1)} %get-tuple-element.49), channel_id=1, source_target_pairs={{0,4},{1,5},{2,6},{3,7},{4,8},{5,9},{6,10},{7,11},{8,12},{9,13},{1... | collective-permute-start | bytes 393224 | tf_op jit(solution)/shard_map/ppermute | solution.py:36
  101.1 12.7 %collective-permute-start.27 = (bf16[32,2048]{1,0:T(8,128)(2,1)S(1)}, bf16[32,2048]{1,0:T(8,128)(2,1)S(1)}, u32[]{:S(2)}, u32[]{:S(2)}) collective-permute-start(bf16[32,2048]{1,0:T(8,128)(2,1)S(1)} %get-tuple-element.50), channel_id=1, source_target_pairs={{0,8},{1,9},{2,10},{3,11},{4,12},{5,13},{6,14},{7,15},{8,0},{9,1},... | collective-permute-start | bytes 393224 | tf_op jit(solution)/shard_map/ppermute | solution.py:36
  102.6 13.1 %collective-permute-start.17 = (bf16[128,2048]{1,0:T(8,128)(2,1)S(1)}, bf16[128,2048]{1,0:T(8,128)(2,1)S(1)}, u32[]{:S(2)}, u32[]{:S(2)}) collective-permute-start(bf16[128,2048]{1,0:T(8,128)(2,1)S(1)} %slice.122), channel_id=1, source_target_pairs={{0,2},{1,3},{2,0},{3,1},{4,6},{5,7},{6,4},{7,5},{8,10},{9,11},{10,... | collective-permute-start | bytes 1572872 | tf_op jit(solution)/shard_map/ppermute | solution.py:36
  113.9 7.5 %collective-permute-start.29 = (bf16[16,2048]{1,0:T(8,128)(2,1)S(1)}, bf16[16,2048]{1,0:T(8,128)(2,1)S(1)}, u32[]{:S(2)}, u32[]{:S(2)}) collective-permute-start(bf16[16,2048]{1,0:T(8,128)(2,1)S(1)} %slice.123), channel_id=1, source_target_pairs={{0,2},{1,3},{2,0},{3,1},{4,6},{5,7},{6,4},{7,5},{8,10},{9,11},{10,... | collective-permute-start | bytes 196616 | tf_op jit(solution)/shard_map/ppermute | solution.py:36
  115.9 9.7 %collective-permute-start.18 = (bf16[32,2048]{1,0:T(8,128)(2,1)S(1)}, bf16[32,2048]{1,0:T(8,128)(2,1)S(1)}, u32[]{:S(2)}, u32[]{:S(2)}) collective-permute-start(bf16[32,2048]{1,0:T(8,128)(2,1)S(1)} %get-tuple-element.45), channel_id=1, source_target_pairs={{0,12},{1,13},{2,14},{3,15},{4,0},{5,1},{6,2},{7,3},{8,4},{9,5},{1... | collective-permute-start | bytes 393224 | tf_op jit(solution)/shard_map/ppermute | solution.py:36
  118.9 8.3 %collective-permute-start.20 = (bf16[32,2048]{1,0:T(8,128)(2,1)S(1)}, bf16[32,2048]{1,0:T(8,128)(2,1)S(1)}, u32[]{:S(2)}, u32[]{:S(2)}) collective-permute-start(bf16[32,2048]{1,0:T(8,128)(2,1)S(1)} %get-tuple-element.46), channel_id=1, source_target_pairs={{0,4},{1,5},{2,6},{3,7},{4,8},{5,9},{6,10},{7,11},{8,12},{9,13},{1... | collective-permute-start | bytes 393224 | tf_op jit(solution)/shard_map/ppermute | solution.py:36
  120.0 10.8 %collective-permute-start.19 = (bf16[32,2048]{1,0:T(8,128)(2,1)S(1)}, bf16[32,2048]{1,0:T(8,128)(2,1)S(1)}, u32[]{:S(2)}, u32[]{:S(2)}) collective-permute-start(bf16[32,2048]{1,0:T(8,128)(2,1)S(1)} %get-tuple-element.47), channel_id=1, source_target_pairs={{0,8},{1,9},{2,10},{3,11},{4,12},{5,13},{6,14},{7,15},{8,0},{9,1},... | collective-permute-start | bytes 393224 | tf_op jit(solution)/shard_map/ppermute | solution.py:36
  (6 other events, 6.1 us)

commit v7 on v6

--- a/solution.py
+++ b/solution.py
@@ -56,7 +56,6 @@
 def exchange_factors(blocks, n):
     outer, middle, cores = split_axis(n)
     stride = middle * cores
-    turned = [blocks[0]] + [shift(blocks[r], n, cores, middle, r) for r in range(1, middle)]
     here, there = [], []
     for q in range(outer):
         pairs = []
@@ -65,7 +64,7 @@
                 place = i // stride
                 to = (i + ((place + q) % outer - place) * stride) ^ g
                 pairs.append((g * n + i, g * n + to))
-        part = jnp.stack([t[q] for t in turned])
+        part = jnp.stack([block[q] for block in blocks])
         part = lax.ppermute(part, ("group", "expert"), pairs)
         here.append(part)
         there.append(lax.ppermute(part, "group", [(0, 1), (1, 0)]))
@@ -239,7 +238,7 @@
     a_gu_hbm, gate_b_hbm, up_b_hbm, down_a_hbm, down_b_hbm = refs[:5]
     w_gate_hbm, w_up_hbm, w_down_hbm, kept_hbm, sent_hbm = refs[5:10]
     x_ref, a_gu_ref, gate_b_ref, up_b_ref, down_a_ref, down_b_ref = refs[10:16]
-    w_gate_ref, w_up_ref, w_down_ref, inner_ref, kept_ref, sent_ref, sem, out_sem = refs[16:]
+    w_gate_ref, w_up_ref, w_down_ref, kept_ref, sent_ref, sem, out_sem = refs[16:]
     rows = pieces[0].shape[0]
     units, width = w_down_ref.shape
     rank = gate_b_ref.shape[0]
@@ -267,32 +266,45 @@
     up_in = begin_rows(w_up_hbm, w_up_ref) + [begin(up_b_hbm, up_b_ref)]
     down_in = [begin(down_a_hbm, down_a_ref), begin(down_b_hbm, down_b_ref)]
     down_in += begin_rows(w_down_hbm, w_down_ref)
-
     wait(x_in)
-    gates = x_ref[:, width:].astype(jnp.float32)
-    lane = lax.broadcasted_iota(jnp.int32, gates.shape, 1)
-    mine = jnp.sum(jnp.where(lane == place_ref[1], gates, 0.0), axis=1, keepdims=True)
-    low = (adapter_scale * dot(x_ref[:, :width], a_gu_ref[...])).astype(jnp.bfloat16)
-    wait(gate_in)
-    g = dot(x_ref[:, :width], w_gate_ref[...]) + dot(low[:, :rank], gate_b_ref[...])
-    wait(up_in)
-    u = dot(x_ref[:, :width], w_up_ref[...]) + dot(low[:, rank:], up_b_ref[...])
-    inner_ref[...] = (g / (1.0 + jnp.exp(-g)) * u).astype(jnp.bfloat16)
-    wait(down_in)
-    low = (adapter_scale * dot(inner_ref[...], down_a_ref[...])).astype(jnp.bfloat16)[:, :rank]
-    out_copies = []
-    block = width // 2
-    for i, cut in enumerate((slice(0, block), slice(block, width))):
-        out = dot(inner_ref[...], w_down_ref[:, cut]) + dot(low, down_b_ref[:, cut])
-        out = out * mine
-        sent_ref[:, cut] = out[own:].astype(jnp.bfloat16)
-        kept_ref[:, cut] = out[:own]
-        for j, (src, dst) in enumerate(((sent_ref, sent_hbm), (kept_ref, kept_hbm))):
-            copy = pltpu.make_async_copy(src.at[:, cut], dst.at[:, cut], out_sem.at[2 * i + j])
-            copy.start()
-            out_copies.append(copy)
-    for copy in out_copies:
-        copy.wait()
+
+    def run_piece(i, carry):
+        here = pl.ds(pl.multiple_of(i * rows, rows), rows)
+        gates = x_ref[here, width:].astype(jnp.float32)
+        lane = lax.broadcasted_iota(jnp.int32, gates.shape, 1)
+        mine = jnp.sum(jnp.where(lane == place_ref[1], gates, 0.0), axis=1, keepdims=True)
+        low = (adapter_scale * dot(x_ref[here, :width], a_gu_ref[...])).astype(jnp.bfloat16)
+        pl.when(i == 0)(lambda: wait(gate_in))
+        g = dot(x_ref[here, :width], w_gate_ref[...]) + dot(low[:, :rank], gate_b_ref[...])
+        pl.when(i == 0)(lambda: wait(up_in))
+        u = dot(x_ref[here, :width], w_up_ref[...]) + dot(low[:, rank:], up_b_ref[...])
+        inner = (g / (1.0 + jnp.exp(-g)) * u).astype(jnp.bfloat16)
+        pl.when(i == 0)(lambda: wait(down_in))
+        low = (adapter_scale * dot(inner, down_a_ref[...])).astype(jnp.bfloat16)[:, :rank]
+        out = (dot(inner, w_down_ref[...]) + dot(low, down_b_ref[...])) * mine
+
+        @pl.when(i < len(pieces) // 2)
+        def _():
+            kept_ref[here, :] = out
+            pltpu.make_async_copy(
+                kept_ref.at[here], kept_hbm.at[here], out_sem.at[i]
+            ).start()
+
+        @pl.when(i >= len(pieces) // 2)
+        def _():
+            there = pl.ds(pl.multiple_of(i * rows - own, rows), rows)
+            sent_ref[there, :] = out.astype(jnp.bfloat16)
+            pltpu.make_async_copy(
+                sent_ref.at[there], sent_hbm.at[there], out_sem.at[i]
+            ).start()
+
+        return carry
+
+    lax.fori_loop(0, len(pieces), run_piece, 0)
+    for i in range(len(pieces)):
+        src, dst = (kept_ref, kept_hbm) if i < len(pieces) // 2 else (sent_ref, sent_hbm)
+        at = pl.ds(i % (len(pieces) // 2) * rows, rows)
+        pltpu.make_async_copy(src.at[at], dst.at[at], out_sem.at[i]).wait()
 
 
 def run_expert(place, pieces, low_rank, w_gate, w_up, w_down):
@@ -317,11 +329,10 @@
         scratch_shapes=[pltpu.VMEM((total, pieces[0].shape[1]), jnp.bfloat16)]
         + [pltpu.VMEM(a.shape, a.dtype) for a in kept]
         + [
-            pltpu.VMEM((total, units), jnp.bfloat16),
             pltpu.VMEM(outs[0].shape, outs[0].dtype),
             pltpu.VMEM(outs[1].shape, outs[1].dtype),
             pltpu.SemaphoreType.DMA((copies,)),
-            pltpu.SemaphoreType.DMA((4,)),
+            pltpu.SemaphoreType.DMA((len(pieces),)),
         ],
         compiler_params=pltpu.CompilerParams(vmem_limit_bytes=EXPERT_GRANT),
         cost_estimate=pl.CostEstimate(
@@ -347,13 +358,16 @@
 
     first = max(1, steps * 2 // 3)
     head, tail = make_payload(hidden, route_ids, route_logits, experts, first)
+    head, factors = lax.optimization_barrier((head, factors))
     tail = gather_along(tail, owners, *along_middle)
     head = gather_along(head, owners, *along_outer)
     blocks = order_factors(place, placement, factors, owners)
+    blocks = [blocks[0]] + [shift(blocks[r], owners, *along_middle, r) for r in range(1, middle)]
+    head, blocks = lax.optimization_barrier((head, blocks))
     here, there = exchange_factors(blocks, owners)
     heads = [head] + [shift(head, owners, *along_middle, k) for k in range(1, middle)]
     heads += [shift(p, owners, 1, cores, 1) for p in heads]
-    tail, here = lax.optimization_barrier((tail, here))
+    tail, there = lax.optimization_barrier((tail, there))
     tail = gather_along(tail, owners, *along_outer)
     tails = [tail, shift(tail, owners, 1, cores, 1)]
 

time: 132 us -> 128 us (0.970)
  waiting for transfers between devices: 54.6 us -> 46.4 us
  starting transfers between devices: 40.3 us -> 43.2 us
  Pallas kernels: 28.3 us -> 30 us
    ppermute x4, waiting for transfers between devices: 11.4 us -> 2.15 us  [exchange_factors(): part = lax.ppermute(part, ('group', 'expert'), pairs)]
    ppermute x22, waiting for transfers between devices: 34.2 us -> 37.6 us  [shift(): return lax.ppermute(x, 'expert', pairs)]
    ppermute x22, starting transfers between devices: 27.3 us -> 29.7 us  [shift(): return lax.ppermute(x, 'expert', pairs)]
    ppermute x4, waiting for transfers between devices: 9.01 us -> 6.68 us  [exchange_factors(): there.append(lax.ppermute(part, 'group', [(0, 1), (1, 0)]))]
    pallas_call x2, Pallas kernels: 24.4 us -> 26.2 us  [run_expert(): pl.pallas_call(functools.partial(expert_kernel, len(pieces)), out_shape=o...]
  transfers between devices with their start and end apart: 30 -> 30, of which waited for: 18 -> 15; matrix products, arithmetic and copies ran while one was open for 1% -> 1% of each run, Pallas kernels for 20% -> 23%
where the time goes in v7:
time: 128 us
  waiting for transfers between devices  46.4 us (36%)
  starting transfers between devices  43.2 us (34%)
  Pallas kernels  30 us (23%)
  local copies, waits for them, and re-layouts  6.29 us (5%)
  other arithmetic  1.72 us (1%)
    ppermute x22, waiting for transfers between devices, shift(): return lax.ppermute(x, 'expert', pairs)  37.6 us
    ppermute x22, starting transfers between devices, shift(): return lax.ppermute(x, 'expert', pairs)  29.7 us
    pallas_call x2, Pallas kernels, run_expert(): pl.pallas_call(functools.partial(expert_kernel, len(pieces)), out_shape=o...  26.2 us
    ppermute x4, starting transfers between devices, exchange_factors(): there.append(lax.ppermute(part, 'group', [(0, 1), (1, 0)]))  7.23 us
    ppermute x4, waiting for transfers between devices, exchange_factors(): there.append(lax.ppermute(part, 'group', [(0, 1), (1, 0)]))  6.68 us
    ppermute x4, starting transfers between devices, exchange_factors(): part = lax.ppermute(part, ('group', 'expert'), pairs)  6.28 us
    unnamed x16, local copies, waits for them, and re-layouts  6.12 us
  transfers between devices with their start and end apart: 30, of which 15 were waited for; matrix products, arithmetic and copies ran while one was open for 1% of the time, Pallas kernels for 23%

profile of v7, /device:TPU:0, one launch (start us, length us, event | category | flops | bytes accessed | tf_op | source)
XLA Modules:
  0.0 127.9 jit_solution(9130029161428963942)
XLA Ops:
  2.7 5.1 %collective-permute-start.2 = (bf16[32,2176]{1,0:T(8,128)(2,1)S(1)}, bf16[32,2176]{1,0:T(8,128)(2,1)S(1)}, u32[]{:S(2)}, u32[]{:S(2)}) collective-permute-start(bf16[32,2176]{1,0:T(8,128)(2,1)S(1)} %get-tuple-element.29), channel_id=1, source_target_pairs={{0,12},{1,13},{2,14},{3,15},{4,0},{5,1},{6,2},{7,3},{8,4},{9,5},{1... | collective-permute-start | bytes 417800 | tf_op jit(solution)/shard_map/ppermute | solution.py:36
  8.9 1.2 copy-done.3
  10.7 1.8 %order_factors.1 = (bf16[4,264,128]{2,1,0:T(8,128)(2,1)S(1)}, bf16[4,264,128]{2,1,0:T(8,128)(2,1)S(1)}) custom-call(s32[2]{0:T(128)S(1)} %pad_add_fusion.place_ref, s32[16]{0:T(128)S(1)} %copy-done.7, bf16[16,33792]{1,0:T(8,128)(2,1)S(1)} %copy-done.3), custom_call_target="tpu_custom_call" | custom-call | tf_op jit(solution)/shard_map/order_factors/pallas_call | solution.py:151
  12.6 1.6 %collective-permute-start.3 = (bf16[4,264,128]{2,1,0:T(8,128)(2,1)S(1)}, bf16[4,264,128]{2,1,0:T(8,128)(2,1)S(1)}, u32[]{:S(2)}, u32[]{:S(2)}) collective-permute-start(bf16[4,264,128]{2,1,0:T(8,128)(2,1)S(1)} %get-tuple-element.32), channel_id=1, source_target_pairs={{0,2},{1,3},{2,0},{3,1},{4,6},{5,7},{6,4},{7,5},{8,10},{9,11},{10,... | collective-permute-start | bytes 811016 | tf_op jit(solution)/shard_map/ppermute | solution.py:36
  14.2 5.4 %collective-permute-done.1 = bf16[32,2176]{1,0:T(8,128)(2,1)S(1)} collective-permute-done((bf16[32,2176]{1,0:T(8,128)(2,1)S(1)}, bf16[32,2176]{1,0:T(8,128)(2,1)S(1)}, u32[]{:S(2)}, u32[]{:S(2)}) %collective-permute-start.1) | collective-permute-done | bytes 139296 | tf_op jit(solution)/shard_map/ppermute | solution.py:36
  20.9 2.5 %collective-permute-start.8 = (bf16[2,264,128]{2,1,0:T(8,128)(2,1)S(1)}, bf16[2,264,128]{2,1,0:T(8,128)(2,1)S(1)}, u32[]{:S(2)}, u32[]{:S(2)}) collective-permute-start(bf16[2,264,128]{2,1,0:T(8,128)(2,1)S(1)} %pad_maximum_fusion.5), channel_id=1, source_target_pairs={{0,4},{1,5},{2,6},{3,7},{4,8},{5,9},{6,10},{7,11},{8,12},{9,13},{1... | collective-permute-start | bytes 405512 | tf_op jit(solution)/shard_map/ppermute | solution.py:68
  23.5 1.2 collective-permute-start.9
  24.8 1.7 %collective-permute-start.10 = (bf16[2,264,128]{2,1,0:T(8,128)(2,1)S(1)}, bf16[2,264,128]{2,1,0:T(8,128)(2,1)S(1)}, u32[]{:S(2)}, u32[]{:S(2)}) collective-permute-start(bf16[2,264,128]{2,1,0:T(8,128)(2,1)S(1)} %pad_maximum_fusion.7), channel_id=1, source_target_pairs={{0,12},{1,13},{2,14},{3,15},{4,0},{5,1},{6,2},{7,3},{8,4},{9,5},{1... | collective-permute-start | bytes 405512 | tf_op jit(solution)/shard_map/ppermute | solution.py:68
  26.5 1.5 %collective-permute-start.11 = (bf16[16,2176]{1,0:T(8,128)(2,1)S(1)}, bf16[16,2176]{1,0:T(8,128)(2,1)S(1)}, u32[]{:S(2)}, u32[]{:S(2)}) collective-permute-start(bf16[16,2176]{1,0:T(8,128)(2,1)S(1)} %get-tuple-element.36), channel_id=1, source_target_pairs={{0,2},{1,3},{2,0},{3,1},{4,6},{5,7},{6,4},{7,5},{8,10},{9,11},{10,... | collective-permute-start | bytes 208904 | tf_op jit(solution)/shard_map/ppermute | solution.py:36
  28.0 2.7 %collective-permute-start.12 = (bf16[2,264,128]{2,1,0:T(8,128)(2,1)S(1)}, bf16[2,264,128]{2,1,0:T(8,128)(2,1)S(1)}, u32[]{:S(2)}, u32[]{:S(2)}) collective-permute-start(bf16[2,264,128]{2,1,0:T(8,128)(2,1)S(1)} %collective-permute-done.7.refs_0_), channel_id=1, source_target_pairs={{0,16},{16,0},{1,17},{17,1},{2,18},{18,2},{3,19},{19,3},{4,20},{20... | collective-permute-start | bytes 405512 | tf_op jit(solution)/shard_map/ppermute | solution.py:70
  31.0 2.1 %collective-permute-done.9.refs_2_ = bf16[2,264,128]{2,1,0:T(8,128)(2,1)S(1)} collective-permute-done((bf16[2,264,128]{2,1,0:T(8,128)(2,1)S(1)}, bf16[2,264,128]{2,1,0:T(8,128)(2,1)S(1)}, u32[]{:S(2)}, u32[]{:S(2)}) %collective-permute-start.9) | collective-permute-done | bytes 135200 | tf_op jit(solution)/shard_map/ppermute | solution.py:68
  33.2 4.2 %collective-permute-start.14 = (bf16[2,264,128]{2,1,0:T(8,128)(2,1)S(1)}, bf16[2,264,128]{2,1,0:T(8,128)(2,1)S(1)}, u32[]{:S(2)}, u32[]{:S(2)}) collective-permute-start(bf16[2,264,128]{2,1,0:T(8,128)(2,1)S(1)} %collective-permute-done.9.refs_2_), channel_id=1, source_target_pairs={{0,16},{16,0},{1,17},{17,1},{2,18},{18,2},{3,19},{19,3},{4,20},{20... | collective-permute-start | bytes 405512 | tf_op jit(solution)/shard_map/ppermute | solution.py:70
  37.4 4.3 %collective-permute-done.14.refs_6_ = bf16[2,264,128]{2,1,0:T(8,128)(2,1)S(1)} collective-permute-done((bf16[2,264,128]{2,1,0:T(8,128)(2,1)S(1)}, bf16[2,264,128]{2,1,0:T(8,128)(2,1)S(1)}, u32[]{:S(2)}, u32[]{:S(2)}) %collective-permute-start.14) | collective-permute-done | bytes 135200 | tf_op jit(solution)/shard_map/ppermute | solution.py:70
  41.7 2.4 %collective-permute-done.15.refs_7_ = bf16[2,264,128]{2,1,0:T(8,128)(2,1)S(1)} collective-permute-done((bf16[2,264,128]{2,1,0:T(8,128)(2,1)S(1)}, bf16[2,264,128]{2,1,0:T(8,128)(2,1)S(1)}, u32[]{:S(2)}, u32[]{:S(2)}) %collective-permute-start.15) | collective-permute-done | bytes 135200 | tf_op jit(solution)/shard_map/ppermute | solution.py:70
  44.1 4.1 %collective-permute-start.23 = (bf16[32,2176]{1,0:T(8,128)(2,1)S(1)}, bf16[32,2176]{1,0:T(8,128)(2,1)S(1)}, u32[]{:S(2)}, u32[]{:S(2)}) collective-permute-start(bf16[32,2176]{1,0:T(8,128)(2,1)S(1)} %bitcast.36), channel_id=1, source_target_pairs={{0,12},{1,13},{2,14},{3,15},{4,0},{5,1},{6,2},{7,3},{8,4},{9,5},{1... | collective-permute-start | bytes 417800 | tf_op jit(solution)/shard_map/ppermute | solution.py:36
  48.8 1.5 %collective-permute-start.4 = (bf16[128,2176]{1,0:T(8,128)(2,1)S(1)}, bf16[128,2176]{1,0:T(8,128)(2,1)S(1)}, u32[]{:S(2)}, u32[]{:S(2)}) collective-permute-start(bf16[128,2176]{1,0:T(8,128)(2,1)S(1)} %bitcast.29), channel_id=1, source_target_pairs={{0,2},{1,3},{2,0},{3,1},{4,6},{5,7},{6,4},{7,5},{8,10},{9,11},{10,... | collective-permute-start | bytes 1671176 | tf_op jit(solution)/shard_map/ppermute | solution.py:36
  50.3 2.0 %collective-permute-done.23 = bf16[32,2176]{1,0:T(8,128)(2,1)S(1)} collective-permute-done((bf16[32,2176]{1,0:T(8,128)(2,1)S(1)}, bf16[32,2176]{1,0:T(8,128)(2,1)S(1)}, u32[]{:S(2)}, u32[]{:S(2)}) %collective-permute-start.23) | collective-permute-done | bytes 139296 | tf_op jit(solution)/shard_map/ppermute | solution.py:36
  52.3 7.9 %collective-permute-done.22 = bf16[32,2176]{1,0:T(8,128)(2,1)S(1)} collective-permute-done((bf16[32,2176]{1,0:T(8,128)(2,1)S(1)}, bf16[32,2176]{1,0:T(8,128)(2,1)S(1)}, u32[]{:S(2)}, u32[]{:S(2)}) %collective-permute-start.22) | collective-permute-done | bytes 139296 | tf_op jit(solution)/shard_map/ppermute | solution.py:36
  60.8 1.8 %collective-permute-done.4.refs_1_ = bf16[128,2176]{1,0:T(8,128)(2,1)S(1)} collective-permute-done((bf16[128,2176]{1,0:T(8,128)(2,1)S(1)}, bf16[128,2176]{1,0:T(8,128)(2,1)S(1)}, u32[]{:S(2)}, u32[]{:S(2)}) %collective-permute-start.4) | collective-permute-done | bytes 557088 | tf_op jit(solution)/shard_map/ppermute | solution.py:36
  62.6 1.6 %relayout_factors.1 = (bf16[2048,128]{1,0:T(8,128)(2,1)S(1)}, bf16[64,768]{1,0:T(8,128)(2,1)S(1)}, bf16[64,768]{1,0:T(8,128)(2,1)S(1)}, bf16[768,128]{1,0:T(8,128)(2,1)S(1)}, bf16[64,2048]{1,0:T(8,128)(2,1)S(1)}) custom-call(s32[2]{0:T(128)S(1)} %pad_add_fusion.place_ref, bf16[2,264,128]{2,1,0:T(8,128)(2,1)S(1)} %collective-permute-done.7.refs_0_, ...), custom_call_target="tpu_custom_call" | custom-call | tf_op jit(solution)/shard_map/relayout_factors/pallas_call | solution.py:222
  64.3 1.9 %copy-done.2 = bf16[1,768,2048]{2,1,0:T(8,128)(2,1)S(1)} copy-done((bf16[1,768,2048]{2,1,0:T(8,128)(2,1)S(1)}, bf16[1,768,2048]{2,1,0:T(8,128)(2,1)}, u32[]{:S(2)}) %copy-start.2) | copy-done | bytes 3145752
  66.1 9.4 %run_expert.3 = (f32[128,2048]{1,0:T(8,128)S(1)}, bf16[128,2048]{1,0:T(8,128)(2,1)S(1)}) custom-call(s32[2]{0:T(128)S(1)} %pad_add_fusion.place_ref, bf16[128,2176]{1,0:T(8,128)(2,1)S(1)} %bitcast.28, bf16[128,2176]{1,0:T(8,128)(2,1)S(1)} %collective-permute-done.24.refs_1_, bf16[2048,128]{1,0:T(8,128)(2,1)S(1)} %get-tuple-element.41.refs_4_.refs_2_, ...), custom_call_target="tpu_custom_call" | custom-call | flops 2785017856 | bytes 12058624 | tf_op jit(solution)/shard_map/run_expert/pallas_call | solution.py:322
  76.1 16.9 %run_expert.2 = (f32[256,2048]{1,0:T(8,128)S(1)}, bf16[256,2048]{1,0:T(8,128)(2,1)S(1)}) custom-call(s32[2]{0:T(128)S(1)} %pad_add_fusion.place_ref, bf16[128,2176]{1,0:T(8,128)(2,1)S(1)} %bitcast.31, bf16[128,2176]{1,0:T(8,128)(2,1)S(1)} %collective-permute-done.4.refs_1_, bf16[128,2176]{1,0:T(8,128)(2,1)S(1)} %collective-permute-done.5.refs_2_, ...), custom_call_target="tpu_custom_call" | custom-call | flops 5570035712 | bytes 14680064 | tf_op jit(solution)/shard_map/run_expert/pallas_call | solution.py:322
  93.3 3.3 %collective-permute-start.26 = (bf16[32,2048]{1,0:T(8,128)(2,1)S(1)}, bf16[32,2048]{1,0:T(8,128)(2,1)S(1)}, u32[]{:S(2)}, u32[]{:S(2)}) collective-permute-start(bf16[32,2048]{1,0:T(8,128)(2,1)S(1)} %get-tuple-element.58), channel_id=1, source_target_pairs={{0,12},{1,13},{2,14},{3,15},{4,0},{5,1},{6,2},{7,3},{8,4},{9,5},{1... | collective-permute-start | bytes 393224 | tf_op jit(solution)/shard_map/ppermute | solution.py:36
  98.1 1.6 %collective-permute-start.17 = (bf16[128,2048]{1,0:T(8,128)(2,1)S(1)}, bf16[128,2048]{1,0:T(8,128)(2,1)S(1)}, u32[]{:S(2)}, u32[]{:S(2)}) collective-permute-start(bf16[128,2048]{1,0:T(8,128)(2,1)S(1)} %slice.118), channel_id=1, source_target_pairs={{0,2},{1,3},{2,0},{3,1},{4,6},{5,7},{6,4},{7,5},{8,10},{9,11},{10,... | collective-permute-start | bytes 1572872 | tf_op jit(solution)/shard_map/ppermute | solution.py:36
  100.4 4.4 %collective-permute-done.28 = bf16[32,2048]{1,0:T(8,128)(2,1)S(1)} collective-permute-done((bf16[32,2048]{1,0:T(8,128)(2,1)S(1)}, bf16[32,2048]{1,0:T(8,128)(2,1)S(1)}, u32[]{:S(2)}, u32[]{:S(2)}) %collective-permute-start.28) | collective-permute-done | bytes 131104 | tf_op jit(solution)/shard_map/ppermute | solution.py:36
  104.8 4.9 %collective-permute-done.27 = bf16[32,2048]{1,0:T(8,128)(2,1)S(1)} collective-permute-done((bf16[32,2048]{1,0:T(8,128)(2,1)S(1)}, bf16[32,2048]{1,0:T(8,128)(2,1)S(1)}, u32[]{:S(2)}, u32[]{:S(2)}) %collective-permute-start.27) | collective-permute-done | bytes 131104 | tf_op jit(solution)/shard_map/ppermute | solution.py:36
  109.8 1.6 %collective-permute-start.29 = (bf16[16,2048]{1,0:T(8,128)(2,1)S(1)}, bf16[16,2048]{1,0:T(8,128)(2,1)S(1)}, u32[]{:S(2)}, u32[]{:S(2)}) collective-permute-start(bf16[16,2048]{1,0:T(8,128)(2,1)S(1)} %slice.119), channel_id=1, source_target_pairs={{0,2},{1,3},{2,0},{3,1},{4,6},{5,7},{6,4},{7,5},{8,10},{9,11},{10,... | collective-permute-start | bytes 196616 | tf_op jit(solution)/shard_map/ppermute | solution.py:36
  111.8 3.0 %collective-permute-start.18 = (bf16[32,2048]{1,0:T(8,128)(2,1)S(1)}, bf16[32,2048]{1,0:T(8,128)(2,1)S(1)}, u32[]{:S(2)}, u32[]{:S(2)}) collective-permute-start(bf16[32,2048]{1,0:T(8,128)(2,1)S(1)} %get-tuple-element.55), channel_id=1, source_target_pairs={{0,12},{1,13},{2,14},{3,15},{4,0},{5,1},{6,2},{7,3},{8,4},{9,5},{1... | collective-permute-start | bytes 393224 | tf_op jit(solution)/shard_map/ppermute | solution.py:36
  115.9 1.4 %collective-permute-start.19 = (bf16[32,2048]{1,0:T(8,128)(2,1)S(1)}, bf16[32,2048]{1,0:T(8,128)(2,1)S(1)}, u32[]{:S(2)}, u32[]{:S(2)}) collective-permute-start(bf16[32,2048]{1,0:T(8,128)(2,1)S(1)} %get-tuple-element.57), channel_id=1, source_target_pairs={{0,8},{1,9},{2,10},{3,11},{4,12},{5,13},{6,14},{7,15},{8,0},{9,1},... | collective-permute-start | bytes 393224 | tf_op jit(solution)/shard_map/ppermute | solution.py:36
  117.3 5.4 %collective-permute-done.18 = bf16[32,2048]{1,0:T(8,128)(2,1)S(1)} collective-permute-done((bf16[32,2048]{1,0:T(8,128)(2,1)S(1)}, bf16[32,2048]{1,0:T(8,128)(2,1)S(1)}, u32[]{:S(2)}, u32[]{:S(2)}) %collective-permute-start.18) | collective-permute-done | bytes 131104 | tf_op jit(solution)/shard_map/ppermute | solution.py:36
  123.1 4.0 %collective-permute-done.19 = bf16[32,2048]{1,0:T(8,128)(2,1)S(1)} collective-permute-done((bf16[32,2048]{1,0:T(8,128)(2,1)S(1)}, bf16[32,2048]{1,0:T(8,128)(2,1)S(1)}, u32[]{:S(2)}, u32[]{:S(2)}) %collective-permute-start.19) | collective-permute-done | bytes 131104 | tf_op jit(solution)/shard_map/ppermute | solution.py:36
  (69 shorter events, 13.3 us)
Async XLA Ops:
  2.7 11.5 %collective-permute-start.2 = (bf16[32,2176]{1,0:T(8,128)(2,1)S(1)}, bf16[32,2176]{1,0:T(8,128)(2,1)S(1)}, u32[]{:S(2)}, u32[]{:S(2)}) collective-permute-start(bf16[32,2176]{1,0:T(8,128)(2,1)S(1)} %get-tuple-element.29), channel_id=1, source_target_pairs={{0,12},{1,13},{2,14},{3,15},{4,0},{5,1},{6,2},{7,3},{8,4},{9,5},{1... | collective-permute-start | bytes 417800 | tf_op jit(solution)/shard_map/ppermute | solution.py:36
  7.8 11.8 %collective-permute-start.1 = (bf16[32,2176]{1,0:T(8,128)(2,1)S(1)}, bf16[32,2176]{1,0:T(8,128)(2,1)S(1)}, u32[]{:S(2)}, u32[]{:S(2)}) collective-permute-start(bf16[32,2176]{1,0:T(8,128)(2,1)S(1)} %get-tuple-element.29), channel_id=1, source_target_pairs={{0,8},{1,9},{2,10},{3,11},{4,12},{5,13},{6,14},{7,15},{8,0},{9,1},... | collective-permute-start | bytes 417800 | tf_op jit(solution)/shard_map/ppermute | solution.py:36
  7.8 11.8 %collective-permute-start = (bf16[32,2176]{1,0:T(8,128)(2,1)S(1)}, bf16[32,2176]{1,0:T(8,128)(2,1)S(1)}, u32[]{:S(2)}, u32[]{:S(2)}) collective-permute-start(bf16[32,2176]{1,0:T(8,128)(2,1)S(1)} %get-tuple-element.29), channel_id=1, source_target_pairs={{0,4},{1,5},{2,6},{3,7},{4,8},{5,9},{6,10},{7,11},{8,12},{9,13},{1... | collective-permute-start | bytes 417800 | tf_op jit(solution)/shard_map/ppermute | solution.py:36
  10.7 53.5 %copy-start.1 = (bf16[1,2048,768]{2,1,0:T(8,128)(2,1)S(1)}, bf16[1,2048,768]{2,1,0:T(8,128)(2,1)}, u32[]{:S(2)}) copy-start(bf16[1,2048,768]{2,1,0:T(8,128)(2,1)} %param.14) | copy-start | bytes 9437188
  12.6 7.4 %collective-permute-start.3 = (bf16[4,264,128]{2,1,0:T(8,128)(2,1)S(1)}, bf16[4,264,128]{2,1,0:T(8,128)(2,1)S(1)}, u32[]{:S(2)}, u32[]{:S(2)}) collective-permute-start(bf16[4,264,128]{2,1,0:T(8,128)(2,1)S(1)} %get-tuple-element.32), channel_id=1, source_target_pairs={{0,2},{1,3},{2,0},{3,1},{4,6},{5,7},{6,4},{7,5},{8,10},{9,11},{10,... | collective-permute-start | bytes 811016 | tf_op jit(solution)/shard_map/ppermute | solution.py:36
  20.1 44.2 %copy-start = (bf16[1,2048,768]{2,1,0:T(8,128)(2,1)S(1)}, bf16[1,2048,768]{2,1,0:T(8,128)(2,1)}, u32[]{:S(2)}) copy-start(bf16[1,2048,768]{2,1,0:T(8,128)(2,1)} %param.13) | copy-start | bytes 9437188
  20.1 7.9 %collective-permute-start.7 = (bf16[2,264,128]{2,1,0:T(8,128)(2,1)S(1)}, bf16[2,264,128]{2,1,0:T(8,128)(2,1)S(1)}, u32[]{:S(2)}, u32[]{:S(2)}) collective-permute-start(bf16[2,264,128]{2,1,0:T(8,128)(2,1)S(1)} %pad_maximum_fusion.4), channel_id=1, source_target_pairs={{0,0},{1,1},{2,2},{3,3},{4,4},{5,5},{6,6},{7,7},{8,8},{9,9},{10,10... | collective-permute-start | bytes 405512 | tf_op jit(solution)/shard_map/ppermute | solution.py:68
  20.9 9.7 %collective-permute-start.8 = (bf16[2,264,128]{2,1,0:T(8,128)(2,1)S(1)}, bf16[2,264,128]{2,1,0:T(8,128)(2,1)S(1)}, u32[]{:S(2)}, u32[]{:S(2)}) collective-permute-start(bf16[2,264,128]{2,1,0:T(8,128)(2,1)S(1)} %pad_maximum_fusion.5), channel_id=1, source_target_pairs={{0,4},{1,5},{2,6},{3,7},{4,8},{5,9},{6,10},{7,11},{8,12},{9,13},{1... | collective-permute-start | bytes 405512 | tf_op jit(solution)/shard_map/ppermute | solution.py:68
  23.5 9.7 %collective-permute-start.9 = (bf16[2,264,128]{2,1,0:T(8,128)(2,1)S(1)}, bf16[2,264,128]{2,1,0:T(8,128)(2,1)S(1)}, u32[]{:S(2)}, u32[]{:S(2)}) collective-permute-start(bf16[2,264,128]{2,1,0:T(8,128)(2,1)S(1)} %pad_maximum_fusion.6), channel_id=1, source_target_pairs={{0,8},{1,9},{2,10},{3,11},{4,12},{5,13},{6,14},{7,15},{8,0},{9,1},... | collective-permute-start | bytes 405512 | tf_op jit(solution)/shard_map/ppermute | solution.py:68
  24.8 12.6 %collective-permute-start.10 = (bf16[2,264,128]{2,1,0:T(8,128)(2,1)S(1)}, bf16[2,264,128]{2,1,0:T(8,128)(2,1)S(1)}, u32[]{:S(2)}, u32[]{:S(2)}) collective-permute-start(bf16[2,264,128]{2,1,0:T(8,128)(2,1)S(1)} %pad_maximum_fusion.7), channel_id=1, source_target_pairs={{0,12},{1,13},{2,14},{3,15},{4,0},{5,1},{6,2},{7,3},{8,4},{9,5},{1... | collective-permute-start | bytes 405512 | tf_op jit(solution)/shard_map/ppermute | solution.py:68
  26.5 10.9 %collective-permute-start.11 = (bf16[16,2176]{1,0:T(8,128)(2,1)S(1)}, bf16[16,2176]{1,0:T(8,128)(2,1)S(1)}, u32[]{:S(2)}, u32[]{:S(2)}) collective-permute-start(bf16[16,2176]{1,0:T(8,128)(2,1)S(1)} %get-tuple-element.36), channel_id=1, source_target_pairs={{0,2},{1,3},{2,0},{3,1},{4,6},{5,7},{6,4},{7,5},{8,10},{9,11},{10,... | collective-permute-start | bytes 208904 | tf_op jit(solution)/shard_map/ppermute | solution.py:36
  28.0 9.4 %collective-permute-start.12 = (bf16[2,264,128]{2,1,0:T(8,128)(2,1)S(1)}, bf16[2,264,128]{2,1,0:T(8,128)(2,1)S(1)}, u32[]{:S(2)}, u32[]{:S(2)}) collective-permute-start(bf16[2,264,128]{2,1,0:T(8,128)(2,1)S(1)} %collective-permute-done.7.refs_0_), channel_id=1, source_target_pairs={{0,16},{16,0},{1,17},{17,1},{2,18},{18,2},{3,19},{19,3},{4,20},{20... | collective-permute-start | bytes 405512 | tf_op jit(solution)/shard_map/ppermute | solution.py:70
  30.7 6.7 %collective-permute-start.13 = (bf16[2,264,128]{2,1,0:T(8,128)(2,1)S(1)}, bf16[2,264,128]{2,1,0:T(8,128)(2,1)S(1)}, u32[]{:S(2)}, u32[]{:S(2)}) collective-permute-start(bf16[2,264,128]{2,1,0:T(8,128)(2,1)S(1)} %collective-permute-done.8.refs_1_), channel_id=1, source_target_pairs={{0,16},{16,0},{1,17},{17,1},{2,18},{18,2},{3,19},{19,3},{4,20},{20... | collective-permute-start | bytes 405512 | tf_op jit(solution)/shard_map/ppermute | solution.py:70
  33.2 8.5 %collective-permute-start.14 = (bf16[2,264,128]{2,1,0:T(8,128)(2,1)S(1)}, bf16[2,264,128]{2,1,0:T(8,128)(2,1)S(1)}, u32[]{:S(2)}, u32[]{:S(2)}) collective-permute-start(bf16[2,264,128]{2,1,0:T(8,128)(2,1)S(1)} %collective-permute-done.9.refs_2_), channel_id=1, source_target_pairs={{0,16},{16,0},{1,17},{17,1},{2,18},{18,2},{3,19},{19,3},{4,20},{20... | collective-permute-start | bytes 405512 | tf_op jit(solution)/shard_map/ppermute | solution.py:70
  37.3 6.8 %collective-permute-start.15 = (bf16[2,264,128]{2,1,0:T(8,128)(2,1)S(1)}, bf16[2,264,128]{2,1,0:T(8,128)(2,1)S(1)}, u32[]{:S(2)}, u32[]{:S(2)}) collective-permute-start(bf16[2,264,128]{2,1,0:T(8,128)(2,1)S(1)} %collective-permute-done.10.refs_3_), channel_id=1, source_target_pairs={{0,16},{16,0},{1,17},{17,1},{2,18},{18,2},{3,19},{19,3},{4,20},{20... | collective-permute-start | bytes 405512 | tf_op jit(solution)/shard_map/ppermute | solution.py:70
  44.1 8.2 %collective-permute-start.23 = (bf16[32,2176]{1,0:T(8,128)(2,1)S(1)}, bf16[32,2176]{1,0:T(8,128)(2,1)S(1)}, u32[]{:S(2)}, u32[]{:S(2)}) collective-permute-start(bf16[32,2176]{1,0:T(8,128)(2,1)S(1)} %bitcast.36), channel_id=1, source_target_pairs={{0,12},{1,13},{2,14},{3,15},{4,0},{5,1},{6,2},{7,3},{8,4},{9,5},{1... | collective-permute-start | bytes 417800 | tf_op jit(solution)/shard_map/ppermute | solution.py:36
  48.2 12.0 %collective-permute-start.22 = (bf16[32,2176]{1,0:T(8,128)(2,1)S(1)}, bf16[32,2176]{1,0:T(8,128)(2,1)S(1)}, u32[]{:S(2)}, u32[]{:S(2)}) collective-permute-start(bf16[32,2176]{1,0:T(8,128)(2,1)S(1)} %bitcast.37), channel_id=1, source_target_pairs={{0,8},{1,9},{2,10},{3,11},{4,12},{5,13},{6,14},{7,15},{8,0},{9,1},... | collective-permute-start | bytes 417800 | tf_op jit(solution)/shard_map/ppermute | solution.py:36
  48.2 12.0 %collective-permute-start.21 = (bf16[32,2176]{1,0:T(8,128)(2,1)S(1)}, bf16[32,2176]{1,0:T(8,128)(2,1)S(1)}, u32[]{:S(2)}, u32[]{:S(2)}) collective-permute-start(bf16[32,2176]{1,0:T(8,128)(2,1)S(1)} %bitcast.38), channel_id=1, source_target_pairs={{0,4},{1,5},{2,6},{3,7},{4,8},{5,9},{6,10},{7,11},{8,12},{9,13},{1... | collective-permute-start | bytes 417800 | tf_op jit(solution)/shard_map/ppermute | solution.py:36
  48.8 13.8 %collective-permute-start.4 = (bf16[128,2176]{1,0:T(8,128)(2,1)S(1)}, bf16[128,2176]{1,0:T(8,128)(2,1)S(1)}, u32[]{:S(2)}, u32[]{:S(2)}) collective-permute-start(bf16[128,2176]{1,0:T(8,128)(2,1)S(1)} %bitcast.29), channel_id=1, source_target_pairs={{0,2},{1,3},{2,0},{3,1},{4,6},{5,7},{6,4},{7,5},{8,10},{9,11},{10,... | collective-permute-start | bytes 1671176 | tf_op jit(solution)/shard_map/ppermute | solution.py:36
  60.3 4.0 %collective-permute-start.24 = (bf16[128,2176]{1,0:T(8,128)(2,1)S(1)}, bf16[128,2176]{1,0:T(8,128)(2,1)S(1)}, u32[]{:S(2)}, u32[]{:S(2)}) collective-permute-start(bf16[128,2176]{1,0:T(8,128)(2,1)S(1)} %bitcast.27), channel_id=1, source_target_pairs={{0,1},{1,0},{2,3},{3,2},{4,5},{5,4},{6,7},{7,6},{8,9},{9,8},{10,11... | collective-permute-start | bytes 1671176 | tf_op jit(solution)/shard_map/ppermute | solution.py:36
  60.3 15.8 %collective-permute-start.5 = (bf16[128,2176]{1,0:T(8,128)(2,1)S(1)}, bf16[128,2176]{1,0:T(8,128)(2,1)S(1)}, u32[]{:S(2)}, u32[]{:S(2)}) collective-permute-start(bf16[128,2176]{1,0:T(8,128)(2,1)S(1)} %bitcast.30), channel_id=1, source_target_pairs={{0,1},{1,0},{2,3},{3,2},{4,5},{5,4},{6,7},{7,6},{8,9},{9,8},{10,11... | collective-permute-start | bytes 1671176 | tf_op jit(solution)/shard_map/ppermute | solution.py:36
  62.6 13.5 %collective-permute-start.6 = (bf16[128,2176]{1,0:T(8,128)(2,1)S(1)}, bf16[128,2176]{1,0:T(8,128)(2,1)S(1)}, u32[]{:S(2)}, u32[]{:S(2)}) collective-permute-start(bf16[128,2176]{1,0:T(8,128)(2,1)S(1)} %collective-permute-done.4.refs_1_), channel_id=1, source_target_pairs={{0,1},{1,0},{2,3},{3,2},{4,5},{5,4},{6,7},{7,6},{8,9},{9,8},{10,11... | collective-permute-start | bytes 1671176 | tf_op jit(solution)/shard_map/ppermute | solution.py:36
  75.5 17.5 %collective-permute-start.25 = (bf16[128,2048]{1,0:T(8,128)(2,1)S(1)}, bf16[128,2048]{1,0:T(8,128)(2,1)S(1)}, u32[]{:S(2)}, u32[]{:S(2)}) collective-permute-start(bf16[128,2048]{1,0:T(8,128)(2,1)S(1)} %get-tuple-element.50), channel_id=1, source_target_pairs={{0,1},{1,0},{2,3},{3,2},{4,5},{5,4},{6,7},{7,6},{8,9},{9,8},{10,11... | collective-permute-start | bytes 1572872 | tf_op jit(solution)/shard_map/ppermute | solution.py:36
  93.0 4.7 %collective-permute-start.16 = (bf16[256,2048]{1,0:T(8,128)(2,1)S(1)}, bf16[256,2048]{1,0:T(8,128)(2,1)S(1)}, u32[]{:S(2)}, u32[]{:S(2)}) collective-permute-start(bf16[256,2048]{1,0:T(8,128)(2,1)S(1)} %get-tuple-element.47), channel_id=1, source_target_pairs={{0,1},{1,0},{2,3},{3,2},{4,5},{5,4},{6,7},{7,6},{8,9},{9,8},{10,11... | collective-permute-start | bytes 3145736 | tf_op jit(solution)/shard_map/ppermute | solution.py:36
  93.3 7.2 %collective-permute-start.26 = (bf16[32,2048]{1,0:T(8,128)(2,1)S(1)}, bf16[32,2048]{1,0:T(8,128)(2,1)S(1)}, u32[]{:S(2)}, u32[]{:S(2)}) collective-permute-start(bf16[32,2048]{1,0:T(8,128)(2,1)S(1)} %get-tuple-element.58), channel_id=1, source_target_pairs={{0,12},{1,13},{2,14},{3,15},{4,0},{5,1},{6,2},{7,3},{8,4},{9,5},{1... | collective-permute-start | bytes 393224 | tf_op jit(solution)/shard_map/ppermute | solution.py:36
  96.6 8.2 %collective-permute-start.28 = (bf16[32,2048]{1,0:T(8,128)(2,1)S(1)}, bf16[32,2048]{1,0:T(8,128)(2,1)S(1)}, u32[]{:S(2)}, u32[]{:S(2)}) collective-permute-start(bf16[32,2048]{1,0:T(8,128)(2,1)S(1)} %get-tuple-element.59), channel_id=1, source_target_pairs={{0,4},{1,5},{2,6},{3,7},{4,8},{5,9},{6,10},{7,11},{8,12},{9,13},{1... | collective-permute-start | bytes 393224 | tf_op jit(solution)/shard_map/ppermute | solution.py:36
  96.6 13.1 %collective-permute-start.27 = (bf16[32,2048]{1,0:T(8,128)(2,1)S(1)}, bf16[32,2048]{1,0:T(8,128)(2,1)S(1)}, u32[]{:S(2)}, u32[]{:S(2)}) collective-permute-start(bf16[32,2048]{1,0:T(8,128)(2,1)S(1)} %get-tuple-element.60), channel_id=1, source_target_pairs={{0,8},{1,9},{2,10},{3,11},{4,12},{5,13},{6,14},{7,15},{8,0},{9,1},... | collective-permute-start | bytes 393224 | tf_op jit(solution)/shard_map/ppermute | solution.py:36
  98.1 13.5 %collective-permute-start.17 = (bf16[128,2048]{1,0:T(8,128)(2,1)S(1)}, bf16[128,2048]{1,0:T(8,128)(2,1)S(1)}, u32[]{:S(2)}, u32[]{:S(2)}) collective-permute-start(bf16[128,2048]{1,0:T(8,128)(2,1)S(1)} %slice.118), channel_id=1, source_target_pairs={{0,2},{1,3},{2,0},{3,1},{4,6},{5,7},{6,4},{7,5},{8,10},{9,11},{10,... | collective-permute-start | bytes 1572872 | tf_op jit(solution)/shard_map/ppermute | solution.py:36
  109.8 7.5 %collective-permute-start.29 = (bf16[16,2048]{1,0:T(8,128)(2,1)S(1)}, bf16[16,2048]{1,0:T(8,128)(2,1)S(1)}, u32[]{:S(2)}, u32[]{:S(2)}) collective-permute-start(bf16[16,2048]{1,0:T(8,128)(2,1)S(1)} %slice.119), channel_id=1, source_target_pairs={{0,2},{1,3},{2,0},{3,1},{4,6},{5,7},{6,4},{7,5},{8,10},{9,11},{10,... | collective-permute-start | bytes 196616 | tf_op jit(solution)/shard_map/ppermute | solution.py:36
  111.8 10.9 %collective-permute-start.18 = (bf16[32,2048]{1,0:T(8,128)(2,1)S(1)}, bf16[32,2048]{1,0:T(8,128)(2,1)S(1)}, u32[]{:S(2)}, u32[]{:S(2)}) collective-permute-start(bf16[32,2048]{1,0:T(8,128)(2,1)S(1)} %get-tuple-element.55), channel_id=1, source_target_pairs={{0,12},{1,13},{2,14},{3,15},{4,0},{5,1},{6,2},{7,3},{8,4},{9,5},{1... | collective-permute-start | bytes 393224 | tf_op jit(solution)/shard_map/ppermute | solution.py:36
  114.8 8.3 %collective-permute-start.20 = (bf16[32,2048]{1,0:T(8,128)(2,1)S(1)}, bf16[32,2048]{1,0:T(8,128)(2,1)S(1)}, u32[]{:S(2)}, u32[]{:S(2)}) collective-permute-start(bf16[32,2048]{1,0:T(8,128)(2,1)S(1)} %get-tuple-element.56), channel_id=1, source_target_pairs={{0,4},{1,5},{2,6},{3,7},{4,8},{5,9},{6,10},{7,11},{8,12},{9,13},{1... | collective-permute-start | bytes 393224 | tf_op jit(solution)/shard_map/ppermute | solution.py:36
  115.9 11.2 %collective-permute-start.19 = (bf16[32,2048]{1,0:T(8,128)(2,1)S(1)}, bf16[32,2048]{1,0:T(8,128)(2,1)S(1)}, u32[]{:S(2)}, u32[]{:S(2)}) collective-permute-start(bf16[32,2048]{1,0:T(8,128)(2,1)S(1)} %get-tuple-element.57), channel_id=1, source_target_pairs={{0,8},{1,9},{2,10},{3,11},{4,12},{5,13},{6,14},{7,15},{8,0},{9,1},... | collective-permute-start | bytes 393224 | tf_op jit(solution)/shard_map/ppermute | solution.py:36
  (6 other events, 6.1 us)

commit v8 on v7

--- a/solution.py
+++ b/solution.py
@@ -10,7 +10,8 @@
 adapter_scale = 2.0
 LANES = 128
 GRANT = 16 << 20
-EXPERT_GRANT = 36 << 20
+EXPERT_GRANT = 32 << 20
+WHOLE_GRANT = 60 << 20
 
 
 def route_gates(logits):
@@ -28,20 +29,8 @@
     return chips // middle, middle, cores
 
 
-def shift(x, n, stride, size, k):
-    pairs = []
-    for i in range(n):
-        place = i // stride % size
-        pairs.append((i, i + ((place + k) % size - place) * stride))
-    return lax.ppermute(x, "expert", pairs)
-
-
-def stack_rows(pieces):
-    return jnp.stack(pieces).reshape(-1, pieces[0].shape[1])
-
-
-def gather_along(x, n, stride, size):
-    return stack_rows([x] + [shift(x, n, stride, size, k) for k in range(1, size)])
+def swap(x, n, stride, k):
+    return lax.ppermute(x, "expert", [(i, i ^ (k * stride)) for i in range(n)])
 
 
 def scatter_along(total, n, stride, size):
@@ -49,21 +38,18 @@
     result = total[:count]
     for k in range(1, size):
         part = total[k * count : (k + 1) * count].astype(jnp.bfloat16)
-        result = result + shift(part, n, stride, size, size - k).astype(jnp.float32)
+        result = result + swap(part, n, stride, k).astype(jnp.float32)
     return result
 
 
 def exchange_factors(blocks, n):
     outer, middle, cores = split_axis(n)
-    stride = middle * cores
     here, there = [], []
     for q in range(outer):
         pairs = []
         for g in range(2):
             for i in range(n):
-                place = i // stride
-                to = (i + ((place + q) % outer - place) * stride) ^ g
-                pairs.append((g * n + i, g * n + to))
+                pairs.append((g * n + i, g * n + (i ^ (q * middle * cores) ^ g)))
         part = jnp.stack([block[q] for block in blocks])
         part = lax.ppermute(part, ("group", "expert"), pairs)
         here.append(part)
@@ -108,12 +94,12 @@
             for count in (first, steps - first)
         ],
         scratch_shapes=[pltpu.VMEM((padded, -(-steps * rows // LANES) * LANES), jnp.float32)],
-        compiler_params=pltpu.CompilerParams(vmem_limit_bytes=GRANT),
+        compiler_params=pltpu.CompilerParams(vmem_limit_bytes=WHOLE_GRANT),
         name="payload",
     )(hidden, jnp.swapaxes(route_ids, 1, 2), jnp.swapaxes(route_logits, 1, 2))
 
 
-def order_kernel(outer, middle, place_ref, placement_ref, factors_ref, *refs):
+def order_kernel(middle, place_ref, placement_ref, factors_ref, *refs):
     out_refs, wide_ref = refs[:-1], refs[-1]
     slots = factors_ref.shape[0]
     length, lanes = out_refs[0].shape[1:]
@@ -129,9 +115,9 @@
 
     def put(s, carry):
         to = placement_ref[s]
-        aside = lax.rem(to // 2 + middle - lax.rem(me // 2, middle), middle)
-        ahead = lax.rem(to // (2 * middle) + outer - me // (2 * middle), outer)
-        ours = lax.rem(to + me + group, 2) == 0
+        away = to ^ me
+        aside, ahead = lax.rem(away // 2, middle), away // (2 * middle)
+        ours = lax.rem(away, 2) == group
         rows = wide_ref[pl.ds(pl.multiple_of(s * length, 8), length), :].astype(jnp.bfloat16)
         for r, out_ref in enumerate(out_refs):
 
@@ -149,7 +135,7 @@
     slots, entries = factors.shape
     length = entries // LANES
     return pl.pallas_call(
-        functools.partial(order_kernel, outer, middle),
+        functools.partial(order_kernel, middle),
         out_shape=[jax.ShapeDtypeStruct((outer, length, LANES), jnp.bfloat16)] * middle,
         in_specs=[
             pl.BlockSpec(memory_space=pltpu.SMEM),
@@ -157,7 +143,7 @@
             pl.BlockSpec(memory_space=pltpu.VMEM),
         ],
         scratch_shapes=[pltpu.VMEM((slots * length, LANES), jnp.float32)],
-        compiler_params=pltpu.CompilerParams(vmem_limit_bytes=GRANT),
+        compiler_params=pltpu.CompilerParams(vmem_limit_bytes=WHOLE_GRANT),
         name="order_factors",
     )(place, placement, factors)
 
@@ -171,11 +157,9 @@
     group, me = place_ref[0], place_ref[1]
     for i, piece in enumerate(pieces):
         swapped, q = i // outer, i % outer
-        core = lax.rem(me + group + swapped, 2)
+        core = group if swapped == 0 else 1 - group
         for r in range(middle):
-            row = lax.rem(me // 2 + middle - r, middle)
-            column = lax.rem(me // (2 * middle) + outer - q, outer)
-            source = (column * middle + row) * 2 + core
+            source = me ^ ((q * middle + r) * 2 + core)
             start = pl.multiple_of(source * length, 8)
             flat_ref[pl.ds(start, length), :] = piece[r].astype(jnp.float32)
 
@@ -233,115 +217,189 @@
     )(place, *here, *there)
 
 
-def expert_kernel(count, place_ref, *refs):
+class Loads:
+    def __init__(self, sem):
+        self.sem, self.count = sem, 0
+
+    def begin(self, src, dst):
+        copy = pltpu.make_async_copy(src, dst, self.sem.at[self.count])
+        copy.start()
+        self.count += 1
+        return [copy]
+
+    def begin_rows(self, src, dst, parts=4):
+        step = src.shape[0] // parts
+        cuts = [pl.ds(at, step) for at in range(0, src.shape[0], step)]
+        return sum([self.begin(src.at[cut], dst.at[cut]) for cut in cuts], [])
+
+
+def wait(copies):
+    for copy in copies:
+        copy.wait()
+
+
+def base_kernel(count, *refs):
+    pieces = refs[:count]
+    w_gate_hbm, w_up_hbm, gate_hbm, up_hbm, x_ref, w_gate_ref, w_up_ref = refs[count : count + 7]
+    gate_ref, up_ref, sem, out_sem = refs[count + 7 :]
+    rows = pieces[0].shape[0]
+    width = w_gate_ref.shape[0]
+    total = gate_ref.shape[0]
+    block = min(128, total)
+    loads = Loads(sem)
+    x_in = [loads.begin(p, x_ref.at[pl.ds(i * rows, rows)]) for i, p in enumerate(pieces)]
+    x_in = sum(x_in, [])
+    gate_in = loads.begin_rows(w_gate_hbm, w_gate_ref)
+    up_in = loads.begin_rows(w_up_hbm, w_up_ref)
+    wait(x_in)
+
+    def store(i):
+        here = pl.ds(pl.multiple_of(i * block, block), block)
+        return [
+            pltpu.make_async_copy(src.at[here], dst.at[here], out_sem.at[j, i])
+            for j, (src, dst) in enumerate(((gate_ref, gate_hbm), (up_ref, up_hbm)))
+        ]
+
+    def run_block(i, carry):
+        here = pl.ds(pl.multiple_of(i * block, block), block)
+        pl.when(i == 0)(lambda: wait(gate_in))
+        gate_ref[here, :] = dot(x_ref[here, :width], w_gate_ref[...])
+        pl.when(i == 0)(lambda: wait(up_in))
+        up_ref[here, :] = dot(x_ref[here, :width], w_up_ref[...])
+        for copy in store(i):
+            copy.start()
+        return carry
+
+    lax.fori_loop(0, total // block, run_block, 0)
+    for i in range(total // block):
+        wait(store(i))
+
+
+def base_products(pieces, w_gate, w_up):
+    width, units = w_gate.shape
+    total = sum(p.shape[0] for p in pieces)
+    out = jax.ShapeDtypeStruct((total, units), jnp.float32)
+    return pl.pallas_call(
+        functools.partial(base_kernel, len(pieces)),
+        out_shape=[out, out],
+        in_specs=[pl.BlockSpec(memory_space=pl.ANY)] * len(pieces)
+        + [pl.BlockSpec(memory_space=pltpu.HBM)] * 2,
+        out_specs=[pl.BlockSpec(memory_space=pl.ANY)] * 2,
+        scratch_shapes=[
+            pltpu.VMEM((total, pieces[0].shape[1]), jnp.bfloat16),
+            pltpu.VMEM(w_gate.shape, w_gate.dtype),
+            pltpu.VMEM(w_up.shape, w_up.dtype),
+            pltpu.VMEM(out.shape, out.dtype),
+            pltpu.VMEM(out.shape, out.dtype),
+            pltpu.SemaphoreType.DMA((len(pieces) + 8,)),
+            pltpu.SemaphoreType.DMA((2, total // min(128, total))),
+        ],
+        compiler_params=pltpu.CompilerParams(vmem_limit_bytes=EXPERT_GRANT),
+        cost_estimate=pl.CostEstimate(
+            flops=4 * total * width * units,
+            bytes_accessed=4 * width * units + 2 * total * width + 8 * total * units,
+            transcendentals=0,
+        ),
+        name="base_products",
+    )(*pieces, w_gate, w_up)
+
+
+def finish_kernel(count, first, rows, place_ref, *refs):
     pieces, refs = refs[:count], refs[count:]
-    a_gu_hbm, gate_b_hbm, up_b_hbm, down_a_hbm, down_b_hbm = refs[:5]
-    w_gate_hbm, w_up_hbm, w_down_hbm, kept_hbm, sent_hbm = refs[5:10]
-    x_ref, a_gu_ref, gate_b_ref, up_b_ref, down_a_ref, down_b_ref = refs[10:16]
-    w_gate_ref, w_up_ref, w_down_ref, kept_ref, sent_ref, sem, out_sem = refs[16:]
-    rows = pieces[0].shape[0]
+    gate_hbm, up_hbm, a_gu_hbm, gate_b_hbm, up_b_hbm, down_a_hbm, down_b_hbm = refs[:7]
+    w_down_hbm, kept_hbm, sent_hbm, x_ref, gate_ref, up_ref = refs[7:13]
+    a_gu_ref, gate_b_ref, up_b_ref, down_a_ref, down_b_ref, w_down_ref = refs[13:19]
+    kept_ref, sent_ref, sem, out_sem = refs[19:]
+    span = pieces[0].shape[0]
     units, width = w_down_ref.shape
     rank = gate_b_ref.shape[0]
     own = kept_ref.shape[0]
-    begun = []
-
-    def begin(src, dst):
-        copy = pltpu.make_async_copy(src, dst, sem.at[len(begun)])
-        copy.start()
-        begun.append(copy)
-        return copy
-
-    def begin_rows(src, dst):
-        quarter = src.shape[0] // 4
-        cuts = [pl.ds(at, quarter) for at in range(0, src.shape[0], quarter)]
-        return [begin(src.at[cut], dst.at[cut]) for cut in cuts]
-
-    def wait(copies):
-        for copy in copies:
-            copy.wait()
-
-    x_in = [begin(p, x_ref.at[pl.ds(i * rows, rows)]) for i, p in enumerate(pieces)]
-    x_in.append(begin(a_gu_hbm, a_gu_ref))
-    gate_in = begin_rows(w_gate_hbm, w_gate_ref) + [begin(gate_b_hbm, gate_b_ref)]
-    up_in = begin_rows(w_up_hbm, w_up_ref) + [begin(up_b_hbm, up_b_ref)]
-    down_in = [begin(down_a_hbm, down_a_ref), begin(down_b_hbm, down_b_ref)]
-    down_in += begin_rows(w_down_hbm, w_down_ref)
+    block = min(128, own)
+    loads = Loads(sem)
+    x_in, base_in = [], []
+    for i, piece in enumerate(pieces):
+        x_in += loads.begin(piece.at[pl.ds(first, rows)], x_ref.at[pl.ds(i * rows, rows)])
+    x_in += loads.begin(a_gu_hbm, a_gu_ref)
+    x_in += loads.begin(gate_b_hbm, gate_b_ref) + loads.begin(up_b_hbm, up_b_ref)
+    for i in range(count):
+        src, dst = pl.ds(i * span + first, rows), pl.ds(i * rows, rows)
+        base_in += loads.begin(gate_hbm.at[src], gate_ref.at[dst])
+        base_in += loads.begin(up_hbm.at[src], up_ref.at[dst])
+    down_in = loads.begin(down_a_hbm, down_a_ref) + loads.begin(down_b_hbm, down_b_ref)
+    down_in += loads.begin_rows(w_down_hbm, w_down_ref)
     wait(x_in)
 
-    def run_piece(i, carry):
-        here = pl.ds(pl.multiple_of(i * rows, rows), rows)
+    def run_block(i, carry):
+        here = pl.ds(pl.multiple_of(i * block, block), block)
         gates = x_ref[here, width:].astype(jnp.float32)
         lane = lax.broadcasted_iota(jnp.int32, gates.shape, 1)
         mine = jnp.sum(jnp.where(lane == place_ref[1], gates, 0.0), axis=1, keepdims=True)
         low = (adapter_scale * dot(x_ref[here, :width], a_gu_ref[...])).astype(jnp.bfloat16)
-        pl.when(i == 0)(lambda: wait(gate_in))
-        g = dot(x_ref[here, :width], w_gate_ref[...]) + dot(low[:, :rank], gate_b_ref[...])
-        pl.when(i == 0)(lambda: wait(up_in))
-        u = dot(x_ref[here, :width], w_up_ref[...]) + dot(low[:, rank:], up_b_ref[...])
+        pl.when(i == 0)(lambda: wait(base_in))
+        g = gate_ref[here, :] + dot(low[:, :rank], gate_b_ref[...])
+        u = up_ref[here, :] + dot(low[:, rank:], up_b_ref[...])
         inner = (g / (1.0 + jnp.exp(-g)) * u).astype(jnp.bfloat16)
         pl.when(i == 0)(lambda: wait(down_in))
         low = (adapter_scale * dot(inner, down_a_ref[...])).astype(jnp.bfloat16)[:, :rank]
         out = (dot(inner, w_down_ref[...]) + dot(low, down_b_ref[...])) * mine
 
-        @pl.when(i < len(pieces) // 2)
+        @pl.when(i < own // block)
         def _():
             kept_ref[here, :] = out
-            pltpu.make_async_copy(
-                kept_ref.at[here], kept_hbm.at[here], out_sem.at[i]
-            ).start()
-
-        @pl.when(i >= len(pieces) // 2)
+            pltpu.make_async_copy(kept_ref.at[here], kept_hbm.at[here], out_sem.at[i]).start()
+
+        @pl.when(i >= own // block)
         def _():
-            there = pl.ds(pl.multiple_of(i * rows - own, rows), rows)
+            there = pl.ds(pl.multiple_of(i * block - own, block), block)
             sent_ref[there, :] = out.astype(jnp.bfloat16)
-            pltpu.make_async_copy(
-                sent_ref.at[there], sent_hbm.at[there], out_sem.at[i]
-            ).start()
+            pltpu.make_async_copy(sent_ref.at[there], sent_hbm.at[there], out_sem.at[i]).start()
 
         return carry
 
-    lax.fori_loop(0, len(pieces), run_piece, 0)
-    for i in range(len(pieces)):
-        src, dst = (kept_ref, kept_hbm) if i < len(pieces) // 2 else (sent_ref, sent_hbm)
-        at = pl.ds(i % (len(pieces) // 2) * rows, rows)
+    lax.fori_loop(0, 2 * own // block, run_block, 0)
+    for i in range(2 * own // block):
+        src, dst = (kept_ref, kept_hbm) if i < own // block else (sent_ref, sent_hbm)
+        at = pl.ds(i % (own // block) * block, block)
         pltpu.make_async_copy(src.at[at], dst.at[at], out_sem.at[i]).wait()
 
 
-def run_expert(place, pieces, low_rank, w_gate, w_up, w_down):
+def finish_step(place, pieces, base, first, rows, low_rank, w_down):
     units, width = w_down.shape
-    total = sum(p.shape[0] for p in pieces)
+    total = rows * len(pieces)
     own = total // 2
     a_gu, gate_b, up_b, down_a, down_b = low_rank
     rank = down_b.shape[0]
     outs = [
         jax.ShapeDtypeStruct((own, width), jnp.float32),
-        jax.ShapeDtypeStruct((total - own, width), jnp.bfloat16),
+        jax.ShapeDtypeStruct((own, width), jnp.bfloat16),
     ]
-    kept = [a_gu, gate_b, up_b, down_a, down_b, w_gate, w_up, w_down]
-    copies = len(pieces) + 5 + 3 * 4
+    held = [*low_rank, w_down]
     return pl.pallas_call(
-        functools.partial(expert_kernel, len(pieces)),
+        functools.partial(finish_kernel, len(pieces), first, rows),
         out_shape=outs,
         in_specs=[pl.BlockSpec(memory_space=pltpu.SMEM)]
-        + [pl.BlockSpec(memory_space=pl.ANY)] * (len(pieces) + len(low_rank))
-        + [pl.BlockSpec(memory_space=pltpu.HBM)] * 3,
+        + [pl.BlockSpec(memory_space=pl.ANY)] * (len(pieces) + 2 + len(low_rank))
+        + [pl.BlockSpec(memory_space=pltpu.HBM)],
         out_specs=[pl.BlockSpec(memory_space=pl.ANY)] * 2,
-        scratch_shapes=[pltpu.VMEM((total, pieces[0].shape[1]), jnp.bfloat16)]
-        + [pltpu.VMEM(a.shape, a.dtype) for a in kept]
+        scratch_shapes=[
+            pltpu.VMEM((total, pieces[0].shape[1]), jnp.bfloat16),
+            pltpu.VMEM((total, units), jnp.float32),
+            pltpu.VMEM((total, units), jnp.float32),
+        ]
+        + [pltpu.VMEM(a.shape, a.dtype) for a in held]
+        + [pltpu.VMEM(o.shape, o.dtype) for o in outs]
         + [
-            pltpu.VMEM(outs[0].shape, outs[0].dtype),
-            pltpu.VMEM(outs[1].shape, outs[1].dtype),
-            pltpu.SemaphoreType.DMA((copies,)),
-            pltpu.SemaphoreType.DMA((len(pieces),)),
+            pltpu.SemaphoreType.DMA((3 * len(pieces) + 9,)),
+            pltpu.SemaphoreType.DMA((2 * own // min(128, own),)),
         ],
         compiler_params=pltpu.CompilerParams(vmem_limit_bytes=EXPERT_GRANT),
         cost_estimate=pl.CostEstimate(
-            flops=2 * total * units * (3 * width + 4 * rank) + 8 * total * width * rank,
-            bytes_accessed=6 * units * width + 5 * total * width,
+            flops=2 * total * units * (width + 4 * rank) + 8 * total * width * rank,
+            bytes_accessed=2 * units * width + 5 * total * width + 8 * total * units,
             transcendentals=total * units,
         ),
-        name="run_expert",
-    )(place, *pieces, *kept)
+        name="finish_step",
+    )(place, *pieces, *base, *held)
 
 
 def dense_shards(
@@ -356,32 +414,48 @@
     along_outer, along_middle = (middle * cores, outer), (cores, middle)
     place = jnp.stack([lax.axis_index("group"), lax.axis_index("expert")]).astype(jnp.int32)
 
+    def along(x, stride, size):
+        return [x] + [swap(x, owners, stride, k) for k in range(1, size)]
+
+    def by_step(pieces, count):
+        column = jnp.stack([p.reshape(count, rows, -1) for p in pieces], axis=1)
+        return column.reshape(count * outer * rows, -1)
+
+    def across(column):
+        sheet = along(column, *along_middle)
+        return sheet + [swap(p, owners, 1, 1) for p in sheet]
+
     first = max(1, steps * 2 // 3)
     head, tail = make_payload(hidden, route_ids, route_logits, experts, first)
     head, factors = lax.optimization_barrier((head, factors))
-    tail = gather_along(tail, owners, *along_middle)
-    head = gather_along(head, owners, *along_outer)
+    head = by_step(along(head, *along_outer), first)
     blocks = order_factors(place, placement, factors, owners)
-    blocks = [blocks[0]] + [shift(blocks[r], owners, *along_middle, r) for r in range(1, middle)]
+    blocks = [blocks[0]] + [swap(blocks[r], owners, cores, r) for r in range(1, middle)]
     head, blocks = lax.optimization_barrier((head, blocks))
     here, there = exchange_factors(blocks, owners)
-    heads = [head] + [shift(head, owners, *along_middle, k) for k in range(1, middle)]
-    heads += [shift(p, owners, 1, cores, 1) for p in heads]
-    tail, there = lax.optimization_barrier((tail, there))
-    tail = gather_along(tail, owners, *along_outer)
-    tails = [tail, shift(tail, owners, 1, cores, 1)]
-
+    heads = across(head)
+    tail, here[1], heads[1] = lax.optimization_barrier((tail, here[1], heads[1]))
+    tails = across(by_step(along(tail, *along_outer), steps - first))
+    head_base = base_products(heads, w_gate[0], w_up[0])
+    here, there, head_base = lax.optimization_barrier((here, there, head_base))
     low_rank = relayout_factors(place, here, there, width, units, rank, owners)
-    weights = (w_gate[0], w_up[0], down_weight[0])
-    head, head_sent = run_expert(place, heads, low_rank, *weights)
-    tail, tail_sent = run_expert(place, tails, low_rank, *weights)
-    head = head + shift(head_sent, owners, 1, cores, 1).astype(jnp.float32)
-    tail = tail + shift(tail_sent, owners, 1, cores, 1).astype(jnp.float32)
-    head = scatter_along(head, owners, *along_middle)
-    tail = scatter_along(tail, owners, *along_outer)
-    head = scatter_along(head, owners, *along_outer)
-    tail = scatter_along(tail, owners, *along_middle)
-    return jnp.concatenate([head, tail]).astype(jnp.bfloat16).reshape(steps, rows, width)
+
+    span = outer * rows
+    results = []
+    for s in range(steps):
+        at = s if s < first else s - first
+        pieces, base = (heads, head_base) if s < first else (tails, None)
+        if base is None:
+            pieces, summed = lax.optimization_barrier((pieces, results[0]))
+            results[0] = summed
+            base = base_products(pieces, w_gate[0], w_up[0])
+        kept, sent = finish_step(
+            place, pieces, base, at * span, span, low_rank, down_weight[0]
+        )
+        results.append(kept + swap(sent, owners, 1, 1).astype(jnp.float32))
+    results = [scatter_along(total, owners, *along_middle) for total in results]
+    results = [scatter_along(total, owners, *along_outer) for total in results]
+    return jnp.stack(results).astype(jnp.bfloat16)
 
 
 def row_capacity(rows, top, experts):
@@ -483,6 +557,8 @@
     rank = factors.shape[1] * owners // (3 * (width + units))
     dense = row_capacity(rows, top, placement.shape[0]) == rows
     dense = dense and lax.axis_size("group") == 2 and split_axis(owners)[2] == 2
+    outer = split_axis(owners)[0]
+    dense = dense and outer > 1 and outer & (outer - 1) == 0 and split_axis(owners)[1] > 1
     dense = dense and 2 * rank == LANES and width % 256 == 0 and units % 256 == 0
     dense = dense and factors.shape[1] % (8 * LANES) == 0 and hidden.shape[0] > 1
     return (dense_shards if dense else sparse_shards)(

time: 128 us -> 128 us (level)
  Pallas kernels: 30 us -> 40 us
  waiting for transfers between devices: 46.4 us -> 36.5 us
  local copies, waits for them, and re-layouts: 6.29 us -> 3.06 us
  starting transfers between devices: 43.2 us -> 45.1 us
  other arithmetic: 1.72 us -> 3.11 us
    ppermute x22 -> x28, waiting for transfers between devices: 37.6 us -> 28.3 us  [swap(): return lax.ppermute(x, 'expert', [(i, i ^ k * stride) for i in range(n)])]
    pallas_call x3 -> x6, Pallas kernels: 28.1 us -> 36.3 us  [the longest x3 20.6 us: finish_step(): pl.pallas_call(functools.partial(finish_kernel, len(pieces), first, rows)...]
    ppermute x4, waiting for transfers between devices: 6.68 us -> 0.01 us  [exchange_factors(): there.append(lax.ppermute(part, 'group', [(0, 1), (1, 0)]))]
    ppermute x4, waiting for transfers between devices: 2.15 us -> 8.18 us  [exchange_factors(): part = lax.ppermute(part, ('group', 'expert'), pairs)]
    unnamed x16 -> x12, local copies, waits for them, and re-layouts: 6.12 us -> 1.91 us
    ppermute x22 -> x28, starting transfers between devices: 29.7 us -> 32.3 us  [swap(): return lax.ppermute(x, 'expert', [(i, i ^ k * stride) for i in range(n)])]
    ppermute x4, starting transfers between devices: 7.23 us -> 5.07 us  [exchange_factors(): there.append(lax.ppermute(part, 'group', [(0, 1), (1, 0)]))]
    pallas_call x1, Pallas kernels: 0.32 us -> 2.12 us  [make_payload(): pl.pallas_call(payload_kernel, out_shape=[jax.ShapeDtypeStruct((count * r...]
  transfers between devices with their start and end apart: 30 -> 36, of which waited for: 15 -> 10; matrix products, arithmetic and copies ran while one was open for 1% -> 3% of each run, Pallas kernels for 23% -> 30%
where the time goes in v8:
time: 128 us
  starting transfers between devices  45.1 us (35%)
  Pallas kernels  40 us (31%)
  waiting for transfers between devices  36.5 us (29%)
  other arithmetic  3.11 us (2%)
  local copies, waits for them, and re-layouts  3.06 us (2%)
    ppermute x28, starting transfers between devices, swap(): return lax.ppermute(x, 'expert', [(i, i ^ k * stride) for i in range(n)])  32.3 us
    ppermute x28, waiting for transfers between devices, swap(): return lax.ppermute(x, 'expert', [(i, i ^ k * stride) for i in range(n)])  28.3 us
    pallas_call x3, Pallas kernels, finish_step(): pl.pallas_call(functools.partial(finish_kernel, len(pieces), first, rows)...  20.6 us
    pallas_call x2, Pallas kernels, base_products(): pl.pallas_call(functools.partial(base_kernel, len(pieces)), out_shape=[ou...  12.5 us
    ppermute x4, waiting for transfers between devices, exchange_factors(): part = lax.ppermute(part, ('group', 'expert'), pairs)  8.18 us
    ppermute x4, starting transfers between devices, exchange_factors(): part = lax.ppermute(part, ('group', 'expert'), pairs)  7.71 us
    ppermute x4, starting transfers between devices, exchange_factors(): there.append(lax.ppermute(part, 'group', [(0, 1), (1, 0)]))  5.07 us
    pallas_call x1, Pallas kernels, order_factors(): pl.pallas_call(functools.partial(order_kernel, middle), out_shape=[jax.Sh...  3.22 us
  transfers between devices with their start and end apart: 36, of which 10 were waited for; matrix products, arithmetic and copies ran while one was open for 3% of the time, Pallas kernels for 30%

profile of v8, /device:TPU:0, one launch (start us, length us, event | category | flops | bytes accessed | tf_op | source)
XLA Modules:
  0.0 128.1 jit_solution(14763898080224308671)
XLA Ops:
  0.0 2.1 %payload.1 = (bf16[32,2176]{1,0:T(8,128)(2,1)}, bf16[16,2176]{1,0:T(8,128)(2,1)}) custom-call(bf16[3,16,2048]{2,1,0:T(8,128)(2,1)} %hidden_ref.1, s32[3,8,16]{2,1,0:T(8,128)} %bitcast.54, f32[3,8,16]{2,1,0:T(8,128)} %bitcast.55), custom_call_target="tpu_custom_call" | custom-call | tf_op jit(solution)/shard_map/payload/pallas_call | solution.py:90
  2.1 3.0 %collective-permute-start = (bf16[32,2176]{1,0:T(8,128)(2,1)}, bf16[32,2176]{1,0:T(8,128)(2,1)S(1)}, u32[]{:S(2)}, u32[]{:S(2)}) collective-permute-start(bf16[32,2176]{1,0:T(8,128)(2,1)} %get-tuple-element.49), channel_id=1, source_target_pairs={{0,4},{1,5},{2,6},{3,7},{4,0},{5,1},{6,2},{7,3},{8,12},{9,13},{10,... | collective-permute-start | bytes 417800 | tf_op jit(solution)/shard_map/ppermute | solution.py:33
  5.1 2.6 %collective-permute-start.1 = (bf16[32,2176]{1,0:T(8,128)(2,1)}, bf16[32,2176]{1,0:T(8,128)(2,1)S(1)}, u32[]{:S(2)}, u32[]{:S(2)}) collective-permute-start(bf16[32,2176]{1,0:T(8,128)(2,1)} %get-tuple-element.49), channel_id=1, source_target_pairs={{0,8},{1,9},{2,10},{3,11},{4,12},{5,13},{6,14},{7,15},{8,0},{9,1},... | collective-permute-start | bytes 417800 | tf_op jit(solution)/shard_map/ppermute | solution.py:33
  8.4 3.2 %order_factors.1 = (bf16[4,264,128]{2,1,0:T(8,128)(2,1)}, bf16[4,264,128]{2,1,0:T(8,128)(2,1)}) custom-call(s32[2]{0:T(128)} %pad_add_fusion.place_ref, s32[16]{0:T(128)} %placement_ref.1, bf16[16,33792]{1,0:T(8,128)(2,1)} %factors_ref), custom_call_target="tpu_custom_call" | custom-call | tf_op jit(solution)/shard_map/order_factors/pallas_call | solution.py:137
  11.6 1.7 %collective-permute-start.3 = (bf16[4,264,128]{2,1,0:T(8,128)(2,1)}, bf16[4,264,128]{2,1,0:T(8,128)(2,1)S(1)}, u32[]{:S(2)}, u32[]{:S(2)}) collective-permute-start(bf16[4,264,128]{2,1,0:T(8,128)(2,1)} %get-tuple-element.52), channel_id=1, source_target_pairs={{0,2},{1,3},{2,0},{3,1},{4,6},{5,7},{6,4},{7,5},{8,10},{9,11},{10,... | collective-permute-start | bytes 811016 | tf_op jit(solution)/shard_map/ppermute | solution.py:33
  13.3 5.5 %collective-permute-done.1 = bf16[32,2176]{1,0:T(8,128)(2,1)S(1)} collective-permute-done((bf16[32,2176]{1,0:T(8,128)(2,1)}, bf16[32,2176]{1,0:T(8,128)(2,1)S(1)}, u32[]{:S(2)}, u32[]{:S(2)}) %collective-permute-start.1) | collective-permute-done | bytes 139296 | tf_op jit(solution)/shard_map/ppermute | solution.py:33
  19.9 1.6 %collective-permute-start.5 = (bf16[128,2176]{1,0:T(8,128)(2,1)S(1)}, bf16[128,2176]{1,0:T(8,128)(2,1)S(1)}, u32[]{:S(2)}, u32[]{:S(2)}) collective-permute-start(bf16[128,2176]{1,0:T(8,128)(2,1)S(1)} %bitcast.34), channel_id=1, source_target_pairs={{0,2},{1,3},{2,0},{3,1},{4,6},{5,7},{6,4},{7,5},{8,10},{9,11},{10,... | collective-permute-start | bytes 1671176 | tf_op jit(solution)/shard_map/ppermute | solution.py:33
  22.5 9.8 %collective-permute-done.5.refs_1_ = bf16[128,2176]{1,0:T(8,128)(2,1)S(1)} collective-permute-done((bf16[128,2176]{1,0:T(8,128)(2,1)S(1)}, bf16[128,2176]{1,0:T(8,128)(2,1)S(1)}, u32[]{:S(2)}, u32[]{:S(2)}) %collective-permute-start.5) | collective-permute-done | bytes 557088 | tf_op jit(solution)/shard_map/ppermute | solution.py:33
  32.4 3.2 %collective-permute-start.4 = (bf16[2,264,128]{2,1,0:T(8,128)(2,1)S(1)}, bf16[2,264,128]{2,1,0:T(8,128)(2,1)S(1)}, u32[]{:S(2)}, u32[]{:S(2)}) collective-permute-start(bf16[2,264,128]{2,1,0:T(8,128)(2,1)S(1)} %pad_maximum_fusion.3), channel_id=1, source_target_pairs={{0,4},{1,5},{2,6},{3,7},{4,0},{5,1},{6,2},{7,3},{8,12},{9,13},{10,... | collective-permute-start | bytes 405512 | tf_op jit(solution)/shard_map/ppermute | solution.py:54
  36.3 1.3 collective-permute-start.15
  37.5 2.3 %collective-permute-done.4.refs_1_ = bf16[2,264,128]{2,1,0:T(8,128)(2,1)S(1)} collective-permute-done((bf16[2,264,128]{2,1,0:T(8,128)(2,1)S(1)}, bf16[2,264,128]{2,1,0:T(8,128)(2,1)S(1)}, u32[]{:S(2)}, u32[]{:S(2)}) %collective-permute-start.4) | collective-permute-done | bytes 135200 | tf_op jit(solution)/shard_map/ppermute | solution.py:54
  39.8 2.6 %collective-permute-start.16 = (bf16[2,264,128]{2,1,0:T(8,128)(2,1)S(1)}, bf16[2,264,128]{2,1,0:T(8,128)(2,1)S(1)}, u32[]{:S(2)}, u32[]{:S(2)}) collective-permute-start(bf16[2,264,128]{2,1,0:T(8,128)(2,1)S(1)} %pad_maximum_fusion.6), channel_id=1, source_target_pairs={{0,12},{1,13},{2,14},{3,15},{4,8},{5,9},{6,10},{7,11},{8,4},{9,5},... | collective-permute-start | bytes 405512 | tf_op jit(solution)/shard_map/ppermute | solution.py:54
  43.5 5.9 %collective-permute-done.15.refs_2_ = bf16[2,264,128]{2,1,0:T(8,128)(2,1)S(1)} collective-permute-done((bf16[2,264,128]{2,1,0:T(8,128)(2,1)S(1)}, bf16[2,264,128]{2,1,0:T(8,128)(2,1)S(1)}, u32[]{:S(2)}, u32[]{:S(2)}) %collective-permute-start.15) | collective-permute-done | bytes 135200 | tf_op jit(solution)/shard_map/ppermute | solution.py:54
  49.4 2.0 %collective-permute-start.17 = (bf16[2,264,128]{2,1,0:T(8,128)(2,1)S(1)}, bf16[2,264,128]{2,1,0:T(8,128)(2,1)S(1)}, u32[]{:S(2)}, u32[]{:S(2)}) collective-permute-start(bf16[2,264,128]{2,1,0:T(8,128)(2,1)S(1)} %collective-permute-done.14.refs_0_), channel_id=1, source_target_pairs={{0,16},{16,0},{1,17},{17,1},{2,18},{18,2},{3,19},{19,3},{4,20},{20... | collective-permute-start | bytes 405512 | tf_op jit(solution)/shard_map/ppermute | solution.py:56
  51.4 2.0 %collective-permute-start.20 = (bf16[2,264,128]{2,1,0:T(8,128)(2,1)S(1)}, bf16[2,264,128]{2,1,0:T(8,128)(2,1)S(1)}, u32[]{:S(2)}, u32[]{:S(2)}) collective-permute-start(bf16[2,264,128]{2,1,0:T(8,128)(2,1)S(1)} %collective-permute-done.16.refs_3_), channel_id=1, source_target_pairs={{0,16},{16,0},{1,17},{17,1},{2,18},{18,2},{3,19},{19,3},{4,20},{20... | collective-permute-start | bytes 405512 | tf_op jit(solution)/shard_map/ppermute | solution.py:56
  53.4 1.5 %collective-permute-start.6 = (bf16[16,2176]{1,0:T(8,128)(2,1)S(1)}, bf16[16,2176]{1,0:T(8,128)(2,1)S(1)}, u32[]{:S(2)}, u32[]{:S(2)}) collective-permute-start(bf16[16,2176]{1,0:T(8,128)(2,1)S(1)} %copy-done.5), channel_id=1, source_target_pairs={{0,4},{1,5},{2,6},{3,7},{4,0},{5,1},{6,2},{7,3},{8,12},{9,13},{10,... | collective-permute-start | bytes 208904 | tf_op jit(solution)/shard_map/ppermute | solution.py:33
  54.9 1.9 %copy-done.2 = bf16[1,2048,768]{2,1,0:T(8,128)(2,1)S(1)} copy-done((bf16[1,2048,768]{2,1,0:T(8,128)(2,1)S(1)}, bf16[1,2048,768]{2,1,0:T(8,128)(2,1)}, u32[]{:S(2)}) %copy-start.2) | copy-done | bytes 3145752
  56.8 8.2 %base_products.2 = (f32[512,768]{1,0:T(8,128)S(1)}, f32[512,768]{1,0:T(8,128)S(1)}) custom-call(bf16[128,2176]{1,0:T(8,128)(2,1)S(1)} %bitcast.36, bf16[128,2176]{1,0:T(8,128)(2,1)S(1)} %collective-permute-done.5.refs_1_, bf16[128,2176]{1,0:T(8,128)(2,1)S(1)} %collective-permute-done.12.refs_2_, bf16[128,2176]{1,0:T(8,128)(2,1)S(1)} %collective-permute-done.13.refs_3_, ...), custom_call_target="tpu_custom_call" | custom-call | flops 3221225472 | bytes 11534336 | tf_op jit(solution)/shard_map/base_products/pallas_call | solution.py:282
  65.0 1.9 %collective-permute-start.7 = (bf16[16,2176]{1,0:T(8,128)(2,1)S(1)}, bf16[16,2176]{1,0:T(8,128)(2,1)S(1)}, u32[]{:S(2)}, u32[]{:S(2)}) collective-permute-start(bf16[16,2176]{1,0:T(8,128)(2,1)S(1)} %copy-done.5), channel_id=1, source_target_pairs={{0,8},{1,9},{2,10},{3,11},{4,12},{5,13},{6,14},{7,15},{8,0},{9,1},... | collective-permute-start | bytes 208904 | tf_op jit(solution)/shard_map/ppermute | solution.py:33
  68.0 1.6 %relayout_factors.1 = (bf16[2048,128]{1,0:T(8,128)(2,1)S(1)}, bf16[64,768]{1,0:T(8,128)(2,1)S(1)}, bf16[64,768]{1,0:T(8,128)(2,1)S(1)}, bf16[768,128]{1,0:T(8,128)(2,1)S(1)}, bf16[64,2048]{1,0:T(8,128)(2,1)S(1)}) custom-call(s32[2]{0:T(128)S(1)} %copy-done.4, bf16[2,264,128]{2,1,0:T(8,128)(2,1)S(1)} %collective-permute-done.14.refs_0_, ...), custom_call_target="tpu_custom_call" | custom-call | tf_op jit(solution)/shard_map/relayout_factors/pallas_call | solution.py:206
  69.6 6.9 %finish_step.3 = (f32[128,2048]{1,0:T(8,128)S(1)}, bf16[128,2048]{1,0:T(8,128)(2,1)S(1)}) custom-call(s32[2]{0:T(128)S(1)} %copy-done.4, bf16[128,2176]{1,0:T(8,128)(2,1)S(1)} %bitcast.37, bf16[128,2176]{1,0:T(8,128)(2,1)S(1)} %collective-permute-done.5.refs_1_, bf16[128,2176]{1,0:T(8,128)(2,1)S(1)} %collective-permute-done.12.refs_2_, ...), custom_call_target="tpu_custom_call" | custom-call | flops 1174405120 | bytes 7340032 | tf_op jit(solution)/shard_map/finish_step/pallas_call | solution.py:377
  76.6 1.6 %collective-permute-start.9 = (bf16[64,2176]{1,0:T(8,128)(2,1)S(1)}, bf16[64,2176]{1,0:T(8,128)(2,1)S(1)}, u32[]{:S(2)}, u32[]{:S(2)}) collective-permute-start(bf16[64,2176]{1,0:T(8,128)(2,1)S(1)} %bitcast.43), channel_id=1, source_target_pairs={{0,2},{1,3},{2,0},{3,1},{4,6},{5,7},{6,4},{7,5},{8,10},{9,11},{10,... | collective-permute-start | bytes 835592 | tf_op jit(solution)/shard_map/ppermute | solution.py:33
  78.2 6.9 %finish_step.4 = (f32[128,2048]{1,0:T(8,128)S(1)}, bf16[128,2048]{1,0:T(8,128)(2,1)S(1)}) custom-call(s32[2]{0:T(128)S(1)} %copy-done.4, bf16[128,2176]{1,0:T(8,128)(2,1)S(1)} %bitcast.38, bf16[128,2176]{1,0:T(8,128)(2,1)S(1)} %collective-permute-done.5.refs_1_, bf16[128,2176]{1,0:T(8,128)(2,1)S(1)} %collective-permute-done.12.refs_2_, ...), custom_call_target="tpu_custom_call" | custom-call | flops 1174405120 | bytes 7340032 | tf_op jit(solution)/shard_map/finish_step/pallas_call | solution.py:377
  85.9 1.5 %collective-permute-done.10.refs_2_ = bf16[64,2176]{1,0:T(8,128)(2,1)S(1)} collective-permute-done((bf16[64,2176]{1,0:T(8,128)(2,1)S(1)}, bf16[64,2176]{1,0:T(8,128)(2,1)S(1)}, u32[]{:S(2)}, u32[]{:S(2)}) %collective-permute-start.10) | collective-permute-done | bytes 278560 | tf_op jit(solution)/shard_map/ppermute | solution.py:33
  90.2 4.4 %base_products.3 = (f32[256,768]{1,0:T(8,128)S(1)}, f32[256,768]{1,0:T(8,128)S(1)}) custom-call(bf16[64,2176]{1,0:T(8,128)(2,1)S(1)} %bitcast.45, bf16[64,2176]{1,0:T(8,128)(2,1)S(1)} %collective-permute-done.9.refs_1_, bf16[64,2176]{1,0:T(8,128)(2,1)S(1)} %collective-permute-done.10.refs_2_, bf16[64,2176]{1,0:T(8,128)(2,1)S(1)} %collective-permute-done.11.refs_3_, ...), custom_call_target="tpu_custom_call" | custom-call | flops 1610612736 | bytes 8912896 | tf_op jit(solution)/shard_map/base_products/pallas_call | solution.py:282
  94.5 6.9 %finish_step.5 = (f32[128,2048]{1,0:T(8,128)S(1)}, bf16[128,2048]{1,0:T(8,128)(2,1)S(1)}) custom-call(s32[2]{0:T(128)S(1)} %copy-done.4, bf16[64,2176]{1,0:T(8,128)(2,1)S(1)} %bitcast.46, bf16[64,2176]{1,0:T(8,128)(2,1)S(1)} %collective-permute-done.9.refs_1_, bf16[64,2176]{1,0:T(8,128)(2,1)S(1)} %collective-permute-done.10.refs_2_, ...), custom_call_target="tpu_custom_call" | custom-call | flops 1174405120 | bytes 7340032 | tf_op jit(solution)/shard_map/finish_step/pallas_call | solution.py:377
  102.2 2.7 %collective-permute-start.24 = (bf16[16,2048]{1,0:T(8,128)(2,1)S(1)}, bf16[16,2048]{1,0:T(8,128)(2,1)S(1)}, u32[]{:S(2)}, u32[]{:S(2)}) collective-permute-start(bf16[16,2048]{1,0:T(8,128)(2,1)S(1)} %get-tuple-element.105), channel_id=1, source_target_pairs={{0,8},{1,9},{2,10},{3,11},{4,12},{5,13},{6,14},{7,15},{8,0},{9,1},... | collective-permute-start | bytes 196616 | tf_op jit(solution)/shard_map/ppermute | solution.py:33
  106.2 3.3 %collective-permute-start.29 = (bf16[16,2048]{1,0:T(8,128)(2,1)S(1)}, bf16[16,2048]{1,0:T(8,128)(2,1)S(1)}, u32[]{:S(2)}, u32[]{:S(2)}) collective-permute-start(bf16[16,2048]{1,0:T(8,128)(2,1)S(1)} %get-tuple-element.108), channel_id=1, source_target_pairs={{0,8},{1,9},{2,10},{3,11},{4,12},{5,13},{6,14},{7,15},{8,0},{9,1},... | collective-permute-start | bytes 196616 | tf_op jit(solution)/shard_map/ppermute | solution.py:33
  111.8 6.0 %collective-permute-done.32 = bf16[64,2048]{1,0:T(8,128)(2,1)S(1)} collective-permute-done((bf16[64,2048]{1,0:T(8,128)(2,1)S(1)}, bf16[64,2048]{1,0:T(8,128)(2,1)S(1)}, u32[]{:S(2)}, u32[]{:S(2)}) %collective-permute-start.32) | collective-permute-done | bytes 262176 | tf_op jit(solution)/shard_map/ppermute | solution.py:33
  118.0 3.3 %collective-permute-start.34 = (bf16[16,2048]{1,0:T(8,128)(2,1)S(1)}, bf16[16,2048]{1,0:T(8,128)(2,1)S(1)}, u32[]{:S(2)}, u32[]{:S(2)}) collective-permute-start(bf16[16,2048]{1,0:T(8,128)(2,1)S(1)} %get-tuple-element.111), channel_id=1, source_target_pairs={{0,8},{1,9},{2,10},{3,11},{4,12},{5,13},{6,14},{7,15},{8,0},{9,1},... | collective-permute-start | bytes 196616 | tf_op jit(solution)/shard_map/ppermute | solution.py:33
  122.4 2.4 %collective-permute-done.34 = bf16[16,2048]{1,0:T(8,128)(2,1)S(1)} collective-permute-done((bf16[16,2048]{1,0:T(8,128)(2,1)S(1)}, bf16[16,2048]{1,0:T(8,128)(2,1)S(1)}, u32[]{:S(2)}, u32[]{:S(2)}) %collective-permute-start.34) | collective-permute-done | bytes 65568 | tf_op jit(solution)/shard_map/ppermute | solution.py:33
  124.8 2.6 %collective-permute-done.35 = bf16[16,2048]{1,0:T(8,128)(2,1)S(1)} collective-permute-done((bf16[16,2048]{1,0:T(8,128)(2,1)S(1)}, bf16[16,2048]{1,0:T(8,128)(2,1)S(1)}, u32[]{:S(2)}, u32[]{:S(2)}) %collective-permute-start.35) | collective-permute-done | bytes 65568 | tf_op jit(solution)/shard_map/ppermute | solution.py:33
  (84 shorter events, 15.6 us)
Async XLA Ops:
  2.1 11.2 %collective-permute-start = (bf16[32,2176]{1,0:T(8,128)(2,1)}, bf16[32,2176]{1,0:T(8,128)(2,1)S(1)}, u32[]{:S(2)}, u32[]{:S(2)}) collective-permute-start(bf16[32,2176]{1,0:T(8,128)(2,1)} %get-tuple-element.49), channel_id=1, source_target_pairs={{0,4},{1,5},{2,6},{3,7},{4,0},{5,1},{6,2},{7,3},{8,12},{9,13},{10,... | collective-permute-start | bytes 417800 | tf_op jit(solution)/shard_map/ppermute | solution.py:33
  5.1 13.7 %collective-permute-start.1 = (bf16[32,2176]{1,0:T(8,128)(2,1)}, bf16[32,2176]{1,0:T(8,128)(2,1)S(1)}, u32[]{:S(2)}, u32[]{:S(2)}) collective-permute-start(bf16[32,2176]{1,0:T(8,128)(2,1)} %get-tuple-element.49), channel_id=1, source_target_pairs={{0,8},{1,9},{2,10},{3,11},{4,12},{5,13},{6,14},{7,15},{8,0},{9,1},... | collective-permute-start | bytes 417800 | tf_op jit(solution)/shard_map/ppermute | solution.py:33
  7.7 11.1 %collective-permute-start.2 = (bf16[32,2176]{1,0:T(8,128)(2,1)}, bf16[32,2176]{1,0:T(8,128)(2,1)}, u32[]{:S(2)}, u32[]{:S(2)}) collective-permute-start(bf16[32,2176]{1,0:T(8,128)(2,1)} %get-tuple-element.49), channel_id=1, source_target_pairs={{0,12},{1,13},{2,14},{3,15},{4,8},{5,9},{6,10},{7,11},{8,4},{9,5},... | collective-permute-start | bytes 417800 | tf_op jit(solution)/shard_map/ppermute | solution.py:33
  11.6 8.3 %collective-permute-start.3 = (bf16[4,264,128]{2,1,0:T(8,128)(2,1)}, bf16[4,264,128]{2,1,0:T(8,128)(2,1)S(1)}, u32[]{:S(2)}, u32[]{:S(2)}) collective-permute-start(bf16[4,264,128]{2,1,0:T(8,128)(2,1)} %get-tuple-element.52), channel_id=1, source_target_pairs={{0,2},{1,3},{2,0},{3,1},{4,6},{5,7},{6,4},{7,5},{8,10},{9,11},{10,... | collective-permute-start | bytes 811016 | tf_op jit(solution)/shard_map/ppermute | solution.py:33
  19.9 12.5 %collective-permute-start.5 = (bf16[128,2176]{1,0:T(8,128)(2,1)S(1)}, bf16[128,2176]{1,0:T(8,128)(2,1)S(1)}, u32[]{:S(2)}, u32[]{:S(2)}) collective-permute-start(bf16[128,2176]{1,0:T(8,128)(2,1)S(1)} %bitcast.34), channel_id=1, source_target_pairs={{0,2},{1,3},{2,0},{3,1},{4,6},{5,7},{6,4},{7,5},{8,10},{9,11},{10,... | collective-permute-start | bytes 1671176 | tf_op jit(solution)/shard_map/ppermute | solution.py:33
  21.5 29.9 %collective-permute-start.12 = (bf16[128,2176]{1,0:T(8,128)(2,1)S(1)}, bf16[128,2176]{1,0:T(8,128)(2,1)S(1)}, u32[]{:S(2)}, u32[]{:S(2)}) collective-permute-start(bf16[128,2176]{1,0:T(8,128)(2,1)S(1)} %bitcast.35), channel_id=1, source_target_pairs={{0,1},{1,0},{2,3},{3,2},{4,5},{5,4},{6,7},{7,6},{8,9},{9,8},{10,11... | collective-permute-start | bytes 1671176 | tf_op jit(solution)/shard_map/ppermute | solution.py:33
  32.4 21.1 %collective-permute-start.13 = (bf16[128,2176]{1,0:T(8,128)(2,1)S(1)}, bf16[128,2176]{1,0:T(8,128)(2,1)S(1)}, u32[]{:S(2)}, u32[]{:S(2)}) collective-permute-start(bf16[128,2176]{1,0:T(8,128)(2,1)S(1)} %collective-permute-done.5.refs_1_), channel_id=1, source_target_pairs={{0,1},{1,0},{2,3},{3,2},{4,5},{5,4},{6,7},{7,6},{8,9},{9,8},{10,11... | collective-permute-start | bytes 1671176 | tf_op jit(solution)/shard_map/ppermute | solution.py:33
  32.4 7.4 %collective-permute-start.4 = (bf16[2,264,128]{2,1,0:T(8,128)(2,1)S(1)}, bf16[2,264,128]{2,1,0:T(8,128)(2,1)S(1)}, u32[]{:S(2)}, u32[]{:S(2)}) collective-permute-start(bf16[2,264,128]{2,1,0:T(8,128)(2,1)S(1)} %pad_maximum_fusion.3), channel_id=1, source_target_pairs={{0,4},{1,5},{2,6},{3,7},{4,0},{5,1},{6,2},{7,3},{8,12},{9,13},{10,... | collective-permute-start | bytes 405512 | tf_op jit(solution)/shard_map/ppermute | solution.py:54
  35.6 6.9 %collective-permute-start.14 = (bf16[2,264,128]{2,1,0:T(8,128)(2,1)S(1)}, bf16[2,264,128]{2,1,0:T(8,128)(2,1)S(1)}, u32[]{:S(2)}, u32[]{:S(2)}) collective-permute-start(bf16[2,264,128]{2,1,0:T(8,128)(2,1)S(1)} %pad_maximum_fusion.4), channel_id=1, source_target_pairs={{0,0},{1,1},{2,2},{3,3},{4,4},{5,5},{6,6},{7,7},{8,8},{9,9},{10,10... | collective-permute-start | bytes 405512 | tf_op jit(solution)/shard_map/ppermute | solution.py:54
  36.3 13.1 %collective-permute-start.15 = (bf16[2,264,128]{2,1,0:T(8,128)(2,1)S(1)}, bf16[2,264,128]{2,1,0:T(8,128)(2,1)S(1)}, u32[]{:S(2)}, u32[]{:S(2)}) collective-permute-start(bf16[2,264,128]{2,1,0:T(8,128)(2,1)S(1)} %pad_maximum_fusion.5), channel_id=1, source_target_pairs={{0,8},{1,9},{2,10},{3,11},{4,12},{5,13},{6,14},{7,15},{8,0},{9,1},... | collective-permute-start | bytes 405512 | tf_op jit(solution)/shard_map/ppermute | solution.py:54
  39.8 11.6 %collective-permute-start.16 = (bf16[2,264,128]{2,1,0:T(8,128)(2,1)S(1)}, bf16[2,264,128]{2,1,0:T(8,128)(2,1)S(1)}, u32[]{:S(2)}, u32[]{:S(2)}) collective-permute-start(bf16[2,264,128]{2,1,0:T(8,128)(2,1)S(1)} %pad_maximum_fusion.6), channel_id=1, source_target_pairs={{0,12},{1,13},{2,14},{3,15},{4,8},{5,9},{6,10},{7,11},{8,4},{9,5},... | collective-permute-start | bytes 405512 | tf_op jit(solution)/shard_map/ppermute | solution.py:54
  42.4 25.5 %collective-permute-start.18 = (bf16[2,264,128]{2,1,0:T(8,128)(2,1)S(1)}, bf16[2,264,128]{2,1,0:T(8,128)(2,1)S(1)}, u32[]{:S(2)}, u32[]{:S(2)}) collective-permute-start(bf16[2,264,128]{2,1,0:T(8,128)(2,1)S(1)} %collective-permute-done.4.refs_1_), channel_id=1, source_target_pairs={{0,16},{16,0},{1,17},{17,1},{2,18},{18,2},{3,19},{19,3},{4,20},{20... | collective-permute-start | bytes 405512 | tf_op jit(solution)/shard_map/ppermute | solution.py:56
  49.4 15.7 %collective-permute-start.17 = (bf16[2,264,128]{2,1,0:T(8,128)(2,1)S(1)}, bf16[2,264,128]{2,1,0:T(8,128)(2,1)S(1)}, u32[]{:S(2)}, u32[]{:S(2)}) collective-permute-start(bf16[2,264,128]{2,1,0:T(8,128)(2,1)S(1)} %collective-permute-done.14.refs_0_), channel_id=1, source_target_pairs={{0,16},{16,0},{1,17},{17,1},{2,18},{18,2},{3,19},{19,3},{4,20},{20... | collective-permute-start | bytes 405512 | tf_op jit(solution)/shard_map/ppermute | solution.py:56
  51.4 15.5 %collective-permute-start.19 = (bf16[2,264,128]{2,1,0:T(8,128)(2,1)S(1)}, bf16[2,264,128]{2,1,0:T(8,128)(2,1)S(1)}, u32[]{:S(2)}, u32[]{:S(2)}) collective-permute-start(bf16[2,264,128]{2,1,0:T(8,128)(2,1)S(1)} %collective-permute-done.15.refs_2_), channel_id=1, source_target_pairs={{0,16},{16,0},{1,17},{17,1},{2,18},{18,2},{3,19},{19,3},{4,20},{20... | collective-permute-start | bytes 405512 | tf_op jit(solution)/shard_map/ppermute | solution.py:56
  51.4 16.5 %collective-permute-start.20 = (bf16[2,264,128]{2,1,0:T(8,128)(2,1)S(1)}, bf16[2,264,128]{2,1,0:T(8,128)(2,1)S(1)}, u32[]{:S(2)}, u32[]{:S(2)}) collective-permute-start(bf16[2,264,128]{2,1,0:T(8,128)(2,1)S(1)} %collective-permute-done.16.refs_3_), channel_id=1, source_target_pairs={{0,16},{16,0},{1,17},{17,1},{2,18},{18,2},{3,19},{19,3},{4,20},{20... | collective-permute-start | bytes 405512 | tf_op jit(solution)/shard_map/ppermute | solution.py:56
  53.4 23.1 %collective-permute-start.6 = (bf16[16,2176]{1,0:T(8,128)(2,1)S(1)}, bf16[16,2176]{1,0:T(8,128)(2,1)S(1)}, u32[]{:S(2)}, u32[]{:S(2)}) collective-permute-start(bf16[16,2176]{1,0:T(8,128)(2,1)S(1)} %copy-done.5), channel_id=1, source_target_pairs={{0,4},{1,5},{2,6},{3,7},{4,0},{5,1},{6,2},{7,3},{8,12},{9,13},{10,... | collective-permute-start | bytes 208904 | tf_op jit(solution)/shard_map/ppermute | solution.py:33
  65.0 11.5 %collective-permute-start.7 = (bf16[16,2176]{1,0:T(8,128)(2,1)S(1)}, bf16[16,2176]{1,0:T(8,128)(2,1)S(1)}, u32[]{:S(2)}, u32[]{:S(2)}) collective-permute-start(bf16[16,2176]{1,0:T(8,128)(2,1)S(1)} %copy-done.5), channel_id=1, source_target_pairs={{0,8},{1,9},{2,10},{3,11},{4,12},{5,13},{6,14},{7,15},{8,0},{9,1},... | collective-permute-start | bytes 208904 | tf_op jit(solution)/shard_map/ppermute | solution.py:33
  66.9 9.6 %collective-permute-start.8 = (bf16[16,2176]{1,0:T(8,128)(2,1)S(1)}, bf16[16,2176]{1,0:T(8,128)(2,1)S(1)}, u32[]{:S(2)}, u32[]{:S(2)}) collective-permute-start(bf16[16,2176]{1,0:T(8,128)(2,1)S(1)} %copy-done.5), channel_id=1, source_target_pairs={{0,12},{1,13},{2,14},{3,15},{4,8},{5,9},{6,10},{7,11},{8,4},{9,5},... | collective-permute-start | bytes 208904 | tf_op jit(solution)/shard_map/ppermute | solution.py:33
  76.4 9.4 %collective-permute-start.21 = (bf16[128,2048]{1,0:T(8,128)(2,1)S(1)}, bf16[128,2048]{1,0:T(8,128)(2,1)S(1)}, u32[]{:S(2)}, u32[]{:S(2)}) collective-permute-start(bf16[128,2048]{1,0:T(8,128)(2,1)S(1)} %get-tuple-element.77), channel_id=1, source_target_pairs={{0,1},{1,0},{2,3},{3,2},{4,5},{5,4},{6,7},{7,6},{8,9},{9,8},{10,11... | collective-permute-start | bytes 1572872 | tf_op jit(solution)/shard_map/ppermute | solution.py:33
  76.6 9.1 %collective-permute-start.9 = (bf16[64,2176]{1,0:T(8,128)(2,1)S(1)}, bf16[64,2176]{1,0:T(8,128)(2,1)S(1)}, u32[]{:S(2)}, u32[]{:S(2)}) collective-permute-start(bf16[64,2176]{1,0:T(8,128)(2,1)S(1)} %bitcast.43), channel_id=1, source_target_pairs={{0,2},{1,3},{2,0},{3,1},{4,6},{5,7},{6,4},{7,5},{8,10},{9,11},{10,... | collective-permute-start | bytes 835592 | tf_op jit(solution)/shard_map/ppermute | solution.py:33
  87.9 13.6 %collective-permute-start.22 = (bf16[64,2048]{1,0:T(8,128)(2,1)S(1)}, bf16[64,2048]{1,0:T(8,128)(2,1)S(1)}, u32[]{:S(2)}, u32[]{:S(2)}) collective-permute-start(bf16[64,2048]{1,0:T(8,128)(2,1)S(1)} %slice.168), channel_id=1, source_target_pairs={{0,2},{1,3},{2,0},{3,1},{4,6},{5,7},{6,4},{7,5},{8,10},{9,11},{10,... | collective-permute-start | bytes 786440 | tf_op jit(solution)/shard_map/ppermute | solution.py:33
  89.0 17.0 %collective-permute-start.27 = (bf16[64,2048]{1,0:T(8,128)(2,1)S(1)}, bf16[64,2048]{1,0:T(8,128)(2,1)S(1)}, u32[]{:S(2)}, u32[]{:S(2)}) collective-permute-start(bf16[64,2048]{1,0:T(8,128)(2,1)S(1)} %slice.167), channel_id=1, source_target_pairs={{0,2},{1,3},{2,0},{3,1},{4,6},{5,7},{6,4},{7,5},{8,10},{9,11},{10,... | collective-permute-start | bytes 786440 | tf_op jit(solution)/shard_map/ppermute | solution.py:33
  101.4 4.8 %collective-permute-start.31 = (bf16[128,2048]{1,0:T(8,128)(2,1)S(1)}, bf16[128,2048]{1,0:T(8,128)(2,1)S(1)}, u32[]{:S(2)}, u32[]{:S(2)}) collective-permute-start(bf16[128,2048]{1,0:T(8,128)(2,1)S(1)} %get-tuple-element.88), channel_id=1, source_target_pairs={{0,1},{1,0},{2,3},{3,2},{4,5},{5,4},{6,7},{7,6},{8,9},{9,8},{10,11... | collective-permute-start | bytes 1572872 | tf_op jit(solution)/shard_map/ppermute | solution.py:33
  101.6 8.1 %collective-permute-start.23 = (bf16[16,2048]{1,0:T(8,128)(2,1)S(1)}, bf16[16,2048]{1,0:T(8,128)(2,1)S(1)}, u32[]{:S(2)}, u32[]{:S(2)}) collective-permute-start(bf16[16,2048]{1,0:T(8,128)(2,1)S(1)} %get-tuple-element.103), channel_id=1, source_target_pairs={{0,4},{1,5},{2,6},{3,7},{4,0},{5,1},{6,2},{7,3},{8,12},{9,13},{10,... | collective-permute-start | bytes 196616 | tf_op jit(solution)/shard_map/ppermute | solution.py:33
  102.2 8.6 %collective-permute-start.24 = (bf16[16,2048]{1,0:T(8,128)(2,1)S(1)}, bf16[16,2048]{1,0:T(8,128)(2,1)S(1)}, u32[]{:S(2)}, u32[]{:S(2)}) collective-permute-start(bf16[16,2048]{1,0:T(8,128)(2,1)S(1)} %get-tuple-element.105), channel_id=1, source_target_pairs={{0,8},{1,9},{2,10},{3,11},{4,12},{5,13},{6,14},{7,15},{8,0},{9,1},... | collective-permute-start | bytes 196616 | tf_op jit(solution)/shard_map/ppermute | solution.py:33
  105.0 6.8 %collective-permute-start.25 = (bf16[16,2048]{1,0:T(8,128)(2,1)S(1)}, bf16[16,2048]{1,0:T(8,128)(2,1)S(1)}, u32[]{:S(2)}, u32[]{:S(2)}) collective-permute-start(bf16[16,2048]{1,0:T(8,128)(2,1)S(1)} %get-tuple-element.104), channel_id=1, source_target_pairs={{0,12},{1,13},{2,14},{3,15},{4,8},{5,9},{6,10},{7,11},{8,4},{9,5},... | collective-permute-start | bytes 196616 | tf_op jit(solution)/shard_map/ppermute | solution.py:33
  106.1 15.2 %collective-permute-start.28 = (bf16[16,2048]{1,0:T(8,128)(2,1)S(1)}, bf16[16,2048]{1,0:T(8,128)(2,1)S(1)}, u32[]{:S(2)}, u32[]{:S(2)}) collective-permute-start(bf16[16,2048]{1,0:T(8,128)(2,1)S(1)} %get-tuple-element.106), channel_id=1, source_target_pairs={{0,4},{1,5},{2,6},{3,7},{4,0},{5,1},{6,2},{7,3},{8,12},{9,13},{10,... | collective-permute-start | bytes 196616 | tf_op jit(solution)/shard_map/ppermute | solution.py:33
  106.2 16.2 %collective-permute-start.29 = (bf16[16,2048]{1,0:T(8,128)(2,1)S(1)}, bf16[16,2048]{1,0:T(8,128)(2,1)S(1)}, u32[]{:S(2)}, u32[]{:S(2)}) collective-permute-start(bf16[16,2048]{1,0:T(8,128)(2,1)S(1)} %get-tuple-element.108), channel_id=1, source_target_pairs={{0,8},{1,9},{2,10},{3,11},{4,12},{5,13},{6,14},{7,15},{8,0},{9,1},... | collective-permute-start | bytes 196616 | tf_op jit(solution)/shard_map/ppermute | solution.py:33
  109.7 12.7 %collective-permute-start.30 = (bf16[16,2048]{1,0:T(8,128)(2,1)S(1)}, bf16[16,2048]{1,0:T(8,128)(2,1)S(1)}, u32[]{:S(2)}, u32[]{:S(2)}) collective-permute-start(bf16[16,2048]{1,0:T(8,128)(2,1)S(1)} %get-tuple-element.107), channel_id=1, source_target_pairs={{0,12},{1,13},{2,14},{3,15},{4,8},{5,9},{6,10},{7,11},{8,4},{9,5},... | collective-permute-start | bytes 196616 | tf_op jit(solution)/shard_map/ppermute | solution.py:33
  110.8 7.0 %collective-permute-start.32 = (bf16[64,2048]{1,0:T(8,128)(2,1)S(1)}, bf16[64,2048]{1,0:T(8,128)(2,1)S(1)}, u32[]{:S(2)}, u32[]{:S(2)}) collective-permute-start(bf16[64,2048]{1,0:T(8,128)(2,1)S(1)} %slice.166), channel_id=1, source_target_pairs={{0,2},{1,3},{2,0},{3,1},{4,6},{5,7},{6,4},{7,5},{8,10},{9,11},{10,... | collective-permute-start | bytes 786440 | tf_op jit(solution)/shard_map/ppermute | solution.py:33
  118.0 6.8 %collective-permute-start.34 = (bf16[16,2048]{1,0:T(8,128)(2,1)S(1)}, bf16[16,2048]{1,0:T(8,128)(2,1)S(1)}, u32[]{:S(2)}, u32[]{:S(2)}) collective-permute-start(bf16[16,2048]{1,0:T(8,128)(2,1)S(1)} %get-tuple-element.111), channel_id=1, source_target_pairs={{0,8},{1,9},{2,10},{3,11},{4,12},{5,13},{6,14},{7,15},{8,0},{9,1},... | collective-permute-start | bytes 196616 | tf_op jit(solution)/shard_map/ppermute | solution.py:33
  121.3 6.1 %collective-permute-start.35 = (bf16[16,2048]{1,0:T(8,128)(2,1)S(1)}, bf16[16,2048]{1,0:T(8,128)(2,1)S(1)}, u32[]{:S(2)}, u32[]{:S(2)}) collective-permute-start(bf16[16,2048]{1,0:T(8,128)(2,1)S(1)} %get-tuple-element.110), channel_id=1, source_target_pairs={{0,12},{1,13},{2,14},{3,15},{4,8},{5,9},{6,10},{7,11},{8,4},{9,5},... | collective-permute-start | bytes 196616 | tf_op jit(solution)/shard_map/ppermute | solution.py:33
  (10 other events, 148.9 us)

commit v9 on v8

--- a/solution.py
+++ b/solution.py
@@ -12,6 +12,7 @@
 GRANT = 16 << 20
 EXPERT_GRANT = 32 << 20
 WHOLE_GRANT = 60 << 20
+LITTLE = pl.CostEstimate(flops=1, bytes_accessed=1, transcendentals=0)
 
 
 def route_gates(logits):
@@ -95,6 +96,7 @@
         ],
         scratch_shapes=[pltpu.VMEM((padded, -(-steps * rows // LANES) * LANES), jnp.float32)],
         compiler_params=pltpu.CompilerParams(vmem_limit_bytes=WHOLE_GRANT),
+        cost_estimate=LITTLE,
         name="payload",
     )(hidden, jnp.swapaxes(route_ids, 1, 2), jnp.swapaxes(route_logits, 1, 2))
 
@@ -144,6 +146,7 @@
         ],
         scratch_shapes=[pltpu.VMEM((slots * length, LANES), jnp.float32)],
         compiler_params=pltpu.CompilerParams(vmem_limit_bytes=WHOLE_GRANT),
+        cost_estimate=LITTLE,
         name="order_factors",
     )(place, placement, factors)
 
@@ -213,6 +216,7 @@
             pltpu.VMEM((width, LANES), jnp.float32),
         ],
         compiler_params=pltpu.CompilerParams(vmem_limit_bytes=GRANT),
+        cost_estimate=LITTLE,
         name="relayout_factors",
     )(place, *here, *there)
 
@@ -251,7 +255,7 @@
     x_in = sum(x_in, [])
     gate_in = loads.begin_rows(w_gate_hbm, w_gate_ref)
     up_in = loads.begin_rows(w_up_hbm, w_up_ref)
-    wait(x_in)
+    wait(x_in + gate_in + up_in)
 
     def store(i):
         here = pl.ds(pl.multiple_of(i * block, block), block)
@@ -262,9 +266,7 @@
 
     def run_block(i, carry):
         here = pl.ds(pl.multiple_of(i * block, block), block)
-        pl.when(i == 0)(lambda: wait(gate_in))
         gate_ref[here, :] = dot(x_ref[here, :width], w_gate_ref[...])
-        pl.when(i == 0)(lambda: wait(up_in))
         up_ref[here, :] = dot(x_ref[here, :width], w_up_ref[...])
         for copy in store(i):
             copy.start()
@@ -295,11 +297,7 @@
             pltpu.SemaphoreType.DMA((2, total // min(128, total))),
         ],
         compiler_params=pltpu.CompilerParams(vmem_limit_bytes=EXPERT_GRANT),
-        cost_estimate=pl.CostEstimate(
-            flops=4 * total * width * units,
-            bytes_accessed=4 * width * units + 2 * total * width + 8 * total * units,
-            transcendentals=0,
-        ),
+        cost_estimate=LITTLE,
         name="base_products",
     )(*pieces, w_gate, w_up)
 
@@ -309,7 +307,7 @@
     gate_hbm, up_hbm, a_gu_hbm, gate_b_hbm, up_b_hbm, down_a_hbm, down_b_hbm = refs[:7]
     w_down_hbm, kept_hbm, sent_hbm, x_ref, gate_ref, up_ref = refs[7:13]
     a_gu_ref, gate_b_ref, up_b_ref, down_a_ref, down_b_ref, w_down_ref = refs[13:19]
-    kept_ref, sent_ref, sem, out_sem = refs[19:]
+    inner_ref, mine_ref, kept_ref, sent_ref, sem, out_sem = refs[19:]
     span = pieces[0].shape[0]
     units, width = w_down_ref.shape
     rank = gate_b_ref.shape[0]
@@ -327,21 +325,28 @@
         base_in += loads.begin(up_hbm.at[src], up_ref.at[dst])
     down_in = loads.begin(down_a_hbm, down_a_ref) + loads.begin(down_b_hbm, down_b_ref)
     down_in += loads.begin_rows(w_down_hbm, w_down_ref)
-    wait(x_in)
-
-    def run_block(i, carry):
+    wait(x_in + base_in)
+
+    def run_inner(i, carry):
         here = pl.ds(pl.multiple_of(i * block, block), block)
         gates = x_ref[here, width:].astype(jnp.float32)
         lane = lax.broadcasted_iota(jnp.int32, gates.shape, 1)
         mine = jnp.sum(jnp.where(lane == place_ref[1], gates, 0.0), axis=1, keepdims=True)
         low = (adapter_scale * dot(x_ref[here, :width], a_gu_ref[...])).astype(jnp.bfloat16)
-        pl.when(i == 0)(lambda: wait(base_in))
         g = gate_ref[here, :] + dot(low[:, :rank], gate_b_ref[...])
         u = up_ref[here, :] + dot(low[:, rank:], up_b_ref[...])
-        inner = (g / (1.0 + jnp.exp(-g)) * u).astype(jnp.bfloat16)
-        pl.when(i == 0)(lambda: wait(down_in))
+        inner_ref[here, :] = (g / (1.0 + jnp.exp(-g)) * u).astype(jnp.bfloat16)
+        mine_ref[here, :] = jnp.broadcast_to(mine, (block, LANES))
+        return carry
+
+    def run_down(i, carry):
+        here = pl.ds(pl.multiple_of(i * block, block), block)
+        inner, mine = inner_ref[here, :], mine_ref[here, :1]
         low = (adapter_scale * dot(inner, down_a_ref[...])).astype(jnp.bfloat16)[:, :rank]
-        out = (dot(inner, w_down_ref[...]) + dot(low, down_b_ref[...])) * mine
+        half = width // 2
+        left = dot(inner, w_down_ref[:, :half]) + dot(low, down_b_ref[:, :half])
+        right = dot(inner, w_down_ref[:, half:]) + dot(low, down_b_ref[:, half:])
+        out = jnp.concatenate([left * mine, right * mine], axis=1)
 
         @pl.when(i < own // block)
         def _():
@@ -356,7 +361,9 @@
 
         return carry
 
-    lax.fori_loop(0, 2 * own // block, run_block, 0)
+    lax.fori_loop(0, 2 * own // block, run_inner, 0)
+    wait(down_in)
+    lax.fori_loop(0, 2 * own // block, run_down, 0)
     for i in range(2 * own // block):
         src, dst = (kept_ref, kept_hbm) if i < own // block else (sent_ref, sent_hbm)
         at = pl.ds(i % (own // block) * block, block)
@@ -387,17 +394,14 @@
             pltpu.VMEM((total, units), jnp.float32),
         ]
         + [pltpu.VMEM(a.shape, a.dtype) for a in held]
+        + [pltpu.VMEM((total, units), jnp.bfloat16), pltpu.VMEM((total, LANES), jnp.float32)]
         + [pltpu.VMEM(o.shape, o.dtype) for o in outs]
         + [
             pltpu.SemaphoreType.DMA((3 * len(pieces) + 9,)),
             pltpu.SemaphoreType.DMA((2 * own // min(128, own),)),
         ],
         compiler_params=pltpu.CompilerParams(vmem_limit_bytes=EXPERT_GRANT),
-        cost_estimate=pl.CostEstimate(
-            flops=2 * total * units * (width + 4 * rank) + 8 * total * width * rank,
-            bytes_accessed=2 * units * width + 5 * total * width + 8 * total * units,
-            transcendentals=total * units,
-        ),
+        cost_estimate=LITTLE,
         name="finish_step",
     )(place, *pieces, *base, *held)
 
@@ -421,8 +425,7 @@
         column = jnp.stack([p.reshape(count, rows, -1) for p in pieces], axis=1)
         return column.reshape(count * outer * rows, -1)
 
-    def across(column):
-        sheet = along(column, *along_middle)
+    def to_other_core(sheet):
         return sheet + [swap(p, owners, 1, 1) for p in sheet]
 
     first = max(1, steps * 2 // 3)
@@ -433,9 +436,11 @@
     blocks = [blocks[0]] + [swap(blocks[r], owners, cores, r) for r in range(1, middle)]
     head, blocks = lax.optimization_barrier((head, blocks))
     here, there = exchange_factors(blocks, owners)
-    heads = across(head)
-    tail, here[1], heads[1] = lax.optimization_barrier((tail, here[1], heads[1]))
-    tails = across(by_step(along(tail, *along_outer), steps - first))
+    heads = along(head, *along_middle)
+    tail, here, heads[1:] = lax.optimization_barrier((tail, here, heads[1:]))
+    heads = to_other_core(heads)
+    tails = by_step(along(tail, *along_outer), steps - first)
+    tails = to_other_core(along(tails, *along_middle))
     head_base = base_products(heads, w_gate[0], w_up[0])
     here, there, head_base = lax.optimization_barrier((here, there, head_base))
     low_rank = relayout_factors(place, here, there, width, units, rank, owners)

time: 128 us -> 118 us (0.922)
  waiting for transfers between devices: 36.5 us -> 28.9 us
  Pallas kernels: 40 us -> 37 us
    ppermute x28, waiting for transfers between devices: 28.3 us -> 17.5 us  [swap(): return lax.ppermute(x, 'expert', [(i, i ^ k * stride) for i in range(n)])]
    ppermute x4, starting transfers between devices: 5.07 us -> 8.48 us  [exchange_factors(): there.append(lax.ppermute(part, 'group', [(0, 1), (1, 0)]))]
    ppermute x4, waiting for transfers between devices: 0.01 us -> 3.27 us  [exchange_factors(): there.append(lax.ppermute(part, 'group', [(0, 1), (1, 0)]))]
    pallas_call x2, Pallas kernels: 12.5 us -> 9.84 us  [base_products(): pl.pallas_call(functools.partial(base_kernel, len(pieces)), out_shape=[ou...]
    ppermute x4, starting transfers between devices: 7.71 us -> 5.25 us  [exchange_factors(): part = lax.ppermute(part, ('group', 'expert'), pairs)]
  transfers between devices with their start and end apart: 36 -> 36, of which waited for: 10 -> 11; matrix products, arithmetic and copies ran while one was open for 3% -> 3% of each run, Pallas kernels for 30% -> 30%
where the time goes in v9:
time: 118 us; the launch traced here: 117 us
  starting transfers between devices  44.9 us (38%)
  Pallas kernels  37 us (31%)
  waiting for transfers between devices  28.9 us (24%)
  other arithmetic  3.14 us (3%)
  local copies, waits for them, and re-layouts  3.06 us (3%)
    ppermute x28, starting transfers between devices, swap(): return lax.ppermute(x, 'expert', [(i, i ^ k * stride) for i in range(n)])  31.2 us
    pallas_call x3, Pallas kernels, finish_step(): pl.pallas_call(functools.partial(finish_kernel, len(pieces), first, rows)...  20.2 us
    ppermute x28, waiting for transfers between devices, swap(): return lax.ppermute(x, 'expert', [(i, i ^ k * stride) for i in range(n)])  17.5 us
    pallas_call x2, Pallas kernels, base_products(): pl.pallas_call(functools.partial(base_kernel, len(pieces)), out_shape=[ou...  9.84 us
    ppermute x4, starting transfers between devices, exchange_factors(): there.append(lax.ppermute(part, 'group', [(0, 1), (1, 0)]))  8.48 us
    ppermute x4, waiting for transfers between devices, exchange_factors(): part = lax.ppermute(part, ('group', 'expert'), pairs)  8.1 us
    ppermute x4, starting transfers between devices, exchange_factors(): part = lax.ppermute(part, ('group', 'expert'), pairs)  5.25 us
    ppermute x4, waiting for transfers between devices, exchange_factors(): there.append(lax.ppermute(part, 'group', [(0, 1), (1, 0)]))  3.27 us
  transfers between devices with their start and end apart: 36, of which 11 were waited for; matrix products, arithmetic and copies ran while one was open for 3% of the time, Pallas kernels for 30%

profile of v9, /device:TPU:0, one launch (start us, length us, event | category | flops | bytes accessed | tf_op | source)
XLA Modules:
  0.0 117.4 jit_solution(14964812181821540160)
XLA Ops:
  0.0 2.1 %payload.1 = (bf16[32,2176]{1,0:T(8,128)(2,1)}, bf16[16,2176]{1,0:T(8,128)(2,1)}) custom-call(bf16[3,16,2048]{2,1,0:T(8,128)(2,1)} %hidden_ref.1, s32[3,8,16]{2,1,0:T(8,128)} %bitcast.54, f32[3,8,16]{2,1,0:T(8,128)} %bitcast.55), custom_call_target="tpu_custom_call" | custom-call | flops 1 | bytes 1 | tf_op jit(solution)/shard_map/payload/pallas_call | solution.py:91
  2.1 3.0 %collective-permute-start = (bf16[32,2176]{1,0:T(8,128)(2,1)}, bf16[32,2176]{1,0:T(8,128)(2,1)S(1)}, u32[]{:S(2)}, u32[]{:S(2)}) collective-permute-start(bf16[32,2176]{1,0:T(8,128)(2,1)} %get-tuple-element.52), channel_id=1, source_target_pairs={{0,4},{1,5},{2,6},{3,7},{4,0},{5,1},{6,2},{7,3},{8,12},{9,13},{10,... | collective-permute-start | bytes 417800 | tf_op jit(solution)/shard_map/ppermute | solution.py:34
  5.1 2.6 %collective-permute-start.1 = (bf16[32,2176]{1,0:T(8,128)(2,1)}, bf16[32,2176]{1,0:T(8,128)(2,1)S(1)}, u32[]{:S(2)}, u32[]{:S(2)}) collective-permute-start(bf16[32,2176]{1,0:T(8,128)(2,1)} %get-tuple-element.52), channel_id=1, source_target_pairs={{0,8},{1,9},{2,10},{3,11},{4,12},{5,13},{6,14},{7,15},{8,0},{9,1},... | collective-permute-start | bytes 417800 | tf_op jit(solution)/shard_map/ppermute | solution.py:34
  8.4 3.2 %order_factors.1 = (bf16[4,264,128]{2,1,0:T(8,128)(2,1)}, bf16[4,264,128]{2,1,0:T(8,128)(2,1)}) custom-call(s32[2]{0:T(128)} %pad_add_fusion.place_ref, s32[16]{0:T(128)} %placement_ref.1, bf16[16,33792]{1,0:T(8,128)(2,1)} %factors_ref), custom_call_target="tpu_custom_call" | custom-call | flops 1 | bytes 1 | tf_op jit(solution)/shard_map/order_factors/pallas_call | solution.py:139
  11.6 1.7 %collective-permute-start.3 = (bf16[4,264,128]{2,1,0:T(8,128)(2,1)}, bf16[4,264,128]{2,1,0:T(8,128)(2,1)S(1)}, u32[]{:S(2)}, u32[]{:S(2)}) collective-permute-start(bf16[4,264,128]{2,1,0:T(8,128)(2,1)} %get-tuple-element.55), channel_id=1, source_target_pairs={{0,2},{1,3},{2,0},{3,1},{4,6},{5,7},{6,4},{7,5},{8,10},{9,11},{10,... | collective-permute-start | bytes 811016 | tf_op jit(solution)/shard_map/ppermute | solution.py:34
  13.3 5.5 %collective-permute-done.1 = bf16[32,2176]{1,0:T(8,128)(2,1)S(1)} collective-permute-done((bf16[32,2176]{1,0:T(8,128)(2,1)}, bf16[32,2176]{1,0:T(8,128)(2,1)S(1)}, u32[]{:S(2)}, u32[]{:S(2)}) %collective-permute-start.1) | collective-permute-done | bytes 139296 | tf_op jit(solution)/shard_map/ppermute | solution.py:34
  19.9 1.6 %collective-permute-start.8 = (bf16[128,2176]{1,0:T(8,128)(2,1)S(1)}, bf16[128,2176]{1,0:T(8,128)(2,1)S(1)}, u32[]{:S(2)}, u32[]{:S(2)}) collective-permute-start(bf16[128,2176]{1,0:T(8,128)(2,1)S(1)} %bitcast.38), channel_id=1, source_target_pairs={{0,2},{1,3},{2,0},{3,1},{4,6},{5,7},{6,4},{7,5},{8,10},{9,11},{10,... | collective-permute-start | bytes 1671176 | tf_op jit(solution)/shard_map/ppermute | solution.py:34
  22.5 3.1 %collective-permute-start.7 = (bf16[2,264,128]{2,1,0:T(8,128)(2,1)S(1)}, bf16[2,264,128]{2,1,0:T(8,128)(2,1)S(1)}, u32[]{:S(2)}, u32[]{:S(2)}) collective-permute-start(bf16[2,264,128]{2,1,0:T(8,128)(2,1)S(1)} %pad_maximum_fusion.6), channel_id=1, source_target_pairs={{0,12},{1,13},{2,14},{3,15},{4,8},{5,9},{6,10},{7,11},{8,4},{9,5},... | collective-permute-start | bytes 405512 | tf_op jit(solution)/shard_map/ppermute | solution.py:55
  27.8 3.1 %collective-permute-done.7.refs_3_ = bf16[2,264,128]{2,1,0:T(8,128)(2,1)S(1)} collective-permute-done((bf16[2,264,128]{2,1,0:T(8,128)(2,1)S(1)}, bf16[2,264,128]{2,1,0:T(8,128)(2,1)S(1)}, u32[]{:S(2)}, u32[]{:S(2)}) %collective-permute-start.7) | collective-permute-done | bytes 135200 | tf_op jit(solution)/shard_map/ppermute | solution.py:55
  30.9 5.0 %collective-permute-done.6.refs_2_ = bf16[2,264,128]{2,1,0:T(8,128)(2,1)S(1)} collective-permute-done((bf16[2,264,128]{2,1,0:T(8,128)(2,1)S(1)}, bf16[2,264,128]{2,1,0:T(8,128)(2,1)S(1)}, u32[]{:S(2)}, u32[]{:S(2)}) %collective-permute-start.6) | collective-permute-done | bytes 135200 | tf_op jit(solution)/shard_map/ppermute | solution.py:55
  36.0 4.5 %collective-permute-start.20 = (bf16[2,264,128]{2,1,0:T(8,128)(2,1)S(1)}, bf16[2,264,128]{2,1,0:T(8,128)(2,1)S(1)}, u32[]{:S(2)}, u32[]{:S(2)}) collective-permute-start(bf16[2,264,128]{2,1,0:T(8,128)(2,1)S(1)} %collective-permute-done.7.refs_3_), channel_id=1, source_target_pairs={{0,16},{16,0},{1,17},{17,1},{2,18},{18,2},{3,19},{19,3},{4,20},{20... | collective-permute-start | bytes 405512 | tf_op jit(solution)/shard_map/ppermute | solution.py:57
  40.5 2.0 %collective-permute-start.18 = (bf16[2,264,128]{2,1,0:T(8,128)(2,1)S(1)}, bf16[2,264,128]{2,1,0:T(8,128)(2,1)S(1)}, u32[]{:S(2)}, u32[]{:S(2)}) collective-permute-start(bf16[2,264,128]{2,1,0:T(8,128)(2,1)S(1)} %collective-permute-done.5.refs_1_), channel_id=1, source_target_pairs={{0,16},{16,0},{1,17},{17,1},{2,18},{18,2},{3,19},{19,3},{4,20},{20... | collective-permute-start | bytes 405512 | tf_op jit(solution)/shard_map/ppermute | solution.py:57
  42.5 2.4 %collective-permute-done.20.refs_7_ = bf16[2,264,128]{2,1,0:T(8,128)(2,1)S(1)} collective-permute-done((bf16[2,264,128]{2,1,0:T(8,128)(2,1)S(1)}, bf16[2,264,128]{2,1,0:T(8,128)(2,1)S(1)}, u32[]{:S(2)}, u32[]{:S(2)}) %collective-permute-start.20) | collective-permute-done | bytes 135200 | tf_op jit(solution)/shard_map/ppermute | solution.py:57
  44.9 2.0 %collective-permute-start.17 = (bf16[2,264,128]{2,1,0:T(8,128)(2,1)S(1)}, bf16[2,264,128]{2,1,0:T(8,128)(2,1)S(1)}, u32[]{:S(2)}, u32[]{:S(2)}) collective-permute-start(bf16[2,264,128]{2,1,0:T(8,128)(2,1)S(1)} %collective-permute-done.4.refs_0_), channel_id=1, source_target_pairs={{0,16},{16,0},{1,17},{17,1},{2,18},{18,2},{3,19},{19,3},{4,20},{20... | collective-permute-start | bytes 405512 | tf_op jit(solution)/shard_map/ppermute | solution.py:57
  47.8 1.7 %collective-permute-start.10 = (bf16[16,2176]{1,0:T(8,128)(2,1)S(1)}, bf16[16,2176]{1,0:T(8,128)(2,1)S(1)}, u32[]{:S(2)}, u32[]{:S(2)}) collective-permute-start(bf16[16,2176]{1,0:T(8,128)(2,1)S(1)} %copy-done.5), channel_id=1, source_target_pairs={{0,8},{1,9},{2,10},{3,11},{4,12},{5,13},{6,14},{7,15},{8,0},{9,1},... | collective-permute-start | bytes 208904 | tf_op jit(solution)/shard_map/ppermute | solution.py:34
  49.5 2.6 %collective-permute-start.11 = (bf16[16,2176]{1,0:T(8,128)(2,1)S(1)}, bf16[16,2176]{1,0:T(8,128)(2,1)S(1)}, u32[]{:S(2)}, u32[]{:S(2)}) collective-permute-start(bf16[16,2176]{1,0:T(8,128)(2,1)S(1)} %copy-done.5), channel_id=1, source_target_pairs={{0,12},{1,13},{2,14},{3,15},{4,8},{5,9},{6,10},{7,11},{8,4},{9,5},... | collective-permute-start | bytes 208904 | tf_op jit(solution)/shard_map/ppermute | solution.py:34
  52.2 1.9 %copy-done.2 = bf16[1,2048,768]{2,1,0:T(8,128)(2,1)S(1)} copy-done((bf16[1,2048,768]{2,1,0:T(8,128)(2,1)S(1)}, bf16[1,2048,768]{2,1,0:T(8,128)(2,1)}, u32[]{:S(2)}) %copy-start.2) | copy-done | bytes 3145752
  54.1 6.4 %base_products.2 = (f32[512,768]{1,0:T(8,128)S(1)}, f32[512,768]{1,0:T(8,128)S(1)}) custom-call(bf16[128,2176]{1,0:T(8,128)(2,1)S(1)} %bitcast.40, bf16[128,2176]{1,0:T(8,128)(2,1)S(1)} %collective-permute-done.8.refs_1_, bf16[128,2176]{1,0:T(8,128)(2,1)S(1)} %collective-permute-done.15.refs_2_, bf16[128,2176]{1,0:T(8,128)(2,1)S(1)} %collective-permute-done.16.refs_3_, ...), custom_call_target="tpu_custom_call" | custom-call | flops 1 | bytes 1 | tf_op jit(solution)/shard_map/base_products/pallas_call | solution.py:284
  60.5 1.6 %relayout_factors.1 = (bf16[2048,128]{1,0:T(8,128)(2,1)S(1)}, bf16[64,768]{1,0:T(8,128)(2,1)S(1)}, bf16[64,768]{1,0:T(8,128)(2,1)S(1)}, bf16[768,128]{1,0:T(8,128)(2,1)S(1)}, bf16[64,2048]{1,0:T(8,128)(2,1)S(1)}) custom-call(s32[2]{0:T(128)S(1)} %copy-done.4, bf16[2,264,128]{2,1,0:T(8,128)(2,1)S(1)} %collective-permute-done.4.refs_0_, ...), custom_call_target="tpu_custom_call" | custom-call | flops 1 | bytes 1 | tf_op jit(solution)/shard_map/relayout_factors/pallas_call | solution.py:209
  62.1 6.7 %finish_step.3 = (f32[128,2048]{1,0:T(8,128)S(1)}, bf16[128,2048]{1,0:T(8,128)(2,1)S(1)}) custom-call(s32[2]{0:T(128)S(1)} %copy-done.4, bf16[128,2176]{1,0:T(8,128)(2,1)S(1)} %bitcast.41, bf16[128,2176]{1,0:T(8,128)(2,1)S(1)} %collective-permute-done.8.refs_1_, bf16[128,2176]{1,0:T(8,128)(2,1)S(1)} %collective-permute-done.15.refs_2_, ...), custom_call_target="tpu_custom_call" | custom-call | flops 1 | bytes 1 | tf_op jit(solution)/shard_map/finish_step/pallas_call | solution.py:384
  69.6 6.7 %finish_step.4 = (f32[128,2048]{1,0:T(8,128)S(1)}, bf16[128,2048]{1,0:T(8,128)(2,1)S(1)}) custom-call(s32[2]{0:T(128)S(1)} %copy-done.4, bf16[128,2176]{1,0:T(8,128)(2,1)S(1)} %bitcast.42, bf16[128,2176]{1,0:T(8,128)(2,1)S(1)} %collective-permute-done.8.refs_1_, bf16[128,2176]{1,0:T(8,128)(2,1)S(1)} %collective-permute-done.15.refs_2_, ...), custom_call_target="tpu_custom_call" | custom-call | flops 1 | bytes 1 | tf_op jit(solution)/shard_map/finish_step/pallas_call | solution.py:384
  82.0 3.5 %base_products.3 = (f32[256,768]{1,0:T(8,128)S(1)}, f32[256,768]{1,0:T(8,128)S(1)}) custom-call(bf16[64,2176]{1,0:T(8,128)(2,1)S(1)} %bitcast.45, bf16[64,2176]{1,0:T(8,128)(2,1)S(1)} %collective-permute-done.12.refs_1_, bf16[64,2176]{1,0:T(8,128)(2,1)S(1)} %collective-permute-done.13.refs_2_, bf16[64,2176]{1,0:T(8,128)(2,1)S(1)} %collective-permute-done.14.refs_3_, ...), custom_call_target="tpu_custom_call" | custom-call | flops 1 | bytes 1 | tf_op jit(solution)/shard_map/base_products/pallas_call | solution.py:284
  85.5 6.7 %finish_step.5 = (f32[128,2048]{1,0:T(8,128)S(1)}, bf16[128,2048]{1,0:T(8,128)(2,1)S(1)}) custom-call(s32[2]{0:T(128)S(1)} %copy-done.4, bf16[64,2176]{1,0:T(8,128)(2,1)S(1)} %bitcast.46, bf16[64,2176]{1,0:T(8,128)(2,1)S(1)} %collective-permute-done.12.refs_1_, bf16[64,2176]{1,0:T(8,128)(2,1)S(1)} %collective-permute-done.13.refs_2_, ...), custom_call_target="tpu_custom_call" | custom-call | flops 1 | bytes 1 | tf_op jit(solution)/shard_map/finish_step/pallas_call | solution.py:384
  92.5 1.7 %collective-permute-start.24 = (bf16[16,2048]{1,0:T(8,128)(2,1)S(1)}, bf16[16,2048]{1,0:T(8,128)(2,1)S(1)}, u32[]{:S(2)}, u32[]{:S(2)}) collective-permute-start(bf16[16,2048]{1,0:T(8,128)(2,1)S(1)} %get-tuple-element.111), channel_id=1, source_target_pairs={{0,8},{1,9},{2,10},{3,11},{4,12},{5,13},{6,14},{7,15},{8,0},{9,1},... | collective-permute-start | bytes 196616 | tf_op jit(solution)/shard_map/ppermute | solution.py:34
  94.2 2.6 %collective-permute-start.25 = (bf16[16,2048]{1,0:T(8,128)(2,1)S(1)}, bf16[16,2048]{1,0:T(8,128)(2,1)S(1)}, u32[]{:S(2)}, u32[]{:S(2)}) collective-permute-start(bf16[16,2048]{1,0:T(8,128)(2,1)S(1)} %get-tuple-element.110), channel_id=1, source_target_pairs={{0,12},{1,13},{2,14},{3,15},{4,8},{5,9},{6,10},{7,11},{8,4},{9,5},... | collective-permute-start | bytes 196616 | tf_op jit(solution)/shard_map/ppermute | solution.py:34
  97.1 1.7 %collective-permute-start.29 = (bf16[16,2048]{1,0:T(8,128)(2,1)S(1)}, bf16[16,2048]{1,0:T(8,128)(2,1)S(1)}, u32[]{:S(2)}, u32[]{:S(2)}) collective-permute-start(bf16[16,2048]{1,0:T(8,128)(2,1)S(1)} %get-tuple-element.114), channel_id=1, source_target_pairs={{0,8},{1,9},{2,10},{3,11},{4,12},{5,13},{6,14},{7,15},{8,0},{9,1},... | collective-permute-start | bytes 196616 | tf_op jit(solution)/shard_map/ppermute | solution.py:34
  99.0 2.7 %collective-permute-start.30 = (bf16[16,2048]{1,0:T(8,128)(2,1)S(1)}, bf16[16,2048]{1,0:T(8,128)(2,1)S(1)}, u32[]{:S(2)}, u32[]{:S(2)}) collective-permute-start(bf16[16,2048]{1,0:T(8,128)(2,1)S(1)} %get-tuple-element.113), channel_id=1, source_target_pairs={{0,12},{1,13},{2,14},{3,15},{4,8},{5,9},{6,10},{7,11},{8,4},{9,5},... | collective-permute-start | bytes 196616 | tf_op jit(solution)/shard_map/ppermute | solution.py:34
  102.7 6.0 %collective-permute-done.32 = bf16[64,2048]{1,0:T(8,128)(2,1)S(1)} collective-permute-done((bf16[64,2048]{1,0:T(8,128)(2,1)S(1)}, bf16[64,2048]{1,0:T(8,128)(2,1)S(1)}, u32[]{:S(2)}, u32[]{:S(2)}) %collective-permute-start.32) | collective-permute-done | bytes 262176 | tf_op jit(solution)/shard_map/ppermute | solution.py:34
  108.9 1.7 %collective-permute-start.34 = (bf16[16,2048]{1,0:T(8,128)(2,1)S(1)}, bf16[16,2048]{1,0:T(8,128)(2,1)S(1)}, u32[]{:S(2)}, u32[]{:S(2)}) collective-permute-start(bf16[16,2048]{1,0:T(8,128)(2,1)S(1)} %get-tuple-element.117), channel_id=1, source_target_pairs={{0,8},{1,9},{2,10},{3,11},{4,12},{5,13},{6,14},{7,15},{8,0},{9,1},... | collective-permute-start | bytes 196616 | tf_op jit(solution)/shard_map/ppermute | solution.py:34
  110.6 2.6 %collective-permute-start.35 = (bf16[16,2048]{1,0:T(8,128)(2,1)S(1)}, bf16[16,2048]{1,0:T(8,128)(2,1)S(1)}, u32[]{:S(2)}, u32[]{:S(2)}) collective-permute-start(bf16[16,2048]{1,0:T(8,128)(2,1)S(1)} %get-tuple-element.116), channel_id=1, source_target_pairs={{0,12},{1,13},{2,14},{3,15},{4,8},{5,9},{6,10},{7,11},{8,4},{9,5},... | collective-permute-start | bytes 196616 | tf_op jit(solution)/shard_map/ppermute | solution.py:34
  113.3 1.2 %collective-permute-done.33 = bf16[16,2048]{1,0:T(8,128)(2,1)S(1)} collective-permute-done((bf16[16,2048]{1,0:T(8,128)(2,1)S(1)}, bf16[16,2048]{1,0:T(8,128)(2,1)S(1)}, u32[]{:S(2)}, u32[]{:S(2)}) %collective-permute-start.33) | collective-permute-done | bytes 65568 | tf_op jit(solution)/shard_map/ppermute | solution.py:34
  114.5 2.1 %collective-permute-done.35 = bf16[16,2048]{1,0:T(8,128)(2,1)S(1)} collective-permute-done((bf16[16,2048]{1,0:T(8,128)(2,1)S(1)}, bf16[16,2048]{1,0:T(8,128)(2,1)S(1)}, u32[]{:S(2)}, u32[]{:S(2)}) %collective-permute-start.35) | collective-permute-done | bytes 65568 | tf_op jit(solution)/shard_map/ppermute | solution.py:34
  (84 shorter events, 14.8 us)
Async XLA Ops:
  2.1 11.2 %collective-permute-start = (bf16[32,2176]{1,0:T(8,128)(2,1)}, bf16[32,2176]{1,0:T(8,128)(2,1)S(1)}, u32[]{:S(2)}, u32[]{:S(2)}) collective-permute-start(bf16[32,2176]{1,0:T(8,128)(2,1)} %get-tuple-element.52), channel_id=1, source_target_pairs={{0,4},{1,5},{2,6},{3,7},{4,0},{5,1},{6,2},{7,3},{8,12},{9,13},{10,... | collective-permute-start | bytes 417800 | tf_op jit(solution)/shard_map/ppermute | solution.py:34
  5.1 13.7 %collective-permute-start.1 = (bf16[32,2176]{1,0:T(8,128)(2,1)}, bf16[32,2176]{1,0:T(8,128)(2,1)S(1)}, u32[]{:S(2)}, u32[]{:S(2)}) collective-permute-start(bf16[32,2176]{1,0:T(8,128)(2,1)} %get-tuple-element.52), channel_id=1, source_target_pairs={{0,8},{1,9},{2,10},{3,11},{4,12},{5,13},{6,14},{7,15},{8,0},{9,1},... | collective-permute-start | bytes 417800 | tf_op jit(solution)/shard_map/ppermute | solution.py:34
  7.7 11.1 %collective-permute-start.2 = (bf16[32,2176]{1,0:T(8,128)(2,1)}, bf16[32,2176]{1,0:T(8,128)(2,1)}, u32[]{:S(2)}, u32[]{:S(2)}) collective-permute-start(bf16[32,2176]{1,0:T(8,128)(2,1)} %get-tuple-element.52), channel_id=1, source_target_pairs={{0,12},{1,13},{2,14},{3,15},{4,8},{5,9},{6,10},{7,11},{8,4},{9,5},... | collective-permute-start | bytes 417800 | tf_op jit(solution)/shard_map/ppermute | solution.py:34
  11.6 8.3 %collective-permute-start.3 = (bf16[4,264,128]{2,1,0:T(8,128)(2,1)}, bf16[4,264,128]{2,1,0:T(8,128)(2,1)S(1)}, u32[]{:S(2)}, u32[]{:S(2)}) collective-permute-start(bf16[4,264,128]{2,1,0:T(8,128)(2,1)} %get-tuple-element.55), channel_id=1, source_target_pairs={{0,2},{1,3},{2,0},{3,1},{4,6},{5,7},{6,4},{7,5},{8,10},{9,11},{10,... | collective-permute-start | bytes 811016 | tf_op jit(solution)/shard_map/ppermute | solution.py:34
  19.9 16.1 %collective-permute-start.8 = (bf16[128,2176]{1,0:T(8,128)(2,1)S(1)}, bf16[128,2176]{1,0:T(8,128)(2,1)S(1)}, u32[]{:S(2)}, u32[]{:S(2)}) collective-permute-start(bf16[128,2176]{1,0:T(8,128)(2,1)S(1)} %bitcast.38), channel_id=1, source_target_pairs={{0,2},{1,3},{2,0},{3,1},{4,6},{5,7},{6,4},{7,5},{8,10},{9,11},{10,... | collective-permute-start | bytes 1671176 | tf_op jit(solution)/shard_map/ppermute | solution.py:34
  22.5 8.4 %collective-permute-start.7 = (bf16[2,264,128]{2,1,0:T(8,128)(2,1)S(1)}, bf16[2,264,128]{2,1,0:T(8,128)(2,1)S(1)}, u32[]{:S(2)}, u32[]{:S(2)}) collective-permute-start(bf16[2,264,128]{2,1,0:T(8,128)(2,1)S(1)} %pad_maximum_fusion.6), channel_id=1, source_target_pairs={{0,12},{1,13},{2,14},{3,15},{4,8},{5,9},{6,10},{7,11},{8,4},{9,5},... | collective-permute-start | bytes 405512 | tf_op jit(solution)/shard_map/ppermute | solution.py:55
  25.7 10.3 %collective-permute-start.6 = (bf16[2,264,128]{2,1,0:T(8,128)(2,1)S(1)}, bf16[2,264,128]{2,1,0:T(8,128)(2,1)S(1)}, u32[]{:S(2)}, u32[]{:S(2)}) collective-permute-start(bf16[2,264,128]{2,1,0:T(8,128)(2,1)S(1)} %pad_maximum_fusion.5), channel_id=1, source_target_pairs={{0,8},{1,9},{2,10},{3,11},{4,12},{5,13},{6,14},{7,15},{8,0},{9,1},... | collective-permute-start | bytes 405512 | tf_op jit(solution)/shard_map/ppermute | solution.py:55
  26.4 9.5 %collective-permute-start.5 = (bf16[2,264,128]{2,1,0:T(8,128)(2,1)S(1)}, bf16[2,264,128]{2,1,0:T(8,128)(2,1)S(1)}, u32[]{:S(2)}, u32[]{:S(2)}) collective-permute-start(bf16[2,264,128]{2,1,0:T(8,128)(2,1)S(1)} %pad_maximum_fusion.4), channel_id=1, source_target_pairs={{0,4},{1,5},{2,6},{3,7},{4,0},{5,1},{6,2},{7,3},{8,12},{9,13},{10,... | collective-permute-start | bytes 405512 | tf_op jit(solution)/shard_map/ppermute | solution.py:55
  27.2 8.8 %collective-permute-start.4 = (bf16[2,264,128]{2,1,0:T(8,128)(2,1)S(1)}, bf16[2,264,128]{2,1,0:T(8,128)(2,1)S(1)}, u32[]{:S(2)}, u32[]{:S(2)}) collective-permute-start(bf16[2,264,128]{2,1,0:T(8,128)(2,1)S(1)} %pad_maximum_fusion.3), channel_id=1, source_target_pairs={{0,0},{1,1},{2,2},{3,3},{4,4},{5,5},{6,6},{7,7},{8,8},{9,9},{10,10... | collective-permute-start | bytes 405512 | tf_op jit(solution)/shard_map/ppermute | solution.py:55
  30.9 16.9 %collective-permute-start.15 = (bf16[128,2176]{1,0:T(8,128)(2,1)S(1)}, bf16[128,2176]{1,0:T(8,128)(2,1)S(1)}, u32[]{:S(2)}, u32[]{:S(2)}) collective-permute-start(bf16[128,2176]{1,0:T(8,128)(2,1)S(1)} %bitcast.39), channel_id=1, source_target_pairs={{0,1},{1,0},{2,3},{3,2},{4,5},{5,4},{6,7},{7,6},{8,9},{9,8},{10,11... | collective-permute-start | bytes 1671176 | tf_op jit(solution)/shard_map/ppermute | solution.py:34
  36.0 13.6 %collective-permute-start.16 = (bf16[128,2176]{1,0:T(8,128)(2,1)S(1)}, bf16[128,2176]{1,0:T(8,128)(2,1)S(1)}, u32[]{:S(2)}, u32[]{:S(2)}) collective-permute-start(bf16[128,2176]{1,0:T(8,128)(2,1)S(1)} %collective-permute-done.8.refs_1_), channel_id=1, source_target_pairs={{0,1},{1,0},{2,3},{3,2},{4,5},{5,4},{6,7},{7,6},{8,9},{9,8},{10,11... | collective-permute-start | bytes 1671176 | tf_op jit(solution)/shard_map/ppermute | solution.py:34
  36.0 8.9 %collective-permute-start.20 = (bf16[2,264,128]{2,1,0:T(8,128)(2,1)S(1)}, bf16[2,264,128]{2,1,0:T(8,128)(2,1)S(1)}, u32[]{:S(2)}, u32[]{:S(2)}) collective-permute-start(bf16[2,264,128]{2,1,0:T(8,128)(2,1)S(1)} %collective-permute-done.7.refs_3_), channel_id=1, source_target_pairs={{0,16},{16,0},{1,17},{17,1},{2,18},{18,2},{3,19},{19,3},{4,20},{20... | collective-permute-start | bytes 405512 | tf_op jit(solution)/shard_map/ppermute | solution.py:57
  40.5 7.3 %collective-permute-start.19 = (bf16[2,264,128]{2,1,0:T(8,128)(2,1)S(1)}, bf16[2,264,128]{2,1,0:T(8,128)(2,1)S(1)}, u32[]{:S(2)}, u32[]{:S(2)}) collective-permute-start(bf16[2,264,128]{2,1,0:T(8,128)(2,1)S(1)} %collective-permute-done.6.refs_2_), channel_id=1, source_target_pairs={{0,16},{16,0},{1,17},{17,1},{2,18},{18,2},{3,19},{19,3},{4,20},{20... | collective-permute-start | bytes 405512 | tf_op jit(solution)/shard_map/ppermute | solution.py:57
  40.5 19.9 %collective-permute-start.18 = (bf16[2,264,128]{2,1,0:T(8,128)(2,1)S(1)}, bf16[2,264,128]{2,1,0:T(8,128)(2,1)S(1)}, u32[]{:S(2)}, u32[]{:S(2)}) collective-permute-start(bf16[2,264,128]{2,1,0:T(8,128)(2,1)S(1)} %collective-permute-done.5.refs_1_), channel_id=1, source_target_pairs={{0,16},{16,0},{1,17},{17,1},{2,18},{18,2},{3,19},{19,3},{4,20},{20... | collective-permute-start | bytes 405512 | tf_op jit(solution)/shard_map/ppermute | solution.py:57
  44.9 15.6 %collective-permute-start.17 = (bf16[2,264,128]{2,1,0:T(8,128)(2,1)S(1)}, bf16[2,264,128]{2,1,0:T(8,128)(2,1)S(1)}, u32[]{:S(2)}, u32[]{:S(2)}) collective-permute-start(bf16[2,264,128]{2,1,0:T(8,128)(2,1)S(1)} %collective-permute-done.4.refs_0_), channel_id=1, source_target_pairs={{0,16},{16,0},{1,17},{17,1},{2,18},{18,2},{3,19},{19,3},{4,20},{20... | collective-permute-start | bytes 405512 | tf_op jit(solution)/shard_map/ppermute | solution.py:57
  47.8 21.1 %collective-permute-start.9 = (bf16[16,2176]{1,0:T(8,128)(2,1)S(1)}, bf16[16,2176]{1,0:T(8,128)(2,1)S(1)}, u32[]{:S(2)}, u32[]{:S(2)}) collective-permute-start(bf16[16,2176]{1,0:T(8,128)(2,1)S(1)} %copy-done.5), channel_id=1, source_target_pairs={{0,4},{1,5},{2,6},{3,7},{4,0},{5,1},{6,2},{7,3},{8,12},{9,13},{10,... | collective-permute-start | bytes 208904 | tf_op jit(solution)/shard_map/ppermute | solution.py:34
  47.8 21.1 %collective-permute-start.10 = (bf16[16,2176]{1,0:T(8,128)(2,1)S(1)}, bf16[16,2176]{1,0:T(8,128)(2,1)S(1)}, u32[]{:S(2)}, u32[]{:S(2)}) collective-permute-start(bf16[16,2176]{1,0:T(8,128)(2,1)S(1)} %copy-done.5), channel_id=1, source_target_pairs={{0,8},{1,9},{2,10},{3,11},{4,12},{5,13},{6,14},{7,15},{8,0},{9,1},... | collective-permute-start | bytes 208904 | tf_op jit(solution)/shard_map/ppermute | solution.py:34
  49.5 19.4 %collective-permute-start.11 = (bf16[16,2176]{1,0:T(8,128)(2,1)S(1)}, bf16[16,2176]{1,0:T(8,128)(2,1)S(1)}, u32[]{:S(2)}, u32[]{:S(2)}) collective-permute-start(bf16[16,2176]{1,0:T(8,128)(2,1)S(1)} %copy-done.5), channel_id=1, source_target_pairs={{0,12},{1,13},{2,14},{3,15},{4,8},{5,9},{6,10},{7,11},{8,4},{9,5},... | collective-permute-start | bytes 208904 | tf_op jit(solution)/shard_map/ppermute | solution.py:34
  68.9 9.3 %collective-permute-start.21 = (bf16[128,2048]{1,0:T(8,128)(2,1)S(1)}, bf16[128,2048]{1,0:T(8,128)(2,1)S(1)}, u32[]{:S(2)}, u32[]{:S(2)}) collective-permute-start(bf16[128,2048]{1,0:T(8,128)(2,1)S(1)} %get-tuple-element.83), channel_id=1, source_target_pairs={{0,1},{1,0},{2,3},{3,2},{4,5},{5,4},{6,7},{7,6},{8,9},{9,8},{10,11... | collective-permute-start | bytes 1572872 | tf_op jit(solution)/shard_map/ppermute | solution.py:34
  69.0 9.1 %collective-permute-start.12 = (bf16[64,2176]{1,0:T(8,128)(2,1)S(1)}, bf16[64,2176]{1,0:T(8,128)(2,1)S(1)}, u32[]{:S(2)}, u32[]{:S(2)}) collective-permute-start(bf16[64,2176]{1,0:T(8,128)(2,1)S(1)} %bitcast.43), channel_id=1, source_target_pairs={{0,2},{1,3},{2,0},{3,1},{4,6},{5,7},{6,4},{7,5},{8,10},{9,11},{10,... | collective-permute-start | bytes 835592 | tf_op jit(solution)/shard_map/ppermute | solution.py:34
  79.7 12.6 %collective-permute-start.22 = (bf16[64,2048]{1,0:T(8,128)(2,1)S(1)}, bf16[64,2048]{1,0:T(8,128)(2,1)S(1)}, u32[]{:S(2)}, u32[]{:S(2)}) collective-permute-start(bf16[64,2048]{1,0:T(8,128)(2,1)S(1)} %slice.168), channel_id=1, source_target_pairs={{0,2},{1,3},{2,0},{3,1},{4,6},{5,7},{6,4},{7,5},{8,10},{9,11},{10,... | collective-permute-start | bytes 786440 | tf_op jit(solution)/shard_map/ppermute | solution.py:34
  80.9 16.0 %collective-permute-start.27 = (bf16[64,2048]{1,0:T(8,128)(2,1)S(1)}, bf16[64,2048]{1,0:T(8,128)(2,1)S(1)}, u32[]{:S(2)}, u32[]{:S(2)}) collective-permute-start(bf16[64,2048]{1,0:T(8,128)(2,1)S(1)} %slice.167), channel_id=1, source_target_pairs={{0,2},{1,3},{2,0},{3,1},{4,6},{5,7},{6,4},{7,5},{8,10},{9,11},{10,... | collective-permute-start | bytes 786440 | tf_op jit(solution)/shard_map/ppermute | solution.py:34
  92.4 6.5 %collective-permute-start.23 = (bf16[16,2048]{1,0:T(8,128)(2,1)S(1)}, bf16[16,2048]{1,0:T(8,128)(2,1)S(1)}, u32[]{:S(2)}, u32[]{:S(2)}) collective-permute-start(bf16[16,2048]{1,0:T(8,128)(2,1)S(1)} %get-tuple-element.109), channel_id=1, source_target_pairs={{0,4},{1,5},{2,6},{3,7},{4,0},{5,1},{6,2},{7,3},{8,12},{9,13},{10,... | collective-permute-start | bytes 196616 | tf_op jit(solution)/shard_map/ppermute | solution.py:34
  92.5 9.2 %collective-permute-start.24 = (bf16[16,2048]{1,0:T(8,128)(2,1)S(1)}, bf16[16,2048]{1,0:T(8,128)(2,1)S(1)}, u32[]{:S(2)}, u32[]{:S(2)}) collective-permute-start(bf16[16,2048]{1,0:T(8,128)(2,1)S(1)} %get-tuple-element.111), channel_id=1, source_target_pairs={{0,8},{1,9},{2,10},{3,11},{4,12},{5,13},{6,14},{7,15},{8,0},{9,1},... | collective-permute-start | bytes 196616 | tf_op jit(solution)/shard_map/ppermute | solution.py:34
  94.2 8.4 %collective-permute-start.25 = (bf16[16,2048]{1,0:T(8,128)(2,1)S(1)}, bf16[16,2048]{1,0:T(8,128)(2,1)S(1)}, u32[]{:S(2)}, u32[]{:S(2)}) collective-permute-start(bf16[16,2048]{1,0:T(8,128)(2,1)S(1)} %get-tuple-element.110), channel_id=1, source_target_pairs={{0,12},{1,13},{2,14},{3,15},{4,8},{5,9},{6,10},{7,11},{8,4},{9,5},... | collective-permute-start | bytes 196616 | tf_op jit(solution)/shard_map/ppermute | solution.py:34
  97.0 13.6 %collective-permute-start.28 = (bf16[16,2048]{1,0:T(8,128)(2,1)S(1)}, bf16[16,2048]{1,0:T(8,128)(2,1)S(1)}, u32[]{:S(2)}, u32[]{:S(2)}) collective-permute-start(bf16[16,2048]{1,0:T(8,128)(2,1)S(1)} %get-tuple-element.112), channel_id=1, source_target_pairs={{0,4},{1,5},{2,6},{3,7},{4,0},{5,1},{6,2},{7,3},{8,12},{9,13},{10,... | collective-permute-start | bytes 196616 | tf_op jit(solution)/shard_map/ppermute | solution.py:34
  97.1 16.2 %collective-permute-start.29 = (bf16[16,2048]{1,0:T(8,128)(2,1)S(1)}, bf16[16,2048]{1,0:T(8,128)(2,1)S(1)}, u32[]{:S(2)}, u32[]{:S(2)}) collective-permute-start(bf16[16,2048]{1,0:T(8,128)(2,1)S(1)} %get-tuple-element.114), channel_id=1, source_target_pairs={{0,8},{1,9},{2,10},{3,11},{4,12},{5,13},{6,14},{7,15},{8,0},{9,1},... | collective-permute-start | bytes 196616 | tf_op jit(solution)/shard_map/ppermute | solution.py:34
  99.0 14.3 %collective-permute-start.30 = (bf16[16,2048]{1,0:T(8,128)(2,1)S(1)}, bf16[16,2048]{1,0:T(8,128)(2,1)S(1)}, u32[]{:S(2)}, u32[]{:S(2)}) collective-permute-start(bf16[16,2048]{1,0:T(8,128)(2,1)S(1)} %get-tuple-element.113), channel_id=1, source_target_pairs={{0,12},{1,13},{2,14},{3,15},{4,8},{5,9},{6,10},{7,11},{8,4},{9,5},... | collective-permute-start | bytes 196616 | tf_op jit(solution)/shard_map/ppermute | solution.py:34
  101.7 7.0 %collective-permute-start.32 = (bf16[64,2048]{1,0:T(8,128)(2,1)S(1)}, bf16[64,2048]{1,0:T(8,128)(2,1)S(1)}, u32[]{:S(2)}, u32[]{:S(2)}) collective-permute-start(bf16[64,2048]{1,0:T(8,128)(2,1)S(1)} %slice.166), channel_id=1, source_target_pairs={{0,2},{1,3},{2,0},{3,1},{4,6},{5,7},{6,4},{7,5},{8,10},{9,11},{10,... | collective-permute-start | bytes 786440 | tf_op jit(solution)/shard_map/ppermute | solution.py:34
  108.8 5.7 %collective-permute-start.33 = (bf16[16,2048]{1,0:T(8,128)(2,1)S(1)}, bf16[16,2048]{1,0:T(8,128)(2,1)S(1)}, u32[]{:S(2)}, u32[]{:S(2)}) collective-permute-start(bf16[16,2048]{1,0:T(8,128)(2,1)S(1)} %get-tuple-element.115), channel_id=1, source_target_pairs={{0,4},{1,5},{2,6},{3,7},{4,0},{5,1},{6,2},{7,3},{8,12},{9,13},{10,... | collective-permute-start | bytes 196616 | tf_op jit(solution)/shard_map/ppermute | solution.py:34
  108.9 5.7 %collective-permute-start.34 = (bf16[16,2048]{1,0:T(8,128)(2,1)S(1)}, bf16[16,2048]{1,0:T(8,128)(2,1)S(1)}, u32[]{:S(2)}, u32[]{:S(2)}) collective-permute-start(bf16[16,2048]{1,0:T(8,128)(2,1)S(1)} %get-tuple-element.117), channel_id=1, source_target_pairs={{0,8},{1,9},{2,10},{3,11},{4,12},{5,13},{6,14},{7,15},{8,0},{9,1},... | collective-permute-start | bytes 196616 | tf_op jit(solution)/shard_map/ppermute | solution.py:34
  110.6 6.1 %collective-permute-start.35 = (bf16[16,2048]{1,0:T(8,128)(2,1)S(1)}, bf16[16,2048]{1,0:T(8,128)(2,1)S(1)}, u32[]{:S(2)}, u32[]{:S(2)}) collective-permute-start(bf16[16,2048]{1,0:T(8,128)(2,1)S(1)} %get-tuple-element.116), channel_id=1, source_target_pairs={{0,12},{1,13},{2,14},{3,15},{4,8},{5,9},{6,10},{7,11},{8,4},{9,5},... | collective-permute-start | bytes 196616 | tf_op jit(solution)/shard_map/ppermute | solution.py:34
  (10 other events, 130.9 us)

commit v10 on v9

--- a/solution.py
+++ b/solution.py
@@ -45,25 +45,22 @@
 
 def exchange_factors(blocks, n):
     outer, middle, cores = split_axis(n)
-    here, there = [], []
+    here = []
     for q in range(outer):
         pairs = []
         for g in range(2):
             for i in range(n):
                 pairs.append((g * n + i, g * n + (i ^ (q * middle * cores) ^ g)))
         part = jnp.stack([block[q] for block in blocks])
-        part = lax.ppermute(part, ("group", "expert"), pairs)
-        here.append(part)
-        there.append(lax.ppermute(part, "group", [(0, 1), (1, 0)]))
-    return here, there
+        here.append(lax.ppermute(part, ("group", "expert"), pairs))
+    return here
 
 
 def dot(a, b):
     return jnp.dot(a, b, preferred_element_type=jnp.float32)
 
 
-def payload_kernel(hidden_ref, ids_ref, logits_ref, *refs):
-    out_refs, turned_ref = refs[:-1], refs[-1]
+def payload_kernel(hidden_ref, ids_ref, logits_ref, out_ref, turned_ref):
     steps, top, rows = ids_ref.shape
     width = hidden_ref.shape[2]
     turned_ref[...] = jnp.zeros_like(turned_ref)
@@ -77,23 +74,17 @@
             dense += jnp.where(ids[k : k + 1, :] == expert, gates[k : k + 1, :], 0.0)
         turned_ref[:, s * rows : (s + 1) * rows] = dense
     dense = turned_ref[...].T.astype(jnp.bfloat16)
-    s = 0
-    for out_ref in out_refs:
-        for at in range(0, out_ref.shape[0], rows):
-            out_ref[at : at + rows, :width] = hidden_ref[s]
-            out_ref[at : at + rows, width:] = dense[s * rows : (s + 1) * rows, :]
-            s += 1
-
-
-def make_payload(hidden, route_ids, route_logits, experts, first):
+    for s in range(steps):
+        out_ref[s * rows : (s + 1) * rows, :width] = hidden_ref[s]
+    out_ref[:, width:] = dense[: steps * rows]
+
+
+def make_payload(hidden, route_ids, route_logits, experts):
     steps, rows, width = hidden.shape
     padded = -(-experts // LANES) * LANES
     return pl.pallas_call(
         payload_kernel,
-        out_shape=[
-            jax.ShapeDtypeStruct((count * rows, width + padded), jnp.bfloat16)
-            for count in (first, steps - first)
-        ],
+        out_shape=jax.ShapeDtypeStruct((steps * rows, width + padded), jnp.bfloat16),
         scratch_shapes=[pltpu.VMEM((padded, -(-steps * rows // LANES) * LANES), jnp.float32)],
         compiler_params=pltpu.CompilerParams(vmem_limit_bytes=WHOLE_GRANT),
         cost_estimate=LITTLE,
@@ -152,19 +143,18 @@
 
 
 def relayout_kernel(outer, middle, place_ref, *refs):
-    pieces = refs[: 2 * outer]
-    a_gu_ref, gate_b_ref, up_b_ref, down_a_ref, down_b_ref, flat_ref, wide_ref = refs[2 * outer :]
+    a_gu_ref, gate_b_ref, up_b_ref, down_a_ref, down_b_ref, flat_ref, wide_ref = refs[2:]
     width, units = a_gu_ref.shape[0], gate_b_ref.shape[1]
     rank = gate_b_ref.shape[0]
-    length = pieces[0].shape[1]
+    length = refs[0].shape[2]
     group, me = place_ref[0], place_ref[1]
-    for i, piece in enumerate(pieces):
-        swapped, q = i // outer, i % outer
+    for swapped, part in enumerate(refs[:2]):
         core = group if swapped == 0 else 1 - group
-        for r in range(middle):
-            source = me ^ ((q * middle + r) * 2 + core)
-            start = pl.multiple_of(source * length, 8)
-            flat_ref[pl.ds(start, length), :] = piece[r].astype(jnp.float32)
+        for q in range(outer):
+            for r in range(middle):
+                source = me ^ ((q * middle + r) * 2 + core)
+                start = pl.multiple_of(source * length, 8)
+                flat_ref[pl.ds(start, length), :] = part[q, r].astype(jnp.float32)
 
     n_wide, n_unit = width // 2, units // 2
     at_ub = 2 * n_wide + n_unit
@@ -205,12 +195,12 @@
 def relayout_factors(place, here, there, width, units, rank, n):
     outer, middle, _ = split_axis(n)
     shapes = [(width, 2 * rank), (rank, units), (rank, units), (units, 2 * rank), (rank, width)]
-    length = here[0].shape[1]
+    length = here.shape[2]
     return pl.pallas_call(
         functools.partial(relayout_kernel, outer, middle),
         out_shape=[jax.ShapeDtypeStruct(shape, jnp.bfloat16) for shape in shapes],
         in_specs=[pl.BlockSpec(memory_space=pltpu.SMEM)]
-        + [pl.BlockSpec(memory_space=pltpu.VMEM)] * (2 * outer),
+        + [pl.BlockSpec(memory_space=pltpu.VMEM)] * 2,
         scratch_shapes=[
             pltpu.VMEM((n * length, LANES), jnp.float32),
             pltpu.VMEM((width, LANES), jnp.float32),
@@ -218,7 +208,7 @@
         compiler_params=pltpu.CompilerParams(vmem_limit_bytes=GRANT),
         cost_estimate=LITTLE,
         name="relayout_factors",
-    )(place, *here, *there)
+    )(place, here, there)
 
 
 class Loads:
@@ -307,7 +297,7 @@
     gate_hbm, up_hbm, a_gu_hbm, gate_b_hbm, up_b_hbm, down_a_hbm, down_b_hbm = refs[:7]
     w_down_hbm, kept_hbm, sent_hbm, x_ref, gate_ref, up_ref = refs[7:13]
     a_gu_ref, gate_b_ref, up_b_ref, down_a_ref, down_b_ref, w_down_ref = refs[13:19]
-    inner_ref, mine_ref, kept_ref, sent_ref, sem, out_sem = refs[19:]
+    inner_ref, kept_ref, sent_ref, sem, out_sem = refs[19:]
     span = pieces[0].shape[0]
     units, width = w_down_ref.shape
     rank = gate_b_ref.shape[0]
@@ -325,49 +315,36 @@
         base_in += loads.begin(up_hbm.at[src], up_ref.at[dst])
     down_in = loads.begin(down_a_hbm, down_a_ref) + loads.begin(down_b_hbm, down_b_ref)
     down_in += loads.begin_rows(w_down_hbm, w_down_ref)
-    wait(x_in + base_in)
-
-    def run_inner(i, carry):
-        here = pl.ds(pl.multiple_of(i * block, block), block)
-        gates = x_ref[here, width:].astype(jnp.float32)
+    cuts = [slice(at, at + block) for at in range(0, 2 * own, block)]
+    wait(x_in)
+    lows = []
+    for cut in cuts:
+        low = adapter_scale * dot(x_ref[cut, :width], a_gu_ref[...])
+        lows.append(low.astype(jnp.bfloat16))
+    wait(base_in)
+    for cut, low in zip(cuts, lows):
+        g = gate_ref[cut, :] + dot(low[:, :rank], gate_b_ref[...])
+        u = up_ref[cut, :] + dot(low[:, rank:], up_b_ref[...])
+        inner_ref[cut, :] = (g / (1.0 + jnp.exp(-g)) * u).astype(jnp.bfloat16)
+    wait(down_in)
+    lows = []
+    for cut in cuts:
+        low = adapter_scale * dot(inner_ref[cut, :], down_a_ref[...])
+        lows.append(low.astype(jnp.bfloat16)[:, :rank])
+    out_copies = []
+    for cut, low in zip(cuts, lows):
+        gates = x_ref[cut, width:].astype(jnp.float32)
         lane = lax.broadcasted_iota(jnp.int32, gates.shape, 1)
         mine = jnp.sum(jnp.where(lane == place_ref[1], gates, 0.0), axis=1, keepdims=True)
-        low = (adapter_scale * dot(x_ref[here, :width], a_gu_ref[...])).astype(jnp.bfloat16)
-        g = gate_ref[here, :] + dot(low[:, :rank], gate_b_ref[...])
-        u = up_ref[here, :] + dot(low[:, rank:], up_b_ref[...])
-        inner_ref[here, :] = (g / (1.0 + jnp.exp(-g)) * u).astype(jnp.bfloat16)
-        mine_ref[here, :] = jnp.broadcast_to(mine, (block, LANES))
-        return carry
-
-    def run_down(i, carry):
-        here = pl.ds(pl.multiple_of(i * block, block), block)
-        inner, mine = inner_ref[here, :], mine_ref[here, :1]
-        low = (adapter_scale * dot(inner, down_a_ref[...])).astype(jnp.bfloat16)[:, :rank]
-        half = width // 2
-        left = dot(inner, w_down_ref[:, :half]) + dot(low, down_b_ref[:, :half])
-        right = dot(inner, w_down_ref[:, half:]) + dot(low, down_b_ref[:, half:])
-        out = jnp.concatenate([left * mine, right * mine], axis=1)
-
-        @pl.when(i < own // block)
-        def _():
-            kept_ref[here, :] = out
-            pltpu.make_async_copy(kept_ref.at[here], kept_hbm.at[here], out_sem.at[i]).start()
-
-        @pl.when(i >= own // block)
-        def _():
-            there = pl.ds(pl.multiple_of(i * block - own, block), block)
-            sent_ref[there, :] = out.astype(jnp.bfloat16)
-            pltpu.make_async_copy(sent_ref.at[there], sent_hbm.at[there], out_sem.at[i]).start()
-
-        return carry
-
-    lax.fori_loop(0, 2 * own // block, run_inner, 0)
-    wait(down_in)
-    lax.fori_loop(0, 2 * own // block, run_down, 0)
-    for i in range(2 * own // block):
-        src, dst = (kept_ref, kept_hbm) if i < own // block else (sent_ref, sent_hbm)
-        at = pl.ds(i % (own // block) * block, block)
-        pltpu.make_async_copy(src.at[at], dst.at[at], out_sem.at[i]).wait()
+        out = (dot(inner_ref[cut, :], w_down_ref[...]) + dot(low, down_b_ref[...])) * mine
+        keep = cut.start < own
+        out_ref, out_hbm = (kept_ref, kept_hbm) if keep else (sent_ref, sent_hbm)
+        at = pl.ds(cut.start if keep else cut.start - own, block)
+        out_ref[at, :] = out.astype(out_ref.dtype)
+        sem_out = out_sem.at[len(out_copies)]
+        out_copies.append(pltpu.make_async_copy(out_ref.at[at], out_hbm.at[at], sem_out))
+        out_copies[-1].start()
+    wait(out_copies)
 
 
 def finish_step(place, pieces, base, first, rows, low_rank, w_down):
@@ -394,7 +371,7 @@
             pltpu.VMEM((total, units), jnp.float32),
         ]
         + [pltpu.VMEM(a.shape, a.dtype) for a in held]
-        + [pltpu.VMEM((total, units), jnp.bfloat16), pltpu.VMEM((total, LANES), jnp.float32)]
+        + [pltpu.VMEM((total, units), jnp.bfloat16)]
         + [pltpu.VMEM(o.shape, o.dtype) for o in outs]
         + [
             pltpu.SemaphoreType.DMA((3 * len(pieces) + 9,)),
@@ -421,42 +398,29 @@
     def along(x, stride, size):
         return [x] + [swap(x, owners, stride, k) for k in range(1, size)]
 
-    def by_step(pieces, count):
-        column = jnp.stack([p.reshape(count, rows, -1) for p in pieces], axis=1)
-        return column.reshape(count * outer * rows, -1)
-
-    def to_other_core(sheet):
-        return sheet + [swap(p, owners, 1, 1) for p in sheet]
-
-    first = max(1, steps * 2 // 3)
-    head, tail = make_payload(hidden, route_ids, route_logits, experts, first)
-    head, factors = lax.optimization_barrier((head, factors))
-    head = by_step(along(head, *along_outer), first)
+    rows_in = make_payload(hidden, route_ids, route_logits, experts)
+    rows_in, factors = lax.optimization_barrier((rows_in, factors))
+    column = [p.reshape(steps, rows, -1) for p in along(rows_in, *along_outer)]
+    column = jnp.stack(column, axis=1).reshape(steps * outer * rows, -1)
     blocks = order_factors(place, placement, factors, owners)
     blocks = [blocks[0]] + [swap(blocks[r], owners, cores, r) for r in range(1, middle)]
-    head, blocks = lax.optimization_barrier((head, blocks))
-    here, there = exchange_factors(blocks, owners)
-    heads = along(head, *along_middle)
-    tail, here, heads[1:] = lax.optimization_barrier((tail, here, heads[1:]))
-    heads = to_other_core(heads)
-    tails = by_step(along(tail, *along_outer), steps - first)
-    tails = to_other_core(along(tails, *along_middle))
-    head_base = base_products(heads, w_gate[0], w_up[0])
-    here, there, head_base = lax.optimization_barrier((here, there, head_base))
+    column, blocks = lax.optimization_barrier((column, blocks))
+    here = exchange_factors(blocks, owners)
+    sheet = along(column, *along_middle)
+    here, sheet[1:] = lax.optimization_barrier((here, sheet[1:]))
+    here = jnp.stack(here)
+    there = lax.ppermute(here, "group", [(0, 1), (1, 0)])
+    pieces = sheet + [swap(p, owners, 1, 1) for p in sheet]
+    base = base_products(pieces, w_gate[0], w_up[0])
+    here, there, base = lax.optimization_barrier((here, there, base))
     low_rank = relayout_factors(place, here, there, width, units, rank, owners)
 
     span = outer * rows
     results = []
     for s in range(steps):
-        at = s if s < first else s - first
-        pieces, base = (heads, head_base) if s < first else (tails, None)
-        if base is None:
-            pieces, summed = lax.optimization_barrier((pieces, results[0]))
-            results[0] = summed
-            base = base_products(pieces, w_gate[0], w_up[0])
-        kept, sent = finish_step(
-            place, pieces, base, at * span, span, low_rank, down_weight[0]
-        )
+        if s >= 2:
+            pieces, results[s - 2] = lax.optimization_barrier((pieces, results[s - 2]))
+        kept, sent = finish_step(place, pieces, base, s * span, span, low_rank, down_weight[0])
         results.append(kept + swap(sent, owners, 1, 1).astype(jnp.float32))
     results = [scatter_along(total, owners, *along_middle) for total in results]
     results = [scatter_along(total, owners, *along_outer) for total in results]
@@ -565,7 +529,7 @@
     outer = split_axis(owners)[0]
     dense = dense and outer > 1 and outer & (outer - 1) == 0 and split_axis(owners)[1] > 1
     dense = dense and 2 * rank == LANES and width % 256 == 0 and units % 256 == 0
-    dense = dense and factors.shape[1] % (8 * LANES) == 0 and hidden.shape[0] > 1
+    dense = dense and factors.shape[1] % (8 * LANES) == 0
     return (dense_shards if dense else sparse_shards)(
         hidden, route_ids, route_logits, placement, factors, w_gate, w_up, down_weight
     )

time: 118 us -> 111 us (0.941)
  starting transfers between devices: 44.9 us -> 32.3 us
  waiting for transfers between devices: 28.9 us -> 38.6 us
  Pallas kernels: 37 us -> 34.9 us
  local copies, waits for them, and re-layouts: 3.06 us -> 1.17 us
    ppermute x28 -> x22, waiting for transfers between devices: 17.5 us -> 27.4 us  [swap(): return lax.ppermute(x, 'expert', [(i, i ^ k * stride) for i in range(n)])]
    ppermute x8 -> x5, starting transfers between devices: 13.7 us -> 6.79 us  [the longest x4 5.24 us: exchange_factors(): here.append(lax.ppermute(part, ('group', 'expert'), pairs))]
    ppermute x28 -> x22, starting transfers between devices: 31.2 us -> 25.5 us  [swap(): return lax.ppermute(x, 'expert', [(i, i ^ k * stride) for i in range(n)])]
    unnamed x12 -> x8, local copies, waits for them, and re-layouts: 1.91 us -> 0.01 us
    pallas_call x3, Pallas kernels: 20.2 us -> 18.7 us  [finish_step(): pl.pallas_call(functools.partial(finish_kernel, len(pieces), first, rows)...]
    pallas_call x2 -> x1, Pallas kernels: 9.84 us -> 9.3 us  [base_products(): pl.pallas_call(functools.partial(base_kernel, len(pieces)), out_shape=[ou...]
    ppermute x8 -> x5, waiting for transfers between devices: 11.4 us -> 11.2 us  [the longest x4 8.09 us: exchange_factors(): here.append(lax.ppermute(part, ('group', 'expert'), pairs))]
  transfers between devices with their start and end apart: 36 -> 27, of which waited for: 11 -> 13; matrix products, arithmetic and copies ran while one was open for 3% -> 3% of each run, Pallas kernels for 30% -> 23%
where the time goes in v10:
time: 111 us
  waiting for transfers between devices  38.6 us (35%)
  Pallas kernels  34.9 us (31%)
  starting transfers between devices  32.3 us (29%)
  other arithmetic  3.28 us (3%)
  local copies, waits for them, and re-layouts  1.17 us (1%)
    ppermute x22, waiting for transfers between devices, swap(): return lax.ppermute(x, 'expert', [(i, i ^ k * stride) for i in range(n)])  27.4 us
    ppermute x22, starting transfers between devices, swap(): return lax.ppermute(x, 'expert', [(i, i ^ k * stride) for i in range(n)])  25.5 us
    pallas_call x3, Pallas kernels, finish_step(): pl.pallas_call(functools.partial(finish_kernel, len(pieces), first, rows)...  18.7 us
    pallas_call x1, Pallas kernels, base_products(): pl.pallas_call(functools.partial(base_kernel, len(pieces)), out_shape=[ou...  9.3 us
    ppermute x4, waiting for transfers between devices, exchange_factors(): here.append(lax.ppermute(part, ('group', 'expert'), pairs))  8.09 us
    ppermute x4, starting transfers between devices, exchange_factors(): here.append(lax.ppermute(part, ('group', 'expert'), pairs))  5.24 us
    pallas_call x1, Pallas kernels, order_factors(): pl.pallas_call(functools.partial(order_kernel, middle), out_shape=[jax.Sh...  3.2 us
    ppermute x1, waiting for transfers between devices, dense_shards(): there = lax.ppermute(here, 'group', [(0, 1), (1, 0)])  3.15 us
  transfers between devices with their start and end apart: 27, of which 13 were waited for; matrix products, arithmetic and copies ran while one was open for 3% of the time, Pallas kernels for 23%

profile of v10, /device:TPU:0, one launch (start us, length us, event | category | flops | bytes accessed | tf_op | source)
XLA Modules:
  0.0 110.5 jit_solution(13851559829151799285)
XLA Ops:
  0.0 2.1 %payload.1 = bf16[48,2176]{1,0:T(8,128)(2,1)} custom-call(bf16[3,16,2048]{2,1,0:T(8,128)(2,1)} %hidden_ref.1, s32[3,8,16]{2,1,0:T(8,128)} %bitcast.47, f32[3,8,16]{2,1,0:T(8,128)} %bitcast.48), custom_call_target="tpu_custom_call" | custom-call | flops 1 | bytes 1 | tf_op jit(solution)/shard_map/payload/pallas_call | solution.py:85
  2.1 5.0 %collective-permute-start.2 = (bf16[48,2176]{1,0:T(8,128)(2,1)}, bf16[48,2176]{1,0:T(8,128)(2,1)S(1)}, u32[]{:S(2)}, u32[]{:S(2)}) collective-permute-start(bf16[48,2176]{1,0:T(8,128)(2,1)} %payload.1), channel_id=1, source_target_pairs={{0,12},{1,13},{2,14},{3,15},{4,8},{5,9},{6,10},{7,11},{8,4},{9,5},... | collective-permute-start | bytes 626696 | tf_op jit(solution)/shard_map/ppermute | solution.py:34
  8.3 3.2 %order_factors.1 = (bf16[4,264,128]{2,1,0:T(8,128)(2,1)}, bf16[4,264,128]{2,1,0:T(8,128)(2,1)}) custom-call(s32[2]{0:T(128)} %pad_add_fusion.place_ref, s32[16]{0:T(128)} %placement_ref.1, bf16[16,33792]{1,0:T(8,128)(2,1)} %factors_ref), custom_call_target="tpu_custom_call" | custom-call | flops 1 | bytes 1 | tf_op jit(solution)/shard_map/order_factors/pallas_call | solution.py:130
  11.5 1.7 %collective-permute-start.3 = (bf16[4,264,128]{2,1,0:T(8,128)(2,1)}, bf16[4,264,128]{2,1,0:T(8,128)(2,1)S(1)}, u32[]{:S(2)}, u32[]{:S(2)}) collective-permute-start(bf16[4,264,128]{2,1,0:T(8,128)(2,1)} %get-tuple-element.42), channel_id=1, source_target_pairs={{0,2},{1,3},{2,0},{3,1},{4,6},{5,7},{6,4},{7,5},{8,10},{9,11},{10,... | collective-permute-start | bytes 811016 | tf_op jit(solution)/shard_map/ppermute | solution.py:34
  13.5 11.7 %collective-permute-done.1 = bf16[48,2176]{1,0:T(8,128)(2,1)} collective-permute-done((bf16[48,2176]{1,0:T(8,128)(2,1)}, bf16[48,2176]{1,0:T(8,128)(2,1)}, u32[]{:S(2)}, u32[]{:S(2)}) %collective-permute-start.1) | collective-permute-done | bytes 208928 | tf_op jit(solution)/shard_map/ppermute | solution.py:34
  25.3 1.3 %pad_maximum_fusion = bf16[3,4,16,2176]{3,2,1,0:T(8,128)(2,1)S(1)} fusion(bf16[3,1,16,2176]{3,2,1,0:T(8,128)(2,1)S(1)} %bitcast.42, bf16[3,1,16,2176]{3,2,1,0:T(8,128)(2,1)} %bitcast.7, bf16[3,1,16,2176]{3,2,1,0:T(8,128)(2,1)} %bitcast.5, bf16[3,1,16,2176]{3,2,1,0:T(8,128)(2,1)} %bitcast.41), kind=kLoop, calls=%fused_computation.3 | loop fusion | flops 1253376 | bytes 1671168 | tf_op jit(solution)/shard_map/stack | solution.py:404
  26.5 1.6 %collective-permute-start.8 = (bf16[192,2176]{1,0:T(8,128)(2,1)S(1)}, bf16[192,2176]{1,0:T(8,128)(2,1)S(1)}, u32[]{:S(2)}, u32[]{:S(2)}) collective-permute-start(bf16[192,2176]{1,0:T(8,128)(2,1)S(1)} %bitcast.33), channel_id=1, source_target_pairs={{0,2},{1,3},{2,0},{3,1},{4,6},{5,7},{6,4},{7,5},{8,10},{9,11},{10,... | collective-permute-start | bytes 2506760 | tf_op jit(solution)/shard_map/ppermute | solution.py:34
  28.1 1.0 fusion.15
  30.0 3.1 %collective-permute-start.6 = (bf16[2,264,128]{2,1,0:T(8,128)(2,1)S(1)}, bf16[2,264,128]{2,1,0:T(8,128)(2,1)S(1)}, u32[]{:S(2)}, u32[]{:S(2)}) collective-permute-start(bf16[2,264,128]{2,1,0:T(8,128)(2,1)S(1)} %pad_maximum_fusion.5), channel_id=1, source_target_pairs={{0,8},{1,9},{2,10},{3,11},{4,12},{5,13},{6,14},{7,15},{8,0},{9,1},... | collective-permute-start | bytes 405512 | tf_op jit(solution)/shard_map/ppermute | solution.py:55
  33.1 1.4 %collective-permute-start.7 = (bf16[2,264,128]{2,1,0:T(8,128)(2,1)S(1)}, bf16[2,264,128]{2,1,0:T(8,128)(2,1)S(1)}, u32[]{:S(2)}, u32[]{:S(2)}) collective-permute-start(bf16[2,264,128]{2,1,0:T(8,128)(2,1)S(1)} %pad_maximum_fusion.6), channel_id=1, source_target_pairs={{0,12},{1,13},{2,14},{3,15},{4,8},{5,9},{6,10},{7,11},{8,4},{9,5},... | collective-permute-start | bytes 405512 | tf_op jit(solution)/shard_map/ppermute | solution.py:55
  34.5 1.6 %collective-permute-done.5 = bf16[2,264,128]{2,1,0:T(8,128)(2,1)S(1)} collective-permute-done((bf16[2,264,128]{2,1,0:T(8,128)(2,1)S(1)}, bf16[2,264,128]{2,1,0:T(8,128)(2,1)S(1)}, u32[]{:S(2)}, u32[]{:S(2)}) %collective-permute-start.5) | collective-permute-done | bytes 135200 | tf_op jit(solution)/shard_map/ppermute | solution.py:55
  36.1 6.5 %collective-permute-done.6 = bf16[2,264,128]{2,1,0:T(8,128)(2,1)S(1)} collective-permute-done((bf16[2,264,128]{2,1,0:T(8,128)(2,1)S(1)}, bf16[2,264,128]{2,1,0:T(8,128)(2,1)S(1)}, u32[]{:S(2)}, u32[]{:S(2)}) %collective-permute-start.6) | collective-permute-done | bytes 135200 | tf_op jit(solution)/shard_map/ppermute | solution.py:55
  42.6 3.7 %collective-permute-done.8.refs_1_ = bf16[192,2176]{1,0:T(8,128)(2,1)S(1)} collective-permute-done((bf16[192,2176]{1,0:T(8,128)(2,1)S(1)}, bf16[192,2176]{1,0:T(8,128)(2,1)S(1)}, u32[]{:S(2)}, u32[]{:S(2)}) %collective-permute-start.8) | collective-permute-done | bytes 835616 | tf_op jit(solution)/shard_map/ppermute | solution.py:34
  46.3 1.6 %collective-permute-start.11 = (bf16[4,2,264,128]{3,2,1,0:T(8,128)(2,1)S(1)}, bf16[4,2,264,128]{3,2,1,0:T(8,128)(2,1)S(1)}, u32[]{:S(2)}, u32[]{:S(2)}) collective-permute-start(bf16[4,2,264,128]{3,2,1,0:T(8,128)(2,1)S(1)} %pad_maximum_fusion.1.refs_0_), channel_id=1, source_target_pairs={{0,16},{16,0},{1,17},{17,1},{2,18},{18,2},{3,19},{19,3},{4,20},{20... | collective-permute-start | bytes 1622024 | tf_op jit(solution)/shard_map/ppermute | solution.py:412
  48.6 9.3 %base_products.1 = (f32[768,768]{1,0:T(8,128)S(1)}, f32[768,768]{1,0:T(8,128)S(1)}) custom-call(bf16[192,2176]{1,0:T(8,128)(2,1)S(1)} %bitcast.35, bf16[192,2176]{1,0:T(8,128)(2,1)S(1)} %collective-permute-done.8.refs_1_, bf16[192,2176]{1,0:T(8,128)(2,1)S(1)} %collective-permute-done.9.refs_2_, bf16[192,2176]{1,0:T(8,128)(2,1)S(1)} %collective-permute-done.10.refs_3_, ...), custom_call_target="tpu_custom_call" | custom-call | flops 1 | bytes 1 | tf_op jit(solution)/shard_map/base_products/pallas_call | solution.py:274
  57.9 3.1 %collective-permute-done.11.refs_1_ = bf16[4,2,264,128]{3,2,1,0:T(8,128)(2,1)S(1)} collective-permute-done((bf16[4,2,264,128]{3,2,1,0:T(8,128)(2,1)S(1)}, bf16[4,2,264,128]{3,2,1,0:T(8,128)(2,1)S(1)}, u32[]{:S(2)}, u32[]{:S(2)}) %collective-permute-start.11) | collective-permute-done | bytes 540704 | tf_op jit(solution)/shard_map/ppermute | solution.py:412
  61.1 1.6 %relayout_factors.1 = (bf16[2048,128]{1,0:T(8,128)(2,1)S(1)}, bf16[64,768]{1,0:T(8,128)(2,1)S(1)}, bf16[64,768]{1,0:T(8,128)(2,1)S(1)}, bf16[768,128]{1,0:T(8,128)(2,1)S(1)}, bf16[64,2048]{1,0:T(8,128)(2,1)S(1)}) custom-call(s32[2]{0:T(128)S(1)} %copy-done.3, bf16[4,2,264,128]{3,2,1,0:T(8,128)(2,1)S(1)} %pad_maximum_fusion.1.refs_0_, ...), custom_call_target="tpu_custom_call" | custom-call | flops 1 | bytes 1 | tf_op jit(solution)/shard_map/relayout_factors/pallas_call | solution.py:199
  62.7 6.2 %finish_step.4 = (f32[128,2048]{1,0:T(8,128)S(1)}, bf16[128,2048]{1,0:T(8,128)(2,1)S(1)}) custom-call(s32[2]{0:T(128)S(1)} %copy-done.3, bf16[192,2176]{1,0:T(8,128)(2,1)S(1)} %bitcast.36, bf16[192,2176]{1,0:T(8,128)(2,1)S(1)} %collective-permute-done.8.refs_1_, bf16[192,2176]{1,0:T(8,128)(2,1)S(1)} %collective-permute-done.9.refs_2_, ...), custom_call_target="tpu_custom_call" | custom-call | flops 1 | bytes 1 | tf_op jit(solution)/shard_map/finish_step/pallas_call | solution.py:361
  69.0 6.2 %finish_step.3 = (f32[128,2048]{1,0:T(8,128)S(1)}, bf16[128,2048]{1,0:T(8,128)(2,1)S(1)}) custom-call(s32[2]{0:T(128)S(1)} %copy-done.3, bf16[192,2176]{1,0:T(8,128)(2,1)S(1)} %bitcast.37, bf16[192,2176]{1,0:T(8,128)(2,1)S(1)} %collective-permute-done.8.refs_1_, bf16[192,2176]{1,0:T(8,128)(2,1)S(1)} %collective-permute-done.9.refs_2_, ...), custom_call_target="tpu_custom_call" | custom-call | flops 1 | bytes 1 | tf_op jit(solution)/shard_map/finish_step/pallas_call | solution.py:361
  75.9 1.6 %collective-permute-start.18 = (bf16[64,2048]{1,0:T(8,128)(2,1)S(1)}, bf16[64,2048]{1,0:T(8,128)(2,1)S(1)}, u32[]{:S(2)}, u32[]{:S(2)}) collective-permute-start(bf16[64,2048]{1,0:T(8,128)(2,1)S(1)} %slice.167), channel_id=1, source_target_pairs={{0,2},{1,3},{2,0},{3,1},{4,6},{5,7},{6,4},{7,5},{8,10},{9,11},{10,... | collective-permute-start | bytes 786440 | tf_op jit(solution)/shard_map/ppermute | solution.py:34
  77.7 1.4 %collective-permute-start.13 = (bf16[64,2048]{1,0:T(8,128)(2,1)S(1)}, bf16[64,2048]{1,0:T(8,128)(2,1)S(1)}, u32[]{:S(2)}, u32[]{:S(2)}) collective-permute-start(bf16[64,2048]{1,0:T(8,128)(2,1)S(1)} %slice.168), channel_id=1, source_target_pairs={{0,2},{1,3},{2,0},{3,1},{4,6},{5,7},{6,4},{7,5},{8,10},{9,11},{10,... | collective-permute-start | bytes 786440 | tf_op jit(solution)/shard_map/ppermute | solution.py:34
  79.1 6.2 %finish_step.5 = (f32[128,2048]{1,0:T(8,128)S(1)}, bf16[128,2048]{1,0:T(8,128)(2,1)S(1)}) custom-call(s32[2]{0:T(128)S(1)} %copy-done.3, bf16[192,2176]{1,0:T(8,128)(2,1)S(1)} %bitcast.38, bf16[192,2176]{1,0:T(8,128)(2,1)S(1)} %collective-permute-done.8.refs_1_, bf16[192,2176]{1,0:T(8,128)(2,1)S(1)} %collective-permute-done.9.refs_2_, ...), custom_call_target="tpu_custom_call" | custom-call | flops 1 | bytes 1 | tf_op jit(solution)/shard_map/finish_step/pallas_call | solution.py:361
  85.7 2.4 %collective-permute-start.21 = (bf16[16,2048]{1,0:T(8,128)(2,1)S(1)}, bf16[16,2048]{1,0:T(8,128)(2,1)S(1)}, u32[]{:S(2)}, u32[]{:S(2)}) collective-permute-start(bf16[16,2048]{1,0:T(8,128)(2,1)S(1)} %get-tuple-element.91), channel_id=1, source_target_pairs={{0,12},{1,13},{2,14},{3,15},{4,8},{5,9},{6,10},{7,11},{8,4},{9,5},... | collective-permute-start | bytes 196616 | tf_op jit(solution)/shard_map/ppermute | solution.py:34
  88.1 1.0 collective-permute-start.20
  90.4 2.4 %collective-permute-start.16 = (bf16[16,2048]{1,0:T(8,128)(2,1)S(1)}, bf16[16,2048]{1,0:T(8,128)(2,1)S(1)}, u32[]{:S(2)}, u32[]{:S(2)}) collective-permute-start(bf16[16,2048]{1,0:T(8,128)(2,1)S(1)} %get-tuple-element.88), channel_id=1, source_target_pairs={{0,12},{1,13},{2,14},{3,15},{4,8},{5,9},{6,10},{7,11},{8,4},{9,5},... | collective-permute-start | bytes 196616 | tf_op jit(solution)/shard_map/ppermute | solution.py:34
  93.7 1.5 %collective-permute-start.23 = (bf16[64,2048]{1,0:T(8,128)(2,1)S(1)}, bf16[64,2048]{1,0:T(8,128)(2,1)S(1)}, u32[]{:S(2)}, u32[]{:S(2)}) collective-permute-start(bf16[64,2048]{1,0:T(8,128)(2,1)S(1)} %slice.166), channel_id=1, source_target_pairs={{0,2},{1,3},{2,0},{3,1},{4,6},{5,7},{6,4},{7,5},{8,10},{9,11},{10,... | collective-permute-start | bytes 786440 | tf_op jit(solution)/shard_map/ppermute | solution.py:34
  95.3 3.7 %collective-permute-done.20 = bf16[16,2048]{1,0:T(8,128)(2,1)S(1)} collective-permute-done((bf16[16,2048]{1,0:T(8,128)(2,1)S(1)}, bf16[16,2048]{1,0:T(8,128)(2,1)S(1)}, u32[]{:S(2)}, u32[]{:S(2)}) %collective-permute-start.20) | collective-permute-done | bytes 65568 | tf_op jit(solution)/shard_map/ppermute | solution.py:34
  98.9 1.4 %collective-permute-done.23 = bf16[64,2048]{1,0:T(8,128)(2,1)S(1)} collective-permute-done((bf16[64,2048]{1,0:T(8,128)(2,1)S(1)}, bf16[64,2048]{1,0:T(8,128)(2,1)S(1)}, u32[]{:S(2)}, u32[]{:S(2)}) %collective-permute-start.23) | collective-permute-done | bytes 262176 | tf_op jit(solution)/shard_map/ppermute | solution.py:34
  100.5 1.8 %collective-permute-start.24 = (bf16[16,2048]{1,0:T(8,128)(2,1)S(1)}, bf16[16,2048]{1,0:T(8,128)(2,1)S(1)}, u32[]{:S(2)}, u32[]{:S(2)}) collective-permute-start(bf16[16,2048]{1,0:T(8,128)(2,1)S(1)} %get-tuple-element.93), channel_id=1, source_target_pairs={{0,4},{1,5},{2,6},{3,7},{4,0},{5,1},{6,2},{7,3},{8,12},{9,13},{10,... | collective-permute-start | bytes 196616 | tf_op jit(solution)/shard_map/ppermute | solution.py:34
  102.3 2.3 %collective-permute-start.26 = (bf16[16,2048]{1,0:T(8,128)(2,1)S(1)}, bf16[16,2048]{1,0:T(8,128)(2,1)S(1)}, u32[]{:S(2)}, u32[]{:S(2)}) collective-permute-start(bf16[16,2048]{1,0:T(8,128)(2,1)S(1)} %get-tuple-element.94), channel_id=1, source_target_pairs={{0,12},{1,13},{2,14},{3,15},{4,8},{5,9},{6,10},{7,11},{8,4},{9,5},... | collective-permute-start | bytes 196616 | tf_op jit(solution)/shard_map/ppermute | solution.py:34
  105.3 3.0 %collective-permute-done.26 = bf16[16,2048]{1,0:T(8,128)(2,1)S(1)} collective-permute-done((bf16[16,2048]{1,0:T(8,128)(2,1)S(1)}, bf16[16,2048]{1,0:T(8,128)(2,1)S(1)}, u32[]{:S(2)}, u32[]{:S(2)}) %collective-permute-start.26) | collective-permute-done | bytes 65568 | tf_op jit(solution)/shard_map/ppermute | solution.py:34
  108.4 1.4 %collective-permute-done.25 = bf16[16,2048]{1,0:T(8,128)(2,1)S(1)} collective-permute-done((bf16[16,2048]{1,0:T(8,128)(2,1)S(1)}, bf16[16,2048]{1,0:T(8,128)(2,1)S(1)}, u32[]{:S(2)}, u32[]{:S(2)}) %collective-permute-start.25) | collective-permute-done | bytes 65568 | tf_op jit(solution)/shard_map/ppermute | solution.py:34
  (61 shorter events, 8.1 us)
Async XLA Ops:
  0.0 48.6 %copy-start.1 = (bf16[1,2048,768]{2,1,0:T(8,128)(2,1)S(1)}, bf16[1,2048,768]{2,1,0:T(8,128)(2,1)}, u32[]{:S(2)}) copy-start(bf16[1,2048,768]{2,1,0:T(8,128)(2,1)} %param.13) | copy-start | bytes 9437188
  2.1 11.4 %collective-permute-start.2 = (bf16[48,2176]{1,0:T(8,128)(2,1)}, bf16[48,2176]{1,0:T(8,128)(2,1)S(1)}, u32[]{:S(2)}, u32[]{:S(2)}) collective-permute-start(bf16[48,2176]{1,0:T(8,128)(2,1)} %payload.1), channel_id=1, source_target_pairs={{0,12},{1,13},{2,14},{3,15},{4,8},{5,9},{6,10},{7,11},{8,4},{9,5},... | collective-permute-start | bytes 626696 | tf_op jit(solution)/shard_map/ppermute | solution.py:34
  7.2 18.1 %collective-permute-start.1 = (bf16[48,2176]{1,0:T(8,128)(2,1)}, bf16[48,2176]{1,0:T(8,128)(2,1)}, u32[]{:S(2)}, u32[]{:S(2)}) collective-permute-start(bf16[48,2176]{1,0:T(8,128)(2,1)} %payload.1), channel_id=1, source_target_pairs={{0,8},{1,9},{2,10},{3,11},{4,12},{5,13},{6,14},{7,15},{8,0},{9,1},... | collective-permute-start | bytes 626696 | tf_op jit(solution)/shard_map/ppermute | solution.py:34
  7.2 18.1 %collective-permute-start = (bf16[48,2176]{1,0:T(8,128)(2,1)}, bf16[48,2176]{1,0:T(8,128)(2,1)}, u32[]{:S(2)}, u32[]{:S(2)}) collective-permute-start(bf16[48,2176]{1,0:T(8,128)(2,1)} %payload.1), channel_id=1, source_target_pairs={{0,4},{1,5},{2,6},{3,7},{4,0},{5,1},{6,2},{7,3},{8,12},{9,13},{10,... | collective-permute-start | bytes 626696 | tf_op jit(solution)/shard_map/ppermute | solution.py:34
  11.5 37.1 %copy-start.2 = (bf16[1,2048,768]{2,1,0:T(8,128)(2,1)S(1)}, bf16[1,2048,768]{2,1,0:T(8,128)(2,1)}, u32[]{:S(2)}) copy-start(bf16[1,2048,768]{2,1,0:T(8,128)(2,1)} %param.14) | copy-start | bytes 9437188
  11.5 15.0 %collective-permute-start.3 = (bf16[4,264,128]{2,1,0:T(8,128)(2,1)}, bf16[4,264,128]{2,1,0:T(8,128)(2,1)S(1)}, u32[]{:S(2)}, u32[]{:S(2)}) collective-permute-start(bf16[4,264,128]{2,1,0:T(8,128)(2,1)} %get-tuple-element.42), channel_id=1, source_target_pairs={{0,2},{1,3},{2,0},{3,1},{4,6},{5,7},{6,4},{7,5},{8,10},{9,11},{10,... | collective-permute-start | bytes 811016 | tf_op jit(solution)/shard_map/ppermute | solution.py:34
  26.5 19.7 %collective-permute-start.8 = (bf16[192,2176]{1,0:T(8,128)(2,1)S(1)}, bf16[192,2176]{1,0:T(8,128)(2,1)S(1)}, u32[]{:S(2)}, u32[]{:S(2)}) collective-permute-start(bf16[192,2176]{1,0:T(8,128)(2,1)S(1)} %bitcast.33), channel_id=1, source_target_pairs={{0,2},{1,3},{2,0},{3,1},{4,6},{5,7},{6,4},{7,5},{8,10},{9,11},{10,... | collective-permute-start | bytes 2506760 | tf_op jit(solution)/shard_map/ppermute | solution.py:34
  29.1 5.3 %collective-permute-start.4 = (bf16[2,264,128]{2,1,0:T(8,128)(2,1)S(1)}, bf16[2,264,128]{2,1,0:T(8,128)(2,1)S(1)}, u32[]{:S(2)}, u32[]{:S(2)}) collective-permute-start(bf16[2,264,128]{2,1,0:T(8,128)(2,1)S(1)} %pad_maximum_fusion.3), channel_id=1, source_target_pairs={{0,0},{1,1},{2,2},{3,3},{4,4},{5,5},{6,6},{7,7},{8,8},{9,9},{10,10... | collective-permute-start | bytes 405512 | tf_op jit(solution)/shard_map/ppermute | solution.py:55
  29.9 6.2 %collective-permute-start.5 = (bf16[2,264,128]{2,1,0:T(8,128)(2,1)S(1)}, bf16[2,264,128]{2,1,0:T(8,128)(2,1)S(1)}, u32[]{:S(2)}, u32[]{:S(2)}) collective-permute-start(bf16[2,264,128]{2,1,0:T(8,128)(2,1)S(1)} %pad_maximum_fusion.4), channel_id=1, source_target_pairs={{0,4},{1,5},{2,6},{3,7},{4,0},{5,1},{6,2},{7,3},{8,12},{9,13},{10,... | collective-permute-start | bytes 405512 | tf_op jit(solution)/shard_map/ppermute | solution.py:55
  30.0 12.6 %collective-permute-start.6 = (bf16[2,264,128]{2,1,0:T(8,128)(2,1)S(1)}, bf16[2,264,128]{2,1,0:T(8,128)(2,1)S(1)}, u32[]{:S(2)}, u32[]{:S(2)}) collective-permute-start(bf16[2,264,128]{2,1,0:T(8,128)(2,1)S(1)} %pad_maximum_fusion.5), channel_id=1, source_target_pairs={{0,8},{1,9},{2,10},{3,11},{4,12},{5,13},{6,14},{7,15},{8,0},{9,1},... | collective-permute-start | bytes 405512 | tf_op jit(solution)/shard_map/ppermute | solution.py:55
  33.1 9.5 %collective-permute-start.7 = (bf16[2,264,128]{2,1,0:T(8,128)(2,1)S(1)}, bf16[2,264,128]{2,1,0:T(8,128)(2,1)S(1)}, u32[]{:S(2)}, u32[]{:S(2)}) collective-permute-start(bf16[2,264,128]{2,1,0:T(8,128)(2,1)S(1)} %pad_maximum_fusion.6), channel_id=1, source_target_pairs={{0,12},{1,13},{2,14},{3,15},{4,8},{5,9},{6,10},{7,11},{8,4},{9,5},... | collective-permute-start | bytes 405512 | tf_op jit(solution)/shard_map/ppermute | solution.py:55
  34.5 13.4 %collective-permute-start.9 = (bf16[192,2176]{1,0:T(8,128)(2,1)S(1)}, bf16[192,2176]{1,0:T(8,128)(2,1)S(1)}, u32[]{:S(2)}, u32[]{:S(2)}) collective-permute-start(bf16[192,2176]{1,0:T(8,128)(2,1)S(1)} %bitcast.34), channel_id=1, source_target_pairs={{0,1},{1,0},{2,3},{3,2},{4,5},{5,4},{6,7},{7,6},{8,9},{9,8},{10,11... | collective-permute-start | bytes 2506760 | tf_op jit(solution)/shard_map/ppermute | solution.py:34
  46.2 2.4 %collective-permute-start.10 = (bf16[192,2176]{1,0:T(8,128)(2,1)S(1)}, bf16[192,2176]{1,0:T(8,128)(2,1)S(1)}, u32[]{:S(2)}, u32[]{:S(2)}) collective-permute-start(bf16[192,2176]{1,0:T(8,128)(2,1)S(1)} %collective-permute-done.8.refs_1_), channel_id=1, source_target_pairs={{0,1},{1,0},{2,3},{3,2},{4,5},{5,4},{6,7},{7,6},{8,9},{9,8},{10,11... | collective-permute-start | bytes 2506760 | tf_op jit(solution)/shard_map/ppermute | solution.py:34
  46.3 14.8 %collective-permute-start.11 = (bf16[4,2,264,128]{3,2,1,0:T(8,128)(2,1)S(1)}, bf16[4,2,264,128]{3,2,1,0:T(8,128)(2,1)S(1)}, u32[]{:S(2)}, u32[]{:S(2)}) collective-permute-start(bf16[4,2,264,128]{3,2,1,0:T(8,128)(2,1)S(1)} %pad_maximum_fusion.1.refs_0_), channel_id=1, source_target_pairs={{0,16},{16,0},{1,17},{17,1},{2,18},{18,2},{3,19},{19,3},{4,20},{20... | collective-permute-start | bytes 1622024 | tf_op jit(solution)/shard_map/ppermute | solution.py:412
  48.6 12.5 %copy-start.3 = (s32[2]{0:T(128)S(1)}, s32[2]{0:T(128)}, u32[]{:S(2)}) copy-start(s32[2]{0:T(128)} %pad_add_fusion.place_ref) | copy-start | bytes 28
  48.6 14.1 %copy-start = (bf16[1,768,2048]{2,1,0:T(8,128)(2,1)S(1)}, bf16[1,768,2048]{2,1,0:T(8,128)(2,1)}, u32[]{:S(2)}) copy-start(bf16[1,768,2048]{2,1,0:T(8,128)(2,1)} %param.15) | copy-start | bytes 9437188
  68.9 6.9 %collective-permute-start.17 = (bf16[128,2048]{1,0:T(8,128)(2,1)S(1)}, bf16[128,2048]{1,0:T(8,128)(2,1)S(1)}, u32[]{:S(2)}, u32[]{:S(2)}) collective-permute-start(bf16[128,2048]{1,0:T(8,128)(2,1)S(1)} %get-tuple-element.66), channel_id=1, source_target_pairs={{0,1},{1,0},{2,3},{3,2},{4,5},{5,4},{6,7},{7,6},{8,9},{9,8},{10,11... | collective-permute-start | bytes 1572872 | tf_op jit(solution)/shard_map/ppermute | solution.py:34
  75.2 2.3 %collective-permute-start.12 = (bf16[128,2048]{1,0:T(8,128)(2,1)S(1)}, bf16[128,2048]{1,0:T(8,128)(2,1)S(1)}, u32[]{:S(2)}, u32[]{:S(2)}) collective-permute-start(bf16[128,2048]{1,0:T(8,128)(2,1)S(1)} %get-tuple-element.63), channel_id=1, source_target_pairs={{0,1},{1,0},{2,3},{3,2},{4,5},{5,4},{6,7},{7,6},{8,9},{9,8},{10,11... | collective-permute-start | bytes 1572872 | tf_op jit(solution)/shard_map/ppermute | solution.py:34
  75.9 9.5 %collective-permute-start.18 = (bf16[64,2048]{1,0:T(8,128)(2,1)S(1)}, bf16[64,2048]{1,0:T(8,128)(2,1)S(1)}, u32[]{:S(2)}, u32[]{:S(2)}) collective-permute-start(bf16[64,2048]{1,0:T(8,128)(2,1)S(1)} %slice.167), channel_id=1, source_target_pairs={{0,2},{1,3},{2,0},{3,1},{4,6},{5,7},{6,4},{7,5},{8,10},{9,11},{10,... | collective-permute-start | bytes 786440 | tf_op jit(solution)/shard_map/ppermute | solution.py:34
  77.7 12.2 %collective-permute-start.13 = (bf16[64,2048]{1,0:T(8,128)(2,1)S(1)}, bf16[64,2048]{1,0:T(8,128)(2,1)S(1)}, u32[]{:S(2)}, u32[]{:S(2)}) collective-permute-start(bf16[64,2048]{1,0:T(8,128)(2,1)S(1)} %slice.168), channel_id=1, source_target_pairs={{0,2},{1,3},{2,0},{3,1},{4,6},{5,7},{6,4},{7,5},{8,10},{9,11},{10,... | collective-permute-start | bytes 786440 | tf_op jit(solution)/shard_map/ppermute | solution.py:34
  85.3 5.0 %collective-permute-start.22 = (bf16[128,2048]{1,0:T(8,128)(2,1)S(1)}, bf16[128,2048]{1,0:T(8,128)(2,1)S(1)}, u32[]{:S(2)}, u32[]{:S(2)}) collective-permute-start(bf16[128,2048]{1,0:T(8,128)(2,1)S(1)} %get-tuple-element.72), channel_id=1, source_target_pairs={{0,1},{1,0},{2,3},{3,2},{4,5},{5,4},{6,7},{7,6},{8,9},{9,8},{10,11... | collective-permute-start | bytes 1572872 | tf_op jit(solution)/shard_map/ppermute | solution.py:34
  85.6 7.3 %collective-permute-start.19 = (bf16[16,2048]{1,0:T(8,128)(2,1)S(1)}, bf16[16,2048]{1,0:T(8,128)(2,1)S(1)}, u32[]{:S(2)}, u32[]{:S(2)}) collective-permute-start(bf16[16,2048]{1,0:T(8,128)(2,1)S(1)} %get-tuple-element.90), channel_id=1, source_target_pairs={{0,4},{1,5},{2,6},{3,7},{4,0},{5,1},{6,2},{7,3},{8,12},{9,13},{10,... | collective-permute-start | bytes 196616 | tf_op jit(solution)/shard_map/ppermute | solution.py:34
  85.7 8.1 %collective-permute-start.21 = (bf16[16,2048]{1,0:T(8,128)(2,1)S(1)}, bf16[16,2048]{1,0:T(8,128)(2,1)S(1)}, u32[]{:S(2)}, u32[]{:S(2)}) collective-permute-start(bf16[16,2048]{1,0:T(8,128)(2,1)S(1)} %get-tuple-element.91), channel_id=1, source_target_pairs={{0,12},{1,13},{2,14},{3,15},{4,8},{5,9},{6,10},{7,11},{8,4},{9,5},... | collective-permute-start | bytes 196616 | tf_op jit(solution)/shard_map/ppermute | solution.py:34
  88.1 10.8 %collective-permute-start.20 = (bf16[16,2048]{1,0:T(8,128)(2,1)S(1)}, bf16[16,2048]{1,0:T(8,128)(2,1)S(1)}, u32[]{:S(2)}, u32[]{:S(2)}) collective-permute-start(bf16[16,2048]{1,0:T(8,128)(2,1)S(1)} %get-tuple-element.92), channel_id=1, source_target_pairs={{0,8},{1,9},{2,10},{3,11},{4,12},{5,13},{6,14},{7,15},{8,0},{9,1},... | collective-permute-start | bytes 196616 | tf_op jit(solution)/shard_map/ppermute | solution.py:34
  89.9 14.6 %collective-permute-start.14 = (bf16[16,2048]{1,0:T(8,128)(2,1)S(1)}, bf16[16,2048]{1,0:T(8,128)(2,1)S(1)}, u32[]{:S(2)}, u32[]{:S(2)}) collective-permute-start(bf16[16,2048]{1,0:T(8,128)(2,1)S(1)} %get-tuple-element.87), channel_id=1, source_target_pairs={{0,4},{1,5},{2,6},{3,7},{4,0},{5,1},{6,2},{7,3},{8,12},{9,13},{10,... | collective-permute-start | bytes 196616 | tf_op jit(solution)/shard_map/ppermute | solution.py:34
  90.4 14.2 %collective-permute-start.16 = (bf16[16,2048]{1,0:T(8,128)(2,1)S(1)}, bf16[16,2048]{1,0:T(8,128)(2,1)S(1)}, u32[]{:S(2)}, u32[]{:S(2)}) collective-permute-start(bf16[16,2048]{1,0:T(8,128)(2,1)S(1)} %get-tuple-element.88), channel_id=1, source_target_pairs={{0,12},{1,13},{2,14},{3,15},{4,8},{5,9},{6,10},{7,11},{8,4},{9,5},... | collective-permute-start | bytes 196616 | tf_op jit(solution)/shard_map/ppermute | solution.py:34
  92.9 11.7 %collective-permute-start.15 = (bf16[16,2048]{1,0:T(8,128)(2,1)S(1)}, bf16[16,2048]{1,0:T(8,128)(2,1)S(1)}, u32[]{:S(2)}, u32[]{:S(2)}) collective-permute-start(bf16[16,2048]{1,0:T(8,128)(2,1)S(1)} %get-tuple-element.89), channel_id=1, source_target_pairs={{0,8},{1,9},{2,10},{3,11},{4,12},{5,13},{6,14},{7,15},{8,0},{9,1},... | collective-permute-start | bytes 196616 | tf_op jit(solution)/shard_map/ppermute | solution.py:34
  93.7 6.7 %collective-permute-start.23 = (bf16[64,2048]{1,0:T(8,128)(2,1)S(1)}, bf16[64,2048]{1,0:T(8,128)(2,1)S(1)}, u32[]{:S(2)}, u32[]{:S(2)}) collective-permute-start(bf16[64,2048]{1,0:T(8,128)(2,1)S(1)} %slice.166), channel_id=1, source_target_pairs={{0,2},{1,3},{2,0},{3,1},{4,6},{5,7},{6,4},{7,5},{8,10},{9,11},{10,... | collective-permute-start | bytes 786440 | tf_op jit(solution)/shard_map/ppermute | solution.py:34
  100.5 4.8 %collective-permute-start.24 = (bf16[16,2048]{1,0:T(8,128)(2,1)S(1)}, bf16[16,2048]{1,0:T(8,128)(2,1)S(1)}, u32[]{:S(2)}, u32[]{:S(2)}) collective-permute-start(bf16[16,2048]{1,0:T(8,128)(2,1)S(1)} %get-tuple-element.93), channel_id=1, source_target_pairs={{0,4},{1,5},{2,6},{3,7},{4,0},{5,1},{6,2},{7,3},{8,12},{9,13},{10,... | collective-permute-start | bytes 196616 | tf_op jit(solution)/shard_map/ppermute | solution.py:34
  102.3 6.1 %collective-permute-start.26 = (bf16[16,2048]{1,0:T(8,128)(2,1)S(1)}, bf16[16,2048]{1,0:T(8,128)(2,1)S(1)}, u32[]{:S(2)}, u32[]{:S(2)}) collective-permute-start(bf16[16,2048]{1,0:T(8,128)(2,1)S(1)} %get-tuple-element.94), channel_id=1, source_target_pairs={{0,12},{1,13},{2,14},{3,15},{4,8},{5,9},{6,10},{7,11},{8,4},{9,5},... | collective-permute-start | bytes 196616 | tf_op jit(solution)/shard_map/ppermute | solution.py:34
  104.6 5.2 %collective-permute-start.25 = (bf16[16,2048]{1,0:T(8,128)(2,1)S(1)}, bf16[16,2048]{1,0:T(8,128)(2,1)S(1)}, u32[]{:S(2)}, u32[]{:S(2)}) collective-permute-start(bf16[16,2048]{1,0:T(8,128)(2,1)S(1)} %get-tuple-element.95), channel_id=1, source_target_pairs={{0,8},{1,9},{2,10},{3,11},{4,12},{5,13},{6,14},{7,15},{8,0},{9,1},... | collective-permute-start | bytes 196616 | tf_op jit(solution)/shard_map/ppermute | solution.py:34

commit v11 on v10

--- a/solution.py
+++ b/solution.py
@@ -41,6 +41,15 @@
         part = total[k * count : (k + 1) * count].astype(jnp.bfloat16)
         result = result + swap(part, n, stride, k).astype(jnp.float32)
     return result
+
+
+def exchange_along(x, n, stride, size):
+    lines = [
+        [start + k * stride for k in range(size)]
+        for start in range(n)
+        if start // stride % size == 0
+    ]
+    return lax.all_to_all(x, "expert", 0, 0, axis_index_groups=lines, tiled=True)
 
 
 def exchange_factors(blocks, n):
@@ -142,17 +151,18 @@
     )(place, placement, factors)
 
 
-def relayout_kernel(outer, middle, place_ref, *refs):
-    a_gu_ref, gate_b_ref, up_b_ref, down_a_ref, down_b_ref, flat_ref, wide_ref = refs[2:]
+def relayout_kernel(middle, place_ref, *refs):
+    parts, refs = refs[:4], refs[4:]
+    a_gu_ref, gate_b_ref, up_b_ref, down_a_ref, down_b_ref, flat_ref, wide_ref = refs
     width, units = a_gu_ref.shape[0], gate_b_ref.shape[1]
     rank = gate_b_ref.shape[0]
-    length = refs[0].shape[2]
+    half, _, length, _ = parts[0].shape
     group, me = place_ref[0], place_ref[1]
-    for swapped, part in enumerate(refs[:2]):
-        core = group if swapped == 0 else 1 - group
-        for q in range(outer):
+    for i, part in enumerate(parts):
+        core = group if i < 2 else 1 - group
+        for q in range(half):
             for r in range(middle):
-                source = me ^ ((q * middle + r) * 2 + core)
+                source = me ^ (((i % 2 * half + q) * middle + r) * 2 + core)
                 start = pl.multiple_of(source * length, 8)
                 flat_ref[pl.ds(start, length), :] = part[q, r].astype(jnp.float32)
 
@@ -193,14 +203,14 @@
 
 
 def relayout_factors(place, here, there, width, units, rank, n):
-    outer, middle, _ = split_axis(n)
+    middle = split_axis(n)[1]
     shapes = [(width, 2 * rank), (rank, units), (rank, units), (units, 2 * rank), (rank, width)]
-    length = here.shape[2]
+    length = here[0].shape[2]
     return pl.pallas_call(
-        functools.partial(relayout_kernel, outer, middle),
+        functools.partial(relayout_kernel, middle),
         out_shape=[jax.ShapeDtypeStruct(shape, jnp.bfloat16) for shape in shapes],
         in_specs=[pl.BlockSpec(memory_space=pltpu.SMEM)]
-        + [pl.BlockSpec(memory_space=pltpu.VMEM)] * 2,
+        + [pl.BlockSpec(memory_space=pltpu.VMEM)] * 4,
         scratch_shapes=[
             pltpu.VMEM((n * length, LANES), jnp.float32),
             pltpu.VMEM((width, LANES), jnp.float32),
@@ -208,7 +218,7 @@
         compiler_params=pltpu.CompilerParams(vmem_limit_bytes=GRANT),
         cost_estimate=LITTLE,
         name="relayout_factors",
-    )(place, here, there)
+    )(place, *here, *there)
 
 
 class Loads:
@@ -294,10 +304,11 @@
 
 def finish_kernel(count, first, rows, place_ref, *refs):
     pieces, refs = refs[:count], refs[count:]
-    gate_hbm, up_hbm, a_gu_hbm, gate_b_hbm, up_b_hbm, down_a_hbm, down_b_hbm = refs[:7]
-    w_down_hbm, kept_hbm, sent_hbm, x_ref, gate_ref, up_ref = refs[7:13]
-    a_gu_ref, gate_b_ref, up_b_ref, down_a_ref, down_b_ref, w_down_ref = refs[13:19]
-    inner_ref, kept_ref, sent_ref, sem, out_sem = refs[19:]
+    base, refs = refs[:count], refs[count:]
+    a_gu_hbm, gate_b_hbm, up_b_hbm, down_a_hbm, down_b_hbm = refs[:5]
+    w_down_hbm, kept_hbm, sent_hbm, x_ref, gate_ref, up_ref = refs[5:11]
+    a_gu_ref, gate_b_ref, up_b_ref, down_a_ref, down_b_ref, w_down_ref = refs[11:17]
+    inner_ref, kept_ref, sent_ref, sem, out_sem = refs[17:]
     span = pieces[0].shape[0]
     units, width = w_down_ref.shape
     rank = gate_b_ref.shape[0]
@@ -310,9 +321,10 @@
     x_in += loads.begin(a_gu_hbm, a_gu_ref)
     x_in += loads.begin(gate_b_hbm, gate_b_ref) + loads.begin(up_b_hbm, up_b_ref)
     for i in range(count):
-        src, dst = pl.ds(i * span + first, rows), pl.ds(i * rows, rows)
-        base_in += loads.begin(gate_hbm.at[src], gate_ref.at[dst])
-        base_in += loads.begin(up_hbm.at[src], up_ref.at[dst])
+        half, r = i // (count // 2), i % (count // 2)
+        src, dst = pl.ds(half * span + first, rows), pl.ds(i * rows, rows)
+        base_in += loads.begin(base[2 * r].at[src], gate_ref.at[dst])
+        base_in += loads.begin(base[2 * r + 1].at[src], up_ref.at[dst])
     down_in = loads.begin(down_a_hbm, down_a_ref) + loads.begin(down_b_hbm, down_b_ref)
     down_in += loads.begin_rows(w_down_hbm, w_down_ref)
     cuts = [slice(at, at + block) for at in range(0, 2 * own, block)]
@@ -362,7 +374,7 @@
         functools.partial(finish_kernel, len(pieces), first, rows),
         out_shape=outs,
         in_specs=[pl.BlockSpec(memory_space=pltpu.SMEM)]
-        + [pl.BlockSpec(memory_space=pl.ANY)] * (len(pieces) + 2 + len(low_rank))
+        + [pl.BlockSpec(memory_space=pl.ANY)] * (2 * len(pieces) + len(low_rank))
         + [pl.BlockSpec(memory_space=pltpu.HBM)],
         out_specs=[pl.BlockSpec(memory_space=pl.ANY)] * 2,
         scratch_shapes=[
@@ -400,20 +412,25 @@
 
     rows_in = make_payload(hidden, route_ids, route_logits, experts)
     rows_in, factors = lax.optimization_barrier((rows_in, factors))
-    column = [p.reshape(steps, rows, -1) for p in along(rows_in, *along_outer)]
-    column = jnp.stack(column, axis=1).reshape(steps * outer * rows, -1)
+    column = jnp.broadcast_to(rows_in, (outer, *rows_in.shape))
+    column = exchange_along(column, owners, *along_outer).reshape(outer, steps, rows, -1)
+    column = jnp.swapaxes(column, 0, 1).reshape(steps * outer * rows, -1)
     blocks = order_factors(place, placement, factors, owners)
     blocks = [blocks[0]] + [swap(blocks[r], owners, cores, r) for r in range(1, middle)]
     column, blocks = lax.optimization_barrier((column, blocks))
     here = exchange_factors(blocks, owners)
+    here = [jnp.stack(here[: outer // 2]), jnp.stack(here[outer // 2 :])]
     sheet = along(column, *along_middle)
-    here, sheet[1:] = lax.optimization_barrier((here, sheet[1:]))
-    here = jnp.stack(here)
-    there = lax.ppermute(here, "group", [(0, 1), (1, 0)])
-    pieces = sheet + [swap(p, owners, 1, 1) for p in sheet]
-    base = base_products(pieces, w_gate[0], w_up[0])
+    others = [swap(column, owners, 1, 1)]
+    base = [base_products([sheet[0], others[0]], w_gate[0], w_up[0])]
+    here[0], base = lax.optimization_barrier((here[0], base))
+    there = [lax.ppermute(p, "group", [(0, 1), (1, 0)]) for p in here]
+    for r in range(1, middle):
+        others.append(swap(sheet[r], owners, 1, 1))
+        base.append(base_products([sheet[r], others[r]], w_gate[0], w_up[0]))
     here, there, base = lax.optimization_barrier((here, there, base))
     low_rank = relayout_factors(place, here, there, width, units, rank, owners)
+    pieces, base = sheet + others, [b for pair in base for b in pair]
 
     span = outer * rows
     results = []
@@ -423,8 +440,12 @@
         kept, sent = finish_step(place, pieces, base, s * span, span, low_rank, down_weight[0])
         results.append(kept + swap(sent, owners, 1, 1).astype(jnp.float32))
     results = [scatter_along(total, owners, *along_middle) for total in results]
-    results = [scatter_along(total, owners, *along_outer) for total in results]
-    return jnp.stack(results).astype(jnp.bfloat16)
+    finals = []
+    for total in results:
+        parts = total.astype(jnp.bfloat16).reshape(outer, rows, width)
+        parts = exchange_along(parts, owners, *along_outer)
+        finals.append(jnp.sum(parts, axis=0, dtype=jnp.float32))
+    return jnp.stack(finals).astype(jnp.bfloat16)
 
 
 def row_capacity(rows, top, experts):

time: 111 us -> 137 us (1.23)
  waiting for transfers between devices: 38.6 us -> 57.5 us
  local copies, waits for them, and re-layouts: 1.17 us -> 6.1 us
  other arithmetic: 3.28 us -> 5.13 us
    all_to_all x0 -> x4, waiting for transfers between devices: none -> 32.9 us  [exchange_along(): lax.all_to_all(x, 'expert', 0, 0, axis_index_groups=lines, tiled=True)]
    ppermute x22 -> x10, starting transfers between devices: 25.5 us -> 7.64 us  [swap(): return lax.ppermute(x, 'expert', [(i, i ^ k * stride) for i in range(n)])]
    all_to_all x0 -> x4, starting transfers between devices: none -> 16.8 us  [exchange_along(): lax.all_to_all(x, 'expert', 0, 0, axis_index_groups=lines, tiled=True)]
    ppermute x22 -> x10, waiting for transfers between devices: 27.4 us -> 16.8 us  [swap(): return lax.ppermute(x, 'expert', [(i, i ^ k * stride) for i in range(n)])]
    convert_element_type x0 -> x3, other arithmetic: none -> 3.23 us  [dense_shards(): parts = total.astype(jnp.bfloat16).reshape(outer, rows, width)]
    ppermute x1 -> x2, starting transfers between devices: 1.56 us -> 4.29 us  [dense_shards(): there = [lax.ppermute(p, 'group', [(0, 1), (1, 0)]) for p in here]]
    ppermute x4, waiting for transfers between devices: 8.09 us -> 5.91 us  [exchange_factors(): here.append(lax.ppermute(part, ('group', 'expert'), pairs))]
    broadcast_in_dim x0 -> x1, local copies, waits for them, and re-layouts: none -> 1.91 us  [dense_shards(): column = jnp.broadcast_to(rows_in, (outer, *rows_in.shape))]
  transfers between devices with their start and end apart: 27 -> 20, of which waited for: 13 -> 8; matrix products, arithmetic and copies ran while one was open for 3% -> 6% of each run, Pallas kernels for 23% -> 19%
where the time goes in v11:
time: 137 us
  waiting for transfers between devices  57.5 us (42%)
  Pallas kernels  35.3 us (26%)
  starting transfers between devices  32.6 us (24%)
  local copies, waits for them, and re-layouts  6.1 us (4%)
  other arithmetic  5.13 us (4%)
    all_to_all x4, waiting for transfers between devices, exchange_along(): lax.all_to_all(x, 'expert', 0, 0, axis_index_groups=lines, tiled=True)  32.9 us
    pallas_call x3, Pallas kernels, finish_step(): pl.pallas_call(functools.partial(finish_kernel, len(pieces), first, rows)...  18.7 us
    all_to_all x4, starting transfers between devices, exchange_along(): lax.all_to_all(x, 'expert', 0, 0, axis_index_groups=lines, tiled=True)  16.8 us
    ppermute x10, waiting for transfers between devices, swap(): return lax.ppermute(x, 'expert', [(i, i ^ k * stride) for i in range(n)])  16.8 us
    pallas_call x2, Pallas kernels, base_products(): pl.pallas_call(functools.partial(base_kernel, len(pieces)), out_shape=[ou...  9.8 us
    ppermute x10, starting transfers between devices, swap(): return lax.ppermute(x, 'expert', [(i, i ^ k * stride) for i in range(n)])  7.64 us
    ppermute x4, waiting for transfers between devices, exchange_factors(): here.append(lax.ppermute(part, ('group', 'expert'), pairs))  5.91 us
    ppermute x2, starting transfers between devices, dense_shards(): there = [lax.ppermute(p, 'group', [(0, 1), (1, 0)]) for p in here]  4.29 us
  transfers between devices with their start and end apart: 20, of which 8 were waited for; matrix products, arithmetic and copies ran while one was open for 6% of the time, Pallas kernels for 19%

profile of v11, /device:TPU:0, one launch (start us, length us, event | category | flops | bytes accessed | tf_op | source)
XLA Modules:
  0.0 136.9 jit_solution(8395432627873690589)
XLA Ops:
  0.0 2.0 %payload.1 = bf16[48,2176]{1,0:T(8,128)(2,1)} custom-call(bf16[3,16,2048]{2,1,0:T(8,128)(2,1)} %hidden_ref.1, s32[3,8,16]{2,1,0:T(8,128)} %bitcast.41, f32[3,8,16]{2,1,0:T(8,128)} %bitcast.42), custom_call_target="tpu_custom_call" | custom-call | flops 1 | bytes 1 | tf_op jit(solution)/shard_map/payload/pallas_call | solution.py:94
  2.0 1.9 %broadcast_in_dim.3 = bf16[4,48,2176]{2,1,0:T(8,128)(2,1)} broadcast(bf16[48,2176]{1,0:T(8,128)(2,1)} %payload.1), dimensions={1,2} | broadcast | bytes 1044480 | tf_op jit(solution)/shard_map/broadcast_in_dim | solution.py:415
  3.9 6.6 %all-to-all-start = ((bf16[4,48,2176]{2,1,0:T(8,128)(2,1)}), bf16[4,48,2176]{2,1,0:T(8,128)(2,1)}, u32[]{:S(2)}, u32[]{:S(2)}) async-start(bf16[4,48,2176]{2,1,0:T(8,128)(2,1)} %broadcast_in_dim.3), calls=%async_computation | async-start | bytes 1671168 | tf_op jit(solution)/shard_map/all_to_all | solution.py:52
  11.1 3.2 %order_factors.1 = (bf16[4,264,128]{2,1,0:T(8,128)(2,1)}, bf16[4,264,128]{2,1,0:T(8,128)(2,1)}) custom-call(s32[2]{0:T(128)} %pad_add_fusion.place_ref, s32[16]{0:T(128)} %placement_ref.1, bf16[16,33792]{1,0:T(8,128)(2,1)} %factors_ref), custom_call_target="tpu_custom_call" | custom-call | flops 1 | bytes 1 | tf_op jit(solution)/shard_map/order_factors/pallas_call | solution.py:139
  14.3 1.5 %collective-permute-start = (bf16[4,264,128]{2,1,0:T(8,128)(2,1)}, bf16[4,264,128]{2,1,0:T(8,128)(2,1)}, u32[]{:S(2)}, u32[]{:S(2)}) collective-permute-start(bf16[4,264,128]{2,1,0:T(8,128)(2,1)} %get-tuple-element.46), channel_id=1, source_target_pairs={{0,2},{1,3},{2,0},{3,1},{4,6},{5,7},{6,4},{7,5},{8,10},{9,11},{10,... | collective-permute-start | bytes 811016 | tf_op jit(solution)/shard_map/ppermute | solution.py:34
  15.9 15.9 %all-to-all-done = bf16[4,48,2176]{2,1,0:T(8,128)(2,1)} async-done(((bf16[4,48,2176]{2,1,0:T(8,128)(2,1)}), bf16[4,48,2176]{2,1,0:T(8,128)(2,1)}, u32[]{:S(2)}, u32[]{:S(2)}) %all-to-all-start) | async-done | bytes 835616 | tf_op jit(solution)/shard_map/all_to_all | solution.py:52
  31.7 1.2 copy.9
  33.0 1.6 %collective-permute-start.1 = (bf16[192,2176]{1,0:T(8,128)(2,1)S(1)}, bf16[192,2176]{1,0:T(8,128)(2,1)S(1)}, u32[]{:S(2)}, u32[]{:S(2)}) collective-permute-start(bf16[192,2176]{1,0:T(8,128)(2,1)S(1)} %bitcast.24), channel_id=1, source_target_pairs={{0,2},{1,3},{2,0},{3,1},{4,6},{5,7},{6,4},{7,5},{8,10},{9,11},{10,... | collective-permute-start | bytes 2506760 | tf_op jit(solution)/shard_map/ppermute | solution.py:34
  34.6 1.2 fusion.2
  35.8 1.5 %collective-permute-start.7 = (bf16[2,264,128]{2,1,0:T(8,128)(2,1)S(1)}, bf16[2,264,128]{2,1,0:T(8,128)(2,1)S(1)}, u32[]{:S(2)}, u32[]{:S(2)}) collective-permute-start(bf16[2,264,128]{2,1,0:T(8,128)(2,1)S(1)} %pad_maximum_fusion.6), channel_id=1, source_target_pairs={{0,12},{1,13},{2,14},{3,15},{4,8},{5,9},{6,10},{7,11},{8,4},{9,5},... | collective-permute-start | bytes 405512 | tf_op jit(solution)/shard_map/ppermute | solution.py:64
  37.3 15.3 %collective-permute-done.1.refs_0_.refs_1_ = bf16[192,2176]{1,0:T(8,128)(2,1)S(1)} collective-permute-done((bf16[192,2176]{1,0:T(8,128)(2,1)S(1)}, bf16[192,2176]{1,0:T(8,128)(2,1)S(1)}, u32[]{:S(2)}, u32[]{:S(2)}) %collective-permute-start.1) | collective-permute-done | bytes 835616 | tf_op jit(solution)/shard_map/ppermute | solution.py:34
  53.4 1.7 %collective-permute-start.5 = (bf16[2,264,128]{2,1,0:T(8,128)(2,1)S(1)}, bf16[2,264,128]{2,1,0:T(8,128)(2,1)S(1)}, u32[]{:S(2)}, u32[]{:S(2)}) collective-permute-start(bf16[2,264,128]{2,1,0:T(8,128)(2,1)S(1)} %pad_maximum_fusion.4), channel_id=1, source_target_pairs={{0,4},{1,5},{2,6},{3,7},{4,0},{5,1},{6,2},{7,3},{8,12},{9,13},{10,... | collective-permute-start | bytes 405512 | tf_op jit(solution)/shard_map/ppermute | solution.py:64
  55.1 5.9 %collective-permute-done.6 = bf16[2,264,128]{2,1,0:T(8,128)(2,1)S(1)} collective-permute-done((bf16[2,264,128]{2,1,0:T(8,128)(2,1)S(1)}, bf16[2,264,128]{2,1,0:T(8,128)(2,1)S(1)}, u32[]{:S(2)}, u32[]{:S(2)}) %collective-permute-start.6) | collective-permute-done | bytes 135200 | tf_op jit(solution)/shard_map/ppermute | solution.py:64
  61.0 1.5 %collective-permute-start.9 = (bf16[2,2,264,128]{3,2,1,0:T(8,128)(2,1)S(1)}, bf16[2,2,264,128]{3,2,1,0:T(8,128)(2,1)S(1)}, u32[]{:S(2)}, u32[]{:S(2)}) collective-permute-start(bf16[2,2,264,128]{3,2,1,0:T(8,128)(2,1)S(1)} %pad_maximum_fusion.1.refs_1_), channel_id=1, source_target_pairs={{0,16},{16,0},{1,17},{17,1},{2,18},{18,2},{3,19},{19,3},{4,20},{20... | collective-permute-start | bytes 811016 | tf_op jit(solution)/shard_map/ppermute | solution.py:427
  62.6 4.9 %base_products.2 = (f32[384,768]{1,0:T(8,128)S(1)}, f32[384,768]{1,0:T(8,128)S(1)}) custom-call(bf16[192,2176]{1,0:T(8,128)(2,1)S(1)} %bitcast.26, bf16[192,2176]{1,0:T(8,128)(2,1)S(1)} %collective-permute-done.2.refs_1_.refs_2_, bf16[2048,768]{1,0:T(8,128)(2,1)S(1)} %bitcast.30, bf16[2048,768]{1,0:T(8,128)(2,1)S(1)} %bitcast.32), custom_call_target="tpu_custom_call" | custom-call | flops 1 | bytes 1 | tf_op jit(solution)/shard_map/base_products/pallas_call | solution.py:284
  67.5 2.8 %collective-permute-start.8 = (bf16[2,2,264,128]{3,2,1,0:T(8,128)(2,1)S(1)}, bf16[2,2,264,128]{3,2,1,0:T(8,128)(2,1)S(1)}, u32[]{:S(2)}, u32[]{:S(2)}) collective-permute-start(bf16[2,2,264,128]{3,2,1,0:T(8,128)(2,1)S(1)} %pad_maximum_fusion.refs_0_), channel_id=1, source_target_pairs={{0,16},{16,0},{1,17},{17,1},{2,18},{18,2},{3,19},{19,3},{4,20},{20... | collective-permute-start | bytes 811016 | tf_op jit(solution)/shard_map/ppermute | solution.py:427
  70.3 4.9 %base_products.3 = (f32[384,768]{1,0:T(8,128)S(1)}, f32[384,768]{1,0:T(8,128)S(1)}) custom-call(bf16[192,2176]{1,0:T(8,128)(2,1)S(1)} %collective-permute-done.1.refs_0_.refs_1_, bf16[192,2176]{1,0:T(8,128)(2,1)S(1)} %collective-permute-done.3.refs_1_.refs_3_, bf16[2048,768]{1,0:T(8,128)(2,1)S(1)} %bitcast.31, bf16[2048,768]{1,0:T(8,128)(2,1)S(1)} %bitcast.33), custom_call_target="tpu_custom_call" | custom-call | flops 1 | bytes 1 | tf_op jit(solution)/shard_map/base_products/pallas_call | solution.py:284
  75.2 1.8 %collective-permute-done.8.refs_2_ = bf16[2,2,264,128]{3,2,1,0:T(8,128)(2,1)S(1)} collective-permute-done((bf16[2,2,264,128]{3,2,1,0:T(8,128)(2,1)S(1)}, bf16[2,2,264,128]{3,2,1,0:T(8,128)(2,1)S(1)}, u32[]{:S(2)}, u32[]{:S(2)}) %collective-permute-start.8) | collective-permute-done | bytes 270368 | tf_op jit(solution)/shard_map/ppermute | solution.py:427
  77.1 1.6 %relayout_factors.1 = (bf16[2048,128]{1,0:T(8,128)(2,1)S(1)}, bf16[64,768]{1,0:T(8,128)(2,1)S(1)}, bf16[64,768]{1,0:T(8,128)(2,1)S(1)}, bf16[768,128]{1,0:T(8,128)(2,1)S(1)}, bf16[64,2048]{1,0:T(8,128)(2,1)S(1)}) custom-call(s32[2]{0:T(128)S(1)} %copy-done.3, bf16[2,2,264,128]{3,2,1,0:T(8,128)(2,1)S(1)} %pad_maximum_fusion.refs_0_, ...), custom_call_target="tpu_custom_call" | custom-call | flops 1 | bytes 1 | tf_op jit(solution)/shard_map/relayout_factors/pallas_call | solution.py:209
  78.7 6.2 %finish_step.4 = (f32[128,2048]{1,0:T(8,128)S(1)}, bf16[128,2048]{1,0:T(8,128)(2,1)S(1)}) custom-call(s32[2]{0:T(128)S(1)} %copy-done.3, bf16[192,2176]{1,0:T(8,128)(2,1)S(1)} %bitcast.27, bf16[192,2176]{1,0:T(8,128)(2,1)S(1)} %collective-permute-done.1.refs_0_.refs_1_, bf16[192,2176]{1,0:T(8,128)(2,1)S(1)} %collective-permute-done.2.refs_1_.refs_2_, ...), custom_call_target="tpu_custom_call" | custom-call | flops 1 | bytes 1 | tf_op jit(solution)/shard_map/finish_step/pallas_call | solution.py:373
  85.0 6.2 %finish_step.3 = (f32[128,2048]{1,0:T(8,128)S(1)}, bf16[128,2048]{1,0:T(8,128)(2,1)S(1)}) custom-call(s32[2]{0:T(128)S(1)} %copy-done.3, bf16[192,2176]{1,0:T(8,128)(2,1)S(1)} %bitcast.28, bf16[192,2176]{1,0:T(8,128)(2,1)S(1)} %collective-permute-done.1.refs_0_.refs_1_, bf16[192,2176]{1,0:T(8,128)(2,1)S(1)} %collective-permute-done.2.refs_1_.refs_2_, ...), custom_call_target="tpu_custom_call" | custom-call | flops 1 | bytes 1 | tf_op jit(solution)/shard_map/finish_step/pallas_call | solution.py:373
  91.9 1.6 %collective-permute-start.13 = (bf16[64,2048]{1,0:T(8,128)(2,1)S(1)}, bf16[64,2048]{1,0:T(8,128)(2,1)S(1)}, u32[]{:S(2)}, u32[]{:S(2)}) collective-permute-start(bf16[64,2048]{1,0:T(8,128)(2,1)S(1)} %slice.75), channel_id=1, source_target_pairs={{0,2},{1,3},{2,0},{3,1},{4,6},{5,7},{6,4},{7,5},{8,10},{9,11},{10,... | collective-permute-start | bytes 786440 | tf_op jit(solution)/shard_map/ppermute | solution.py:34
  93.6 6.2 %finish_step.5 = (f32[128,2048]{1,0:T(8,128)S(1)}, bf16[128,2048]{1,0:T(8,128)(2,1)S(1)}) custom-call(s32[2]{0:T(128)S(1)} %copy-done.3, bf16[192,2176]{1,0:T(8,128)(2,1)S(1)} %bitcast.29, bf16[192,2176]{1,0:T(8,128)(2,1)S(1)} %collective-permute-done.1.refs_0_.refs_1_, bf16[192,2176]{1,0:T(8,128)(2,1)S(1)} %collective-permute-done.2.refs_1_.refs_2_, ...), custom_call_target="tpu_custom_call" | custom-call | flops 1 | bytes 1 | tf_op jit(solution)/shard_map/finish_step/pallas_call | solution.py:373
  100.9 1.5 %collective-permute-start.11 = (bf16[64,2048]{1,0:T(8,128)(2,1)}, bf16[64,2048]{1,0:T(8,128)(2,1)}, u32[]{:S(2)}, u32[]{:S(2)}) collective-permute-start(bf16[64,2048]{1,0:T(8,128)(2,1)} %slice.76), channel_id=1, source_target_pairs={{0,2},{1,3},{2,0},{3,1},{4,6},{5,7},{6,4},{7,5},{8,10},{9,11},{10,... | collective-permute-start | bytes 786440 | tf_op jit(solution)/shard_map/ppermute | solution.py:34
  103.1 3.4 %all-to-all-start.2 = ((bf16[4,16,2048]{2,1,0:T(8,128)(2,1)}), bf16[4,16,2048]{2,1,0:T(8,128)(2,1)S(1)}, u32[]{:S(2)}, u32[]{:S(2)}) async-start(bf16[4,16,2048]{2,1,0:T(8,128)(2,1)} %bitcast.16), calls=%async_computation.2 | async-start | bytes 524288 | tf_op jit(solution)/shard_map/all_to_all | solution.py:52
  108.3 1.4 %collective-permute-done.11 = bf16[64,2048]{1,0:T(8,128)(2,1)} collective-permute-done((bf16[64,2048]{1,0:T(8,128)(2,1)}, bf16[64,2048]{1,0:T(8,128)(2,1)}, u32[]{:S(2)}, u32[]{:S(2)}) %collective-permute-start.11) | collective-permute-done | bytes 262176 | tf_op jit(solution)/shard_map/ppermute | solution.py:34
  109.7 1.7 %add_convert_fusion = bf16[64,2048]{1,0:T(8,128)(2,1)} fusion(bf16[64,2048]{1,0:T(8,128)(2,1)} %collective-permute-done.11, f32[128,2048]{1,0:T(8,128)S(1)} %convert_add_fusion.2), kind=kLoop, calls=%fused_computation.10 | loop fusion | flops 393216 | bytes 1048576 | tf_op jit(solution)/shard_map/convert_element_type | solution.py:445
  111.4 4.3 %all-to-all-done.2 = bf16[4,16,2048]{2,1,0:T(8,128)(2,1)S(1)} async-done(((bf16[4,16,2048]{2,1,0:T(8,128)(2,1)}), bf16[4,16,2048]{2,1,0:T(8,128)(2,1)S(1)}, u32[]{:S(2)}, u32[]{:S(2)}) %all-to-all-start.2) | async-done | bytes 262176 | tf_op jit(solution)/shard_map/all_to_all | solution.py:52
  115.7 3.4 %all-to-all-start.1 = ((bf16[4,16,2048]{2,1,0:T(8,128)(2,1)}), bf16[4,16,2048]{2,1,0:T(8,128)(2,1)S(1)}, u32[]{:S(2)}, u32[]{:S(2)}) async-start(bf16[4,16,2048]{2,1,0:T(8,128)(2,1)} %bitcast.14), calls=%async_computation.1 | async-start | bytes 524288 | tf_op jit(solution)/shard_map/all_to_all | solution.py:52
  119.9 6.1 %all-to-all-done.1 = bf16[4,16,2048]{2,1,0:T(8,128)(2,1)S(1)} async-done(((bf16[4,16,2048]{2,1,0:T(8,128)(2,1)}), bf16[4,16,2048]{2,1,0:T(8,128)(2,1)S(1)}, u32[]{:S(2)}, u32[]{:S(2)}) %all-to-all-start.1) | async-done | bytes 262176 | tf_op jit(solution)/shard_map/all_to_all | solution.py:52
  126.0 3.4 %all-to-all-start.3 = ((bf16[4,16,2048]{2,1,0:T(8,128)(2,1)}), bf16[4,16,2048]{2,1,0:T(8,128)(2,1)S(1)}, u32[]{:S(2)}, u32[]{:S(2)}) async-start(bf16[4,16,2048]{2,1,0:T(8,128)(2,1)} %bitcast.18), calls=%async_computation.3 | async-start | bytes 524288 | tf_op jit(solution)/shard_map/all_to_all | solution.py:52
  129.5 6.6 %all-to-all-done.3 = bf16[4,16,2048]{2,1,0:T(8,128)(2,1)S(1)} async-done(((bf16[4,16,2048]{2,1,0:T(8,128)(2,1)}), bf16[4,16,2048]{2,1,0:T(8,128)(2,1)S(1)}, u32[]{:S(2)}, u32[]{:S(2)}) %all-to-all-start.3) | async-done | bytes 262176 | tf_op jit(solution)/shard_map/all_to_all | solution.py:52
  (53 shorter events, 7.4 us)
Async XLA Ops:
  3.9 58.7 %copy-start.2 = (bf16[1,2048,768]{2,1,0:T(8,128)(2,1)S(1)}, bf16[1,2048,768]{2,1,0:T(8,128)(2,1)}, u32[]{:S(2)}) copy-start(bf16[1,2048,768]{2,1,0:T(8,128)(2,1)} %param.14) | copy-start | bytes 9437188
  3.9 27.8 %all-to-all-start = ((bf16[4,48,2176]{2,1,0:T(8,128)(2,1)}), bf16[4,48,2176]{2,1,0:T(8,128)(2,1)}, u32[]{:S(2)}, u32[]{:S(2)}) async-start(bf16[4,48,2176]{2,1,0:T(8,128)(2,1)} %broadcast_in_dim.3), calls=%async_computation | async-start | bytes 1671168 | tf_op jit(solution)/shard_map/all_to_all | solution.py:52
  14.3 20.2 %copy-start.6 = (bf16[4,264,128]{2,1,0:T(8,128)(2,1)S(1)}, bf16[4,264,128]{2,1,0:T(8,128)(2,1)}, u32[]{:S(2)}) copy-start(bf16[4,264,128]{2,1,0:T(8,128)(2,1)} %get-tuple-element.48) | copy-start | bytes 811012
  14.3 18.6 %collective-permute-start = (bf16[4,264,128]{2,1,0:T(8,128)(2,1)}, bf16[4,264,128]{2,1,0:T(8,128)(2,1)}, u32[]{:S(2)}, u32[]{:S(2)}) collective-permute-start(bf16[4,264,128]{2,1,0:T(8,128)(2,1)} %get-tuple-element.46), channel_id=1, source_target_pairs={{0,2},{1,3},{2,0},{3,1},{4,6},{5,7},{6,4},{7,5},{8,10},{9,11},{10,... | collective-permute-start | bytes 811016 | tf_op jit(solution)/shard_map/ppermute | solution.py:34
  33.0 19.6 %collective-permute-start.1 = (bf16[192,2176]{1,0:T(8,128)(2,1)S(1)}, bf16[192,2176]{1,0:T(8,128)(2,1)S(1)}, u32[]{:S(2)}, u32[]{:S(2)}) collective-permute-start(bf16[192,2176]{1,0:T(8,128)(2,1)S(1)} %bitcast.24), channel_id=1, source_target_pairs={{0,2},{1,3},{2,0},{3,1},{4,6},{5,7},{6,4},{7,5},{8,10},{9,11},{10,... | collective-permute-start | bytes 2506760 | tf_op jit(solution)/shard_map/ppermute | solution.py:34
  34.6 28.0 %collective-permute-start.2 = (bf16[192,2176]{1,0:T(8,128)(2,1)S(1)}, bf16[192,2176]{1,0:T(8,128)(2,1)S(1)}, u32[]{:S(2)}, u32[]{:S(2)}) collective-permute-start(bf16[192,2176]{1,0:T(8,128)(2,1)S(1)} %bitcast.25), channel_id=1, source_target_pairs={{0,1},{1,0},{2,3},{3,2},{4,5},{5,4},{6,7},{7,6},{8,9},{9,8},{10,11... | collective-permute-start | bytes 2506760 | tf_op jit(solution)/shard_map/ppermute | solution.py:34
  34.6 28.0 %copy-start.1 = (bf16[1,2048,768]{2,1,0:T(8,128)(2,1)S(1)}, bf16[1,2048,768]{2,1,0:T(8,128)(2,1)}, u32[]{:S(2)}) copy-start(bf16[1,2048,768]{2,1,0:T(8,128)(2,1)} %param.13) | copy-start | bytes 9437188
  35.8 17.7 %collective-permute-start.7 = (bf16[2,264,128]{2,1,0:T(8,128)(2,1)S(1)}, bf16[2,264,128]{2,1,0:T(8,128)(2,1)S(1)}, u32[]{:S(2)}, u32[]{:S(2)}) collective-permute-start(bf16[2,264,128]{2,1,0:T(8,128)(2,1)S(1)} %pad_maximum_fusion.6), channel_id=1, source_target_pairs={{0,12},{1,13},{2,14},{3,15},{4,8},{5,9},{6,10},{7,11},{8,4},{9,5},... | collective-permute-start | bytes 405512 | tf_op jit(solution)/shard_map/ppermute | solution.py:64
  52.6 17.7 %collective-permute-start.3 = (bf16[192,2176]{1,0:T(8,128)(2,1)S(1)}, bf16[192,2176]{1,0:T(8,128)(2,1)S(1)}, u32[]{:S(2)}, u32[]{:S(2)}) collective-permute-start(bf16[192,2176]{1,0:T(8,128)(2,1)S(1)} %collective-permute-done.1.refs_0_.refs_1_), channel_id=1, source_target_pairs={{0,1},{1,0},{2,3},{3,2},{4,5},{5,4},{6,7},{7,6},{8,9},{9,8},{10,11... | collective-permute-start | bytes 2506760 | tf_op jit(solution)/shard_map/ppermute | solution.py:34
  52.6 8.4 %collective-permute-start.6 = (bf16[2,264,128]{2,1,0:T(8,128)(2,1)S(1)}, bf16[2,264,128]{2,1,0:T(8,128)(2,1)S(1)}, u32[]{:S(2)}, u32[]{:S(2)}) collective-permute-start(bf16[2,264,128]{2,1,0:T(8,128)(2,1)S(1)} %pad_maximum_fusion.5), channel_id=1, source_target_pairs={{0,8},{1,9},{2,10},{3,11},{4,12},{5,13},{6,14},{7,15},{8,0},{9,1},... | collective-permute-start | bytes 405512 | tf_op jit(solution)/shard_map/ppermute | solution.py:64
  52.7 9.8 %collective-permute-start.4 = (bf16[2,264,128]{2,1,0:T(8,128)(2,1)S(1)}, bf16[2,264,128]{2,1,0:T(8,128)(2,1)S(1)}, u32[]{:S(2)}, u32[]{:S(2)}) collective-permute-start(bf16[2,264,128]{2,1,0:T(8,128)(2,1)S(1)} %pad_maximum_fusion.3), channel_id=1, source_target_pairs={{0,0},{1,1},{2,2},{3,3},{4,4},{5,5},{6,6},{7,7},{8,8},{9,9},{10,10... | collective-permute-start | bytes 405512 | tf_op jit(solution)/shard_map/ppermute | solution.py:64
  53.4 9.1 %collective-permute-start.5 = (bf16[2,264,128]{2,1,0:T(8,128)(2,1)S(1)}, bf16[2,264,128]{2,1,0:T(8,128)(2,1)S(1)}, u32[]{:S(2)}, u32[]{:S(2)}) collective-permute-start(bf16[2,264,128]{2,1,0:T(8,128)(2,1)S(1)} %pad_maximum_fusion.4), channel_id=1, source_target_pairs={{0,4},{1,5},{2,6},{3,7},{4,0},{5,1},{6,2},{7,3},{8,12},{9,13},{10,... | collective-permute-start | bytes 405512 | tf_op jit(solution)/shard_map/ppermute | solution.py:64
  61.0 14.2 %collective-permute-start.9 = (bf16[2,2,264,128]{3,2,1,0:T(8,128)(2,1)S(1)}, bf16[2,2,264,128]{3,2,1,0:T(8,128)(2,1)S(1)}, u32[]{:S(2)}, u32[]{:S(2)}) collective-permute-start(bf16[2,2,264,128]{3,2,1,0:T(8,128)(2,1)S(1)} %pad_maximum_fusion.1.refs_1_), channel_id=1, source_target_pairs={{0,16},{16,0},{1,17},{17,1},{2,18},{18,2},{3,19},{19,3},{4,20},{20... | collective-permute-start | bytes 811016 | tf_op jit(solution)/shard_map/ppermute | solution.py:427
  67.5 9.6 %copy-start.3 = (s32[2]{0:T(128)S(1)}, s32[2]{0:T(128)}, u32[]{:S(2)}) copy-start(s32[2]{0:T(128)} %pad_add_fusion.place_ref) | copy-start | bytes 28
  67.5 9.6 %collective-permute-start.8 = (bf16[2,2,264,128]{3,2,1,0:T(8,128)(2,1)S(1)}, bf16[2,2,264,128]{3,2,1,0:T(8,128)(2,1)S(1)}, u32[]{:S(2)}, u32[]{:S(2)}) collective-permute-start(bf16[2,2,264,128]{3,2,1,0:T(8,128)(2,1)S(1)} %pad_maximum_fusion.refs_0_), channel_id=1, source_target_pairs={{0,16},{16,0},{1,17},{17,1},{2,18},{18,2},{3,19},{19,3},{4,20},{20... | collective-permute-start | bytes 811016 | tf_op jit(solution)/shard_map/ppermute | solution.py:427
  70.3 8.3 %copy-start = (bf16[1,768,2048]{2,1,0:T(8,128)(2,1)S(1)}, bf16[1,768,2048]{2,1,0:T(8,128)(2,1)}, u32[]{:S(2)}) copy-start(bf16[1,768,2048]{2,1,0:T(8,128)(2,1)} %param.15) | copy-start | bytes 9437188
  84.9 6.9 %collective-permute-start.12 = (bf16[128,2048]{1,0:T(8,128)(2,1)S(1)}, bf16[128,2048]{1,0:T(8,128)(2,1)S(1)}, u32[]{:S(2)}, u32[]{:S(2)}) collective-permute-start(bf16[128,2048]{1,0:T(8,128)(2,1)S(1)} %get-tuple-element.74), channel_id=1, source_target_pairs={{0,1},{1,0},{2,3},{3,2},{4,5},{5,4},{6,7},{7,6},{8,9},{9,8},{10,11... | collective-permute-start | bytes 1572872 | tf_op jit(solution)/shard_map/ppermute | solution.py:34
  91.2 2.3 %collective-permute-start.10 = (bf16[128,2048]{1,0:T(8,128)(2,1)S(1)}, bf16[128,2048]{1,0:T(8,128)(2,1)S(1)}, u32[]{:S(2)}, u32[]{:S(2)}) collective-permute-start(bf16[128,2048]{1,0:T(8,128)(2,1)S(1)} %get-tuple-element.71), channel_id=1, source_target_pairs={{0,1},{1,0},{2,3},{3,2},{4,5},{5,4},{6,7},{7,6},{8,9},{9,8},{10,11... | collective-permute-start | bytes 1572872 | tf_op jit(solution)/shard_map/ppermute | solution.py:34
  91.9 10.5 %collective-permute-start.13 = (bf16[64,2048]{1,0:T(8,128)(2,1)S(1)}, bf16[64,2048]{1,0:T(8,128)(2,1)S(1)}, u32[]{:S(2)}, u32[]{:S(2)}) collective-permute-start(bf16[64,2048]{1,0:T(8,128)(2,1)S(1)} %slice.75), channel_id=1, source_target_pairs={{0,2},{1,3},{2,0},{3,1},{4,6},{5,7},{6,4},{7,5},{8,10},{9,11},{10,... | collective-permute-start | bytes 786440 | tf_op jit(solution)/shard_map/ppermute | solution.py:34
  99.9 6.7 %collective-permute-start.14 = (bf16[128,2048]{1,0:T(8,128)(2,1)S(1)}, bf16[128,2048]{1,0:T(8,128)(2,1)S(1)}, u32[]{:S(2)}, u32[]{:S(2)}) collective-permute-start(bf16[128,2048]{1,0:T(8,128)(2,1)S(1)} %get-tuple-element.80), channel_id=1, source_target_pairs={{0,1},{1,0},{2,3},{3,2},{4,5},{5,4},{6,7},{7,6},{8,9},{9,8},{10,11... | collective-permute-start | bytes 1572872 | tf_op jit(solution)/shard_map/ppermute | solution.py:34
  100.9 8.9 %collective-permute-start.11 = (bf16[64,2048]{1,0:T(8,128)(2,1)}, bf16[64,2048]{1,0:T(8,128)(2,1)}, u32[]{:S(2)}, u32[]{:S(2)}) collective-permute-start(bf16[64,2048]{1,0:T(8,128)(2,1)} %slice.76), channel_id=1, source_target_pairs={{0,2},{1,3},{2,0},{3,1},{4,6},{5,7},{6,4},{7,5},{8,10},{9,11},{10,... | collective-permute-start | bytes 786440 | tf_op jit(solution)/shard_map/ppermute | solution.py:34
  103.1 12.6 %all-to-all-start.2 = ((bf16[4,16,2048]{2,1,0:T(8,128)(2,1)}), bf16[4,16,2048]{2,1,0:T(8,128)(2,1)S(1)}, u32[]{:S(2)}, u32[]{:S(2)}) async-start(bf16[4,16,2048]{2,1,0:T(8,128)(2,1)} %bitcast.16), calls=%async_computation.2 | async-start | bytes 524288 | tf_op jit(solution)/shard_map/all_to_all | solution.py:52
  106.7 1.0 copy-start.4
  107.7 11.5 %copy-start.5 = (f32[128,2048]{1,0:T(8,128)S(1)}, f32[128,2048]{1,0:T(8,128)}, u32[]{:S(2)}) copy-start(f32[128,2048]{1,0:T(8,128)} %copy-done.4) | copy-start | bytes 3145732
  107.7 11.4 %collective-permute-start.15 = (bf16[64,2048]{1,0:T(8,128)(2,1)S(1)}, bf16[64,2048]{1,0:T(8,128)(2,1)S(1)}, u32[]{:S(2)}, u32[]{:S(2)}) collective-permute-start(bf16[64,2048]{1,0:T(8,128)(2,1)S(1)} %slice.74), channel_id=1, source_target_pairs={{0,2},{1,3},{2,0},{3,1},{4,6},{5,7},{6,4},{7,5},{8,10},{9,11},{10,... | collective-permute-start | bytes 786440 | tf_op jit(solution)/shard_map/ppermute | solution.py:34
  115.7 10.3 %all-to-all-start.1 = ((bf16[4,16,2048]{2,1,0:T(8,128)(2,1)}), bf16[4,16,2048]{2,1,0:T(8,128)(2,1)S(1)}, u32[]{:S(2)}, u32[]{:S(2)}) async-start(bf16[4,16,2048]{2,1,0:T(8,128)(2,1)} %bitcast.14), calls=%async_computation.1 | async-start | bytes 524288 | tf_op jit(solution)/shard_map/all_to_all | solution.py:52
  126.0 10.2 %all-to-all-start.3 = ((bf16[4,16,2048]{2,1,0:T(8,128)(2,1)}), bf16[4,16,2048]{2,1,0:T(8,128)(2,1)S(1)}, u32[]{:S(2)}, u32[]{:S(2)}) async-start(bf16[4,16,2048]{2,1,0:T(8,128)(2,1)} %bitcast.18), calls=%async_computation.3 | async-start | bytes 524288 | tf_op jit(solution)/shard_map/all_to_all | solution.py:52

commit v12 on v10

--- a/solution.py
+++ b/solution.py
@@ -34,13 +34,22 @@
     return lax.ppermute(x, "expert", [(i, i ^ (k * stride)) for i in range(n)])
 
 
-def scatter_along(total, n, stride, size):
-    count = total.shape[0] // size
-    result = total[:count]
-    for k in range(1, size):
-        part = total[k * count : (k + 1) * count].astype(jnp.bfloat16)
-        result = result + swap(part, n, stride, k).astype(jnp.float32)
-    return result
+def double_along(x, n, stride, size):
+    step = size // 2
+    while step:
+        x = jnp.concatenate([x, swap(x, n, stride, step)])
+        step //= 2
+    return x
+
+
+def halve_along(total, n, stride, size):
+    step = 1
+    while step < size:
+        half = total.shape[0] // 2
+        sent = swap(total[half:].astype(jnp.bfloat16), n, stride, step)
+        total = total[:half] + sent.astype(jnp.float32)
+        step *= 2
+    return total
 
 
 def exchange_factors(blocks, n):
@@ -142,13 +151,14 @@
     )(place, placement, factors)
 
 
-def relayout_kernel(outer, middle, place_ref, *refs):
-    a_gu_ref, gate_b_ref, up_b_ref, down_a_ref, down_b_ref, flat_ref, wide_ref = refs[2:]
+def relayout_kernel(middle, place_ref, *refs):
+    parts, refs = refs[:2], refs[2:]
+    a_gu_ref, gate_b_ref, up_b_ref, down_a_ref, down_b_ref, flat_ref, wide_ref = refs
     width, units = a_gu_ref.shape[0], gate_b_ref.shape[1]
     rank = gate_b_ref.shape[0]
-    length = refs[0].shape[2]
+    outer, _, length, _ = parts[0].shape
     group, me = place_ref[0], place_ref[1]
-    for swapped, part in enumerate(refs[:2]):
+    for swapped, part in enumerate(parts):
         core = group if swapped == 0 else 1 - group
         for q in range(outer):
             for r in range(middle):
@@ -193,11 +203,11 @@
 
 
 def relayout_factors(place, here, there, width, units, rank, n):
-    outer, middle, _ = split_axis(n)
+    middle = split_axis(n)[1]
     shapes = [(width, 2 * rank), (rank, units), (rank, units), (units, 2 * rank), (rank, width)]
     length = here.shape[2]
     return pl.pallas_call(
-        functools.partial(relayout_kernel, outer, middle),
+        functools.partial(relayout_kernel, middle),
         out_shape=[jax.ShapeDtypeStruct(shape, jnp.bfloat16) for shape in shapes],
         in_specs=[pl.BlockSpec(memory_space=pltpu.SMEM)]
         + [pl.BlockSpec(memory_space=pltpu.VMEM)] * 2,
@@ -267,7 +277,7 @@
         wait(store(i))
 
 
-def base_products(pieces, w_gate, w_up):
+def base_products(pieces, w_gate, w_up, cost):
     width, units = w_gate.shape
     total = sum(p.shape[0] for p in pieces)
     out = jax.ShapeDtypeStruct((total, units), jnp.float32)
@@ -287,18 +297,19 @@
             pltpu.SemaphoreType.DMA((2, total // min(128, total))),
         ],
         compiler_params=pltpu.CompilerParams(vmem_limit_bytes=EXPERT_GRANT),
-        cost_estimate=LITTLE,
+        cost_estimate=cost,
         name="base_products",
     )(*pieces, w_gate, w_up)
 
 
-def finish_kernel(count, first, rows, place_ref, *refs):
+def finish_kernel(firsts, rows, place_ref, *refs):
+    count = len(firsts)
     pieces, refs = refs[:count], refs[count:]
-    gate_hbm, up_hbm, a_gu_hbm, gate_b_hbm, up_b_hbm, down_a_hbm, down_b_hbm = refs[:7]
-    w_down_hbm, kept_hbm, sent_hbm, x_ref, gate_ref, up_ref = refs[7:13]
-    a_gu_ref, gate_b_ref, up_b_ref, down_a_ref, down_b_ref, w_down_ref = refs[13:19]
-    inner_ref, kept_ref, sent_ref, sem, out_sem = refs[19:]
-    span = pieces[0].shape[0]
+    base, refs = refs[:count], refs[count:]
+    a_gu_hbm, gate_b_hbm, up_b_hbm, down_a_hbm, down_b_hbm = refs[:5]
+    w_down_hbm, kept_hbm, sent_hbm, x_ref, gate_ref, up_ref = refs[5:11]
+    a_gu_ref, gate_b_ref, up_b_ref, down_a_ref, down_b_ref, w_down_ref = refs[11:17]
+    inner_ref, kept_ref, sent_ref, sem, out_sem = refs[17:]
     units, width = w_down_ref.shape
     rank = gate_b_ref.shape[0]
     own = kept_ref.shape[0]
@@ -306,13 +317,16 @@
     loads = Loads(sem)
     x_in, base_in = [], []
     for i, piece in enumerate(pieces):
-        x_in += loads.begin(piece.at[pl.ds(first, rows)], x_ref.at[pl.ds(i * rows, rows)])
+        src = pl.ds(firsts[i], rows)
+        x_in += loads.begin(piece.at[src], x_ref.at[pl.ds(i * rows, rows)])
     x_in += loads.begin(a_gu_hbm, a_gu_ref)
     x_in += loads.begin(gate_b_hbm, gate_b_ref) + loads.begin(up_b_hbm, up_b_ref)
     for i in range(count):
-        src, dst = pl.ds(i * span + first, rows), pl.ds(i * rows, rows)
-        base_in += loads.begin(gate_hbm.at[src], gate_ref.at[dst])
-        base_in += loads.begin(up_hbm.at[src], up_ref.at[dst])
+        half, r = i // (count // 2), i % (count // 2)
+        src = pl.ds(half * pieces[i].shape[0] + firsts[i], rows)
+        dst = pl.ds(i * rows, rows)
+        base_in += loads.begin(base[2 * r].at[src], gate_ref.at[dst])
+        base_in += loads.begin(base[2 * r + 1].at[src], up_ref.at[dst])
     down_in = loads.begin(down_a_hbm, down_a_ref) + loads.begin(down_b_hbm, down_b_ref)
     down_in += loads.begin_rows(w_down_hbm, w_down_ref)
     cuts = [slice(at, at + block) for at in range(0, 2 * own, block)]
@@ -347,7 +361,7 @@
     wait(out_copies)
 
 
-def finish_step(place, pieces, base, first, rows, low_rank, w_down):
+def finish_step(place, pieces, base, firsts, rows, low_rank, w_down, cost):
     units, width = w_down.shape
     total = rows * len(pieces)
     own = total // 2
@@ -359,10 +373,10 @@
     ]
     held = [*low_rank, w_down]
     return pl.pallas_call(
-        functools.partial(finish_kernel, len(pieces), first, rows),
+        functools.partial(finish_kernel, firsts, rows),
         out_shape=outs,
         in_specs=[pl.BlockSpec(memory_space=pltpu.SMEM)]
-        + [pl.BlockSpec(memory_space=pl.ANY)] * (len(pieces) + 2 + len(low_rank))
+        + [pl.BlockSpec(memory_space=pl.ANY)] * (2 * len(pieces) + len(low_rank))
         + [pl.BlockSpec(memory_space=pltpu.HBM)],
         out_specs=[pl.BlockSpec(memory_space=pl.ANY)] * 2,
         scratch_shapes=[
@@ -378,7 +392,7 @@
             pltpu.SemaphoreType.DMA((2 * own // min(128, own),)),
         ],
         compiler_params=pltpu.CompilerParams(vmem_limit_bytes=EXPERT_GRANT),
-        cost_estimate=LITTLE,
+        cost_estimate=cost,
         name="finish_step",
     )(place, *pieces, *base, *held)
 
@@ -395,35 +409,58 @@
     along_outer, along_middle = (middle * cores, outer), (cores, middle)
     place = jnp.stack([lax.axis_index("group"), lax.axis_index("expert")]).astype(jnp.int32)
 
-    def along(x, stride, size):
-        return [x] + [swap(x, owners, stride, k) for k in range(1, size)]
-
+    blocks = order_factors(place, placement, factors, owners)
+    hidden, blocks = lax.optimization_barrier((hidden, blocks))
     rows_in = make_payload(hidden, route_ids, route_logits, experts)
-    rows_in, factors = lax.optimization_barrier((rows_in, factors))
-    column = [p.reshape(steps, rows, -1) for p in along(rows_in, *along_outer)]
-    column = jnp.stack(column, axis=1).reshape(steps * outer * rows, -1)
-    blocks = order_factors(place, placement, factors, owners)
     blocks = [blocks[0]] + [swap(blocks[r], owners, cores, r) for r in range(1, middle)]
-    column, blocks = lax.optimization_barrier((column, blocks))
-    here = exchange_factors(blocks, owners)
-    sheet = along(column, *along_middle)
-    here, sheet[1:] = lax.optimization_barrier((here, sheet[1:]))
-    here = jnp.stack(here)
+    here = jnp.stack(exchange_factors(blocks, owners))
+    column = double_along(rows_in, owners, *along_outer)
+    column, here = lax.optimization_barrier((column, here))
     there = lax.ppermute(here, "group", [(0, 1), (1, 0)])
-    pieces = sheet + [swap(p, owners, 1, 1) for p in sheet]
-    base = base_products(pieces, w_gate[0], w_up[0])
-    here, there, base = lax.optimization_barrier((here, there, base))
+    column = jnp.swapaxes(column.reshape(outer, steps, rows, -1), 0, 1)
+    column = column.reshape(steps * outer * rows, -1)
+    span = outer * rows
+    weights = (w_gate[0], w_up[0])
+
+    def with_other_core(piece):
+        return [piece, swap(piece, owners, 1, 1)]
+
+    def along_middle_of(part):
+        return [swap(part, owners, cores, r) for r in range(1, middle)]
+
+    near = with_other_core(column)
+    flops = 8 * near[0].shape[0] * width * units
+    cost = pl.CostEstimate(flops=flops, bytes_accessed=1, transcendentals=0)
+    near_base = base_products(near, *weights, cost)
+    far, near_base, rest = lax.optimization_barrier(
+        (along_middle_of(column[:span]), near_base, column[span:])
+    )
+    rest_far = along_middle_of(rest)
+    far = [with_other_core(part) for part in far]
+    far_base = [base_products(pair, *weights, LITTLE) for pair in far]
     low_rank = relayout_factors(place, here, there, width, units, rank, owners)
 
-    span = outer * rows
-    results = []
+    summed, across = [], []
     for s in range(steps):
+        if s == 1:
+            far = [with_other_core(part) for part in rest_far]
+            far_base = [base_products(pair, *weights, LITTLE) for pair in far]
+        at = max(0, s - 1) * span
+        pairs = [near] + far
+        firsts = [s * span] + [at] * len(far)
+        pieces = [pair[0] for pair in pairs] + [pair[1] for pair in pairs]
+        base = [b for pair in [near_base] + far_base for b in pair]
+        if s >= 1:
+            pieces, summed[s - 1] = lax.optimization_barrier((pieces, summed[s - 1]))
+            across.append(halve_along(summed[s - 1], owners, *along_middle))
         if s >= 2:
-            pieces, results[s - 2] = lax.optimization_barrier((pieces, results[s - 2]))
-        kept, sent = finish_step(place, pieces, base, s * span, span, low_rank, down_weight[0])
-        results.append(kept + swap(sent, owners, 1, 1).astype(jnp.float32))
-    results = [scatter_along(total, owners, *along_middle) for total in results]
-    results = [scatter_along(total, owners, *along_outer) for total in results]
+            pieces, across[s - 2] = lax.optimization_barrier((pieces, across[s - 2]))
+        kept, sent = finish_step(
+            place, pieces, base, firsts * 2, span, low_rank, down_weight[0], cost if s >= 2 else LITTLE
+        )
+        summed.append(kept + swap(sent, owners, 1, 1).astype(jnp.float32))
+    across.append(halve_along(summed[-1], owners, *along_middle))
+    results = [halve_along(total, owners, *along_outer) for total in across]
     return jnp.stack(results).astype(jnp.bfloat16)
 
 

time: 111 us -> 121 us (1.090)
  waiting for transfers between devices: 38.6 us -> 56.6 us
  starting transfers between devices: 32.3 us -> 23.5 us
    ppermute x22 -> x20, starting transfers between devices: 25.5 us -> 16.6 us  [swap(): return lax.ppermute(x, 'expert', [(i, i ^ k * stride) for i in range(n)])]
    ppermute x22 -> x20, waiting for transfers between devices: 27.4 us -> 35.8 us  [swap(): return lax.ppermute(x, 'expert', [(i, i ^ k * stride) for i in range(n)])]
    ppermute x4, waiting for transfers between devices: 8.09 us -> 15.5 us  [exchange_factors(): here.append(lax.ppermute(part, ('group', 'expert'), pairs))]
    ppermute x1, waiting for transfers between devices: 3.15 us -> 5.33 us  [dense_shards(): there = lax.ppermute(here, 'group', [(0, 1), (1, 0)])]
    another operation x5 -> x1, other arithmetic: 1.52 us -> 0.07 us  [dense_shards(): here = jnp.stack(exchange_factors(blocks, owners))]
    pallas_call x1 -> x3, Pallas kernels: 9.3 us -> 10.3 us  [base_products(): pl.pallas_call(functools.partial(base_kernel, len(pieces)), out_shape=[ou...]
  transfers between devices with their start and end apart: 27 -> 25, of which waited for: 13 -> 16; matrix products, arithmetic and copies ran while one was open for 3% -> 2% of each run, Pallas kernels for 23% -> 27%
where the time goes in v12:
time: 121 us
  waiting for transfers between devices  56.6 us (47%)
  Pallas kernels  35.8 us (30%)
  starting transfers between devices  23.5 us (19%)
  other arithmetic  3.17 us (3%)
  local copies, waits for them, and re-layouts  1.33 us (1%)
    ppermute x20, waiting for transfers between devices, swap(): return lax.ppermute(x, 'expert', [(i, i ^ k * stride) for i in range(n)])  35.8 us
    pallas_call x3, Pallas kernels, finish_step(): pl.pallas_call(functools.partial(finish_kernel, firsts, rows), out_shape=...  18.7 us
    ppermute x20, starting transfers between devices, swap(): return lax.ppermute(x, 'expert', [(i, i ^ k * stride) for i in range(n)])  16.6 us
    ppermute x4, waiting for transfers between devices, exchange_factors(): here.append(lax.ppermute(part, ('group', 'expert'), pairs))  15.5 us
    pallas_call x3, Pallas kernels, base_products(): pl.pallas_call(functools.partial(base_kernel, len(pieces)), out_shape=[ou...  10.3 us
    ppermute x4, starting transfers between devices, exchange_factors(): here.append(lax.ppermute(part, ('group', 'expert'), pairs))  5.63 us
    ppermute x1, waiting for transfers between devices, dense_shards(): there = lax.ppermute(here, 'group', [(0, 1), (1, 0)])  5.33 us
    pallas_call x1, Pallas kernels, order_factors(): pl.pallas_call(functools.partial(order_kernel, middle), out_shape=[jax.Sh...  3.19 us
  transfers between devices with their start and end apart: 25, of which 16 were waited for; matrix products, arithmetic and copies ran while one was open for 2% of the time, Pallas kernels for 27%

profile of v12, /device:TPU:0, one launch (start us, length us, event | category | flops | bytes accessed | tf_op | source)
XLA Modules:
  0.0 120.7 jit_solution(3130522797114632321)
XLA Ops:
  0.6 3.2 %order_factors.1 = (bf16[4,264,128]{2,1,0:T(8,128)(2,1)}, bf16[4,264,128]{2,1,0:T(8,128)(2,1)}) custom-call(s32[2]{0:T(128)} %pad_add_fusion.place_ref, s32[16]{0:T(128)} %placement_ref.1, bf16[16,33792]{1,0:T(8,128)(2,1)} %factors_ref.1), custom_call_target="tpu_custom_call" | custom-call | flops 1 | bytes 1 | tf_op jit(solution)/shard_map/order_factors/pallas_call | solution.py:139
  3.8 3.0 %collective-permute-start.2 = (bf16[4,264,128]{2,1,0:T(8,128)(2,1)}, bf16[4,264,128]{2,1,0:T(8,128)(2,1)S(1)}, u32[]{:S(2)}, u32[]{:S(2)}) collective-permute-start(bf16[4,264,128]{2,1,0:T(8,128)(2,1)} %get-tuple-element.52), channel_id=1, source_target_pairs={{0,2},{1,3},{2,0},{3,1},{4,6},{5,7},{6,4},{7,5},{8,10},{9,11},{10,... | collective-permute-start | bytes 811016 | tf_op jit(solution)/shard_map/ppermute | solution.py:34
  6.8 2.0 %payload.1 = bf16[48,2176]{1,0:T(8,128)(2,1)} custom-call(bf16[3,16,2048]{2,1,0:T(8,128)(2,1)} %hidden_ref, s32[3,8,16]{2,1,0:T(8,128)} %bitcast.48, f32[3,8,16]{2,1,0:T(8,128)} %bitcast.49), custom_call_target="tpu_custom_call" | custom-call | flops 1 | bytes 1 | tf_op jit(solution)/shard_map/payload/pallas_call | solution.py:94
  8.8 2.6 %collective-permute-start = (bf16[48,2176]{1,0:T(8,128)(2,1)}, bf16[48,2176]{1,0:T(8,128)(2,1)S(1)}, u32[]{:S(2)}, u32[]{:S(2)}) collective-permute-start(bf16[48,2176]{1,0:T(8,128)(2,1)} %payload.1), channel_id=1, source_target_pairs={{0,8},{1,9},{2,10},{3,11},{4,12},{5,13},{6,14},{7,15},{8,0},{9,1},... | collective-permute-start | bytes 626696 | tf_op jit(solution)/shard_map/ppermute | solution.py:34
  11.4 1.0 fusion.6
  12.4 8.6 %collective-permute-done = bf16[48,2176]{1,0:T(8,128)(2,1)S(1)} collective-permute-done((bf16[48,2176]{1,0:T(8,128)(2,1)}, bf16[48,2176]{1,0:T(8,128)(2,1)S(1)}, u32[]{:S(2)}, u32[]{:S(2)}) %collective-permute-start) | collective-permute-done | bytes 208928 | tf_op jit(solution)/shard_map/ppermute | solution.py:34
  21.0 1.0 pad_maximum_fusion.2
  23.6 1.3 %collective-permute-start.4 = (bf16[2,264,128]{2,1,0:T(8,128)(2,1)S(1)}, bf16[2,264,128]{2,1,0:T(8,128)(2,1)S(1)}, u32[]{:S(2)}, u32[]{:S(2)}) collective-permute-start(bf16[2,264,128]{2,1,0:T(8,128)(2,1)S(1)} %pad_maximum_fusion.5), channel_id=1, source_target_pairs={{0,4},{1,5},{2,6},{3,7},{4,0},{5,1},{6,2},{7,3},{8,12},{9,13},{10,... | collective-permute-start | bytes 405512 | tf_op jit(solution)/shard_map/ppermute | solution.py:64
  24.9 2.1 %collective-permute-start.5 = (bf16[2,264,128]{2,1,0:T(8,128)(2,1)S(1)}, bf16[2,264,128]{2,1,0:T(8,128)(2,1)S(1)}, u32[]{:S(2)}, u32[]{:S(2)}) collective-permute-start(bf16[2,264,128]{2,1,0:T(8,128)(2,1)S(1)} %pad_maximum_fusion.6), channel_id=1, source_target_pairs={{0,8},{1,9},{2,10},{3,11},{4,12},{5,13},{6,14},{7,15},{8,0},{9,1},... | collective-permute-start | bytes 405512 | tf_op jit(solution)/shard_map/ppermute | solution.py:64
  27.0 1.5 %collective-permute-start.6 = (bf16[2,264,128]{2,1,0:T(8,128)(2,1)S(1)}, bf16[2,264,128]{2,1,0:T(8,128)(2,1)S(1)}, u32[]{:S(2)}, u32[]{:S(2)}) collective-permute-start(bf16[2,264,128]{2,1,0:T(8,128)(2,1)S(1)} %pad_maximum_fusion.7), channel_id=1, source_target_pairs={{0,12},{1,13},{2,14},{3,15},{4,8},{5,9},{6,10},{7,11},{8,4},{9,5},... | collective-permute-start | bytes 405512 | tf_op jit(solution)/shard_map/ppermute | solution.py:64
  28.6 9.9 %collective-permute-done.4 = bf16[2,264,128]{2,1,0:T(8,128)(2,1)S(1)} collective-permute-done((bf16[2,264,128]{2,1,0:T(8,128)(2,1)S(1)}, bf16[2,264,128]{2,1,0:T(8,128)(2,1)S(1)}, u32[]{:S(2)}, u32[]{:S(2)}) %collective-permute-start.4) | collective-permute-done | bytes 135200 | tf_op jit(solution)/shard_map/ppermute | solution.py:64
  38.6 5.4 %collective-permute-done.6 = bf16[2,264,128]{2,1,0:T(8,128)(2,1)S(1)} collective-permute-done((bf16[2,264,128]{2,1,0:T(8,128)(2,1)S(1)}, bf16[2,264,128]{2,1,0:T(8,128)(2,1)S(1)}, u32[]{:S(2)}, u32[]{:S(2)}) %collective-permute-start.6) | collective-permute-done | bytes 135200 | tf_op jit(solution)/shard_map/ppermute | solution.py:64
  45.0 1.3 %collective-permute-start.12 = (bf16[4,2,264,128]{3,2,1,0:T(8,128)(2,1)S(1)}, bf16[4,2,264,128]{3,2,1,0:T(8,128)(2,1)S(1)}, u32[]{:S(2)}, u32[]{:S(2)}) collective-permute-start(bf16[4,2,264,128]{3,2,1,0:T(8,128)(2,1)S(1)} %pad_maximum_fusion.1.refs_0_), channel_id=1, source_target_pairs={{0,16},{16,0},{1,17},{17,1},{2,18},{18,2},{3,19},{19,3},{4,20},{20... | collective-permute-start | bytes 1622024 | tf_op jit(solution)/shard_map/ppermute | solution.py:419
  46.7 4.9 %base_products.3 = (f32[384,768]{1,0:T(8,128)S(1)}, f32[384,768]{1,0:T(8,128)S(1)}) custom-call(bf16[192,2176]{1,0:T(8,128)(2,1)S(1)} %bitcast.31, bf16[192,2176]{1,0:T(8,128)(2,1)S(1)} %collective-permute-done.8.refs_1_.refs_2_, bf16[2048,768]{1,0:T(8,128)(2,1)S(1)} %bitcast.35, bf16[2048,768]{1,0:T(8,128)(2,1)S(1)} %bitcast.38), custom_call_target="tpu_custom_call" | custom-call | flops 2415919104 | bytes 1 | tf_op jit(solution)/shard_map/base_products/pallas_call | solution.py:284
  51.6 1.9 %collective-permute-done.7.refs_0_.refs_1_ = bf16[64,2176]{1,0:T(8,128)(2,1)S(1)} collective-permute-done((bf16[64,2176]{1,0:T(8,128)(2,1)S(1)}, bf16[64,2176]{1,0:T(8,128)(2,1)S(1)}, u32[]{:S(2)}, u32[]{:S(2)}) %collective-permute-start.7) | collective-permute-done | bytes 278560 | tf_op jit(solution)/shard_map/ppermute | solution.py:34
  54.0 5.3 %collective-permute-done.12.refs_1_ = bf16[4,2,264,128]{3,2,1,0:T(8,128)(2,1)S(1)} collective-permute-done((bf16[4,2,264,128]{3,2,1,0:T(8,128)(2,1)S(1)}, bf16[4,2,264,128]{3,2,1,0:T(8,128)(2,1)S(1)}, u32[]{:S(2)}, u32[]{:S(2)}) %collective-permute-start.12) | collective-permute-done | bytes 540704 | tf_op jit(solution)/shard_map/ppermute | solution.py:419
  59.4 1.6 %relayout_factors.1 = (bf16[2048,128]{1,0:T(8,128)(2,1)S(1)}, bf16[64,768]{1,0:T(8,128)(2,1)S(1)}, bf16[64,768]{1,0:T(8,128)(2,1)S(1)}, bf16[768,128]{1,0:T(8,128)(2,1)S(1)}, bf16[64,2048]{1,0:T(8,128)(2,1)S(1)}) custom-call(s32[2]{0:T(128)S(1)} %copy-done.3, bf16[4,2,264,128]{3,2,1,0:T(8,128)(2,1)S(1)} %pad_maximum_fusion.1.refs_0_, ...), custom_call_target="tpu_custom_call" | custom-call | flops 1 | bytes 1 | tf_op jit(solution)/shard_map/relayout_factors/pallas_call | solution.py:209
  61.0 2.0 %base_products.4 = (f32[128,768]{1,0:T(8,128)S(1)}, f32[128,768]{1,0:T(8,128)S(1)}) custom-call(bf16[64,2176]{1,0:T(8,128)(2,1)S(1)} %collective-permute-done.7.refs_0_.refs_1_, bf16[64,2176]{1,0:T(8,128)(2,1)S(1)} %collective-permute-done.11.refs_1_.refs_3_, bf16[2048,768]{1,0:T(8,128)(2,1)S(1)} %bitcast.36, bf16[2048,768]{1,0:T(8,128)(2,1)S(1)} %bitcast.39), custom_call_target="tpu_custom_call" | custom-call | flops 1 | bytes 1 | tf_op jit(solution)/shard_map/base_products/pallas_call | solution.py:284
  63.0 6.2 %finish_step.3 = (f32[128,2048]{1,0:T(8,128)S(1)}, bf16[128,2048]{1,0:T(8,128)(2,1)S(1)}) custom-call(s32[2]{0:T(128)S(1)} %copy-done.3, bf16[192,2176]{1,0:T(8,128)(2,1)S(1)} %bitcast.32, bf16[64,2176]{1,0:T(8,128)(2,1)S(1)} %collective-permute-done.7.refs_0_.refs_1_, bf16[192,2176]{1,0:T(8,128)(2,1)S(1)} %collective-permute-done.8.refs_1_.refs_2_, ...), custom_call_target="tpu_custom_call" | custom-call | flops 1 | bytes 1 | tf_op jit(solution)/shard_map/finish_step/pallas_call | solution.py:375
  69.8 1.4 %collective-permute-done.13 = bf16[128,2048]{1,0:T(8,128)(2,1)S(1)} collective-permute-done((bf16[128,2048]{1,0:T(8,128)(2,1)S(1)}, bf16[128,2048]{1,0:T(8,128)(2,1)S(1)}, u32[]{:S(2)}, u32[]{:S(2)}) %collective-permute-start.13) | collective-permute-done | bytes 524320 | tf_op jit(solution)/shard_map/ppermute | solution.py:34
  72.0 1.6 %collective-permute-start.15 = (bf16[64,2048]{1,0:T(8,128)(2,1)S(1)}, bf16[64,2048]{1,0:T(8,128)(2,1)S(1)}, u32[]{:S(2)}, u32[]{:S(2)}) collective-permute-start(bf16[64,2048]{1,0:T(8,128)(2,1)S(1)} %slice.182), channel_id=1, source_target_pairs={{0,2},{1,3},{2,0},{3,1},{4,6},{5,7},{6,4},{7,5},{8,10},{9,11},{10,... | collective-permute-start | bytes 786440 | tf_op jit(solution)/shard_map/ppermute | solution.py:34
  73.6 3.4 %base_products.5 = (f32[256,768]{1,0:T(8,128)S(1)}, f32[256,768]{1,0:T(8,128)S(1)}) custom-call(bf16[128,2176]{1,0:T(8,128)(2,1)S(1)} %collective-permute-done.9.refs_0_.refs_1_, bf16[128,2176]{1,0:T(8,128)(2,1)S(1)} %collective-permute-done.10.refs_1_.refs_3_, bf16[2048,768]{1,0:T(8,128)(2,1)S(1)} %bitcast.37, bf16[2048,768]{1,0:T(8,128)(2,1)S(1)} %bitcast.40), custom_call_target="tpu_custom_call" | custom-call | flops 1 | bytes 1 | tf_op jit(solution)/shard_map/base_products/pallas_call | solution.py:284
  77.0 6.2 %finish_step.4 = (f32[128,2048]{1,0:T(8,128)S(1)}, bf16[128,2048]{1,0:T(8,128)(2,1)S(1)}) custom-call(s32[2]{0:T(128)S(1)} %copy-done.3, bf16[192,2176]{1,0:T(8,128)(2,1)S(1)} %bitcast.33, bf16[128,2176]{1,0:T(8,128)(2,1)S(1)} %collective-permute-done.9.refs_0_.refs_1_, bf16[192,2176]{1,0:T(8,128)(2,1)S(1)} %collective-permute-done.8.refs_1_.refs_2_, ...), custom_call_target="tpu_custom_call" | custom-call | flops 1 | bytes 1 | tf_op jit(solution)/shard_map/finish_step/pallas_call | solution.py:375
  83.4 1.8 %collective-permute-done.14 = bf16[128,2048]{1,0:T(8,128)(2,1)S(1)} collective-permute-done((bf16[128,2048]{1,0:T(8,128)(2,1)S(1)}, bf16[128,2048]{1,0:T(8,128)(2,1)S(1)}, u32[]{:S(2)}, u32[]{:S(2)}) %collective-permute-start.14) | collective-permute-done | bytes 524320 | tf_op jit(solution)/shard_map/ppermute | solution.py:34
  85.5 6.2 %finish_step.5 = (f32[128,2048]{1,0:T(8,128)S(1)}, bf16[128,2048]{1,0:T(8,128)(2,1)S(1)}) custom-call(s32[2]{0:T(128)S(1)} %copy-done.3, bf16[192,2176]{1,0:T(8,128)(2,1)S(1)} %bitcast.34, bf16[128,2176]{1,0:T(8,128)(2,1)S(1)} %collective-permute-done.9.refs_0_.refs_1_, bf16[192,2176]{1,0:T(8,128)(2,1)S(1)} %collective-permute-done.8.refs_1_.refs_2_, ...), custom_call_target="tpu_custom_call" | custom-call | flops 2415919104 | bytes 1 | tf_op jit(solution)/shard_map/finish_step/pallas_call | solution.py:375
  92.0 2.2 %collective-permute-start.17 = (bf16[16,2048]{1,0:T(8,128)(2,1)S(1)}, bf16[16,2048]{1,0:T(8,128)(2,1)S(1)}, u32[]{:S(2)}, u32[]{:S(2)}) collective-permute-start(bf16[16,2048]{1,0:T(8,128)(2,1)S(1)} %slice.188), channel_id=1, source_target_pairs={{0,8},{1,9},{2,10},{3,11},{4,12},{5,13},{6,14},{7,15},{8,0},{9,1},... | collective-permute-start | bytes 196616 | tf_op jit(solution)/shard_map/ppermute | solution.py:34
  94.8 2.5 %collective-permute-done.17 = bf16[16,2048]{1,0:T(8,128)(2,1)S(1)} collective-permute-done((bf16[16,2048]{1,0:T(8,128)(2,1)S(1)}, bf16[16,2048]{1,0:T(8,128)(2,1)S(1)}, u32[]{:S(2)}, u32[]{:S(2)}) %collective-permute-start.17) | collective-permute-done | bytes 65568 | tf_op jit(solution)/shard_map/ppermute | solution.py:34
  98.1 5.4 %collective-permute-done.18 = bf16[64,2048]{1,0:T(8,128)(2,1)S(1)} collective-permute-done((bf16[64,2048]{1,0:T(8,128)(2,1)S(1)}, bf16[64,2048]{1,0:T(8,128)(2,1)S(1)}, u32[]{:S(2)}, u32[]{:S(2)}) %collective-permute-start.18) | collective-permute-done | bytes 262176 | tf_op jit(solution)/shard_map/ppermute | solution.py:34
  103.7 4.6 %collective-permute-done.22 = bf16[64,2048]{1,0:T(8,128)(2,1)S(1)} collective-permute-done((bf16[64,2048]{1,0:T(8,128)(2,1)S(1)}, bf16[64,2048]{1,0:T(8,128)(2,1)S(1)}, u32[]{:S(2)}, u32[]{:S(2)}) %collective-permute-start.22) | collective-permute-done | bytes 262176 | tf_op jit(solution)/shard_map/ppermute | solution.py:34
  108.7 2.6 %collective-permute-start.20 = (bf16[16,2048]{1,0:T(8,128)(2,1)S(1)}, bf16[16,2048]{1,0:T(8,128)(2,1)S(1)}, u32[]{:S(2)}, u32[]{:S(2)}) collective-permute-start(bf16[16,2048]{1,0:T(8,128)(2,1)S(1)} %slice.187), channel_id=1, source_target_pairs={{0,8},{1,9},{2,10},{3,11},{4,12},{5,13},{6,14},{7,15},{8,0},{9,1},... | collective-permute-start | bytes 196616 | tf_op jit(solution)/shard_map/ppermute | solution.py:34
  111.3 3.4 %collective-permute-done.23 = bf16[32,2048]{1,0:T(8,128)(2,1)S(1)} collective-permute-done((bf16[32,2048]{1,0:T(8,128)(2,1)S(1)}, bf16[32,2048]{1,0:T(8,128)(2,1)S(1)}, u32[]{:S(2)}, u32[]{:S(2)}) %collective-permute-start.23) | collective-permute-done | bytes 131104 | tf_op jit(solution)/shard_map/ppermute | solution.py:34
  115.0 4.9 %collective-permute-done.24 = bf16[16,2048]{1,0:T(8,128)(2,1)S(1)} collective-permute-done((bf16[16,2048]{1,0:T(8,128)(2,1)S(1)}, bf16[16,2048]{1,0:T(8,128)(2,1)S(1)}, u32[]{:S(2)}, u32[]{:S(2)}) %collective-permute-start.24) | collective-permute-done | bytes 65568 | tf_op jit(solution)/shard_map/ppermute | solution.py:34
  (72 shorter events, 9.1 us)
Async XLA Ops:
  3.8 19.0 %collective-permute-start.2 = (bf16[4,264,128]{2,1,0:T(8,128)(2,1)}, bf16[4,264,128]{2,1,0:T(8,128)(2,1)S(1)}, u32[]{:S(2)}, u32[]{:S(2)}) collective-permute-start(bf16[4,264,128]{2,1,0:T(8,128)(2,1)} %get-tuple-element.52), channel_id=1, source_target_pairs={{0,2},{1,3},{2,0},{3,1},{4,6},{5,7},{6,4},{7,5},{8,10},{9,11},{10,... | collective-permute-start | bytes 811016 | tf_op jit(solution)/shard_map/ppermute | solution.py:34
  8.8 12.2 %collective-permute-start = (bf16[48,2176]{1,0:T(8,128)(2,1)}, bf16[48,2176]{1,0:T(8,128)(2,1)S(1)}, u32[]{:S(2)}, u32[]{:S(2)}) collective-permute-start(bf16[48,2176]{1,0:T(8,128)(2,1)} %payload.1), channel_id=1, source_target_pairs={{0,8},{1,9},{2,10},{3,11},{4,12},{5,13},{6,14},{7,15},{8,0},{9,1},... | collective-permute-start | bytes 626696 | tf_op jit(solution)/shard_map/ppermute | solution.py:34
  12.4 31.7 %copy-start.4 = (bf16[48,2176]{1,0:T(8,128)(2,1)S(1)}, bf16[48,2176]{1,0:T(8,128)(2,1)}, u32[]{:S(2)}) copy-start(bf16[48,2176]{1,0:T(8,128)(2,1)} %payload.1) | copy-start | bytes 626692
  22.0 22.1 %collective-permute-start.1 = (bf16[96,2176]{1,0:T(8,128)(2,1)S(1)}, bf16[96,2176]{1,0:T(8,128)(2,1)S(1)}, u32[]{:S(2)}, u32[]{:S(2)}) collective-permute-start(bf16[96,2176]{1,0:T(8,128)(2,1)S(1)} %pad_maximum_fusion.2), channel_id=1, source_target_pairs={{0,4},{1,5},{2,6},{3,7},{4,0},{5,1},{6,2},{7,3},{8,12},{9,13},{10,... | collective-permute-start | bytes 1253384 | tf_op jit(solution)/shard_map/ppermute | solution.py:34
  22.9 5.7 %collective-permute-start.3 = (bf16[2,264,128]{2,1,0:T(8,128)(2,1)S(1)}, bf16[2,264,128]{2,1,0:T(8,128)(2,1)S(1)}, u32[]{:S(2)}, u32[]{:S(2)}) collective-permute-start(bf16[2,264,128]{2,1,0:T(8,128)(2,1)S(1)} %pad_maximum_fusion.4), channel_id=1, source_target_pairs={{0,0},{1,1},{2,2},{3,3},{4,4},{5,5},{6,6},{7,7},{8,8},{9,9},{10,10... | collective-permute-start | bytes 405512 | tf_op jit(solution)/shard_map/ppermute | solution.py:64
  23.6 14.9 %collective-permute-start.4 = (bf16[2,264,128]{2,1,0:T(8,128)(2,1)S(1)}, bf16[2,264,128]{2,1,0:T(8,128)(2,1)S(1)}, u32[]{:S(2)}, u32[]{:S(2)}) collective-permute-start(bf16[2,264,128]{2,1,0:T(8,128)(2,1)S(1)} %pad_maximum_fusion.5), channel_id=1, source_target_pairs={{0,4},{1,5},{2,6},{3,7},{4,0},{5,1},{6,2},{7,3},{8,12},{9,13},{10,... | collective-permute-start | bytes 405512 | tf_op jit(solution)/shard_map/ppermute | solution.py:64
  24.9 13.7 %collective-permute-start.5 = (bf16[2,264,128]{2,1,0:T(8,128)(2,1)S(1)}, bf16[2,264,128]{2,1,0:T(8,128)(2,1)S(1)}, u32[]{:S(2)}, u32[]{:S(2)}) collective-permute-start(bf16[2,264,128]{2,1,0:T(8,128)(2,1)S(1)} %pad_maximum_fusion.6), channel_id=1, source_target_pairs={{0,8},{1,9},{2,10},{3,11},{4,12},{5,13},{6,14},{7,15},{8,0},{9,1},... | collective-permute-start | bytes 405512 | tf_op jit(solution)/shard_map/ppermute | solution.py:64
  27.0 19.7 %copy-start.2 = (bf16[1,2048,768]{2,1,0:T(8,128)(2,1)S(1)}, bf16[1,2048,768]{2,1,0:T(8,128)(2,1)}, u32[]{:S(2)}) copy-start(bf16[1,2048,768]{2,1,0:T(8,128)(2,1)} %param.14) | copy-start | bytes 9437188
  27.0 17.0 %collective-permute-start.6 = (bf16[2,264,128]{2,1,0:T(8,128)(2,1)S(1)}, bf16[2,264,128]{2,1,0:T(8,128)(2,1)S(1)}, u32[]{:S(2)}, u32[]{:S(2)}) collective-permute-start(bf16[2,264,128]{2,1,0:T(8,128)(2,1)S(1)} %pad_maximum_fusion.7), channel_id=1, source_target_pairs={{0,12},{1,13},{2,14},{3,15},{4,8},{5,9},{6,10},{7,11},{8,4},{9,5},... | collective-permute-start | bytes 405512 | tf_op jit(solution)/shard_map/ppermute | solution.py:64
  44.2 2.5 %copy-start.1 = (bf16[1,2048,768]{2,1,0:T(8,128)(2,1)S(1)}, bf16[1,2048,768]{2,1,0:T(8,128)(2,1)}, u32[]{:S(2)}) copy-start(bf16[1,2048,768]{2,1,0:T(8,128)(2,1)} %param.13) | copy-start | bytes 9437188
  44.3 2.4 %collective-permute-start.8 = (bf16[192,2176]{1,0:T(8,128)(2,1)S(1)}, bf16[192,2176]{1,0:T(8,128)(2,1)S(1)}, u32[]{:S(2)}, u32[]{:S(2)}) collective-permute-start(bf16[192,2176]{1,0:T(8,128)(2,1)S(1)} %bitcast.28), channel_id=1, source_target_pairs={{0,1},{1,0},{2,3},{3,2},{4,5},{5,4},{6,7},{7,6},{8,9},{9,8},{10,11... | collective-permute-start | bytes 2506760 | tf_op jit(solution)/shard_map/ppermute | solution.py:34
  44.4 9.1 %collective-permute-start.7 = (bf16[64,2176]{1,0:T(8,128)(2,1)S(1)}, bf16[64,2176]{1,0:T(8,128)(2,1)S(1)}, u32[]{:S(2)}, u32[]{:S(2)}) collective-permute-start(bf16[64,2176]{1,0:T(8,128)(2,1)S(1)} %bitcast.43), channel_id=1, source_target_pairs={{0,2},{1,3},{2,0},{3,1},{4,6},{5,7},{6,4},{7,5},{8,10},{9,11},{10,... | collective-permute-start | bytes 835592 | tf_op jit(solution)/shard_map/ppermute | solution.py:34
  45.0 14.4 %collective-permute-start.12 = (bf16[4,2,264,128]{3,2,1,0:T(8,128)(2,1)S(1)}, bf16[4,2,264,128]{3,2,1,0:T(8,128)(2,1)S(1)}, u32[]{:S(2)}, u32[]{:S(2)}) collective-permute-start(bf16[4,2,264,128]{3,2,1,0:T(8,128)(2,1)S(1)} %pad_maximum_fusion.1.refs_0_), channel_id=1, source_target_pairs={{0,16},{16,0},{1,17},{17,1},{2,18},{18,2},{3,19},{19,3},{4,20},{20... | collective-permute-start | bytes 1622024 | tf_op jit(solution)/shard_map/ppermute | solution.py:419
  46.7 12.6 %copy-start.3 = (s32[2]{0:T(128)S(1)}, s32[2]{0:T(128)}, u32[]{:S(2)}) copy-start(s32[2]{0:T(128)} %pad_add_fusion.place_ref) | copy-start | bytes 28
  53.5 7.4 %collective-permute-start.11 = (bf16[64,2176]{1,0:T(8,128)(2,1)S(1)}, bf16[64,2176]{1,0:T(8,128)(2,1)S(1)}, u32[]{:S(2)}, u32[]{:S(2)}) collective-permute-start(bf16[64,2176]{1,0:T(8,128)(2,1)S(1)} %collective-permute-done.7.refs_0_.refs_1_), channel_id=1, source_target_pairs={{0,1},{1,0},{2,3},{3,2},{4,5},{5,4},{6,7},{7,6},{8,9},{9,8},{10,11... | collective-permute-start | bytes 835592 | tf_op jit(solution)/shard_map/ppermute | solution.py:34
  53.5 15.8 %collective-permute-start.9 = (bf16[128,2176]{1,0:T(8,128)(2,1)S(1)}, bf16[128,2176]{1,0:T(8,128)(2,1)S(1)}, u32[]{:S(2)}, u32[]{:S(2)}) collective-permute-start(bf16[128,2176]{1,0:T(8,128)(2,1)S(1)} %bitcast.42), channel_id=1, source_target_pairs={{0,2},{1,3},{2,0},{3,1},{4,6},{5,7},{6,4},{7,5},{8,10},{9,11},{10,... | collective-permute-start | bytes 1671176 | tf_op jit(solution)/shard_map/ppermute | solution.py:34
  61.0 2.0 %copy-start = (bf16[1,768,2048]{2,1,0:T(8,128)(2,1)S(1)}, bf16[1,768,2048]{2,1,0:T(8,128)(2,1)}, u32[]{:S(2)}) copy-start(bf16[1,768,2048]{2,1,0:T(8,128)(2,1)} %param.15) | copy-start | bytes 9437188
  69.2 2.0 %collective-permute-start.13 = (bf16[128,2048]{1,0:T(8,128)(2,1)S(1)}, bf16[128,2048]{1,0:T(8,128)(2,1)S(1)}, u32[]{:S(2)}, u32[]{:S(2)}) collective-permute-start(bf16[128,2048]{1,0:T(8,128)(2,1)S(1)} %get-tuple-element.69), channel_id=1, source_target_pairs={{0,1},{1,0},{2,3},{3,2},{4,5},{5,4},{6,7},{7,6},{8,9},{9,8},{10,11... | collective-permute-start | bytes 1572872 | tf_op jit(solution)/shard_map/ppermute | solution.py:34
  69.3 2.7 %collective-permute-start.10 = (bf16[128,2176]{1,0:T(8,128)(2,1)S(1)}, bf16[128,2176]{1,0:T(8,128)(2,1)S(1)}, u32[]{:S(2)}, u32[]{:S(2)}) collective-permute-start(bf16[128,2176]{1,0:T(8,128)(2,1)S(1)} %collective-permute-done.9.refs_0_.refs_1_), channel_id=1, source_target_pairs={{0,1},{1,0},{2,3},{3,2},{4,5},{5,4},{6,7},{7,6},{8,9},{9,8},{10,11... | collective-permute-start | bytes 1671176 | tf_op jit(solution)/shard_map/ppermute | solution.py:34
  72.0 11.4 %collective-permute-start.15 = (bf16[64,2048]{1,0:T(8,128)(2,1)S(1)}, bf16[64,2048]{1,0:T(8,128)(2,1)S(1)}, u32[]{:S(2)}, u32[]{:S(2)}) collective-permute-start(bf16[64,2048]{1,0:T(8,128)(2,1)S(1)} %slice.182), channel_id=1, source_target_pairs={{0,2},{1,3},{2,0},{3,1},{4,6},{5,7},{6,4},{7,5},{8,10},{9,11},{10,... | collective-permute-start | bytes 786440 | tf_op jit(solution)/shard_map/ppermute | solution.py:34
  83.3 2.0 %collective-permute-start.14 = (bf16[128,2048]{1,0:T(8,128)(2,1)S(1)}, bf16[128,2048]{1,0:T(8,128)(2,1)S(1)}, u32[]{:S(2)}, u32[]{:S(2)}) collective-permute-start(bf16[128,2048]{1,0:T(8,128)(2,1)S(1)} %get-tuple-element.77), channel_id=1, source_target_pairs={{0,1},{1,0},{2,3},{3,2},{4,5},{5,4},{6,7},{7,6},{8,9},{9,8},{10,11... | collective-permute-start | bytes 1572872 | tf_op jit(solution)/shard_map/ppermute | solution.py:34
  85.4 6.5 %collective-permute-start.16 = (bf16[32,2048]{1,0:T(8,128)(2,1)S(1)}, bf16[32,2048]{1,0:T(8,128)(2,1)S(1)}, u32[]{:S(2)}, u32[]{:S(2)}) collective-permute-start(bf16[32,2048]{1,0:T(8,128)(2,1)S(1)} %slice.185), channel_id=1, source_target_pairs={{0,4},{1,5},{2,6},{3,7},{4,0},{5,1},{6,2},{7,3},{8,12},{9,13},{10,... | collective-permute-start | bytes 393224 | tf_op jit(solution)/shard_map/ppermute | solution.py:34
  91.7 5.6 %collective-permute-start.21 = (bf16[128,2048]{1,0:T(8,128)(2,1)S(1)}, bf16[128,2048]{1,0:T(8,128)(2,1)S(1)}, u32[]{:S(2)}, u32[]{:S(2)}) collective-permute-start(bf16[128,2048]{1,0:T(8,128)(2,1)S(1)} %get-tuple-element.90), channel_id=1, source_target_pairs={{0,1},{1,0},{2,3},{3,2},{4,5},{5,4},{6,7},{7,6},{8,9},{9,8},{10,11... | collective-permute-start | bytes 1572872 | tf_op jit(solution)/shard_map/ppermute | solution.py:34
  92.0 5.3 %collective-permute-start.17 = (bf16[16,2048]{1,0:T(8,128)(2,1)S(1)}, bf16[16,2048]{1,0:T(8,128)(2,1)S(1)}, u32[]{:S(2)}, u32[]{:S(2)}) collective-permute-start(bf16[16,2048]{1,0:T(8,128)(2,1)S(1)} %slice.188), channel_id=1, source_target_pairs={{0,8},{1,9},{2,10},{3,11},{4,12},{5,13},{6,14},{7,15},{8,0},{9,1},... | collective-permute-start | bytes 196616 | tf_op jit(solution)/shard_map/ppermute | solution.py:34
  94.3 9.2 %collective-permute-start.18 = (bf16[64,2048]{1,0:T(8,128)(2,1)S(1)}, bf16[64,2048]{1,0:T(8,128)(2,1)S(1)}, u32[]{:S(2)}, u32[]{:S(2)}) collective-permute-start(bf16[64,2048]{1,0:T(8,128)(2,1)S(1)} %slice.181), channel_id=1, source_target_pairs={{0,2},{1,3},{2,0},{3,1},{4,6},{5,7},{6,4},{7,5},{8,10},{9,11},{10,... | collective-permute-start | bytes 786440 | tf_op jit(solution)/shard_map/ppermute | solution.py:34
  97.5 10.8 %collective-permute-start.22 = (bf16[64,2048]{1,0:T(8,128)(2,1)S(1)}, bf16[64,2048]{1,0:T(8,128)(2,1)S(1)}, u32[]{:S(2)}, u32[]{:S(2)}) collective-permute-start(bf16[64,2048]{1,0:T(8,128)(2,1)S(1)} %slice.180), channel_id=1, source_target_pairs={{0,2},{1,3},{2,0},{3,1},{4,6},{5,7},{6,4},{7,5},{8,10},{9,11},{10,... | collective-permute-start | bytes 786440 | tf_op jit(solution)/shard_map/ppermute | solution.py:34
  103.6 5.0 %collective-permute-start.19 = (bf16[32,2048]{1,0:T(8,128)(2,1)S(1)}, bf16[32,2048]{1,0:T(8,128)(2,1)S(1)}, u32[]{:S(2)}, u32[]{:S(2)}) collective-permute-start(bf16[32,2048]{1,0:T(8,128)(2,1)S(1)} %slice.184), channel_id=1, source_target_pairs={{0,4},{1,5},{2,6},{3,7},{4,0},{5,1},{6,2},{7,3},{8,12},{9,13},{10,... | collective-permute-start | bytes 393224 | tf_op jit(solution)/shard_map/ppermute | solution.py:34
  108.4 6.3 %collective-permute-start.23 = (bf16[32,2048]{1,0:T(8,128)(2,1)S(1)}, bf16[32,2048]{1,0:T(8,128)(2,1)S(1)}, u32[]{:S(2)}, u32[]{:S(2)}) collective-permute-start(bf16[32,2048]{1,0:T(8,128)(2,1)S(1)} %slice.183), channel_id=1, source_target_pairs={{0,4},{1,5},{2,6},{3,7},{4,0},{5,1},{6,2},{7,3},{8,12},{9,13},{10,... | collective-permute-start | bytes 393224 | tf_op jit(solution)/shard_map/ppermute | solution.py:34
  108.7 6.4 %collective-permute-start.20 = (bf16[16,2048]{1,0:T(8,128)(2,1)S(1)}, bf16[16,2048]{1,0:T(8,128)(2,1)S(1)}, u32[]{:S(2)}, u32[]{:S(2)}) collective-permute-start(bf16[16,2048]{1,0:T(8,128)(2,1)S(1)} %slice.187), channel_id=1, source_target_pairs={{0,8},{1,9},{2,10},{3,11},{4,12},{5,13},{6,14},{7,15},{8,0},{9,1},... | collective-permute-start | bytes 196616 | tf_op jit(solution)/shard_map/ppermute | solution.py:34
  114.8 5.2 %collective-permute-start.24 = (bf16[16,2048]{1,0:T(8,128)(2,1)S(1)}, bf16[16,2048]{1,0:T(8,128)(2,1)S(1)}, u32[]{:S(2)}, u32[]{:S(2)}) collective-permute-start(bf16[16,2048]{1,0:T(8,128)(2,1)S(1)} %slice.186), channel_id=1, source_target_pairs={{0,8},{1,9},{2,10},{3,11},{4,12},{5,13},{6,14},{7,15},{8,0},{9,1},... | collective-permute-start | bytes 196616 | tf_op jit(solution)/shard_map/ppermute | solution.py:34

commit v13 on v12

--- a/solution.py
+++ b/solution.py
@@ -12,6 +12,7 @@
 GRANT = 16 << 20
 EXPERT_GRANT = 32 << 20
 WHOLE_GRANT = 60 << 20
+MUCH = pl.CostEstimate(flops=1 << 33, bytes_accessed=1, transcendentals=0)
 LITTLE = pl.CostEstimate(flops=1, bytes_accessed=1, transcendentals=0)
 
 
@@ -34,44 +35,45 @@
     return lax.ppermute(x, "expert", [(i, i ^ (k * stride)) for i in range(n)])
 
 
-def double_along(x, n, stride, size):
+def double_along(arrays, n, stride, size, first=lambda arrays: arrays):
     step = size // 2
     while step:
-        x = jnp.concatenate([x, swap(x, n, stride, step)])
+        arrays = [jnp.concatenate([x, swap(x, n, stride, step)]) for x in arrays]
+        if step == size // 2:
+            arrays = first(arrays)
         step //= 2
-    return x
-
-
-def halve_along(total, n, stride, size):
-    step = 1
-    while step < size:
-        half = total.shape[0] // 2
-        sent = swap(total[half:].astype(jnp.bfloat16), n, stride, step)
-        total = total[:half] + sent.astype(jnp.float32)
-        step *= 2
-    return total
-
-
-def exchange_factors(blocks, n):
-    outer, middle, cores = split_axis(n)
+    return arrays
+
+
+def scatter_along(total, n, stride, size):
+    places = [0]
+    step = size // 2
+    while step:
+        places += [k ^ step for k in places]
+        step //= 2
+    count = total.shape[0] // size
+    result = total[:count]
+    for i in range(1, size):
+        part = total[i * count : (i + 1) * count].astype(jnp.bfloat16)
+        result = result + swap(part, n, stride, places[i]).astype(jnp.float32)
+    return result
+
+
+def exchange_factors(blocks, n, stride):
     here = []
-    for q in range(outer):
-        pairs = []
-        for g in range(2):
-            for i in range(n):
-                pairs.append((g * n + i, g * n + (i ^ (q * middle * cores) ^ g)))
+    for q in range(blocks[0].shape[0]):
+        pairs = [(g * n + i, g * n + (i ^ (q * stride) ^ g)) for g in range(2) for i in range(n)]
         part = jnp.stack([block[q] for block in blocks])
         here.append(lax.ppermute(part, ("group", "expert"), pairs))
-    return here
+    return jnp.concatenate(here)
 
 
 def dot(a, b):
     return jnp.dot(a, b, preferred_element_type=jnp.float32)
 
 
-def payload_kernel(hidden_ref, ids_ref, logits_ref, out_ref, turned_ref):
+def gates_kernel(ids_ref, logits_ref, out_ref, turned_ref):
     steps, top, rows = ids_ref.shape
-    width = hidden_ref.shape[2]
     turned_ref[...] = jnp.zeros_like(turned_ref)
     for s in range(steps):
         logits, ids = logits_ref[s], ids_ref[s]
@@ -82,29 +84,26 @@
         for k in range(top):
             dense += jnp.where(ids[k : k + 1, :] == expert, gates[k : k + 1, :], 0.0)
         turned_ref[:, s * rows : (s + 1) * rows] = dense
-    dense = turned_ref[...].T.astype(jnp.bfloat16)
-    for s in range(steps):
-        out_ref[s * rows : (s + 1) * rows, :width] = hidden_ref[s]
-    out_ref[:, width:] = dense[: steps * rows]
-
-
-def make_payload(hidden, route_ids, route_logits, experts):
-    steps, rows, width = hidden.shape
+    out_ref[...] = turned_ref[...].T.astype(jnp.bfloat16)[: steps * rows]
+
+
+def dense_gates(route_ids, route_logits, experts):
+    steps, rows, _ = route_ids.shape
     padded = -(-experts // LANES) * LANES
     return pl.pallas_call(
-        payload_kernel,
-        out_shape=jax.ShapeDtypeStruct((steps * rows, width + padded), jnp.bfloat16),
+        gates_kernel,
+        out_shape=jax.ShapeDtypeStruct((steps * rows, padded), jnp.bfloat16),
         scratch_shapes=[pltpu.VMEM((padded, -(-steps * rows // LANES) * LANES), jnp.float32)],
         compiler_params=pltpu.CompilerParams(vmem_limit_bytes=WHOLE_GRANT),
-        cost_estimate=LITTLE,
-        name="payload",
-    )(hidden, jnp.swapaxes(route_ids, 1, 2), jnp.swapaxes(route_logits, 1, 2))
-
-
-def order_kernel(middle, place_ref, placement_ref, factors_ref, *refs):
-    out_refs, wide_ref = refs[:-1], refs[-1]
+        cost_estimate=MUCH,
+        name="dense_gates",
+    )(jnp.swapaxes(route_ids, 1, 2), jnp.swapaxes(route_logits, 1, 2))
+
+
+def order_kernel(place_ref, placement_ref, factors_ref, *refs):
+    out_refs, wide_ref, slot_ref = refs[:-2], refs[-2], refs[-1]
     slots = factors_ref.shape[0]
-    length, lanes = out_refs[0].shape[1:]
+    outer, length, lanes = out_refs[0].shape
     group, me = place_ref[0], place_ref[1]
 
     def cut(t, carry):
@@ -114,57 +113,48 @@
         return carry
 
     lax.fori_loop(0, length, cut, 0, unroll=8)
-
-    def put(s, carry):
-        to = placement_ref[s]
-        away = to ^ me
-        aside, ahead = lax.rem(away // 2, middle), away // (2 * middle)
-        ours = lax.rem(away, 2) == group
-        rows = wide_ref[pl.ds(pl.multiple_of(s * length, 8), length), :].astype(jnp.bfloat16)
-        for r, out_ref in enumerate(out_refs):
-
-            @pl.when(jnp.logical_and(ours, aside == r))
-            def _():
-                out_ref[ahead] = rows
-
-        return carry
-
-    lax.fori_loop(0, slots, put, 0)
-
-
-def order_factors(place, placement, factors, n):
-    outer, middle, _ = split_axis(n)
+    for s in range(slots):
+        slot_ref[placement_ref[s]] = s
+    for r, out_ref in enumerate(out_refs):
+        for q in range(outer):
+            slot = slot_ref[me ^ (2 * (q * len(out_refs) + r) + group)]
+            rows = wide_ref[pl.ds(pl.multiple_of(slot * length, 8), length), :]
+            out_ref[q] = rows.astype(jnp.bfloat16)
+
+
+def order_factors(place, placement, factors, outer, middle):
     slots, entries = factors.shape
     length = entries // LANES
     return pl.pallas_call(
-        functools.partial(order_kernel, middle),
+        order_kernel,
         out_shape=[jax.ShapeDtypeStruct((outer, length, LANES), jnp.bfloat16)] * middle,
         in_specs=[
             pl.BlockSpec(memory_space=pltpu.SMEM),
             pl.BlockSpec(memory_space=pltpu.SMEM),
             pl.BlockSpec(memory_space=pltpu.VMEM),
         ],
-        scratch_shapes=[pltpu.VMEM((slots * length, LANES), jnp.float32)],
+        scratch_shapes=[
+            pltpu.VMEM((slots * length, LANES), jnp.float32),
+            pltpu.SMEM((slots,), jnp.int32),
+        ],
         compiler_params=pltpu.CompilerParams(vmem_limit_bytes=WHOLE_GRANT),
-        cost_estimate=LITTLE,
+        cost_estimate=MUCH,
         name="order_factors",
     )(place, placement, factors)
 
 
-def relayout_kernel(middle, place_ref, *refs):
+def relayout_kernel(place_ref, *refs):
     parts, refs = refs[:2], refs[2:]
     a_gu_ref, gate_b_ref, up_b_ref, down_a_ref, down_b_ref, flat_ref, wide_ref = refs
     width, units = a_gu_ref.shape[0], gate_b_ref.shape[1]
     rank = gate_b_ref.shape[0]
-    outer, _, length, _ = parts[0].shape
+    chips, length, _ = parts[0].shape
     group, me = place_ref[0], place_ref[1]
     for swapped, part in enumerate(parts):
         core = group if swapped == 0 else 1 - group
-        for q in range(outer):
-            for r in range(middle):
-                source = me ^ ((q * middle + r) * 2 + core)
-                start = pl.multiple_of(source * length, 8)
-                flat_ref[pl.ds(start, length), :] = part[q, r].astype(jnp.float32)
+        for d in range(chips):
+            start = pl.multiple_of((me ^ (2 * d + core)) * length, 8)
+            flat_ref[pl.ds(start, length), :] = part[d].astype(jnp.float32)
 
     n_wide, n_unit = width // 2, units // 2
     at_ub = 2 * n_wide + n_unit
@@ -203,11 +193,10 @@
 
 
 def relayout_factors(place, here, there, width, units, rank, n):
-    middle = split_axis(n)[1]
     shapes = [(width, 2 * rank), (rank, units), (rank, units), (units, 2 * rank), (rank, width)]
-    length = here.shape[2]
+    length = here.shape[1]
     return pl.pallas_call(
-        functools.partial(relayout_kernel, middle),
+        relayout_kernel,
         out_shape=[jax.ShapeDtypeStruct(shape, jnp.bfloat16) for shape in shapes],
         in_specs=[pl.BlockSpec(memory_space=pltpu.SMEM)]
         + [pl.BlockSpec(memory_space=pltpu.VMEM)] * 2,
@@ -409,16 +398,22 @@
     along_outer, along_middle = (middle * cores, outer), (cores, middle)
     place = jnp.stack([lax.axis_index("group"), lax.axis_index("expert")]).astype(jnp.int32)
 
-    blocks = order_factors(place, placement, factors, owners)
-    hidden, blocks = lax.optimization_barrier((hidden, blocks))
-    rows_in = make_payload(hidden, route_ids, route_logits, experts)
+    blocks = order_factors(place, placement, factors, outer, middle)
     blocks = [blocks[0]] + [swap(blocks[r], owners, cores, r) for r in range(1, middle)]
-    here = jnp.stack(exchange_factors(blocks, owners))
-    column = double_along(rows_in, owners, *along_outer)
-    column, here = lax.optimization_barrier((column, here))
+    gates = dense_gates(route_ids, route_logits, experts)
+    arrays = [hidden.reshape(steps * rows, width), gates]
+
+    def after_first(arrays):
+        nonlocal blocks
+        arrays, blocks = lax.optimization_barrier((arrays, blocks))
+        return arrays
+
+    column, gates = double_along(arrays, owners, *along_outer, after_first)
+    here = exchange_factors(blocks, owners, along_outer[0])
+    column, gates, here = lax.optimization_barrier((column, gates, here))
     there = lax.ppermute(here, "group", [(0, 1), (1, 0)])
-    column = jnp.swapaxes(column.reshape(outer, steps, rows, -1), 0, 1)
-    column = column.reshape(steps * outer * rows, -1)
+    column = jnp.concatenate([column, gates], axis=1).reshape(outer, steps, rows, -1)
+    column = jnp.swapaxes(column, 0, 1).reshape(steps * outer * rows, -1)
     span = outer * rows
     weights = (w_gate[0], w_up[0])
 
@@ -429,9 +424,7 @@
         return [swap(part, owners, cores, r) for r in range(1, middle)]
 
     near = with_other_core(column)
-    flops = 8 * near[0].shape[0] * width * units
-    cost = pl.CostEstimate(flops=flops, bytes_accessed=1, transcendentals=0)
-    near_base = base_products(near, *weights, cost)
+    near_base = base_products(near, *weights, MUCH)
     far, near_base, rest = lax.optimization_barrier(
         (along_middle_of(column[:span]), near_base, column[span:])
     )
@@ -440,7 +433,7 @@
     far_base = [base_products(pair, *weights, LITTLE) for pair in far]
     low_rank = relayout_factors(place, here, there, width, units, rank, owners)
 
-    summed, across = [], []
+    summed = []
     for s in range(steps):
         if s == 1:
             far = [with_other_core(part) for part in rest_far]
@@ -450,17 +443,14 @@
         firsts = [s * span] + [at] * len(far)
         pieces = [pair[0] for pair in pairs] + [pair[1] for pair in pairs]
         base = [b for pair in [near_base] + far_base for b in pair]
-        if s >= 1:
-            pieces, summed[s - 1] = lax.optimization_barrier((pieces, summed[s - 1]))
-            across.append(halve_along(summed[s - 1], owners, *along_middle))
         if s >= 2:
-            pieces, across[s - 2] = lax.optimization_barrier((pieces, across[s - 2]))
+            pieces, summed[s - 2] = lax.optimization_barrier((pieces, summed[s - 2]))
         kept, sent = finish_step(
-            place, pieces, base, firsts * 2, span, low_rank, down_weight[0], cost if s >= 2 else LITTLE
+            place, pieces, base, firsts * 2, span, low_rank, down_weight[0], LITTLE
         )
         summed.append(kept + swap(sent, owners, 1, 1).astype(jnp.float32))
-    across.append(halve_along(summed[-1], owners, *along_middle))
-    results = [halve_along(total, owners, *along_outer) for total in across]
+    results = [scatter_along(total, owners, *along_middle) for total in summed]
+    results = [scatter_along(total, owners, *along_outer) for total in results]
     return jnp.stack(results).astype(jnp.bfloat16)
 
 

time: 121 us -> 122 us (level)
  starting transfers between devices: 23.5 us -> 42.3 us
  waiting for transfers between devices: 56.6 us -> 40.1 us
    ppermute x4, waiting for transfers between devices: 15.5 us -> 3.54 us  [exchange_factors(): here.append(lax.ppermute(part, ('group', 'expert'), pairs))]
    ppermute x20 -> x25, starting transfers between devices: 16.6 us -> 28.4 us  [swap(): return lax.ppermute(x, 'expert', [(i, i ^ k * stride) for i in range(n)])]
    ppermute x20 -> x25, waiting for transfers between devices: 35.8 us -> 29.5 us  [swap(): return lax.ppermute(x, 'expert', [(i, i ^ k * stride) for i in range(n)])]
    ppermute x1, starting transfers between devices: 1.29 us -> 5.46 us  [dense_shards(): there = lax.ppermute(here, 'group', [(0, 1), (1, 0)])]
    ppermute x4, starting transfers between devices: 5.63 us -> 8.43 us  [exchange_factors(): here.append(lax.ppermute(part, ('group', 'expert'), pairs))]
    ppermute x1, waiting for transfers between devices: 5.33 us -> 7 us  [dense_shards(): there = lax.ppermute(here, 'group', [(0, 1), (1, 0)])]
  transfers between devices with their start and end apart: 25 -> 30, of which waited for: 16 -> 13; matrix products, arithmetic and copies ran while one was open for 2% -> 1% of each run, Pallas kernels for 27% -> 29%
where the time goes in v13:
time: 122 us
  starting transfers between devices  42.3 us (35%)
  waiting for transfers between devices  40.1 us (33%)
  Pallas kernels  35.1 us (29%)
  other arithmetic  2.27 us (2%)
  local copies, waits for them, and re-layouts  1.35 us (1%)
    ppermute x25, waiting for transfers between devices, swap(): return lax.ppermute(x, 'expert', [(i, i ^ k * stride) for i in range(n)])  29.5 us
    ppermute x25, starting transfers between devices, swap(): return lax.ppermute(x, 'expert', [(i, i ^ k * stride) for i in range(n)])  28.4 us
    pallas_call x3, Pallas kernels, finish_step(): pl.pallas_call(functools.partial(finish_kernel, firsts, rows), out_shape=...  18.7 us
    pallas_call x3, Pallas kernels, base_products(): pl.pallas_call(functools.partial(base_kernel, len(pieces)), out_shape=[ou...  10.3 us
    ppermute x4, starting transfers between devices, exchange_factors(): here.append(lax.ppermute(part, ('group', 'expert'), pairs))  8.43 us
    ppermute x1, waiting for transfers between devices, dense_shards(): there = lax.ppermute(here, 'group', [(0, 1), (1, 0)])  7 us
    ppermute x1, starting transfers between devices, dense_shards(): there = lax.ppermute(here, 'group', [(0, 1), (1, 0)])  5.46 us
    ppermute x4, waiting for transfers between devices, exchange_factors(): here.append(lax.ppermute(part, ('group', 'expert'), pairs))  3.54 us
  transfers between devices with their start and end apart: 30, of which 13 were waited for; matrix products, arithmetic and copies ran while one was open for 1% of the time, Pallas kernels for 29%

profile of v13, /device:TPU:0, one launch (start us, length us, event | category | flops | bytes accessed | tf_op | source)
XLA Modules:
  0.0 121.5 jit_solution(5457473494807198742)
XLA Ops:
  0.0 4.0 %collective-permute-start = (bf16[48,2048]{1,0:T(8,128)(2,1)}, bf16[48,2048]{1,0:T(8,128)(2,1)S(1)}, u32[]{:S(2)}, u32[]{:S(2)}) collective-permute-start(bf16[48,2048]{1,0:T(8,128)(2,1)} %bitcast.39), channel_id=1, source_target_pairs={{0,8},{1,9},{2,10},{3,11},{4,12},{5,13},{6,14},{7,15},{8,0},{9,1},... | collective-permute-start | bytes 589832 | tf_op jit(solution)/shard_map/ppermute | solution.py:35
  4.0 1.7 %dense_gates.1 = bf16[48,128]{1,0:T(8,128)(2,1)} custom-call(s32[3,8,16]{2,1,0:T(8,128)} %bitcast.41, f32[3,8,16]{2,1,0:T(8,128)} %bitcast.42), custom_call_target="tpu_custom_call" | custom-call | flops 8589934592 | bytes 1 | tf_op jit(solution)/shard_map/dense_gates/pallas_call | solution.py:93
  6.4 2.8 %order_factors.1 = (bf16[4,264,128]{2,1,0:T(8,128)(2,1)}, bf16[4,264,128]{2,1,0:T(8,128)(2,1)}) custom-call(s32[2]{0:T(128)} %pad_add_fusion.place_ref, s32[16]{0:T(128)} %placement_ref.1, bf16[16,33792]{1,0:T(8,128)(2,1)} %factors_ref.1), custom_call_target="tpu_custom_call" | custom-call | flops 8589934592 | bytes 1 | tf_op jit(solution)/shard_map/order_factors/pallas_call | solution.py:128
  9.2 1.9 %collective-permute-start.2 = (bf16[4,264,128]{2,1,0:T(8,128)(2,1)}, bf16[4,264,128]{2,1,0:T(8,128)(2,1)S(1)}, u32[]{:S(2)}, u32[]{:S(2)}) collective-permute-start(bf16[4,264,128]{2,1,0:T(8,128)(2,1)} %get-tuple-element.41), channel_id=1, source_target_pairs={{0,2},{1,3},{2,0},{3,1},{4,6},{5,7},{6,4},{7,5},{8,10},{9,11},{10,... | collective-permute-start | bytes 811016 | tf_op jit(solution)/shard_map/ppermute | solution.py:35
  11.1 2.8 %collective-permute-done.1 = bf16[48,128]{1,0:T(8,128)(2,1)S(1)} collective-permute-done((bf16[48,128]{1,0:T(8,128)(2,1)}, bf16[48,128]{1,0:T(8,128)(2,1)S(1)}, u32[]{:S(2)}, u32[]{:S(2)}) %collective-permute-start.1) | collective-permute-done | bytes 12320 | tf_op jit(solution)/shard_map/ppermute | solution.py:35
  13.9 3.4 %collective-permute-done.2 = bf16[4,264,128]{2,1,0:T(8,128)(2,1)S(1)} collective-permute-done((bf16[4,264,128]{2,1,0:T(8,128)(2,1)}, bf16[4,264,128]{2,1,0:T(8,128)(2,1)S(1)}, u32[]{:S(2)}, u32[]{:S(2)}) %collective-permute-start.2) | collective-permute-done | bytes 270368 | tf_op jit(solution)/shard_map/ppermute | solution.py:35
  19.1 1.7 %collective-permute-start.6 = (bf16[2,264,128]{2,1,0:T(8,128)(2,1)S(1)}, bf16[2,264,128]{2,1,0:T(8,128)(2,1)S(1)}, u32[]{:S(2)}, u32[]{:S(2)}) collective-permute-start(bf16[2,264,128]{2,1,0:T(8,128)(2,1)S(1)} %pad_maximum_fusion.6), channel_id=1, source_target_pairs={{0,4},{1,5},{2,6},{3,7},{4,0},{5,1},{6,2},{7,3},{8,12},{9,13},{10,... | collective-permute-start | bytes 405512 | tf_op jit(solution)/shard_map/ppermute | solution.py:67
  21.2 2.7 %collective-permute-start.7 = (bf16[2,264,128]{2,1,0:T(8,128)(2,1)S(1)}, bf16[2,264,128]{2,1,0:T(8,128)(2,1)S(1)}, u32[]{:S(2)}, u32[]{:S(2)}) collective-permute-start(bf16[2,264,128]{2,1,0:T(8,128)(2,1)S(1)} %pad_maximum_fusion.7), channel_id=1, source_target_pairs={{0,8},{1,9},{2,10},{3,11},{4,12},{5,13},{6,14},{7,15},{8,0},{9,1},... | collective-permute-start | bytes 405512 | tf_op jit(solution)/shard_map/ppermute | solution.py:67
  23.9 1.6 %collective-permute-start.4 = (bf16[96,128]{1,0:T(8,128)(2,1)S(1)}, bf16[96,128]{1,0:T(8,128)(2,1)S(1)}, u32[]{:S(2)}, u32[]{:S(2)}) collective-permute-start(bf16[96,128]{1,0:T(8,128)(2,1)S(1)} %pad_maximum_fusion.10), channel_id=1, source_target_pairs={{0,4},{1,5},{2,6},{3,7},{4,0},{5,1},{6,2},{7,3},{8,12},{9,13},{10,... | collective-permute-start | bytes 73736 | tf_op jit(solution)/shard_map/ppermute | solution.py:35
  25.5 9.6 %collective-permute-done.4 = bf16[96,128]{1,0:T(8,128)(2,1)S(1)} collective-permute-done((bf16[96,128]{1,0:T(8,128)(2,1)S(1)}, bf16[96,128]{1,0:T(8,128)(2,1)S(1)}, u32[]{:S(2)}, u32[]{:S(2)}) %collective-permute-start.4) | collective-permute-done | bytes 24608 | tf_op jit(solution)/shard_map/ppermute | solution.py:35
  35.1 3.4 %collective-permute-start.8 = (bf16[2,264,128]{2,1,0:T(8,128)(2,1)S(1)}, bf16[2,264,128]{2,1,0:T(8,128)(2,1)S(1)}, u32[]{:S(2)}, u32[]{:S(2)}) collective-permute-start(bf16[2,264,128]{2,1,0:T(8,128)(2,1)S(1)} %pad_maximum_fusion.8), channel_id=1, source_target_pairs={{0,12},{1,13},{2,14},{3,15},{4,8},{5,9},{6,10},{7,11},{8,4},{9,5},... | collective-permute-start | bytes 405512 | tf_op jit(solution)/shard_map/ppermute | solution.py:67
  38.5 3.5 %collective-permute-done.8 = bf16[2,264,128]{2,1,0:T(8,128)(2,1)S(1)} collective-permute-done((bf16[2,264,128]{2,1,0:T(8,128)(2,1)S(1)}, bf16[2,264,128]{2,1,0:T(8,128)(2,1)S(1)}, u32[]{:S(2)}, u32[]{:S(2)}) %collective-permute-start.8) | collective-permute-done | bytes 135200 | tf_op jit(solution)/shard_map/ppermute | solution.py:67
  43.9 5.5 %collective-permute-start.14 = (bf16[8,264,128]{2,1,0:T(8,128)(2,1)S(1)}, bf16[8,264,128]{2,1,0:T(8,128)(2,1)S(1)}, u32[]{:S(2)}, u32[]{:S(2)}) collective-permute-start(bf16[8,264,128]{2,1,0:T(8,128)(2,1)S(1)} %pad_maximum_fusion.2.refs_0_), channel_id=1, source_target_pairs={{0,16},{16,0},{1,17},{17,1},{2,18},{18,2},{3,19},{19,3},{4,20},{20... | collective-permute-start | bytes 1622024 | tf_op jit(solution)/shard_map/ppermute | solution.py:414
  49.4 4.9 %base_products.3 = (f32[384,768]{1,0:T(8,128)S(1)}, f32[384,768]{1,0:T(8,128)S(1)}) custom-call(bf16[192,2176]{1,0:T(8,128)(2,1)S(1)} %bitcast.24, bf16[192,2176]{1,0:T(8,128)(2,1)S(1)} %collective-permute-done.10.refs_1_.refs_2_, bf16[2048,768]{1,0:T(8,128)(2,1)S(1)} %bitcast.28, bf16[2048,768]{1,0:T(8,128)(2,1)S(1)} %bitcast.31), custom_call_target="tpu_custom_call" | custom-call | flops 8589934592 | bytes 1 | tf_op jit(solution)/shard_map/base_products/pallas_call | solution.py:273
  55.0 7.0 %collective-permute-done.14.refs_1_ = bf16[8,264,128]{2,1,0:T(8,128)(2,1)S(1)} collective-permute-done((bf16[8,264,128]{2,1,0:T(8,128)(2,1)S(1)}, bf16[8,264,128]{2,1,0:T(8,128)(2,1)S(1)}, u32[]{:S(2)}, u32[]{:S(2)}) %collective-permute-start.14) | collective-permute-done | bytes 540704 | tf_op jit(solution)/shard_map/ppermute | solution.py:414
  62.0 1.6 %relayout_factors.1 = (bf16[2048,128]{1,0:T(8,128)(2,1)S(1)}, bf16[64,768]{1,0:T(8,128)(2,1)S(1)}, bf16[64,768]{1,0:T(8,128)(2,1)S(1)}, bf16[768,128]{1,0:T(8,128)(2,1)S(1)}, bf16[64,2048]{1,0:T(8,128)(2,1)S(1)}) custom-call(s32[2]{0:T(128)S(1)} %copy-done.3, bf16[8,264,128]{2,1,0:T(8,128)(2,1)S(1)} %pad_maximum_fusion.2.refs_0_, ...), custom_call_target="tpu_custom_call" | custom-call | flops 1 | bytes 1 | tf_op jit(solution)/shard_map/relayout_factors/pallas_call | solution.py:198
  63.6 2.0 %base_products.4 = (f32[128,768]{1,0:T(8,128)S(1)}, f32[128,768]{1,0:T(8,128)S(1)}) custom-call(bf16[64,2176]{1,0:T(8,128)(2,1)S(1)} %collective-permute-done.9.refs_0_.refs_1_, bf16[64,2176]{1,0:T(8,128)(2,1)S(1)} %collective-permute-done.13.refs_1_.refs_3_, bf16[2048,768]{1,0:T(8,128)(2,1)S(1)} %bitcast.29, bf16[2048,768]{1,0:T(8,128)(2,1)S(1)} %bitcast.32), custom_call_target="tpu_custom_call" | custom-call | flops 1 | bytes 1 | tf_op jit(solution)/shard_map/base_products/pallas_call | solution.py:273
  65.6 6.2 %finish_step.3 = (f32[128,2048]{1,0:T(8,128)S(1)}, bf16[128,2048]{1,0:T(8,128)(2,1)S(1)}) custom-call(s32[2]{0:T(128)S(1)} %copy-done.3, bf16[192,2176]{1,0:T(8,128)(2,1)S(1)} %bitcast.25, bf16[64,2176]{1,0:T(8,128)(2,1)S(1)} %collective-permute-done.9.refs_0_.refs_1_, bf16[192,2176]{1,0:T(8,128)(2,1)S(1)} %collective-permute-done.10.refs_1_.refs_2_, ...), custom_call_target="tpu_custom_call" | custom-call | flops 1 | bytes 1 | tf_op jit(solution)/shard_map/finish_step/pallas_call | solution.py:364
  72.4 1.4 %collective-permute-done.15 = bf16[128,2048]{1,0:T(8,128)(2,1)S(1)} collective-permute-done((bf16[128,2048]{1,0:T(8,128)(2,1)S(1)}, bf16[128,2048]{1,0:T(8,128)(2,1)S(1)}, u32[]{:S(2)}, u32[]{:S(2)}) %collective-permute-start.15) | collective-permute-done | bytes 524320 | tf_op jit(solution)/shard_map/ppermute | solution.py:35
  75.2 3.4 %base_products.5 = (f32[256,768]{1,0:T(8,128)S(1)}, f32[256,768]{1,0:T(8,128)S(1)}) custom-call(bf16[128,2176]{1,0:T(8,128)(2,1)S(1)} %collective-permute-done.11.refs_0_.refs_1_, bf16[128,2176]{1,0:T(8,128)(2,1)S(1)} %collective-permute-done.12.refs_1_.refs_3_, bf16[2048,768]{1,0:T(8,128)(2,1)S(1)} %bitcast.30, bf16[2048,768]{1,0:T(8,128)(2,1)S(1)} %bitcast.33), custom_call_target="tpu_custom_call" | custom-call | flops 1 | bytes 1 | tf_op jit(solution)/shard_map/base_products/pallas_call | solution.py:273
  78.7 6.2 %finish_step.4 = (f32[128,2048]{1,0:T(8,128)S(1)}, bf16[128,2048]{1,0:T(8,128)(2,1)S(1)}) custom-call(s32[2]{0:T(128)S(1)} %copy-done.3, bf16[192,2176]{1,0:T(8,128)(2,1)S(1)} %bitcast.26, bf16[128,2176]{1,0:T(8,128)(2,1)S(1)} %collective-permute-done.11.refs_0_.refs_1_, bf16[192,2176]{1,0:T(8,128)(2,1)S(1)} %collective-permute-done.10.refs_1_.refs_2_, ...), custom_call_target="tpu_custom_call" | custom-call | flops 1 | bytes 1 | tf_op jit(solution)/shard_map/finish_step/pallas_call | solution.py:364
  85.1 3.3 %collective-permute-start.17 = (bf16[16,2048]{1,0:T(8,128)(2,1)S(1)}, bf16[16,2048]{1,0:T(8,128)(2,1)S(1)}, u32[]{:S(2)}, u32[]{:S(2)}) collective-permute-start(bf16[16,2048]{1,0:T(8,128)(2,1)S(1)} %get-tuple-element.89), channel_id=1, source_target_pairs={{0,8},{1,9},{2,10},{3,11},{4,12},{5,13},{6,14},{7,15},{8,0},{9,1},... | collective-permute-start | bytes 196616 | tf_op jit(solution)/shard_map/ppermute | solution.py:35
  90.2 6.2 %finish_step.5 = (f32[128,2048]{1,0:T(8,128)S(1)}, bf16[128,2048]{1,0:T(8,128)(2,1)S(1)}) custom-call(s32[2]{0:T(128)S(1)} %copy-done.3, bf16[192,2176]{1,0:T(8,128)(2,1)S(1)} %bitcast.27, bf16[128,2176]{1,0:T(8,128)(2,1)S(1)} %collective-permute-done.11.refs_0_.refs_1_, bf16[192,2176]{1,0:T(8,128)(2,1)S(1)} %collective-permute-done.10.refs_1_.refs_2_, ...), custom_call_target="tpu_custom_call" | custom-call | flops 1 | bytes 1 | tf_op jit(solution)/shard_map/finish_step/pallas_call | solution.py:364
  96.7 1.6 %collective-permute-start.21 = (bf16[64,2048]{1,0:T(8,128)(2,1)S(1)}, bf16[64,2048]{1,0:T(8,128)(2,1)S(1)}, u32[]{:S(2)}, u32[]{:S(2)}) collective-permute-start(bf16[64,2048]{1,0:T(8,128)(2,1)S(1)} %slice.185), channel_id=1, source_target_pairs={{0,2},{1,3},{2,0},{3,1},{4,6},{5,7},{6,4},{7,5},{8,10},{9,11},{10,... | collective-permute-start | bytes 786440 | tf_op jit(solution)/shard_map/ppermute | solution.py:35
  98.6 1.6 %collective-permute-start.26 = (bf16[64,2048]{1,0:T(8,128)(2,1)S(1)}, bf16[64,2048]{1,0:T(8,128)(2,1)S(1)}, u32[]{:S(2)}, u32[]{:S(2)}) collective-permute-start(bf16[64,2048]{1,0:T(8,128)(2,1)S(1)} %slice.184), channel_id=1, source_target_pairs={{0,2},{1,3},{2,0},{3,1},{4,6},{5,7},{6,4},{7,5},{8,10},{9,11},{10,... | collective-permute-start | bytes 786440 | tf_op jit(solution)/shard_map/ppermute | solution.py:35
  100.2 5.7 %collective-permute-done.21 = bf16[64,2048]{1,0:T(8,128)(2,1)S(1)} collective-permute-done((bf16[64,2048]{1,0:T(8,128)(2,1)S(1)}, bf16[64,2048]{1,0:T(8,128)(2,1)S(1)}, u32[]{:S(2)}, u32[]{:S(2)}) %collective-permute-start.21) | collective-permute-done | bytes 262176 | tf_op jit(solution)/shard_map/ppermute | solution.py:35
  106.0 1.7 %collective-permute-start.22 = (bf16[16,2048]{1,0:T(8,128)(2,1)S(1)}, bf16[16,2048]{1,0:T(8,128)(2,1)S(1)}, u32[]{:S(2)}, u32[]{:S(2)}) collective-permute-start(bf16[16,2048]{1,0:T(8,128)(2,1)S(1)} %get-tuple-element.92), channel_id=1, source_target_pairs={{0,8},{1,9},{2,10},{3,11},{4,12},{5,13},{6,14},{7,15},{8,0},{9,1},... | collective-permute-start | bytes 196616 | tf_op jit(solution)/shard_map/ppermute | solution.py:35
  107.7 1.8 %collective-permute-start.23 = (bf16[16,2048]{1,0:T(8,128)(2,1)S(1)}, bf16[16,2048]{1,0:T(8,128)(2,1)S(1)}, u32[]{:S(2)}, u32[]{:S(2)}) collective-permute-start(bf16[16,2048]{1,0:T(8,128)(2,1)S(1)} %get-tuple-element.94), channel_id=1, source_target_pairs={{0,4},{1,5},{2,6},{3,7},{4,0},{5,1},{6,2},{7,3},{8,12},{9,13},{10,... | collective-permute-start | bytes 196616 | tf_op jit(solution)/shard_map/ppermute | solution.py:35
  111.2 1.7 %collective-permute-start.27 = (bf16[16,2048]{1,0:T(8,128)(2,1)S(1)}, bf16[16,2048]{1,0:T(8,128)(2,1)S(1)}, u32[]{:S(2)}, u32[]{:S(2)}) collective-permute-start(bf16[16,2048]{1,0:T(8,128)(2,1)S(1)} %get-tuple-element.95), channel_id=1, source_target_pairs={{0,8},{1,9},{2,10},{3,11},{4,12},{5,13},{6,14},{7,15},{8,0},{9,1},... | collective-permute-start | bytes 196616 | tf_op jit(solution)/shard_map/ppermute | solution.py:35
  112.9 1.8 %collective-permute-start.28 = (bf16[16,2048]{1,0:T(8,128)(2,1)S(1)}, bf16[16,2048]{1,0:T(8,128)(2,1)S(1)}, u32[]{:S(2)}, u32[]{:S(2)}) collective-permute-start(bf16[16,2048]{1,0:T(8,128)(2,1)S(1)} %get-tuple-element.97), channel_id=1, source_target_pairs={{0,4},{1,5},{2,6},{3,7},{4,0},{5,1},{6,2},{7,3},{8,12},{9,13},{10,... | collective-permute-start | bytes 196616 | tf_op jit(solution)/shard_map/ppermute | solution.py:35
  116.2 2.4 %collective-permute-done.27 = bf16[16,2048]{1,0:T(8,128)(2,1)S(1)} collective-permute-done((bf16[16,2048]{1,0:T(8,128)(2,1)S(1)}, bf16[16,2048]{1,0:T(8,128)(2,1)S(1)}, u32[]{:S(2)}, u32[]{:S(2)}) %collective-permute-start.27) | collective-permute-done | bytes 65568 | tf_op jit(solution)/shard_map/ppermute | solution.py:35
  118.6 2.2 %collective-permute-done.29 = bf16[16,2048]{1,0:T(8,128)(2,1)S(1)} collective-permute-done((bf16[16,2048]{1,0:T(8,128)(2,1)S(1)}, bf16[16,2048]{1,0:T(8,128)(2,1)S(1)}, u32[]{:S(2)}, u32[]{:S(2)}) %collective-permute-start.29) | collective-permute-done | bytes 65568 | tf_op jit(solution)/shard_map/ppermute | solution.py:35
  (81 shorter events, 13.8 us)
Async XLA Ops:
  0.0 13.9 %collective-permute-start = (bf16[48,2048]{1,0:T(8,128)(2,1)}, bf16[48,2048]{1,0:T(8,128)(2,1)S(1)}, u32[]{:S(2)}, u32[]{:S(2)}) collective-permute-start(bf16[48,2048]{1,0:T(8,128)(2,1)} %bitcast.39), channel_id=1, source_target_pairs={{0,8},{1,9},{2,10},{3,11},{4,12},{5,13},{6,14},{7,15},{8,0},{9,1},... | collective-permute-start | bytes 589832 | tf_op jit(solution)/shard_map/ppermute | solution.py:35
  5.7 8.2 %collective-permute-start.1 = (bf16[48,128]{1,0:T(8,128)(2,1)}, bf16[48,128]{1,0:T(8,128)(2,1)S(1)}, u32[]{:S(2)}, u32[]{:S(2)}) collective-permute-start(bf16[48,128]{1,0:T(8,128)(2,1)} %dense_gates.1), channel_id=1, source_target_pairs={{0,8},{1,9},{2,10},{3,11},{4,12},{5,13},{6,14},{7,15},{8,0},{9,1},... | collective-permute-start | bytes 36872 | tf_op jit(solution)/shard_map/ppermute | solution.py:35
  6.4 7.5 %copy-start.4 = (bf16[3,16,2048]{2,1,0:T(8,128)(2,1)S(1)}, bf16[3,16,2048]{2,1,0:T(8,128)(2,1)}, u32[]{:S(2)}) copy-start(bf16[3,16,2048]{2,1,0:T(8,128)(2,1)} %param.8) | copy-start | bytes 589828
  9.2 8.2 %collective-permute-start.2 = (bf16[4,264,128]{2,1,0:T(8,128)(2,1)}, bf16[4,264,128]{2,1,0:T(8,128)(2,1)S(1)}, u32[]{:S(2)}, u32[]{:S(2)}) collective-permute-start(bf16[4,264,128]{2,1,0:T(8,128)(2,1)} %get-tuple-element.41), channel_id=1, source_target_pairs={{0,2},{1,3},{2,0},{3,1},{4,6},{5,7},{6,4},{7,5},{8,10},{9,11},{10,... | collective-permute-start | bytes 811016 | tf_op jit(solution)/shard_map/ppermute | solution.py:35
  18.4 20.1 %collective-permute-start.5 = (bf16[2,264,128]{2,1,0:T(8,128)(2,1)S(1)}, bf16[2,264,128]{2,1,0:T(8,128)(2,1)S(1)}, u32[]{:S(2)}, u32[]{:S(2)}) collective-permute-start(bf16[2,264,128]{2,1,0:T(8,128)(2,1)S(1)} %pad_maximum_fusion.5), channel_id=1, source_target_pairs={{0,0},{1,1},{2,2},{3,3},{4,4},{5,5},{6,6},{7,7},{8,8},{9,9},{10,10... | collective-permute-start | bytes 405512 | tf_op jit(solution)/shard_map/ppermute | solution.py:67
  19.1 19.4 %collective-permute-start.6 = (bf16[2,264,128]{2,1,0:T(8,128)(2,1)S(1)}, bf16[2,264,128]{2,1,0:T(8,128)(2,1)S(1)}, u32[]{:S(2)}, u32[]{:S(2)}) collective-permute-start(bf16[2,264,128]{2,1,0:T(8,128)(2,1)S(1)} %pad_maximum_fusion.6), channel_id=1, source_target_pairs={{0,4},{1,5},{2,6},{3,7},{4,0},{5,1},{6,2},{7,3},{8,12},{9,13},{10,... | collective-permute-start | bytes 405512 | tf_op jit(solution)/shard_map/ppermute | solution.py:67
  20.8 21.3 %collective-permute-start.3 = (bf16[96,2048]{1,0:T(8,128)(2,1)S(1)}, bf16[96,2048]{1,0:T(8,128)(2,1)S(1)}, u32[]{:S(2)}, u32[]{:S(2)}) collective-permute-start(bf16[96,2048]{1,0:T(8,128)(2,1)S(1)} %pad_maximum_fusion.3), channel_id=1, source_target_pairs={{0,4},{1,5},{2,6},{3,7},{4,0},{5,1},{6,2},{7,3},{8,12},{9,13},{10,... | collective-permute-start | bytes 1179656 | tf_op jit(solution)/shard_map/ppermute | solution.py:35
  21.2 17.3 %collective-permute-start.7 = (bf16[2,264,128]{2,1,0:T(8,128)(2,1)S(1)}, bf16[2,264,128]{2,1,0:T(8,128)(2,1)S(1)}, u32[]{:S(2)}, u32[]{:S(2)}) collective-permute-start(bf16[2,264,128]{2,1,0:T(8,128)(2,1)S(1)} %pad_maximum_fusion.7), channel_id=1, source_target_pairs={{0,8},{1,9},{2,10},{3,11},{4,12},{5,13},{6,14},{7,15},{8,0},{9,1},... | collective-permute-start | bytes 405512 | tf_op jit(solution)/shard_map/ppermute | solution.py:67
  23.9 11.2 %collective-permute-start.4 = (bf16[96,128]{1,0:T(8,128)(2,1)S(1)}, bf16[96,128]{1,0:T(8,128)(2,1)S(1)}, u32[]{:S(2)}, u32[]{:S(2)}) collective-permute-start(bf16[96,128]{1,0:T(8,128)(2,1)S(1)} %pad_maximum_fusion.10), channel_id=1, source_target_pairs={{0,4},{1,5},{2,6},{3,7},{4,0},{5,1},{6,2},{7,3},{8,12},{9,13},{10,... | collective-permute-start | bytes 73736 | tf_op jit(solution)/shard_map/ppermute | solution.py:35
  35.1 6.9 %collective-permute-start.8 = (bf16[2,264,128]{2,1,0:T(8,128)(2,1)S(1)}, bf16[2,264,128]{2,1,0:T(8,128)(2,1)S(1)}, u32[]{:S(2)}, u32[]{:S(2)}) collective-permute-start(bf16[2,264,128]{2,1,0:T(8,128)(2,1)S(1)} %pad_maximum_fusion.8), channel_id=1, source_target_pairs={{0,12},{1,13},{2,14},{3,15},{4,8},{5,9},{6,10},{7,11},{8,4},{9,5},... | collective-permute-start | bytes 405512 | tf_op jit(solution)/shard_map/ppermute | solution.py:67
  42.4 7.0 %collective-permute-start.10 = (bf16[192,2176]{1,0:T(8,128)(2,1)S(1)}, bf16[192,2176]{1,0:T(8,128)(2,1)S(1)}, u32[]{:S(2)}, u32[]{:S(2)}) collective-permute-start(bf16[192,2176]{1,0:T(8,128)(2,1)S(1)} %bitcast.23), channel_id=1, source_target_pairs={{0,1},{1,0},{2,3},{3,2},{4,5},{5,4},{6,7},{7,6},{8,9},{9,8},{10,11... | collective-permute-start | bytes 2506760 | tf_op jit(solution)/shard_map/ppermute | solution.py:35
  42.6 11.7 %collective-permute-start.9 = (bf16[64,2176]{1,0:T(8,128)(2,1)S(1)}, bf16[64,2176]{1,0:T(8,128)(2,1)S(1)}, u32[]{:S(2)}, u32[]{:S(2)}) collective-permute-start(bf16[64,2176]{1,0:T(8,128)(2,1)S(1)} %bitcast.38), channel_id=1, source_target_pairs={{0,2},{1,3},{2,0},{3,1},{4,6},{5,7},{6,4},{7,5},{8,10},{9,11},{10,... | collective-permute-start | bytes 835592 | tf_op jit(solution)/shard_map/ppermute | solution.py:35
  43.9 18.1 %collective-permute-start.14 = (bf16[8,264,128]{2,1,0:T(8,128)(2,1)S(1)}, bf16[8,264,128]{2,1,0:T(8,128)(2,1)S(1)}, u32[]{:S(2)}, u32[]{:S(2)}) collective-permute-start(bf16[8,264,128]{2,1,0:T(8,128)(2,1)S(1)} %pad_maximum_fusion.2.refs_0_), channel_id=1, source_target_pairs={{0,16},{16,0},{1,17},{17,1},{2,18},{18,2},{3,19},{19,3},{4,20},{20... | collective-permute-start | bytes 1622024 | tf_op jit(solution)/shard_map/ppermute | solution.py:414
  49.4 12.6 %copy-start.3 = (s32[2]{0:T(128)S(1)}, s32[2]{0:T(128)}, u32[]{:S(2)}) copy-start(s32[2]{0:T(128)} %pad_add_fusion.place_ref) | copy-start | bytes 28
  54.3 9.2 %collective-permute-start.13 = (bf16[64,2176]{1,0:T(8,128)(2,1)S(1)}, bf16[64,2176]{1,0:T(8,128)(2,1)S(1)}, u32[]{:S(2)}, u32[]{:S(2)}) collective-permute-start(bf16[64,2176]{1,0:T(8,128)(2,1)S(1)} %collective-permute-done.9.refs_0_.refs_1_), channel_id=1, source_target_pairs={{0,1},{1,0},{2,3},{3,2},{4,5},{5,4},{6,7},{7,6},{8,9},{9,8},{10,11... | collective-permute-start | bytes 835592 | tf_op jit(solution)/shard_map/ppermute | solution.py:35
  54.4 17.5 %collective-permute-start.11 = (bf16[128,2176]{1,0:T(8,128)(2,1)S(1)}, bf16[128,2176]{1,0:T(8,128)(2,1)S(1)}, u32[]{:S(2)}, u32[]{:S(2)}) collective-permute-start(bf16[128,2176]{1,0:T(8,128)(2,1)S(1)} %bitcast.37), channel_id=1, source_target_pairs={{0,2},{1,3},{2,0},{3,1},{4,6},{5,7},{6,4},{7,5},{8,10},{9,11},{10,... | collective-permute-start | bytes 1671176 | tf_op jit(solution)/shard_map/ppermute | solution.py:35
  71.8 2.0 %collective-permute-start.15 = (bf16[128,2048]{1,0:T(8,128)(2,1)S(1)}, bf16[128,2048]{1,0:T(8,128)(2,1)S(1)}, u32[]{:S(2)}, u32[]{:S(2)}) collective-permute-start(bf16[128,2048]{1,0:T(8,128)(2,1)S(1)} %get-tuple-element.63), channel_id=1, source_target_pairs={{0,1},{1,0},{2,3},{3,2},{4,5},{5,4},{6,7},{7,6},{8,9},{9,8},{10,11... | collective-permute-start | bytes 1572872 | tf_op jit(solution)/shard_map/ppermute | solution.py:35
  71.9 2.7 %collective-permute-start.12 = (bf16[128,2176]{1,0:T(8,128)(2,1)S(1)}, bf16[128,2176]{1,0:T(8,128)(2,1)S(1)}, u32[]{:S(2)}, u32[]{:S(2)}) collective-permute-start(bf16[128,2176]{1,0:T(8,128)(2,1)S(1)} %collective-permute-done.11.refs_0_.refs_1_), channel_id=1, source_target_pairs={{0,1},{1,0},{2,3},{3,2},{4,5},{5,4},{6,7},{7,6},{8,9},{9,8},{10,11... | collective-permute-start | bytes 1671176 | tf_op jit(solution)/shard_map/ppermute | solution.py:35
  74.6 10.3 %collective-permute-start.16 = (bf16[64,2048]{1,0:T(8,128)(2,1)S(1)}, bf16[64,2048]{1,0:T(8,128)(2,1)S(1)}, u32[]{:S(2)}, u32[]{:S(2)}) collective-permute-start(bf16[64,2048]{1,0:T(8,128)(2,1)S(1)} %slice.186), channel_id=1, source_target_pairs={{0,2},{1,3},{2,0},{3,1},{4,6},{5,7},{6,4},{7,5},{8,10},{9,11},{10,... | collective-permute-start | bytes 786440 | tf_op jit(solution)/shard_map/ppermute | solution.py:35
  84.9 11.7 %collective-permute-start.20 = (bf16[128,2048]{1,0:T(8,128)(2,1)S(1)}, bf16[128,2048]{1,0:T(8,128)(2,1)S(1)}, u32[]{:S(2)}, u32[]{:S(2)}) collective-permute-start(bf16[128,2048]{1,0:T(8,128)(2,1)S(1)} %get-tuple-element.68), channel_id=1, source_target_pairs={{0,1},{1,0},{2,3},{3,2},{4,5},{5,4},{6,7},{7,6},{8,9},{9,8},{10,11... | collective-permute-start | bytes 1572872 | tf_op jit(solution)/shard_map/ppermute | solution.py:35
  85.1 11.4 %collective-permute-start.17 = (bf16[16,2048]{1,0:T(8,128)(2,1)S(1)}, bf16[16,2048]{1,0:T(8,128)(2,1)S(1)}, u32[]{:S(2)}, u32[]{:S(2)}) collective-permute-start(bf16[16,2048]{1,0:T(8,128)(2,1)S(1)} %get-tuple-element.89), channel_id=1, source_target_pairs={{0,8},{1,9},{2,10},{3,11},{4,12},{5,13},{6,14},{7,15},{8,0},{9,1},... | collective-permute-start | bytes 196616 | tf_op jit(solution)/shard_map/ppermute | solution.py:35
  88.4 8.2 %collective-permute-start.18 = (bf16[16,2048]{1,0:T(8,128)(2,1)S(1)}, bf16[16,2048]{1,0:T(8,128)(2,1)S(1)}, u32[]{:S(2)}, u32[]{:S(2)}) collective-permute-start(bf16[16,2048]{1,0:T(8,128)(2,1)S(1)} %get-tuple-element.91), channel_id=1, source_target_pairs={{0,4},{1,5},{2,6},{3,7},{4,0},{5,1},{6,2},{7,3},{8,12},{9,13},{10,... | collective-permute-start | bytes 196616 | tf_op jit(solution)/shard_map/ppermute | solution.py:35
  89.2 7.3 %collective-permute-start.19 = (bf16[16,2048]{1,0:T(8,128)(2,1)S(1)}, bf16[16,2048]{1,0:T(8,128)(2,1)S(1)}, u32[]{:S(2)}, u32[]{:S(2)}) collective-permute-start(bf16[16,2048]{1,0:T(8,128)(2,1)S(1)} %get-tuple-element.90), channel_id=1, source_target_pairs={{0,12},{1,13},{2,14},{3,15},{4,8},{5,9},{6,10},{7,11},{8,4},{9,5},... | collective-permute-start | bytes 196616 | tf_op jit(solution)/shard_map/ppermute | solution.py:35
  96.4 2.0 %collective-permute-start.25 = (bf16[128,2048]{1,0:T(8,128)(2,1)S(1)}, bf16[128,2048]{1,0:T(8,128)(2,1)S(1)}, u32[]{:S(2)}, u32[]{:S(2)}) collective-permute-start(bf16[128,2048]{1,0:T(8,128)(2,1)S(1)} %get-tuple-element.74), channel_id=1, source_target_pairs={{0,1},{1,0},{2,3},{3,2},{4,5},{5,4},{6,7},{7,6},{8,9},{9,8},{10,11... | collective-permute-start | bytes 1572872 | tf_op jit(solution)/shard_map/ppermute | solution.py:35
  96.7 9.2 %collective-permute-start.21 = (bf16[64,2048]{1,0:T(8,128)(2,1)S(1)}, bf16[64,2048]{1,0:T(8,128)(2,1)S(1)}, u32[]{:S(2)}, u32[]{:S(2)}) collective-permute-start(bf16[64,2048]{1,0:T(8,128)(2,1)S(1)} %slice.185), channel_id=1, source_target_pairs={{0,2},{1,3},{2,0},{3,1},{4,6},{5,7},{6,4},{7,5},{8,10},{9,11},{10,... | collective-permute-start | bytes 786440 | tf_op jit(solution)/shard_map/ppermute | solution.py:35
  98.6 12.5 %collective-permute-start.26 = (bf16[64,2048]{1,0:T(8,128)(2,1)S(1)}, bf16[64,2048]{1,0:T(8,128)(2,1)S(1)}, u32[]{:S(2)}, u32[]{:S(2)}) collective-permute-start(bf16[64,2048]{1,0:T(8,128)(2,1)S(1)} %slice.184), channel_id=1, source_target_pairs={{0,2},{1,3},{2,0},{3,1},{4,6},{5,7},{6,4},{7,5},{8,10},{9,11},{10,... | collective-permute-start | bytes 786440 | tf_op jit(solution)/shard_map/ppermute | solution.py:35
  106.0 8.7 %collective-permute-start.22 = (bf16[16,2048]{1,0:T(8,128)(2,1)S(1)}, bf16[16,2048]{1,0:T(8,128)(2,1)S(1)}, u32[]{:S(2)}, u32[]{:S(2)}) collective-permute-start(bf16[16,2048]{1,0:T(8,128)(2,1)S(1)} %get-tuple-element.92), channel_id=1, source_target_pairs={{0,8},{1,9},{2,10},{3,11},{4,12},{5,13},{6,14},{7,15},{8,0},{9,1},... | collective-permute-start | bytes 196616 | tf_op jit(solution)/shard_map/ppermute | solution.py:35
  107.7 8.0 %collective-permute-start.23 = (bf16[16,2048]{1,0:T(8,128)(2,1)S(1)}, bf16[16,2048]{1,0:T(8,128)(2,1)S(1)}, u32[]{:S(2)}, u32[]{:S(2)}) collective-permute-start(bf16[16,2048]{1,0:T(8,128)(2,1)S(1)} %get-tuple-element.94), channel_id=1, source_target_pairs={{0,4},{1,5},{2,6},{3,7},{4,0},{5,1},{6,2},{7,3},{8,12},{9,13},{10,... | collective-permute-start | bytes 196616 | tf_op jit(solution)/shard_map/ppermute | solution.py:35
  109.5 6.7 %collective-permute-start.24 = (bf16[16,2048]{1,0:T(8,128)(2,1)S(1)}, bf16[16,2048]{1,0:T(8,128)(2,1)S(1)}, u32[]{:S(2)}, u32[]{:S(2)}) collective-permute-start(bf16[16,2048]{1,0:T(8,128)(2,1)S(1)} %get-tuple-element.93), channel_id=1, source_target_pairs={{0,12},{1,13},{2,14},{3,15},{4,8},{5,9},{6,10},{7,11},{8,4},{9,5},... | collective-permute-start | bytes 196616 | tf_op jit(solution)/shard_map/ppermute | solution.py:35
  111.2 7.4 %collective-permute-start.27 = (bf16[16,2048]{1,0:T(8,128)(2,1)S(1)}, bf16[16,2048]{1,0:T(8,128)(2,1)S(1)}, u32[]{:S(2)}, u32[]{:S(2)}) collective-permute-start(bf16[16,2048]{1,0:T(8,128)(2,1)S(1)} %get-tuple-element.95), channel_id=1, source_target_pairs={{0,8},{1,9},{2,10},{3,11},{4,12},{5,13},{6,14},{7,15},{8,0},{9,1},... | collective-permute-start | bytes 196616 | tf_op jit(solution)/shard_map/ppermute | solution.py:35
  112.9 5.7 %collective-permute-start.28 = (bf16[16,2048]{1,0:T(8,128)(2,1)S(1)}, bf16[16,2048]{1,0:T(8,128)(2,1)S(1)}, u32[]{:S(2)}, u32[]{:S(2)}) collective-permute-start(bf16[16,2048]{1,0:T(8,128)(2,1)S(1)} %get-tuple-element.97), channel_id=1, source_target_pairs={{0,4},{1,5},{2,6},{3,7},{4,0},{5,1},{6,2},{7,3},{8,12},{9,13},{10,... | collective-permute-start | bytes 196616 | tf_op jit(solution)/shard_map/ppermute | solution.py:35
  114.7 6.1 %collective-permute-start.29 = (bf16[16,2048]{1,0:T(8,128)(2,1)S(1)}, bf16[16,2048]{1,0:T(8,128)(2,1)S(1)}, u32[]{:S(2)}, u32[]{:S(2)}) collective-permute-start(bf16[16,2048]{1,0:T(8,128)(2,1)S(1)} %get-tuple-element.96), channel_id=1, source_target_pairs={{0,12},{1,13},{2,14},{3,15},{4,8},{5,9},{6,10},{7,11},{8,4},{9,5},... | collective-permute-start | bytes 196616 | tf_op jit(solution)/shard_map/ppermute | solution.py:35
  (4 other events, 23.9 us)

commit v14 on v11

--- a/solution.py
+++ b/solution.py
@@ -41,15 +41,6 @@
         part = total[k * count : (k + 1) * count].astype(jnp.bfloat16)
         result = result + swap(part, n, stride, k).astype(jnp.float32)
     return result
-
-
-def exchange_along(x, n, stride, size):
-    lines = [
-        [start + k * stride for k in range(size)]
-        for start in range(n)
-        if start // stride % size == 0
-    ]
-    return lax.all_to_all(x, "expert", 0, 0, axis_index_groups=lines, tiled=True)
 
 
 def exchange_factors(blocks, n):
@@ -101,10 +92,10 @@
     )(hidden, jnp.swapaxes(route_ids, 1, 2), jnp.swapaxes(route_logits, 1, 2))
 
 
-def order_kernel(middle, place_ref, placement_ref, factors_ref, *refs):
-    out_refs, wide_ref = refs[:-1], refs[-1]
+def order_kernel(place_ref, placement_ref, factors_ref, *refs):
+    out_refs, wide_ref, slot_ref = refs[:-2], refs[-2], refs[-1]
     slots = factors_ref.shape[0]
-    length, lanes = out_refs[0].shape[1:]
+    outer, length, lanes = out_refs[0].shape
     group, me = place_ref[0], place_ref[1]
 
     def cut(t, carry):
@@ -114,37 +105,30 @@
         return carry
 
     lax.fori_loop(0, length, cut, 0, unroll=8)
-
-    def put(s, carry):
-        to = placement_ref[s]
-        away = to ^ me
-        aside, ahead = lax.rem(away // 2, middle), away // (2 * middle)
-        ours = lax.rem(away, 2) == group
-        rows = wide_ref[pl.ds(pl.multiple_of(s * length, 8), length), :].astype(jnp.bfloat16)
-        for r, out_ref in enumerate(out_refs):
-
-            @pl.when(jnp.logical_and(ours, aside == r))
-            def _():
-                out_ref[ahead] = rows
-
-        return carry
-
-    lax.fori_loop(0, slots, put, 0)
-
-
-def order_factors(place, placement, factors, n):
-    outer, middle, _ = split_axis(n)
+    for s in range(slots):
+        slot_ref[placement_ref[s]] = s
+    for r, out_ref in enumerate(out_refs):
+        for q in range(outer):
+            slot = slot_ref[me ^ (2 * (q * len(out_refs) + r) + group)]
+            rows = wide_ref[pl.ds(pl.multiple_of(slot * length, 8), length), :]
+            out_ref[q] = rows.astype(jnp.bfloat16)
+
+
+def order_factors(place, placement, factors, outer, middle):
     slots, entries = factors.shape
     length = entries // LANES
     return pl.pallas_call(
-        functools.partial(order_kernel, middle),
+        order_kernel,
         out_shape=[jax.ShapeDtypeStruct((outer, length, LANES), jnp.bfloat16)] * middle,
         in_specs=[
             pl.BlockSpec(memory_space=pltpu.SMEM),
             pl.BlockSpec(memory_space=pltpu.SMEM),
             pl.BlockSpec(memory_space=pltpu.VMEM),
         ],
-        scratch_shapes=[pltpu.VMEM((slots * length, LANES), jnp.float32)],
+        scratch_shapes=[
+            pltpu.VMEM((slots * length, LANES), jnp.float32),
+            pltpu.SMEM((slots,), jnp.int32),
+        ],
         compiler_params=pltpu.CompilerParams(vmem_limit_bytes=WHOLE_GRANT),
         cost_estimate=LITTLE,
         name="order_factors",
@@ -412,10 +396,9 @@
 
     rows_in = make_payload(hidden, route_ids, route_logits, experts)
     rows_in, factors = lax.optimization_barrier((rows_in, factors))
-    column = jnp.broadcast_to(rows_in, (outer, *rows_in.shape))
-    column = exchange_along(column, owners, *along_outer).reshape(outer, steps, rows, -1)
-    column = jnp.swapaxes(column, 0, 1).reshape(steps * outer * rows, -1)
-    blocks = order_factors(place, placement, factors, owners)
+    column = [p.reshape(steps, rows, -1) for p in along(rows_in, *along_outer)]
+    column = jnp.stack(column, axis=1).reshape(steps * outer * rows, -1)
+    blocks = order_factors(place, placement, factors, outer, middle)
     blocks = [blocks[0]] + [swap(blocks[r], owners, cores, r) for r in range(1, middle)]
     column, blocks = lax.optimization_barrier((column, blocks))
     here = exchange_factors(blocks, owners)
@@ -423,8 +406,9 @@
     sheet = along(column, *along_middle)
     others = [swap(column, owners, 1, 1)]
     base = [base_products([sheet[0], others[0]], w_gate[0], w_up[0])]
-    here[0], base = lax.optimization_barrier((here[0], base))
     there = [lax.ppermute(p, "group", [(0, 1), (1, 0)]) for p in here]
+    early = (there[0], here[1], base, sheet[1:])
+    there[0], here[1], base, sheet[1:] = lax.optimization_barrier(early)
     for r in range(1, middle):
         others.append(swap(sheet[r], owners, 1, 1))
         base.append(base_products([sheet[r], others[r]], w_gate[0], w_up[0]))
@@ -440,12 +424,8 @@
         kept, sent = finish_step(place, pieces, base, s * span, span, low_rank, down_weight[0])
         results.append(kept + swap(sent, owners, 1, 1).astype(jnp.float32))
     results = [scatter_along(total, owners, *along_middle) for total in results]
-    finals = []
-    for total in results:
-        parts = total.astype(jnp.bfloat16).reshape(outer, rows, width)
-        parts = exchange_along(parts, owners, *along_outer)
-        finals.append(jnp.sum(parts, axis=0, dtype=jnp.float32))
-    return jnp.stack(finals).astype(jnp.bfloat16)
+    results = [scatter_along(total, owners, *along_outer) for total in results]
+    return jnp.stack(results).astype(jnp.bfloat16)
 
 
 def row_capacity(rows, top, experts):

time: 137 us -> 113 us (0.82)
  waiting for transfers between devices: 57.5 us -> 39 us
  local copies, waits for them, and re-layouts: 6.1 us -> 1.32 us
  other arithmetic: 5.13 us -> 3.35 us
  starting transfers between devices: 32.6 us -> 34 us
    all_to_all x4 -> x0, waiting for transfers between devices: 32.9 us -> none  [exchange_along(): lax.all_to_all(x, 'expert', 0, 0, axis_index_groups=lines, tiled=True)]
    all_to_all x4 -> x0, starting transfers between devices: 16.8 us -> none  [exchange_along(): lax.all_to_all(x, 'expert', 0, 0, axis_index_groups=lines, tiled=True)]
    ppermute x10 -> x22, starting transfers between devices: 7.64 us -> 23.9 us  [swap(): return lax.ppermute(x, 'expert', [(i, i ^ k * stride) for i in range(n)])]
    ppermute x10 -> x22, waiting for transfers between devices: 16.8 us -> 27.8 us  [swap(): return lax.ppermute(x, 'expert', [(i, i ^ k * stride) for i in range(n)])]
    ppermute x4, waiting for transfers between devices: 5.91 us -> 9.57 us  [exchange_factors(): here.append(lax.ppermute(part, ('group', 'expert'), pairs))]
    convert_element_type x3 -> x0, other arithmetic: 3.23 us -> none  [dense_shards(): parts = total.astype(jnp.bfloat16).reshape(outer, rows, width)]
    ppermute x4, starting transfers between devices: 3.92 us -> 6.91 us  [exchange_factors(): here.append(lax.ppermute(part, ('group', 'expert'), pairs))]
    broadcast_in_dim x1 -> x0, local copies, waits for them, and re-layouts: 1.91 us -> none  [dense_shards(): column = jnp.broadcast_to(rows_in, (outer, *rows_in.shape))]
  transfers between devices with their start and end apart: 20 -> 28, of which waited for: 8 -> 14; matrix products, arithmetic and copies ran while one was open for 6% -> 3% of each run, Pallas kernels for 19% -> 22%
where the time goes in v14:
time: 113 us
  waiting for transfers between devices  39 us (35%)
  Pallas kernels  35 us (31%)
  starting transfers between devices  34 us (30%)
  other arithmetic  3.35 us (3%)
  local copies, waits for them, and re-layouts  1.32 us (1%)
    ppermute x22, waiting for transfers between devices, swap(): return lax.ppermute(x, 'expert', [(i, i ^ k * stride) for i in range(n)])  27.8 us
    ppermute x22, starting transfers between devices, swap(): return lax.ppermute(x, 'expert', [(i, i ^ k * stride) for i in range(n)])  23.9 us
    pallas_call x3, Pallas kernels, finish_step(): pl.pallas_call(functools.partial(finish_kernel, len(pieces), first, rows)...  18.7 us
    pallas_call x2, Pallas kernels, base_products(): pl.pallas_call(functools.partial(base_kernel, len(pieces)), out_shape=[ou...  9.8 us
    ppermute x4, waiting for transfers between devices, exchange_factors(): here.append(lax.ppermute(part, ('group', 'expert'), pairs))  9.57 us
    ppermute x4, starting transfers between devices, exchange_factors(): here.append(lax.ppermute(part, ('group', 'expert'), pairs))  6.91 us
    ppermute x2, starting transfers between devices, dense_shards(): there = [lax.ppermute(p, 'group', [(0, 1), (1, 0)]) for p in here]  3.18 us
    pallas_call x1, Pallas kernels, order_factors(): pl.pallas_call(order_kernel, out_shape=[jax.ShapeDtypeStruct((outer, leng...  2.78 us
  transfers between devices with their start and end apart: 28, of which 14 were waited for; matrix products, arithmetic and copies ran while one was open for 3% of the time, Pallas kernels for 22%

profile of v14, /device:TPU:0, one launch (start us, length us, event | category | flops | bytes accessed | tf_op | source)
XLA Modules:
  0.0 113.1 jit_solution(14950996348723625928)
XLA Ops:
  0.0 2.1 %payload.1 = bf16[48,2176]{1,0:T(8,128)(2,1)} custom-call(bf16[3,16,2048]{2,1,0:T(8,128)(2,1)} %hidden_ref.1, s32[3,8,16]{2,1,0:T(8,128)} %bitcast.49, f32[3,8,16]{2,1,0:T(8,128)} %bitcast.50), custom_call_target="tpu_custom_call" | custom-call | flops 1 | bytes 1 | tf_op jit(solution)/shard_map/payload/pallas_call | solution.py:85
  2.1 5.0 %collective-permute-start.2 = (bf16[48,2176]{1,0:T(8,128)(2,1)}, bf16[48,2176]{1,0:T(8,128)(2,1)S(1)}, u32[]{:S(2)}, u32[]{:S(2)}) collective-permute-start(bf16[48,2176]{1,0:T(8,128)(2,1)} %payload.1), channel_id=1, source_target_pairs={{0,12},{1,13},{2,14},{3,15},{4,8},{5,9},{6,10},{7,11},{8,4},{9,5},... | collective-permute-start | bytes 626696 | tf_op jit(solution)/shard_map/ppermute | solution.py:34
  8.4 2.8 %order_factors.1 = (bf16[4,264,128]{2,1,0:T(8,128)(2,1)}, bf16[4,264,128]{2,1,0:T(8,128)(2,1)}) custom-call(s32[2]{0:T(128)} %pad_add_fusion.place_ref, s32[16]{0:T(128)} %placement_ref.1, bf16[16,33792]{1,0:T(8,128)(2,1)} %factors_ref), custom_call_target="tpu_custom_call" | custom-call | flops 1 | bytes 1 | tf_op jit(solution)/shard_map/order_factors/pallas_call | solution.py:120
  11.2 1.7 %collective-permute-start.3 = (bf16[4,264,128]{2,1,0:T(8,128)(2,1)}, bf16[4,264,128]{2,1,0:T(8,128)(2,1)S(1)}, u32[]{:S(2)}, u32[]{:S(2)}) collective-permute-start(bf16[4,264,128]{2,1,0:T(8,128)(2,1)} %get-tuple-element.48), channel_id=1, source_target_pairs={{0,2},{1,3},{2,0},{3,1},{4,6},{5,7},{6,4},{7,5},{8,10},{9,11},{10,... | collective-permute-start | bytes 811016 | tf_op jit(solution)/shard_map/ppermute | solution.py:34
  13.5 11.7 %collective-permute-done.1 = bf16[48,2176]{1,0:T(8,128)(2,1)} collective-permute-done((bf16[48,2176]{1,0:T(8,128)(2,1)}, bf16[48,2176]{1,0:T(8,128)(2,1)}, u32[]{:S(2)}, u32[]{:S(2)}) %collective-permute-start.1) | collective-permute-done | bytes 208928 | tf_op jit(solution)/shard_map/ppermute | solution.py:34
  25.3 1.3 %pad_maximum_fusion = bf16[3,4,16,2176]{3,2,1,0:T(8,128)(2,1)S(1)} fusion(bf16[3,1,16,2176]{3,2,1,0:T(8,128)(2,1)S(1)} %bitcast.44, bf16[3,1,16,2176]{3,2,1,0:T(8,128)(2,1)} %bitcast.7, bf16[3,1,16,2176]{3,2,1,0:T(8,128)(2,1)} %bitcast.5, bf16[3,1,16,2176]{3,2,1,0:T(8,128)(2,1)} %bitcast.43), kind=kLoop, calls=%fused_computation.3 | loop fusion | flops 1253376 | bytes 1671168 | tf_op jit(solution)/shard_map/stack | solution.py:400
  26.5 1.6 %collective-permute-start.10 = (bf16[192,2176]{1,0:T(8,128)(2,1)S(1)}, bf16[192,2176]{1,0:T(8,128)(2,1)S(1)}, u32[]{:S(2)}, u32[]{:S(2)}) collective-permute-start(bf16[192,2176]{1,0:T(8,128)(2,1)S(1)} %bitcast.33), channel_id=1, source_target_pairs={{0,2},{1,3},{2,0},{3,1},{4,6},{5,7},{6,4},{7,5},{8,10},{9,11},{10,... | collective-permute-start | bytes 2506760 | tf_op jit(solution)/shard_map/ppermute | solution.py:34
  28.1 1.2 %fusion.15 = (bf16[1,264,128]{2,1,0:T(8,128)(2,1)S(1)}, bf16[1,264,128]{2,1,0:T(8,128)(2,1)S(1)}, bf16[1,264,128]{2,1,0:T(8,128)(2,1)S(1)}, bf16[1,264,128]{2,1,...) fusion(bf16[4,264,128]{2,1,0:T(8,128)(2,1)} %get-tuple-element., ...), kind=kLoop, calls=%fused_computation.36 | loop fusion | bytes 1081344 | tf_op jit(solution)/shard_map/slice | solution.py:54
  30.1 2.5 %collective-permute-start.8 = (bf16[2,264,128]{2,1,0:T(8,128)(2,1)S(1)}, bf16[2,264,128]{2,1,0:T(8,128)(2,1)S(1)}, u32[]{:S(2)}, u32[]{:S(2)}) collective-permute-start(bf16[2,264,128]{2,1,0:T(8,128)(2,1)S(1)} %pad_maximum_fusion.7), channel_id=1, source_target_pairs={{0,12},{1,13},{2,14},{3,15},{4,8},{5,9},{6,10},{7,11},{8,4},{9,5},... | collective-permute-start | bytes 405512 | tf_op jit(solution)/shard_map/ppermute | solution.py:55
  32.7 3.4 %collective-permute-done.5 = bf16[2,264,128]{2,1,0:T(8,128)(2,1)S(1)} collective-permute-done((bf16[2,264,128]{2,1,0:T(8,128)(2,1)S(1)}, bf16[2,264,128]{2,1,0:T(8,128)(2,1)S(1)}, u32[]{:S(2)}, u32[]{:S(2)}) %collective-permute-start.5) | collective-permute-done | bytes 135200 | tf_op jit(solution)/shard_map/ppermute | solution.py:55
  36.1 3.1 %collective-permute-start.6 = (bf16[2,2,264,128]{3,2,1,0:T(8,128)(2,1)S(1)}, bf16[2,2,264,128]{3,2,1,0:T(8,128)(2,1)S(1)}, u32[]{:S(2)}, u32[]{:S(2)}) collective-permute-start(bf16[2,2,264,128]{3,2,1,0:T(8,128)(2,1)S(1)} %pad_maximum_fusion.1.refs_0_), channel_id=1, source_target_pairs={{0,16},{16,0},{1,17},{17,1},{2,18},{18,2},{3,19},{19,3},{4,20},{20... | collective-permute-start | bytes 811016 | tf_op jit(solution)/shard_map/ppermute | solution.py:409
  39.2 3.6 %collective-permute-start.7 = (bf16[2,264,128]{2,1,0:T(8,128)(2,1)S(1)}, bf16[2,264,128]{2,1,0:T(8,128)(2,1)S(1)}, u32[]{:S(2)}, u32[]{:S(2)}) collective-permute-start(bf16[2,264,128]{2,1,0:T(8,128)(2,1)S(1)} %pad_maximum_fusion.6), channel_id=1, source_target_pairs={{0,8},{1,9},{2,10},{3,11},{4,12},{5,13},{6,14},{7,15},{8,0},{9,1},... | collective-permute-start | bytes 405512 | tf_op jit(solution)/shard_map/ppermute | solution.py:55
  42.8 6.1 %collective-permute-done.7 = bf16[2,264,128]{2,1,0:T(8,128)(2,1)S(1)} collective-permute-done((bf16[2,264,128]{2,1,0:T(8,128)(2,1)S(1)}, bf16[2,264,128]{2,1,0:T(8,128)(2,1)S(1)}, u32[]{:S(2)}, u32[]{:S(2)}) %collective-permute-start.7) | collective-permute-done | bytes 135200 | tf_op jit(solution)/shard_map/ppermute | solution.py:55
  49.0 4.9 %base_products.2 = (f32[384,768]{1,0:T(8,128)S(1)}, f32[384,768]{1,0:T(8,128)S(1)}) custom-call(bf16[192,2176]{1,0:T(8,128)(2,1)S(1)} %bitcast.35, bf16[192,2176]{1,0:T(8,128)(2,1)S(1)} %collective-permute-done.9.refs_1_.refs_2_, bf16[2048,768]{1,0:T(8,128)(2,1)S(1)} %bitcast.39, bf16[2048,768]{1,0:T(8,128)(2,1)S(1)} %bitcast.41), custom_call_target="tpu_custom_call" | custom-call | flops 1 | bytes 1 | tf_op jit(solution)/shard_map/base_products/pallas_call | solution.py:268
  54.2 2.2 %collective-permute-done.11.refs_1_.refs_3_ = bf16[192,2176]{1,0:T(8,128)(2,1)S(1)} collective-permute-done((bf16[192,2176]{1,0:T(8,128)(2,1)S(1)}, bf16[192,2176]{1,0:T(8,128)(2,1)S(1)}, u32[]{:S(2)}, u32[]{:S(2)}) %collective-permute-start.11) | collective-permute-done | bytes 835616 | tf_op jit(solution)/shard_map/ppermute | solution.py:34
  56.4 4.9 %base_products.3 = (f32[384,768]{1,0:T(8,128)S(1)}, f32[384,768]{1,0:T(8,128)S(1)}) custom-call(bf16[192,2176]{1,0:T(8,128)(2,1)S(1)} %collective-permute-done.10.refs_0_.refs_1_, bf16[192,2176]{1,0:T(8,128)(2,1)S(1)} %collective-permute-done.11.refs_1_.refs_3_, bf16[2048,768]{1,0:T(8,128)(2,1)S(1)} %bitcast.40, bf16[2048,768]{1,0:T(8,128)(2,1)S(1)} %bitcast.42), custom_call_target="tpu_custom_call" | custom-call | flops 1 | bytes 1 | tf_op jit(solution)/shard_map/base_products/pallas_call | solution.py:268
  61.3 1.6 %collective-permute-done.12.refs_3_ = bf16[2,2,264,128]{3,2,1,0:T(8,128)(2,1)S(1)} collective-permute-done((bf16[2,2,264,128]{3,2,1,0:T(8,128)(2,1)S(1)}, bf16[2,2,264,128]{3,2,1,0:T(8,128)(2,1)S(1)}, u32[]{:S(2)}, u32[]{:S(2)}) %collective-permute-start.12) | collective-permute-done | bytes 270368 | tf_op jit(solution)/shard_map/ppermute | solution.py:409
  63.0 1.6 %relayout_factors.1 = (bf16[2048,128]{1,0:T(8,128)(2,1)S(1)}, bf16[64,768]{1,0:T(8,128)(2,1)S(1)}, bf16[64,768]{1,0:T(8,128)(2,1)S(1)}, bf16[768,128]{1,0:T(8,128)(2,1)S(1)}, bf16[64,2048]{1,0:T(8,128)(2,1)S(1)}) custom-call(s32[2]{0:T(128)S(1)} %copy-done.3, bf16[2,2,264,128]{3,2,1,0:T(8,128)(2,1)S(1)} %pad_maximum_fusion.1.refs_0_, ...), custom_call_target="tpu_custom_call" | custom-call | flops 1 | bytes 1 | tf_op jit(solution)/shard_map/relayout_factors/pallas_call | solution.py:193
  64.6 6.2 %finish_step.4 = (f32[128,2048]{1,0:T(8,128)S(1)}, bf16[128,2048]{1,0:T(8,128)(2,1)S(1)}) custom-call(s32[2]{0:T(128)S(1)} %copy-done.3, bf16[192,2176]{1,0:T(8,128)(2,1)S(1)} %bitcast.36, bf16[192,2176]{1,0:T(8,128)(2,1)S(1)} %collective-permute-done.10.refs_0_.refs_1_, bf16[192,2176]{1,0:T(8,128)(2,1)S(1)} %collective-permute-done.9.refs_1_.refs_2_, ...), custom_call_target="tpu_custom_call" | custom-call | flops 1 | bytes 1 | tf_op jit(solution)/shard_map/finish_step/pallas_call | solution.py:357
  70.9 6.2 %finish_step.3 = (f32[128,2048]{1,0:T(8,128)S(1)}, bf16[128,2048]{1,0:T(8,128)(2,1)S(1)}) custom-call(s32[2]{0:T(128)S(1)} %copy-done.3, bf16[192,2176]{1,0:T(8,128)(2,1)S(1)} %bitcast.37, bf16[192,2176]{1,0:T(8,128)(2,1)S(1)} %collective-permute-done.10.refs_0_.refs_1_, bf16[192,2176]{1,0:T(8,128)(2,1)S(1)} %collective-permute-done.9.refs_1_.refs_2_, ...), custom_call_target="tpu_custom_call" | custom-call | flops 1 | bytes 1 | tf_op jit(solution)/shard_map/finish_step/pallas_call | solution.py:357
  78.4 0.8 collective-permute-done.13
  80.2 6.2 %finish_step.5 = (f32[128,2048]{1,0:T(8,128)S(1)}, bf16[128,2048]{1,0:T(8,128)(2,1)S(1)}) custom-call(s32[2]{0:T(128)S(1)} %copy-done.3, bf16[192,2176]{1,0:T(8,128)(2,1)S(1)} %bitcast.38, bf16[192,2176]{1,0:T(8,128)(2,1)S(1)} %collective-permute-done.10.refs_0_.refs_1_, bf16[192,2176]{1,0:T(8,128)(2,1)S(1)} %collective-permute-done.9.refs_1_.refs_2_, ...), custom_call_target="tpu_custom_call" | custom-call | flops 1 | bytes 1 | tf_op jit(solution)/shard_map/finish_step/pallas_call | solution.py:357
  87.2 0.8 collective-permute-start.20
  88.0 2.9 %collective-permute-start.22 = (bf16[16,2048]{1,0:T(8,128)(2,1)S(1)}, bf16[16,2048]{1,0:T(8,128)(2,1)S(1)}, u32[]{:S(2)}, u32[]{:S(2)}) collective-permute-start(bf16[16,2048]{1,0:T(8,128)(2,1)S(1)} %get-tuple-element.103), channel_id=1, source_target_pairs={{0,12},{1,13},{2,14},{3,15},{4,8},{5,9},{6,10},{7,11},{8,4},{9,5},... | collective-permute-start | bytes 196616 | tf_op jit(solution)/shard_map/ppermute | solution.py:34
  91.9 0.8 collective-permute-start.15
  92.6 2.9 %collective-permute-start.17 = (bf16[16,2048]{1,0:T(8,128)(2,1)S(1)}, bf16[16,2048]{1,0:T(8,128)(2,1)S(1)}, u32[]{:S(2)}, u32[]{:S(2)}) collective-permute-start(bf16[16,2048]{1,0:T(8,128)(2,1)S(1)} %get-tuple-element.100), channel_id=1, source_target_pairs={{0,12},{1,13},{2,14},{3,15},{4,8},{5,9},{6,10},{7,11},{8,4},{9,5},... | collective-permute-start | bytes 196616 | tf_op jit(solution)/shard_map/ppermute | solution.py:34
  96.8 3.0 %collective-permute-done.21 = bf16[16,2048]{1,0:T(8,128)(2,1)S(1)} collective-permute-done((bf16[16,2048]{1,0:T(8,128)(2,1)S(1)}, bf16[16,2048]{1,0:T(8,128)(2,1)S(1)}, u32[]{:S(2)}, u32[]{:S(2)}) %collective-permute-start.21) | collective-permute-done | bytes 65568 | tf_op jit(solution)/shard_map/ppermute | solution.py:34
  99.8 3.3 %collective-permute-done.24 = bf16[64,2048]{1,0:T(8,128)(2,1)S(1)} collective-permute-done((bf16[64,2048]{1,0:T(8,128)(2,1)S(1)}, bf16[64,2048]{1,0:T(8,128)(2,1)S(1)}, u32[]{:S(2)}, u32[]{:S(2)}) %collective-permute-start.24) | collective-permute-done | bytes 262176 | tf_op jit(solution)/shard_map/ppermute | solution.py:34
  103.2 0.8 collective-permute-start.25
  104.0 3.2 %collective-permute-start.27 = (bf16[16,2048]{1,0:T(8,128)(2,1)S(1)}, bf16[16,2048]{1,0:T(8,128)(2,1)S(1)}, u32[]{:S(2)}, u32[]{:S(2)}) collective-permute-start(bf16[16,2048]{1,0:T(8,128)(2,1)S(1)} %get-tuple-element.106), channel_id=1, source_target_pairs={{0,12},{1,13},{2,14},{3,15},{4,8},{5,9},{6,10},{7,11},{8,4},{9,5},... | collective-permute-start | bytes 196616 | tf_op jit(solution)/shard_map/ppermute | solution.py:34
  107.5 2.6 %collective-permute-done.27 = bf16[16,2048]{1,0:T(8,128)(2,1)S(1)} collective-permute-done((bf16[16,2048]{1,0:T(8,128)(2,1)S(1)}, bf16[16,2048]{1,0:T(8,128)(2,1)S(1)}, u32[]{:S(2)}, u32[]{:S(2)}) %collective-permute-start.27) | collective-permute-done | bytes 65568 | tf_op jit(solution)/shard_map/ppermute | solution.py:34
  110.1 2.2 %collective-permute-done.26 = bf16[16,2048]{1,0:T(8,128)(2,1)S(1)} collective-permute-done((bf16[16,2048]{1,0:T(8,128)(2,1)S(1)}, bf16[16,2048]{1,0:T(8,128)(2,1)S(1)}, u32[]{:S(2)}, u32[]{:S(2)}) %collective-permute-start.26) | collective-permute-done | bytes 65568 | tf_op jit(solution)/shard_map/ppermute | solution.py:34
  (65 shorter events, 9.3 us)
Async XLA Ops:
  0.0 49.0 %copy-start.2 = (bf16[1,2048,768]{2,1,0:T(8,128)(2,1)S(1)}, bf16[1,2048,768]{2,1,0:T(8,128)(2,1)}, u32[]{:S(2)}) copy-start(bf16[1,2048,768]{2,1,0:T(8,128)(2,1)} %param.14) | copy-start | bytes 9437188
  2.1 11.4 %collective-permute-start.2 = (bf16[48,2176]{1,0:T(8,128)(2,1)}, bf16[48,2176]{1,0:T(8,128)(2,1)S(1)}, u32[]{:S(2)}, u32[]{:S(2)}) collective-permute-start(bf16[48,2176]{1,0:T(8,128)(2,1)} %payload.1), channel_id=1, source_target_pairs={{0,12},{1,13},{2,14},{3,15},{4,8},{5,9},{6,10},{7,11},{8,4},{9,5},... | collective-permute-start | bytes 626696 | tf_op jit(solution)/shard_map/ppermute | solution.py:34
  7.2 18.1 %collective-permute-start.1 = (bf16[48,2176]{1,0:T(8,128)(2,1)}, bf16[48,2176]{1,0:T(8,128)(2,1)}, u32[]{:S(2)}, u32[]{:S(2)}) collective-permute-start(bf16[48,2176]{1,0:T(8,128)(2,1)} %payload.1), channel_id=1, source_target_pairs={{0,8},{1,9},{2,10},{3,11},{4,12},{5,13},{6,14},{7,15},{8,0},{9,1},... | collective-permute-start | bytes 626696 | tf_op jit(solution)/shard_map/ppermute | solution.py:34
  7.2 18.1 %collective-permute-start = (bf16[48,2176]{1,0:T(8,128)(2,1)}, bf16[48,2176]{1,0:T(8,128)(2,1)}, u32[]{:S(2)}, u32[]{:S(2)}) collective-permute-start(bf16[48,2176]{1,0:T(8,128)(2,1)} %payload.1), channel_id=1, source_target_pairs={{0,4},{1,5},{2,6},{3,7},{4,0},{5,1},{6,2},{7,3},{8,12},{9,13},{10,... | collective-permute-start | bytes 626696 | tf_op jit(solution)/shard_map/ppermute | solution.py:34
  11.2 15.3 %collective-permute-start.3 = (bf16[4,264,128]{2,1,0:T(8,128)(2,1)}, bf16[4,264,128]{2,1,0:T(8,128)(2,1)S(1)}, u32[]{:S(2)}, u32[]{:S(2)}) collective-permute-start(bf16[4,264,128]{2,1,0:T(8,128)(2,1)} %get-tuple-element.48), channel_id=1, source_target_pairs={{0,2},{1,3},{2,0},{3,1},{4,6},{5,7},{6,4},{7,5},{8,10},{9,11},{10,... | collective-permute-start | bytes 811016 | tf_op jit(solution)/shard_map/ppermute | solution.py:34
  26.5 27.4 %collective-permute-start.10 = (bf16[192,2176]{1,0:T(8,128)(2,1)S(1)}, bf16[192,2176]{1,0:T(8,128)(2,1)S(1)}, u32[]{:S(2)}, u32[]{:S(2)}) collective-permute-start(bf16[192,2176]{1,0:T(8,128)(2,1)S(1)} %bitcast.33), channel_id=1, source_target_pairs={{0,2},{1,3},{2,0},{3,1},{4,6},{5,7},{6,4},{7,5},{8,10},{9,11},{10,... | collective-permute-start | bytes 2506760 | tf_op jit(solution)/shard_map/ppermute | solution.py:34
  28.1 20.9 %collective-permute-start.9 = (bf16[192,2176]{1,0:T(8,128)(2,1)S(1)}, bf16[192,2176]{1,0:T(8,128)(2,1)S(1)}, u32[]{:S(2)}, u32[]{:S(2)}) collective-permute-start(bf16[192,2176]{1,0:T(8,128)(2,1)S(1)} %bitcast.34), channel_id=1, source_target_pairs={{0,1},{1,0},{2,3},{3,2},{4,5},{5,4},{6,7},{7,6},{8,9},{9,8},{10,11... | collective-permute-start | bytes 2506760 | tf_op jit(solution)/shard_map/ppermute | solution.py:34
  28.1 20.9 %copy-start.1 = (bf16[1,2048,768]{2,1,0:T(8,128)(2,1)S(1)}, bf16[1,2048,768]{2,1,0:T(8,128)(2,1)}, u32[]{:S(2)}) copy-start(bf16[1,2048,768]{2,1,0:T(8,128)(2,1)} %param.13) | copy-start | bytes 9437188
  29.3 3.3 %collective-permute-start.4 = (bf16[2,264,128]{2,1,0:T(8,128)(2,1)S(1)}, bf16[2,264,128]{2,1,0:T(8,128)(2,1)S(1)}, u32[]{:S(2)}, u32[]{:S(2)}) collective-permute-start(bf16[2,264,128]{2,1,0:T(8,128)(2,1)S(1)} %pad_maximum_fusion.4), channel_id=1, source_target_pairs={{0,0},{1,1},{2,2},{3,3},{4,4},{5,5},{6,6},{7,7},{8,8},{9,9},{10,10... | collective-permute-start | bytes 405512 | tf_op jit(solution)/shard_map/ppermute | solution.py:55
  30.0 6.1 %collective-permute-start.5 = (bf16[2,264,128]{2,1,0:T(8,128)(2,1)S(1)}, bf16[2,264,128]{2,1,0:T(8,128)(2,1)S(1)}, u32[]{:S(2)}, u32[]{:S(2)}) collective-permute-start(bf16[2,264,128]{2,1,0:T(8,128)(2,1)S(1)} %pad_maximum_fusion.5), channel_id=1, source_target_pairs={{0,4},{1,5},{2,6},{3,7},{4,0},{5,1},{6,2},{7,3},{8,12},{9,13},{10,... | collective-permute-start | bytes 405512 | tf_op jit(solution)/shard_map/ppermute | solution.py:55
  30.1 12.7 %collective-permute-start.8 = (bf16[2,264,128]{2,1,0:T(8,128)(2,1)S(1)}, bf16[2,264,128]{2,1,0:T(8,128)(2,1)S(1)}, u32[]{:S(2)}, u32[]{:S(2)}) collective-permute-start(bf16[2,264,128]{2,1,0:T(8,128)(2,1)S(1)} %pad_maximum_fusion.7), channel_id=1, source_target_pairs={{0,12},{1,13},{2,14},{3,15},{4,8},{5,9},{6,10},{7,11},{8,4},{9,5},... | collective-permute-start | bytes 405512 | tf_op jit(solution)/shard_map/ppermute | solution.py:55
  36.1 17.9 %collective-permute-start.6 = (bf16[2,2,264,128]{3,2,1,0:T(8,128)(2,1)S(1)}, bf16[2,2,264,128]{3,2,1,0:T(8,128)(2,1)S(1)}, u32[]{:S(2)}, u32[]{:S(2)}) collective-permute-start(bf16[2,2,264,128]{3,2,1,0:T(8,128)(2,1)S(1)} %pad_maximum_fusion.1.refs_0_), channel_id=1, source_target_pairs={{0,16},{16,0},{1,17},{17,1},{2,18},{18,2},{3,19},{19,3},{4,20},{20... | collective-permute-start | bytes 811016 | tf_op jit(solution)/shard_map/ppermute | solution.py:409
  39.2 9.8 %collective-permute-start.7 = (bf16[2,264,128]{2,1,0:T(8,128)(2,1)S(1)}, bf16[2,264,128]{2,1,0:T(8,128)(2,1)S(1)}, u32[]{:S(2)}, u32[]{:S(2)}) collective-permute-start(bf16[2,264,128]{2,1,0:T(8,128)(2,1)S(1)} %pad_maximum_fusion.6), channel_id=1, source_target_pairs={{0,8},{1,9},{2,10},{3,11},{4,12},{5,13},{6,14},{7,15},{8,0},{9,1},... | collective-permute-start | bytes 405512 | tf_op jit(solution)/shard_map/ppermute | solution.py:55
  54.0 9.0 %copy-start.3 = (s32[2]{0:T(128)S(1)}, s32[2]{0:T(128)}, u32[]{:S(2)}) copy-start(s32[2]{0:T(128)} %pad_add_fusion.place_ref) | copy-start | bytes 28
  54.0 2.4 %collective-permute-start.11 = (bf16[192,2176]{1,0:T(8,128)(2,1)S(1)}, bf16[192,2176]{1,0:T(8,128)(2,1)S(1)}, u32[]{:S(2)}, u32[]{:S(2)}) collective-permute-start(bf16[192,2176]{1,0:T(8,128)(2,1)S(1)} %collective-permute-done.10.refs_0_.refs_1_), channel_id=1, source_target_pairs={{0,1},{1,0},{2,3},{3,2},{4,5},{5,4},{6,7},{7,6},{8,9},{9,8},{10,11... | collective-permute-start | bytes 2506760 | tf_op jit(solution)/shard_map/ppermute | solution.py:34
  54.1 8.9 %collective-permute-start.12 = (bf16[2,2,264,128]{3,2,1,0:T(8,128)(2,1)S(1)}, bf16[2,2,264,128]{3,2,1,0:T(8,128)(2,1)S(1)}, u32[]{:S(2)}, u32[]{:S(2)}) collective-permute-start(bf16[2,2,264,128]{3,2,1,0:T(8,128)(2,1)S(1)} %pad_maximum_fusion.2.refs_1_), channel_id=1, source_target_pairs={{0,16},{16,0},{1,17},{17,1},{2,18},{18,2},{3,19},{19,3},{4,20},{20... | collective-permute-start | bytes 811016 | tf_op jit(solution)/shard_map/ppermute | solution.py:409
  56.4 8.1 %copy-start = (bf16[1,768,2048]{2,1,0:T(8,128)(2,1)S(1)}, bf16[1,768,2048]{2,1,0:T(8,128)(2,1)}, u32[]{:S(2)}) copy-start(bf16[1,768,2048]{2,1,0:T(8,128)(2,1)} %param.15) | copy-start | bytes 9437188
  70.8 6.9 %collective-permute-start.18 = (bf16[128,2048]{1,0:T(8,128)(2,1)S(1)}, bf16[128,2048]{1,0:T(8,128)(2,1)S(1)}, u32[]{:S(2)}, u32[]{:S(2)}) collective-permute-start(bf16[128,2048]{1,0:T(8,128)(2,1)S(1)} %get-tuple-element.78), channel_id=1, source_target_pairs={{0,1},{1,0},{2,3},{3,2},{4,5},{5,4},{6,7},{7,6},{8,9},{9,8},{10,11... | collective-permute-start | bytes 1572872 | tf_op jit(solution)/shard_map/ppermute | solution.py:34
  77.1 2.1 %collective-permute-start.13 = (bf16[128,2048]{1,0:T(8,128)(2,1)S(1)}, bf16[128,2048]{1,0:T(8,128)(2,1)S(1)}, u32[]{:S(2)}, u32[]{:S(2)}) collective-permute-start(bf16[128,2048]{1,0:T(8,128)(2,1)S(1)} %get-tuple-element.75), channel_id=1, source_target_pairs={{0,1},{1,0},{2,3},{3,2},{4,5},{5,4},{6,7},{7,6},{8,9},{9,8},{10,11... | collective-permute-start | bytes 1572872 | tf_op jit(solution)/shard_map/ppermute | solution.py:34
  77.8 9.2 %collective-permute-start.19 = (bf16[64,2048]{1,0:T(8,128)(2,1)S(1)}, bf16[64,2048]{1,0:T(8,128)(2,1)S(1)}, u32[]{:S(2)}, u32[]{:S(2)}) collective-permute-start(bf16[64,2048]{1,0:T(8,128)(2,1)S(1)} %slice.167), channel_id=1, source_target_pairs={{0,2},{1,3},{2,0},{3,1},{4,6},{5,7},{6,4},{7,5},{8,10},{9,11},{10,... | collective-permute-start | bytes 786440 | tf_op jit(solution)/shard_map/ppermute | solution.py:34
  79.4 12.4 %collective-permute-start.14 = (bf16[64,2048]{1,0:T(8,128)(2,1)S(1)}, bf16[64,2048]{1,0:T(8,128)(2,1)S(1)}, u32[]{:S(2)}, u32[]{:S(2)}) collective-permute-start(bf16[64,2048]{1,0:T(8,128)(2,1)S(1)} %slice.168), channel_id=1, source_target_pairs={{0,2},{1,3},{2,0},{3,1},{4,6},{5,7},{6,4},{7,5},{8,10},{9,11},{10,... | collective-permute-start | bytes 786440 | tf_op jit(solution)/shard_map/ppermute | solution.py:34
  86.4 6.3 %collective-permute-start.23 = (bf16[128,2048]{1,0:T(8,128)(2,1)S(1)}, bf16[128,2048]{1,0:T(8,128)(2,1)S(1)}, u32[]{:S(2)}, u32[]{:S(2)}) collective-permute-start(bf16[128,2048]{1,0:T(8,128)(2,1)S(1)} %get-tuple-element.84), channel_id=1, source_target_pairs={{0,1},{1,0},{2,3},{3,2},{4,5},{5,4},{6,7},{7,6},{8,9},{9,8},{10,11... | collective-permute-start | bytes 1572872 | tf_op jit(solution)/shard_map/ppermute | solution.py:34
  87.2 8.5 %collective-permute-start.20 = (bf16[16,2048]{1,0:T(8,128)(2,1)S(1)}, bf16[16,2048]{1,0:T(8,128)(2,1)S(1)}, u32[]{:S(2)}, u32[]{:S(2)}) collective-permute-start(bf16[16,2048]{1,0:T(8,128)(2,1)S(1)} %get-tuple-element.102), channel_id=1, source_target_pairs={{0,4},{1,5},{2,6},{3,7},{4,0},{5,1},{6,2},{7,3},{8,12},{9,13},{10,... | collective-permute-start | bytes 196616 | tf_op jit(solution)/shard_map/ppermute | solution.py:34
  88.0 8.3 %collective-permute-start.22 = (bf16[16,2048]{1,0:T(8,128)(2,1)S(1)}, bf16[16,2048]{1,0:T(8,128)(2,1)S(1)}, u32[]{:S(2)}, u32[]{:S(2)}) collective-permute-start(bf16[16,2048]{1,0:T(8,128)(2,1)S(1)} %get-tuple-element.103), channel_id=1, source_target_pairs={{0,12},{1,13},{2,14},{3,15},{4,8},{5,9},{6,10},{7,11},{8,4},{9,5},... | collective-permute-start | bytes 196616 | tf_op jit(solution)/shard_map/ppermute | solution.py:34
  90.8 8.9 %collective-permute-start.21 = (bf16[16,2048]{1,0:T(8,128)(2,1)S(1)}, bf16[16,2048]{1,0:T(8,128)(2,1)S(1)}, u32[]{:S(2)}, u32[]{:S(2)}) collective-permute-start(bf16[16,2048]{1,0:T(8,128)(2,1)S(1)} %get-tuple-element.104), channel_id=1, source_target_pairs={{0,8},{1,9},{2,10},{3,11},{4,12},{5,13},{6,14},{7,15},{8,0},{9,1},... | collective-permute-start | bytes 196616 | tf_op jit(solution)/shard_map/ppermute | solution.py:34
  91.9 15.3 %collective-permute-start.15 = (bf16[16,2048]{1,0:T(8,128)(2,1)S(1)}, bf16[16,2048]{1,0:T(8,128)(2,1)S(1)}, u32[]{:S(2)}, u32[]{:S(2)}) collective-permute-start(bf16[16,2048]{1,0:T(8,128)(2,1)S(1)} %get-tuple-element.99), channel_id=1, source_target_pairs={{0,4},{1,5},{2,6},{3,7},{4,0},{5,1},{6,2},{7,3},{8,12},{9,13},{10,... | collective-permute-start | bytes 196616 | tf_op jit(solution)/shard_map/ppermute | solution.py:34
  92.6 14.5 %collective-permute-start.17 = (bf16[16,2048]{1,0:T(8,128)(2,1)S(1)}, bf16[16,2048]{1,0:T(8,128)(2,1)S(1)}, u32[]{:S(2)}, u32[]{:S(2)}) collective-permute-start(bf16[16,2048]{1,0:T(8,128)(2,1)S(1)} %get-tuple-element.100), channel_id=1, source_target_pairs={{0,12},{1,13},{2,14},{3,15},{4,8},{5,9},{6,10},{7,11},{8,4},{9,5},... | collective-permute-start | bytes 196616 | tf_op jit(solution)/shard_map/ppermute | solution.py:34
  95.7 11.5 %collective-permute-start.16 = (bf16[16,2048]{1,0:T(8,128)(2,1)S(1)}, bf16[16,2048]{1,0:T(8,128)(2,1)S(1)}, u32[]{:S(2)}, u32[]{:S(2)}) collective-permute-start(bf16[16,2048]{1,0:T(8,128)(2,1)S(1)} %get-tuple-element.101), channel_id=1, source_target_pairs={{0,8},{1,9},{2,10},{3,11},{4,12},{5,13},{6,14},{7,15},{8,0},{9,1},... | collective-permute-start | bytes 196616 | tf_op jit(solution)/shard_map/ppermute | solution.py:34
  96.3 6.8 %collective-permute-start.24 = (bf16[64,2048]{1,0:T(8,128)(2,1)S(1)}, bf16[64,2048]{1,0:T(8,128)(2,1)S(1)}, u32[]{:S(2)}, u32[]{:S(2)}) collective-permute-start(bf16[64,2048]{1,0:T(8,128)(2,1)S(1)} %slice.166), channel_id=1, source_target_pairs={{0,2},{1,3},{2,0},{3,1},{4,6},{5,7},{6,4},{7,5},{8,10},{9,11},{10,... | collective-permute-start | bytes 786440 | tf_op jit(solution)/shard_map/ppermute | solution.py:34
  103.2 4.3 %collective-permute-start.25 = (bf16[16,2048]{1,0:T(8,128)(2,1)S(1)}, bf16[16,2048]{1,0:T(8,128)(2,1)S(1)}, u32[]{:S(2)}, u32[]{:S(2)}) collective-permute-start(bf16[16,2048]{1,0:T(8,128)(2,1)S(1)} %get-tuple-element.105), channel_id=1, source_target_pairs={{0,4},{1,5},{2,6},{3,7},{4,0},{5,1},{6,2},{7,3},{8,12},{9,13},{10,... | collective-permute-start | bytes 196616 | tf_op jit(solution)/shard_map/ppermute | solution.py:34
  104.0 6.1 %collective-permute-start.27 = (bf16[16,2048]{1,0:T(8,128)(2,1)S(1)}, bf16[16,2048]{1,0:T(8,128)(2,1)S(1)}, u32[]{:S(2)}, u32[]{:S(2)}) collective-permute-start(bf16[16,2048]{1,0:T(8,128)(2,1)S(1)} %get-tuple-element.106), channel_id=1, source_target_pairs={{0,12},{1,13},{2,14},{3,15},{4,8},{5,9},{6,10},{7,11},{8,4},{9,5},... | collective-permute-start | bytes 196616 | tf_op jit(solution)/shard_map/ppermute | solution.py:34
  107.2 5.2 %collective-permute-start.26 = (bf16[16,2048]{1,0:T(8,128)(2,1)S(1)}, bf16[16,2048]{1,0:T(8,128)(2,1)S(1)}, u32[]{:S(2)}, u32[]{:S(2)}) collective-permute-start(bf16[16,2048]{1,0:T(8,128)(2,1)S(1)} %get-tuple-element.107), channel_id=1, source_target_pairs={{0,8},{1,9},{2,10},{3,11},{4,12},{5,13},{6,14},{7,15},{8,0},{9,1},... | collective-permute-start | bytes 196616 | tf_op jit(solution)/shard_map/ppermute | solution.py:34

commit v15 on v10

--- a/solution.py
+++ b/solution.py
@@ -41,6 +41,18 @@
         part = total[k * count : (k + 1) * count].astype(jnp.bfloat16)
         result = result + swap(part, n, stride, k).astype(jnp.float32)
     return result
+
+
+def halve_along(total, n, stride, size):
+    count = total.shape[0] // size
+    step = 1
+    while step < size:
+        total = total.reshape(-1, 2, count, total.shape[1])
+        sent = total[:, 1].reshape(-1, total.shape[3]).astype(jnp.bfloat16)
+        kept = total[:, 0].reshape(-1, total.shape[3])
+        total = kept + swap(sent, n, stride, step).astype(jnp.float32)
+        step *= 2
+    return total
 
 
 def exchange_factors(blocks, n):
@@ -92,10 +104,10 @@
     )(hidden, jnp.swapaxes(route_ids, 1, 2), jnp.swapaxes(route_logits, 1, 2))
 
 
-def order_kernel(middle, place_ref, placement_ref, factors_ref, *refs):
-    out_refs, wide_ref = refs[:-1], refs[-1]
+def order_kernel(place_ref, placement_ref, factors_ref, *refs):
+    out_refs, wide_ref, slot_ref = refs[:-2], refs[-2], refs[-1]
     slots = factors_ref.shape[0]
-    length, lanes = out_refs[0].shape[1:]
+    outer, length, lanes = out_refs[0].shape
     group, me = place_ref[0], place_ref[1]
 
     def cut(t, carry):
@@ -105,37 +117,30 @@
         return carry
 
     lax.fori_loop(0, length, cut, 0, unroll=8)
-
-    def put(s, carry):
-        to = placement_ref[s]
-        away = to ^ me
-        aside, ahead = lax.rem(away // 2, middle), away // (2 * middle)
-        ours = lax.rem(away, 2) == group
-        rows = wide_ref[pl.ds(pl.multiple_of(s * length, 8), length), :].astype(jnp.bfloat16)
-        for r, out_ref in enumerate(out_refs):
-
-            @pl.when(jnp.logical_and(ours, aside == r))
-            def _():
-                out_ref[ahead] = rows
-
-        return carry
-
-    lax.fori_loop(0, slots, put, 0)
-
-
-def order_factors(place, placement, factors, n):
-    outer, middle, _ = split_axis(n)
+    for s in range(slots):
+        slot_ref[placement_ref[s]] = s
+    for r, out_ref in enumerate(out_refs):
+        for q in range(outer):
+            slot = slot_ref[me ^ (2 * (q * len(out_refs) + r) + group)]
+            rows = wide_ref[pl.ds(pl.multiple_of(slot * length, 8), length), :]
+            out_ref[q] = rows.astype(jnp.bfloat16)
+
+
+def order_factors(place, placement, factors, outer, middle):
     slots, entries = factors.shape
     length = entries // LANES
     return pl.pallas_call(
-        functools.partial(order_kernel, middle),
+        order_kernel,
         out_shape=[jax.ShapeDtypeStruct((outer, length, LANES), jnp.bfloat16)] * middle,
         in_specs=[
             pl.BlockSpec(memory_space=pltpu.SMEM),
             pl.BlockSpec(memory_space=pltpu.SMEM),
             pl.BlockSpec(memory_space=pltpu.VMEM),
         ],
-        scratch_shapes=[pltpu.VMEM((slots * length, LANES), jnp.float32)],
+        scratch_shapes=[
+            pltpu.VMEM((slots * length, LANES), jnp.float32),
+            pltpu.SMEM((slots,), jnp.int32),
+        ],
         compiler_params=pltpu.CompilerParams(vmem_limit_bytes=WHOLE_GRANT),
         cost_estimate=LITTLE,
         name="order_factors",
@@ -402,7 +407,7 @@
     rows_in, factors = lax.optimization_barrier((rows_in, factors))
     column = [p.reshape(steps, rows, -1) for p in along(rows_in, *along_outer)]
     column = jnp.stack(column, axis=1).reshape(steps * outer * rows, -1)
-    blocks = order_factors(place, placement, factors, owners)
+    blocks = order_factors(place, placement, factors, outer, middle)
     blocks = [blocks[0]] + [swap(blocks[r], owners, cores, r) for r in range(1, middle)]
     column, blocks = lax.optimization_barrier((column, blocks))
     here = exchange_factors(blocks, owners)
@@ -422,8 +427,11 @@
             pieces, results[s - 2] = lax.optimization_barrier((pieces, results[s - 2]))
         kept, sent = finish_step(place, pieces, base, s * span, span, low_rank, down_weight[0])
         results.append(kept + swap(sent, owners, 1, 1).astype(jnp.float32))
-    results = [scatter_along(total, owners, *along_middle) for total in results]
-    results = [scatter_along(total, owners, *along_outer) for total in results]
+    results[:-1] = [scatter_along(total, owners, *along_middle) for total in results[:-1]]
+    results = lax.optimization_barrier(results)
+    results[-1] = scatter_along(results[-1], owners, *along_middle)
+    results[:-1] = [halve_along(total, owners, *along_outer) for total in results[:-1]]
+    results[-1] = scatter_along(results[-1], owners, *along_outer)
     return jnp.stack(results).astype(jnp.bfloat16)
 
 

time: 111 us -> 112 us (level)
  waiting for transfers between devices: 38.6 us -> 42.5 us
  starting transfers between devices: 32.3 us -> 29.9 us
    ppermute x22 -> x20, waiting for transfers between devices: 27.4 us -> 31.3 us  [swap(): return lax.ppermute(x, 'expert', [(i, i ^ k * stride) for i in range(n)])]
    ppermute x22 -> x20, starting transfers between devices: 25.5 us -> 23.1 us  [swap(): return lax.ppermute(x, 'expert', [(i, i ^ k * stride) for i in range(n)])]
  transfers between devices with their start and end apart: 27 -> 25, of which waited for: 13 -> 15; matrix products, arithmetic and copies ran while one was open for 3% -> 3% of each run, Pallas kernels for 23% -> 22%
where the time goes in v15:
time: 112 us
  waiting for transfers between devices  42.5 us (38%)
  Pallas kernels  34.5 us (31%)
  starting transfers between devices  29.9 us (27%)
  other arithmetic  3.33 us (3%)
  local copies, waits for them, and re-layouts  1.22 us (1%)
    ppermute x20, waiting for transfers between devices, swap(): return lax.ppermute(x, 'expert', [(i, i ^ k * stride) for i in range(n)])  31.3 us
    ppermute x20, starting transfers between devices, swap(): return lax.ppermute(x, 'expert', [(i, i ^ k * stride) for i in range(n)])  23.1 us
    pallas_call x3, Pallas kernels, finish_step(): pl.pallas_call(functools.partial(finish_kernel, len(pieces), first, rows)...  18.7 us
    pallas_call x1, Pallas kernels, base_products(): pl.pallas_call(functools.partial(base_kernel, len(pieces)), out_shape=[ou...  9.3 us
    ppermute x4, waiting for transfers between devices, exchange_factors(): here.append(lax.ppermute(part, ('group', 'expert'), pairs))  8.09 us
    ppermute x4, starting transfers between devices, exchange_factors(): here.append(lax.ppermute(part, ('group', 'expert'), pairs))  5.24 us
    ppermute x1, waiting for transfers between devices, dense_shards(): there = lax.ppermute(here, 'group', [(0, 1), (1, 0)])  3.15 us
    pallas_call x1, Pallas kernels, order_factors(): pl.pallas_call(order_kernel, out_shape=[jax.ShapeDtypeStruct((outer, leng...  2.77 us
  transfers between devices with their start and end apart: 25, of which 15 were waited for; matrix products, arithmetic and copies ran while one was open for 3% of the time, Pallas kernels for 22%

profile of v15, /device:TPU:0, one launch (start us, length us, event | category | flops | bytes accessed | tf_op | source)
XLA Modules:
  0.0 111.7 jit_solution(1270617175707378511)
XLA Ops:
  0.0 2.1 %payload.1 = bf16[48,2176]{1,0:T(8,128)(2,1)} custom-call(bf16[3,16,2048]{2,1,0:T(8,128)(2,1)} %hidden_ref.1, s32[3,8,16]{2,1,0:T(8,128)} %bitcast.87, f32[3,8,16]{2,1,0:T(8,128)} %bitcast.88), custom_call_target="tpu_custom_call" | custom-call | flops 1 | bytes 1 | tf_op jit(solution)/shard_map/payload/pallas_call | solution.py:97
  2.1 5.0 %collective-permute-start.2 = (bf16[48,2176]{1,0:T(8,128)(2,1)}, bf16[48,2176]{1,0:T(8,128)(2,1)S(1)}, u32[]{:S(2)}, u32[]{:S(2)}) collective-permute-start(bf16[48,2176]{1,0:T(8,128)(2,1)} %payload.1), channel_id=1, source_target_pairs={{0,12},{1,13},{2,14},{3,15},{4,8},{5,9},{6,10},{7,11},{8,4},{9,5},... | collective-permute-start | bytes 626696 | tf_op jit(solution)/shard_map/ppermute | solution.py:34
  8.3 2.8 %order_factors.1 = (bf16[4,264,128]{2,1,0:T(8,128)(2,1)}, bf16[4,264,128]{2,1,0:T(8,128)(2,1)}) custom-call(s32[2]{0:T(128)} %pad_add_fusion.place_ref, s32[16]{0:T(128)} %placement_ref.1, bf16[16,33792]{1,0:T(8,128)(2,1)} %factors_ref), custom_call_target="tpu_custom_call" | custom-call | flops 1 | bytes 1 | tf_op jit(solution)/shard_map/order_factors/pallas_call | solution.py:132
  11.1 1.7 %collective-permute-start.3 = (bf16[4,264,128]{2,1,0:T(8,128)(2,1)}, bf16[4,264,128]{2,1,0:T(8,128)(2,1)S(1)}, u32[]{:S(2)}, u32[]{:S(2)}) collective-permute-start(bf16[4,264,128]{2,1,0:T(8,128)(2,1)} %get-tuple-element.45), channel_id=1, source_target_pairs={{0,2},{1,3},{2,0},{3,1},{4,6},{5,7},{6,4},{7,5},{8,10},{9,11},{10,... | collective-permute-start | bytes 811016 | tf_op jit(solution)/shard_map/ppermute | solution.py:34
  13.5 11.7 %collective-permute-done.1 = bf16[48,2176]{1,0:T(8,128)(2,1)} collective-permute-done((bf16[48,2176]{1,0:T(8,128)(2,1)}, bf16[48,2176]{1,0:T(8,128)(2,1)}, u32[]{:S(2)}, u32[]{:S(2)}) %collective-permute-start.1) | collective-permute-done | bytes 208928 | tf_op jit(solution)/shard_map/ppermute | solution.py:34
  25.2 1.3 %pad_maximum_fusion = bf16[3,4,16,2176]{3,2,1,0:T(8,128)(2,1)S(1)} fusion(bf16[3,1,16,2176]{3,2,1,0:T(8,128)(2,1)S(1)} %bitcast.80, bf16[3,1,16,2176]{3,2,1,0:T(8,128)(2,1)} %bitcast.7, bf16[3,1,16,2176]{3,2,1,0:T(8,128)(2,1)} %bitcast.5, bf16[3,1,16,2176]{3,2,1,0:T(8,128)(2,1)} %bitcast.75), kind=kLoop, calls=%fused_computation.3 | loop fusion | flops 1253376 | bytes 1671168 | tf_op jit(solution)/shard_map/stack | solution.py:409
  26.5 1.6 %collective-permute-start.8 = (bf16[192,2176]{1,0:T(8,128)(2,1)S(1)}, bf16[192,2176]{1,0:T(8,128)(2,1)S(1)}, u32[]{:S(2)}, u32[]{:S(2)}) collective-permute-start(bf16[192,2176]{1,0:T(8,128)(2,1)S(1)} %bitcast.63), channel_id=1, source_target_pairs={{0,2},{1,3},{2,0},{3,1},{4,6},{5,7},{6,4},{7,5},{8,10},{9,11},{10,... | collective-permute-start | bytes 2506760 | tf_op jit(solution)/shard_map/ppermute | solution.py:34
  28.1 1.0 fusion.13
  29.9 3.1 %collective-permute-start.6 = (bf16[2,264,128]{2,1,0:T(8,128)(2,1)S(1)}, bf16[2,264,128]{2,1,0:T(8,128)(2,1)S(1)}, u32[]{:S(2)}, u32[]{:S(2)}) collective-permute-start(bf16[2,264,128]{2,1,0:T(8,128)(2,1)S(1)} %pad_maximum_fusion.5), channel_id=1, source_target_pairs={{0,8},{1,9},{2,10},{3,11},{4,12},{5,13},{6,14},{7,15},{8,0},{9,1},... | collective-permute-start | bytes 405512 | tf_op jit(solution)/shard_map/ppermute | solution.py:67
  33.0 1.4 %collective-permute-start.7 = (bf16[2,264,128]{2,1,0:T(8,128)(2,1)S(1)}, bf16[2,264,128]{2,1,0:T(8,128)(2,1)S(1)}, u32[]{:S(2)}, u32[]{:S(2)}) collective-permute-start(bf16[2,264,128]{2,1,0:T(8,128)(2,1)S(1)} %pad_maximum_fusion.6), channel_id=1, source_target_pairs={{0,12},{1,13},{2,14},{3,15},{4,8},{5,9},{6,10},{7,11},{8,4},{9,5},... | collective-permute-start | bytes 405512 | tf_op jit(solution)/shard_map/ppermute | solution.py:67
  34.5 1.6 %collective-permute-done.5 = bf16[2,264,128]{2,1,0:T(8,128)(2,1)S(1)} collective-permute-done((bf16[2,264,128]{2,1,0:T(8,128)(2,1)S(1)}, bf16[2,264,128]{2,1,0:T(8,128)(2,1)S(1)}, u32[]{:S(2)}, u32[]{:S(2)}) %collective-permute-start.5) | collective-permute-done | bytes 135200 | tf_op jit(solution)/shard_map/ppermute | solution.py:67
  36.0 6.5 %collective-permute-done.6 = bf16[2,264,128]{2,1,0:T(8,128)(2,1)S(1)} collective-permute-done((bf16[2,264,128]{2,1,0:T(8,128)(2,1)S(1)}, bf16[2,264,128]{2,1,0:T(8,128)(2,1)S(1)}, u32[]{:S(2)}, u32[]{:S(2)}) %collective-permute-start.6) | collective-permute-done | bytes 135200 | tf_op jit(solution)/shard_map/ppermute | solution.py:67
  42.6 3.7 %collective-permute-done.8.refs_1_ = bf16[192,2176]{1,0:T(8,128)(2,1)S(1)} collective-permute-done((bf16[192,2176]{1,0:T(8,128)(2,1)S(1)}, bf16[192,2176]{1,0:T(8,128)(2,1)S(1)}, u32[]{:S(2)}, u32[]{:S(2)}) %collective-permute-start.8) | collective-permute-done | bytes 835616 | tf_op jit(solution)/shard_map/ppermute | solution.py:34
  46.3 1.6 %collective-permute-start.11 = (bf16[4,2,264,128]{3,2,1,0:T(8,128)(2,1)S(1)}, bf16[4,2,264,128]{3,2,1,0:T(8,128)(2,1)S(1)}, u32[]{:S(2)}, u32[]{:S(2)}) collective-permute-start(bf16[4,2,264,128]{3,2,1,0:T(8,128)(2,1)S(1)} %pad_maximum_fusion.1.refs_0_), channel_id=1, source_target_pairs={{0,16},{16,0},{1,17},{17,1},{2,18},{18,2},{3,19},{19,3},{4,20},{20... | collective-permute-start | bytes 1622024 | tf_op jit(solution)/shard_map/ppermute | solution.py:417
  48.6 9.3 %base_products.1 = (f32[768,768]{1,0:T(8,128)S(1)}, f32[768,768]{1,0:T(8,128)S(1)}) custom-call(bf16[192,2176]{1,0:T(8,128)(2,1)S(1)} %bitcast.65, bf16[192,2176]{1,0:T(8,128)(2,1)S(1)} %collective-permute-done.8.refs_1_, bf16[192,2176]{1,0:T(8,128)(2,1)S(1)} %collective-permute-done.9.refs_2_, bf16[192,2176]{1,0:T(8,128)(2,1)S(1)} %collective-permute-done.10.refs_3_, ...), custom_call_target="tpu_custom_call" | custom-call | flops 1 | bytes 1 | tf_op jit(solution)/shard_map/base_products/pallas_call | solution.py:279
  57.9 3.1 %collective-permute-done.11.refs_1_ = bf16[4,2,264,128]{3,2,1,0:T(8,128)(2,1)S(1)} collective-permute-done((bf16[4,2,264,128]{3,2,1,0:T(8,128)(2,1)S(1)}, bf16[4,2,264,128]{3,2,1,0:T(8,128)(2,1)S(1)}, u32[]{:S(2)}, u32[]{:S(2)}) %collective-permute-start.11) | collective-permute-done | bytes 540704 | tf_op jit(solution)/shard_map/ppermute | solution.py:417
  61.1 1.6 %relayout_factors.1 = (bf16[2048,128]{1,0:T(8,128)(2,1)S(1)}, bf16[64,768]{1,0:T(8,128)(2,1)S(1)}, bf16[64,768]{1,0:T(8,128)(2,1)S(1)}, bf16[768,128]{1,0:T(8,128)(2,1)S(1)}, bf16[64,2048]{1,0:T(8,128)(2,1)S(1)}) custom-call(s32[2]{0:T(128)S(1)} %copy-done.3, bf16[4,2,264,128]{3,2,1,0:T(8,128)(2,1)S(1)} %pad_maximum_fusion.1.refs_0_, ...), custom_call_target="tpu_custom_call" | custom-call | flops 1 | bytes 1 | tf_op jit(solution)/shard_map/relayout_factors/pallas_call | solution.py:204
  62.6 6.2 %finish_step.4 = (f32[128,2048]{1,0:T(8,128)S(1)}, bf16[128,2048]{1,0:T(8,128)(2,1)S(1)}) custom-call(s32[2]{0:T(128)S(1)} %copy-done.3, bf16[192,2176]{1,0:T(8,128)(2,1)S(1)} %bitcast.66, bf16[192,2176]{1,0:T(8,128)(2,1)S(1)} %collective-permute-done.8.refs_1_, bf16[192,2176]{1,0:T(8,128)(2,1)S(1)} %collective-permute-done.9.refs_2_, ...), custom_call_target="tpu_custom_call" | custom-call | flops 1 | bytes 1 | tf_op jit(solution)/shard_map/finish_step/pallas_call | solution.py:366
  69.0 6.2 %finish_step.3 = (f32[128,2048]{1,0:T(8,128)S(1)}, bf16[128,2048]{1,0:T(8,128)(2,1)S(1)}) custom-call(s32[2]{0:T(128)S(1)} %copy-done.3, bf16[192,2176]{1,0:T(8,128)(2,1)S(1)} %bitcast.67, bf16[192,2176]{1,0:T(8,128)(2,1)S(1)} %collective-permute-done.8.refs_1_, bf16[192,2176]{1,0:T(8,128)(2,1)S(1)} %collective-permute-done.9.refs_2_, ...), custom_call_target="tpu_custom_call" | custom-call | flops 1 | bytes 1 | tf_op jit(solution)/shard_map/finish_step/pallas_call | solution.py:366
  75.9 1.6 %collective-permute-start.15 = (bf16[64,2048]{1,0:T(8,128)(2,1)S(1)}, bf16[64,2048]{1,0:T(8,128)(2,1)S(1)}, u32[]{:S(2)}, u32[]{:S(2)}) collective-permute-start(bf16[64,2048]{1,0:T(8,128)(2,1)S(1)} %slice.168), channel_id=1, source_target_pairs={{0,2},{1,3},{2,0},{3,1},{4,6},{5,7},{6,4},{7,5},{8,10},{9,11},{10,... | collective-permute-start | bytes 786440 | tf_op jit(solution)/shard_map/ppermute | solution.py:34
  77.7 1.4 %collective-permute-start.13 = (bf16[64,2048]{1,0:T(8,128)(2,1)S(1)}, bf16[64,2048]{1,0:T(8,128)(2,1)S(1)}, u32[]{:S(2)}, u32[]{:S(2)}) collective-permute-start(bf16[64,2048]{1,0:T(8,128)(2,1)S(1)} %slice.169), channel_id=1, source_target_pairs={{0,2},{1,3},{2,0},{3,1},{4,6},{5,7},{6,4},{7,5},{8,10},{9,11},{10,... | collective-permute-start | bytes 786440 | tf_op jit(solution)/shard_map/ppermute | solution.py:34
  79.1 6.2 %finish_step.5 = (f32[128,2048]{1,0:T(8,128)S(1)}, bf16[128,2048]{1,0:T(8,128)(2,1)S(1)}) custom-call(s32[2]{0:T(128)S(1)} %copy-done.3, bf16[192,2176]{1,0:T(8,128)(2,1)S(1)} %bitcast.68, bf16[192,2176]{1,0:T(8,128)(2,1)S(1)} %collective-permute-done.8.refs_1_, bf16[192,2176]{1,0:T(8,128)(2,1)S(1)} %collective-permute-done.9.refs_2_, ...), custom_call_target="tpu_custom_call" | custom-call | flops 1 | bytes 1 | tf_op jit(solution)/shard_map/finish_step/pallas_call | solution.py:366
  85.5 4.3 %collective-permute-done.13 = bf16[64,2048]{1,0:T(8,128)(2,1)S(1)} collective-permute-done((bf16[64,2048]{1,0:T(8,128)(2,1)S(1)}, bf16[64,2048]{1,0:T(8,128)(2,1)S(1)}, u32[]{:S(2)}, u32[]{:S(2)}) %collective-permute-start.13) | collective-permute-done | bytes 262176 | tf_op jit(solution)/shard_map/ppermute | solution.py:34
  90.5 1.8 %collective-permute-start.19 = (bf16[32,2048]{1,0:T(8,128)(2,1)S(1)}, bf16[32,2048]{1,0:T(8,128)(2,1)S(1)}, u32[]{:S(2)}, u32[]{:S(2)}) collective-permute-start(bf16[32,2048]{1,0:T(8,128)(2,1)S(1)} %bitcast.85), channel_id=1, source_target_pairs={{0,4},{1,5},{2,6},{3,7},{4,0},{5,1},{6,2},{7,3},{8,12},{9,13},{10,... | collective-permute-start | bytes 393224 | tf_op jit(solution)/shard_map/ppermute | solution.py:34
  92.3 1.6 %collective-permute-start.21 = (bf16[64,2048]{1,0:T(8,128)(2,1)S(1)}, bf16[64,2048]{1,0:T(8,128)(2,1)S(1)}, u32[]{:S(2)}, u32[]{:S(2)}) collective-permute-start(bf16[64,2048]{1,0:T(8,128)(2,1)S(1)} %slice.167), channel_id=1, source_target_pairs={{0,2},{1,3},{2,0},{3,1},{4,6},{5,7},{6,4},{7,5},{8,10},{9,11},{10,... | collective-permute-start | bytes 786440 | tf_op jit(solution)/shard_map/ppermute | solution.py:34
  93.9 2.2 %collective-permute-done.17 = bf16[32,2048]{1,0:T(8,128)(2,1)S(1)} collective-permute-done((bf16[32,2048]{1,0:T(8,128)(2,1)S(1)}, bf16[32,2048]{1,0:T(8,128)(2,1)S(1)}, u32[]{:S(2)}, u32[]{:S(2)}) %collective-permute-start.17) | collective-permute-done | bytes 131104 | tf_op jit(solution)/shard_map/ppermute | solution.py:34
  96.2 1.7 %collective-permute-start.18 = (bf16[16,2048]{1,0:T(8,128)(2,1)S(1)}, bf16[16,2048]{1,0:T(8,128)(2,1)S(1)}, u32[]{:S(2)}, u32[]{:S(2)}) collective-permute-start(bf16[16,2048]{1,0:T(8,128)(2,1)S(1)} %fusion.8), channel_id=1, source_target_pairs={{0,8},{1,9},{2,10},{3,11},{4,12},{5,13},{6,14},{7,15},{8,0},{9,1},... | collective-permute-start | bytes 196616 | tf_op jit(solution)/shard_map/ppermute | solution.py:34
  98.3 1.4 %collective-permute-start.20 = (bf16[16,2048]{1,0:T(8,128)(2,1)S(1)}, bf16[16,2048]{1,0:T(8,128)(2,1)S(1)}, u32[]{:S(2)}, u32[]{:S(2)}) collective-permute-start(bf16[16,2048]{1,0:T(8,128)(2,1)S(1)} %fusion.10), channel_id=1, source_target_pairs={{0,8},{1,9},{2,10},{3,11},{4,12},{5,13},{6,14},{7,15},{8,0},{9,1},... | collective-permute-start | bytes 196616 | tf_op jit(solution)/shard_map/ppermute | solution.py:34
  99.6 2.8 %collective-permute-done.18 = bf16[16,2048]{1,0:T(8,128)(2,1)S(1)} collective-permute-done((bf16[16,2048]{1,0:T(8,128)(2,1)S(1)}, bf16[16,2048]{1,0:T(8,128)(2,1)S(1)}, u32[]{:S(2)}, u32[]{:S(2)}) %collective-permute-start.18) | collective-permute-done | bytes 65568 | tf_op jit(solution)/shard_map/ppermute | solution.py:34
  102.6 2.6 %collective-permute-start.24 = (bf16[16,2048]{1,0:T(8,128)(2,1)S(1)}, bf16[16,2048]{1,0:T(8,128)(2,1)S(1)}, u32[]{:S(2)}, u32[]{:S(2)}) collective-permute-start(bf16[16,2048]{1,0:T(8,128)(2,1)S(1)} %get-tuple-element.90), channel_id=1, source_target_pairs={{0,12},{1,13},{2,14},{3,15},{4,8},{5,9},{6,10},{7,11},{8,4},{9,5},... | collective-permute-start | bytes 196616 | tf_op jit(solution)/shard_map/ppermute | solution.py:34
  107.1 1.8 %collective-permute-done.24 = bf16[16,2048]{1,0:T(8,128)(2,1)S(1)} collective-permute-done((bf16[16,2048]{1,0:T(8,128)(2,1)S(1)}, bf16[16,2048]{1,0:T(8,128)(2,1)S(1)}, u32[]{:S(2)}, u32[]{:S(2)}) %collective-permute-start.24) | collective-permute-done | bytes 65568 | tf_op jit(solution)/shard_map/ppermute | solution.py:34
  108.9 2.1 %collective-permute-done.23 = bf16[16,2048]{1,0:T(8,128)(2,1)S(1)} collective-permute-done((bf16[16,2048]{1,0:T(8,128)(2,1)S(1)}, bf16[16,2048]{1,0:T(8,128)(2,1)S(1)}, u32[]{:S(2)}, u32[]{:S(2)}) %collective-permute-start.23) | collective-permute-done | bytes 65568 | tf_op jit(solution)/shard_map/ppermute | solution.py:34
  (63 shorter events, 8.4 us)
Async XLA Ops:
  0.0 48.6 %copy-start.1 = (bf16[1,2048,768]{2,1,0:T(8,128)(2,1)S(1)}, bf16[1,2048,768]{2,1,0:T(8,128)(2,1)}, u32[]{:S(2)}) copy-start(bf16[1,2048,768]{2,1,0:T(8,128)(2,1)} %param.13) | copy-start | bytes 9437188
  2.1 11.4 %collective-permute-start.2 = (bf16[48,2176]{1,0:T(8,128)(2,1)}, bf16[48,2176]{1,0:T(8,128)(2,1)S(1)}, u32[]{:S(2)}, u32[]{:S(2)}) collective-permute-start(bf16[48,2176]{1,0:T(8,128)(2,1)} %payload.1), channel_id=1, source_target_pairs={{0,12},{1,13},{2,14},{3,15},{4,8},{5,9},{6,10},{7,11},{8,4},{9,5},... | collective-permute-start | bytes 626696 | tf_op jit(solution)/shard_map/ppermute | solution.py:34
  7.2 18.1 %collective-permute-start.1 = (bf16[48,2176]{1,0:T(8,128)(2,1)}, bf16[48,2176]{1,0:T(8,128)(2,1)}, u32[]{:S(2)}, u32[]{:S(2)}) collective-permute-start(bf16[48,2176]{1,0:T(8,128)(2,1)} %payload.1), channel_id=1, source_target_pairs={{0,8},{1,9},{2,10},{3,11},{4,12},{5,13},{6,14},{7,15},{8,0},{9,1},... | collective-permute-start | bytes 626696 | tf_op jit(solution)/shard_map/ppermute | solution.py:34
  7.2 18.1 %collective-permute-start = (bf16[48,2176]{1,0:T(8,128)(2,1)}, bf16[48,2176]{1,0:T(8,128)(2,1)}, u32[]{:S(2)}, u32[]{:S(2)}) collective-permute-start(bf16[48,2176]{1,0:T(8,128)(2,1)} %payload.1), channel_id=1, source_target_pairs={{0,4},{1,5},{2,6},{3,7},{4,0},{5,1},{6,2},{7,3},{8,12},{9,13},{10,... | collective-permute-start | bytes 626696 | tf_op jit(solution)/shard_map/ppermute | solution.py:34
  11.1 37.5 %copy-start.2 = (bf16[1,2048,768]{2,1,0:T(8,128)(2,1)S(1)}, bf16[1,2048,768]{2,1,0:T(8,128)(2,1)}, u32[]{:S(2)}) copy-start(bf16[1,2048,768]{2,1,0:T(8,128)(2,1)} %param.14) | copy-start | bytes 9437188
  11.1 15.4 %collective-permute-start.3 = (bf16[4,264,128]{2,1,0:T(8,128)(2,1)}, bf16[4,264,128]{2,1,0:T(8,128)(2,1)S(1)}, u32[]{:S(2)}, u32[]{:S(2)}) collective-permute-start(bf16[4,264,128]{2,1,0:T(8,128)(2,1)} %get-tuple-element.45), channel_id=1, source_target_pairs={{0,2},{1,3},{2,0},{3,1},{4,6},{5,7},{6,4},{7,5},{8,10},{9,11},{10,... | collective-permute-start | bytes 811016 | tf_op jit(solution)/shard_map/ppermute | solution.py:34
  26.5 19.7 %collective-permute-start.8 = (bf16[192,2176]{1,0:T(8,128)(2,1)S(1)}, bf16[192,2176]{1,0:T(8,128)(2,1)S(1)}, u32[]{:S(2)}, u32[]{:S(2)}) collective-permute-start(bf16[192,2176]{1,0:T(8,128)(2,1)S(1)} %bitcast.63), channel_id=1, source_target_pairs={{0,2},{1,3},{2,0},{3,1},{4,6},{5,7},{6,4},{7,5},{8,10},{9,11},{10,... | collective-permute-start | bytes 2506760 | tf_op jit(solution)/shard_map/ppermute | solution.py:34
  29.1 5.3 %collective-permute-start.4 = (bf16[2,264,128]{2,1,0:T(8,128)(2,1)S(1)}, bf16[2,264,128]{2,1,0:T(8,128)(2,1)S(1)}, u32[]{:S(2)}, u32[]{:S(2)}) collective-permute-start(bf16[2,264,128]{2,1,0:T(8,128)(2,1)S(1)} %pad_maximum_fusion.3), channel_id=1, source_target_pairs={{0,0},{1,1},{2,2},{3,3},{4,4},{5,5},{6,6},{7,7},{8,8},{9,9},{10,10... | collective-permute-start | bytes 405512 | tf_op jit(solution)/shard_map/ppermute | solution.py:67
  29.8 6.2 %collective-permute-start.5 = (bf16[2,264,128]{2,1,0:T(8,128)(2,1)S(1)}, bf16[2,264,128]{2,1,0:T(8,128)(2,1)S(1)}, u32[]{:S(2)}, u32[]{:S(2)}) collective-permute-start(bf16[2,264,128]{2,1,0:T(8,128)(2,1)S(1)} %pad_maximum_fusion.4), channel_id=1, source_target_pairs={{0,4},{1,5},{2,6},{3,7},{4,0},{5,1},{6,2},{7,3},{8,12},{9,13},{10,... | collective-permute-start | bytes 405512 | tf_op jit(solution)/shard_map/ppermute | solution.py:67
  29.9 12.6 %collective-permute-start.6 = (bf16[2,264,128]{2,1,0:T(8,128)(2,1)S(1)}, bf16[2,264,128]{2,1,0:T(8,128)(2,1)S(1)}, u32[]{:S(2)}, u32[]{:S(2)}) collective-permute-start(bf16[2,264,128]{2,1,0:T(8,128)(2,1)S(1)} %pad_maximum_fusion.5), channel_id=1, source_target_pairs={{0,8},{1,9},{2,10},{3,11},{4,12},{5,13},{6,14},{7,15},{8,0},{9,1},... | collective-permute-start | bytes 405512 | tf_op jit(solution)/shard_map/ppermute | solution.py:67
  33.0 9.5 %collective-permute-start.7 = (bf16[2,264,128]{2,1,0:T(8,128)(2,1)S(1)}, bf16[2,264,128]{2,1,0:T(8,128)(2,1)S(1)}, u32[]{:S(2)}, u32[]{:S(2)}) collective-permute-start(bf16[2,264,128]{2,1,0:T(8,128)(2,1)S(1)} %pad_maximum_fusion.6), channel_id=1, source_target_pairs={{0,12},{1,13},{2,14},{3,15},{4,8},{5,9},{6,10},{7,11},{8,4},{9,5},... | collective-permute-start | bytes 405512 | tf_op jit(solution)/shard_map/ppermute | solution.py:67
  34.5 13.4 %collective-permute-start.9 = (bf16[192,2176]{1,0:T(8,128)(2,1)S(1)}, bf16[192,2176]{1,0:T(8,128)(2,1)S(1)}, u32[]{:S(2)}, u32[]{:S(2)}) collective-permute-start(bf16[192,2176]{1,0:T(8,128)(2,1)S(1)} %bitcast.64), channel_id=1, source_target_pairs={{0,1},{1,0},{2,3},{3,2},{4,5},{5,4},{6,7},{7,6},{8,9},{9,8},{10,11... | collective-permute-start | bytes 2506760 | tf_op jit(solution)/shard_map/ppermute | solution.py:34
  46.2 2.4 %collective-permute-start.10 = (bf16[192,2176]{1,0:T(8,128)(2,1)S(1)}, bf16[192,2176]{1,0:T(8,128)(2,1)S(1)}, u32[]{:S(2)}, u32[]{:S(2)}) collective-permute-start(bf16[192,2176]{1,0:T(8,128)(2,1)S(1)} %collective-permute-done.8.refs_1_), channel_id=1, source_target_pairs={{0,1},{1,0},{2,3},{3,2},{4,5},{5,4},{6,7},{7,6},{8,9},{9,8},{10,11... | collective-permute-start | bytes 2506760 | tf_op jit(solution)/shard_map/ppermute | solution.py:34
  46.3 14.8 %collective-permute-start.11 = (bf16[4,2,264,128]{3,2,1,0:T(8,128)(2,1)S(1)}, bf16[4,2,264,128]{3,2,1,0:T(8,128)(2,1)S(1)}, u32[]{:S(2)}, u32[]{:S(2)}) collective-permute-start(bf16[4,2,264,128]{3,2,1,0:T(8,128)(2,1)S(1)} %pad_maximum_fusion.1.refs_0_), channel_id=1, source_target_pairs={{0,16},{16,0},{1,17},{17,1},{2,18},{18,2},{3,19},{19,3},{4,20},{20... | collective-permute-start | bytes 1622024 | tf_op jit(solution)/shard_map/ppermute | solution.py:417
  48.6 12.5 %copy-start.3 = (s32[2]{0:T(128)S(1)}, s32[2]{0:T(128)}, u32[]{:S(2)}) copy-start(s32[2]{0:T(128)} %pad_add_fusion.place_ref) | copy-start | bytes 28
  48.6 14.1 %copy-start = (bf16[1,768,2048]{2,1,0:T(8,128)(2,1)S(1)}, bf16[1,768,2048]{2,1,0:T(8,128)(2,1)}, u32[]{:S(2)}) copy-start(bf16[1,768,2048]{2,1,0:T(8,128)(2,1)} %param.15) | copy-start | bytes 9437188
  68.9 6.9 %collective-permute-start.14 = (bf16[128,2048]{1,0:T(8,128)(2,1)S(1)}, bf16[128,2048]{1,0:T(8,128)(2,1)S(1)}, u32[]{:S(2)}, u32[]{:S(2)}) collective-permute-start(bf16[128,2048]{1,0:T(8,128)(2,1)S(1)} %get-tuple-element.69), channel_id=1, source_target_pairs={{0,1},{1,0},{2,3},{3,2},{4,5},{5,4},{6,7},{7,6},{8,9},{9,8},{10,11... | collective-permute-start | bytes 1572872 | tf_op jit(solution)/shard_map/ppermute | solution.py:34
  75.2 2.3 %collective-permute-start.12 = (bf16[128,2048]{1,0:T(8,128)(2,1)S(1)}, bf16[128,2048]{1,0:T(8,128)(2,1)S(1)}, u32[]{:S(2)}, u32[]{:S(2)}) collective-permute-start(bf16[128,2048]{1,0:T(8,128)(2,1)S(1)} %get-tuple-element.66), channel_id=1, source_target_pairs={{0,1},{1,0},{2,3},{3,2},{4,5},{5,4},{6,7},{7,6},{8,9},{9,8},{10,11... | collective-permute-start | bytes 1572872 | tf_op jit(solution)/shard_map/ppermute | solution.py:34
  75.9 9.5 %collective-permute-start.15 = (bf16[64,2048]{1,0:T(8,128)(2,1)S(1)}, bf16[64,2048]{1,0:T(8,128)(2,1)S(1)}, u32[]{:S(2)}, u32[]{:S(2)}) collective-permute-start(bf16[64,2048]{1,0:T(8,128)(2,1)S(1)} %slice.168), channel_id=1, source_target_pairs={{0,2},{1,3},{2,0},{3,1},{4,6},{5,7},{6,4},{7,5},{8,10},{9,11},{10,... | collective-permute-start | bytes 786440 | tf_op jit(solution)/shard_map/ppermute | solution.py:34
  77.7 12.2 %collective-permute-start.13 = (bf16[64,2048]{1,0:T(8,128)(2,1)S(1)}, bf16[64,2048]{1,0:T(8,128)(2,1)S(1)}, u32[]{:S(2)}, u32[]{:S(2)}) collective-permute-start(bf16[64,2048]{1,0:T(8,128)(2,1)S(1)} %slice.169), channel_id=1, source_target_pairs={{0,2},{1,3},{2,0},{3,1},{4,6},{5,7},{6,4},{7,5},{8,10},{9,11},{10,... | collective-permute-start | bytes 786440 | tf_op jit(solution)/shard_map/ppermute | solution.py:34
  85.3 4.6 %collective-permute-start.16 = (bf16[128,2048]{1,0:T(8,128)(2,1)S(1)}, bf16[128,2048]{1,0:T(8,128)(2,1)S(1)}, u32[]{:S(2)}, u32[]{:S(2)}) collective-permute-start(bf16[128,2048]{1,0:T(8,128)(2,1)S(1)} %get-tuple-element.75), channel_id=1, source_target_pairs={{0,1},{1,0},{2,3},{3,2},{4,5},{5,4},{6,7},{7,6},{8,9},{9,8},{10,11... | collective-permute-start | bytes 1572872 | tf_op jit(solution)/shard_map/ppermute | solution.py:34
  90.1 6.0 %collective-permute-start.17 = (bf16[32,2048]{1,0:T(8,128)(2,1)S(1)}, bf16[32,2048]{1,0:T(8,128)(2,1)S(1)}, u32[]{:S(2)}, u32[]{:S(2)}) collective-permute-start(bf16[32,2048]{1,0:T(8,128)(2,1)S(1)} %bitcast.86), channel_id=1, source_target_pairs={{0,4},{1,5},{2,6},{3,7},{4,0},{5,1},{6,2},{7,3},{8,12},{9,13},{10,... | collective-permute-start | bytes 393224 | tf_op jit(solution)/shard_map/ppermute | solution.py:34
  90.5 7.7 %collective-permute-start.19 = (bf16[32,2048]{1,0:T(8,128)(2,1)S(1)}, bf16[32,2048]{1,0:T(8,128)(2,1)S(1)}, u32[]{:S(2)}, u32[]{:S(2)}) collective-permute-start(bf16[32,2048]{1,0:T(8,128)(2,1)S(1)} %bitcast.85), channel_id=1, source_target_pairs={{0,4},{1,5},{2,6},{3,7},{4,0},{5,1},{6,2},{7,3},{8,12},{9,13},{10,... | collective-permute-start | bytes 393224 | tf_op jit(solution)/shard_map/ppermute | solution.py:34
  92.3 10.1 %collective-permute-start.21 = (bf16[64,2048]{1,0:T(8,128)(2,1)S(1)}, bf16[64,2048]{1,0:T(8,128)(2,1)S(1)}, u32[]{:S(2)}, u32[]{:S(2)}) collective-permute-start(bf16[64,2048]{1,0:T(8,128)(2,1)S(1)} %slice.167), channel_id=1, source_target_pairs={{0,2},{1,3},{2,0},{3,1},{4,6},{5,7},{6,4},{7,5},{8,10},{9,11},{10,... | collective-permute-start | bytes 786440 | tf_op jit(solution)/shard_map/ppermute | solution.py:34
  96.2 6.2 %collective-permute-start.18 = (bf16[16,2048]{1,0:T(8,128)(2,1)S(1)}, bf16[16,2048]{1,0:T(8,128)(2,1)S(1)}, u32[]{:S(2)}, u32[]{:S(2)}) collective-permute-start(bf16[16,2048]{1,0:T(8,128)(2,1)S(1)} %fusion.8), channel_id=1, source_target_pairs={{0,8},{1,9},{2,10},{3,11},{4,12},{5,13},{6,14},{7,15},{8,0},{9,1},... | collective-permute-start | bytes 196616 | tf_op jit(solution)/shard_map/ppermute | solution.py:34
  98.3 8.0 %collective-permute-start.20 = (bf16[16,2048]{1,0:T(8,128)(2,1)S(1)}, bf16[16,2048]{1,0:T(8,128)(2,1)S(1)}, u32[]{:S(2)}, u32[]{:S(2)}) collective-permute-start(bf16[16,2048]{1,0:T(8,128)(2,1)S(1)} %fusion.10), channel_id=1, source_target_pairs={{0,8},{1,9},{2,10},{3,11},{4,12},{5,13},{6,14},{7,15},{8,0},{9,1},... | collective-permute-start | bytes 196616 | tf_op jit(solution)/shard_map/ppermute | solution.py:34
  102.5 4.6 %collective-permute-start.22 = (bf16[16,2048]{1,0:T(8,128)(2,1)S(1)}, bf16[16,2048]{1,0:T(8,128)(2,1)S(1)}, u32[]{:S(2)}, u32[]{:S(2)}) collective-permute-start(bf16[16,2048]{1,0:T(8,128)(2,1)S(1)} %get-tuple-element.89), channel_id=1, source_target_pairs={{0,4},{1,5},{2,6},{3,7},{4,0},{5,1},{6,2},{7,3},{8,12},{9,13},{10,... | collective-permute-start | bytes 196616 | tf_op jit(solution)/shard_map/ppermute | solution.py:34
  102.6 6.2 %collective-permute-start.24 = (bf16[16,2048]{1,0:T(8,128)(2,1)S(1)}, bf16[16,2048]{1,0:T(8,128)(2,1)S(1)}, u32[]{:S(2)}, u32[]{:S(2)}) collective-permute-start(bf16[16,2048]{1,0:T(8,128)(2,1)S(1)} %get-tuple-element.90), channel_id=1, source_target_pairs={{0,12},{1,13},{2,14},{3,15},{4,8},{5,9},{6,10},{7,11},{8,4},{9,5},... | collective-permute-start | bytes 196616 | tf_op jit(solution)/shard_map/ppermute | solution.py:34
  105.2 5.7 %collective-permute-start.23 = (bf16[16,2048]{1,0:T(8,128)(2,1)S(1)}, bf16[16,2048]{1,0:T(8,128)(2,1)S(1)}, u32[]{:S(2)}, u32[]{:S(2)}) collective-permute-start(bf16[16,2048]{1,0:T(8,128)(2,1)S(1)} %get-tuple-element.91), channel_id=1, source_target_pairs={{0,8},{1,9},{2,10},{3,11},{4,12},{5,13},{6,14},{7,15},{8,0},{9,1},... | collective-permute-start | bytes 196616 | tf_op jit(solution)/shard_map/ppermute | solution.py:34

commit v16 on v15

--- a/solution.py
+++ b/solution.py
@@ -12,6 +12,7 @@
 GRANT = 16 << 20
 EXPERT_GRANT = 32 << 20
 WHOLE_GRANT = 60 << 20
+MUCH = pl.CostEstimate(flops=1 << 33, bytes_accessed=1, transcendentals=0)
 LITTLE = pl.CostEstimate(flops=1, bytes_accessed=1, transcendentals=0)
 
 
@@ -56,15 +57,12 @@
 
 
 def exchange_factors(blocks, n):
-    outer, middle, cores = split_axis(n)
+    _, middle, cores = split_axis(n)
     here = []
-    for q in range(outer):
-        pairs = []
-        for g in range(2):
-            for i in range(n):
-                pairs.append((g * n + i, g * n + (i ^ (q * middle * cores) ^ g)))
-        part = jnp.stack([block[q] for block in blocks])
-        here.append(lax.ppermute(part, ("group", "expert"), pairs))
+    for q, block in enumerate(blocks):
+        turn = q * middle * cores
+        pairs = [(g * n + i, g * n + (i ^ turn ^ g)) for g in range(2) for i in range(n)]
+        here.append(lax.ppermute(block, ("group", "expert"), pairs))
     return here
 
 
@@ -297,7 +295,7 @@
     )(*pieces, w_gate, w_up)
 
 
-def finish_kernel(count, first, rows, place_ref, *refs):
+def finish_kernel(count, first, rows, block, parts, place_ref, *refs):
     pieces, refs = refs[:count], refs[count:]
     gate_hbm, up_hbm, a_gu_hbm, gate_b_hbm, up_b_hbm, down_a_hbm, down_b_hbm = refs[:7]
     w_down_hbm, kept_hbm, sent_hbm, x_ref, gate_ref, up_ref = refs[7:13]
@@ -307,7 +305,6 @@
     units, width = w_down_ref.shape
     rank = gate_b_ref.shape[0]
     own = kept_ref.shape[0]
-    block = min(128, own)
     loads = Loads(sem)
     x_in, base_in = [], []
     for i, piece in enumerate(pieces):
@@ -337,22 +334,32 @@
         low = adapter_scale * dot(inner_ref[cut, :], down_a_ref[...])
         lows.append(low.astype(jnp.bfloat16)[:, :rank])
     out_copies = []
+    half = width // parts
+    columns = [slice(at, at + half) for at in range(0, width, half)]
     for cut, low in zip(cuts, lows):
         gates = x_ref[cut, width:].astype(jnp.float32)
         lane = lax.broadcasted_iota(jnp.int32, gates.shape, 1)
         mine = jnp.sum(jnp.where(lane == place_ref[1], gates, 0.0), axis=1, keepdims=True)
-        out = (dot(inner_ref[cut, :], w_down_ref[...]) + dot(low, down_b_ref[...])) * mine
-        keep = cut.start < own
-        out_ref, out_hbm = (kept_ref, kept_hbm) if keep else (sent_ref, sent_hbm)
-        at = pl.ds(cut.start if keep else cut.start - own, block)
-        out_ref[at, :] = out.astype(out_ref.dtype)
-        sem_out = out_sem.at[len(out_copies)]
-        out_copies.append(pltpu.make_async_copy(out_ref.at[at], out_hbm.at[at], sem_out))
-        out_copies[-1].start()
+        outs = [
+            (dot(inner_ref[cut, :], w_down_ref[:, c]) + dot(low, down_b_ref[:, c])) * mine
+            for c in columns
+        ]
+        ends = [(kept_ref, kept_hbm, 0), (sent_ref, sent_hbm, own)]
+        for out_ref, out_hbm, start in ends:
+            at, to = max(cut.start, start), min(cut.stop, start + own)
+            if at < to:
+                for c, out in zip(columns, outs):
+                    part = out[at - cut.start : to - cut.start]
+                    out_ref[at - start : to - start, c] = part.astype(out_ref.dtype)
+                rows_out = pl.ds(at - start, to - at)
+                sem_out = out_sem.at[len(out_copies)]
+                copy = pltpu.make_async_copy(out_ref.at[rows_out], out_hbm.at[rows_out], sem_out)
+                copy.start()
+                out_copies.append(copy)
     wait(out_copies)
 
 
-def finish_step(place, pieces, base, first, rows, low_rank, w_down):
+def finish_step(place, pieces, base, first, rows, low_rank, w_down, block, parts):
     units, width = w_down.shape
     total = rows * len(pieces)
     own = total // 2
@@ -364,7 +371,7 @@
     ]
     held = [*low_rank, w_down]
     return pl.pallas_call(
-        functools.partial(finish_kernel, len(pieces), first, rows),
+        functools.partial(finish_kernel, len(pieces), first, rows, block, parts),
         out_shape=outs,
         in_specs=[pl.BlockSpec(memory_space=pltpu.SMEM)]
         + [pl.BlockSpec(memory_space=pl.ANY)] * (len(pieces) + 2 + len(low_rank))
@@ -380,10 +387,10 @@
         + [pltpu.VMEM(o.shape, o.dtype) for o in outs]
         + [
             pltpu.SemaphoreType.DMA((3 * len(pieces) + 9,)),
-            pltpu.SemaphoreType.DMA((2 * own // min(128, own),)),
+            pltpu.SemaphoreType.DMA((2 * own // min(block, own),)),
         ],
         compiler_params=pltpu.CompilerParams(vmem_limit_bytes=EXPERT_GRANT),
-        cost_estimate=LITTLE,
+        cost_estimate=MUCH,
         name="finish_step",
     )(place, *pieces, *base, *held)
 
@@ -409,6 +416,7 @@
     column = jnp.stack(column, axis=1).reshape(steps * outer * rows, -1)
     blocks = order_factors(place, placement, factors, outer, middle)
     blocks = [blocks[0]] + [swap(blocks[r], owners, cores, r) for r in range(1, middle)]
+    blocks = [jnp.stack([block[q] for block in blocks]) for q in range(outer)]
     column, blocks = lax.optimization_barrier((column, blocks))
     here = exchange_factors(blocks, owners)
     sheet = along(column, *along_middle)
@@ -421,17 +429,22 @@
     low_rank = relayout_factors(place, here, there, width, units, rank, owners)
 
     span = outer * rows
-    results = []
+    def after(x, other):
+        return lax.optimization_barrier((x, other))[0]
+
+    summed, across = [], []
     for s in range(steps):
-        if s >= 2:
-            pieces, results[s - 2] = lax.optimization_barrier((pieces, results[s - 2]))
-        kept, sent = finish_step(place, pieces, base, s * span, span, low_rank, down_weight[0])
-        results.append(kept + swap(sent, owners, 1, 1).astype(jnp.float32))
-    results[:-1] = [scatter_along(total, owners, *along_middle) for total in results[:-1]]
-    results = lax.optimization_barrier(results)
-    results[-1] = scatter_along(results[-1], owners, *along_middle)
-    results[:-1] = [halve_along(total, owners, *along_outer) for total in results[:-1]]
-    results[-1] = scatter_along(results[-1], owners, *along_outer)
+        if s >= 1:
+            pieces = lax.optimization_barrier((pieces, summed[s - 1], across[: s - 1]))[0]
+        block, parts = [(128, 1), (256, 1), (256, 2)][s % 3]
+        kept, sent = finish_step(
+            place, pieces, base, s * span, span, low_rank, down_weight[0], block, parts
+        )
+        summed.append(kept + swap(sent, owners, 1, 1).astype(jnp.float32))
+        across.append(scatter_along(summed[s], owners, *along_middle))
+    across[:-1] = [after(total, summed[-1]) for total in across[:-1]]
+    results = [halve_along(total, owners, *along_outer) for total in across[:-1]]
+    results.append(scatter_along(across[-1], owners, *along_outer))
     return jnp.stack(results).astype(jnp.bfloat16)
 
 

time: 112 us -> 112 us (level)
  waiting for transfers between devices: 42.5 us -> 45.2 us
  starting transfers between devices: 29.9 us -> 27.6 us
    ppermute x20, waiting for transfers between devices: 31.3 us -> 33.8 us  [swap(): return lax.ppermute(x, 'expert', [(i, i ^ k * stride) for i in range(n)])]
    ppermute x20, starting transfers between devices: 23.1 us -> 20.9 us  [swap(): return lax.ppermute(x, 'expert', [(i, i ^ k * stride) for i in range(n)])]
  transfers between devices with their start and end apart: 25 -> 25, of which waited for: 15 -> 17; matrix products, arithmetic and copies ran while one was open for 3% -> 3% of each run, Pallas kernels for 22% -> 22%
where the time goes in v16:
time: 112 us
  waiting for transfers between devices  45.2 us (40%)
  Pallas kernels  34.5 us (31%)
  starting transfers between devices  27.6 us (25%)
  other arithmetic  3.34 us (3%)
  local copies, waits for them, and re-layouts  1.23 us (1%)
    ppermute x20, waiting for transfers between devices, swap(): return lax.ppermute(x, 'expert', [(i, i ^ k * stride) for i in range(n)])  33.8 us
    ppermute x20, starting transfers between devices, swap(): return lax.ppermute(x, 'expert', [(i, i ^ k * stride) for i in range(n)])  20.9 us
    pallas_call x3, Pallas kernels, finish_step(): pl.pallas_call(functools.partial(finish_kernel, len(pieces), first, rows,...  18.7 us
    pallas_call x1, Pallas kernels, base_products(): pl.pallas_call(functools.partial(base_kernel, len(pieces)), out_shape=[ou...  9.3 us
    ppermute x4, waiting for transfers between devices, exchange_factors(): here.append(lax.ppermute(block, ('group', 'expert'), pairs))  8.23 us
    ppermute x4, starting transfers between devices, exchange_factors(): here.append(lax.ppermute(block, ('group', 'expert'), pairs))  5.1 us
    ppermute x1, waiting for transfers between devices, dense_shards(): there = lax.ppermute(here, 'group', [(0, 1), (1, 0)])  3.15 us
    pallas_call x1, Pallas kernels, order_factors(): pl.pallas_call(order_kernel, out_shape=[jax.ShapeDtypeStruct((outer, leng...  2.8 us
  transfers between devices with their start and end apart: 25, of which 17 were waited for; matrix products, arithmetic and copies ran while one was open for 3% of the time, Pallas kernels for 22%

profile of v16, /device:TPU:0, one launch (start us, length us, event | category | flops | bytes accessed | tf_op | source)
XLA Modules:
  0.0 112.1 jit_solution(10727667391119394854)
XLA Ops:
  0.0 2.1 %payload.1 = bf16[48,2176]{1,0:T(8,128)(2,1)} custom-call(bf16[3,16,2048]{2,1,0:T(8,128)(2,1)} %hidden_ref.1, s32[3,8,16]{2,1,0:T(8,128)} %bitcast.87, f32[3,8,16]{2,1,0:T(8,128)} %bitcast.88), custom_call_target="tpu_custom_call" | custom-call | flops 1 | bytes 1 | tf_op jit(solution)/shard_map/payload/pallas_call | solution.py:95
  2.1 5.0 %collective-permute-start.2 = (bf16[48,2176]{1,0:T(8,128)(2,1)}, bf16[48,2176]{1,0:T(8,128)(2,1)S(1)}, u32[]{:S(2)}, u32[]{:S(2)}) collective-permute-start(bf16[48,2176]{1,0:T(8,128)(2,1)} %payload.1), channel_id=1, source_target_pairs={{0,12},{1,13},{2,14},{3,15},{4,8},{5,9},{6,10},{7,11},{8,4},{9,5},... | collective-permute-start | bytes 626696 | tf_op jit(solution)/shard_map/ppermute | solution.py:35
  8.4 2.8 %order_factors.1 = (bf16[4,264,128]{2,1,0:T(8,128)(2,1)}, bf16[4,264,128]{2,1,0:T(8,128)(2,1)}) custom-call(s32[2]{0:T(128)} %pad_add_fusion.place_ref, s32[16]{0:T(128)} %placement_ref.1, bf16[16,33792]{1,0:T(8,128)(2,1)} %factors_ref), custom_call_target="tpu_custom_call" | custom-call | flops 1 | bytes 1 | tf_op jit(solution)/shard_map/order_factors/pallas_call | solution.py:130
  11.2 1.7 %collective-permute-start.3 = (bf16[4,264,128]{2,1,0:T(8,128)(2,1)}, bf16[4,264,128]{2,1,0:T(8,128)(2,1)S(1)}, u32[]{:S(2)}, u32[]{:S(2)}) collective-permute-start(bf16[4,264,128]{2,1,0:T(8,128)(2,1)} %get-tuple-element.49), channel_id=1, source_target_pairs={{0,2},{1,3},{2,0},{3,1},{4,6},{5,7},{6,4},{7,5},{8,10},{9,11},{10,... | collective-permute-start | bytes 811016 | tf_op jit(solution)/shard_map/ppermute | solution.py:35
  14.0 11.3 %collective-permute-done.1 = bf16[48,2176]{1,0:T(8,128)(2,1)} collective-permute-done((bf16[48,2176]{1,0:T(8,128)(2,1)}, bf16[48,2176]{1,0:T(8,128)(2,1)}, u32[]{:S(2)}, u32[]{:S(2)}) %collective-permute-start.1) | collective-permute-done | bytes 208928 | tf_op jit(solution)/shard_map/ppermute | solution.py:35
  25.3 1.3 %pad_maximum_fusion = bf16[3,4,16,2176]{3,2,1,0:T(8,128)(2,1)S(1)} fusion(bf16[3,1,16,2176]{3,2,1,0:T(8,128)(2,1)S(1)} %bitcast.80, bf16[3,1,16,2176]{3,2,1,0:T(8,128)(2,1)} %bitcast.9, bf16[3,1,16,2176]{3,2,1,0:T(8,128)(2,1)} %bitcast.7, bf16[3,1,16,2176]{3,2,1,0:T(8,128)(2,1)} %bitcast.75), kind=kLoop, calls=%fused_computation.3 | loop fusion | flops 1253376 | bytes 1671168 | tf_op jit(solution)/shard_map/stack | solution.py:416
  26.6 1.6 %collective-permute-start.8 = (bf16[192,2176]{1,0:T(8,128)(2,1)S(1)}, bf16[192,2176]{1,0:T(8,128)(2,1)S(1)}, u32[]{:S(2)}, u32[]{:S(2)}) collective-permute-start(bf16[192,2176]{1,0:T(8,128)(2,1)S(1)} %bitcast.60), channel_id=1, source_target_pairs={{0,2},{1,3},{2,0},{3,1},{4,6},{5,7},{6,4},{7,5},{8,10},{9,11},{10,... | collective-permute-start | bytes 2506760 | tf_op jit(solution)/shard_map/ppermute | solution.py:35
  28.9 3.0 %collective-permute-start.6 = (bf16[2,264,128]{2,1,0:T(8,128)(2,1)S(1)}, bf16[2,264,128]{2,1,0:T(8,128)(2,1)S(1)}, u32[]{:S(2)}, u32[]{:S(2)}) collective-permute-start(bf16[2,264,128]{2,1,0:T(8,128)(2,1)S(1)} %get-tuple-element.53), channel_id=1, source_target_pairs={{0,8},{1,9},{2,10},{3,11},{4,12},{5,13},{6,14},{7,15},{8,0},{9,1},... | collective-permute-start | bytes 405512 | tf_op jit(solution)/shard_map/ppermute | solution.py:65
  32.0 1.3 %collective-permute-start.7 = (bf16[2,264,128]{2,1,0:T(8,128)(2,1)S(1)}, bf16[2,264,128]{2,1,0:T(8,128)(2,1)S(1)}, u32[]{:S(2)}, u32[]{:S(2)}) collective-permute-start(bf16[2,264,128]{2,1,0:T(8,128)(2,1)S(1)} %get-tuple-element.54), channel_id=1, source_target_pairs={{0,12},{1,13},{2,14},{3,15},{4,8},{5,9},{6,10},{7,11},{8,4},{9,5},... | collective-permute-start | bytes 405512 | tf_op jit(solution)/shard_map/ppermute | solution.py:65
  33.3 2.0 %collective-permute-done.5 = bf16[2,264,128]{2,1,0:T(8,128)(2,1)S(1)} collective-permute-done((bf16[2,264,128]{2,1,0:T(8,128)(2,1)S(1)}, bf16[2,264,128]{2,1,0:T(8,128)(2,1)S(1)}, u32[]{:S(2)}, u32[]{:S(2)}) %collective-permute-start.5) | collective-permute-done | bytes 135200 | tf_op jit(solution)/shard_map/ppermute | solution.py:65
  35.4 6.2 %collective-permute-done.6 = bf16[2,264,128]{2,1,0:T(8,128)(2,1)S(1)} collective-permute-done((bf16[2,264,128]{2,1,0:T(8,128)(2,1)S(1)}, bf16[2,264,128]{2,1,0:T(8,128)(2,1)S(1)}, u32[]{:S(2)}, u32[]{:S(2)}) %collective-permute-start.6) | collective-permute-done | bytes 135200 | tf_op jit(solution)/shard_map/ppermute | solution.py:65
  41.6 4.8 %collective-permute-done.8.refs_1_ = bf16[192,2176]{1,0:T(8,128)(2,1)S(1)} collective-permute-done((bf16[192,2176]{1,0:T(8,128)(2,1)S(1)}, bf16[192,2176]{1,0:T(8,128)(2,1)S(1)}, u32[]{:S(2)}, u32[]{:S(2)}) %collective-permute-start.8) | collective-permute-done | bytes 835616 | tf_op jit(solution)/shard_map/ppermute | solution.py:35
  46.4 1.6 %collective-permute-start.11 = (bf16[4,2,264,128]{3,2,1,0:T(8,128)(2,1)S(1)}, bf16[4,2,264,128]{3,2,1,0:T(8,128)(2,1)S(1)}, u32[]{:S(2)}, u32[]{:S(2)}) collective-permute-start(bf16[4,2,264,128]{3,2,1,0:T(8,128)(2,1)S(1)} %pad_maximum_fusion.1.refs_0_), channel_id=1, source_target_pairs={{0,16},{16,0},{1,17},{17,1},{2,18},{18,2},{3,19},{19,3},{4,20},{20... | collective-permute-start | bytes 1622024 | tf_op jit(solution)/shard_map/ppermute | solution.py:425
  48.7 9.3 %base_products.1 = (f32[768,768]{1,0:T(8,128)S(1)}, f32[768,768]{1,0:T(8,128)S(1)}) custom-call(bf16[192,2176]{1,0:T(8,128)(2,1)S(1)} %bitcast.62, bf16[192,2176]{1,0:T(8,128)(2,1)S(1)} %collective-permute-done.8.refs_1_, bf16[192,2176]{1,0:T(8,128)(2,1)S(1)} %collective-permute-done.9.refs_2_, bf16[192,2176]{1,0:T(8,128)(2,1)S(1)} %collective-permute-done.10.refs_3_, ...), custom_call_target="tpu_custom_call" | custom-call | flops 1 | bytes 1 | tf_op jit(solution)/shard_map/base_products/pallas_call | solution.py:277
  58.0 3.1 %collective-permute-done.11.refs_1_ = bf16[4,2,264,128]{3,2,1,0:T(8,128)(2,1)S(1)} collective-permute-done((bf16[4,2,264,128]{3,2,1,0:T(8,128)(2,1)S(1)}, bf16[4,2,264,128]{3,2,1,0:T(8,128)(2,1)S(1)}, u32[]{:S(2)}, u32[]{:S(2)}) %collective-permute-start.11) | collective-permute-done | bytes 540704 | tf_op jit(solution)/shard_map/ppermute | solution.py:425
  61.2 1.6 %relayout_factors.1 = (bf16[2048,128]{1,0:T(8,128)(2,1)S(1)}, bf16[64,768]{1,0:T(8,128)(2,1)S(1)}, bf16[64,768]{1,0:T(8,128)(2,1)S(1)}, bf16[768,128]{1,0:T(8,128)(2,1)S(1)}, bf16[64,2048]{1,0:T(8,128)(2,1)S(1)}) custom-call(s32[2]{0:T(128)S(1)} %copy-done.2, bf16[4,2,264,128]{3,2,1,0:T(8,128)(2,1)S(1)} %pad_maximum_fusion.1.refs_0_, ...), custom_call_target="tpu_custom_call" | custom-call | flops 1 | bytes 1 | tf_op jit(solution)/shard_map/relayout_factors/pallas_call | solution.py:202
  62.8 6.2 %finish_step.3 = (f32[128,2048]{1,0:T(8,128)S(1)}, bf16[128,2048]{1,0:T(8,128)(2,1)S(1)}) custom-call(s32[2]{0:T(128)S(1)} %copy-done.2, bf16[192,2176]{1,0:T(8,128)(2,1)S(1)} %bitcast.63, bf16[192,2176]{1,0:T(8,128)(2,1)S(1)} %collective-permute-done.8.refs_1_, bf16[192,2176]{1,0:T(8,128)(2,1)S(1)} %collective-permute-done.9.refs_2_, ...), custom_call_target="tpu_custom_call" | custom-call | flops 8589934592 | bytes 1 | tf_op jit(solution)/shard_map/finish_step/pallas_call | solution.py:373
  69.1 1.9 %collective-permute-done.12 = bf16[128,2048]{1,0:T(8,128)(2,1)S(1)} collective-permute-done((bf16[128,2048]{1,0:T(8,128)(2,1)S(1)}, bf16[128,2048]{1,0:T(8,128)(2,1)S(1)}, u32[]{:S(2)}, u32[]{:S(2)}) %collective-permute-start.12) | collective-permute-done | bytes 524320 | tf_op jit(solution)/shard_map/ppermute | solution.py:35
  71.1 1.6 %collective-permute-start.13 = (bf16[64,2048]{1,0:T(8,128)(2,1)S(1)}, bf16[64,2048]{1,0:T(8,128)(2,1)S(1)}, u32[]{:S(2)}, u32[]{:S(2)}) collective-permute-start(bf16[64,2048]{1,0:T(8,128)(2,1)S(1)} %slice.175), channel_id=1, source_target_pairs={{0,2},{1,3},{2,0},{3,1},{4,6},{5,7},{6,4},{7,5},{8,10},{9,11},{10,... | collective-permute-start | bytes 786440 | tf_op jit(solution)/shard_map/ppermute | solution.py:35
  72.7 6.2 %finish_step.4 = (f32[128,2048]{1,0:T(8,128)S(1)}, bf16[128,2048]{1,0:T(8,128)(2,1)S(1)}) custom-call(s32[2]{0:T(128)S(1)} %copy-done.2, bf16[192,2176]{1,0:T(8,128)(2,1)S(1)} %bitcast.64, bf16[192,2176]{1,0:T(8,128)(2,1)S(1)} %collective-permute-done.8.refs_1_, bf16[192,2176]{1,0:T(8,128)(2,1)S(1)} %collective-permute-done.9.refs_2_, ...), custom_call_target="tpu_custom_call" | custom-call | flops 8589934592 | bytes 1 | tf_op jit(solution)/shard_map/finish_step/pallas_call | solution.py:373
  79.6 1.3 %collective-permute-done.14 = bf16[128,2048]{1,0:T(8,128)(2,1)S(1)} collective-permute-done((bf16[128,2048]{1,0:T(8,128)(2,1)S(1)}, bf16[128,2048]{1,0:T(8,128)(2,1)S(1)}, u32[]{:S(2)}, u32[]{:S(2)}) %collective-permute-start.14) | collective-permute-done | bytes 524320 | tf_op jit(solution)/shard_map/ppermute | solution.py:35
  81.6 6.2 %finish_step.5 = (f32[128,2048]{1,0:T(8,128)S(1)}, bf16[128,2048]{1,0:T(8,128)(2,1)S(1)}) custom-call(s32[2]{0:T(128)S(1)} %copy-done.2, bf16[192,2176]{1,0:T(8,128)(2,1)S(1)} %bitcast.65, bf16[192,2176]{1,0:T(8,128)(2,1)S(1)} %collective-permute-done.8.refs_1_, bf16[192,2176]{1,0:T(8,128)(2,1)S(1)} %collective-permute-done.9.refs_2_, ...), custom_call_target="tpu_custom_call" | custom-call | flops 8589934592 | bytes 1 | tf_op jit(solution)/shard_map/finish_step/pallas_call | solution.py:373
  87.9 1.5 %collective-permute-done.18 = bf16[64,2048]{1,0:T(8,128)(2,1)S(1)} collective-permute-done((bf16[64,2048]{1,0:T(8,128)(2,1)S(1)}, bf16[64,2048]{1,0:T(8,128)(2,1)S(1)}, u32[]{:S(2)}, u32[]{:S(2)}) %collective-permute-start.18) | collective-permute-done | bytes 262176 | tf_op jit(solution)/shard_map/ppermute | solution.py:35
  90.2 2.1 %collective-permute-start.16 = (bf16[32,2048]{1,0:T(8,128)(2,1)S(1)}, bf16[32,2048]{1,0:T(8,128)(2,1)S(1)}, u32[]{:S(2)}, u32[]{:S(2)}) collective-permute-start(bf16[32,2048]{1,0:T(8,128)(2,1)S(1)} %bitcast.85), channel_id=1, source_target_pairs={{0,4},{1,5},{2,6},{3,7},{4,0},{5,1},{6,2},{7,3},{8,12},{9,13},{10,... | collective-permute-start | bytes 393224 | tf_op jit(solution)/shard_map/ppermute | solution.py:35
  92.2 1.5 %collective-permute-start.21 = (bf16[64,2048]{1,0:T(8,128)(2,1)S(1)}, bf16[64,2048]{1,0:T(8,128)(2,1)S(1)}, u32[]{:S(2)}, u32[]{:S(2)}) collective-permute-start(bf16[64,2048]{1,0:T(8,128)(2,1)S(1)} %slice.173), channel_id=1, source_target_pairs={{0,2},{1,3},{2,0},{3,1},{4,6},{5,7},{6,4},{7,5},{8,10},{9,11},{10,... | collective-permute-start | bytes 786440 | tf_op jit(solution)/shard_map/ppermute | solution.py:35
  93.8 2.6 %collective-permute-done.19 = bf16[32,2048]{1,0:T(8,128)(2,1)S(1)} collective-permute-done((bf16[32,2048]{1,0:T(8,128)(2,1)S(1)}, bf16[32,2048]{1,0:T(8,128)(2,1)S(1)}, u32[]{:S(2)}, u32[]{:S(2)}) %collective-permute-start.19) | collective-permute-done | bytes 131104 | tf_op jit(solution)/shard_map/ppermute | solution.py:35
  98.4 1.5 %collective-permute-start.17 = (bf16[16,2048]{1,0:T(8,128)(2,1)S(1)}, bf16[16,2048]{1,0:T(8,128)(2,1)S(1)}, u32[]{:S(2)}, u32[]{:S(2)}) collective-permute-start(bf16[16,2048]{1,0:T(8,128)(2,1)S(1)} %fusion.8), channel_id=1, source_target_pairs={{0,8},{1,9},{2,10},{3,11},{4,12},{5,13},{6,14},{7,15},{8,0},{9,1},... | collective-permute-start | bytes 196616 | tf_op jit(solution)/shard_map/ppermute | solution.py:35
  99.9 3.0 %collective-permute-done.20 = bf16[16,2048]{1,0:T(8,128)(2,1)S(1)} collective-permute-done((bf16[16,2048]{1,0:T(8,128)(2,1)S(1)}, bf16[16,2048]{1,0:T(8,128)(2,1)S(1)}, u32[]{:S(2)}, u32[]{:S(2)}) %collective-permute-start.20) | collective-permute-done | bytes 65568 | tf_op jit(solution)/shard_map/ppermute | solution.py:35
  103.2 2.4 %collective-permute-start.24 = (bf16[16,2048]{1,0:T(8,128)(2,1)S(1)}, bf16[16,2048]{1,0:T(8,128)(2,1)S(1)}, u32[]{:S(2)}, u32[]{:S(2)}) collective-permute-start(bf16[16,2048]{1,0:T(8,128)(2,1)S(1)} %get-tuple-element.98), channel_id=1, source_target_pairs={{0,12},{1,13},{2,14},{3,15},{4,8},{5,9},{6,10},{7,11},{8,4},{9,5},... | collective-permute-start | bytes 196616 | tf_op jit(solution)/shard_map/ppermute | solution.py:35
  106.7 1.4 %collective-permute-done.22 = bf16[16,2048]{1,0:T(8,128)(2,1)S(1)} collective-permute-done((bf16[16,2048]{1,0:T(8,128)(2,1)S(1)}, bf16[16,2048]{1,0:T(8,128)(2,1)S(1)}, u32[]{:S(2)}, u32[]{:S(2)}) %collective-permute-start.22) | collective-permute-done | bytes 65568 | tf_op jit(solution)/shard_map/ppermute | solution.py:35
  108.1 1.3 %collective-permute-done.24 = bf16[16,2048]{1,0:T(8,128)(2,1)S(1)} collective-permute-done((bf16[16,2048]{1,0:T(8,128)(2,1)S(1)}, bf16[16,2048]{1,0:T(8,128)(2,1)S(1)}, u32[]{:S(2)}, u32[]{:S(2)}) %collective-permute-start.24) | collective-permute-done | bytes 65568 | tf_op jit(solution)/shard_map/ppermute | solution.py:35
  109.4 2.0 %collective-permute-done.23 = bf16[16,2048]{1,0:T(8,128)(2,1)S(1)} collective-permute-done((bf16[16,2048]{1,0:T(8,128)(2,1)S(1)}, bf16[16,2048]{1,0:T(8,128)(2,1)S(1)}, u32[]{:S(2)}, u32[]{:S(2)}) %collective-permute-start.23) | collective-permute-done | bytes 65568 | tf_op jit(solution)/shard_map/ppermute | solution.py:35
  (62 shorter events, 10.2 us)
Async XLA Ops:
  0.0 48.7 %copy-start = (bf16[1,2048,768]{2,1,0:T(8,128)(2,1)S(1)}, bf16[1,2048,768]{2,1,0:T(8,128)(2,1)}, u32[]{:S(2)}) copy-start(bf16[1,2048,768]{2,1,0:T(8,128)(2,1)} %param.13) | copy-start | bytes 9437188
  2.1 11.8 %collective-permute-start.2 = (bf16[48,2176]{1,0:T(8,128)(2,1)}, bf16[48,2176]{1,0:T(8,128)(2,1)S(1)}, u32[]{:S(2)}, u32[]{:S(2)}) collective-permute-start(bf16[48,2176]{1,0:T(8,128)(2,1)} %payload.1), channel_id=1, source_target_pairs={{0,12},{1,13},{2,14},{3,15},{4,8},{5,9},{6,10},{7,11},{8,4},{9,5},... | collective-permute-start | bytes 626696 | tf_op jit(solution)/shard_map/ppermute | solution.py:35
  7.2 18.1 %collective-permute-start.1 = (bf16[48,2176]{1,0:T(8,128)(2,1)}, bf16[48,2176]{1,0:T(8,128)(2,1)}, u32[]{:S(2)}, u32[]{:S(2)}) collective-permute-start(bf16[48,2176]{1,0:T(8,128)(2,1)} %payload.1), channel_id=1, source_target_pairs={{0,8},{1,9},{2,10},{3,11},{4,12},{5,13},{6,14},{7,15},{8,0},{9,1},... | collective-permute-start | bytes 626696 | tf_op jit(solution)/shard_map/ppermute | solution.py:35
  7.2 18.1 %collective-permute-start = (bf16[48,2176]{1,0:T(8,128)(2,1)}, bf16[48,2176]{1,0:T(8,128)(2,1)}, u32[]{:S(2)}, u32[]{:S(2)}) collective-permute-start(bf16[48,2176]{1,0:T(8,128)(2,1)} %payload.1), channel_id=1, source_target_pairs={{0,4},{1,5},{2,6},{3,7},{4,0},{5,1},{6,2},{7,3},{8,12},{9,13},{10,... | collective-permute-start | bytes 626696 | tf_op jit(solution)/shard_map/ppermute | solution.py:35
  11.2 37.5 %copy-start.1 = (bf16[1,2048,768]{2,1,0:T(8,128)(2,1)S(1)}, bf16[1,2048,768]{2,1,0:T(8,128)(2,1)}, u32[]{:S(2)}) copy-start(bf16[1,2048,768]{2,1,0:T(8,128)(2,1)} %param.14) | copy-start | bytes 9437188
  11.2 15.3 %collective-permute-start.3 = (bf16[4,264,128]{2,1,0:T(8,128)(2,1)}, bf16[4,264,128]{2,1,0:T(8,128)(2,1)S(1)}, u32[]{:S(2)}, u32[]{:S(2)}) collective-permute-start(bf16[4,264,128]{2,1,0:T(8,128)(2,1)} %get-tuple-element.49), channel_id=1, source_target_pairs={{0,2},{1,3},{2,0},{3,1},{4,6},{5,7},{6,4},{7,5},{8,10},{9,11},{10,... | collective-permute-start | bytes 811016 | tf_op jit(solution)/shard_map/ppermute | solution.py:35
  26.6 19.7 %collective-permute-start.8 = (bf16[192,2176]{1,0:T(8,128)(2,1)S(1)}, bf16[192,2176]{1,0:T(8,128)(2,1)S(1)}, u32[]{:S(2)}, u32[]{:S(2)}) collective-permute-start(bf16[192,2176]{1,0:T(8,128)(2,1)S(1)} %bitcast.60), channel_id=1, source_target_pairs={{0,2},{1,3},{2,0},{3,1},{4,6},{5,7},{6,4},{7,5},{8,10},{9,11},{10,... | collective-permute-start | bytes 2506760 | tf_op jit(solution)/shard_map/ppermute | solution.py:35
  28.2 5.1 %collective-permute-start.4 = (bf16[2,264,128]{2,1,0:T(8,128)(2,1)S(1)}, bf16[2,264,128]{2,1,0:T(8,128)(2,1)S(1)}, u32[]{:S(2)}, u32[]{:S(2)}) collective-permute-start(bf16[2,264,128]{2,1,0:T(8,128)(2,1)S(1)} %get-tuple-element.51), channel_id=1, source_target_pairs={{0,0},{1,1},{2,2},{3,3},{4,4},{5,5},{6,6},{7,7},{8,8},{9,9},{10,10... | collective-permute-start | bytes 405512 | tf_op jit(solution)/shard_map/ppermute | solution.py:65
  28.9 6.5 %collective-permute-start.5 = (bf16[2,264,128]{2,1,0:T(8,128)(2,1)S(1)}, bf16[2,264,128]{2,1,0:T(8,128)(2,1)S(1)}, u32[]{:S(2)}, u32[]{:S(2)}) collective-permute-start(bf16[2,264,128]{2,1,0:T(8,128)(2,1)S(1)} %get-tuple-element.52), channel_id=1, source_target_pairs={{0,4},{1,5},{2,6},{3,7},{4,0},{5,1},{6,2},{7,3},{8,12},{9,13},{10,... | collective-permute-start | bytes 405512 | tf_op jit(solution)/shard_map/ppermute | solution.py:65
  28.9 12.6 %collective-permute-start.6 = (bf16[2,264,128]{2,1,0:T(8,128)(2,1)S(1)}, bf16[2,264,128]{2,1,0:T(8,128)(2,1)S(1)}, u32[]{:S(2)}, u32[]{:S(2)}) collective-permute-start(bf16[2,264,128]{2,1,0:T(8,128)(2,1)S(1)} %get-tuple-element.53), channel_id=1, source_target_pairs={{0,8},{1,9},{2,10},{3,11},{4,12},{5,13},{6,14},{7,15},{8,0},{9,1},... | collective-permute-start | bytes 405512 | tf_op jit(solution)/shard_map/ppermute | solution.py:65
  32.0 9.6 %collective-permute-start.7 = (bf16[2,264,128]{2,1,0:T(8,128)(2,1)S(1)}, bf16[2,264,128]{2,1,0:T(8,128)(2,1)S(1)}, u32[]{:S(2)}, u32[]{:S(2)}) collective-permute-start(bf16[2,264,128]{2,1,0:T(8,128)(2,1)S(1)} %get-tuple-element.54), channel_id=1, source_target_pairs={{0,12},{1,13},{2,14},{3,15},{4,8},{5,9},{6,10},{7,11},{8,4},{9,5},... | collective-permute-start | bytes 405512 | tf_op jit(solution)/shard_map/ppermute | solution.py:65
  33.3 14.6 %collective-permute-start.9 = (bf16[192,2176]{1,0:T(8,128)(2,1)S(1)}, bf16[192,2176]{1,0:T(8,128)(2,1)S(1)}, u32[]{:S(2)}, u32[]{:S(2)}) collective-permute-start(bf16[192,2176]{1,0:T(8,128)(2,1)S(1)} %bitcast.61), channel_id=1, source_target_pairs={{0,1},{1,0},{2,3},{3,2},{4,5},{5,4},{6,7},{7,6},{8,9},{9,8},{10,11... | collective-permute-start | bytes 2506760 | tf_op jit(solution)/shard_map/ppermute | solution.py:35
  46.3 2.4 %collective-permute-start.10 = (bf16[192,2176]{1,0:T(8,128)(2,1)S(1)}, bf16[192,2176]{1,0:T(8,128)(2,1)S(1)}, u32[]{:S(2)}, u32[]{:S(2)}) collective-permute-start(bf16[192,2176]{1,0:T(8,128)(2,1)S(1)} %collective-permute-done.8.refs_1_), channel_id=1, source_target_pairs={{0,1},{1,0},{2,3},{3,2},{4,5},{5,4},{6,7},{7,6},{8,9},{9,8},{10,11... | collective-permute-start | bytes 2506760 | tf_op jit(solution)/shard_map/ppermute | solution.py:35
  46.4 14.8 %collective-permute-start.11 = (bf16[4,2,264,128]{3,2,1,0:T(8,128)(2,1)S(1)}, bf16[4,2,264,128]{3,2,1,0:T(8,128)(2,1)S(1)}, u32[]{:S(2)}, u32[]{:S(2)}) collective-permute-start(bf16[4,2,264,128]{3,2,1,0:T(8,128)(2,1)S(1)} %pad_maximum_fusion.1.refs_0_), channel_id=1, source_target_pairs={{0,16},{16,0},{1,17},{17,1},{2,18},{18,2},{3,19},{19,3},{4,20},{20... | collective-permute-start | bytes 1622024 | tf_op jit(solution)/shard_map/ppermute | solution.py:425
  48.7 12.5 %copy-start.2 = (s32[2]{0:T(128)S(1)}, s32[2]{0:T(128)}, u32[]{:S(2)}) copy-start(s32[2]{0:T(128)} %pad_add_fusion.place_ref) | copy-start | bytes 28
  48.7 14.1 %copy-start.3 = (bf16[1,768,2048]{2,1,0:T(8,128)(2,1)S(1)}, bf16[1,768,2048]{2,1,0:T(8,128)(2,1)}, u32[]{:S(2)}) copy-start(bf16[1,768,2048]{2,1,0:T(8,128)(2,1)} %param.15) | copy-start | bytes 9437188
  69.0 2.0 %collective-permute-start.12 = (bf16[128,2048]{1,0:T(8,128)(2,1)S(1)}, bf16[128,2048]{1,0:T(8,128)(2,1)S(1)}, u32[]{:S(2)}, u32[]{:S(2)}) collective-permute-start(bf16[128,2048]{1,0:T(8,128)(2,1)S(1)} %get-tuple-element.72), channel_id=1, source_target_pairs={{0,1},{1,0},{2,3},{3,2},{4,5},{5,4},{6,7},{7,6},{8,9},{9,8},{10,11... | collective-permute-start | bytes 1572872 | tf_op jit(solution)/shard_map/ppermute | solution.py:35
  71.1 8.4 %collective-permute-start.13 = (bf16[64,2048]{1,0:T(8,128)(2,1)S(1)}, bf16[64,2048]{1,0:T(8,128)(2,1)S(1)}, u32[]{:S(2)}, u32[]{:S(2)}) collective-permute-start(bf16[64,2048]{1,0:T(8,128)(2,1)S(1)} %slice.175), channel_id=1, source_target_pairs={{0,2},{1,3},{2,0},{3,1},{4,6},{5,7},{6,4},{7,5},{8,10},{9,11},{10,... | collective-permute-start | bytes 786440 | tf_op jit(solution)/shard_map/ppermute | solution.py:35
  78.9 2.0 %collective-permute-start.14 = (bf16[128,2048]{1,0:T(8,128)(2,1)S(1)}, bf16[128,2048]{1,0:T(8,128)(2,1)S(1)}, u32[]{:S(2)}, u32[]{:S(2)}) collective-permute-start(bf16[128,2048]{1,0:T(8,128)(2,1)S(1)} %get-tuple-element.78), channel_id=1, source_target_pairs={{0,1},{1,0},{2,3},{3,2},{4,5},{5,4},{6,7},{7,6},{8,9},{9,8},{10,11... | collective-permute-start | bytes 1572872 | tf_op jit(solution)/shard_map/ppermute | solution.py:35
  81.1 8.4 %collective-permute-start.18 = (bf16[64,2048]{1,0:T(8,128)(2,1)S(1)}, bf16[64,2048]{1,0:T(8,128)(2,1)S(1)}, u32[]{:S(2)}, u32[]{:S(2)}) collective-permute-start(bf16[64,2048]{1,0:T(8,128)(2,1)S(1)} %slice.174), channel_id=1, source_target_pairs={{0,2},{1,3},{2,0},{3,1},{4,6},{5,7},{6,4},{7,5},{8,10},{9,11},{10,... | collective-permute-start | bytes 786440 | tf_op jit(solution)/shard_map/ppermute | solution.py:35
  87.8 2.0 %collective-permute-start.15 = (bf16[128,2048]{1,0:T(8,128)(2,1)S(1)}, bf16[128,2048]{1,0:T(8,128)(2,1)S(1)}, u32[]{:S(2)}, u32[]{:S(2)}) collective-permute-start(bf16[128,2048]{1,0:T(8,128)(2,1)S(1)} %get-tuple-element.84), channel_id=1, source_target_pairs={{0,1},{1,0},{2,3},{3,2},{4,5},{5,4},{6,7},{7,6},{8,9},{9,8},{10,11... | collective-permute-start | bytes 1572872 | tf_op jit(solution)/shard_map/ppermute | solution.py:35
  90.0 6.4 %collective-permute-start.19 = (bf16[32,2048]{1,0:T(8,128)(2,1)S(1)}, bf16[32,2048]{1,0:T(8,128)(2,1)S(1)}, u32[]{:S(2)}, u32[]{:S(2)}) collective-permute-start(bf16[32,2048]{1,0:T(8,128)(2,1)S(1)} %bitcast.86), channel_id=1, source_target_pairs={{0,4},{1,5},{2,6},{3,7},{4,0},{5,1},{6,2},{7,3},{8,12},{9,13},{10,... | collective-permute-start | bytes 393224 | tf_op jit(solution)/shard_map/ppermute | solution.py:35
  90.2 8.2 %collective-permute-start.16 = (bf16[32,2048]{1,0:T(8,128)(2,1)S(1)}, bf16[32,2048]{1,0:T(8,128)(2,1)S(1)}, u32[]{:S(2)}, u32[]{:S(2)}) collective-permute-start(bf16[32,2048]{1,0:T(8,128)(2,1)S(1)} %bitcast.85), channel_id=1, source_target_pairs={{0,4},{1,5},{2,6},{3,7},{4,0},{5,1},{6,2},{7,3},{8,12},{9,13},{10,... | collective-permute-start | bytes 393224 | tf_op jit(solution)/shard_map/ppermute | solution.py:35
  92.2 10.7 %collective-permute-start.21 = (bf16[64,2048]{1,0:T(8,128)(2,1)S(1)}, bf16[64,2048]{1,0:T(8,128)(2,1)S(1)}, u32[]{:S(2)}, u32[]{:S(2)}) collective-permute-start(bf16[64,2048]{1,0:T(8,128)(2,1)S(1)} %slice.173), channel_id=1, source_target_pairs={{0,2},{1,3},{2,0},{3,1},{4,6},{5,7},{6,4},{7,5},{8,10},{9,11},{10,... | collective-permute-start | bytes 786440 | tf_op jit(solution)/shard_map/ppermute | solution.py:35
  96.4 6.5 %collective-permute-start.20 = (bf16[16,2048]{1,0:T(8,128)(2,1)S(1)}, bf16[16,2048]{1,0:T(8,128)(2,1)S(1)}, u32[]{:S(2)}, u32[]{:S(2)}) collective-permute-start(bf16[16,2048]{1,0:T(8,128)(2,1)S(1)} %fusion.10), channel_id=1, source_target_pairs={{0,8},{1,9},{2,10},{3,11},{4,12},{5,13},{6,14},{7,15},{8,0},{9,1},... | collective-permute-start | bytes 196616 | tf_op jit(solution)/shard_map/ppermute | solution.py:35
  98.4 8.2 %collective-permute-start.17 = (bf16[16,2048]{1,0:T(8,128)(2,1)S(1)}, bf16[16,2048]{1,0:T(8,128)(2,1)S(1)}, u32[]{:S(2)}, u32[]{:S(2)}) collective-permute-start(bf16[16,2048]{1,0:T(8,128)(2,1)S(1)} %fusion.8), channel_id=1, source_target_pairs={{0,8},{1,9},{2,10},{3,11},{4,12},{5,13},{6,14},{7,15},{8,0},{9,1},... | collective-permute-start | bytes 196616 | tf_op jit(solution)/shard_map/ppermute | solution.py:35
  103.1 5.0 %collective-permute-start.22 = (bf16[16,2048]{1,0:T(8,128)(2,1)S(1)}, bf16[16,2048]{1,0:T(8,128)(2,1)S(1)}, u32[]{:S(2)}, u32[]{:S(2)}) collective-permute-start(bf16[16,2048]{1,0:T(8,128)(2,1)S(1)} %get-tuple-element.97), channel_id=1, source_target_pairs={{0,4},{1,5},{2,6},{3,7},{4,0},{5,1},{6,2},{7,3},{8,12},{9,13},{10,... | collective-permute-start | bytes 196616 | tf_op jit(solution)/shard_map/ppermute | solution.py:35
  103.2 6.2 %collective-permute-start.24 = (bf16[16,2048]{1,0:T(8,128)(2,1)S(1)}, bf16[16,2048]{1,0:T(8,128)(2,1)S(1)}, u32[]{:S(2)}, u32[]{:S(2)}) collective-permute-start(bf16[16,2048]{1,0:T(8,128)(2,1)S(1)} %get-tuple-element.98), channel_id=1, source_target_pairs={{0,12},{1,13},{2,14},{3,15},{4,8},{5,9},{6,10},{7,11},{8,4},{9,5},... | collective-permute-start | bytes 196616 | tf_op jit(solution)/shard_map/ppermute | solution.py:35
  105.5 5.9 %collective-permute-start.23 = (bf16[16,2048]{1,0:T(8,128)(2,1)S(1)}, bf16[16,2048]{1,0:T(8,128)(2,1)S(1)}, u32[]{:S(2)}, u32[]{:S(2)}) collective-permute-start(bf16[16,2048]{1,0:T(8,128)(2,1)S(1)} %get-tuple-element.99), channel_id=1, source_target_pairs={{0,8},{1,9},{2,10},{3,11},{4,12},{5,13},{6,14},{7,15},{8,0},{9,1},... | collective-permute-start | bytes 196616 | tf_op jit(solution)/shard_map/ppermute | solution.py:35

commit v17 on v16

--- a/solution.py
+++ b/solution.py
@@ -35,23 +35,26 @@
     return lax.ppermute(x, "expert", [(i, i ^ (k * stride)) for i in range(n)])
 
 
-def scatter_along(total, n, stride, size):
+def scatter_along(total, n, stride, size, received=None):
     count = total.shape[0] // size
-    result = total[:count]
+    received = [] if received is None else received
     for k in range(1, size):
         part = total[k * count : (k + 1) * count].astype(jnp.bfloat16)
-        result = result + swap(part, n, stride, k).astype(jnp.float32)
-    return result
-
-
-def halve_along(total, n, stride, size):
+        received.append(swap(part, n, stride, k))
+    return sum([part.astype(jnp.float32) for part in received], total[:count])
+
+
+def halve_along(total, n, stride, size, last):
     count = total.shape[0] // size
     step = 1
     while step < size:
         total = total.reshape(-1, 2, count, total.shape[1])
         sent = total[:, 1].reshape(-1, total.shape[3]).astype(jnp.bfloat16)
         kept = total[:, 0].reshape(-1, total.shape[3])
-        total = kept + swap(sent, n, stride, step).astype(jnp.float32)
+        sent = swap(sent, n, stride, step)
+        if 2 * step == size:
+            sent = lax.optimization_barrier((sent, last))[0]
+        total = kept + sent.astype(jnp.float32)
         step *= 2
     return total
 
@@ -295,7 +298,7 @@
     )(*pieces, w_gate, w_up)
 
 
-def finish_kernel(count, first, rows, block, parts, place_ref, *refs):
+def finish_kernel(count, first, rows, place_ref, *refs):
     pieces, refs = refs[:count], refs[count:]
     gate_hbm, up_hbm, a_gu_hbm, gate_b_hbm, up_b_hbm, down_a_hbm, down_b_hbm = refs[:7]
     w_down_hbm, kept_hbm, sent_hbm, x_ref, gate_ref, up_ref = refs[7:13]
@@ -317,49 +320,29 @@
         base_in += loads.begin(up_hbm.at[src], up_ref.at[dst])
     down_in = loads.begin(down_a_hbm, down_a_ref) + loads.begin(down_b_hbm, down_b_ref)
     down_in += loads.begin_rows(w_down_hbm, w_down_ref)
-    cuts = [slice(at, at + block) for at in range(0, 2 * own, block)]
     wait(x_in)
-    lows = []
-    for cut in cuts:
-        low = adapter_scale * dot(x_ref[cut, :width], a_gu_ref[...])
-        lows.append(low.astype(jnp.bfloat16))
+    low = (adapter_scale * dot(x_ref[:, :width], a_gu_ref[...])).astype(jnp.bfloat16)
+    gates = x_ref[:, width:].astype(jnp.float32)
+    lane = lax.broadcasted_iota(jnp.int32, gates.shape, 1)
+    mine = jnp.sum(jnp.where(lane == place_ref[1], gates, 0.0), axis=1, keepdims=True)
     wait(base_in)
-    for cut, low in zip(cuts, lows):
-        g = gate_ref[cut, :] + dot(low[:, :rank], gate_b_ref[...])
-        u = up_ref[cut, :] + dot(low[:, rank:], up_b_ref[...])
-        inner_ref[cut, :] = (g / (1.0 + jnp.exp(-g)) * u).astype(jnp.bfloat16)
+    g = gate_ref[...] + dot(low[:, :rank], gate_b_ref[...])
+    u = up_ref[...] + dot(low[:, rank:], up_b_ref[...])
+    half = 0.5 * g
+    inner_ref[...] = ((half + half * jnp.tanh(half)) * u).astype(jnp.bfloat16)
     wait(down_in)
-    lows = []
-    for cut in cuts:
-        low = adapter_scale * dot(inner_ref[cut, :], down_a_ref[...])
-        lows.append(low.astype(jnp.bfloat16)[:, :rank])
-    out_copies = []
-    half = width // parts
-    columns = [slice(at, at + half) for at in range(0, width, half)]
-    for cut, low in zip(cuts, lows):
-        gates = x_ref[cut, width:].astype(jnp.float32)
-        lane = lax.broadcasted_iota(jnp.int32, gates.shape, 1)
-        mine = jnp.sum(jnp.where(lane == place_ref[1], gates, 0.0), axis=1, keepdims=True)
-        outs = [
-            (dot(inner_ref[cut, :], w_down_ref[:, c]) + dot(low, down_b_ref[:, c])) * mine
-            for c in columns
-        ]
-        ends = [(kept_ref, kept_hbm, 0), (sent_ref, sent_hbm, own)]
-        for out_ref, out_hbm, start in ends:
-            at, to = max(cut.start, start), min(cut.stop, start + own)
-            if at < to:
-                for c, out in zip(columns, outs):
-                    part = out[at - cut.start : to - cut.start]
-                    out_ref[at - start : to - start, c] = part.astype(out_ref.dtype)
-                rows_out = pl.ds(at - start, to - at)
-                sem_out = out_sem.at[len(out_copies)]
-                copy = pltpu.make_async_copy(out_ref.at[rows_out], out_hbm.at[rows_out], sem_out)
-                copy.start()
-                out_copies.append(copy)
-    wait(out_copies)
-
-
-def finish_step(place, pieces, base, first, rows, low_rank, w_down, block, parts):
+    low = (adapter_scale * dot(inner_ref[...], down_a_ref[...])).astype(jnp.bfloat16)[:, :rank]
+    out = (dot(inner_ref[...], w_down_ref[...]) + dot(low, down_b_ref[...])) * mine
+    sent_ref[...] = out[own:].astype(jnp.bfloat16)
+    sent_out = pltpu.make_async_copy(sent_ref, sent_hbm, out_sem.at[0])
+    sent_out.start()
+    kept_ref[...] = out[:own]
+    kept_out = pltpu.make_async_copy(kept_ref, kept_hbm, out_sem.at[1])
+    kept_out.start()
+    wait([sent_out, kept_out])
+
+
+def finish_step(place, pieces, base, first, rows, low_rank, w_down):
     units, width = w_down.shape
     total = rows * len(pieces)
     own = total // 2
@@ -371,7 +354,7 @@
     ]
     held = [*low_rank, w_down]
     return pl.pallas_call(
-        functools.partial(finish_kernel, len(pieces), first, rows, block, parts),
+        functools.partial(finish_kernel, len(pieces), first, rows),
         out_shape=outs,
         in_specs=[pl.BlockSpec(memory_space=pltpu.SMEM)]
         + [pl.BlockSpec(memory_space=pl.ANY)] * (len(pieces) + 2 + len(low_rank))
@@ -387,7 +370,7 @@
         + [pltpu.VMEM(o.shape, o.dtype) for o in outs]
         + [
             pltpu.SemaphoreType.DMA((3 * len(pieces) + 9,)),
-            pltpu.SemaphoreType.DMA((2 * own // min(block, own),)),
+            pltpu.SemaphoreType.DMA((2,)),
         ],
         compiler_params=pltpu.CompilerParams(vmem_limit_bytes=EXPERT_GRANT),
         cost_estimate=MUCH,
@@ -436,16 +419,16 @@
     for s in range(steps):
         if s >= 1:
             pieces = lax.optimization_barrier((pieces, summed[s - 1], across[: s - 1]))[0]
-        block, parts = [(128, 1), (256, 1), (256, 2)][s % 3]
         kept, sent = finish_step(
-            place, pieces, base, s * span, span, low_rank, down_weight[0], block, parts
+            place, pieces, base, s * span, span, low_rank, down_weight[0]
         )
         summed.append(kept + swap(sent, owners, 1, 1).astype(jnp.float32))
         across.append(scatter_along(summed[s], owners, *along_middle))
     across[:-1] = [after(total, summed[-1]) for total in across[:-1]]
-    results = [halve_along(total, owners, *along_outer) for total in across[:-1]]
-    results.append(scatter_along(across[-1], owners, *along_outer))
-    return jnp.stack(results).astype(jnp.bfloat16)
+    ends = []
+    final = scatter_along(across[-1], owners, *along_outer, ends)
+    results = [halve_along(total, owners, *along_outer, ends[0]) for total in across[:-1]]
+    return jnp.stack(results + [final]).astype(jnp.bfloat16)
 
 
 def row_capacity(rows, top, experts):

time: 112 us -> 112 us (level)
  no operation moved by 1% of the time
where the time goes in v17:
time: 112 us
  waiting for transfers between devices  45.5 us (41%)
  Pallas kernels  34.6 us (31%)
  starting transfers between devices  27.3 us (24%)
  other arithmetic  3.34 us (3%)
  local copies, waits for them, and re-layouts  1.23 us (1%)
    ppermute x20, waiting for transfers between devices, swap(): return lax.ppermute(x, 'expert', [(i, i ^ k * stride) for i in range(n)])  34.1 us
    ppermute x20, starting transfers between devices, swap(): return lax.ppermute(x, 'expert', [(i, i ^ k * stride) for i in range(n)])  20.6 us
    pallas_call x3, Pallas kernels, finish_step(): pl.pallas_call(functools.partial(finish_kernel, len(pieces), first, rows)...  18.7 us
    pallas_call x1, Pallas kernels, base_products(): pl.pallas_call(functools.partial(base_kernel, len(pieces)), out_shape=[ou...  9.3 us
    ppermute x4, waiting for transfers between devices, exchange_factors(): here.append(lax.ppermute(block, ('group', 'expert'), pairs))  8.23 us
    ppermute x4, starting transfers between devices, exchange_factors(): here.append(lax.ppermute(block, ('group', 'expert'), pairs))  5.1 us
    ppermute x1, waiting for transfers between devices, dense_shards(): there = lax.ppermute(here, 'group', [(0, 1), (1, 0)])  3.15 us
    pallas_call x1, Pallas kernels, order_factors(): pl.pallas_call(order_kernel, out_shape=[jax.ShapeDtypeStruct((outer, leng...  2.8 us
  transfers between devices with their start and end apart: 25, of which 17 were waited for; matrix products, arithmetic and copies ran while one was open for 3% of the time, Pallas kernels for 22%

profile of v17, /device:TPU:0, one launch (start us, length us, event | category | flops | bytes accessed | tf_op | source)
XLA Modules:
  0.0 112.2 jit_solution(12749858394453901830)
XLA Ops:
  0.0 2.1 %payload.1 = bf16[48,2176]{1,0:T(8,128)(2,1)} custom-call(bf16[3,16,2048]{2,1,0:T(8,128)(2,1)} %hidden_ref.1, s32[3,8,16]{2,1,0:T(8,128)} %bitcast.87, f32[3,8,16]{2,1,0:T(8,128)} %bitcast.88), custom_call_target="tpu_custom_call" | custom-call | flops 1 | bytes 1 | tf_op jit(solution)/shard_map/payload/pallas_call | solution.py:98
  2.1 5.0 %collective-permute-start.2 = (bf16[48,2176]{1,0:T(8,128)(2,1)}, bf16[48,2176]{1,0:T(8,128)(2,1)S(1)}, u32[]{:S(2)}, u32[]{:S(2)}) collective-permute-start(bf16[48,2176]{1,0:T(8,128)(2,1)} %payload.1), channel_id=1, source_target_pairs={{0,12},{1,13},{2,14},{3,15},{4,8},{5,9},{6,10},{7,11},{8,4},{9,5},... | collective-permute-start | bytes 626696 | tf_op jit(solution)/shard_map/ppermute | solution.py:35
  8.4 2.8 %order_factors.1 = (bf16[4,264,128]{2,1,0:T(8,128)(2,1)}, bf16[4,264,128]{2,1,0:T(8,128)(2,1)}) custom-call(s32[2]{0:T(128)} %pad_add_fusion.place_ref, s32[16]{0:T(128)} %placement_ref.1, bf16[16,33792]{1,0:T(8,128)(2,1)} %factors_ref), custom_call_target="tpu_custom_call" | custom-call | flops 1 | bytes 1 | tf_op jit(solution)/shard_map/order_factors/pallas_call | solution.py:133
  11.2 1.7 %collective-permute-start.3 = (bf16[4,264,128]{2,1,0:T(8,128)(2,1)}, bf16[4,264,128]{2,1,0:T(8,128)(2,1)S(1)}, u32[]{:S(2)}, u32[]{:S(2)}) collective-permute-start(bf16[4,264,128]{2,1,0:T(8,128)(2,1)} %get-tuple-element.51), channel_id=1, source_target_pairs={{0,2},{1,3},{2,0},{3,1},{4,6},{5,7},{6,4},{7,5},{8,10},{9,11},{10,... | collective-permute-start | bytes 811016 | tf_op jit(solution)/shard_map/ppermute | solution.py:35
  14.0 11.3 %collective-permute-done.1 = bf16[48,2176]{1,0:T(8,128)(2,1)} collective-permute-done((bf16[48,2176]{1,0:T(8,128)(2,1)}, bf16[48,2176]{1,0:T(8,128)(2,1)}, u32[]{:S(2)}, u32[]{:S(2)}) %collective-permute-start.1) | collective-permute-done | bytes 208928 | tf_op jit(solution)/shard_map/ppermute | solution.py:35
  25.3 1.3 %pad_maximum_fusion = bf16[3,4,16,2176]{3,2,1,0:T(8,128)(2,1)S(1)} fusion(bf16[3,1,16,2176]{3,2,1,0:T(8,128)(2,1)S(1)} %bitcast.80, bf16[3,1,16,2176]{3,2,1,0:T(8,128)(2,1)} %bitcast.9, bf16[3,1,16,2176]{3,2,1,0:T(8,128)(2,1)} %bitcast.7, bf16[3,1,16,2176]{3,2,1,0:T(8,128)(2,1)} %bitcast.75), kind=kLoop, calls=%fused_computation.3 | loop fusion | flops 1253376 | bytes 1671168 | tf_op jit(solution)/shard_map/stack | solution.py:399
  26.6 1.6 %collective-permute-start.8 = (bf16[192,2176]{1,0:T(8,128)(2,1)S(1)}, bf16[192,2176]{1,0:T(8,128)(2,1)S(1)}, u32[]{:S(2)}, u32[]{:S(2)}) collective-permute-start(bf16[192,2176]{1,0:T(8,128)(2,1)S(1)} %bitcast.60), channel_id=1, source_target_pairs={{0,2},{1,3},{2,0},{3,1},{4,6},{5,7},{6,4},{7,5},{8,10},{9,11},{10,... | collective-permute-start | bytes 2506760 | tf_op jit(solution)/shard_map/ppermute | solution.py:35
  28.9 3.0 %collective-permute-start.6 = (bf16[2,264,128]{2,1,0:T(8,128)(2,1)S(1)}, bf16[2,264,128]{2,1,0:T(8,128)(2,1)S(1)}, u32[]{:S(2)}, u32[]{:S(2)}) collective-permute-start(bf16[2,264,128]{2,1,0:T(8,128)(2,1)S(1)} %get-tuple-element.55), channel_id=1, source_target_pairs={{0,8},{1,9},{2,10},{3,11},{4,12},{5,13},{6,14},{7,15},{8,0},{9,1},... | collective-permute-start | bytes 405512 | tf_op jit(solution)/shard_map/ppermute | solution.py:68
  32.0 1.3 %collective-permute-start.7 = (bf16[2,264,128]{2,1,0:T(8,128)(2,1)S(1)}, bf16[2,264,128]{2,1,0:T(8,128)(2,1)S(1)}, u32[]{:S(2)}, u32[]{:S(2)}) collective-permute-start(bf16[2,264,128]{2,1,0:T(8,128)(2,1)S(1)} %get-tuple-element.56), channel_id=1, source_target_pairs={{0,12},{1,13},{2,14},{3,15},{4,8},{5,9},{6,10},{7,11},{8,4},{9,5},... | collective-permute-start | bytes 405512 | tf_op jit(solution)/shard_map/ppermute | solution.py:68
  33.3 2.0 %collective-permute-done.5 = bf16[2,264,128]{2,1,0:T(8,128)(2,1)S(1)} collective-permute-done((bf16[2,264,128]{2,1,0:T(8,128)(2,1)S(1)}, bf16[2,264,128]{2,1,0:T(8,128)(2,1)S(1)}, u32[]{:S(2)}, u32[]{:S(2)}) %collective-permute-start.5) | collective-permute-done | bytes 135200 | tf_op jit(solution)/shard_map/ppermute | solution.py:68
  35.4 6.2 %collective-permute-done.6 = bf16[2,264,128]{2,1,0:T(8,128)(2,1)S(1)} collective-permute-done((bf16[2,264,128]{2,1,0:T(8,128)(2,1)S(1)}, bf16[2,264,128]{2,1,0:T(8,128)(2,1)S(1)}, u32[]{:S(2)}, u32[]{:S(2)}) %collective-permute-start.6) | collective-permute-done | bytes 135200 | tf_op jit(solution)/shard_map/ppermute | solution.py:68
  41.6 4.8 %collective-permute-done.8.refs_1_ = bf16[192,2176]{1,0:T(8,128)(2,1)S(1)} collective-permute-done((bf16[192,2176]{1,0:T(8,128)(2,1)S(1)}, bf16[192,2176]{1,0:T(8,128)(2,1)S(1)}, u32[]{:S(2)}, u32[]{:S(2)}) %collective-permute-start.8) | collective-permute-done | bytes 835616 | tf_op jit(solution)/shard_map/ppermute | solution.py:35
  46.4 1.6 %collective-permute-start.11 = (bf16[4,2,264,128]{3,2,1,0:T(8,128)(2,1)S(1)}, bf16[4,2,264,128]{3,2,1,0:T(8,128)(2,1)S(1)}, u32[]{:S(2)}, u32[]{:S(2)}) collective-permute-start(bf16[4,2,264,128]{3,2,1,0:T(8,128)(2,1)S(1)} %pad_maximum_fusion.1.refs_0_), channel_id=1, source_target_pairs={{0,16},{16,0},{1,17},{17,1},{2,18},{18,2},{3,19},{19,3},{4,20},{20... | collective-permute-start | bytes 1622024 | tf_op jit(solution)/shard_map/ppermute | solution.py:408
  48.7 9.3 %base_products.1 = (f32[768,768]{1,0:T(8,128)S(1)}, f32[768,768]{1,0:T(8,128)S(1)}) custom-call(bf16[192,2176]{1,0:T(8,128)(2,1)S(1)} %bitcast.62, bf16[192,2176]{1,0:T(8,128)(2,1)S(1)} %collective-permute-done.8.refs_1_, bf16[192,2176]{1,0:T(8,128)(2,1)S(1)} %collective-permute-done.9.refs_2_, bf16[192,2176]{1,0:T(8,128)(2,1)S(1)} %collective-permute-done.10.refs_3_, ...), custom_call_target="tpu_custom_call" | custom-call | flops 1 | bytes 1 | tf_op jit(solution)/shard_map/base_products/pallas_call | solution.py:280
  58.0 3.1 %collective-permute-done.11.refs_1_ = bf16[4,2,264,128]{3,2,1,0:T(8,128)(2,1)S(1)} collective-permute-done((bf16[4,2,264,128]{3,2,1,0:T(8,128)(2,1)S(1)}, bf16[4,2,264,128]{3,2,1,0:T(8,128)(2,1)S(1)}, u32[]{:S(2)}, u32[]{:S(2)}) %collective-permute-start.11) | collective-permute-done | bytes 540704 | tf_op jit(solution)/shard_map/ppermute | solution.py:408
  61.2 1.6 %relayout_factors.1 = (bf16[2048,128]{1,0:T(8,128)(2,1)S(1)}, bf16[64,768]{1,0:T(8,128)(2,1)S(1)}, bf16[64,768]{1,0:T(8,128)(2,1)S(1)}, bf16[768,128]{1,0:T(8,128)(2,1)S(1)}, bf16[64,2048]{1,0:T(8,128)(2,1)S(1)}) custom-call(s32[2]{0:T(128)S(1)} %copy-done.2, bf16[4,2,264,128]{3,2,1,0:T(8,128)(2,1)S(1)} %pad_maximum_fusion.1.refs_0_, ...), custom_call_target="tpu_custom_call" | custom-call | flops 1 | bytes 1 | tf_op jit(solution)/shard_map/relayout_factors/pallas_call | solution.py:205
  62.8 6.2 %finish_step.3 = (f32[128,2048]{1,0:T(8,128)S(1)}, bf16[128,2048]{1,0:T(8,128)(2,1)S(1)}) custom-call(s32[2]{0:T(128)S(1)} %copy-done.2, bf16[192,2176]{1,0:T(8,128)(2,1)S(1)} %bitcast.63, bf16[192,2176]{1,0:T(8,128)(2,1)S(1)} %collective-permute-done.8.refs_1_, bf16[192,2176]{1,0:T(8,128)(2,1)S(1)} %collective-permute-done.9.refs_2_, ...), custom_call_target="tpu_custom_call" | custom-call | flops 8589934592 | bytes 1 | tf_op jit(solution)/shard_map/finish_step/pallas_call | solution.py:356
  69.1 1.9 %collective-permute-done.12 = bf16[128,2048]{1,0:T(8,128)(2,1)S(1)} collective-permute-done((bf16[128,2048]{1,0:T(8,128)(2,1)S(1)}, bf16[128,2048]{1,0:T(8,128)(2,1)S(1)}, u32[]{:S(2)}, u32[]{:S(2)}) %collective-permute-start.12) | collective-permute-done | bytes 524320 | tf_op jit(solution)/shard_map/ppermute | solution.py:35
  71.1 1.6 %collective-permute-start.13 = (bf16[64,2048]{1,0:T(8,128)(2,1)S(1)}, bf16[64,2048]{1,0:T(8,128)(2,1)S(1)}, u32[]{:S(2)}, u32[]{:S(2)}) collective-permute-start(bf16[64,2048]{1,0:T(8,128)(2,1)S(1)} %slice.175), channel_id=1, source_target_pairs={{0,2},{1,3},{2,0},{3,1},{4,6},{5,7},{6,4},{7,5},{8,10},{9,11},{10,... | collective-permute-start | bytes 786440 | tf_op jit(solution)/shard_map/ppermute | solution.py:35
  72.7 6.2 %finish_step.4 = (f32[128,2048]{1,0:T(8,128)S(1)}, bf16[128,2048]{1,0:T(8,128)(2,1)S(1)}) custom-call(s32[2]{0:T(128)S(1)} %copy-done.2, bf16[192,2176]{1,0:T(8,128)(2,1)S(1)} %bitcast.64, bf16[192,2176]{1,0:T(8,128)(2,1)S(1)} %collective-permute-done.8.refs_1_, bf16[192,2176]{1,0:T(8,128)(2,1)S(1)} %collective-permute-done.9.refs_2_, ...), custom_call_target="tpu_custom_call" | custom-call | flops 8589934592 | bytes 1 | tf_op jit(solution)/shard_map/finish_step/pallas_call | solution.py:356
  79.6 1.3 %collective-permute-done.14 = bf16[128,2048]{1,0:T(8,128)(2,1)S(1)} collective-permute-done((bf16[128,2048]{1,0:T(8,128)(2,1)S(1)}, bf16[128,2048]{1,0:T(8,128)(2,1)S(1)}, u32[]{:S(2)}, u32[]{:S(2)}) %collective-permute-start.14) | collective-permute-done | bytes 524320 | tf_op jit(solution)/shard_map/ppermute | solution.py:35
  81.7 6.2 %finish_step.5 = (f32[128,2048]{1,0:T(8,128)S(1)}, bf16[128,2048]{1,0:T(8,128)(2,1)S(1)}) custom-call(s32[2]{0:T(128)S(1)} %copy-done.2, bf16[192,2176]{1,0:T(8,128)(2,1)S(1)} %bitcast.65, bf16[192,2176]{1,0:T(8,128)(2,1)S(1)} %collective-permute-done.8.refs_1_, bf16[192,2176]{1,0:T(8,128)(2,1)S(1)} %collective-permute-done.9.refs_2_, ...), custom_call_target="tpu_custom_call" | custom-call | flops 8589934592 | bytes 1 | tf_op jit(solution)/shard_map/finish_step/pallas_call | solution.py:356
  88.0 1.5 %collective-permute-done.20 = bf16[64,2048]{1,0:T(8,128)(2,1)S(1)} collective-permute-done((bf16[64,2048]{1,0:T(8,128)(2,1)S(1)}, bf16[64,2048]{1,0:T(8,128)(2,1)S(1)}, u32[]{:S(2)}, u32[]{:S(2)}) %collective-permute-start.20) | collective-permute-done | bytes 262176 | tf_op jit(solution)/shard_map/ppermute | solution.py:35
  90.2 2.1 %collective-permute-start.16 = (bf16[32,2048]{1,0:T(8,128)(2,1)S(1)}, bf16[32,2048]{1,0:T(8,128)(2,1)S(1)}, u32[]{:S(2)}, u32[]{:S(2)}) collective-permute-start(bf16[32,2048]{1,0:T(8,128)(2,1)S(1)} %bitcast.85), channel_id=1, source_target_pairs={{0,4},{1,5},{2,6},{3,7},{4,0},{5,1},{6,2},{7,3},{8,12},{9,13},{10,... | collective-permute-start | bytes 393224 | tf_op jit(solution)/shard_map/ppermute | solution.py:35
  92.3 1.5 %collective-permute-start.18 = (bf16[64,2048]{1,0:T(8,128)(2,1)S(1)}, bf16[64,2048]{1,0:T(8,128)(2,1)S(1)}, u32[]{:S(2)}, u32[]{:S(2)}) collective-permute-start(bf16[64,2048]{1,0:T(8,128)(2,1)S(1)} %slice.174), channel_id=1, source_target_pairs={{0,2},{1,3},{2,0},{3,1},{4,6},{5,7},{6,4},{7,5},{8,10},{9,11},{10,... | collective-permute-start | bytes 786440 | tf_op jit(solution)/shard_map/ppermute | solution.py:35
  93.8 2.6 %collective-permute-done.21 = bf16[32,2048]{1,0:T(8,128)(2,1)S(1)} collective-permute-done((bf16[32,2048]{1,0:T(8,128)(2,1)S(1)}, bf16[32,2048]{1,0:T(8,128)(2,1)S(1)}, u32[]{:S(2)}, u32[]{:S(2)}) %collective-permute-start.21) | collective-permute-done | bytes 131104 | tf_op jit(solution)/shard_map/ppermute | solution.py:35
  98.5 1.6 %collective-permute-done.18 = bf16[64,2048]{1,0:T(8,128)(2,1)S(1)} collective-permute-done((bf16[64,2048]{1,0:T(8,128)(2,1)S(1)}, bf16[64,2048]{1,0:T(8,128)(2,1)S(1)}, u32[]{:S(2)}, u32[]{:S(2)}) %collective-permute-start.18) | collective-permute-done | bytes 262176 | tf_op jit(solution)/shard_map/ppermute | solution.py:35
  100.6 2.6 %collective-permute-start.17 = (bf16[16,2048]{1,0:T(8,128)(2,1)S(1)}, bf16[16,2048]{1,0:T(8,128)(2,1)S(1)}, u32[]{:S(2)}, u32[]{:S(2)}) collective-permute-start(bf16[16,2048]{1,0:T(8,128)(2,1)S(1)} %fusion.8), channel_id=1, source_target_pairs={{0,8},{1,9},{2,10},{3,11},{4,12},{5,13},{6,14},{7,15},{8,0},{9,1},... | collective-permute-start | bytes 196616 | tf_op jit(solution)/shard_map/ppermute | solution.py:35
  103.2 1.5 %collective-permute-start.24 = (bf16[16,2048]{1,0:T(8,128)(2,1)S(1)}, bf16[16,2048]{1,0:T(8,128)(2,1)S(1)}, u32[]{:S(2)}, u32[]{:S(2)}) collective-permute-start(bf16[16,2048]{1,0:T(8,128)(2,1)S(1)} %get-tuple-element.102), channel_id=1, source_target_pairs={{0,12},{1,13},{2,14},{3,15},{4,8},{5,9},{6,10},{7,11},{8,4},{9,5},... | collective-permute-start | bytes 196616 | tf_op jit(solution)/shard_map/ppermute | solution.py:35
  105.0 3.0 %collective-permute-done.17 = bf16[16,2048]{1,0:T(8,128)(2,1)S(1)} collective-permute-done((bf16[16,2048]{1,0:T(8,128)(2,1)S(1)}, bf16[16,2048]{1,0:T(8,128)(2,1)S(1)}, u32[]{:S(2)}, u32[]{:S(2)}) %collective-permute-start.17) | collective-permute-done | bytes 65568 | tf_op jit(solution)/shard_map/ppermute | solution.py:35
  108.1 1.3 %collective-permute-done.24 = bf16[16,2048]{1,0:T(8,128)(2,1)S(1)} collective-permute-done((bf16[16,2048]{1,0:T(8,128)(2,1)S(1)}, bf16[16,2048]{1,0:T(8,128)(2,1)S(1)}, u32[]{:S(2)}, u32[]{:S(2)}) %collective-permute-start.24) | collective-permute-done | bytes 65568 | tf_op jit(solution)/shard_map/ppermute | solution.py:35
  109.3 2.1 %collective-permute-done.23 = bf16[16,2048]{1,0:T(8,128)(2,1)S(1)} collective-permute-done((bf16[16,2048]{1,0:T(8,128)(2,1)S(1)}, bf16[16,2048]{1,0:T(8,128)(2,1)S(1)}, u32[]{:S(2)}, u32[]{:S(2)}) %collective-permute-start.23) | collective-permute-done | bytes 65568 | tf_op jit(solution)/shard_map/ppermute | solution.py:35
  (62 shorter events, 9.7 us)
Async XLA Ops:
  0.0 48.7 %copy-start = (bf16[1,2048,768]{2,1,0:T(8,128)(2,1)S(1)}, bf16[1,2048,768]{2,1,0:T(8,128)(2,1)}, u32[]{:S(2)}) copy-start(bf16[1,2048,768]{2,1,0:T(8,128)(2,1)} %param.13) | copy-start | bytes 9437188
  2.1 11.8 %collective-permute-start.2 = (bf16[48,2176]{1,0:T(8,128)(2,1)}, bf16[48,2176]{1,0:T(8,128)(2,1)S(1)}, u32[]{:S(2)}, u32[]{:S(2)}) collective-permute-start(bf16[48,2176]{1,0:T(8,128)(2,1)} %payload.1), channel_id=1, source_target_pairs={{0,12},{1,13},{2,14},{3,15},{4,8},{5,9},{6,10},{7,11},{8,4},{9,5},... | collective-permute-start | bytes 626696 | tf_op jit(solution)/shard_map/ppermute | solution.py:35
  7.2 18.1 %collective-permute-start.1 = (bf16[48,2176]{1,0:T(8,128)(2,1)}, bf16[48,2176]{1,0:T(8,128)(2,1)}, u32[]{:S(2)}, u32[]{:S(2)}) collective-permute-start(bf16[48,2176]{1,0:T(8,128)(2,1)} %payload.1), channel_id=1, source_target_pairs={{0,8},{1,9},{2,10},{3,11},{4,12},{5,13},{6,14},{7,15},{8,0},{9,1},... | collective-permute-start | bytes 626696 | tf_op jit(solution)/shard_map/ppermute | solution.py:35
  7.2 18.1 %collective-permute-start = (bf16[48,2176]{1,0:T(8,128)(2,1)}, bf16[48,2176]{1,0:T(8,128)(2,1)}, u32[]{:S(2)}, u32[]{:S(2)}) collective-permute-start(bf16[48,2176]{1,0:T(8,128)(2,1)} %payload.1), channel_id=1, source_target_pairs={{0,4},{1,5},{2,6},{3,7},{4,0},{5,1},{6,2},{7,3},{8,12},{9,13},{10,... | collective-permute-start | bytes 626696 | tf_op jit(solution)/shard_map/ppermute | solution.py:35
  11.2 37.5 %copy-start.1 = (bf16[1,2048,768]{2,1,0:T(8,128)(2,1)S(1)}, bf16[1,2048,768]{2,1,0:T(8,128)(2,1)}, u32[]{:S(2)}) copy-start(bf16[1,2048,768]{2,1,0:T(8,128)(2,1)} %param.14) | copy-start | bytes 9437188
  11.2 15.3 %collective-permute-start.3 = (bf16[4,264,128]{2,1,0:T(8,128)(2,1)}, bf16[4,264,128]{2,1,0:T(8,128)(2,1)S(1)}, u32[]{:S(2)}, u32[]{:S(2)}) collective-permute-start(bf16[4,264,128]{2,1,0:T(8,128)(2,1)} %get-tuple-element.51), channel_id=1, source_target_pairs={{0,2},{1,3},{2,0},{3,1},{4,6},{5,7},{6,4},{7,5},{8,10},{9,11},{10,... | collective-permute-start | bytes 811016 | tf_op jit(solution)/shard_map/ppermute | solution.py:35
  26.6 19.7 %collective-permute-start.8 = (bf16[192,2176]{1,0:T(8,128)(2,1)S(1)}, bf16[192,2176]{1,0:T(8,128)(2,1)S(1)}, u32[]{:S(2)}, u32[]{:S(2)}) collective-permute-start(bf16[192,2176]{1,0:T(8,128)(2,1)S(1)} %bitcast.60), channel_id=1, source_target_pairs={{0,2},{1,3},{2,0},{3,1},{4,6},{5,7},{6,4},{7,5},{8,10},{9,11},{10,... | collective-permute-start | bytes 2506760 | tf_op jit(solution)/shard_map/ppermute | solution.py:35
  28.2 5.1 %collective-permute-start.4 = (bf16[2,264,128]{2,1,0:T(8,128)(2,1)S(1)}, bf16[2,264,128]{2,1,0:T(8,128)(2,1)S(1)}, u32[]{:S(2)}, u32[]{:S(2)}) collective-permute-start(bf16[2,264,128]{2,1,0:T(8,128)(2,1)S(1)} %get-tuple-element.53), channel_id=1, source_target_pairs={{0,0},{1,1},{2,2},{3,3},{4,4},{5,5},{6,6},{7,7},{8,8},{9,9},{10,10... | collective-permute-start | bytes 405512 | tf_op jit(solution)/shard_map/ppermute | solution.py:68
  28.9 6.5 %collective-permute-start.5 = (bf16[2,264,128]{2,1,0:T(8,128)(2,1)S(1)}, bf16[2,264,128]{2,1,0:T(8,128)(2,1)S(1)}, u32[]{:S(2)}, u32[]{:S(2)}) collective-permute-start(bf16[2,264,128]{2,1,0:T(8,128)(2,1)S(1)} %get-tuple-element.54), channel_id=1, source_target_pairs={{0,4},{1,5},{2,6},{3,7},{4,0},{5,1},{6,2},{7,3},{8,12},{9,13},{10,... | collective-permute-start | bytes 405512 | tf_op jit(solution)/shard_map/ppermute | solution.py:68
  28.9 12.6 %collective-permute-start.6 = (bf16[2,264,128]{2,1,0:T(8,128)(2,1)S(1)}, bf16[2,264,128]{2,1,0:T(8,128)(2,1)S(1)}, u32[]{:S(2)}, u32[]{:S(2)}) collective-permute-start(bf16[2,264,128]{2,1,0:T(8,128)(2,1)S(1)} %get-tuple-element.55), channel_id=1, source_target_pairs={{0,8},{1,9},{2,10},{3,11},{4,12},{5,13},{6,14},{7,15},{8,0},{9,1},... | collective-permute-start | bytes 405512 | tf_op jit(solution)/shard_map/ppermute | solution.py:68
  32.0 9.6 %collective-permute-start.7 = (bf16[2,264,128]{2,1,0:T(8,128)(2,1)S(1)}, bf16[2,264,128]{2,1,0:T(8,128)(2,1)S(1)}, u32[]{:S(2)}, u32[]{:S(2)}) collective-permute-start(bf16[2,264,128]{2,1,0:T(8,128)(2,1)S(1)} %get-tuple-element.56), channel_id=1, source_target_pairs={{0,12},{1,13},{2,14},{3,15},{4,8},{5,9},{6,10},{7,11},{8,4},{9,5},... | collective-permute-start | bytes 405512 | tf_op jit(solution)/shard_map/ppermute | solution.py:68
  33.3 14.6 %collective-permute-start.9 = (bf16[192,2176]{1,0:T(8,128)(2,1)S(1)}, bf16[192,2176]{1,0:T(8,128)(2,1)S(1)}, u32[]{:S(2)}, u32[]{:S(2)}) collective-permute-start(bf16[192,2176]{1,0:T(8,128)(2,1)S(1)} %bitcast.61), channel_id=1, source_target_pairs={{0,1},{1,0},{2,3},{3,2},{4,5},{5,4},{6,7},{7,6},{8,9},{9,8},{10,11... | collective-permute-start | bytes 2506760 | tf_op jit(solution)/shard_map/ppermute | solution.py:35
  46.3 2.4 %collective-permute-start.10 = (bf16[192,2176]{1,0:T(8,128)(2,1)S(1)}, bf16[192,2176]{1,0:T(8,128)(2,1)S(1)}, u32[]{:S(2)}, u32[]{:S(2)}) collective-permute-start(bf16[192,2176]{1,0:T(8,128)(2,1)S(1)} %collective-permute-done.8.refs_1_), channel_id=1, source_target_pairs={{0,1},{1,0},{2,3},{3,2},{4,5},{5,4},{6,7},{7,6},{8,9},{9,8},{10,11... | collective-permute-start | bytes 2506760 | tf_op jit(solution)/shard_map/ppermute | solution.py:35
  46.4 14.8 %collective-permute-start.11 = (bf16[4,2,264,128]{3,2,1,0:T(8,128)(2,1)S(1)}, bf16[4,2,264,128]{3,2,1,0:T(8,128)(2,1)S(1)}, u32[]{:S(2)}, u32[]{:S(2)}) collective-permute-start(bf16[4,2,264,128]{3,2,1,0:T(8,128)(2,1)S(1)} %pad_maximum_fusion.1.refs_0_), channel_id=1, source_target_pairs={{0,16},{16,0},{1,17},{17,1},{2,18},{18,2},{3,19},{19,3},{4,20},{20... | collective-permute-start | bytes 1622024 | tf_op jit(solution)/shard_map/ppermute | solution.py:408
  48.7 12.5 %copy-start.2 = (s32[2]{0:T(128)S(1)}, s32[2]{0:T(128)}, u32[]{:S(2)}) copy-start(s32[2]{0:T(128)} %pad_add_fusion.place_ref) | copy-start | bytes 28
  48.7 14.1 %copy-start.3 = (bf16[1,768,2048]{2,1,0:T(8,128)(2,1)S(1)}, bf16[1,768,2048]{2,1,0:T(8,128)(2,1)}, u32[]{:S(2)}) copy-start(bf16[1,768,2048]{2,1,0:T(8,128)(2,1)} %param.15) | copy-start | bytes 9437188
  69.0 2.0 %collective-permute-start.12 = (bf16[128,2048]{1,0:T(8,128)(2,1)S(1)}, bf16[128,2048]{1,0:T(8,128)(2,1)S(1)}, u32[]{:S(2)}, u32[]{:S(2)}) collective-permute-start(bf16[128,2048]{1,0:T(8,128)(2,1)S(1)} %get-tuple-element.74), channel_id=1, source_target_pairs={{0,1},{1,0},{2,3},{3,2},{4,5},{5,4},{6,7},{7,6},{8,9},{9,8},{10,11... | collective-permute-start | bytes 1572872 | tf_op jit(solution)/shard_map/ppermute | solution.py:35
  71.1 8.4 %collective-permute-start.13 = (bf16[64,2048]{1,0:T(8,128)(2,1)S(1)}, bf16[64,2048]{1,0:T(8,128)(2,1)S(1)}, u32[]{:S(2)}, u32[]{:S(2)}) collective-permute-start(bf16[64,2048]{1,0:T(8,128)(2,1)S(1)} %slice.175), channel_id=1, source_target_pairs={{0,2},{1,3},{2,0},{3,1},{4,6},{5,7},{6,4},{7,5},{8,10},{9,11},{10,... | collective-permute-start | bytes 786440 | tf_op jit(solution)/shard_map/ppermute | solution.py:35
  79.0 2.0 %collective-permute-start.14 = (bf16[128,2048]{1,0:T(8,128)(2,1)S(1)}, bf16[128,2048]{1,0:T(8,128)(2,1)S(1)}, u32[]{:S(2)}, u32[]{:S(2)}) collective-permute-start(bf16[128,2048]{1,0:T(8,128)(2,1)S(1)} %get-tuple-element.80), channel_id=1, source_target_pairs={{0,1},{1,0},{2,3},{3,2},{4,5},{5,4},{6,7},{7,6},{8,9},{9,8},{10,11... | collective-permute-start | bytes 1572872 | tf_op jit(solution)/shard_map/ppermute | solution.py:35
  81.1 8.4 %collective-permute-start.20 = (bf16[64,2048]{1,0:T(8,128)(2,1)S(1)}, bf16[64,2048]{1,0:T(8,128)(2,1)S(1)}, u32[]{:S(2)}, u32[]{:S(2)}) collective-permute-start(bf16[64,2048]{1,0:T(8,128)(2,1)S(1)} %slice.173), channel_id=1, source_target_pairs={{0,2},{1,3},{2,0},{3,1},{4,6},{5,7},{6,4},{7,5},{8,10},{9,11},{10,... | collective-permute-start | bytes 786440 | tf_op jit(solution)/shard_map/ppermute | solution.py:35
  87.9 2.0 %collective-permute-start.15 = (bf16[128,2048]{1,0:T(8,128)(2,1)S(1)}, bf16[128,2048]{1,0:T(8,128)(2,1)S(1)}, u32[]{:S(2)}, u32[]{:S(2)}) collective-permute-start(bf16[128,2048]{1,0:T(8,128)(2,1)S(1)} %get-tuple-element.86), channel_id=1, source_target_pairs={{0,1},{1,0},{2,3},{3,2},{4,5},{5,4},{6,7},{7,6},{8,9},{9,8},{10,11... | collective-permute-start | bytes 1572872 | tf_op jit(solution)/shard_map/ppermute | solution.py:35
  90.0 6.4 %collective-permute-start.21 = (bf16[32,2048]{1,0:T(8,128)(2,1)S(1)}, bf16[32,2048]{1,0:T(8,128)(2,1)S(1)}, u32[]{:S(2)}, u32[]{:S(2)}) collective-permute-start(bf16[32,2048]{1,0:T(8,128)(2,1)S(1)} %bitcast.86), channel_id=1, source_target_pairs={{0,4},{1,5},{2,6},{3,7},{4,0},{5,1},{6,2},{7,3},{8,12},{9,13},{10,... | collective-permute-start | bytes 393224 | tf_op jit(solution)/shard_map/ppermute | solution.py:35
  90.2 8.2 %collective-permute-start.16 = (bf16[32,2048]{1,0:T(8,128)(2,1)S(1)}, bf16[32,2048]{1,0:T(8,128)(2,1)S(1)}, u32[]{:S(2)}, u32[]{:S(2)}) collective-permute-start(bf16[32,2048]{1,0:T(8,128)(2,1)S(1)} %bitcast.85), channel_id=1, source_target_pairs={{0,4},{1,5},{2,6},{3,7},{4,0},{5,1},{6,2},{7,3},{8,12},{9,13},{10,... | collective-permute-start | bytes 393224 | tf_op jit(solution)/shard_map/ppermute | solution.py:35
  92.3 7.8 %collective-permute-start.18 = (bf16[64,2048]{1,0:T(8,128)(2,1)S(1)}, bf16[64,2048]{1,0:T(8,128)(2,1)S(1)}, u32[]{:S(2)}, u32[]{:S(2)}) collective-permute-start(bf16[64,2048]{1,0:T(8,128)(2,1)S(1)} %slice.174), channel_id=1, source_target_pairs={{0,2},{1,3},{2,0},{3,1},{4,6},{5,7},{6,4},{7,5},{8,10},{9,11},{10,... | collective-permute-start | bytes 786440 | tf_op jit(solution)/shard_map/ppermute | solution.py:35
  96.5 8.5 %collective-permute-start.22 = (bf16[16,2048]{1,0:T(8,128)(2,1)S(1)}, bf16[16,2048]{1,0:T(8,128)(2,1)S(1)}, u32[]{:S(2)}, u32[]{:S(2)}) collective-permute-start(bf16[16,2048]{1,0:T(8,128)(2,1)S(1)} %fusion.10), channel_id=1, source_target_pairs={{0,8},{1,9},{2,10},{3,11},{4,12},{5,13},{6,14},{7,15},{8,0},{9,1},... | collective-permute-start | bytes 196616 | tf_op jit(solution)/shard_map/ppermute | solution.py:35
  100.2 4.8 %collective-permute-start.19 = (bf16[16,2048]{1,0:T(8,128)(2,1)S(1)}, bf16[16,2048]{1,0:T(8,128)(2,1)S(1)}, u32[]{:S(2)}, u32[]{:S(2)}) collective-permute-start(bf16[16,2048]{1,0:T(8,128)(2,1)S(1)} %get-tuple-element.101), channel_id=1, source_target_pairs={{0,4},{1,5},{2,6},{3,7},{4,0},{5,1},{6,2},{7,3},{8,12},{9,13},{10,... | collective-permute-start | bytes 196616 | tf_op jit(solution)/shard_map/ppermute | solution.py:35
  100.6 7.4 %collective-permute-start.17 = (bf16[16,2048]{1,0:T(8,128)(2,1)S(1)}, bf16[16,2048]{1,0:T(8,128)(2,1)S(1)}, u32[]{:S(2)}, u32[]{:S(2)}) collective-permute-start(bf16[16,2048]{1,0:T(8,128)(2,1)S(1)} %fusion.8), channel_id=1, source_target_pairs={{0,8},{1,9},{2,10},{3,11},{4,12},{5,13},{6,14},{7,15},{8,0},{9,1},... | collective-permute-start | bytes 196616 | tf_op jit(solution)/shard_map/ppermute | solution.py:35
  103.2 6.2 %collective-permute-start.24 = (bf16[16,2048]{1,0:T(8,128)(2,1)S(1)}, bf16[16,2048]{1,0:T(8,128)(2,1)S(1)}, u32[]{:S(2)}, u32[]{:S(2)}) collective-permute-start(bf16[16,2048]{1,0:T(8,128)(2,1)S(1)} %get-tuple-element.102), channel_id=1, source_target_pairs={{0,12},{1,13},{2,14},{3,15},{4,8},{5,9},{6,10},{7,11},{8,4},{9,5},... | collective-permute-start | bytes 196616 | tf_op jit(solution)/shard_map/ppermute | solution.py:35
  104.7 6.8 %collective-permute-start.23 = (bf16[16,2048]{1,0:T(8,128)(2,1)S(1)}, bf16[16,2048]{1,0:T(8,128)(2,1)S(1)}, u32[]{:S(2)}, u32[]{:S(2)}) collective-permute-start(bf16[16,2048]{1,0:T(8,128)(2,1)S(1)} %get-tuple-element.103), channel_id=1, source_target_pairs={{0,8},{1,9},{2,10},{3,11},{4,12},{5,13},{6,14},{7,15},{8,0},{9,1},... | collective-permute-start | bytes 196616 | tf_op jit(solution)/shard_map/ppermute | solution.py:35

commit v18 on v17

--- a/solution.py
+++ b/solution.py
@@ -10,7 +10,7 @@
 adapter_scale = 2.0
 LANES = 128
 GRANT = 16 << 20
-EXPERT_GRANT = 32 << 20
+EXPERT_GRANT = 30 << 20
 WHOLE_GRANT = 60 << 20
 MUCH = pl.CostEstimate(flops=1 << 33, bytes_accessed=1, transcendentals=0)
 LITTLE = pl.CostEstimate(flops=1, bytes_accessed=1, transcendentals=0)
@@ -44,8 +44,7 @@
     return sum([part.astype(jnp.float32) for part in received], total[:count])
 
 
-def halve_along(total, n, stride, size, last):
-    count = total.shape[0] // size
+def halve_along(total, n, stride, size, count, last):
     step = 1
     while step < size:
         total = total.reshape(-1, 2, count, total.shape[1])
@@ -300,82 +299,54 @@
 
 def finish_kernel(count, first, rows, place_ref, *refs):
     pieces, refs = refs[:count], refs[count:]
-    gate_hbm, up_hbm, a_gu_hbm, gate_b_hbm, up_b_hbm, down_a_hbm, down_b_hbm = refs[:7]
-    w_down_hbm, kept_hbm, sent_hbm, x_ref, gate_ref, up_ref = refs[7:13]
-    a_gu_ref, gate_b_ref, up_b_ref, down_a_ref, down_b_ref, w_down_ref = refs[13:19]
-    inner_ref, kept_ref, sent_ref, sem, out_sem = refs[19:]
+    gate_ref, up_ref, a_gu_ref, gate_b_ref, up_b_ref, down_a_ref, down_b_ref = refs[:7]
+    w_down_ref, kept_ref, sent_ref, x_ref, inner_ref = refs[7:]
+    width = w_down_ref.shape[1]
+    rank = gate_b_ref.shape[0]
     span = pieces[0].shape[0]
-    units, width = w_down_ref.shape
-    rank = gate_b_ref.shape[0]
     own = kept_ref.shape[0]
-    loads = Loads(sem)
-    x_in, base_in = [], []
     for i, piece in enumerate(pieces):
-        x_in += loads.begin(piece.at[pl.ds(first, rows)], x_ref.at[pl.ds(i * rows, rows)])
-    x_in += loads.begin(a_gu_hbm, a_gu_ref)
-    x_in += loads.begin(gate_b_hbm, gate_b_ref) + loads.begin(up_b_hbm, up_b_ref)
-    for i in range(count):
-        src, dst = pl.ds(i * span + first, rows), pl.ds(i * rows, rows)
-        base_in += loads.begin(gate_hbm.at[src], gate_ref.at[dst])
-        base_in += loads.begin(up_hbm.at[src], up_ref.at[dst])
-    down_in = loads.begin(down_a_hbm, down_a_ref) + loads.begin(down_b_hbm, down_b_ref)
-    down_in += loads.begin_rows(w_down_hbm, w_down_ref)
-    wait(x_in)
+        x_ref[i * rows : (i + 1) * rows, :] = piece[first : first + rows, :]
+
+    def of_step(ref):
+        starts = [i * span + first for i in range(count)]
+        return jnp.concatenate([ref[at : at + rows, :] for at in starts])
+
     low = (adapter_scale * dot(x_ref[:, :width], a_gu_ref[...])).astype(jnp.bfloat16)
     gates = x_ref[:, width:].astype(jnp.float32)
     lane = lax.broadcasted_iota(jnp.int32, gates.shape, 1)
     mine = jnp.sum(jnp.where(lane == place_ref[1], gates, 0.0), axis=1, keepdims=True)
-    wait(base_in)
-    g = gate_ref[...] + dot(low[:, :rank], gate_b_ref[...])
-    u = up_ref[...] + dot(low[:, rank:], up_b_ref[...])
+    g = of_step(gate_ref) + dot(low[:, :rank], gate_b_ref[...])
+    u = of_step(up_ref) + dot(low[:, rank:], up_b_ref[...])
     half = 0.5 * g
     inner_ref[...] = ((half + half * jnp.tanh(half)) * u).astype(jnp.bfloat16)
-    wait(down_in)
     low = (adapter_scale * dot(inner_ref[...], down_a_ref[...])).astype(jnp.bfloat16)[:, :rank]
     out = (dot(inner_ref[...], w_down_ref[...]) + dot(low, down_b_ref[...])) * mine
+    kept_ref[...] = out[:own]
     sent_ref[...] = out[own:].astype(jnp.bfloat16)
-    sent_out = pltpu.make_async_copy(sent_ref, sent_hbm, out_sem.at[0])
-    sent_out.start()
-    kept_ref[...] = out[:own]
-    kept_out = pltpu.make_async_copy(kept_ref, kept_hbm, out_sem.at[1])
-    kept_out.start()
-    wait([sent_out, kept_out])
 
 
 def finish_step(place, pieces, base, first, rows, low_rank, w_down):
     units, width = w_down.shape
     total = rows * len(pieces)
     own = total // 2
-    a_gu, gate_b, up_b, down_a, down_b = low_rank
-    rank = down_b.shape[0]
-    outs = [
-        jax.ShapeDtypeStruct((own, width), jnp.float32),
-        jax.ShapeDtypeStruct((own, width), jnp.bfloat16),
-    ]
-    held = [*low_rank, w_down]
+    operands = [*pieces, *base, *low_rank, w_down]
     return pl.pallas_call(
         functools.partial(finish_kernel, len(pieces), first, rows),
-        out_shape=outs,
+        out_shape=[
+            jax.ShapeDtypeStruct((own, width), jnp.float32),
+            jax.ShapeDtypeStruct((own, width), jnp.bfloat16),
+        ],
         in_specs=[pl.BlockSpec(memory_space=pltpu.SMEM)]
-        + [pl.BlockSpec(memory_space=pl.ANY)] * (len(pieces) + 2 + len(low_rank))
-        + [pl.BlockSpec(memory_space=pltpu.HBM)],
-        out_specs=[pl.BlockSpec(memory_space=pl.ANY)] * 2,
+        + [pl.BlockSpec(memory_space=pltpu.VMEM)] * len(operands),
         scratch_shapes=[
             pltpu.VMEM((total, pieces[0].shape[1]), jnp.bfloat16),
-            pltpu.VMEM((total, units), jnp.float32),
-            pltpu.VMEM((total, units), jnp.float32),
-        ]
-        + [pltpu.VMEM(a.shape, a.dtype) for a in held]
-        + [pltpu.VMEM((total, units), jnp.bfloat16)]
-        + [pltpu.VMEM(o.shape, o.dtype) for o in outs]
-        + [
-            pltpu.SemaphoreType.DMA((3 * len(pieces) + 9,)),
-            pltpu.SemaphoreType.DMA((2,)),
+            pltpu.VMEM((total, units), jnp.bfloat16),
         ],
         compiler_params=pltpu.CompilerParams(vmem_limit_bytes=EXPERT_GRANT),
         cost_estimate=MUCH,
         name="finish_step",
-    )(place, *pieces, *base, *held)
+    )(place, *operands)
 
 
 def dense_shards(
@@ -422,13 +393,15 @@
         kept, sent = finish_step(
             place, pieces, base, s * span, span, low_rank, down_weight[0]
         )
+        if s >= 1:
+            kept = after(kept, across[s - 1])
         summed.append(kept + swap(sent, owners, 1, 1).astype(jnp.float32))
         across.append(scatter_along(summed[s], owners, *along_middle))
     across[:-1] = [after(total, summed[-1]) for total in across[:-1]]
     ends = []
     final = scatter_along(across[-1], owners, *along_outer, ends)
-    results = [halve_along(total, owners, *along_outer, ends[0]) for total in across[:-1]]
-    return jnp.stack(results + [final]).astype(jnp.bfloat16)
+    others = halve_along(jnp.concatenate(across[:-1]), owners, *along_outer, rows, ends[0])
+    return jnp.concatenate([others, final]).astype(jnp.bfloat16).reshape(hidden.shape)
 
 
 def row_capacity(rows, top, experts):

time: 112 us -> 106 us (0.946)
  Pallas kernels: 34.6 us -> 23.8 us
  waiting for transfers between devices: 45.5 us -> 51.6 us
  starting transfers between devices: 27.3 us -> 25.2 us
    pallas_call x3, Pallas kernels: 18.7 us -> 7.99 us  [finish_step(): pl.pallas_call(functools.partial(finish_kernel, len(pieces), first, rows)...]
    ppermute x20 -> x18, waiting for transfers between devices: 34.1 us -> 40.2 us  [swap(): return lax.ppermute(x, 'expert', [(i, i ^ k * stride) for i in range(n)])]
    ppermute x20 -> x18, starting transfers between devices: 20.6 us -> 18.5 us  [swap(): return lax.ppermute(x, 'expert', [(i, i ^ k * stride) for i in range(n)])]
  transfers between devices with their start and end apart: 25 -> 23, of which waited for: 17 -> 13; matrix products, arithmetic and copies ran while one was open for 3% -> 3% of each run, Pallas kernels for 22% -> 17%
where the time goes in v18:
time: 106 us; the launch traced here: 105 us
  waiting for transfers between devices  51.6 us (49%)
  starting transfers between devices  25.2 us (24%)
  Pallas kernels  23.8 us (22%)
  other arithmetic  3.34 us (3%)
  local copies, waits for them, and re-layouts  1.25 us (1%)
    ppermute x18, waiting for transfers between devices, swap(): return lax.ppermute(x, 'expert', [(i, i ^ k * stride) for i in range(n)])  40.2 us
    ppermute x18, starting transfers between devices, swap(): return lax.ppermute(x, 'expert', [(i, i ^ k * stride) for i in range(n)])  18.5 us
    pallas_call x1, Pallas kernels, base_products(): pl.pallas_call(functools.partial(base_kernel, len(pieces)), out_shape=[ou...  9.3 us
    ppermute x4, waiting for transfers between devices, exchange_factors(): here.append(lax.ppermute(block, ('group', 'expert'), pairs))  8.23 us
    pallas_call x3, Pallas kernels, finish_step(): pl.pallas_call(functools.partial(finish_kernel, len(pieces), first, rows)...  7.99 us
    ppermute x4, starting transfers between devices, exchange_factors(): here.append(lax.ppermute(block, ('group', 'expert'), pairs))  5.1 us
    ppermute x1, waiting for transfers between devices, dense_shards(): there = lax.ppermute(here, 'group', [(0, 1), (1, 0)])  3.15 us
    pallas_call x1, Pallas kernels, order_factors(): pl.pallas_call(order_kernel, out_shape=[jax.ShapeDtypeStruct((outer, leng...  2.79 us
  transfers between devices with their start and end apart: 23, of which 13 were waited for; matrix products, arithmetic and copies ran while one was open for 3% of the time, Pallas kernels for 17%

profile of v18, /device:TPU:0, one launch (start us, length us, event | category | flops | bytes accessed | tf_op | source)
XLA Modules:
  0.0 105.5 jit_solution(6168577722451654389)
XLA Ops:
  0.0 2.1 %payload.1 = bf16[48,2176]{1,0:T(8,128)(2,1)} custom-call(bf16[3,16,2048]{2,1,0:T(8,128)(2,1)} %hidden_ref.1, s32[3,8,16]{2,1,0:T(8,128)} %bitcast.60, f32[3,8,16]{2,1,0:T(8,128)} %bitcast.61), custom_call_target="tpu_custom_call" | custom-call | flops 1 | bytes 1 | tf_op jit(solution)/shard_map/payload/pallas_call | solution.py:97
  2.1 5.0 %collective-permute-start.2 = (bf16[48,2176]{1,0:T(8,128)(2,1)}, bf16[48,2176]{1,0:T(8,128)(2,1)S(1)}, u32[]{:S(2)}, u32[]{:S(2)}) collective-permute-start(bf16[48,2176]{1,0:T(8,128)(2,1)} %payload.1), channel_id=1, source_target_pairs={{0,12},{1,13},{2,14},{3,15},{4,8},{5,9},{6,10},{7,11},{8,4},{9,5},... | collective-permute-start | bytes 626696 | tf_op jit(solution)/shard_map/ppermute | solution.py:35
  8.3 2.8 %order_factors.1 = (bf16[4,264,128]{2,1,0:T(8,128)(2,1)}, bf16[4,264,128]{2,1,0:T(8,128)(2,1)}) custom-call(s32[2]{0:T(128)} %pad_add_fusion.place_ref, s32[16]{0:T(128)} %placement_ref.1, bf16[16,33792]{1,0:T(8,128)(2,1)} %factors_ref), custom_call_target="tpu_custom_call" | custom-call | flops 1 | bytes 1 | tf_op jit(solution)/shard_map/order_factors/pallas_call | solution.py:132
  11.1 1.7 %collective-permute-start.3 = (bf16[4,264,128]{2,1,0:T(8,128)(2,1)}, bf16[4,264,128]{2,1,0:T(8,128)(2,1)S(1)}, u32[]{:S(2)}, u32[]{:S(2)}) collective-permute-start(bf16[4,264,128]{2,1,0:T(8,128)(2,1)} %get-tuple-element.52), channel_id=1, source_target_pairs={{0,2},{1,3},{2,0},{3,1},{4,6},{5,7},{6,4},{7,5},{8,10},{9,11},{10,... | collective-permute-start | bytes 811016 | tf_op jit(solution)/shard_map/ppermute | solution.py:35
  12.9 1.0 fusion.5
  13.9 4.3 %collective-permute-done = bf16[48,2176]{1,0:T(8,128)(2,1)} collective-permute-done((bf16[48,2176]{1,0:T(8,128)(2,1)}, bf16[48,2176]{1,0:T(8,128)(2,1)}, u32[]{:S(2)}, u32[]{:S(2)}) %collective-permute-start) | collective-permute-done | bytes 208928 | tf_op jit(solution)/shard_map/ppermute | solution.py:35
  18.2 7.0 %collective-permute-done.1 = bf16[48,2176]{1,0:T(8,128)(2,1)} collective-permute-done((bf16[48,2176]{1,0:T(8,128)(2,1)}, bf16[48,2176]{1,0:T(8,128)(2,1)}, u32[]{:S(2)}, u32[]{:S(2)}) %collective-permute-start.1) | collective-permute-done | bytes 208928 | tf_op jit(solution)/shard_map/ppermute | solution.py:35
  25.2 1.3 %pad_maximum_fusion.1 = bf16[3,4,16,2176]{3,2,1,0:T(8,128)(2,1)S(1)} fusion(bf16[3,1,16,2176]{3,2,1,0:T(8,128)(2,1)S(1)} %bitcast.54, bf16[3,1,16,2176]{3,2,1,0:T(8,128)(2,1)} %bitcast.9, bf16[3,1,16,2176]{3,2,1,0:T(8,128)(2,1)} %bitcast.7, bf16[3,1,16,2176]{3,2,1,0:T(8,128)(2,1)} %bitcast.52), kind=kLoop, calls=%fused_computation.4 | loop fusion | flops 1253376 | bytes 1671168 | tf_op jit(solution)/shard_map/stack | solution.py:370
  26.6 1.6 %collective-permute-start.8 = (bf16[192,2176]{1,0:T(8,128)(2,1)S(1)}, bf16[192,2176]{1,0:T(8,128)(2,1)S(1)}, u32[]{:S(2)}, u32[]{:S(2)}) collective-permute-start(bf16[192,2176]{1,0:T(8,128)(2,1)S(1)} %bitcast.37), channel_id=1, source_target_pairs={{0,2},{1,3},{2,0},{3,1},{4,6},{5,7},{6,4},{7,5},{8,10},{9,11},{10,... | collective-permute-start | bytes 2506760 | tf_op jit(solution)/shard_map/ppermute | solution.py:35
  28.9 3.0 %collective-permute-start.6 = (bf16[2,264,128]{2,1,0:T(8,128)(2,1)S(1)}, bf16[2,264,128]{2,1,0:T(8,128)(2,1)S(1)}, u32[]{:S(2)}, u32[]{:S(2)}) collective-permute-start(bf16[2,264,128]{2,1,0:T(8,128)(2,1)S(1)} %get-tuple-element.56), channel_id=1, source_target_pairs={{0,8},{1,9},{2,10},{3,11},{4,12},{5,13},{6,14},{7,15},{8,0},{9,1},... | collective-permute-start | bytes 405512 | tf_op jit(solution)/shard_map/ppermute | solution.py:67
  32.0 1.3 %collective-permute-start.7 = (bf16[2,264,128]{2,1,0:T(8,128)(2,1)S(1)}, bf16[2,264,128]{2,1,0:T(8,128)(2,1)S(1)}, u32[]{:S(2)}, u32[]{:S(2)}) collective-permute-start(bf16[2,264,128]{2,1,0:T(8,128)(2,1)S(1)} %get-tuple-element.57), channel_id=1, source_target_pairs={{0,12},{1,13},{2,14},{3,15},{4,8},{5,9},{6,10},{7,11},{8,4},{9,5},... | collective-permute-start | bytes 405512 | tf_op jit(solution)/shard_map/ppermute | solution.py:67
  33.3 2.0 %collective-permute-done.5 = bf16[2,264,128]{2,1,0:T(8,128)(2,1)S(1)} collective-permute-done((bf16[2,264,128]{2,1,0:T(8,128)(2,1)S(1)}, bf16[2,264,128]{2,1,0:T(8,128)(2,1)S(1)}, u32[]{:S(2)}, u32[]{:S(2)}) %collective-permute-start.5) | collective-permute-done | bytes 135200 | tf_op jit(solution)/shard_map/ppermute | solution.py:67
  35.3 6.2 %collective-permute-done.6 = bf16[2,264,128]{2,1,0:T(8,128)(2,1)S(1)} collective-permute-done((bf16[2,264,128]{2,1,0:T(8,128)(2,1)S(1)}, bf16[2,264,128]{2,1,0:T(8,128)(2,1)S(1)}, u32[]{:S(2)}, u32[]{:S(2)}) %collective-permute-start.6) | collective-permute-done | bytes 135200 | tf_op jit(solution)/shard_map/ppermute | solution.py:67
  41.5 4.8 %collective-permute-done.8.refs_1_ = bf16[192,2176]{1,0:T(8,128)(2,1)S(1)} collective-permute-done((bf16[192,2176]{1,0:T(8,128)(2,1)S(1)}, bf16[192,2176]{1,0:T(8,128)(2,1)S(1)}, u32[]{:S(2)}, u32[]{:S(2)}) %collective-permute-start.8) | collective-permute-done | bytes 835616 | tf_op jit(solution)/shard_map/ppermute | solution.py:35
  46.4 1.6 %collective-permute-start.11 = (bf16[4,2,264,128]{3,2,1,0:T(8,128)(2,1)S(1)}, bf16[4,2,264,128]{3,2,1,0:T(8,128)(2,1)S(1)}, u32[]{:S(2)}, u32[]{:S(2)}) collective-permute-start(bf16[4,2,264,128]{3,2,1,0:T(8,128)(2,1)S(1)} %pad_maximum_fusion.2.refs_0_), channel_id=1, source_target_pairs={{0,16},{16,0},{1,17},{17,1},{2,18},{18,2},{3,19},{19,3},{4,20},{20... | collective-permute-start | bytes 1622024 | tf_op jit(solution)/shard_map/ppermute | solution.py:379
  48.7 9.3 %base_products.1 = (f32[768,768]{1,0:T(8,128)S(1)}, f32[768,768]{1,0:T(8,128)S(1)}) custom-call(bf16[192,2176]{1,0:T(8,128)(2,1)S(1)} %bitcast.39, bf16[192,2176]{1,0:T(8,128)(2,1)S(1)} %collective-permute-done.8.refs_1_, bf16[192,2176]{1,0:T(8,128)(2,1)S(1)} %collective-permute-done.9.refs_2_, bf16[192,2176]{1,0:T(8,128)(2,1)S(1)} %collective-permute-done.10.refs_3_, ...), custom_call_target="tpu_custom_call" | custom-call | flops 1 | bytes 1 | tf_op jit(solution)/shard_map/base_products/pallas_call | solution.py:279
  58.0 3.1 %collective-permute-done.11.refs_1_ = bf16[4,2,264,128]{3,2,1,0:T(8,128)(2,1)S(1)} collective-permute-done((bf16[4,2,264,128]{3,2,1,0:T(8,128)(2,1)S(1)}, bf16[4,2,264,128]{3,2,1,0:T(8,128)(2,1)S(1)}, u32[]{:S(2)}, u32[]{:S(2)}) %collective-permute-start.11) | collective-permute-done | bytes 540704 | tf_op jit(solution)/shard_map/ppermute | solution.py:379
  61.2 1.6 %relayout_factors.1 = (bf16[2048,128]{1,0:T(8,128)(2,1)S(1)}, bf16[64,768]{1,0:T(8,128)(2,1)S(1)}, bf16[64,768]{1,0:T(8,128)(2,1)S(1)}, bf16[768,128]{1,0:T(8,128)(2,1)S(1)}, bf16[64,2048]{1,0:T(8,128)(2,1)S(1)}) custom-call(s32[2]{0:T(128)S(1)} %copy-done.2, bf16[4,2,264,128]{3,2,1,0:T(8,128)(2,1)S(1)} %pad_maximum_fusion.2.refs_0_, ...), custom_call_target="tpu_custom_call" | custom-call | flops 1 | bytes 1 | tf_op jit(solution)/shard_map/relayout_factors/pallas_call | solution.py:204
  62.7 2.7 %finish_step.3 = (f32[128,2048]{1,0:T(8,128)S(1)}, bf16[128,2048]{1,0:T(8,128)(2,1)S(1)}) custom-call(s32[2]{0:T(128)S(1)} %copy-done.2, bf16[192,2176]{1,0:T(8,128)(2,1)S(1)} %bitcast.40, bf16[192,2176]{1,0:T(8,128)(2,1)S(1)} %collective-permute-done.8.refs_1_, bf16[192,2176]{1,0:T(8,128)(2,1)S(1)} %collective-permute-done.9.refs_2_, ...), custom_call_target="tpu_custom_call" | custom-call | flops 8589934592 | bytes 1 | tf_op jit(solution)/shard_map/finish_step/pallas_call | solution.py:334
  65.5 1.9 %collective-permute-done.12 = bf16[128,2048]{1,0:T(8,128)(2,1)S(1)} collective-permute-done((bf16[128,2048]{1,0:T(8,128)(2,1)S(1)}, bf16[128,2048]{1,0:T(8,128)(2,1)S(1)}, u32[]{:S(2)}, u32[]{:S(2)}) %collective-permute-start.12) | collective-permute-done | bytes 524320 | tf_op jit(solution)/shard_map/ppermute | solution.py:35
  67.5 1.6 %collective-permute-start.13 = (bf16[64,2048]{1,0:T(8,128)(2,1)S(1)}, bf16[64,2048]{1,0:T(8,128)(2,1)S(1)}, u32[]{:S(2)}, u32[]{:S(2)}) collective-permute-start(bf16[64,2048]{1,0:T(8,128)(2,1)S(1)} %slice.131), channel_id=1, source_target_pairs={{0,2},{1,3},{2,0},{3,1},{4,6},{5,7},{6,4},{7,5},{8,10},{9,11},{10,... | collective-permute-start | bytes 786440 | tf_op jit(solution)/shard_map/ppermute | solution.py:35
  69.1 2.7 %finish_step.4 = (f32[128,2048]{1,0:T(8,128)S(1)}, bf16[128,2048]{1,0:T(8,128)(2,1)S(1)}) custom-call(s32[2]{0:T(128)S(1)} %copy-done.2, bf16[192,2176]{1,0:T(8,128)(2,1)S(1)} %bitcast.41, bf16[192,2176]{1,0:T(8,128)(2,1)S(1)} %collective-permute-done.8.refs_1_, bf16[192,2176]{1,0:T(8,128)(2,1)S(1)} %collective-permute-done.9.refs_2_, ...), custom_call_target="tpu_custom_call" | custom-call | flops 8589934592 | bytes 1 | tf_op jit(solution)/shard_map/finish_step/pallas_call | solution.py:334
  71.9 4.1 %collective-permute-done.13 = bf16[64,2048]{1,0:T(8,128)(2,1)S(1)} collective-permute-done((bf16[64,2048]{1,0:T(8,128)(2,1)S(1)}, bf16[64,2048]{1,0:T(8,128)(2,1)S(1)}, u32[]{:S(2)}, u32[]{:S(2)}) %collective-permute-start.13) | collective-permute-done | bytes 262176 | tf_op jit(solution)/shard_map/ppermute | solution.py:35
  76.2 1.6 %collective-permute-start.15 = (bf16[64,2048]{1,0:T(8,128)(2,1)S(1)}, bf16[64,2048]{1,0:T(8,128)(2,1)S(1)}, u32[]{:S(2)}, u32[]{:S(2)}) collective-permute-start(bf16[64,2048]{1,0:T(8,128)(2,1)S(1)} %slice.130), channel_id=1, source_target_pairs={{0,2},{1,3},{2,0},{3,1},{4,6},{5,7},{6,4},{7,5},{8,10},{9,11},{10,... | collective-permute-start | bytes 786440 | tf_op jit(solution)/shard_map/ppermute | solution.py:35
  77.8 2.7 %finish_step.5 = (f32[128,2048]{1,0:T(8,128)S(1)}, bf16[128,2048]{1,0:T(8,128)(2,1)S(1)}) custom-call(s32[2]{0:T(128)S(1)} %copy-done.2, bf16[192,2176]{1,0:T(8,128)(2,1)S(1)} %bitcast.42, bf16[192,2176]{1,0:T(8,128)(2,1)S(1)} %collective-permute-done.8.refs_1_, bf16[192,2176]{1,0:T(8,128)(2,1)S(1)} %collective-permute-done.9.refs_2_, ...), custom_call_target="tpu_custom_call" | custom-call | flops 8589934592 | bytes 1 | tf_op jit(solution)/shard_map/finish_step/pallas_call | solution.py:334
  80.5 3.3 %collective-permute-done.15 = bf16[64,2048]{1,0:T(8,128)(2,1)S(1)} collective-permute-done((bf16[64,2048]{1,0:T(8,128)(2,1)S(1)}, bf16[64,2048]{1,0:T(8,128)(2,1)S(1)}, u32[]{:S(2)}, u32[]{:S(2)}) %collective-permute-start.15) | collective-permute-done | bytes 262176 | tf_op jit(solution)/shard_map/ppermute | solution.py:35
  84.0 1.6 %collective-permute-start.19 = (bf16[64,2048]{1,0:T(8,128)(2,1)S(1)}, bf16[64,2048]{1,0:T(8,128)(2,1)S(1)}, u32[]{:S(2)}, u32[]{:S(2)}) collective-permute-start(bf16[64,2048]{1,0:T(8,128)(2,1)S(1)} %slice.128), channel_id=1, source_target_pairs={{0,2},{1,3},{2,0},{3,1},{4,6},{5,7},{6,4},{7,5},{8,10},{9,11},{10,... | collective-permute-start | bytes 786440 | tf_op jit(solution)/shard_map/ppermute | solution.py:35
  85.8 5.1 %collective-permute-done.19 = bf16[64,2048]{1,0:T(8,128)(2,1)S(1)} collective-permute-done((bf16[64,2048]{1,0:T(8,128)(2,1)S(1)}, bf16[64,2048]{1,0:T(8,128)(2,1)S(1)}, u32[]{:S(2)}, u32[]{:S(2)}) %collective-permute-start.19) | collective-permute-done | bytes 262176 | tf_op jit(solution)/shard_map/ppermute | solution.py:35
  91.1 2.8 %collective-permute-start.21 = (bf16[16,2048]{1,0:T(8,128)(2,1)S(1)}, bf16[16,2048]{1,0:T(8,128)(2,1)S(1)}, u32[]{:S(2)}, u32[]{:S(2)}) collective-permute-start(bf16[16,2048]{1,0:T(8,128)(2,1)S(1)} %get-tuple-element.105), channel_id=1, source_target_pairs={{0,8},{1,9},{2,10},{3,11},{4,12},{5,13},{6,14},{7,15},{8,0},{9,1},... | collective-permute-start | bytes 196616 | tf_op jit(solution)/shard_map/ppermute | solution.py:35
  94.0 1.5 %collective-permute-start.22 = (bf16[16,2048]{1,0:T(8,128)(2,1)S(1)}, bf16[16,2048]{1,0:T(8,128)(2,1)S(1)}, u32[]{:S(2)}, u32[]{:S(2)}) collective-permute-start(bf16[16,2048]{1,0:T(8,128)(2,1)S(1)} %get-tuple-element.104), channel_id=1, source_target_pairs={{0,12},{1,13},{2,14},{3,15},{4,8},{5,9},{6,10},{7,11},{8,4},{9,5},... | collective-permute-start | bytes 196616 | tf_op jit(solution)/shard_map/ppermute | solution.py:35
  95.7 6.0 %collective-permute-done.21 = bf16[16,2048]{1,0:T(8,128)(2,1)S(1)} collective-permute-done((bf16[16,2048]{1,0:T(8,128)(2,1)S(1)}, bf16[16,2048]{1,0:T(8,128)(2,1)S(1)}, u32[]{:S(2)}, u32[]{:S(2)}) %collective-permute-start.21) | collective-permute-done | bytes 65568 | tf_op jit(solution)/shard_map/ppermute | solution.py:35
  101.8 2.9 %collective-permute-done.18 = bf16[32,2048]{1,0:T(8,128)(2,1)S(1)} collective-permute-done((bf16[32,2048]{1,0:T(8,128)(2,1)S(1)}, bf16[32,2048]{1,0:T(8,128)(2,1)S(1)}, u32[]{:S(2)}, u32[]{:S(2)}) %collective-permute-start.18) | collective-permute-done | bytes 131104 | tf_op jit(solution)/shard_map/ppermute | solution.py:35
  (56 shorter events, 4.8 us)
Async XLA Ops:
  0.0 48.7 %copy-start = (bf16[1,2048,768]{2,1,0:T(8,128)(2,1)S(1)}, bf16[1,2048,768]{2,1,0:T(8,128)(2,1)}, u32[]{:S(2)}) copy-start(bf16[1,2048,768]{2,1,0:T(8,128)(2,1)} %param.13) | copy-start | bytes 9437188
  2.1 11.7 %collective-permute-start.2 = (bf16[48,2176]{1,0:T(8,128)(2,1)}, bf16[48,2176]{1,0:T(8,128)(2,1)S(1)}, u32[]{:S(2)}, u32[]{:S(2)}) collective-permute-start(bf16[48,2176]{1,0:T(8,128)(2,1)} %payload.1), channel_id=1, source_target_pairs={{0,12},{1,13},{2,14},{3,15},{4,8},{5,9},{6,10},{7,11},{8,4},{9,5},... | collective-permute-start | bytes 626696 | tf_op jit(solution)/shard_map/ppermute | solution.py:35
  7.2 11.0 %collective-permute-start = (bf16[48,2176]{1,0:T(8,128)(2,1)}, bf16[48,2176]{1,0:T(8,128)(2,1)}, u32[]{:S(2)}, u32[]{:S(2)}) collective-permute-start(bf16[48,2176]{1,0:T(8,128)(2,1)} %payload.1), channel_id=1, source_target_pairs={{0,4},{1,5},{2,6},{3,7},{4,0},{5,1},{6,2},{7,3},{8,12},{9,13},{10,... | collective-permute-start | bytes 626696 | tf_op jit(solution)/shard_map/ppermute | solution.py:35
  7.2 18.1 %collective-permute-start.1 = (bf16[48,2176]{1,0:T(8,128)(2,1)}, bf16[48,2176]{1,0:T(8,128)(2,1)}, u32[]{:S(2)}, u32[]{:S(2)}) collective-permute-start(bf16[48,2176]{1,0:T(8,128)(2,1)} %payload.1), channel_id=1, source_target_pairs={{0,8},{1,9},{2,10},{3,11},{4,12},{5,13},{6,14},{7,15},{8,0},{9,1},... | collective-permute-start | bytes 626696 | tf_op jit(solution)/shard_map/ppermute | solution.py:35
  11.1 37.6 %copy-start.1 = (bf16[1,2048,768]{2,1,0:T(8,128)(2,1)S(1)}, bf16[1,2048,768]{2,1,0:T(8,128)(2,1)}, u32[]{:S(2)}) copy-start(bf16[1,2048,768]{2,1,0:T(8,128)(2,1)} %param.14) | copy-start | bytes 9437188
  11.1 15.4 %collective-permute-start.3 = (bf16[4,264,128]{2,1,0:T(8,128)(2,1)}, bf16[4,264,128]{2,1,0:T(8,128)(2,1)S(1)}, u32[]{:S(2)}, u32[]{:S(2)}) collective-permute-start(bf16[4,264,128]{2,1,0:T(8,128)(2,1)} %get-tuple-element.52), channel_id=1, source_target_pairs={{0,2},{1,3},{2,0},{3,1},{4,6},{5,7},{6,4},{7,5},{8,10},{9,11},{10,... | collective-permute-start | bytes 811016 | tf_op jit(solution)/shard_map/ppermute | solution.py:35
  26.6 19.7 %collective-permute-start.8 = (bf16[192,2176]{1,0:T(8,128)(2,1)S(1)}, bf16[192,2176]{1,0:T(8,128)(2,1)S(1)}, u32[]{:S(2)}, u32[]{:S(2)}) collective-permute-start(bf16[192,2176]{1,0:T(8,128)(2,1)S(1)} %bitcast.37), channel_id=1, source_target_pairs={{0,2},{1,3},{2,0},{3,1},{4,6},{5,7},{6,4},{7,5},{8,10},{9,11},{10,... | collective-permute-start | bytes 2506760 | tf_op jit(solution)/shard_map/ppermute | solution.py:35
  28.2 5.1 %collective-permute-start.4 = (bf16[2,264,128]{2,1,0:T(8,128)(2,1)S(1)}, bf16[2,264,128]{2,1,0:T(8,128)(2,1)S(1)}, u32[]{:S(2)}, u32[]{:S(2)}) collective-permute-start(bf16[2,264,128]{2,1,0:T(8,128)(2,1)S(1)} %get-tuple-element.54), channel_id=1, source_target_pairs={{0,0},{1,1},{2,2},{3,3},{4,4},{5,5},{6,6},{7,7},{8,8},{9,9},{10,10... | collective-permute-start | bytes 405512 | tf_op jit(solution)/shard_map/ppermute | solution.py:67
  28.9 6.5 %collective-permute-start.5 = (bf16[2,264,128]{2,1,0:T(8,128)(2,1)S(1)}, bf16[2,264,128]{2,1,0:T(8,128)(2,1)S(1)}, u32[]{:S(2)}, u32[]{:S(2)}) collective-permute-start(bf16[2,264,128]{2,1,0:T(8,128)(2,1)S(1)} %get-tuple-element.55), channel_id=1, source_target_pairs={{0,4},{1,5},{2,6},{3,7},{4,0},{5,1},{6,2},{7,3},{8,12},{9,13},{10,... | collective-permute-start | bytes 405512 | tf_op jit(solution)/shard_map/ppermute | solution.py:67
  28.9 12.6 %collective-permute-start.6 = (bf16[2,264,128]{2,1,0:T(8,128)(2,1)S(1)}, bf16[2,264,128]{2,1,0:T(8,128)(2,1)S(1)}, u32[]{:S(2)}, u32[]{:S(2)}) collective-permute-start(bf16[2,264,128]{2,1,0:T(8,128)(2,1)S(1)} %get-tuple-element.56), channel_id=1, source_target_pairs={{0,8},{1,9},{2,10},{3,11},{4,12},{5,13},{6,14},{7,15},{8,0},{9,1},... | collective-permute-start | bytes 405512 | tf_op jit(solution)/shard_map/ppermute | solution.py:67
  32.0 9.6 %collective-permute-start.7 = (bf16[2,264,128]{2,1,0:T(8,128)(2,1)S(1)}, bf16[2,264,128]{2,1,0:T(8,128)(2,1)S(1)}, u32[]{:S(2)}, u32[]{:S(2)}) collective-permute-start(bf16[2,264,128]{2,1,0:T(8,128)(2,1)S(1)} %get-tuple-element.57), channel_id=1, source_target_pairs={{0,12},{1,13},{2,14},{3,15},{4,8},{5,9},{6,10},{7,11},{8,4},{9,5},... | collective-permute-start | bytes 405512 | tf_op jit(solution)/shard_map/ppermute | solution.py:67
  33.3 14.6 %collective-permute-start.9 = (bf16[192,2176]{1,0:T(8,128)(2,1)S(1)}, bf16[192,2176]{1,0:T(8,128)(2,1)S(1)}, u32[]{:S(2)}, u32[]{:S(2)}) collective-permute-start(bf16[192,2176]{1,0:T(8,128)(2,1)S(1)} %bitcast.38), channel_id=1, source_target_pairs={{0,1},{1,0},{2,3},{3,2},{4,5},{5,4},{6,7},{7,6},{8,9},{9,8},{10,11... | collective-permute-start | bytes 2506760 | tf_op jit(solution)/shard_map/ppermute | solution.py:35
  46.3 2.4 %collective-permute-start.10 = (bf16[192,2176]{1,0:T(8,128)(2,1)S(1)}, bf16[192,2176]{1,0:T(8,128)(2,1)S(1)}, u32[]{:S(2)}, u32[]{:S(2)}) collective-permute-start(bf16[192,2176]{1,0:T(8,128)(2,1)S(1)} %collective-permute-done.8.refs_1_), channel_id=1, source_target_pairs={{0,1},{1,0},{2,3},{3,2},{4,5},{5,4},{6,7},{7,6},{8,9},{9,8},{10,11... | collective-permute-start | bytes 2506760 | tf_op jit(solution)/shard_map/ppermute | solution.py:35
  46.4 14.8 %collective-permute-start.11 = (bf16[4,2,264,128]{3,2,1,0:T(8,128)(2,1)S(1)}, bf16[4,2,264,128]{3,2,1,0:T(8,128)(2,1)S(1)}, u32[]{:S(2)}, u32[]{:S(2)}) collective-permute-start(bf16[4,2,264,128]{3,2,1,0:T(8,128)(2,1)S(1)} %pad_maximum_fusion.2.refs_0_), channel_id=1, source_target_pairs={{0,16},{16,0},{1,17},{17,1},{2,18},{18,2},{3,19},{19,3},{4,20},{20... | collective-permute-start | bytes 1622024 | tf_op jit(solution)/shard_map/ppermute | solution.py:379
  48.7 12.5 %copy-start.2 = (s32[2]{0:T(128)S(1)}, s32[2]{0:T(128)}, u32[]{:S(2)}) copy-start(s32[2]{0:T(128)} %pad_add_fusion.place_ref) | copy-start | bytes 28
  48.7 14.1 %copy-start.3 = (bf16[1,768,2048]{2,1,0:T(8,128)(2,1)S(1)}, bf16[1,768,2048]{2,1,0:T(8,128)(2,1)}, u32[]{:S(2)}) copy-start(bf16[1,768,2048]{2,1,0:T(8,128)(2,1)} %param.15) | copy-start | bytes 9437188
  65.4 2.0 %collective-permute-start.12 = (bf16[128,2048]{1,0:T(8,128)(2,1)S(1)}, bf16[128,2048]{1,0:T(8,128)(2,1)S(1)}, u32[]{:S(2)}, u32[]{:S(2)}) collective-permute-start(bf16[128,2048]{1,0:T(8,128)(2,1)S(1)} %get-tuple-element.75), channel_id=1, source_target_pairs={{0,1},{1,0},{2,3},{3,2},{4,5},{5,4},{6,7},{7,6},{8,9},{9,8},{10,11... | collective-permute-start | bytes 1572872 | tf_op jit(solution)/shard_map/ppermute | solution.py:35
  67.5 8.4 %collective-permute-start.13 = (bf16[64,2048]{1,0:T(8,128)(2,1)S(1)}, bf16[64,2048]{1,0:T(8,128)(2,1)S(1)}, u32[]{:S(2)}, u32[]{:S(2)}) collective-permute-start(bf16[64,2048]{1,0:T(8,128)(2,1)S(1)} %slice.131), channel_id=1, source_target_pairs={{0,2},{1,3},{2,0},{3,1},{4,6},{5,7},{6,4},{7,5},{8,10},{9,11},{10,... | collective-permute-start | bytes 786440 | tf_op jit(solution)/shard_map/ppermute | solution.py:35
  71.8 4.2 %collective-permute-start.14 = (bf16[128,2048]{1,0:T(8,128)(2,1)S(1)}, bf16[128,2048]{1,0:T(8,128)(2,1)S(1)}, u32[]{:S(2)}, u32[]{:S(2)}) collective-permute-start(bf16[128,2048]{1,0:T(8,128)(2,1)S(1)} %get-tuple-element.82), channel_id=1, source_target_pairs={{0,1},{1,0},{2,3},{3,2},{4,5},{5,4},{6,7},{7,6},{8,9},{9,8},{10,11... | collective-permute-start | bytes 1572872 | tf_op jit(solution)/shard_map/ppermute | solution.py:35
  76.2 7.6 %collective-permute-start.15 = (bf16[64,2048]{1,0:T(8,128)(2,1)S(1)}, bf16[64,2048]{1,0:T(8,128)(2,1)S(1)}, u32[]{:S(2)}, u32[]{:S(2)}) collective-permute-start(bf16[64,2048]{1,0:T(8,128)(2,1)S(1)} %slice.130), channel_id=1, source_target_pairs={{0,2},{1,3},{2,0},{3,1},{4,6},{5,7},{6,4},{7,5},{8,10},{9,11},{10,... | collective-permute-start | bytes 786440 | tf_op jit(solution)/shard_map/ppermute | solution.py:35
  80.4 3.4 %collective-permute-start.16 = (bf16[128,2048]{1,0:T(8,128)(2,1)S(1)}, bf16[128,2048]{1,0:T(8,128)(2,1)S(1)}, u32[]{:S(2)}, u32[]{:S(2)}) collective-permute-start(bf16[128,2048]{1,0:T(8,128)(2,1)S(1)} %get-tuple-element.89), channel_id=1, source_target_pairs={{0,1},{1,0},{2,3},{3,2},{4,5},{5,4},{6,7},{7,6},{8,9},{9,8},{10,11... | collective-permute-start | bytes 1572872 | tf_op jit(solution)/shard_map/ppermute | solution.py:35
  84.0 7.0 %collective-permute-start.19 = (bf16[64,2048]{1,0:T(8,128)(2,1)S(1)}, bf16[64,2048]{1,0:T(8,128)(2,1)S(1)}, u32[]{:S(2)}, u32[]{:S(2)}) collective-permute-start(bf16[64,2048]{1,0:T(8,128)(2,1)S(1)} %slice.128), channel_id=1, source_target_pairs={{0,2},{1,3},{2,0},{3,1},{4,6},{5,7},{6,4},{7,5},{8,10},{9,11},{10,... | collective-permute-start | bytes 786440 | tf_op jit(solution)/shard_map/ppermute | solution.py:35
  85.7 9.8 %collective-permute-start.17 = (bf16[64,2048]{1,0:T(8,128)(2,1)S(1)}, bf16[64,2048]{1,0:T(8,128)(2,1)S(1)}, u32[]{:S(2)}, u32[]{:S(2)}) collective-permute-start(bf16[64,2048]{1,0:T(8,128)(2,1)S(1)} %bitcast.53), channel_id=1, source_target_pairs={{0,4},{1,5},{2,6},{3,7},{4,0},{5,1},{6,2},{7,3},{8,12},{9,13},{10,... | collective-permute-start | bytes 786440 | tf_op jit(solution)/shard_map/ppermute | solution.py:35
  91.1 4.7 %collective-permute-start.20 = (bf16[16,2048]{1,0:T(8,128)(2,1)S(1)}, bf16[16,2048]{1,0:T(8,128)(2,1)S(1)}, u32[]{:S(2)}, u32[]{:S(2)}) collective-permute-start(bf16[16,2048]{1,0:T(8,128)(2,1)S(1)} %get-tuple-element.103), channel_id=1, source_target_pairs={{0,4},{1,5},{2,6},{3,7},{4,0},{5,1},{6,2},{7,3},{8,12},{9,13},{10,... | collective-permute-start | bytes 196616 | tf_op jit(solution)/shard_map/ppermute | solution.py:35
  91.1 10.6 %collective-permute-start.21 = (bf16[16,2048]{1,0:T(8,128)(2,1)S(1)}, bf16[16,2048]{1,0:T(8,128)(2,1)S(1)}, u32[]{:S(2)}, u32[]{:S(2)}) collective-permute-start(bf16[16,2048]{1,0:T(8,128)(2,1)S(1)} %get-tuple-element.105), channel_id=1, source_target_pairs={{0,8},{1,9},{2,10},{3,11},{4,12},{5,13},{6,14},{7,15},{8,0},{9,1},... | collective-permute-start | bytes 196616 | tf_op jit(solution)/shard_map/ppermute | solution.py:35
  94.0 7.8 %collective-permute-start.22 = (bf16[16,2048]{1,0:T(8,128)(2,1)S(1)}, bf16[16,2048]{1,0:T(8,128)(2,1)S(1)}, u32[]{:S(2)}, u32[]{:S(2)}) collective-permute-start(bf16[16,2048]{1,0:T(8,128)(2,1)S(1)} %get-tuple-element.104), channel_id=1, source_target_pairs={{0,12},{1,13},{2,14},{3,15},{4,8},{5,9},{6,10},{7,11},{8,4},{9,5},... | collective-permute-start | bytes 196616 | tf_op jit(solution)/shard_map/ppermute | solution.py:35
  95.6 9.1 %collective-permute-start.18 = (bf16[32,2048]{1,0:T(8,128)(2,1)S(1)}, bf16[32,2048]{1,0:T(8,128)(2,1)S(1)}, u32[]{:S(2)}, u32[]{:S(2)}) collective-permute-start(bf16[32,2048]{1,0:T(8,128)(2,1)S(1)} %bitcast.59), channel_id=1, source_target_pairs={{0,8},{1,9},{2,10},{3,11},{4,12},{5,13},{6,14},{7,15},{8,0},{9,1},... | collective-permute-start | bytes 393224 | tf_op jit(solution)/shard_map/ppermute | solution.py:35

commit v19 on v18

--- a/solution.py
+++ b/solution.py
@@ -56,16 +56,6 @@
         total = kept + sent.astype(jnp.float32)
         step *= 2
     return total
-
-
-def exchange_factors(blocks, n):
-    _, middle, cores = split_axis(n)
-    here = []
-    for q, block in enumerate(blocks):
-        turn = q * middle * cores
-        pairs = [(g * n + i, g * n + (i ^ turn ^ g)) for g in range(2) for i in range(n)]
-        here.append(lax.ppermute(block, ("group", "expert"), pairs))
-    return here
 
 
 def dot(a, b):
@@ -107,8 +97,7 @@
 def order_kernel(place_ref, placement_ref, factors_ref, *refs):
     out_refs, wide_ref, slot_ref = refs[:-2], refs[-2], refs[-1]
     slots = factors_ref.shape[0]
-    outer, length, lanes = out_refs[0].shape
-    group, me = place_ref[0], place_ref[1]
+    middle, outer, length, lanes = out_refs[0].shape
 
     def cut(t, carry):
         start = pl.multiple_of(t * lanes, lanes)
@@ -119,19 +108,21 @@
     lax.fori_loop(0, length, cut, 0, unroll=8)
     for s in range(slots):
         slot_ref[placement_ref[s]] = s
-    for r, out_ref in enumerate(out_refs):
-        for q in range(outer):
-            slot = slot_ref[me ^ (2 * (q * len(out_refs) + r) + group)]
-            rows = wide_ref[pl.ds(pl.multiple_of(slot * length, 8), length), :]
-            out_ref[q] = rows.astype(jnp.bfloat16)
-
-
-def order_factors(place, placement, factors, outer, middle):
+    for core, out_ref in enumerate(out_refs):
+        for r in range(middle):
+            for q in range(outer):
+                slot = slot_ref[place_ref[0] ^ ((q * middle + r) * len(out_refs) + core)]
+                rows = wide_ref[pl.ds(pl.multiple_of(slot * length, 8), length), :]
+                out_ref[r, q] = rows.astype(jnp.bfloat16)
+
+
+def order_factors(place, placement, factors, outer, middle, cores):
     slots, entries = factors.shape
     length = entries // LANES
+    shape = jax.ShapeDtypeStruct((middle, outer, length, LANES), jnp.bfloat16)
     return pl.pallas_call(
         order_kernel,
-        out_shape=[jax.ShapeDtypeStruct((outer, length, LANES), jnp.bfloat16)] * middle,
+        out_shape=[shape] * cores,
         in_specs=[
             pl.BlockSpec(memory_space=pltpu.SMEM),
             pl.BlockSpec(memory_space=pltpu.SMEM),
@@ -142,24 +133,21 @@
             pltpu.SMEM((slots,), jnp.int32),
         ],
         compiler_params=pltpu.CompilerParams(vmem_limit_bytes=WHOLE_GRANT),
-        cost_estimate=LITTLE,
+        cost_estimate=MUCH,
         name="order_factors",
     )(place, placement, factors)
 
 
-def relayout_kernel(outer, middle, place_ref, *refs):
-    a_gu_ref, gate_b_ref, up_b_ref, down_a_ref, down_b_ref, flat_ref, wide_ref = refs[2:]
+def relayout_kernel(place_ref, *refs):
+    parts, refs = refs[:-7], refs[-7:]
+    a_gu_ref, gate_b_ref, up_b_ref, down_a_ref, down_b_ref, flat_ref, wide_ref = refs
     width, units = a_gu_ref.shape[0], gate_b_ref.shape[1]
     rank = gate_b_ref.shape[0]
-    length = refs[0].shape[2]
-    group, me = place_ref[0], place_ref[1]
-    for swapped, part in enumerate(refs[:2]):
-        core = group if swapped == 0 else 1 - group
-        for q in range(outer):
-            for r in range(middle):
-                source = me ^ ((q * middle + r) * 2 + core)
-                start = pl.multiple_of(source * length, 8)
-                flat_ref[pl.ds(start, length), :] = part[q, r].astype(jnp.float32)
+    near, length, _ = parts[0].shape
+    for q, part in enumerate(parts):
+        for j in range(near):
+            start = pl.multiple_of((place_ref[0] ^ (near * q + j)) * length, 8)
+            flat_ref[pl.ds(start, length), :] = part[j].astype(jnp.float32)
 
     n_wide, n_unit = width // 2, units // 2
     at_ub = 2 * n_wide + n_unit
@@ -197,15 +185,14 @@
             b_ref[:, j * LANES : (j + 1) * LANES] = row.astype(jnp.bfloat16)
 
 
-def relayout_factors(place, here, there, width, units, rank, n):
-    outer, middle, _ = split_axis(n)
+def relayout_factors(place, parts, width, units, rank, n):
     shapes = [(width, 2 * rank), (rank, units), (rank, units), (units, 2 * rank), (rank, width)]
-    length = here.shape[2]
+    length = parts[0].shape[1]
     return pl.pallas_call(
-        functools.partial(relayout_kernel, outer, middle),
+        relayout_kernel,
         out_shape=[jax.ShapeDtypeStruct(shape, jnp.bfloat16) for shape in shapes],
         in_specs=[pl.BlockSpec(memory_space=pltpu.SMEM)]
-        + [pl.BlockSpec(memory_space=pltpu.VMEM)] * 2,
+        + [pl.BlockSpec(memory_space=pltpu.VMEM)] * len(parts),
         scratch_shapes=[
             pltpu.VMEM((n * length, LANES), jnp.float32),
             pltpu.VMEM((width, LANES), jnp.float32),
@@ -213,84 +200,24 @@
         compiler_params=pltpu.CompilerParams(vmem_limit_bytes=GRANT),
         cost_estimate=LITTLE,
         name="relayout_factors",
-    )(place, here, there)
-
-
-class Loads:
-    def __init__(self, sem):
-        self.sem, self.count = sem, 0
-
-    def begin(self, src, dst):
-        copy = pltpu.make_async_copy(src, dst, self.sem.at[self.count])
-        copy.start()
-        self.count += 1
-        return [copy]
-
-    def begin_rows(self, src, dst, parts=4):
-        step = src.shape[0] // parts
-        cuts = [pl.ds(at, step) for at in range(0, src.shape[0], step)]
-        return sum([self.begin(src.at[cut], dst.at[cut]) for cut in cuts], [])
-
-
-def wait(copies):
-    for copy in copies:
-        copy.wait()
-
-
-def base_kernel(count, *refs):
-    pieces = refs[:count]
-    w_gate_hbm, w_up_hbm, gate_hbm, up_hbm, x_ref, w_gate_ref, w_up_ref = refs[count : count + 7]
-    gate_ref, up_ref, sem, out_sem = refs[count + 7 :]
-    rows = pieces[0].shape[0]
-    width = w_gate_ref.shape[0]
-    total = gate_ref.shape[0]
-    block = min(128, total)
-    loads = Loads(sem)
-    x_in = [loads.begin(p, x_ref.at[pl.ds(i * rows, rows)]) for i, p in enumerate(pieces)]
-    x_in = sum(x_in, [])
-    gate_in = loads.begin_rows(w_gate_hbm, w_gate_ref)
-    up_in = loads.begin_rows(w_up_hbm, w_up_ref)
-    wait(x_in + gate_in + up_in)
-
-    def store(i):
-        here = pl.ds(pl.multiple_of(i * block, block), block)
-        return [
-            pltpu.make_async_copy(src.at[here], dst.at[here], out_sem.at[j, i])
-            for j, (src, dst) in enumerate(((gate_ref, gate_hbm), (up_ref, up_hbm)))
-        ]
-
-    def run_block(i, carry):
-        here = pl.ds(pl.multiple_of(i * block, block), block)
-        gate_ref[here, :] = dot(x_ref[here, :width], w_gate_ref[...])
-        up_ref[here, :] = dot(x_ref[here, :width], w_up_ref[...])
-        for copy in store(i):
-            copy.start()
-        return carry
-
-    lax.fori_loop(0, total // block, run_block, 0)
-    for i in range(total // block):
-        wait(store(i))
+    )(place, *parts)
+
+
+def base_kernel(x_ref, other_ref, w_gate_ref, w_up_ref, gate_ref, up_ref):
+    width, rows = w_gate_ref.shape[0], x_ref.shape[0]
+    for i, piece in enumerate((x_ref, other_ref)):
+        at = slice(i * rows, (i + 1) * rows)
+        gate_ref[at, :] = dot(piece[:, :width], w_gate_ref[...])
+        up_ref[at, :] = dot(piece[:, :width], w_up_ref[...])
 
 
 def base_products(pieces, w_gate, w_up):
-    width, units = w_gate.shape
     total = sum(p.shape[0] for p in pieces)
-    out = jax.ShapeDtypeStruct((total, units), jnp.float32)
+    out = jax.ShapeDtypeStruct((total, w_gate.shape[1]), jnp.float32)
     return pl.pallas_call(
-        functools.partial(base_kernel, len(pieces)),
+        base_kernel,
         out_shape=[out, out],
-        in_specs=[pl.BlockSpec(memory_space=pl.ANY)] * len(pieces)
-        + [pl.BlockSpec(memory_space=pltpu.HBM)] * 2,
-        out_specs=[pl.BlockSpec(memory_space=pl.ANY)] * 2,
-        scratch_shapes=[
-            pltpu.VMEM((total, pieces[0].shape[1]), jnp.bfloat16),
-            pltpu.VMEM(w_gate.shape, w_gate.dtype),
-            pltpu.VMEM(w_up.shape, w_up.dtype),
-            pltpu.VMEM(out.shape, out.dtype),
-            pltpu.VMEM(out.shape, out.dtype),
-            pltpu.SemaphoreType.DMA((len(pieces) + 8,)),
-            pltpu.SemaphoreType.DMA((2, total // min(128, total))),
-        ],
+        in_specs=[pl.BlockSpec(memory_space=pltpu.VMEM)] * 4,
         compiler_params=pltpu.CompilerParams(vmem_limit_bytes=EXPERT_GRANT),
         cost_estimate=LITTLE,
         name="base_products",
@@ -299,8 +226,9 @@
 
 def finish_kernel(count, first, rows, place_ref, *refs):
     pieces, refs = refs[:count], refs[count:]
-    gate_ref, up_ref, a_gu_ref, gate_b_ref, up_b_ref, down_a_ref, down_b_ref = refs[:7]
-    w_down_ref, kept_ref, sent_ref, x_ref, inner_ref = refs[7:]
+    base, refs = refs[:count], refs[count:]
+    a_gu_ref, gate_b_ref, up_b_ref, down_a_ref, down_b_ref, w_down_ref = refs[:6]
+    kept_ref, sent_ref, x_ref, inner_ref = refs[6:]
     width = w_down_ref.shape[1]
     rank = gate_b_ref.shape[0]
     span = pieces[0].shape[0]
@@ -308,16 +236,16 @@
     for i, piece in enumerate(pieces):
         x_ref[i * rows : (i + 1) * rows, :] = piece[first : first + rows, :]
 
-    def of_step(ref):
-        starts = [i * span + first for i in range(count)]
-        return jnp.concatenate([ref[at : at + rows, :] for at in starts])
+    def of_step(refs):
+        at = [first, span + first]
+        return jnp.concatenate([ref[i : i + rows, :] for i in at for ref in refs])
 
     low = (adapter_scale * dot(x_ref[:, :width], a_gu_ref[...])).astype(jnp.bfloat16)
     gates = x_ref[:, width:].astype(jnp.float32)
     lane = lax.broadcasted_iota(jnp.int32, gates.shape, 1)
-    mine = jnp.sum(jnp.where(lane == place_ref[1], gates, 0.0), axis=1, keepdims=True)
-    g = of_step(gate_ref) + dot(low[:, :rank], gate_b_ref[...])
-    u = of_step(up_ref) + dot(low[:, rank:], up_b_ref[...])
+    mine = jnp.sum(jnp.where(lane == place_ref[0], gates, 0.0), axis=1, keepdims=True)
+    g = of_step(base[::2]) + dot(low[:, :rank], gate_b_ref[...])
+    u = of_step(base[1::2]) + dot(low[:, rank:], up_b_ref[...])
     half = 0.5 * g
     inner_ref[...] = ((half + half * jnp.tanh(half)) * u).astype(jnp.bfloat16)
     low = (adapter_scale * dot(inner_ref[...], down_a_ref[...])).astype(jnp.bfloat16)[:, :rank]
@@ -359,7 +287,7 @@
     rank = factors.shape[1] * owners // (3 * (width + units))
     outer, middle, cores = split_axis(owners)
     along_outer, along_middle = (middle * cores, outer), (cores, middle)
-    place = jnp.stack([lax.axis_index("group"), lax.axis_index("expert")]).astype(jnp.int32)
+    place = lax.axis_index("expert").astype(jnp.int32).reshape(1)
 
     def along(x, stride, size):
         return [x] + [swap(x, owners, stride, k) for k in range(1, size)]
@@ -368,21 +296,26 @@
     rows_in, factors = lax.optimization_barrier((rows_in, factors))
     column = [p.reshape(steps, rows, -1) for p in along(rows_in, *along_outer)]
     column = jnp.stack(column, axis=1).reshape(steps * outer * rows, -1)
-    blocks = order_factors(place, placement, factors, outer, middle)
-    blocks = [blocks[0]] + [swap(blocks[r], owners, cores, r) for r in range(1, middle)]
-    blocks = [jnp.stack([block[q] for block in blocks]) for q in range(outer)]
+    kept, sent = order_factors(place, placement, factors, outer, middle, cores)
+    blocks = jnp.stack([kept, swap(sent, owners, 1, 1)])
+    blocks = [blocks[:, 0], swap(blocks[:, 1], owners, cores, 1)]
+    blocks = [jnp.concatenate([block[:, q] for block in blocks]) for q in range(outer)]
     column, blocks = lax.optimization_barrier((column, blocks))
-    here = exchange_factors(blocks, owners)
+    here = blocks[:1] + [
+        swap(block, owners, middle * cores, q) for q, block in enumerate(blocks) if q
+    ]
     sheet = along(column, *along_middle)
-    here, sheet[1:] = lax.optimization_barrier((here, sheet[1:]))
-    here = jnp.stack(here)
-    there = lax.ppermute(here, "group", [(0, 1), (1, 0)])
-    pieces = sheet + [swap(p, owners, 1, 1) for p in sheet]
-    base = base_products(pieces, w_gate[0], w_up[0])
-    here, there, base = lax.optimization_barrier((here, there, base))
-    low_rank = relayout_factors(place, here, there, width, units, rank, owners)
-
+    others = [swap(column, owners, 1, 1)]
+    weights = (w_gate[0], w_up[0])
+    base = [base_products([column, others[0]], *weights)]
+    here, sheet[1:], base = lax.optimization_barrier((here, sheet[1:], base))
+    for r in range(1, middle):
+        others.append(swap(sheet[r], owners, 1, 1))
+        base.append(base_products([sheet[r], others[r]], *weights))
+    low_rank = relayout_factors(place, here, width, units, rank, owners)
+    pieces, base = sheet + others, [b for pair in base for b in pair]
     span = outer * rows
+
     def after(x, other):
         return lax.optimization_barrier((x, other))[0]
 
@@ -502,7 +435,7 @@
     owners = lax.axis_size("expert")
     rank = factors.shape[1] * owners // (3 * (width + units))
     dense = row_capacity(rows, top, placement.shape[0]) == rows
-    dense = dense and lax.axis_size("group") == 2 and split_axis(owners)[2] == 2
+    dense = dense and split_axis(owners)[1:] == (2, 2)
     outer = split_axis(owners)[0]
     dense = dense and outer > 1 and outer & (outer - 1) == 0 and split_axis(owners)[1] > 1
     dense = dense and 2 * rank == LANES and width % 256 == 0 and units % 256 == 0

time: 106 us -> 104 us (0.981)
  starting transfers between devices: 25.2 us -> 31.3 us
  Pallas kernels: 23.8 us -> 18 us
    ppermute x18 -> x22, starting transfers between devices: 18.5 us -> 31.3 us  [swap(): return lax.ppermute(x, 'expert', [(i, i ^ k * stride) for i in range(n)])]
    ppermute x5 -> x0, waiting for transfers between devices: 11.4 us -> none  [the longest x4 8.23 us: exchange_factors(): here.append(lax.ppermute(block, ('group', 'expert'), pairs))]
    ppermute x18 -> x22, waiting for transfers between devices: 40.2 us -> 50.7 us  [swap(): return lax.ppermute(x, 'expert', [(i, i ^ k * stride) for i in range(n)])]
    ppermute x5 -> x0, starting transfers between devices: 6.66 us -> none  [the longest x4 5.1 us: exchange_factors(): here.append(lax.ppermute(block, ('group', 'expert'), pairs))]
    pallas_call x3 -> x4, Pallas kernels: 13.7 us -> 9.57 us  [the longest x2 5.28 us: base_products(): pl.pallas_call(base_kernel, out_shape=[out, out], in_specs=[pl.BlockSpec(...]
    pallas_call x3, Pallas kernels: 7.99 us -> 6.49 us  [finish_step(): pl.pallas_call(functools.partial(finish_kernel, len(pieces), first, rows)...]
    squeeze x0 -> x1, other arithmetic: none -> 1.28 us  [dense_shards(): blocks = [blocks[:, 0], swap(blocks[:, 1], owners, cores, 1)]]
    another operation x1, other arithmetic: 1.25 us -> 0.12 us  [dense_shards(): column = jnp.stack(column, axis=1).reshape(steps * outer * rows, -1)]
  transfers between devices with their start and end apart: 23 -> 22, of which waited for: 13 -> 12; matrix products, arithmetic and copies ran while one was open for 3% -> 2% of each run, Pallas kernels for 17% -> 8%
where the time goes in v19:
time: 104 us; the launch traced here: 103 us
  waiting for transfers between devices  50.7 us (49%)
  starting transfers between devices  31.3 us (30%)
  Pallas kernels  18 us (17%)
  other arithmetic  2.88 us (3%)
    ppermute x22, waiting for transfers between devices, swap(): return lax.ppermute(x, 'expert', [(i, i ^ k * stride) for i in range(n)])  50.7 us
    ppermute x22, starting transfers between devices, swap(): return lax.ppermute(x, 'expert', [(i, i ^ k * stride) for i in range(n)])  31.3 us
    pallas_call x3, Pallas kernels, finish_step(): pl.pallas_call(functools.partial(finish_kernel, len(pieces), first, rows)...  6.49 us
    pallas_call x2, Pallas kernels, base_products(): pl.pallas_call(base_kernel, out_shape=[out, out], in_specs=[pl.BlockSpec(...  5.28 us
    pallas_call x1, Pallas kernels, order_factors(): pl.pallas_call(order_kernel, out_shape=[shape] * cores, in_specs=[pl.Bloc...  3.07 us
  transfers between devices with their start and end apart: 22, of which 12 were waited for; matrix products, arithmetic and copies ran while one was open for 2% of the time, Pallas kernels for 8%

profile of v19, /device:TPU:0, one launch (start us, length us, event | category | flops | bytes accessed | tf_op | source)
XLA Modules:
  0.0 103.4 jit_solution(18083091887091479517)
XLA Ops:
  0.0 2.0 %payload.1 = bf16[48,2176]{1,0:T(8,128)(2,1)} custom-call(bf16[3,16,2048]{2,1,0:T(8,128)(2,1)} %hidden_ref.1, s32[3,8,16]{2,1,0:T(8,128)} %bitcast.79, f32[3,8,16]{2,1,0:T(8,128)} %bitcast.80), custom_call_target="tpu_custom_call" | custom-call | flops 1 | bytes 1 | tf_op jit(solution)/shard_map/payload/pallas_call | solution.py:87
  2.0 3.1 %order_factors.1 = (bf16[2,4,264,128]{3,2,1,0:T(8,128)(2,1)}, bf16[2,4,264,128]{3,2,1,0:T(8,128)(2,1)}) custom-call(s32[1]{0:T(128)} %bitcast.place_ref, s32[16]{0:T(128)} %placement_ref.1, bf16[16,33792]{1,0:T(8,128)(2,1)} %factors_ref), custom_call_target="tpu_custom_call" | custom-call | flops 8589934592 | bytes 1 | tf_op jit(solution)/shard_map/order_factors/pallas_call | solution.py:123
  5.5 4.6 %collective-permute-start.2 = (bf16[48,2176]{1,0:T(8,128)(2,1)S(1)}, bf16[48,2176]{1,0:T(8,128)(2,1)S(1)}, u32[]{:S(2)}, u32[]{:S(2)}) collective-permute-start(bf16[48,2176]{1,0:T(8,128)(2,1)S(1)} %copy-done.3), channel_id=1, source_target_pairs={{0,12},{1,13},{2,14},{3,15},{4,8},{5,9},{6,10},{7,11},{8,4},{9,5},... | collective-permute-start | bytes 626696 | tf_op jit(solution)/shard_map/ppermute | solution.py:35
  10.1 0.6 collective-permute-start.1
  10.8 1.3 %fusion.1 = (bf16[2,4,264,128]{3,2,0,1:T(8,128)(2,1)S(1)}, bf16[2,4,264,128]{3,2,0,1:T(8,128)(2,1)S(1)}) fusion(bf16[1,2,4,264,128]{4,3,0,2,1:T(8,128)(2,1)} %bitcast.72, bf16[1,2,4,264,128]{4,3,0,2,1:T(8,128)(2,1)S(1)} %bitcast.73), kind=kLoop, calls=%fused_computation.8 | loop fusion | flops 540672 | bytes 2162688 | tf_op jit(solution)/shard_map/squeeze | solution.py:301
  12.0 1.7 %collective-permute-start.4 = (bf16[2,4,264,128]{3,2,0,1:T(8,128)(2,1)S(1)}, bf16[2,4,264,128]{3,2,0,1:T(8,128)(2,1)S(1)}, u32[]{:S(2)}, u32[]{:S(2)}) collective-permute-start(bf16[2,4,264,128]{3,2,0,1:T(8,128)(2,1)S(1)} %get-tuple-element.96), channel_id=1, source_target_pairs={{0,2},{1,3},{2,0},{3,1},{4,6},{5,7},{6,4},{7,5},{8,10},{9,11},{10,... | collective-permute-start | bytes 1622024 | tf_op jit(solution)/shard_map/ppermute | solution.py:35
  13.8 2.4 %collective-permute-done.2 = bf16[48,2176]{1,0:T(8,128)(2,1)S(1)} collective-permute-done((bf16[48,2176]{1,0:T(8,128)(2,1)S(1)}, bf16[48,2176]{1,0:T(8,128)(2,1)S(1)}, u32[]{:S(2)}, u32[]{:S(2)}) %collective-permute-start.2) | collective-permute-done | bytes 208928 | tf_op jit(solution)/shard_map/ppermute | solution.py:35
  16.2 5.3 %collective-permute-done = bf16[48,2176]{1,0:T(8,128)(2,1)S(1)} collective-permute-done((bf16[48,2176]{1,0:T(8,128)(2,1)S(1)}, bf16[48,2176]{1,0:T(8,128)(2,1)S(1)}, u32[]{:S(2)}, u32[]{:S(2)}) %collective-permute-start) | collective-permute-done | bytes 208928 | tf_op jit(solution)/shard_map/ppermute | solution.py:35
  21.6 7.0 %collective-permute-done.1 = bf16[48,2176]{1,0:T(8,128)(2,1)S(1)} collective-permute-done((bf16[48,2176]{1,0:T(8,128)(2,1)S(1)}, bf16[48,2176]{1,0:T(8,128)(2,1)S(1)}, u32[]{:S(2)}, u32[]{:S(2)}) %collective-permute-start.1) | collective-permute-done | bytes 208928 | tf_op jit(solution)/shard_map/ppermute | solution.py:35
  29.0 1.6 %collective-permute-start.8 = (bf16[192,2176]{1,0:T(8,128)(2,1)S(1)}, bf16[192,2176]{1,0:T(8,128)(2,1)S(1)}, u32[]{:S(2)}, u32[]{:S(2)}) collective-permute-start(bf16[192,2176]{1,0:T(8,128)(2,1)S(1)} %bitcast.59), channel_id=1, source_target_pairs={{0,2},{1,3},{2,0},{3,1},{4,6},{5,7},{6,4},{7,5},{8,10},{9,11},{10,... | collective-permute-start | bytes 2506760 | tf_op jit(solution)/shard_map/ppermute | solution.py:35
  30.5 3.1 %collective-permute-start.6 = (bf16[4,264,128]{2,1,0:T(8,128)(2,1)S(1)}, bf16[4,264,128]{2,1,0:T(8,128)(2,1)S(1)}, u32[]{:S(2)}, u32[]{:S(2)}) collective-permute-start(bf16[4,264,128]{2,1,0:T(8,128)(2,1)S(1)} %get-tuple-element.56), channel_id=1, source_target_pairs={{0,8},{1,9},{2,10},{3,11},{4,12},{5,13},{6,14},{7,15},{8,0},{9,1},... | collective-permute-start | bytes 811016 | tf_op jit(solution)/shard_map/ppermute | solution.py:35
  33.6 1.3 %collective-permute-start.7 = (bf16[4,264,128]{2,1,0:T(8,128)(2,1)S(1)}, bf16[4,264,128]{2,1,0:T(8,128)(2,1)S(1)}, u32[]{:S(2)}, u32[]{:S(2)}) collective-permute-start(bf16[4,264,128]{2,1,0:T(8,128)(2,1)S(1)} %get-tuple-element.57), channel_id=1, source_target_pairs={{0,12},{1,13},{2,14},{3,15},{4,8},{5,9},{6,10},{7,11},{8,4},{9,5},... | collective-permute-start | bytes 811016 | tf_op jit(solution)/shard_map/ppermute | solution.py:35
  34.9 2.6 %base_products.2 = (f32[384,768]{1,0:T(8,128)S(1)}, f32[384,768]{1,0:T(8,128)S(1)}) custom-call(bf16[192,2176]{1,0:T(8,128)(2,1)S(1)} %bitcast.60, bf16[192,2176]{1,0:T(8,128)(2,1)S(1)} %collective-permute-done.9.other_ref.refs_2_, bf16[2048,768]{1,0:T(8,128)(2,1)S(1)} %bitcast.54, bf16[2048,768]{1,0:T(8,128)(2,1)S(1)} %bitcast.56), custom_call_target="tpu_custom_call" | custom-call | flops 1 | bytes 1 | tf_op jit(solution)/shard_map/base_products/pallas_call | solution.py:217
  37.6 6.8 %collective-permute-done.5.refs_1_ = bf16[4,264,128]{2,1,0:T(8,128)(2,1)S(1)} collective-permute-done((bf16[4,264,128]{2,1,0:T(8,128)(2,1)S(1)}, bf16[4,264,128]{2,1,0:T(8,128)(2,1)S(1)}, u32[]{:S(2)}, u32[]{:S(2)}) %collective-permute-start.5) | collective-permute-done | bytes 270368 | tf_op jit(solution)/shard_map/ppermute | solution.py:35
  44.4 8.2 %collective-permute-done.6.refs_2_ = bf16[4,264,128]{2,1,0:T(8,128)(2,1)S(1)} collective-permute-done((bf16[4,264,128]{2,1,0:T(8,128)(2,1)S(1)}, bf16[4,264,128]{2,1,0:T(8,128)(2,1)S(1)}, u32[]{:S(2)}, u32[]{:S(2)}) %collective-permute-start.6) | collective-permute-done | bytes 270368 | tf_op jit(solution)/shard_map/ppermute | solution.py:35
  52.6 1.2 %relayout_factors.1 = (bf16[2048,128]{1,0:T(8,128)(2,1)S(1)}, bf16[64,768]{1,0:T(8,128)(2,1)S(1)}, bf16[64,768]{1,0:T(8,128)(2,1)S(1)}, bf16[768,128]{1,0:T(8,128)(2,1)S(1)}, bf16[64,2048]{1,0:T(8,128)(2,1)S(1)}) custom-call(s32[1]{0:T(128)} %bitcast.place_ref, bf16[4,264,128]{2,1,0:T(8,128)(2,1)S(1)} %get-tuple-element.65.refs_0_, ...), custom_call_target="tpu_custom_call" | custom-call | flops 1 | bytes 1 | tf_op jit(solution)/shard_map/relayout_factors/pallas_call | solution.py:191
  53.8 1.1 %collective-permute-done.10.other_ref.refs_3_ = bf16[192,2176]{1,0:T(8,128)(2,1)S(1)} collective-permute-done((bf16[192,2176]{1,0:T(8,128)(2,1)S(1)}, bf16[192,2176]{1,0:T(8,128)(2,1)S(1)}, u32[]{:S(2)}, u32[]{:S(2)}) %collective-permute-start.10) | collective-permute-done | bytes 835616 | tf_op jit(solution)/shard_map/ppermute | solution.py:35
  54.9 2.7 %base_products.3 = (f32[384,768]{1,0:T(8,128)S(1)}, f32[384,768]{1,0:T(8,128)S(1)}) custom-call(bf16[192,2176]{1,0:T(8,128)(2,1)S(1)} %collective-permute-done.8.x_ref.refs_1_, bf16[192,2176]{1,0:T(8,128)(2,1)S(1)} %collective-permute-done.10.other_ref.refs_3_, bf16[2048,768]{1,0:T(8,128)(2,1)S(1)} %bitcast.55, bf16[2048,768]{1,0:T(8,128)(2,1)S(1)} %bitcast.57), custom_call_target="tpu_custom_call" | custom-call | flops 1 | bytes 1 | tf_op jit(solution)/shard_map/base_products/pallas_call | solution.py:217
  57.6 2.2 %finish_step.3 = (f32[128,2048]{1,0:T(8,128)S(1)}, bf16[128,2048]{1,0:T(8,128)(2,1)S(1)}) custom-call(s32[1]{0:T(128)} %bitcast.place_ref, bf16[192,2176]{1,0:T(8,128)(2,1)S(1)} %bitcast.61, bf16[192,2176]{1,0:T(8,128)(2,1)S(1)} %collective-permute-done.8.x_ref.refs_1_, bf16[192,2176]{1,0:T(8,128)(2,1)S(1)} %collective-permute-done.9.other_ref.refs_2_, ...), custom_call_target="tpu_custom_call" | custom-call | flops 8589934592 | bytes 1 | tf_op jit(solution)/shard_map/finish_step/pallas_call | solution.py:262
  60.0 1.8 %collective-permute-done.11 = bf16[128,2048]{1,0:T(8,128)(2,1)S(1)} collective-permute-done((bf16[128,2048]{1,0:T(8,128)(2,1)S(1)}, bf16[128,2048]{1,0:T(8,128)(2,1)S(1)}, u32[]{:S(2)}, u32[]{:S(2)}) %collective-permute-start.11) | collective-permute-done | bytes 524320 | tf_op jit(solution)/shard_map/ppermute | solution.py:35
  62.5 2.2 %finish_step.4 = (f32[128,2048]{1,0:T(8,128)S(1)}, bf16[128,2048]{1,0:T(8,128)(2,1)S(1)}) custom-call(s32[1]{0:T(128)} %bitcast.place_ref, bf16[192,2176]{1,0:T(8,128)(2,1)S(1)} %bitcast.62, bf16[192,2176]{1,0:T(8,128)(2,1)S(1)} %collective-permute-done.8.x_ref.refs_1_, bf16[192,2176]{1,0:T(8,128)(2,1)S(1)} %collective-permute-done.9.other_ref.refs_2_, ...), custom_call_target="tpu_custom_call" | custom-call | flops 8589934592 | bytes 1 | tf_op jit(solution)/shard_map/finish_step/pallas_call | solution.py:262
  64.7 5.6 %collective-permute-done.12 = bf16[64,2048]{1,0:T(8,128)(2,1)S(1)} collective-permute-done((bf16[64,2048]{1,0:T(8,128)(2,1)S(1)}, bf16[64,2048]{1,0:T(8,128)(2,1)S(1)}, u32[]{:S(2)}, u32[]{:S(2)}) %collective-permute-start.12) | collective-permute-done | bytes 262176 | tf_op jit(solution)/shard_map/ppermute | solution.py:35
  71.1 2.2 %finish_step.5 = (f32[128,2048]{1,0:T(8,128)S(1)}, bf16[128,2048]{1,0:T(8,128)(2,1)S(1)}) custom-call(s32[1]{0:T(128)} %bitcast.place_ref, bf16[192,2176]{1,0:T(8,128)(2,1)S(1)} %bitcast.63, bf16[192,2176]{1,0:T(8,128)(2,1)S(1)} %collective-permute-done.8.x_ref.refs_1_, bf16[192,2176]{1,0:T(8,128)(2,1)S(1)} %collective-permute-done.9.other_ref.refs_2_, ...), custom_call_target="tpu_custom_call" | custom-call | flops 8589934592 | bytes 1 | tf_op jit(solution)/shard_map/finish_step/pallas_call | solution.py:262
  73.4 4.8 %collective-permute-done.14 = bf16[64,2048]{1,0:T(8,128)(2,1)S(1)} collective-permute-done((bf16[64,2048]{1,0:T(8,128)(2,1)S(1)}, bf16[64,2048]{1,0:T(8,128)(2,1)S(1)}, u32[]{:S(2)}, u32[]{:S(2)}) %collective-permute-start.14) | collective-permute-done | bytes 262176 | tf_op jit(solution)/shard_map/ppermute | solution.py:35
  79.1 5.6 %collective-permute-start.16 = (bf16[64,2048]{1,0:T(8,128)(2,1)S(1)}, bf16[64,2048]{1,0:T(8,128)(2,1)S(1)}, u32[]{:S(2)}, u32[]{:S(2)}) collective-permute-start(bf16[64,2048]{1,0:T(8,128)(2,1)S(1)} %bitcast.74), channel_id=1, source_target_pairs={{0,4},{1,5},{2,6},{3,7},{4,0},{5,1},{6,2},{7,3},{8,12},{9,13},{10,... | collective-permute-start | bytes 786440 | tf_op jit(solution)/shard_map/ppermute | solution.py:35
  85.1 5.6 %collective-permute-start.19 = (bf16[16,2048]{1,0:T(8,128)(2,1)S(1)}, bf16[16,2048]{1,0:T(8,128)(2,1)S(1)}, u32[]{:S(2)}, u32[]{:S(2)}) collective-permute-start(bf16[16,2048]{1,0:T(8,128)(2,1)S(1)} %get-tuple-element.105), channel_id=1, source_target_pairs={{0,4},{1,5},{2,6},{3,7},{4,0},{5,1},{6,2},{7,3},{8,12},{9,13},{10,... | collective-permute-start | bytes 196616 | tf_op jit(solution)/shard_map/ppermute | solution.py:35
  90.8 1.0 collective-permute-start.20
  91.8 1.5 %collective-permute-start.21 = (bf16[16,2048]{1,0:T(8,128)(2,1)S(1)}, bf16[16,2048]{1,0:T(8,128)(2,1)S(1)}, u32[]{:S(2)}, u32[]{:S(2)}) collective-permute-start(bf16[16,2048]{1,0:T(8,128)(2,1)S(1)} %get-tuple-element.106), channel_id=1, source_target_pairs={{0,12},{1,13},{2,14},{3,15},{4,8},{5,9},{6,10},{7,11},{8,4},{9,5},... | collective-permute-start | bytes 196616 | tf_op jit(solution)/shard_map/ppermute | solution.py:35
  93.4 2.0 %collective-permute-start.17 = (bf16[32,2048]{1,0:T(8,128)(2,1)S(1)}, bf16[32,2048]{1,0:T(8,128)(2,1)S(1)}, u32[]{:S(2)}, u32[]{:S(2)}) collective-permute-start(bf16[32,2048]{1,0:T(8,128)(2,1)S(1)} %bitcast.78), channel_id=1, source_target_pairs={{0,8},{1,9},{2,10},{3,11},{4,12},{5,13},{6,14},{7,15},{8,0},{9,1},... | collective-permute-start | bytes 393224 | tf_op jit(solution)/shard_map/ppermute | solution.py:35
  95.4 4.6 %collective-permute-done.20 = bf16[16,2048]{1,0:T(8,128)(2,1)S(1)} collective-permute-done((bf16[16,2048]{1,0:T(8,128)(2,1)S(1)}, bf16[16,2048]{1,0:T(8,128)(2,1)S(1)}, u32[]{:S(2)}, u32[]{:S(2)}) %collective-permute-start.20) | collective-permute-done | bytes 65568 | tf_op jit(solution)/shard_map/ppermute | solution.py:35
  100.0 2.7 %collective-permute-done.17 = bf16[32,2048]{1,0:T(8,128)(2,1)S(1)} collective-permute-done((bf16[32,2048]{1,0:T(8,128)(2,1)S(1)}, bf16[32,2048]{1,0:T(8,128)(2,1)S(1)}, u32[]{:S(2)}, u32[]{:S(2)}) %collective-permute-start.17) | collective-permute-done | bytes 131104 | tf_op jit(solution)/shard_map/ppermute | solution.py:35
  102.7 0.7 pad_maximum_fusion.7
  (54 shorter events, 4.1 us)
Async XLA Ops:
  2.0 3.5 %copy-start.3 = (bf16[48,2176]{1,0:T(8,128)(2,1)S(1)}, bf16[48,2176]{1,0:T(8,128)(2,1)}, u32[]{:S(2)}) copy-start(bf16[48,2176]{1,0:T(8,128)(2,1)} %payload.1) | copy-start | bytes 626692
  5.0 5.7 %collective-permute-start.3 = (bf16[2,4,264,128]{3,2,1,0:T(8,128)(2,1)}, bf16[2,4,264,128]{3,2,1,0:T(8,128)(2,1)S(1)}, u32[]{:S(2)}, u32[]{:S(2)}) collective-permute-start(bf16[2,4,264,128]{3,2,1,0:T(8,128)(2,1)} %get-tuple-element.52), channel_id=1, source_target_pairs={{0,1},{1,0},{2,3},{3,2},{4,5},{5,4},{6,7},{7,6},{8,9},{9,8},{10,11... | collective-permute-start | bytes 1622024 | tf_op jit(solution)/shard_map/ppermute | solution.py:35
  5.5 10.7 %collective-permute-start.2 = (bf16[48,2176]{1,0:T(8,128)(2,1)S(1)}, bf16[48,2176]{1,0:T(8,128)(2,1)S(1)}, u32[]{:S(2)}, u32[]{:S(2)}) collective-permute-start(bf16[48,2176]{1,0:T(8,128)(2,1)S(1)} %copy-done.3), channel_id=1, source_target_pairs={{0,12},{1,13},{2,14},{3,15},{4,8},{5,9},{6,10},{7,11},{8,4},{9,5},... | collective-permute-start | bytes 626696 | tf_op jit(solution)/shard_map/ppermute | solution.py:35
  10.1 11.4 %collective-permute-start = (bf16[48,2176]{1,0:T(8,128)(2,1)S(1)}, bf16[48,2176]{1,0:T(8,128)(2,1)S(1)}, u32[]{:S(2)}, u32[]{:S(2)}) collective-permute-start(bf16[48,2176]{1,0:T(8,128)(2,1)S(1)} %copy-done.3), channel_id=1, source_target_pairs={{0,4},{1,5},{2,6},{3,7},{4,0},{5,1},{6,2},{7,3},{8,12},{9,13},{10,... | collective-permute-start | bytes 626696 | tf_op jit(solution)/shard_map/ppermute | solution.py:35
  10.1 18.4 %collective-permute-start.1 = (bf16[48,2176]{1,0:T(8,128)(2,1)S(1)}, bf16[48,2176]{1,0:T(8,128)(2,1)S(1)}, u32[]{:S(2)}, u32[]{:S(2)}) collective-permute-start(bf16[48,2176]{1,0:T(8,128)(2,1)S(1)} %copy-done.3), channel_id=1, source_target_pairs={{0,8},{1,9},{2,10},{3,11},{4,12},{5,13},{6,14},{7,15},{8,0},{9,1},... | collective-permute-start | bytes 626696 | tf_op jit(solution)/shard_map/ppermute | solution.py:35
  10.8 24.2 %copy-start.1 = (bf16[1,2048,768]{2,1,0:T(8,128)(2,1)S(1)}, bf16[1,2048,768]{2,1,0:T(8,128)(2,1)}, u32[]{:S(2)}) copy-start(bf16[1,2048,768]{2,1,0:T(8,128)(2,1)} %param.14) | copy-start | bytes 9437188
  12.0 16.7 %collective-permute-start.4 = (bf16[2,4,264,128]{3,2,0,1:T(8,128)(2,1)S(1)}, bf16[2,4,264,128]{3,2,0,1:T(8,128)(2,1)S(1)}, u32[]{:S(2)}, u32[]{:S(2)}) collective-permute-start(bf16[2,4,264,128]{3,2,0,1:T(8,128)(2,1)S(1)} %get-tuple-element.96), channel_id=1, source_target_pairs={{0,2},{1,3},{2,0},{3,1},{4,6},{5,7},{6,4},{7,5},{8,10},{9,11},{10,... | collective-permute-start | bytes 1622024 | tf_op jit(solution)/shard_map/ppermute | solution.py:35
  28.7 6.2 %copy-start = (bf16[1,2048,768]{2,1,0:T(8,128)(2,1)S(1)}, bf16[1,2048,768]{2,1,0:T(8,128)(2,1)}, u32[]{:S(2)}) copy-start(bf16[1,2048,768]{2,1,0:T(8,128)(2,1)} %param.13) | copy-start | bytes 9437188
  28.9 6.1 %collective-permute-start.9 = (bf16[192,2176]{1,0:T(8,128)(2,1)S(1)}, bf16[192,2176]{1,0:T(8,128)(2,1)S(1)}, u32[]{:S(2)}, u32[]{:S(2)}) collective-permute-start(bf16[192,2176]{1,0:T(8,128)(2,1)S(1)} %bitcast.58), channel_id=1, source_target_pairs={{0,1},{1,0},{2,3},{3,2},{4,5},{5,4},{6,7},{7,6},{8,9},{9,8},{10,11... | collective-permute-start | bytes 2506760 | tf_op jit(solution)/shard_map/ppermute | solution.py:35
  29.0 23.6 %collective-permute-start.8 = (bf16[192,2176]{1,0:T(8,128)(2,1)S(1)}, bf16[192,2176]{1,0:T(8,128)(2,1)S(1)}, u32[]{:S(2)}, u32[]{:S(2)}) collective-permute-start(bf16[192,2176]{1,0:T(8,128)(2,1)S(1)} %bitcast.59), channel_id=1, source_target_pairs={{0,2},{1,3},{2,0},{3,1},{4,6},{5,7},{6,4},{7,5},{8,10},{9,11},{10,... | collective-permute-start | bytes 2506760 | tf_op jit(solution)/shard_map/ppermute | solution.py:35
  30.5 13.8 %collective-permute-start.5 = (bf16[4,264,128]{2,1,0:T(8,128)(2,1)S(1)}, bf16[4,264,128]{2,1,0:T(8,128)(2,1)S(1)}, u32[]{:S(2)}, u32[]{:S(2)}) collective-permute-start(bf16[4,264,128]{2,1,0:T(8,128)(2,1)S(1)} %get-tuple-element.55), channel_id=1, source_target_pairs={{0,4},{1,5},{2,6},{3,7},{4,0},{5,1},{6,2},{7,3},{8,12},{9,13},{10,... | collective-permute-start | bytes 811016 | tf_op jit(solution)/shard_map/ppermute | solution.py:35
  30.5 22.0 %collective-permute-start.6 = (bf16[4,264,128]{2,1,0:T(8,128)(2,1)S(1)}, bf16[4,264,128]{2,1,0:T(8,128)(2,1)S(1)}, u32[]{:S(2)}, u32[]{:S(2)}) collective-permute-start(bf16[4,264,128]{2,1,0:T(8,128)(2,1)S(1)} %get-tuple-element.56), channel_id=1, source_target_pairs={{0,8},{1,9},{2,10},{3,11},{4,12},{5,13},{6,14},{7,15},{8,0},{9,1},... | collective-permute-start | bytes 811016 | tf_op jit(solution)/shard_map/ppermute | solution.py:35
  33.6 18.9 %collective-permute-start.7 = (bf16[4,264,128]{2,1,0:T(8,128)(2,1)S(1)}, bf16[4,264,128]{2,1,0:T(8,128)(2,1)S(1)}, u32[]{:S(2)}, u32[]{:S(2)}) collective-permute-start(bf16[4,264,128]{2,1,0:T(8,128)(2,1)S(1)} %get-tuple-element.57), channel_id=1, source_target_pairs={{0,12},{1,13},{2,14},{3,15},{4,8},{5,9},{6,10},{7,11},{8,4},{9,5},... | collective-permute-start | bytes 811016 | tf_op jit(solution)/shard_map/ppermute | solution.py:35
  52.6 2.4 %collective-permute-start.10 = (bf16[192,2176]{1,0:T(8,128)(2,1)S(1)}, bf16[192,2176]{1,0:T(8,128)(2,1)S(1)}, u32[]{:S(2)}, u32[]{:S(2)}) collective-permute-start(bf16[192,2176]{1,0:T(8,128)(2,1)S(1)} %collective-permute-done.8.x_ref.refs_1_), channel_id=1, source_target_pairs={{0,1},{1,0},{2,3},{3,2},{4,5},{5,4},{6,7},{7,6},{8,9},{9,8},{10,11... | collective-permute-start | bytes 2506760 | tf_op jit(solution)/shard_map/ppermute | solution.py:35
  53.8 3.8 %copy-start.2 = (bf16[1,768,2048]{2,1,0:T(8,128)(2,1)S(1)}, bf16[1,768,2048]{2,1,0:T(8,128)(2,1)}, u32[]{:S(2)}) copy-start(bf16[1,768,2048]{2,1,0:T(8,128)(2,1)} %param.15) | copy-start | bytes 9437188
  59.8 2.0 %collective-permute-start.11 = (bf16[128,2048]{1,0:T(8,128)(2,1)S(1)}, bf16[128,2048]{1,0:T(8,128)(2,1)S(1)}, u32[]{:S(2)}, u32[]{:S(2)}) collective-permute-start(bf16[128,2048]{1,0:T(8,128)(2,1)S(1)} %get-tuple-element.75), channel_id=1, source_target_pairs={{0,1},{1,0},{2,3},{3,2},{4,5},{5,4},{6,7},{7,6},{8,9},{9,8},{10,11... | collective-permute-start | bytes 1572872 | tf_op jit(solution)/shard_map/ppermute | solution.py:35
  61.9 8.4 %collective-permute-start.12 = (bf16[64,2048]{1,0:T(8,128)(2,1)S(1)}, bf16[64,2048]{1,0:T(8,128)(2,1)S(1)}, u32[]{:S(2)}, u32[]{:S(2)}) collective-permute-start(bf16[64,2048]{1,0:T(8,128)(2,1)S(1)} %slice.161), channel_id=1, source_target_pairs={{0,2},{1,3},{2,0},{3,1},{4,6},{5,7},{6,4},{7,5},{8,10},{9,11},{10,... | collective-permute-start | bytes 786440 | tf_op jit(solution)/shard_map/ppermute | solution.py:35
  64.7 5.7 %collective-permute-start.13 = (bf16[128,2048]{1,0:T(8,128)(2,1)S(1)}, bf16[128,2048]{1,0:T(8,128)(2,1)S(1)}, u32[]{:S(2)}, u32[]{:S(2)}) collective-permute-start(bf16[128,2048]{1,0:T(8,128)(2,1)S(1)} %get-tuple-element.82), channel_id=1, source_target_pairs={{0,1},{1,0},{2,3},{3,2},{4,5},{5,4},{6,7},{7,6},{8,9},{9,8},{10,11... | collective-permute-start | bytes 1572872 | tf_op jit(solution)/shard_map/ppermute | solution.py:35
  70.6 7.6 %collective-permute-start.14 = (bf16[64,2048]{1,0:T(8,128)(2,1)S(1)}, bf16[64,2048]{1,0:T(8,128)(2,1)S(1)}, u32[]{:S(2)}, u32[]{:S(2)}) collective-permute-start(bf16[64,2048]{1,0:T(8,128)(2,1)S(1)} %slice.160), channel_id=1, source_target_pairs={{0,2},{1,3},{2,0},{3,1},{4,6},{5,7},{6,4},{7,5},{8,10},{9,11},{10,... | collective-permute-start | bytes 786440 | tf_op jit(solution)/shard_map/ppermute | solution.py:35
  73.3 4.9 %collective-permute-start.15 = (bf16[128,2048]{1,0:T(8,128)(2,1)S(1)}, bf16[128,2048]{1,0:T(8,128)(2,1)S(1)}, u32[]{:S(2)}, u32[]{:S(2)}) collective-permute-start(bf16[128,2048]{1,0:T(8,128)(2,1)S(1)} %get-tuple-element.89), channel_id=1, source_target_pairs={{0,1},{1,0},{2,3},{3,2},{4,5},{5,4},{6,7},{7,6},{8,9},{9,8},{10,11... | collective-permute-start | bytes 1572872 | tf_op jit(solution)/shard_map/ppermute | solution.py:35
  78.4 6.7 %collective-permute-start.18 = (bf16[64,2048]{1,0:T(8,128)(2,1)S(1)}, bf16[64,2048]{1,0:T(8,128)(2,1)S(1)}, u32[]{:S(2)}, u32[]{:S(2)}) collective-permute-start(bf16[64,2048]{1,0:T(8,128)(2,1)S(1)} %slice.158), channel_id=1, source_target_pairs={{0,2},{1,3},{2,0},{3,1},{4,6},{5,7},{6,4},{7,5},{8,10},{9,11},{10,... | collective-permute-start | bytes 786440 | tf_op jit(solution)/shard_map/ppermute | solution.py:35
  79.1 14.1 %collective-permute-start.16 = (bf16[64,2048]{1,0:T(8,128)(2,1)S(1)}, bf16[64,2048]{1,0:T(8,128)(2,1)S(1)}, u32[]{:S(2)}, u32[]{:S(2)}) collective-permute-start(bf16[64,2048]{1,0:T(8,128)(2,1)S(1)} %bitcast.74), channel_id=1, source_target_pairs={{0,4},{1,5},{2,6},{3,7},{4,0},{5,1},{6,2},{7,3},{8,12},{9,13},{10,... | collective-permute-start | bytes 786440 | tf_op jit(solution)/shard_map/ppermute | solution.py:35
  85.1 10.2 %collective-permute-start.19 = (bf16[16,2048]{1,0:T(8,128)(2,1)S(1)}, bf16[16,2048]{1,0:T(8,128)(2,1)S(1)}, u32[]{:S(2)}, u32[]{:S(2)}) collective-permute-start(bf16[16,2048]{1,0:T(8,128)(2,1)S(1)} %get-tuple-element.105), channel_id=1, source_target_pairs={{0,4},{1,5},{2,6},{3,7},{4,0},{5,1},{6,2},{7,3},{8,12},{9,13},{10,... | collective-permute-start | bytes 196616 | tf_op jit(solution)/shard_map/ppermute | solution.py:35
  90.8 9.2 %collective-permute-start.20 = (bf16[16,2048]{1,0:T(8,128)(2,1)S(1)}, bf16[16,2048]{1,0:T(8,128)(2,1)S(1)}, u32[]{:S(2)}, u32[]{:S(2)}) collective-permute-start(bf16[16,2048]{1,0:T(8,128)(2,1)S(1)} %get-tuple-element.107), channel_id=1, source_target_pairs={{0,8},{1,9},{2,10},{3,11},{4,12},{5,13},{6,14},{7,15},{8,0},{9,1},... | collective-permute-start | bytes 196616 | tf_op jit(solution)/shard_map/ppermute | solution.py:35
  91.8 8.2 %collective-permute-start.21 = (bf16[16,2048]{1,0:T(8,128)(2,1)S(1)}, bf16[16,2048]{1,0:T(8,128)(2,1)S(1)}, u32[]{:S(2)}, u32[]{:S(2)}) collective-permute-start(bf16[16,2048]{1,0:T(8,128)(2,1)S(1)} %get-tuple-element.106), channel_id=1, source_target_pairs={{0,12},{1,13},{2,14},{3,15},{4,8},{5,9},{6,10},{7,11},{8,4},{9,5},... | collective-permute-start | bytes 196616 | tf_op jit(solution)/shard_map/ppermute | solution.py:35
  93.4 9.4 %collective-permute-start.17 = (bf16[32,2048]{1,0:T(8,128)(2,1)S(1)}, bf16[32,2048]{1,0:T(8,128)(2,1)S(1)}, u32[]{:S(2)}, u32[]{:S(2)}) collective-permute-start(bf16[32,2048]{1,0:T(8,128)(2,1)S(1)} %bitcast.78), channel_id=1, source_target_pairs={{0,8},{1,9},{2,10},{3,11},{4,12},{5,13},{6,14},{7,15},{8,0},{9,1},... | collective-permute-start | bytes 393224 | tf_op jit(solution)/shard_map/ppermute | solution.py:35

commit v20 on v19

--- a/solution.py
+++ b/solution.py
@@ -321,20 +321,19 @@
 
     summed, across = [], []
     for s in range(steps):
-        if s >= 1:
-            pieces = lax.optimization_barrier((pieces, summed[s - 1], across[: s - 1]))[0]
+        if s >= 2:
+            pieces = lax.optimization_barrier((pieces, summed[s - 2]))[0]
         kept, sent = finish_step(
             place, pieces, base, s * span, span, low_rank, down_weight[0]
         )
-        if s >= 1:
-            kept = after(kept, across[s - 1])
+        if s == 2:
+            kept = after(kept, across[0])
         summed.append(kept + swap(sent, owners, 1, 1).astype(jnp.float32))
         across.append(scatter_along(summed[s], owners, *along_middle))
-    across[:-1] = [after(total, summed[-1]) for total in across[:-1]]
     ends = []
     final = scatter_along(across[-1], owners, *along_outer, ends)
-    others = halve_along(jnp.concatenate(across[:-1]), owners, *along_outer, rows, ends[0])
-    return jnp.concatenate([others, final]).astype(jnp.bfloat16).reshape(hidden.shape)
+    others = [halve_along(total, owners, *along_outer, rows, ends[0]) for total in across[:-1]]
+    return jnp.stack(others + [final]).astype(jnp.bfloat16)
 
 
 def row_capacity(rows, top, experts):

time: 104 us -> 103 us (level)
  waiting for transfers between devices: 50.7 us -> 46.9 us
  starting transfers between devices: 31.3 us -> 34.6 us
    ppermute x22 -> x24, waiting for transfers between devices: 50.7 us -> 46.9 us  [swap(): return lax.ppermute(x, 'expert', [(i, i ^ k * stride) for i in range(n)])]
    ppermute x22 -> x24, starting transfers between devices: 31.3 us -> 34.6 us  [swap(): return lax.ppermute(x, 'expert', [(i, i ^ k * stride) for i in range(n)])]
  transfers between devices with their start and end apart: 22 -> 24, of which waited for: 12 -> 12; matrix products, arithmetic and copies ran while one was open for 2% -> 2% of each run, Pallas kernels for 8% -> 8%
where the time goes in v20:
time: 103 us
  waiting for transfers between devices  46.9 us (46%)
  starting transfers between devices  34.6 us (34%)
  Pallas kernels  18 us (17%)
  other arithmetic  2.83 us (3%)
    ppermute x24, waiting for transfers between devices, swap(): return lax.ppermute(x, 'expert', [(i, i ^ k * stride) for i in range(n)])  46.9 us
    ppermute x24, starting transfers between devices, swap(): return lax.ppermute(x, 'expert', [(i, i ^ k * stride) for i in range(n)])  34.6 us
    pallas_call x3, Pallas kernels, finish_step(): pl.pallas_call(functools.partial(finish_kernel, len(pieces), first, rows)...  6.49 us
    pallas_call x2, Pallas kernels, base_products(): pl.pallas_call(base_kernel, out_shape=[out, out], in_specs=[pl.BlockSpec(...  5.28 us
    pallas_call x1, Pallas kernels, order_factors(): pl.pallas_call(order_kernel, out_shape=[shape] * cores, in_specs=[pl.Bloc...  3.08 us
  transfers between devices with their start and end apart: 24, of which 12 were waited for; matrix products, arithmetic and copies ran while one was open for 2% of the time, Pallas kernels for 8%

profile of v20, /device:TPU:0, one launch (start us, length us, event | category | flops | bytes accessed | tf_op | source)
XLA Modules:
  0.0 102.9 jit_solution(4745673233336223287)
XLA Ops:
  0.0 2.0 %payload.1 = bf16[48,2176]{1,0:T(8,128)(2,1)} custom-call(bf16[3,16,2048]{2,1,0:T(8,128)(2,1)} %hidden_ref.1, s32[3,8,16]{2,1,0:T(8,128)} %bitcast.106, f32[3,8,16]{2,1,0:T(8,128)} %bitcast.107), custom_call_target="tpu_custom_call" | custom-call | flops 1 | bytes 1 | tf_op jit(solution)/shard_map/payload/pallas_call | solution.py:87
  2.0 3.1 %order_factors.1 = (bf16[2,4,264,128]{3,2,1,0:T(8,128)(2,1)}, bf16[2,4,264,128]{3,2,1,0:T(8,128)(2,1)}) custom-call(s32[1]{0:T(128)} %bitcast.place_ref, s32[16]{0:T(128)} %placement_ref.1, bf16[16,33792]{1,0:T(8,128)(2,1)} %factors_ref), custom_call_target="tpu_custom_call" | custom-call | flops 8589934592 | bytes 1 | tf_op jit(solution)/shard_map/order_factors/pallas_call | solution.py:123
  5.5 4.6 %collective-permute-start.2 = (bf16[48,2176]{1,0:T(8,128)(2,1)S(1)}, bf16[48,2176]{1,0:T(8,128)(2,1)S(1)}, u32[]{:S(2)}, u32[]{:S(2)}) collective-permute-start(bf16[48,2176]{1,0:T(8,128)(2,1)S(1)} %copy-done.3), channel_id=1, source_target_pairs={{0,12},{1,13},{2,14},{3,15},{4,8},{5,9},{6,10},{7,11},{8,4},{9,5},... | collective-permute-start | bytes 626696 | tf_op jit(solution)/shard_map/ppermute | solution.py:35
  10.8 1.3 %fusion.1 = (bf16[2,4,264,128]{3,2,0,1:T(8,128)(2,1)S(1)}, bf16[2,4,264,128]{3,2,0,1:T(8,128)(2,1)S(1)}) fusion(bf16[1,2,4,264,128]{4,3,0,2,1:T(8,128)(2,1)} %bitcast.99, bf16[1,2,4,264,128]{4,3,0,2,1:T(8,128)(2,1)S(1)} %bitcast.100), kind=kLoop, calls=%fused_computation.7 | loop fusion | flops 540672 | bytes 2162688 | tf_op jit(solution)/shard_map/squeeze | solution.py:301
  12.0 1.7 %collective-permute-start.4 = (bf16[2,4,264,128]{3,2,0,1:T(8,128)(2,1)S(1)}, bf16[2,4,264,128]{3,2,0,1:T(8,128)(2,1)S(1)}, u32[]{:S(2)}, u32[]{:S(2)}) collective-permute-start(bf16[2,4,264,128]{3,2,0,1:T(8,128)(2,1)S(1)} %get-tuple-element.84), channel_id=1, source_target_pairs={{0,2},{1,3},{2,0},{3,1},{4,6},{5,7},{6,4},{7,5},{8,10},{9,11},{10,... | collective-permute-start | bytes 1622024 | tf_op jit(solution)/shard_map/ppermute | solution.py:35
  13.8 2.4 %collective-permute-done.2 = bf16[48,2176]{1,0:T(8,128)(2,1)S(1)} collective-permute-done((bf16[48,2176]{1,0:T(8,128)(2,1)S(1)}, bf16[48,2176]{1,0:T(8,128)(2,1)S(1)}, u32[]{:S(2)}, u32[]{:S(2)}) %collective-permute-start.2) | collective-permute-done | bytes 208928 | tf_op jit(solution)/shard_map/ppermute | solution.py:35
  16.2 5.3 %collective-permute-done = bf16[48,2176]{1,0:T(8,128)(2,1)S(1)} collective-permute-done((bf16[48,2176]{1,0:T(8,128)(2,1)S(1)}, bf16[48,2176]{1,0:T(8,128)(2,1)S(1)}, u32[]{:S(2)}, u32[]{:S(2)}) %collective-permute-start) | collective-permute-done | bytes 208928 | tf_op jit(solution)/shard_map/ppermute | solution.py:35
  21.6 7.0 %collective-permute-done.1 = bf16[48,2176]{1,0:T(8,128)(2,1)S(1)} collective-permute-done((bf16[48,2176]{1,0:T(8,128)(2,1)S(1)}, bf16[48,2176]{1,0:T(8,128)(2,1)S(1)}, u32[]{:S(2)}, u32[]{:S(2)}) %collective-permute-start.1) | collective-permute-done | bytes 208928 | tf_op jit(solution)/shard_map/ppermute | solution.py:35
  29.0 1.6 %collective-permute-start.8 = (bf16[192,2176]{1,0:T(8,128)(2,1)S(1)}, bf16[192,2176]{1,0:T(8,128)(2,1)S(1)}, u32[]{:S(2)}, u32[]{:S(2)}) collective-permute-start(bf16[192,2176]{1,0:T(8,128)(2,1)S(1)} %bitcast.82), channel_id=1, source_target_pairs={{0,2},{1,3},{2,0},{3,1},{4,6},{5,7},{6,4},{7,5},{8,10},{9,11},{10,... | collective-permute-start | bytes 2506760 | tf_op jit(solution)/shard_map/ppermute | solution.py:35
  30.6 3.1 %collective-permute-start.6 = (bf16[4,264,128]{2,1,0:T(8,128)(2,1)S(1)}, bf16[4,264,128]{2,1,0:T(8,128)(2,1)S(1)}, u32[]{:S(2)}, u32[]{:S(2)}) collective-permute-start(bf16[4,264,128]{2,1,0:T(8,128)(2,1)S(1)} %get-tuple-element.50), channel_id=1, source_target_pairs={{0,8},{1,9},{2,10},{3,11},{4,12},{5,13},{6,14},{7,15},{8,0},{9,1},... | collective-permute-start | bytes 811016 | tf_op jit(solution)/shard_map/ppermute | solution.py:35
  33.6 1.3 %collective-permute-start.7 = (bf16[4,264,128]{2,1,0:T(8,128)(2,1)S(1)}, bf16[4,264,128]{2,1,0:T(8,128)(2,1)S(1)}, u32[]{:S(2)}, u32[]{:S(2)}) collective-permute-start(bf16[4,264,128]{2,1,0:T(8,128)(2,1)S(1)} %get-tuple-element.51), channel_id=1, source_target_pairs={{0,12},{1,13},{2,14},{3,15},{4,8},{5,9},{6,10},{7,11},{8,4},{9,5},... | collective-permute-start | bytes 811016 | tf_op jit(solution)/shard_map/ppermute | solution.py:35
  34.9 2.6 %base_products.2 = (f32[384,768]{1,0:T(8,128)S(1)}, f32[384,768]{1,0:T(8,128)S(1)}) custom-call(bf16[192,2176]{1,0:T(8,128)(2,1)S(1)} %bitcast.83, bf16[192,2176]{1,0:T(8,128)(2,1)S(1)} %collective-permute-done.9.other_ref.refs_2_, bf16[2048,768]{1,0:T(8,128)(2,1)S(1)} %bitcast.77, bf16[2048,768]{1,0:T(8,128)(2,1)S(1)} %bitcast.79), custom_call_target="tpu_custom_call" | custom-call | flops 1 | bytes 1 | tf_op jit(solution)/shard_map/base_products/pallas_call | solution.py:217
  37.6 6.8 %collective-permute-done.5.refs_1_ = bf16[4,264,128]{2,1,0:T(8,128)(2,1)S(1)} collective-permute-done((bf16[4,264,128]{2,1,0:T(8,128)(2,1)S(1)}, bf16[4,264,128]{2,1,0:T(8,128)(2,1)S(1)}, u32[]{:S(2)}, u32[]{:S(2)}) %collective-permute-start.5) | collective-permute-done | bytes 270368 | tf_op jit(solution)/shard_map/ppermute | solution.py:35
  44.4 8.2 %collective-permute-done.6.refs_2_ = bf16[4,264,128]{2,1,0:T(8,128)(2,1)S(1)} collective-permute-done((bf16[4,264,128]{2,1,0:T(8,128)(2,1)S(1)}, bf16[4,264,128]{2,1,0:T(8,128)(2,1)S(1)}, u32[]{:S(2)}, u32[]{:S(2)}) %collective-permute-start.6) | collective-permute-done | bytes 270368 | tf_op jit(solution)/shard_map/ppermute | solution.py:35
  52.6 1.2 %relayout_factors.1 = (bf16[2048,128]{1,0:T(8,128)(2,1)S(1)}, bf16[64,768]{1,0:T(8,128)(2,1)S(1)}, bf16[64,768]{1,0:T(8,128)(2,1)S(1)}, bf16[768,128]{1,0:T(8,128)(2,1)S(1)}, bf16[64,2048]{1,0:T(8,128)(2,1)S(1)}) custom-call(s32[1]{0:T(128)} %bitcast.place_ref, bf16[4,264,128]{2,1,0:T(8,128)(2,1)S(1)} %get-tuple-element.59.refs_0_, ...), custom_call_target="tpu_custom_call" | custom-call | flops 1 | bytes 1 | tf_op jit(solution)/shard_map/relayout_factors/pallas_call | solution.py:191
  53.8 1.1 %collective-permute-done.10.other_ref.refs_3_ = bf16[192,2176]{1,0:T(8,128)(2,1)S(1)} collective-permute-done((bf16[192,2176]{1,0:T(8,128)(2,1)S(1)}, bf16[192,2176]{1,0:T(8,128)(2,1)S(1)}, u32[]{:S(2)}, u32[]{:S(2)}) %collective-permute-start.10) | collective-permute-done | bytes 835616 | tf_op jit(solution)/shard_map/ppermute | solution.py:35
  54.9 2.7 %base_products.3 = (f32[384,768]{1,0:T(8,128)S(1)}, f32[384,768]{1,0:T(8,128)S(1)}) custom-call(bf16[192,2176]{1,0:T(8,128)(2,1)S(1)} %collective-permute-done.8.x_ref.refs_1_, bf16[192,2176]{1,0:T(8,128)(2,1)S(1)} %collective-permute-done.10.other_ref.refs_3_, bf16[2048,768]{1,0:T(8,128)(2,1)S(1)} %bitcast.78, bf16[2048,768]{1,0:T(8,128)(2,1)S(1)} %bitcast.80), custom_call_target="tpu_custom_call" | custom-call | flops 1 | bytes 1 | tf_op jit(solution)/shard_map/base_products/pallas_call | solution.py:217
  57.6 2.2 %finish_step.3 = (f32[128,2048]{1,0:T(8,128)S(1)}, bf16[128,2048]{1,0:T(8,128)(2,1)S(1)}) custom-call(s32[1]{0:T(128)} %bitcast.place_ref, bf16[192,2176]{1,0:T(8,128)(2,1)S(1)} %bitcast.84, bf16[192,2176]{1,0:T(8,128)(2,1)S(1)} %collective-permute-done.8.x_ref.refs_1_, bf16[192,2176]{1,0:T(8,128)(2,1)S(1)} %collective-permute-done.9.other_ref.refs_2_, ...), custom_call_target="tpu_custom_call" | custom-call | flops 8589934592 | bytes 1 | tf_op jit(solution)/shard_map/finish_step/pallas_call | solution.py:262
  60.0 2.2 %finish_step.5 = (f32[128,2048]{1,0:T(8,128)S(1)}, bf16[128,2048]{1,0:T(8,128)(2,1)S(1)}) custom-call(s32[1]{0:T(128)} %bitcast.place_ref, bf16[192,2176]{1,0:T(8,128)(2,1)S(1)} %bitcast.85, bf16[192,2176]{1,0:T(8,128)(2,1)S(1)} %collective-permute-done.8.x_ref.refs_1_, bf16[192,2176]{1,0:T(8,128)(2,1)S(1)} %collective-permute-done.9.other_ref.refs_2_, ...), custom_call_target="tpu_custom_call" | custom-call | flops 8589934592 | bytes 1 | tf_op jit(solution)/shard_map/finish_step/pallas_call | solution.py:262
  63.3 2.2 %finish_step.4 = (f32[128,2048]{1,0:T(8,128)S(1)}, bf16[128,2048]{1,0:T(8,128)(2,1)S(1)}) custom-call(s32[1]{0:T(128)} %bitcast.place_ref, bf16[192,2176]{1,0:T(8,128)(2,1)S(1)} %bitcast.86, bf16[192,2176]{1,0:T(8,128)(2,1)S(1)} %collective-permute-done.8.x_ref.refs_1_, bf16[192,2176]{1,0:T(8,128)(2,1)S(1)} %collective-permute-done.9.other_ref.refs_2_, ...), custom_call_target="tpu_custom_call" | custom-call | flops 8589934592 | bytes 1 | tf_op jit(solution)/shard_map/finish_step/pallas_call | solution.py:262
  65.7 1.6 %collective-permute-start.19 = (bf16[64,2048]{1,0:T(8,128)(2,1)S(1)}, bf16[64,2048]{1,0:T(8,128)(2,1)S(1)}, u32[]{:S(2)}, u32[]{:S(2)}) collective-permute-start(bf16[64,2048]{1,0:T(8,128)(2,1)S(1)} %slice.203), channel_id=1, source_target_pairs={{0,2},{1,3},{2,0},{3,1},{4,6},{5,7},{6,4},{7,5},{8,10},{9,11},{10,... | collective-permute-start | bytes 786440 | tf_op jit(solution)/shard_map/ppermute | solution.py:35
  67.3 4.7 %collective-permute-done.12 = bf16[64,2048]{1,0:T(8,128)(2,1)S(1)} collective-permute-done((bf16[64,2048]{1,0:T(8,128)(2,1)S(1)}, bf16[64,2048]{1,0:T(8,128)(2,1)S(1)}, u32[]{:S(2)}, u32[]{:S(2)}) %collective-permute-start.12) | collective-permute-done | bytes 262176 | tf_op jit(solution)/shard_map/ppermute | solution.py:35
  72.1 5.6 %collective-permute-start.13 = (bf16[32,2048]{1,0:T(8,128)(2,1)S(1)}, bf16[32,2048]{1,0:T(8,128)(2,1)S(1)}, u32[]{:S(2)}, u32[]{:S(2)}) collective-permute-start(bf16[32,2048]{1,0:T(8,128)(2,1)S(1)} %bitcast.105), channel_id=1, source_target_pairs={{0,4},{1,5},{2,6},{3,7},{4,0},{5,1},{6,2},{7,3},{8,12},{9,13},{10,... | collective-permute-start | bytes 393224 | tf_op jit(solution)/shard_map/ppermute | solution.py:35
  77.9 4.7 %collective-permute-start.20 = (bf16[32,2048]{1,0:T(8,128)(2,1)S(1)}, bf16[32,2048]{1,0:T(8,128)(2,1)S(1)}, u32[]{:S(2)}, u32[]{:S(2)}) collective-permute-start(bf16[32,2048]{1,0:T(8,128)(2,1)S(1)} %bitcast.104), channel_id=1, source_target_pairs={{0,4},{1,5},{2,6},{3,7},{4,0},{5,1},{6,2},{7,3},{8,12},{9,13},{10,... | collective-permute-start | bytes 393224 | tf_op jit(solution)/shard_map/ppermute | solution.py:35
  82.6 1.0 %collective-permute-start.14 = (bf16[16,2048]{1,0:T(8,128)(2,1)S(1)}, bf16[16,2048]{1,0:T(8,128)(2,1)S(1)}, u32[]{:S(2)}, u32[]{:S(2)}) collective-permute-start(bf16[16,2048]{1,0:T(8,128)(2,1)S(1)} %fusion.11), channel_id=1, source_target_pairs={{0,8},{1,9},{2,10},{3,11},{4,12},{5,13},{6,14},{7,15},{8,0},{9,1},... | collective-permute-start | bytes 196616 | tf_op jit(solution)/shard_map/ppermute | solution.py:35
  84.4 1.9 %collective-permute-done.20 = bf16[32,2048]{1,0:T(8,128)(2,1)S(1)} collective-permute-done((bf16[32,2048]{1,0:T(8,128)(2,1)S(1)}, bf16[32,2048]{1,0:T(8,128)(2,1)S(1)}, u32[]{:S(2)}, u32[]{:S(2)}) %collective-permute-start.20) | collective-permute-done | bytes 131104 | tf_op jit(solution)/shard_map/ppermute | solution.py:35
  86.3 4.8 %collective-permute-done.16 = bf16[64,2048]{1,0:T(8,128)(2,1)S(1)} collective-permute-done((bf16[64,2048]{1,0:T(8,128)(2,1)S(1)}, bf16[64,2048]{1,0:T(8,128)(2,1)S(1)}, u32[]{:S(2)}, u32[]{:S(2)}) %collective-permute-start.16) | collective-permute-done | bytes 262176 | tf_op jit(solution)/shard_map/ppermute | solution.py:35
  91.2 1.8 %collective-permute-start.17 = (bf16[16,2048]{1,0:T(8,128)(2,1)S(1)}, bf16[16,2048]{1,0:T(8,128)(2,1)S(1)}, u32[]{:S(2)}, u32[]{:S(2)}) collective-permute-start(bf16[16,2048]{1,0:T(8,128)(2,1)S(1)} %get-tuple-element.93), channel_id=1, source_target_pairs={{0,4},{1,5},{2,6},{3,7},{4,0},{5,1},{6,2},{7,3},{8,12},{9,13},{10,... | collective-permute-start | bytes 196616 | tf_op jit(solution)/shard_map/ppermute | solution.py:35
  93.4 2.6 %collective-permute-start.22 = (bf16[16,2048]{1,0:T(8,128)(2,1)S(1)}, bf16[16,2048]{1,0:T(8,128)(2,1)S(1)}, u32[]{:S(2)}, u32[]{:S(2)}) collective-permute-start(bf16[16,2048]{1,0:T(8,128)(2,1)S(1)} %get-tuple-element.95), channel_id=1, source_target_pairs={{0,8},{1,9},{2,10},{3,11},{4,12},{5,13},{6,14},{7,15},{8,0},{9,1},... | collective-permute-start | bytes 196616 | tf_op jit(solution)/shard_map/ppermute | solution.py:35
  96.0 1.5 %collective-permute-start.23 = (bf16[16,2048]{1,0:T(8,128)(2,1)S(1)}, bf16[16,2048]{1,0:T(8,128)(2,1)S(1)}, u32[]{:S(2)}, u32[]{:S(2)}) collective-permute-start(bf16[16,2048]{1,0:T(8,128)(2,1)S(1)} %get-tuple-element.94), channel_id=1, source_target_pairs={{0,12},{1,13},{2,14},{3,15},{4,8},{5,9},{6,10},{7,11},{8,4},{9,5},... | collective-permute-start | bytes 196616 | tf_op jit(solution)/shard_map/ppermute | solution.py:35
  97.5 2.9 %collective-permute-done.21 = bf16[16,2048]{1,0:T(8,128)(2,1)S(1)} collective-permute-done((bf16[16,2048]{1,0:T(8,128)(2,1)S(1)}, bf16[16,2048]{1,0:T(8,128)(2,1)S(1)}, u32[]{:S(2)}, u32[]{:S(2)}) %collective-permute-start.21) | collective-permute-done | bytes 65568 | tf_op jit(solution)/shard_map/ppermute | solution.py:35
  101.1 1.1 %collective-permute-done.23 = bf16[16,2048]{1,0:T(8,128)(2,1)S(1)} collective-permute-done((bf16[16,2048]{1,0:T(8,128)(2,1)S(1)}, bf16[16,2048]{1,0:T(8,128)(2,1)S(1)}, u32[]{:S(2)}, u32[]{:S(2)}) %collective-permute-start.23) | collective-permute-done | bytes 65568 | tf_op jit(solution)/shard_map/ppermute | solution.py:35
  (60 shorter events, 6.0 us)
Async XLA Ops:
  2.0 3.5 %copy-start.3 = (bf16[48,2176]{1,0:T(8,128)(2,1)S(1)}, bf16[48,2176]{1,0:T(8,128)(2,1)}, u32[]{:S(2)}) copy-start(bf16[48,2176]{1,0:T(8,128)(2,1)} %payload.1) | copy-start | bytes 626692
  5.1 5.7 %collective-permute-start.3 = (bf16[2,4,264,128]{3,2,1,0:T(8,128)(2,1)}, bf16[2,4,264,128]{3,2,1,0:T(8,128)(2,1)S(1)}, u32[]{:S(2)}, u32[]{:S(2)}) collective-permute-start(bf16[2,4,264,128]{3,2,1,0:T(8,128)(2,1)} %get-tuple-element.46), channel_id=1, source_target_pairs={{0,1},{1,0},{2,3},{3,2},{4,5},{5,4},{6,7},{7,6},{8,9},{9,8},{10,11... | collective-permute-start | bytes 1622024 | tf_op jit(solution)/shard_map/ppermute | solution.py:35
  5.5 10.7 %collective-permute-start.2 = (bf16[48,2176]{1,0:T(8,128)(2,1)S(1)}, bf16[48,2176]{1,0:T(8,128)(2,1)S(1)}, u32[]{:S(2)}, u32[]{:S(2)}) collective-permute-start(bf16[48,2176]{1,0:T(8,128)(2,1)S(1)} %copy-done.3), channel_id=1, source_target_pairs={{0,12},{1,13},{2,14},{3,15},{4,8},{5,9},{6,10},{7,11},{8,4},{9,5},... | collective-permute-start | bytes 626696 | tf_op jit(solution)/shard_map/ppermute | solution.py:35
  10.1 11.4 %collective-permute-start = (bf16[48,2176]{1,0:T(8,128)(2,1)S(1)}, bf16[48,2176]{1,0:T(8,128)(2,1)S(1)}, u32[]{:S(2)}, u32[]{:S(2)}) collective-permute-start(bf16[48,2176]{1,0:T(8,128)(2,1)S(1)} %copy-done.3), channel_id=1, source_target_pairs={{0,4},{1,5},{2,6},{3,7},{4,0},{5,1},{6,2},{7,3},{8,12},{9,13},{10,... | collective-permute-start | bytes 626696 | tf_op jit(solution)/shard_map/ppermute | solution.py:35
  10.1 18.4 %collective-permute-start.1 = (bf16[48,2176]{1,0:T(8,128)(2,1)S(1)}, bf16[48,2176]{1,0:T(8,128)(2,1)S(1)}, u32[]{:S(2)}, u32[]{:S(2)}) collective-permute-start(bf16[48,2176]{1,0:T(8,128)(2,1)S(1)} %copy-done.3), channel_id=1, source_target_pairs={{0,8},{1,9},{2,10},{3,11},{4,12},{5,13},{6,14},{7,15},{8,0},{9,1},... | collective-permute-start | bytes 626696 | tf_op jit(solution)/shard_map/ppermute | solution.py:35
  10.8 24.2 %copy-start.1 = (bf16[1,2048,768]{2,1,0:T(8,128)(2,1)S(1)}, bf16[1,2048,768]{2,1,0:T(8,128)(2,1)}, u32[]{:S(2)}) copy-start(bf16[1,2048,768]{2,1,0:T(8,128)(2,1)} %param.14) | copy-start | bytes 9437188
  12.0 16.7 %collective-permute-start.4 = (bf16[2,4,264,128]{3,2,0,1:T(8,128)(2,1)S(1)}, bf16[2,4,264,128]{3,2,0,1:T(8,128)(2,1)S(1)}, u32[]{:S(2)}, u32[]{:S(2)}) collective-permute-start(bf16[2,4,264,128]{3,2,0,1:T(8,128)(2,1)S(1)} %get-tuple-element.84), channel_id=1, source_target_pairs={{0,2},{1,3},{2,0},{3,1},{4,6},{5,7},{6,4},{7,5},{8,10},{9,11},{10,... | collective-permute-start | bytes 1622024 | tf_op jit(solution)/shard_map/ppermute | solution.py:35
  28.7 6.2 %copy-start = (bf16[1,2048,768]{2,1,0:T(8,128)(2,1)S(1)}, bf16[1,2048,768]{2,1,0:T(8,128)(2,1)}, u32[]{:S(2)}) copy-start(bf16[1,2048,768]{2,1,0:T(8,128)(2,1)} %param.13) | copy-start | bytes 9437188
  28.9 6.1 %collective-permute-start.9 = (bf16[192,2176]{1,0:T(8,128)(2,1)S(1)}, bf16[192,2176]{1,0:T(8,128)(2,1)S(1)}, u32[]{:S(2)}, u32[]{:S(2)}) collective-permute-start(bf16[192,2176]{1,0:T(8,128)(2,1)S(1)} %bitcast.81), channel_id=1, source_target_pairs={{0,1},{1,0},{2,3},{3,2},{4,5},{5,4},{6,7},{7,6},{8,9},{9,8},{10,11... | collective-permute-start | bytes 2506760 | tf_op jit(solution)/shard_map/ppermute | solution.py:35
  29.0 23.6 %collective-permute-start.8 = (bf16[192,2176]{1,0:T(8,128)(2,1)S(1)}, bf16[192,2176]{1,0:T(8,128)(2,1)S(1)}, u32[]{:S(2)}, u32[]{:S(2)}) collective-permute-start(bf16[192,2176]{1,0:T(8,128)(2,1)S(1)} %bitcast.82), channel_id=1, source_target_pairs={{0,2},{1,3},{2,0},{3,1},{4,6},{5,7},{6,4},{7,5},{8,10},{9,11},{10,... | collective-permute-start | bytes 2506760 | tf_op jit(solution)/shard_map/ppermute | solution.py:35
  30.5 13.8 %collective-permute-start.5 = (bf16[4,264,128]{2,1,0:T(8,128)(2,1)S(1)}, bf16[4,264,128]{2,1,0:T(8,128)(2,1)S(1)}, u32[]{:S(2)}, u32[]{:S(2)}) collective-permute-start(bf16[4,264,128]{2,1,0:T(8,128)(2,1)S(1)} %get-tuple-element.49), channel_id=1, source_target_pairs={{0,4},{1,5},{2,6},{3,7},{4,0},{5,1},{6,2},{7,3},{8,12},{9,13},{10,... | collective-permute-start | bytes 811016 | tf_op jit(solution)/shard_map/ppermute | solution.py:35
  30.6 22.0 %collective-permute-start.6 = (bf16[4,264,128]{2,1,0:T(8,128)(2,1)S(1)}, bf16[4,264,128]{2,1,0:T(8,128)(2,1)S(1)}, u32[]{:S(2)}, u32[]{:S(2)}) collective-permute-start(bf16[4,264,128]{2,1,0:T(8,128)(2,1)S(1)} %get-tuple-element.50), channel_id=1, source_target_pairs={{0,8},{1,9},{2,10},{3,11},{4,12},{5,13},{6,14},{7,15},{8,0},{9,1},... | collective-permute-start | bytes 811016 | tf_op jit(solution)/shard_map/ppermute | solution.py:35
  33.6 18.9 %collective-permute-start.7 = (bf16[4,264,128]{2,1,0:T(8,128)(2,1)S(1)}, bf16[4,264,128]{2,1,0:T(8,128)(2,1)S(1)}, u32[]{:S(2)}, u32[]{:S(2)}) collective-permute-start(bf16[4,264,128]{2,1,0:T(8,128)(2,1)S(1)} %get-tuple-element.51), channel_id=1, source_target_pairs={{0,12},{1,13},{2,14},{3,15},{4,8},{5,9},{6,10},{7,11},{8,4},{9,5},... | collective-permute-start | bytes 811016 | tf_op jit(solution)/shard_map/ppermute | solution.py:35
  52.6 2.4 %collective-permute-start.10 = (bf16[192,2176]{1,0:T(8,128)(2,1)S(1)}, bf16[192,2176]{1,0:T(8,128)(2,1)S(1)}, u32[]{:S(2)}, u32[]{:S(2)}) collective-permute-start(bf16[192,2176]{1,0:T(8,128)(2,1)S(1)} %collective-permute-done.8.x_ref.refs_1_), channel_id=1, source_target_pairs={{0,1},{1,0},{2,3},{3,2},{4,5},{5,4},{6,7},{7,6},{8,9},{9,8},{10,11... | collective-permute-start | bytes 2506760 | tf_op jit(solution)/shard_map/ppermute | solution.py:35
  53.8 3.8 %copy-start.2 = (bf16[1,768,2048]{2,1,0:T(8,128)(2,1)S(1)}, bf16[1,768,2048]{2,1,0:T(8,128)(2,1)}, u32[]{:S(2)}) copy-start(bf16[1,768,2048]{2,1,0:T(8,128)(2,1)} %param.15) | copy-start | bytes 9437188
  59.8 2.8 %collective-permute-start.11 = (bf16[128,2048]{1,0:T(8,128)(2,1)S(1)}, bf16[128,2048]{1,0:T(8,128)(2,1)S(1)}, u32[]{:S(2)}, u32[]{:S(2)}) collective-permute-start(bf16[128,2048]{1,0:T(8,128)(2,1)S(1)} %get-tuple-element.69), channel_id=1, source_target_pairs={{0,1},{1,0},{2,3},{3,2},{4,5},{5,4},{6,7},{7,6},{8,9},{9,8},{10,11... | collective-permute-start | bytes 1572872 | tf_op jit(solution)/shard_map/ppermute | solution.py:35
  62.2 3.4 %collective-permute-start.18 = (bf16[128,2048]{1,0:T(8,128)(2,1)S(1)}, bf16[128,2048]{1,0:T(8,128)(2,1)S(1)}, u32[]{:S(2)}, u32[]{:S(2)}) collective-permute-start(bf16[128,2048]{1,0:T(8,128)(2,1)S(1)} %get-tuple-element.79), channel_id=1, source_target_pairs={{0,1},{1,0},{2,3},{3,2},{4,5},{5,4},{6,7},{7,6},{8,9},{9,8},{10,11... | collective-permute-start | bytes 1572872 | tf_op jit(solution)/shard_map/ppermute | solution.py:35
  62.8 9.2 %collective-permute-start.12 = (bf16[64,2048]{1,0:T(8,128)(2,1)S(1)}, bf16[64,2048]{1,0:T(8,128)(2,1)S(1)}, u32[]{:S(2)}, u32[]{:S(2)}) collective-permute-start(bf16[64,2048]{1,0:T(8,128)(2,1)S(1)} %slice.205), channel_id=1, source_target_pairs={{0,2},{1,3},{2,0},{3,1},{4,6},{5,7},{6,4},{7,5},{8,10},{9,11},{10,... | collective-permute-start | bytes 786440 | tf_op jit(solution)/shard_map/ppermute | solution.py:35
  65.5 18.2 %collective-permute-start.15 = (bf16[128,2048]{1,0:T(8,128)(2,1)S(1)}, bf16[128,2048]{1,0:T(8,128)(2,1)S(1)}, u32[]{:S(2)}, u32[]{:S(2)}) collective-permute-start(bf16[128,2048]{1,0:T(8,128)(2,1)S(1)} %get-tuple-element.76), channel_id=1, source_target_pairs={{0,1},{1,0},{2,3},{3,2},{4,5},{5,4},{6,7},{7,6},{8,9},{9,8},{10,11... | collective-permute-start | bytes 1572872 | tf_op jit(solution)/shard_map/ppermute | solution.py:35
  65.7 12.0 %collective-permute-start.19 = (bf16[64,2048]{1,0:T(8,128)(2,1)S(1)}, bf16[64,2048]{1,0:T(8,128)(2,1)S(1)}, u32[]{:S(2)}, u32[]{:S(2)}) collective-permute-start(bf16[64,2048]{1,0:T(8,128)(2,1)S(1)} %slice.203), channel_id=1, source_target_pairs={{0,2},{1,3},{2,0},{3,1},{4,6},{5,7},{6,4},{7,5},{8,10},{9,11},{10,... | collective-permute-start | bytes 786440 | tf_op jit(solution)/shard_map/ppermute | solution.py:35
  72.1 10.5 %collective-permute-start.13 = (bf16[32,2048]{1,0:T(8,128)(2,1)S(1)}, bf16[32,2048]{1,0:T(8,128)(2,1)S(1)}, u32[]{:S(2)}, u32[]{:S(2)}) collective-permute-start(bf16[32,2048]{1,0:T(8,128)(2,1)S(1)} %bitcast.105), channel_id=1, source_target_pairs={{0,4},{1,5},{2,6},{3,7},{4,0},{5,1},{6,2},{7,3},{8,12},{9,13},{10,... | collective-permute-start | bytes 393224 | tf_op jit(solution)/shard_map/ppermute | solution.py:35
  77.9 8.4 %collective-permute-start.20 = (bf16[32,2048]{1,0:T(8,128)(2,1)S(1)}, bf16[32,2048]{1,0:T(8,128)(2,1)S(1)}, u32[]{:S(2)}, u32[]{:S(2)}) collective-permute-start(bf16[32,2048]{1,0:T(8,128)(2,1)S(1)} %bitcast.104), channel_id=1, source_target_pairs={{0,4},{1,5},{2,6},{3,7},{4,0},{5,1},{6,2},{7,3},{8,12},{9,13},{10,... | collective-permute-start | bytes 393224 | tf_op jit(solution)/shard_map/ppermute | solution.py:35
  82.6 14.8 %collective-permute-start.14 = (bf16[16,2048]{1,0:T(8,128)(2,1)S(1)}, bf16[16,2048]{1,0:T(8,128)(2,1)S(1)}, u32[]{:S(2)}, u32[]{:S(2)}) collective-permute-start(bf16[16,2048]{1,0:T(8,128)(2,1)S(1)} %fusion.11), channel_id=1, source_target_pairs={{0,8},{1,9},{2,10},{3,11},{4,12},{5,13},{6,14},{7,15},{8,0},{9,1},... | collective-permute-start | bytes 196616 | tf_op jit(solution)/shard_map/ppermute | solution.py:35
  83.8 7.3 %collective-permute-start.16 = (bf16[64,2048]{1,0:T(8,128)(2,1)S(1)}, bf16[64,2048]{1,0:T(8,128)(2,1)S(1)}, u32[]{:S(2)}, u32[]{:S(2)}) collective-permute-start(bf16[64,2048]{1,0:T(8,128)(2,1)S(1)} %slice.204), channel_id=1, source_target_pairs={{0,2},{1,3},{2,0},{3,1},{4,6},{5,7},{6,4},{7,5},{8,10},{9,11},{10,... | collective-permute-start | bytes 786440 | tf_op jit(solution)/shard_map/ppermute | solution.py:35
  91.2 6.3 %collective-permute-start.17 = (bf16[16,2048]{1,0:T(8,128)(2,1)S(1)}, bf16[16,2048]{1,0:T(8,128)(2,1)S(1)}, u32[]{:S(2)}, u32[]{:S(2)}) collective-permute-start(bf16[16,2048]{1,0:T(8,128)(2,1)S(1)} %get-tuple-element.93), channel_id=1, source_target_pairs={{0,4},{1,5},{2,6},{3,7},{4,0},{5,1},{6,2},{7,3},{8,12},{9,13},{10,... | collective-permute-start | bytes 196616 | tf_op jit(solution)/shard_map/ppermute | solution.py:35
  93.0 7.4 %collective-permute-start.21 = (bf16[16,2048]{1,0:T(8,128)(2,1)S(1)}, bf16[16,2048]{1,0:T(8,128)(2,1)S(1)}, u32[]{:S(2)}, u32[]{:S(2)}) collective-permute-start(bf16[16,2048]{1,0:T(8,128)(2,1)S(1)} %fusion.13), channel_id=1, source_target_pairs={{0,8},{1,9},{2,10},{3,11},{4,12},{5,13},{6,14},{7,15},{8,0},{9,1},... | collective-permute-start | bytes 196616 | tf_op jit(solution)/shard_map/ppermute | solution.py:35
  93.4 7.7 %collective-permute-start.22 = (bf16[16,2048]{1,0:T(8,128)(2,1)S(1)}, bf16[16,2048]{1,0:T(8,128)(2,1)S(1)}, u32[]{:S(2)}, u32[]{:S(2)}) collective-permute-start(bf16[16,2048]{1,0:T(8,128)(2,1)S(1)} %get-tuple-element.95), channel_id=1, source_target_pairs={{0,8},{1,9},{2,10},{3,11},{4,12},{5,13},{6,14},{7,15},{8,0},{9,1},... | collective-permute-start | bytes 196616 | tf_op jit(solution)/shard_map/ppermute | solution.py:35
  96.0 6.2 %collective-permute-start.23 = (bf16[16,2048]{1,0:T(8,128)(2,1)S(1)}, bf16[16,2048]{1,0:T(8,128)(2,1)S(1)}, u32[]{:S(2)}, u32[]{:S(2)}) collective-permute-start(bf16[16,2048]{1,0:T(8,128)(2,1)S(1)} %get-tuple-element.94), channel_id=1, source_target_pairs={{0,12},{1,13},{2,14},{3,15},{4,8},{5,9},{6,10},{7,11},{8,4},{9,5},... | collective-permute-start | bytes 196616 | tf_op jit(solution)/shard_map/ppermute | solution.py:35

commit v21 on v20

--- a/solution.py
+++ b/solution.py
@@ -35,27 +35,13 @@
     return lax.ppermute(x, "expert", [(i, i ^ (k * stride)) for i in range(n)])
 
 
-def scatter_along(total, n, stride, size, received=None):
+def scatter_along(total, n, stride, size):
     count = total.shape[0] // size
-    received = [] if received is None else received
+    received = []
     for k in range(1, size):
         part = total[k * count : (k + 1) * count].astype(jnp.bfloat16)
         received.append(swap(part, n, stride, k))
     return sum([part.astype(jnp.float32) for part in received], total[:count])
-
-
-def halve_along(total, n, stride, size, count, last):
-    step = 1
-    while step < size:
-        total = total.reshape(-1, 2, count, total.shape[1])
-        sent = total[:, 1].reshape(-1, total.shape[3]).astype(jnp.bfloat16)
-        kept = total[:, 0].reshape(-1, total.shape[3])
-        sent = swap(sent, n, stride, step)
-        if 2 * step == size:
-            sent = lax.optimization_barrier((sent, last))[0]
-        total = kept + sent.astype(jnp.float32)
-        step *= 2
-    return total
 
 
 def dot(a, b):
@@ -316,24 +302,20 @@
     pieces, base = sheet + others, [b for pair in base for b in pair]
     span = outer * rows
 
-    def after(x, other):
-        return lax.optimization_barrier((x, other))[0]
-
-    summed, across = [], []
+    summed = []
     for s in range(steps):
-        if s >= 2:
-            pieces = lax.optimization_barrier((pieces, summed[s - 2]))[0]
-        kept, sent = finish_step(
-            place, pieces, base, s * span, span, low_rank, down_weight[0]
-        )
-        if s == 2:
-            kept = after(kept, across[0])
-        summed.append(kept + swap(sent, owners, 1, 1).astype(jnp.float32))
-        across.append(scatter_along(summed[s], owners, *along_middle))
-    ends = []
-    final = scatter_along(across[-1], owners, *along_outer, ends)
-    others = [halve_along(total, owners, *along_outer, rows, ends[0]) for total in across[:-1]]
-    return jnp.stack(others + [final]).astype(jnp.bfloat16)
+        kept, sent = finish_step(place, pieces, base, s * span, span, low_rank, down_weight[0])
+        total = kept + swap(sent, owners, 1, 1).astype(jnp.float32)
+        summed.append(total.reshape(middle, outer, rows, width))
+    first = jnp.stack(summed[:-1], axis=1).reshape(-1, width)
+    last = jnp.swapaxes(summed[-1], 0, 1).reshape(-1, width)
+    first = scatter_along(first, owners, *along_middle)
+    last = scatter_along(last, owners, *along_outer)
+    first, last = lax.optimization_barrier((first, last))
+    first = jnp.swapaxes(first.reshape(steps - 1, outer, rows, width), 0, 1).reshape(-1, width)
+    first = scatter_along(first, owners, *along_outer)
+    last = scatter_along(last, owners, *along_middle)
+    return jnp.concatenate([first, last]).astype(jnp.bfloat16).reshape(hidden.shape)
 
 
 def row_capacity(rows, top, experts):

time: 103 us -> 101 us (0.981)
  starting transfers between devices: 34.6 us -> 28 us
  waiting for transfers between devices: 46.9 us -> 51.6 us
    ppermute x24 -> x22, starting transfers between devices: 34.6 us -> 28 us  [swap(): return lax.ppermute(x, 'expert', [(i, i ^ k * stride) for i in range(n)])]
    ppermute x24 -> x22, waiting for transfers between devices: 46.9 us -> 51.6 us  [swap(): return lax.ppermute(x, 'expert', [(i, i ^ k * stride) for i in range(n)])]
  transfers between devices with their start and end apart: 24 -> 22, of which waited for: 12 -> 11; matrix products, arithmetic and copies ran while one was open for 2% -> 2% of each run, Pallas kernels for 8% -> 8%
where the time goes in v21:
time: 101 us
  waiting for transfers between devices  51.6 us (51%)
  starting transfers between devices  28 us (28%)
  Pallas kernels  18 us (18%)
  other arithmetic  2.97 us (3%)
    ppermute x22, waiting for transfers between devices, swap(): return lax.ppermute(x, 'expert', [(i, i ^ k * stride) for i in range(n)])  51.6 us
    ppermute x22, starting transfers between devices, swap(): return lax.ppermute(x, 'expert', [(i, i ^ k * stride) for i in range(n)])  28 us
    pallas_call x3, Pallas kernels, finish_step(): pl.pallas_call(functools.partial(finish_kernel, len(pieces), first, rows)...  6.49 us
    pallas_call x2, Pallas kernels, base_products(): pl.pallas_call(base_kernel, out_shape=[out, out], in_specs=[pl.BlockSpec(...  5.28 us
    pallas_call x1, Pallas kernels, order_factors(): pl.pallas_call(order_kernel, out_shape=[shape] * cores, in_specs=[pl.Bloc...  3.07 us
  transfers between devices with their start and end apart: 22, of which 11 were waited for; matrix products, arithmetic and copies ran while one was open for 2% of the time, Pallas kernels for 8%

profile of v21, /device:TPU:0, one launch (start us, length us, event | category | flops | bytes accessed | tf_op | source)
XLA Modules:
  0.0 101.2 jit_solution(12983260341903237429)
XLA Ops:
  0.0 2.0 %payload.1 = bf16[48,2176]{1,0:T(8,128)(2,1)} custom-call(bf16[3,16,2048]{2,1,0:T(8,128)(2,1)} %hidden_ref.1, s32[3,8,16]{2,1,0:T(8,128)} %bitcast.113, f32[3,8,16]{2,1,0:T(8,128)} %bitcast.114), custom_call_target="tpu_custom_call" | custom-call | flops 1 | bytes 1 | tf_op jit(solution)/shard_map/payload/pallas_call | solution.py:73
  2.0 3.1 %order_factors.1 = (bf16[2,4,264,128]{3,2,1,0:T(8,128)(2,1)}, bf16[2,4,264,128]{3,2,1,0:T(8,128)(2,1)}) custom-call(s32[1]{0:T(128)} %bitcast.place_ref, s32[16]{0:T(128)} %placement_ref.1, bf16[16,33792]{1,0:T(8,128)(2,1)} %factors_ref), custom_call_target="tpu_custom_call" | custom-call | flops 8589934592 | bytes 1 | tf_op jit(solution)/shard_map/order_factors/pallas_call | solution.py:109
  5.5 4.6 %collective-permute-start.2 = (bf16[48,2176]{1,0:T(8,128)(2,1)S(1)}, bf16[48,2176]{1,0:T(8,128)(2,1)S(1)}, u32[]{:S(2)}, u32[]{:S(2)}) collective-permute-start(bf16[48,2176]{1,0:T(8,128)(2,1)S(1)} %copy-done.3), channel_id=1, source_target_pairs={{0,12},{1,13},{2,14},{3,15},{4,8},{5,9},{6,10},{7,11},{8,4},{9,5},... | collective-permute-start | bytes 626696 | tf_op jit(solution)/shard_map/ppermute | solution.py:35
  10.8 1.3 %fusion.3 = (bf16[2,4,264,128]{3,2,0,1:T(8,128)(2,1)S(1)}, bf16[2,4,264,128]{3,2,0,1:T(8,128)(2,1)S(1)}) fusion(bf16[1,2,4,264,128]{4,3,0,2,1:T(8,128)(2,1)} %bitcast.101, bf16[1,2,4,264,128]{4,3,0,2,1:T(8,128)(2,1)S(1)} %bitcast.102), kind=kLoop, calls=%fused_computation.14 | loop fusion | flops 540672 | bytes 2162688 | tf_op jit(solution)/shard_map/squeeze | solution.py:287
  12.0 1.7 %collective-permute-start.4 = (bf16[2,4,264,128]{3,2,0,1:T(8,128)(2,1)S(1)}, bf16[2,4,264,128]{3,2,0,1:T(8,128)(2,1)S(1)}, u32[]{:S(2)}, u32[]{:S(2)}) collective-permute-start(bf16[2,4,264,128]{3,2,0,1:T(8,128)(2,1)S(1)} %get-tuple-element.72), channel_id=1, source_target_pairs={{0,2},{1,3},{2,0},{3,1},{4,6},{5,7},{6,4},{7,5},{8,10},{9,11},{10,... | collective-permute-start | bytes 1622024 | tf_op jit(solution)/shard_map/ppermute | solution.py:35
  13.8 2.4 %collective-permute-done.2 = bf16[48,2176]{1,0:T(8,128)(2,1)S(1)} collective-permute-done((bf16[48,2176]{1,0:T(8,128)(2,1)S(1)}, bf16[48,2176]{1,0:T(8,128)(2,1)S(1)}, u32[]{:S(2)}, u32[]{:S(2)}) %collective-permute-start.2) | collective-permute-done | bytes 208928 | tf_op jit(solution)/shard_map/ppermute | solution.py:35
  16.2 5.3 %collective-permute-done = bf16[48,2176]{1,0:T(8,128)(2,1)S(1)} collective-permute-done((bf16[48,2176]{1,0:T(8,128)(2,1)S(1)}, bf16[48,2176]{1,0:T(8,128)(2,1)S(1)}, u32[]{:S(2)}, u32[]{:S(2)}) %collective-permute-start) | collective-permute-done | bytes 208928 | tf_op jit(solution)/shard_map/ppermute | solution.py:35
  21.6 7.0 %collective-permute-done.1 = bf16[48,2176]{1,0:T(8,128)(2,1)S(1)} collective-permute-done((bf16[48,2176]{1,0:T(8,128)(2,1)S(1)}, bf16[48,2176]{1,0:T(8,128)(2,1)S(1)}, u32[]{:S(2)}, u32[]{:S(2)}) %collective-permute-start.1) | collective-permute-done | bytes 208928 | tf_op jit(solution)/shard_map/ppermute | solution.py:35
  29.0 1.6 %collective-permute-start.8 = (bf16[192,2176]{1,0:T(8,128)(2,1)S(1)}, bf16[192,2176]{1,0:T(8,128)(2,1)S(1)}, u32[]{:S(2)}, u32[]{:S(2)}) collective-permute-start(bf16[192,2176]{1,0:T(8,128)(2,1)S(1)} %bitcast.82), channel_id=1, source_target_pairs={{0,2},{1,3},{2,0},{3,1},{4,6},{5,7},{6,4},{7,5},{8,10},{9,11},{10,... | collective-permute-start | bytes 2506760 | tf_op jit(solution)/shard_map/ppermute | solution.py:35
  30.5 3.1 %collective-permute-start.6 = (bf16[4,264,128]{2,1,0:T(8,128)(2,1)S(1)}, bf16[4,264,128]{2,1,0:T(8,128)(2,1)S(1)}, u32[]{:S(2)}, u32[]{:S(2)}) collective-permute-start(bf16[4,264,128]{2,1,0:T(8,128)(2,1)S(1)} %get-tuple-element.45), channel_id=1, source_target_pairs={{0,8},{1,9},{2,10},{3,11},{4,12},{5,13},{6,14},{7,15},{8,0},{9,1},... | collective-permute-start | bytes 811016 | tf_op jit(solution)/shard_map/ppermute | solution.py:35
  33.6 1.3 %collective-permute-start.7 = (bf16[4,264,128]{2,1,0:T(8,128)(2,1)S(1)}, bf16[4,264,128]{2,1,0:T(8,128)(2,1)S(1)}, u32[]{:S(2)}, u32[]{:S(2)}) collective-permute-start(bf16[4,264,128]{2,1,0:T(8,128)(2,1)S(1)} %get-tuple-element.46), channel_id=1, source_target_pairs={{0,12},{1,13},{2,14},{3,15},{4,8},{5,9},{6,10},{7,11},{8,4},{9,5},... | collective-permute-start | bytes 811016 | tf_op jit(solution)/shard_map/ppermute | solution.py:35
  34.9 2.6 %base_products.2 = (f32[384,768]{1,0:T(8,128)S(1)}, f32[384,768]{1,0:T(8,128)S(1)}) custom-call(bf16[192,2176]{1,0:T(8,128)(2,1)S(1)} %bitcast.83, bf16[192,2176]{1,0:T(8,128)(2,1)S(1)} %collective-permute-done.9.other_ref.refs_2_, bf16[2048,768]{1,0:T(8,128)(2,1)S(1)} %bitcast.77, bf16[2048,768]{1,0:T(8,128)(2,1)S(1)} %bitcast.79), custom_call_target="tpu_custom_call" | custom-call | flops 1 | bytes 1 | tf_op jit(solution)/shard_map/base_products/pallas_call | solution.py:203
  37.6 6.8 %collective-permute-done.5.refs_1_ = bf16[4,264,128]{2,1,0:T(8,128)(2,1)S(1)} collective-permute-done((bf16[4,264,128]{2,1,0:T(8,128)(2,1)S(1)}, bf16[4,264,128]{2,1,0:T(8,128)(2,1)S(1)}, u32[]{:S(2)}, u32[]{:S(2)}) %collective-permute-start.5) | collective-permute-done | bytes 270368 | tf_op jit(solution)/shard_map/ppermute | solution.py:35
  44.4 8.2 %collective-permute-done.6.refs_2_ = bf16[4,264,128]{2,1,0:T(8,128)(2,1)S(1)} collective-permute-done((bf16[4,264,128]{2,1,0:T(8,128)(2,1)S(1)}, bf16[4,264,128]{2,1,0:T(8,128)(2,1)S(1)}, u32[]{:S(2)}, u32[]{:S(2)}) %collective-permute-start.6) | collective-permute-done | bytes 270368 | tf_op jit(solution)/shard_map/ppermute | solution.py:35
  52.6 1.2 %relayout_factors.1 = (bf16[2048,128]{1,0:T(8,128)(2,1)S(1)}, bf16[64,768]{1,0:T(8,128)(2,1)S(1)}, bf16[64,768]{1,0:T(8,128)(2,1)S(1)}, bf16[768,128]{1,0:T(8,128)(2,1)S(1)}, bf16[64,2048]{1,0:T(8,128)(2,1)S(1)}) custom-call(s32[1]{0:T(128)} %bitcast.place_ref, bf16[4,264,128]{2,1,0:T(8,128)(2,1)S(1)} %get-tuple-element.54.refs_0_, ...), custom_call_target="tpu_custom_call" | custom-call | flops 1 | bytes 1 | tf_op jit(solution)/shard_map/relayout_factors/pallas_call | solution.py:177
  53.8 1.1 %collective-permute-done.10.other_ref.refs_3_ = bf16[192,2176]{1,0:T(8,128)(2,1)S(1)} collective-permute-done((bf16[192,2176]{1,0:T(8,128)(2,1)S(1)}, bf16[192,2176]{1,0:T(8,128)(2,1)S(1)}, u32[]{:S(2)}, u32[]{:S(2)}) %collective-permute-start.10) | collective-permute-done | bytes 835616 | tf_op jit(solution)/shard_map/ppermute | solution.py:35
  54.9 2.7 %base_products.3 = (f32[384,768]{1,0:T(8,128)S(1)}, f32[384,768]{1,0:T(8,128)S(1)}) custom-call(bf16[192,2176]{1,0:T(8,128)(2,1)S(1)} %collective-permute-done.8.x_ref.refs_1_, bf16[192,2176]{1,0:T(8,128)(2,1)S(1)} %collective-permute-done.10.other_ref.refs_3_, bf16[2048,768]{1,0:T(8,128)(2,1)S(1)} %bitcast.78, bf16[2048,768]{1,0:T(8,128)(2,1)S(1)} %bitcast.80), custom_call_target="tpu_custom_call" | custom-call | flops 1 | bytes 1 | tf_op jit(solution)/shard_map/base_products/pallas_call | solution.py:203
  57.6 2.2 %finish_step.5 = (f32[128,2048]{1,0:T(8,128)S(1)}, bf16[128,2048]{1,0:T(8,128)(2,1)S(1)}) custom-call(s32[1]{0:T(128)} %bitcast.place_ref, bf16[192,2176]{1,0:T(8,128)(2,1)S(1)} %bitcast.84, bf16[192,2176]{1,0:T(8,128)(2,1)S(1)} %collective-permute-done.8.x_ref.refs_1_, bf16[192,2176]{1,0:T(8,128)(2,1)S(1)} %collective-permute-done.9.other_ref.refs_2_, ...), custom_call_target="tpu_custom_call" | custom-call | flops 8589934592 | bytes 1 | tf_op jit(solution)/shard_map/finish_step/pallas_call | solution.py:248
  60.0 2.2 %finish_step.4 = (f32[128,2048]{1,0:T(8,128)S(1)}, bf16[128,2048]{1,0:T(8,128)(2,1)S(1)}) custom-call(s32[1]{0:T(128)} %bitcast.place_ref, bf16[192,2176]{1,0:T(8,128)(2,1)S(1)} %bitcast.85, bf16[192,2176]{1,0:T(8,128)(2,1)S(1)} %collective-permute-done.8.x_ref.refs_1_, bf16[192,2176]{1,0:T(8,128)(2,1)S(1)} %collective-permute-done.9.other_ref.refs_2_, ...), custom_call_target="tpu_custom_call" | custom-call | flops 8589934592 | bytes 1 | tf_op jit(solution)/shard_map/finish_step/pallas_call | solution.py:248
  62.6 2.2 %finish_step.3 = (f32[128,2048]{1,0:T(8,128)S(1)}, bf16[128,2048]{1,0:T(8,128)(2,1)S(1)}) custom-call(s32[1]{0:T(128)} %bitcast.place_ref, bf16[192,2176]{1,0:T(8,128)(2,1)S(1)} %bitcast.86, bf16[192,2176]{1,0:T(8,128)(2,1)S(1)} %collective-permute-done.8.x_ref.refs_1_, bf16[192,2176]{1,0:T(8,128)(2,1)S(1)} %collective-permute-done.9.other_ref.refs_2_, ...), custom_call_target="tpu_custom_call" | custom-call | flops 8589934592 | bytes 1 | tf_op jit(solution)/shard_map/finish_step/pallas_call | solution.py:248
  65.2 5.7 %collective-permute-start.15 = (bf16[32,2048]{1,0:T(8,128)(2,1)S(1)}, bf16[32,2048]{1,0:T(8,128)(2,1)S(1)}, u32[]{:S(2)}, u32[]{:S(2)}) collective-permute-start(bf16[32,2048]{1,0:T(8,128)(2,1)S(1)} %bitcast.109), channel_id=1, source_target_pairs={{0,4},{1,5},{2,6},{3,7},{4,0},{5,1},{6,2},{7,3},{8,12},{9,13},{10,... | collective-permute-start | bytes 393224 | tf_op jit(solution)/shard_map/ppermute | solution.py:35
  70.8 1.0 collective-permute-start.16
  71.8 1.5 %collective-permute-start.17 = (bf16[32,2048]{1,0:T(8,128)(2,1)S(1)}, bf16[32,2048]{1,0:T(8,128)(2,1)S(1)}, u32[]{:S(2)}, u32[]{:S(2)}) collective-permute-start(bf16[32,2048]{1,0:T(8,128)(2,1)S(1)} %bitcast.107), channel_id=1, source_target_pairs={{0,12},{1,13},{2,14},{3,15},{4,8},{5,9},{6,10},{7,11},{8,4},{9,5},... | collective-permute-start | bytes 393224 | tf_op jit(solution)/shard_map/ppermute | solution.py:35
  74.3 2.6 %collective-permute-done.15 = bf16[32,2048]{1,0:T(8,128)(2,1)S(1)} collective-permute-done((bf16[32,2048]{1,0:T(8,128)(2,1)S(1)}, bf16[32,2048]{1,0:T(8,128)(2,1)S(1)}, u32[]{:S(2)}, u32[]{:S(2)}) %collective-permute-start.15) | collective-permute-done | bytes 131104 | tf_op jit(solution)/shard_map/ppermute | solution.py:35
  76.9 6.8 %collective-permute-done.16 = bf16[32,2048]{1,0:T(8,128)(2,1)S(1)} collective-permute-done((bf16[32,2048]{1,0:T(8,128)(2,1)S(1)}, bf16[32,2048]{1,0:T(8,128)(2,1)S(1)}, u32[]{:S(2)}, u32[]{:S(2)}) %collective-permute-start.16) | collective-permute-done | bytes 131104 | tf_op jit(solution)/shard_map/ppermute | solution.py:35
  83.8 3.5 %collective-permute-done.13 = bf16[128,2048]{1,0:T(8,128)(2,1)S(1)} collective-permute-done((bf16[128,2048]{1,0:T(8,128)(2,1)S(1)}, bf16[128,2048]{1,0:T(8,128)(2,1)S(1)}, u32[]{:S(2)}, u32[]{:S(2)}) %collective-permute-start.13) | collective-permute-done | bytes 524320 | tf_op jit(solution)/shard_map/ppermute | solution.py:35
  88.2 0.8 collective-permute-start.18
  89.0 2.2 %collective-permute-start.19 = (bf16[32,2048]{1,0:T(8,128)(2,1)S(1)}, bf16[32,2048]{1,0:T(8,128)(2,1)S(1)}, u32[]{:S(2)}, u32[]{:S(2)}) collective-permute-start(bf16[32,2048]{1,0:T(8,128)(2,1)S(1)} %bitcast.111), channel_id=1, source_target_pairs={{0,8},{1,9},{2,10},{3,11},{4,12},{5,13},{6,14},{7,15},{8,0},{9,1},... | collective-permute-start | bytes 393224 | tf_op jit(solution)/shard_map/ppermute | solution.py:35
  91.2 1.5 %collective-permute-start.20 = (bf16[32,2048]{1,0:T(8,128)(2,1)S(1)}, bf16[32,2048]{1,0:T(8,128)(2,1)S(1)}, u32[]{:S(2)}, u32[]{:S(2)}) collective-permute-start(bf16[32,2048]{1,0:T(8,128)(2,1)S(1)} %bitcast.110), channel_id=1, source_target_pairs={{0,12},{1,13},{2,14},{3,15},{4,8},{5,9},{6,10},{7,11},{8,4},{9,5},... | collective-permute-start | bytes 393224 | tf_op jit(solution)/shard_map/ppermute | solution.py:35
  92.7 1.4 %collective-permute-done.18 = bf16[32,2048]{1,0:T(8,128)(2,1)S(1)} collective-permute-done((bf16[32,2048]{1,0:T(8,128)(2,1)S(1)}, bf16[32,2048]{1,0:T(8,128)(2,1)S(1)}, u32[]{:S(2)}, u32[]{:S(2)}) %collective-permute-start.18) | collective-permute-done | bytes 131104 | tf_op jit(solution)/shard_map/ppermute | solution.py:35
  94.0 6.4 %collective-permute-done.19 = bf16[32,2048]{1,0:T(8,128)(2,1)S(1)} collective-permute-done((bf16[32,2048]{1,0:T(8,128)(2,1)S(1)}, bf16[32,2048]{1,0:T(8,128)(2,1)S(1)}, u32[]{:S(2)}, u32[]{:S(2)}) %collective-permute-start.19) | collective-permute-done | bytes 131104 | tf_op jit(solution)/shard_map/ppermute | solution.py:35
  100.5 0.7 pad_maximum_fusion.7
  (52 shorter events, 4.5 us)
Async XLA Ops:
  2.0 3.5 %copy-start.3 = (bf16[48,2176]{1,0:T(8,128)(2,1)S(1)}, bf16[48,2176]{1,0:T(8,128)(2,1)}, u32[]{:S(2)}) copy-start(bf16[48,2176]{1,0:T(8,128)(2,1)} %payload.1) | copy-start | bytes 626692
  5.0 5.7 %collective-permute-start.3 = (bf16[2,4,264,128]{3,2,1,0:T(8,128)(2,1)}, bf16[2,4,264,128]{3,2,1,0:T(8,128)(2,1)S(1)}, u32[]{:S(2)}, u32[]{:S(2)}) collective-permute-start(bf16[2,4,264,128]{3,2,1,0:T(8,128)(2,1)} %get-tuple-element.41), channel_id=1, source_target_pairs={{0,1},{1,0},{2,3},{3,2},{4,5},{5,4},{6,7},{7,6},{8,9},{9,8},{10,11... | collective-permute-start | bytes 1622024 | tf_op jit(solution)/shard_map/ppermute | solution.py:35
  5.5 10.7 %collective-permute-start.2 = (bf16[48,2176]{1,0:T(8,128)(2,1)S(1)}, bf16[48,2176]{1,0:T(8,128)(2,1)S(1)}, u32[]{:S(2)}, u32[]{:S(2)}) collective-permute-start(bf16[48,2176]{1,0:T(8,128)(2,1)S(1)} %copy-done.3), channel_id=1, source_target_pairs={{0,12},{1,13},{2,14},{3,15},{4,8},{5,9},{6,10},{7,11},{8,4},{9,5},... | collective-permute-start | bytes 626696 | tf_op jit(solution)/shard_map/ppermute | solution.py:35
  10.1 11.4 %collective-permute-start = (bf16[48,2176]{1,0:T(8,128)(2,1)S(1)}, bf16[48,2176]{1,0:T(8,128)(2,1)S(1)}, u32[]{:S(2)}, u32[]{:S(2)}) collective-permute-start(bf16[48,2176]{1,0:T(8,128)(2,1)S(1)} %copy-done.3), channel_id=1, source_target_pairs={{0,4},{1,5},{2,6},{3,7},{4,0},{5,1},{6,2},{7,3},{8,12},{9,13},{10,... | collective-permute-start | bytes 626696 | tf_op jit(solution)/shard_map/ppermute | solution.py:35
  10.1 18.4 %collective-permute-start.1 = (bf16[48,2176]{1,0:T(8,128)(2,1)S(1)}, bf16[48,2176]{1,0:T(8,128)(2,1)S(1)}, u32[]{:S(2)}, u32[]{:S(2)}) collective-permute-start(bf16[48,2176]{1,0:T(8,128)(2,1)S(1)} %copy-done.3), channel_id=1, source_target_pairs={{0,8},{1,9},{2,10},{3,11},{4,12},{5,13},{6,14},{7,15},{8,0},{9,1},... | collective-permute-start | bytes 626696 | tf_op jit(solution)/shard_map/ppermute | solution.py:35
  10.8 24.2 %copy-start.1 = (bf16[1,2048,768]{2,1,0:T(8,128)(2,1)S(1)}, bf16[1,2048,768]{2,1,0:T(8,128)(2,1)}, u32[]{:S(2)}) copy-start(bf16[1,2048,768]{2,1,0:T(8,128)(2,1)} %param.14) | copy-start | bytes 9437188
  12.0 16.7 %collective-permute-start.4 = (bf16[2,4,264,128]{3,2,0,1:T(8,128)(2,1)S(1)}, bf16[2,4,264,128]{3,2,0,1:T(8,128)(2,1)S(1)}, u32[]{:S(2)}, u32[]{:S(2)}) collective-permute-start(bf16[2,4,264,128]{3,2,0,1:T(8,128)(2,1)S(1)} %get-tuple-element.72), channel_id=1, source_target_pairs={{0,2},{1,3},{2,0},{3,1},{4,6},{5,7},{6,4},{7,5},{8,10},{9,11},{10,... | collective-permute-start | bytes 1622024 | tf_op jit(solution)/shard_map/ppermute | solution.py:35
  28.7 6.2 %copy-start = (bf16[1,2048,768]{2,1,0:T(8,128)(2,1)S(1)}, bf16[1,2048,768]{2,1,0:T(8,128)(2,1)}, u32[]{:S(2)}) copy-start(bf16[1,2048,768]{2,1,0:T(8,128)(2,1)} %param.13) | copy-start | bytes 9437188
  28.9 6.1 %collective-permute-start.9 = (bf16[192,2176]{1,0:T(8,128)(2,1)S(1)}, bf16[192,2176]{1,0:T(8,128)(2,1)S(1)}, u32[]{:S(2)}, u32[]{:S(2)}) collective-permute-start(bf16[192,2176]{1,0:T(8,128)(2,1)S(1)} %bitcast.81), channel_id=1, source_target_pairs={{0,1},{1,0},{2,3},{3,2},{4,5},{5,4},{6,7},{7,6},{8,9},{9,8},{10,11... | collective-permute-start | bytes 2506760 | tf_op jit(solution)/shard_map/ppermute | solution.py:35
  29.0 23.6 %collective-permute-start.8 = (bf16[192,2176]{1,0:T(8,128)(2,1)S(1)}, bf16[192,2176]{1,0:T(8,128)(2,1)S(1)}, u32[]{:S(2)}, u32[]{:S(2)}) collective-permute-start(bf16[192,2176]{1,0:T(8,128)(2,1)S(1)} %bitcast.82), channel_id=1, source_target_pairs={{0,2},{1,3},{2,0},{3,1},{4,6},{5,7},{6,4},{7,5},{8,10},{9,11},{10,... | collective-permute-start | bytes 2506760 | tf_op jit(solution)/shard_map/ppermute | solution.py:35
  30.5 13.8 %collective-permute-start.5 = (bf16[4,264,128]{2,1,0:T(8,128)(2,1)S(1)}, bf16[4,264,128]{2,1,0:T(8,128)(2,1)S(1)}, u32[]{:S(2)}, u32[]{:S(2)}) collective-permute-start(bf16[4,264,128]{2,1,0:T(8,128)(2,1)S(1)} %get-tuple-element.44), channel_id=1, source_target_pairs={{0,4},{1,5},{2,6},{3,7},{4,0},{5,1},{6,2},{7,3},{8,12},{9,13},{10,... | collective-permute-start | bytes 811016 | tf_op jit(solution)/shard_map/ppermute | solution.py:35
  30.5 22.0 %collective-permute-start.6 = (bf16[4,264,128]{2,1,0:T(8,128)(2,1)S(1)}, bf16[4,264,128]{2,1,0:T(8,128)(2,1)S(1)}, u32[]{:S(2)}, u32[]{:S(2)}) collective-permute-start(bf16[4,264,128]{2,1,0:T(8,128)(2,1)S(1)} %get-tuple-element.45), channel_id=1, source_target_pairs={{0,8},{1,9},{2,10},{3,11},{4,12},{5,13},{6,14},{7,15},{8,0},{9,1},... | collective-permute-start | bytes 811016 | tf_op jit(solution)/shard_map/ppermute | solution.py:35
  33.6 18.9 %collective-permute-start.7 = (bf16[4,264,128]{2,1,0:T(8,128)(2,1)S(1)}, bf16[4,264,128]{2,1,0:T(8,128)(2,1)S(1)}, u32[]{:S(2)}, u32[]{:S(2)}) collective-permute-start(bf16[4,264,128]{2,1,0:T(8,128)(2,1)S(1)} %get-tuple-element.46), channel_id=1, source_target_pairs={{0,12},{1,13},{2,14},{3,15},{4,8},{5,9},{6,10},{7,11},{8,4},{9,5},... | collective-permute-start | bytes 811016 | tf_op jit(solution)/shard_map/ppermute | solution.py:35
  52.6 2.4 %collective-permute-start.10 = (bf16[192,2176]{1,0:T(8,128)(2,1)S(1)}, bf16[192,2176]{1,0:T(8,128)(2,1)S(1)}, u32[]{:S(2)}, u32[]{:S(2)}) collective-permute-start(bf16[192,2176]{1,0:T(8,128)(2,1)S(1)} %collective-permute-done.8.x_ref.refs_1_), channel_id=1, source_target_pairs={{0,1},{1,0},{2,3},{3,2},{4,5},{5,4},{6,7},{7,6},{8,9},{9,8},{10,11... | collective-permute-start | bytes 2506760 | tf_op jit(solution)/shard_map/ppermute | solution.py:35
  53.8 3.8 %copy-start.2 = (bf16[1,768,2048]{2,1,0:T(8,128)(2,1)S(1)}, bf16[1,768,2048]{2,1,0:T(8,128)(2,1)}, u32[]{:S(2)}) copy-start(bf16[1,768,2048]{2,1,0:T(8,128)(2,1)} %param.15) | copy-start | bytes 9437188
  59.8 5.2 %collective-permute-start.14 = (bf16[128,2048]{1,0:T(8,128)(2,1)S(1)}, bf16[128,2048]{1,0:T(8,128)(2,1)S(1)}, u32[]{:S(2)}, u32[]{:S(2)}) collective-permute-start(bf16[128,2048]{1,0:T(8,128)(2,1)S(1)} %get-tuple-element.68), channel_id=1, source_target_pairs={{0,1},{1,0},{2,3},{3,2},{4,5},{5,4},{6,7},{7,6},{8,9},{9,8},{10,11... | collective-permute-start | bytes 1572872 | tf_op jit(solution)/shard_map/ppermute | solution.py:35
  62.2 11.1 %collective-permute-start.12 = (bf16[128,2048]{1,0:T(8,128)(2,1)S(1)}, bf16[128,2048]{1,0:T(8,128)(2,1)S(1)}, u32[]{:S(2)}, u32[]{:S(2)}) collective-permute-start(bf16[128,2048]{1,0:T(8,128)(2,1)S(1)} %get-tuple-element.66), channel_id=1, source_target_pairs={{0,1},{1,0},{2,3},{3,2},{4,5},{5,4},{6,7},{7,6},{8,9},{9,8},{10,11... | collective-permute-start | bytes 1572872 | tf_op jit(solution)/shard_map/ppermute | solution.py:35
  64.8 8.6 %collective-permute-start.11 = (bf16[128,2048]{1,0:T(8,128)(2,1)S(1)}, bf16[128,2048]{1,0:T(8,128)(2,1)S(1)}, u32[]{:S(2)}, u32[]{:S(2)}) collective-permute-start(bf16[128,2048]{1,0:T(8,128)(2,1)S(1)} %get-tuple-element.64), channel_id=1, source_target_pairs={{0,1},{1,0},{2,3},{3,2},{4,5},{5,4},{6,7},{7,6},{8,9},{9,8},{10,11... | collective-permute-start | bytes 1572872 | tf_op jit(solution)/shard_map/ppermute | solution.py:35
  65.2 11.8 %collective-permute-start.15 = (bf16[32,2048]{1,0:T(8,128)(2,1)S(1)}, bf16[32,2048]{1,0:T(8,128)(2,1)S(1)}, u32[]{:S(2)}, u32[]{:S(2)}) collective-permute-start(bf16[32,2048]{1,0:T(8,128)(2,1)S(1)} %bitcast.109), channel_id=1, source_target_pairs={{0,4},{1,5},{2,6},{3,7},{4,0},{5,1},{6,2},{7,3},{8,12},{9,13},{10,... | collective-permute-start | bytes 393224 | tf_op jit(solution)/shard_map/ppermute | solution.py:35
  70.8 12.9 %collective-permute-start.16 = (bf16[32,2048]{1,0:T(8,128)(2,1)S(1)}, bf16[32,2048]{1,0:T(8,128)(2,1)S(1)}, u32[]{:S(2)}, u32[]{:S(2)}) collective-permute-start(bf16[32,2048]{1,0:T(8,128)(2,1)S(1)} %bitcast.108), channel_id=1, source_target_pairs={{0,8},{1,9},{2,10},{3,11},{4,12},{5,13},{6,14},{7,15},{8,0},{9,1},... | collective-permute-start | bytes 393224 | tf_op jit(solution)/shard_map/ppermute | solution.py:35
  71.8 11.9 %collective-permute-start.17 = (bf16[32,2048]{1,0:T(8,128)(2,1)S(1)}, bf16[32,2048]{1,0:T(8,128)(2,1)S(1)}, u32[]{:S(2)}, u32[]{:S(2)}) collective-permute-start(bf16[32,2048]{1,0:T(8,128)(2,1)S(1)} %bitcast.107), channel_id=1, source_target_pairs={{0,12},{1,13},{2,14},{3,15},{4,8},{5,9},{6,10},{7,11},{8,4},{9,5},... | collective-permute-start | bytes 393224 | tf_op jit(solution)/shard_map/ppermute | solution.py:35
  73.6 13.7 %collective-permute-start.13 = (bf16[128,2048]{1,0:T(8,128)(2,1)S(1)}, bf16[128,2048]{1,0:T(8,128)(2,1)S(1)}, u32[]{:S(2)}, u32[]{:S(2)}) collective-permute-start(bf16[128,2048]{1,0:T(8,128)(2,1)S(1)} %bitcast.103), channel_id=1, source_target_pairs={{0,2},{1,3},{2,0},{3,1},{4,6},{5,7},{6,4},{7,5},{8,10},{9,11},{10,... | collective-permute-start | bytes 1572872 | tf_op jit(solution)/shard_map/ppermute | solution.py:35
  87.5 5.2 %collective-permute-start.21 = (bf16[16,2048]{1,0:T(8,128)(2,1)S(1)}, bf16[16,2048]{1,0:T(8,128)(2,1)S(1)}, u32[]{:S(2)}, u32[]{:S(2)}) collective-permute-start(bf16[16,2048]{1,0:T(8,128)(2,1)S(1)} %slice.160), channel_id=1, source_target_pairs={{0,2},{1,3},{2,0},{3,1},{4,6},{5,7},{6,4},{7,5},{8,10},{9,11},{10,... | collective-permute-start | bytes 196616 | tf_op jit(solution)/shard_map/ppermute | solution.py:35
  88.2 5.8 %collective-permute-start.18 = (bf16[32,2048]{1,0:T(8,128)(2,1)S(1)}, bf16[32,2048]{1,0:T(8,128)(2,1)S(1)}, u32[]{:S(2)}, u32[]{:S(2)}) collective-permute-start(bf16[32,2048]{1,0:T(8,128)(2,1)S(1)} %bitcast.112), channel_id=1, source_target_pairs={{0,4},{1,5},{2,6},{3,7},{4,0},{5,1},{6,2},{7,3},{8,12},{9,13},{10,... | collective-permute-start | bytes 393224 | tf_op jit(solution)/shard_map/ppermute | solution.py:35
  89.0 11.4 %collective-permute-start.19 = (bf16[32,2048]{1,0:T(8,128)(2,1)S(1)}, bf16[32,2048]{1,0:T(8,128)(2,1)S(1)}, u32[]{:S(2)}, u32[]{:S(2)}) collective-permute-start(bf16[32,2048]{1,0:T(8,128)(2,1)S(1)} %bitcast.111), channel_id=1, source_target_pairs={{0,8},{1,9},{2,10},{3,11},{4,12},{5,13},{6,14},{7,15},{8,0},{9,1},... | collective-permute-start | bytes 393224 | tf_op jit(solution)/shard_map/ppermute | solution.py:35
  91.2 9.2 %collective-permute-start.20 = (bf16[32,2048]{1,0:T(8,128)(2,1)S(1)}, bf16[32,2048]{1,0:T(8,128)(2,1)S(1)}, u32[]{:S(2)}, u32[]{:S(2)}) collective-permute-start(bf16[32,2048]{1,0:T(8,128)(2,1)S(1)} %bitcast.110), channel_id=1, source_target_pairs={{0,12},{1,13},{2,14},{3,15},{4,8},{5,9},{6,10},{7,11},{8,4},{9,5},... | collective-permute-start | bytes 393224 | tf_op jit(solution)/shard_map/ppermute | solution.py:35

commit v22 on v21

--- a/solution.py
+++ b/solution.py
@@ -305,6 +305,8 @@
     summed = []
     for s in range(steps):
         kept, sent = finish_step(place, pieces, base, s * span, span, low_rank, down_weight[0])
+        if s == steps - 2:
+            pieces, kept = lax.optimization_barrier((pieces, kept))
         total = kept + swap(sent, owners, 1, 1).astype(jnp.float32)
         summed.append(total.reshape(middle, outer, rows, width))
     first = jnp.stack(summed[:-1], axis=1).reshape(-1, width)

time: 101 us -> 99.6 us (0.986)
  transfers between devices with their start and end apart: 22 -> 22, of which waited for: 11 -> 10; matrix products, arithmetic and copies ran while one was open for 2% -> 2% of each run, Pallas kernels for 8% -> 8%
where the time goes in v22:
time: 99.6 us; the launch traced here: 99.4 us
  waiting for transfers between devices  50.6 us (51%)
  starting transfers between devices  27.1 us (27%)
  Pallas kernels  18 us (18%)
  other arithmetic  3 us (3%)
    ppermute x22, waiting for transfers between devices, swap(): return lax.ppermute(x, 'expert', [(i, i ^ k * stride) for i in range(n)])  50.6 us
    ppermute x22, starting transfers between devices, swap(): return lax.ppermute(x, 'expert', [(i, i ^ k * stride) for i in range(n)])  27.1 us
    pallas_call x3, Pallas kernels, finish_step(): pl.pallas_call(functools.partial(finish_kernel, len(pieces), first, rows)...  6.49 us
    pallas_call x2, Pallas kernels, base_products(): pl.pallas_call(base_kernel, out_shape=[out, out], in_specs=[pl.BlockSpec(...  5.28 us
    pallas_call x1, Pallas kernels, order_factors(): pl.pallas_call(order_kernel, out_shape=[shape] * cores, in_specs=[pl.Bloc...  3.07 us
  transfers between devices with their start and end apart: 22, of which 10 were waited for; matrix products, arithmetic and copies ran while one was open for 2% of the time, Pallas kernels for 8%

profile of v22, /device:TPU:0, one launch (start us, length us, event | category | flops | bytes accessed | tf_op | source)
XLA Modules:
  0.0 99.4 jit_solution(11505410470886501808)
XLA Ops:
  0.0 2.0 %payload.1 = bf16[48,2176]{1,0:T(8,128)(2,1)} custom-call(bf16[3,16,2048]{2,1,0:T(8,128)(2,1)} %hidden_ref.1, s32[3,8,16]{2,1,0:T(8,128)} %bitcast.113, f32[3,8,16]{2,1,0:T(8,128)} %bitcast.114), custom_call_target="tpu_custom_call" | custom-call | flops 1 | bytes 1 | tf_op jit(solution)/shard_map/payload/pallas_call | solution.py:73
  2.0 3.1 %order_factors.1 = (bf16[2,4,264,128]{3,2,1,0:T(8,128)(2,1)}, bf16[2,4,264,128]{3,2,1,0:T(8,128)(2,1)}) custom-call(s32[1]{0:T(128)} %bitcast.place_ref, s32[16]{0:T(128)} %placement_ref.1, bf16[16,33792]{1,0:T(8,128)(2,1)} %factors_ref), custom_call_target="tpu_custom_call" | custom-call | flops 8589934592 | bytes 1 | tf_op jit(solution)/shard_map/order_factors/pallas_call | solution.py:109
  5.5 4.6 %collective-permute-start.2 = (bf16[48,2176]{1,0:T(8,128)(2,1)S(1)}, bf16[48,2176]{1,0:T(8,128)(2,1)S(1)}, u32[]{:S(2)}, u32[]{:S(2)}) collective-permute-start(bf16[48,2176]{1,0:T(8,128)(2,1)S(1)} %copy-done.3), channel_id=1, source_target_pairs={{0,12},{1,13},{2,14},{3,15},{4,8},{5,9},{6,10},{7,11},{8,4},{9,5},... | collective-permute-start | bytes 626696 | tf_op jit(solution)/shard_map/ppermute | solution.py:35
  10.1 0.6 collective-permute-start
  10.8 1.3 %fusion.3 = (bf16[2,4,264,128]{3,2,0,1:T(8,128)(2,1)S(1)}, bf16[2,4,264,128]{3,2,0,1:T(8,128)(2,1)S(1)}) fusion(bf16[1,2,4,264,128]{4,3,0,2,1:T(8,128)(2,1)} %bitcast.101, bf16[1,2,4,264,128]{4,3,0,2,1:T(8,128)(2,1)S(1)} %bitcast.102), kind=kLoop, calls=%fused_computation.14 | loop fusion | flops 540672 | bytes 2162688 | tf_op jit(solution)/shard_map/squeeze | solution.py:287
  12.0 1.7 %collective-permute-start.4 = (bf16[2,4,264,128]{3,2,0,1:T(8,128)(2,1)S(1)}, bf16[2,4,264,128]{3,2,0,1:T(8,128)(2,1)S(1)}, u32[]{:S(2)}, u32[]{:S(2)}) collective-permute-start(bf16[2,4,264,128]{3,2,0,1:T(8,128)(2,1)S(1)} %get-tuple-element.82), channel_id=1, source_target_pairs={{0,2},{1,3},{2,0},{3,1},{4,6},{5,7},{6,4},{7,5},{8,10},{9,11},{10,... | collective-permute-start | bytes 1622024 | tf_op jit(solution)/shard_map/ppermute | solution.py:35
  13.8 2.5 %collective-permute-done.2 = bf16[48,2176]{1,0:T(8,128)(2,1)S(1)} collective-permute-done((bf16[48,2176]{1,0:T(8,128)(2,1)S(1)}, bf16[48,2176]{1,0:T(8,128)(2,1)S(1)}, u32[]{:S(2)}, u32[]{:S(2)}) %collective-permute-start.2) | collective-permute-done | bytes 208928 | tf_op jit(solution)/shard_map/ppermute | solution.py:35
  16.3 12.2 %collective-permute-done.1 = bf16[48,2176]{1,0:T(8,128)(2,1)S(1)} collective-permute-done((bf16[48,2176]{1,0:T(8,128)(2,1)S(1)}, bf16[48,2176]{1,0:T(8,128)(2,1)S(1)}, u32[]{:S(2)}, u32[]{:S(2)}) %collective-permute-start.1) | collective-permute-done | bytes 208928 | tf_op jit(solution)/shard_map/ppermute | solution.py:35
  29.0 1.6 %collective-permute-start.8 = (bf16[192,2176]{1,0:T(8,128)(2,1)S(1)}, bf16[192,2176]{1,0:T(8,128)(2,1)S(1)}, u32[]{:S(2)}, u32[]{:S(2)}) collective-permute-start(bf16[192,2176]{1,0:T(8,128)(2,1)S(1)} %bitcast.82), channel_id=1, source_target_pairs={{0,2},{1,3},{2,0},{3,1},{4,6},{5,7},{6,4},{7,5},{8,10},{9,11},{10,... | collective-permute-start | bytes 2506760 | tf_op jit(solution)/shard_map/ppermute | solution.py:35
  30.6 3.0 %collective-permute-start.6 = (bf16[4,264,128]{2,1,0:T(8,128)(2,1)S(1)}, bf16[4,264,128]{2,1,0:T(8,128)(2,1)S(1)}, u32[]{:S(2)}, u32[]{:S(2)}) collective-permute-start(bf16[4,264,128]{2,1,0:T(8,128)(2,1)S(1)} %get-tuple-element.50), channel_id=1, source_target_pairs={{0,8},{1,9},{2,10},{3,11},{4,12},{5,13},{6,14},{7,15},{8,0},{9,1},... | collective-permute-start | bytes 811016 | tf_op jit(solution)/shard_map/ppermute | solution.py:35
  33.6 1.3 %collective-permute-start.7 = (bf16[4,264,128]{2,1,0:T(8,128)(2,1)S(1)}, bf16[4,264,128]{2,1,0:T(8,128)(2,1)S(1)}, u32[]{:S(2)}, u32[]{:S(2)}) collective-permute-start(bf16[4,264,128]{2,1,0:T(8,128)(2,1)S(1)} %get-tuple-element.51), channel_id=1, source_target_pairs={{0,12},{1,13},{2,14},{3,15},{4,8},{5,9},{6,10},{7,11},{8,4},{9,5},... | collective-permute-start | bytes 811016 | tf_op jit(solution)/shard_map/ppermute | solution.py:35
  34.9 2.6 %base_products.2 = (f32[384,768]{1,0:T(8,128)S(1)}, f32[384,768]{1,0:T(8,128)S(1)}) custom-call(bf16[192,2176]{1,0:T(8,128)(2,1)S(1)} %bitcast.83, bf16[192,2176]{1,0:T(8,128)(2,1)S(1)} %collective-permute-done.9.other_ref.refs_2_, bf16[2048,768]{1,0:T(8,128)(2,1)S(1)} %bitcast.77, bf16[2048,768]{1,0:T(8,128)(2,1)S(1)} %bitcast.79), custom_call_target="tpu_custom_call" | custom-call | flops 1 | bytes 1 | tf_op jit(solution)/shard_map/base_products/pallas_call | solution.py:203
  37.6 6.8 %collective-permute-done.5.refs_1_ = bf16[4,264,128]{2,1,0:T(8,128)(2,1)S(1)} collective-permute-done((bf16[4,264,128]{2,1,0:T(8,128)(2,1)S(1)}, bf16[4,264,128]{2,1,0:T(8,128)(2,1)S(1)}, u32[]{:S(2)}, u32[]{:S(2)}) %collective-permute-start.5) | collective-permute-done | bytes 270368 | tf_op jit(solution)/shard_map/ppermute | solution.py:35
  44.4 8.1 %collective-permute-done.6.refs_2_ = bf16[4,264,128]{2,1,0:T(8,128)(2,1)S(1)} collective-permute-done((bf16[4,264,128]{2,1,0:T(8,128)(2,1)S(1)}, bf16[4,264,128]{2,1,0:T(8,128)(2,1)S(1)}, u32[]{:S(2)}, u32[]{:S(2)}) %collective-permute-start.6) | collective-permute-done | bytes 270368 | tf_op jit(solution)/shard_map/ppermute | solution.py:35
  52.5 1.2 %relayout_factors.1 = (bf16[2048,128]{1,0:T(8,128)(2,1)S(1)}, bf16[64,768]{1,0:T(8,128)(2,1)S(1)}, bf16[64,768]{1,0:T(8,128)(2,1)S(1)}, bf16[768,128]{1,0:T(8,128)(2,1)S(1)}, bf16[64,2048]{1,0:T(8,128)(2,1)S(1)}) custom-call(s32[1]{0:T(128)} %bitcast.place_ref, bf16[4,264,128]{2,1,0:T(8,128)(2,1)S(1)} %get-tuple-element.59.refs_0_, ...), custom_call_target="tpu_custom_call" | custom-call | flops 1 | bytes 1 | tf_op jit(solution)/shard_map/relayout_factors/pallas_call | solution.py:177
  53.8 1.1 %collective-permute-done.10.other_ref.refs_3_ = bf16[192,2176]{1,0:T(8,128)(2,1)S(1)} collective-permute-done((bf16[192,2176]{1,0:T(8,128)(2,1)S(1)}, bf16[192,2176]{1,0:T(8,128)(2,1)S(1)}, u32[]{:S(2)}, u32[]{:S(2)}) %collective-permute-start.10) | collective-permute-done | bytes 835616 | tf_op jit(solution)/shard_map/ppermute | solution.py:35
  54.9 2.7 %base_products.3 = (f32[384,768]{1,0:T(8,128)S(1)}, f32[384,768]{1,0:T(8,128)S(1)}) custom-call(bf16[192,2176]{1,0:T(8,128)(2,1)S(1)} %collective-permute-done.8.x_ref.refs_1_, bf16[192,2176]{1,0:T(8,128)(2,1)S(1)} %collective-permute-done.10.other_ref.refs_3_, bf16[2048,768]{1,0:T(8,128)(2,1)S(1)} %bitcast.78, bf16[2048,768]{1,0:T(8,128)(2,1)S(1)} %bitcast.80), custom_call_target="tpu_custom_call" | custom-call | flops 1 | bytes 1 | tf_op jit(solution)/shard_map/base_products/pallas_call | solution.py:203
  57.6 2.2 %finish_step.3 = (f32[128,2048]{1,0:T(8,128)S(1)}, bf16[128,2048]{1,0:T(8,128)(2,1)S(1)}) custom-call(s32[1]{0:T(128)} %bitcast.place_ref, bf16[192,2176]{1,0:T(8,128)(2,1)S(1)} %bitcast.84, bf16[192,2176]{1,0:T(8,128)(2,1)S(1)} %collective-permute-done.8.x_ref.refs_1_, bf16[192,2176]{1,0:T(8,128)(2,1)S(1)} %collective-permute-done.9.other_ref.refs_2_, ...), custom_call_target="tpu_custom_call" | custom-call | flops 8589934592 | bytes 1 | tf_op jit(solution)/shard_map/finish_step/pallas_call | solution.py:248
  59.9 2.2 %finish_step.4 = (f32[128,2048]{1,0:T(8,128)S(1)}, bf16[128,2048]{1,0:T(8,128)(2,1)S(1)}) custom-call(s32[1]{0:T(128)} %bitcast.place_ref, bf16[192,2176]{1,0:T(8,128)(2,1)S(1)} %bitcast.85, bf16[192,2176]{1,0:T(8,128)(2,1)S(1)} %collective-permute-done.8.x_ref.refs_1_, bf16[192,2176]{1,0:T(8,128)(2,1)S(1)} %collective-permute-done.9.other_ref.refs_2_, ...), custom_call_target="tpu_custom_call" | custom-call | flops 8589934592 | bytes 1 | tf_op jit(solution)/shard_map/finish_step/pallas_call | solution.py:248
  62.6 2.2 %finish_step.5 = (f32[128,2048]{1,0:T(8,128)S(1)}, bf16[128,2048]{1,0:T(8,128)(2,1)S(1)}) custom-call(s32[1]{0:T(128)} %bitcast.place_ref, bf16[192,2176]{1,0:T(8,128)(2,1)S(1)} %bitcast.86, bf16[192,2176]{1,0:T(8,128)(2,1)S(1)} %collective-permute-done.8.x_ref.refs_1_, bf16[192,2176]{1,0:T(8,128)(2,1)S(1)} %collective-permute-done.9.other_ref.refs_2_, ...), custom_call_target="tpu_custom_call" | custom-call | flops 8589934592 | bytes 1 | tf_op jit(solution)/shard_map/finish_step/pallas_call | solution.py:248
  65.2 0.6 collective-permute-start.13
  65.8 0.9 collective-permute-done.14
  66.9 2.4 %collective-permute-start.17 = (bf16[32,2048]{1,0:T(8,128)(2,1)S(1)}, bf16[32,2048]{1,0:T(8,128)(2,1)S(1)}, u32[]{:S(2)}, u32[]{:S(2)}) collective-permute-start(bf16[32,2048]{1,0:T(8,128)(2,1)S(1)} %bitcast.112), channel_id=1, source_target_pairs={{0,12},{1,13},{2,14},{3,15},{4,8},{5,9},{6,10},{7,11},{8,4},{9,5},... | collective-permute-start | bytes 393224 | tf_op jit(solution)/shard_map/ppermute | solution.py:35
  69.4 4.7 %collective-permute-start.16 = (bf16[32,2048]{1,0:T(8,128)(2,1)S(1)}, bf16[32,2048]{1,0:T(8,128)(2,1)S(1)}, u32[]{:S(2)}, u32[]{:S(2)}) collective-permute-start(bf16[32,2048]{1,0:T(8,128)(2,1)S(1)} %bitcast.111), channel_id=1, source_target_pairs={{0,8},{1,9},{2,10},{3,11},{4,12},{5,13},{6,14},{7,15},{8,0},{9,1},... | collective-permute-start | bytes 393224 | tf_op jit(solution)/shard_map/ppermute | solution.py:35
  74.3 8.8 %collective-permute-done.16 = bf16[32,2048]{1,0:T(8,128)(2,1)S(1)} collective-permute-done((bf16[32,2048]{1,0:T(8,128)(2,1)S(1)}, bf16[32,2048]{1,0:T(8,128)(2,1)S(1)}, u32[]{:S(2)}, u32[]{:S(2)}) %collective-permute-start.16) | collective-permute-done | bytes 131104 | tf_op jit(solution)/shard_map/ppermute | solution.py:35
  83.4 0.7 collective-permute-start.21
  84.3 2.4 %collective-permute-start.20 = (bf16[32,2048]{1,0:T(8,128)(2,1)S(1)}, bf16[32,2048]{1,0:T(8,128)(2,1)S(1)}, u32[]{:S(2)}, u32[]{:S(2)}) collective-permute-start(bf16[32,2048]{1,0:T(8,128)(2,1)S(1)} %bitcast.110), channel_id=1, source_target_pairs={{0,12},{1,13},{2,14},{3,15},{4,8},{5,9},{6,10},{7,11},{8,4},{9,5},... | collective-permute-start | bytes 393224 | tf_op jit(solution)/shard_map/ppermute | solution.py:35
  86.7 0.9 collective-permute-start.19
  87.5 1.2 %collective-permute-start.18 = (bf16[32,2048]{1,0:T(8,128)(2,1)S(1)}, bf16[32,2048]{1,0:T(8,128)(2,1)S(1)}, u32[]{:S(2)}, u32[]{:S(2)}) collective-permute-start(bf16[32,2048]{1,0:T(8,128)(2,1)S(1)} %bitcast.107), channel_id=1, source_target_pairs={{0,4},{1,5},{2,6},{3,7},{4,0},{5,1},{6,2},{7,3},{8,12},{9,13},{10,... | collective-permute-start | bytes 393224 | tf_op jit(solution)/shard_map/ppermute | solution.py:35
  88.7 3.8 %collective-permute-done.20 = bf16[32,2048]{1,0:T(8,128)(2,1)S(1)} collective-permute-done((bf16[32,2048]{1,0:T(8,128)(2,1)S(1)}, bf16[32,2048]{1,0:T(8,128)(2,1)S(1)}, u32[]{:S(2)}, u32[]{:S(2)}) %collective-permute-start.20) | collective-permute-done | bytes 131104 | tf_op jit(solution)/shard_map/ppermute | solution.py:35
  92.5 6.1 %collective-permute-done.19 = bf16[32,2048]{1,0:T(8,128)(2,1)S(1)} collective-permute-done((bf16[32,2048]{1,0:T(8,128)(2,1)S(1)}, bf16[32,2048]{1,0:T(8,128)(2,1)S(1)}, u32[]{:S(2)}, u32[]{:S(2)}) %collective-permute-start.19) | collective-permute-done | bytes 131104 | tf_op jit(solution)/shard_map/ppermute | solution.py:35
  98.7 0.7 pad_maximum_fusion.7
  (52 shorter events, 2.9 us)
Async XLA Ops:
  2.0 3.5 %copy-start.3 = (bf16[48,2176]{1,0:T(8,128)(2,1)S(1)}, bf16[48,2176]{1,0:T(8,128)(2,1)}, u32[]{:S(2)}) copy-start(bf16[48,2176]{1,0:T(8,128)(2,1)} %payload.1) | copy-start | bytes 626692
  5.0 5.7 %collective-permute-start.3 = (bf16[2,4,264,128]{3,2,1,0:T(8,128)(2,1)}, bf16[2,4,264,128]{3,2,1,0:T(8,128)(2,1)S(1)}, u32[]{:S(2)}, u32[]{:S(2)}) collective-permute-start(bf16[2,4,264,128]{3,2,1,0:T(8,128)(2,1)} %get-tuple-element.46), channel_id=1, source_target_pairs={{0,1},{1,0},{2,3},{3,2},{4,5},{5,4},{6,7},{7,6},{8,9},{9,8},{10,11... | collective-permute-start | bytes 1622024 | tf_op jit(solution)/shard_map/ppermute | solution.py:35
  5.5 10.8 %collective-permute-start.2 = (bf16[48,2176]{1,0:T(8,128)(2,1)S(1)}, bf16[48,2176]{1,0:T(8,128)(2,1)S(1)}, u32[]{:S(2)}, u32[]{:S(2)}) collective-permute-start(bf16[48,2176]{1,0:T(8,128)(2,1)S(1)} %copy-done.3), channel_id=1, source_target_pairs={{0,12},{1,13},{2,14},{3,15},{4,8},{5,9},{6,10},{7,11},{8,4},{9,5},... | collective-permute-start | bytes 626696 | tf_op jit(solution)/shard_map/ppermute | solution.py:35
  10.1 18.4 %collective-permute-start.1 = (bf16[48,2176]{1,0:T(8,128)(2,1)S(1)}, bf16[48,2176]{1,0:T(8,128)(2,1)S(1)}, u32[]{:S(2)}, u32[]{:S(2)}) collective-permute-start(bf16[48,2176]{1,0:T(8,128)(2,1)S(1)} %copy-done.3), channel_id=1, source_target_pairs={{0,8},{1,9},{2,10},{3,11},{4,12},{5,13},{6,14},{7,15},{8,0},{9,1},... | collective-permute-start | bytes 626696 | tf_op jit(solution)/shard_map/ppermute | solution.py:35
  10.1 18.4 %collective-permute-start = (bf16[48,2176]{1,0:T(8,128)(2,1)S(1)}, bf16[48,2176]{1,0:T(8,128)(2,1)S(1)}, u32[]{:S(2)}, u32[]{:S(2)}) collective-permute-start(bf16[48,2176]{1,0:T(8,128)(2,1)S(1)} %copy-done.3), channel_id=1, source_target_pairs={{0,4},{1,5},{2,6},{3,7},{4,0},{5,1},{6,2},{7,3},{8,12},{9,13},{10,... | collective-permute-start | bytes 626696 | tf_op jit(solution)/shard_map/ppermute | solution.py:35
  10.8 24.2 %copy-start.1 = (bf16[1,2048,768]{2,1,0:T(8,128)(2,1)S(1)}, bf16[1,2048,768]{2,1,0:T(8,128)(2,1)}, u32[]{:S(2)}) copy-start(bf16[1,2048,768]{2,1,0:T(8,128)(2,1)} %param.14) | copy-start | bytes 9437188
  12.0 16.7 %collective-permute-start.4 = (bf16[2,4,264,128]{3,2,0,1:T(8,128)(2,1)S(1)}, bf16[2,4,264,128]{3,2,0,1:T(8,128)(2,1)S(1)}, u32[]{:S(2)}, u32[]{:S(2)}) collective-permute-start(bf16[2,4,264,128]{3,2,0,1:T(8,128)(2,1)S(1)} %get-tuple-element.82), channel_id=1, source_target_pairs={{0,2},{1,3},{2,0},{3,1},{4,6},{5,7},{6,4},{7,5},{8,10},{9,11},{10,... | collective-permute-start | bytes 1622024 | tf_op jit(solution)/shard_map/ppermute | solution.py:35
  28.7 6.2 %copy-start = (bf16[1,2048,768]{2,1,0:T(8,128)(2,1)S(1)}, bf16[1,2048,768]{2,1,0:T(8,128)(2,1)}, u32[]{:S(2)}) copy-start(bf16[1,2048,768]{2,1,0:T(8,128)(2,1)} %param.13) | copy-start | bytes 9437188
  28.9 6.1 %collective-permute-start.9 = (bf16[192,2176]{1,0:T(8,128)(2,1)S(1)}, bf16[192,2176]{1,0:T(8,128)(2,1)S(1)}, u32[]{:S(2)}, u32[]{:S(2)}) collective-permute-start(bf16[192,2176]{1,0:T(8,128)(2,1)S(1)} %bitcast.81), channel_id=1, source_target_pairs={{0,1},{1,0},{2,3},{3,2},{4,5},{5,4},{6,7},{7,6},{8,9},{9,8},{10,11... | collective-permute-start | bytes 2506760 | tf_op jit(solution)/shard_map/ppermute | solution.py:35
  29.0 23.6 %collective-permute-start.8 = (bf16[192,2176]{1,0:T(8,128)(2,1)S(1)}, bf16[192,2176]{1,0:T(8,128)(2,1)S(1)}, u32[]{:S(2)}, u32[]{:S(2)}) collective-permute-start(bf16[192,2176]{1,0:T(8,128)(2,1)S(1)} %bitcast.82), channel_id=1, source_target_pairs={{0,2},{1,3},{2,0},{3,1},{4,6},{5,7},{6,4},{7,5},{8,10},{9,11},{10,... | collective-permute-start | bytes 2506760 | tf_op jit(solution)/shard_map/ppermute | solution.py:35
  30.5 13.8 %collective-permute-start.5 = (bf16[4,264,128]{2,1,0:T(8,128)(2,1)S(1)}, bf16[4,264,128]{2,1,0:T(8,128)(2,1)S(1)}, u32[]{:S(2)}, u32[]{:S(2)}) collective-permute-start(bf16[4,264,128]{2,1,0:T(8,128)(2,1)S(1)} %get-tuple-element.49), channel_id=1, source_target_pairs={{0,4},{1,5},{2,6},{3,7},{4,0},{5,1},{6,2},{7,3},{8,12},{9,13},{10,... | collective-permute-start | bytes 811016 | tf_op jit(solution)/shard_map/ppermute | solution.py:35
  30.6 22.0 %collective-permute-start.6 = (bf16[4,264,128]{2,1,0:T(8,128)(2,1)S(1)}, bf16[4,264,128]{2,1,0:T(8,128)(2,1)S(1)}, u32[]{:S(2)}, u32[]{:S(2)}) collective-permute-start(bf16[4,264,128]{2,1,0:T(8,128)(2,1)S(1)} %get-tuple-element.50), channel_id=1, source_target_pairs={{0,8},{1,9},{2,10},{3,11},{4,12},{5,13},{6,14},{7,15},{8,0},{9,1},... | collective-permute-start | bytes 811016 | tf_op jit(solution)/shard_map/ppermute | solution.py:35
  33.6 18.9 %collective-permute-start.7 = (bf16[4,264,128]{2,1,0:T(8,128)(2,1)S(1)}, bf16[4,264,128]{2,1,0:T(8,128)(2,1)S(1)}, u32[]{:S(2)}, u32[]{:S(2)}) collective-permute-start(bf16[4,264,128]{2,1,0:T(8,128)(2,1)S(1)} %get-tuple-element.51), channel_id=1, source_target_pairs={{0,12},{1,13},{2,14},{3,15},{4,8},{5,9},{6,10},{7,11},{8,4},{9,5},... | collective-permute-start | bytes 811016 | tf_op jit(solution)/shard_map/ppermute | solution.py:35
  52.5 2.4 %collective-permute-start.10 = (bf16[192,2176]{1,0:T(8,128)(2,1)S(1)}, bf16[192,2176]{1,0:T(8,128)(2,1)S(1)}, u32[]{:S(2)}, u32[]{:S(2)}) collective-permute-start(bf16[192,2176]{1,0:T(8,128)(2,1)S(1)} %collective-permute-done.8.x_ref.refs_1_), channel_id=1, source_target_pairs={{0,1},{1,0},{2,3},{3,2},{4,5},{5,4},{6,7},{7,6},{8,9},{9,8},{10,11... | collective-permute-start | bytes 2506760 | tf_op jit(solution)/shard_map/ppermute | solution.py:35
  53.8 3.8 %copy-start.2 = (bf16[1,768,2048]{2,1,0:T(8,128)(2,1)S(1)}, bf16[1,768,2048]{2,1,0:T(8,128)(2,1)}, u32[]{:S(2)}) copy-start(bf16[1,768,2048]{2,1,0:T(8,128)(2,1)} %param.15) | copy-start | bytes 9437188
  59.8 5.2 %collective-permute-start.11 = (bf16[128,2048]{1,0:T(8,128)(2,1)S(1)}, bf16[128,2048]{1,0:T(8,128)(2,1)S(1)}, u32[]{:S(2)}, u32[]{:S(2)}) collective-permute-start(bf16[128,2048]{1,0:T(8,128)(2,1)S(1)} %get-tuple-element.69), channel_id=1, source_target_pairs={{0,1},{1,0},{2,3},{3,2},{4,5},{5,4},{6,7},{7,6},{8,9},{9,8},{10,11... | collective-permute-start | bytes 1572872 | tf_op jit(solution)/shard_map/ppermute | solution.py:35
  62.1 2.9 %collective-permute-start.12 = (bf16[128,2048]{1,0:T(8,128)(2,1)S(1)}, bf16[128,2048]{1,0:T(8,128)(2,1)S(1)}, u32[]{:S(2)}, u32[]{:S(2)}) collective-permute-start(bf16[128,2048]{1,0:T(8,128)(2,1)S(1)} %get-tuple-element.72), channel_id=1, source_target_pairs={{0,1},{1,0},{2,3},{3,2},{4,5},{5,4},{6,7},{7,6},{8,9},{9,8},{10,11... | collective-permute-start | bytes 1572872 | tf_op jit(solution)/shard_map/ppermute | solution.py:35
  64.7 2.0 %collective-permute-start.14 = (bf16[128,2048]{1,0:T(8,128)(2,1)S(1)}, bf16[128,2048]{1,0:T(8,128)(2,1)S(1)}, u32[]{:S(2)}, u32[]{:S(2)}) collective-permute-start(bf16[128,2048]{1,0:T(8,128)(2,1)S(1)} %get-tuple-element.78), channel_id=1, source_target_pairs={{0,1},{1,0},{2,3},{3,2},{4,5},{5,4},{6,7},{7,6},{8,9},{9,8},{10,11... | collective-permute-start | bytes 1572872 | tf_op jit(solution)/shard_map/ppermute | solution.py:35
  65.2 18.0 %collective-permute-start.13 = (bf16[128,2048]{1,0:T(8,128)(2,1)S(1)}, bf16[128,2048]{1,0:T(8,128)(2,1)S(1)}, u32[]{:S(2)}, u32[]{:S(2)}) collective-permute-start(bf16[128,2048]{1,0:T(8,128)(2,1)S(1)} %bitcast.103), channel_id=1, source_target_pairs={{0,2},{1,3},{2,0},{3,1},{4,6},{5,7},{6,4},{7,5},{8,10},{9,11},{10,... | collective-permute-start | bytes 1572872 | tf_op jit(solution)/shard_map/ppermute | solution.py:35
  66.9 7.4 %collective-permute-start.17 = (bf16[32,2048]{1,0:T(8,128)(2,1)S(1)}, bf16[32,2048]{1,0:T(8,128)(2,1)S(1)}, u32[]{:S(2)}, u32[]{:S(2)}) collective-permute-start(bf16[32,2048]{1,0:T(8,128)(2,1)S(1)} %bitcast.112), channel_id=1, source_target_pairs={{0,12},{1,13},{2,14},{3,15},{4,8},{5,9},{6,10},{7,11},{8,4},{9,5},... | collective-permute-start | bytes 393224 | tf_op jit(solution)/shard_map/ppermute | solution.py:35
  69.4 13.8 %collective-permute-start.16 = (bf16[32,2048]{1,0:T(8,128)(2,1)S(1)}, bf16[32,2048]{1,0:T(8,128)(2,1)S(1)}, u32[]{:S(2)}, u32[]{:S(2)}) collective-permute-start(bf16[32,2048]{1,0:T(8,128)(2,1)S(1)} %bitcast.111), channel_id=1, source_target_pairs={{0,8},{1,9},{2,10},{3,11},{4,12},{5,13},{6,14},{7,15},{8,0},{9,1},... | collective-permute-start | bytes 393224 | tf_op jit(solution)/shard_map/ppermute | solution.py:35
  74.0 9.1 %collective-permute-start.15 = (bf16[32,2048]{1,0:T(8,128)(2,1)S(1)}, bf16[32,2048]{1,0:T(8,128)(2,1)S(1)}, u32[]{:S(2)}, u32[]{:S(2)}) collective-permute-start(bf16[32,2048]{1,0:T(8,128)(2,1)S(1)} %bitcast.109), channel_id=1, source_target_pairs={{0,4},{1,5},{2,6},{3,7},{4,0},{5,1},{6,2},{7,3},{8,12},{9,13},{10,... | collective-permute-start | bytes 393224 | tf_op jit(solution)/shard_map/ppermute | solution.py:35
  83.4 5.3 %collective-permute-start.21 = (bf16[16,2048]{1,0:T(8,128)(2,1)S(1)}, bf16[16,2048]{1,0:T(8,128)(2,1)S(1)}, u32[]{:S(2)}, u32[]{:S(2)}) collective-permute-start(bf16[16,2048]{1,0:T(8,128)(2,1)S(1)} %slice.160), channel_id=1, source_target_pairs={{0,2},{1,3},{2,0},{3,1},{4,6},{5,7},{6,4},{7,5},{8,10},{9,11},{10,... | collective-permute-start | bytes 196616 | tf_op jit(solution)/shard_map/ppermute | solution.py:35
  84.3 8.2 %collective-permute-start.20 = (bf16[32,2048]{1,0:T(8,128)(2,1)S(1)}, bf16[32,2048]{1,0:T(8,128)(2,1)S(1)}, u32[]{:S(2)}, u32[]{:S(2)}) collective-permute-start(bf16[32,2048]{1,0:T(8,128)(2,1)S(1)} %bitcast.110), channel_id=1, source_target_pairs={{0,12},{1,13},{2,14},{3,15},{4,8},{5,9},{6,10},{7,11},{8,4},{9,5},... | collective-permute-start | bytes 393224 | tf_op jit(solution)/shard_map/ppermute | solution.py:35
  86.7 11.9 %collective-permute-start.19 = (bf16[32,2048]{1,0:T(8,128)(2,1)S(1)}, bf16[32,2048]{1,0:T(8,128)(2,1)S(1)}, u32[]{:S(2)}, u32[]{:S(2)}) collective-permute-start(bf16[32,2048]{1,0:T(8,128)(2,1)S(1)} %bitcast.108), channel_id=1, source_target_pairs={{0,8},{1,9},{2,10},{3,11},{4,12},{5,13},{6,14},{7,15},{8,0},{9,1},... | collective-permute-start | bytes 393224 | tf_op jit(solution)/shard_map/ppermute | solution.py:35
  87.5 11.1 %collective-permute-start.18 = (bf16[32,2048]{1,0:T(8,128)(2,1)S(1)}, bf16[32,2048]{1,0:T(8,128)(2,1)S(1)}, u32[]{:S(2)}, u32[]{:S(2)}) collective-permute-start(bf16[32,2048]{1,0:T(8,128)(2,1)S(1)} %bitcast.107), channel_id=1, source_target_pairs={{0,4},{1,5},{2,6},{3,7},{4,0},{5,1},{6,2},{7,3},{8,12},{9,13},{10,... | collective-permute-start | bytes 393224 | tf_op jit(solution)/shard_map/ppermute | solution.py:35

commit v23 on v22

--- a/solution.py
+++ b/solution.py
@@ -48,7 +48,10 @@
     return jnp.dot(a, b, preferred_element_type=jnp.float32)
 
 
-def payload_kernel(hidden_ref, ids_ref, logits_ref, out_ref, turned_ref):
+def first_kernel(
+    place_ref, placement_ref, hidden_ref, ids_ref, logits_ref, factors_ref, out_ref, *refs
+):
+    turned_ref, wide_ref, slot_ref = refs[-3:]
     steps, top, rows = ids_ref.shape
     width = hidden_ref.shape[2]
     turned_ref[...] = jnp.zeros_like(turned_ref)
@@ -66,23 +69,8 @@
         out_ref[s * rows : (s + 1) * rows, :width] = hidden_ref[s]
     out_ref[:, width:] = dense[: steps * rows]
 
-
-def make_payload(hidden, route_ids, route_logits, experts):
-    steps, rows, width = hidden.shape
-    padded = -(-experts // LANES) * LANES
-    return pl.pallas_call(
-        payload_kernel,
-        out_shape=jax.ShapeDtypeStruct((steps * rows, width + padded), jnp.bfloat16),
-        scratch_shapes=[pltpu.VMEM((padded, -(-steps * rows // LANES) * LANES), jnp.float32)],
-        compiler_params=pltpu.CompilerParams(vmem_limit_bytes=WHOLE_GRANT),
-        cost_estimate=LITTLE,
-        name="payload",
-    )(hidden, jnp.swapaxes(route_ids, 1, 2), jnp.swapaxes(route_logits, 1, 2))
-
-
-def order_kernel(place_ref, placement_ref, factors_ref, *refs):
-    out_refs, wide_ref, slot_ref = refs[:-2], refs[-2], refs[-1]
     slots = factors_ref.shape[0]
+    out_refs = refs[:-3]
     middle, outer, length, lanes = out_refs[0].shape
 
     def cut(t, carry):
@@ -98,30 +86,38 @@
         for r in range(middle):
             for q in range(outer):
                 slot = slot_ref[place_ref[0] ^ ((q * middle + r) * len(out_refs) + core)]
-                rows = wide_ref[pl.ds(pl.multiple_of(slot * length, 8), length), :]
-                out_ref[r, q] = rows.astype(jnp.bfloat16)
-
-
-def order_factors(place, placement, factors, outer, middle, cores):
+                block = wide_ref[pl.ds(pl.multiple_of(slot * length, 8), length), :]
+                out_ref[r, q] = block.astype(jnp.bfloat16)
+
+
+def lay_out(place, placement, hidden, route_ids, route_logits, factors, outer, middle, cores):
+    steps, rows, width = hidden.shape
     slots, entries = factors.shape
     length = entries // LANES
+    padded = -(-slots // LANES) * LANES
     shape = jax.ShapeDtypeStruct((middle, outer, length, LANES), jnp.bfloat16)
     return pl.pallas_call(
-        order_kernel,
-        out_shape=[shape] * cores,
-        in_specs=[
-            pl.BlockSpec(memory_space=pltpu.SMEM),
-            pl.BlockSpec(memory_space=pltpu.SMEM),
-            pl.BlockSpec(memory_space=pltpu.VMEM),
-        ],
+        first_kernel,
+        out_shape=[jax.ShapeDtypeStruct((steps * rows, width + padded), jnp.bfloat16)]
+        + [shape] * cores,
+        in_specs=[pl.BlockSpec(memory_space=pltpu.SMEM)] * 2
+        + [pl.BlockSpec(memory_space=pltpu.VMEM)] * 4,
         scratch_shapes=[
+            pltpu.VMEM((padded, -(-steps * rows // LANES) * LANES), jnp.float32),
             pltpu.VMEM((slots * length, LANES), jnp.float32),
             pltpu.SMEM((slots,), jnp.int32),
         ],
         compiler_params=pltpu.CompilerParams(vmem_limit_bytes=WHOLE_GRANT),
-        cost_estimate=MUCH,
-        name="order_factors",
-    )(place, placement, factors)
+        cost_estimate=LITTLE,
+        name="lay_out",
+    )(
+        place,
+        placement,
+        hidden,
+        jnp.swapaxes(route_ids, 1, 2),
+        jnp.swapaxes(route_logits, 1, 2),
+        factors,
+    )
 
 
 def relayout_kernel(place_ref, *refs):
@@ -189,42 +185,37 @@
     )(place, *parts)
 
 
-def base_kernel(x_ref, other_ref, w_gate_ref, w_up_ref, gate_ref, up_ref):
-    width, rows = w_gate_ref.shape[0], x_ref.shape[0]
-    for i, piece in enumerate((x_ref, other_ref)):
-        at = slice(i * rows, (i + 1) * rows)
-        gate_ref[at, :] = dot(piece[:, :width], w_gate_ref[...])
-        up_ref[at, :] = dot(piece[:, :width], w_up_ref[...])
-
-
-def base_products(pieces, w_gate, w_up):
-    total = sum(p.shape[0] for p in pieces)
-    out = jax.ShapeDtypeStruct((total, w_gate.shape[1]), jnp.float32)
+def base_kernel(x_ref, w_gate_ref, w_up_ref, gate_ref, up_ref):
+    width = w_gate_ref.shape[0]
+    gate_ref[...] = dot(x_ref[:, :width], w_gate_ref[...])
+    up_ref[...] = dot(x_ref[:, :width], w_up_ref[...])
+
+
+def base_products(piece, w_gate, w_up):
+    out = jax.ShapeDtypeStruct((piece.shape[0], w_gate.shape[1]), jnp.float32)
     return pl.pallas_call(
         base_kernel,
         out_shape=[out, out],
-        in_specs=[pl.BlockSpec(memory_space=pltpu.VMEM)] * 4,
+        in_specs=[pl.BlockSpec(memory_space=pltpu.VMEM)] * 3,
         compiler_params=pltpu.CompilerParams(vmem_limit_bytes=EXPERT_GRANT),
         cost_estimate=LITTLE,
         name="base_products",
-    )(*pieces, w_gate, w_up)
+    )(piece, w_gate, w_up)
 
 
 def finish_kernel(count, first, rows, place_ref, *refs):
     pieces, refs = refs[:count], refs[count:]
-    base, refs = refs[:count], refs[count:]
+    base, refs = refs[: 2 * count], refs[2 * count :]
     a_gu_ref, gate_b_ref, up_b_ref, down_a_ref, down_b_ref, w_down_ref = refs[:6]
     kept_ref, sent_ref, x_ref, inner_ref = refs[6:]
     width = w_down_ref.shape[1]
     rank = gate_b_ref.shape[0]
-    span = pieces[0].shape[0]
     own = kept_ref.shape[0]
     for i, piece in enumerate(pieces):
         x_ref[i * rows : (i + 1) * rows, :] = piece[first : first + rows, :]
 
     def of_step(refs):
-        at = [first, span + first]
-        return jnp.concatenate([ref[i : i + rows, :] for i in at for ref in refs])
+        return jnp.concatenate([ref[first : first + rows, :] for ref in refs])
 
     low = (adapter_scale * dot(x_ref[:, :width], a_gu_ref[...])).astype(jnp.bfloat16)
     gates = x_ref[:, width:].astype(jnp.float32)
@@ -278,11 +269,11 @@
     def along(x, stride, size):
         return [x] + [swap(x, owners, stride, k) for k in range(1, size)]
 
-    rows_in = make_payload(hidden, route_ids, route_logits, experts)
-    rows_in, factors = lax.optimization_barrier((rows_in, factors))
+    rows_in, kept, sent = lay_out(
+        place, placement, hidden, route_ids, route_logits, factors, outer, middle, cores
+    )
     column = [p.reshape(steps, rows, -1) for p in along(rows_in, *along_outer)]
     column = jnp.stack(column, axis=1).reshape(steps * outer * rows, -1)
-    kept, sent = order_factors(place, placement, factors, outer, middle, cores)
     blocks = jnp.stack([kept, swap(sent, owners, 1, 1)])
     blocks = [blocks[:, 0], swap(blocks[:, 1], owners, cores, 1)]
     blocks = [jnp.concatenate([block[:, q] for block in blocks]) for q in range(outer)]
@@ -293,13 +284,15 @@
     sheet = along(column, *along_middle)
     others = [swap(column, owners, 1, 1)]
     weights = (w_gate[0], w_up[0])
-    base = [base_products([column, others[0]], *weights)]
+    base = [base_products(piece, *weights) for piece in (column, others[0])]
     here, sheet[1:], base = lax.optimization_barrier((here, sheet[1:], base))
     for r in range(1, middle):
         others.append(swap(sheet[r], owners, 1, 1))
-        base.append(base_products([sheet[r], others[r]], *weights))
+        base.append(base_products(sheet[r], *weights))
+        base.append(base_products(others[r], *weights))
     low_rank = relayout_factors(place, here, width, units, rank, owners)
-    pieces, base = sheet + others, [b for pair in base for b in pair]
+    pieces = sheet + others
+    base = [b for pair in base[::2] + base[1::2] for b in pair]
     span = outer * rows
 
     summed = []

time: 99.6 us -> 97.5 us (0.979)
  waiting for transfers between devices: 50.6 us -> 48.9 us
  Pallas kernels: 18 us -> 16.9 us
    ppermute x22, waiting for transfers between devices: 50.6 us -> 48.9 us  [swap(): return lax.ppermute(x, 'expert', [(i, i ^ k * stride) for i in range(n)])]
    pallas_call x2 -> x1, Pallas kernels: 5.04 us -> 3.59 us  [lay_out(): pl.pallas_call(first_kernel, out_shape=[jax.ShapeDtypeStruct((steps * row...]
    pallas_call x2 -> x4, Pallas kernels: 5.28 us -> 5.63 us  [base_products(): pl.pallas_call(base_kernel, out_shape=[out, out], in_specs=[pl.BlockSpec(...]
  transfers between devices with their start and end apart: 22 -> 22, of which waited for: 10 -> 9; matrix products, arithmetic and copies ran while one was open for 2% -> 2% of each run, Pallas kernels for 8% -> 10%
where the time goes in v23:
time: 97.5 us; the launch traced here: 97.4 us
  waiting for transfers between devices  48.9 us (50%)
  starting transfers between devices  27.5 us (28%)
  Pallas kernels  16.9 us (17%)
  other arithmetic  3.03 us (3%)
    ppermute x22, waiting for transfers between devices, swap(): return lax.ppermute(x, 'expert', [(i, i ^ k * stride) for i in range(n)])  48.9 us
    ppermute x22, starting transfers between devices, swap(): return lax.ppermute(x, 'expert', [(i, i ^ k * stride) for i in range(n)])  27.5 us
    pallas_call x3, Pallas kernels, finish_step(): pl.pallas_call(functools.partial(finish_kernel, len(pieces), first, rows)...  6.48 us
    pallas_call x4, Pallas kernels, base_products(): pl.pallas_call(base_kernel, out_shape=[out, out], in_specs=[pl.BlockSpec(...  5.63 us
    pallas_call x1, Pallas kernels, lay_out(): pl.pallas_call(first_kernel, out_shape=[jax.ShapeDtypeStruct((steps * row...  3.59 us
  transfers between devices with their start and end apart: 22, of which 9 were waited for; matrix products, arithmetic and copies ran while one was open for 2% of the time, Pallas kernels for 10%

profile of v23, /device:TPU:0, one launch (start us, length us, event | category | flops | bytes accessed | tf_op | source)
XLA Modules:
  0.0 97.4 jit_solution(12576954696443131366)
XLA Ops:
  0.0 3.6 %lay_out.1 = (bf16[48,2176]{1,0:T(8,128)(2,1)}, bf16[2,4,264,128]{3,2,1,0:T(8,128)(2,1)}, bf16[2,4,264,128]{3,2,1,0:T(8,128)(2,1)}) custom-call(s32[1]{0:T(128)} %bitcast.place_ref, s32[16]{0:T(128)} %placement_ref.1, bf16[3,16,2048]{2,1,0:T(8,128)(2,1)} %hidden_ref.1, s32[3,8,16]{2,1,0:T(8,128)} %bitcast.117, f32[3,8,16]{2,1,0:T(8,128)} %bitcast.118, ...), custom_call_target="tpu_custom_call" | custom-call | flops 1 | bytes 1 | tf_op jit(solution)/shard_map/lay_out/pallas_call | solution.py:99
  4.0 4.7 %collective-permute-start.2 = (bf16[48,2176]{1,0:T(8,128)(2,1)}, bf16[48,2176]{1,0:T(8,128)(2,1)S(1)}, u32[]{:S(2)}, u32[]{:S(2)}) collective-permute-start(bf16[48,2176]{1,0:T(8,128)(2,1)} %get-tuple-element.48), channel_id=1, source_target_pairs={{0,12},{1,13},{2,14},{3,15},{4,8},{5,9},{6,10},{7,11},{8,4},{9,5},... | collective-permute-start | bytes 626696 | tf_op jit(solution)/shard_map/ppermute | solution.py:35
  8.7 0.7 collective-permute-start
  9.4 1.3 %fusion.3 = (bf16[2,4,264,128]{3,2,0,1:T(8,128)(2,1)S(1)}, bf16[2,4,264,128]{3,2,0,1:T(8,128)(2,1)S(1)}) fusion(bf16[1,2,4,264,128]{4,3,0,2,1:T(8,128)(2,1)} %bitcast.104, bf16[1,2,4,264,128]{4,3,0,2,1:T(8,128)(2,1)S(1)} %bitcast.105), kind=kLoop, calls=%fused_computation.14 | loop fusion | flops 540672 | bytes 2162688 | tf_op jit(solution)/shard_map/squeeze | solution.py:278
  10.7 1.7 %collective-permute-start.4 = (bf16[2,4,264,128]{3,2,0,1:T(8,128)(2,1)S(1)}, bf16[2,4,264,128]{3,2,0,1:T(8,128)(2,1)S(1)}, u32[]{:S(2)}, u32[]{:S(2)}) collective-permute-start(bf16[2,4,264,128]{3,2,0,1:T(8,128)(2,1)S(1)} %get-tuple-element.92), channel_id=1, source_target_pairs={{0,2},{1,3},{2,0},{3,1},{4,6},{5,7},{6,4},{7,5},{8,10},{9,11},{10,... | collective-permute-start | bytes 1622024 | tf_op jit(solution)/shard_map/ppermute | solution.py:35
  12.4 2.7 %collective-permute-done.2 = bf16[48,2176]{1,0:T(8,128)(2,1)S(1)} collective-permute-done((bf16[48,2176]{1,0:T(8,128)(2,1)}, bf16[48,2176]{1,0:T(8,128)(2,1)S(1)}, u32[]{:S(2)}, u32[]{:S(2)}) %collective-permute-start.2) | collective-permute-done | bytes 208928 | tf_op jit(solution)/shard_map/ppermute | solution.py:35
  15.1 12.2 %collective-permute-done.1 = bf16[48,2176]{1,0:T(8,128)(2,1)S(1)} collective-permute-done((bf16[48,2176]{1,0:T(8,128)(2,1)}, bf16[48,2176]{1,0:T(8,128)(2,1)S(1)}, u32[]{:S(2)}, u32[]{:S(2)}) %collective-permute-start.1) | collective-permute-done | bytes 208928 | tf_op jit(solution)/shard_map/ppermute | solution.py:35
  27.7 1.6 %collective-permute-start.8 = (bf16[192,2176]{1,0:T(8,128)(2,1)S(1)}, bf16[192,2176]{1,0:T(8,128)(2,1)S(1)}, u32[]{:S(2)}, u32[]{:S(2)}) collective-permute-start(bf16[192,2176]{1,0:T(8,128)(2,1)S(1)} %bitcast.86), channel_id=1, source_target_pairs={{0,2},{1,3},{2,0},{3,1},{4,6},{5,7},{6,4},{7,5},{8,10},{9,11},{10,... | collective-permute-start | bytes 2506760 | tf_op jit(solution)/shard_map/ppermute | solution.py:35
  29.3 3.0 %collective-permute-start.6 = (bf16[4,264,128]{2,1,0:T(8,128)(2,1)S(1)}, bf16[4,264,128]{2,1,0:T(8,128)(2,1)S(1)}, u32[]{:S(2)}, u32[]{:S(2)}) collective-permute-start(bf16[4,264,128]{2,1,0:T(8,128)(2,1)S(1)} %get-tuple-element.54), channel_id=1, source_target_pairs={{0,8},{1,9},{2,10},{3,11},{4,12},{5,13},{6,14},{7,15},{8,0},{9,1},... | collective-permute-start | bytes 811016 | tf_op jit(solution)/shard_map/ppermute | solution.py:35
  32.3 1.3 %collective-permute-start.7 = (bf16[4,264,128]{2,1,0:T(8,128)(2,1)S(1)}, bf16[4,264,128]{2,1,0:T(8,128)(2,1)S(1)}, u32[]{:S(2)}, u32[]{:S(2)}) collective-permute-start(bf16[4,264,128]{2,1,0:T(8,128)(2,1)S(1)} %get-tuple-element.55), channel_id=1, source_target_pairs={{0,12},{1,13},{2,14},{3,15},{4,8},{5,9},{6,10},{7,11},{8,4},{9,5},... | collective-permute-start | bytes 811016 | tf_op jit(solution)/shard_map/ppermute | solution.py:35
  33.7 1.4 %base_products.4 = (f32[192,768]{1,0:T(8,128)S(1)}, f32[192,768]{1,0:T(8,128)S(1)}) custom-call(bf16[192,2176]{1,0:T(8,128)(2,1)S(1)} %bitcast.87, bf16[2048,768]{1,0:T(8,128)(2,1)S(1)} %bitcast.77, bf16[2048,768]{1,0:T(8,128)(2,1)S(1)} %bitcast.81), custom_call_target="tpu_custom_call" | custom-call | flops 1 | bytes 1 | tf_op jit(solution)/shard_map/base_products/pallas_call | solution.py:196
  35.1 1.4 %base_products.5 = (f32[192,768]{1,0:T(8,128)S(1)}, f32[192,768]{1,0:T(8,128)S(1)}) custom-call(bf16[192,2176]{1,0:T(8,128)(2,1)S(1)} %collective-permute-done.9.x_ref.refs_2_, bf16[2048,768]{1,0:T(8,128)(2,1)S(1)} %bitcast.78, bf16[2048,768]{1,0:T(8,128)(2,1)S(1)} %bitcast.82), custom_call_target="tpu_custom_call" | custom-call | flops 1 | bytes 1 | tf_op jit(solution)/shard_map/base_products/pallas_call | solution.py:196
  36.5 6.6 %collective-permute-done.5.refs_1_ = bf16[4,264,128]{2,1,0:T(8,128)(2,1)S(1)} collective-permute-done((bf16[4,264,128]{2,1,0:T(8,128)(2,1)S(1)}, bf16[4,264,128]{2,1,0:T(8,128)(2,1)S(1)}, u32[]{:S(2)}, u32[]{:S(2)}) %collective-permute-start.5) | collective-permute-done | bytes 270368 | tf_op jit(solution)/shard_map/ppermute | solution.py:35
  43.1 8.1 %collective-permute-done.6.refs_2_ = bf16[4,264,128]{2,1,0:T(8,128)(2,1)S(1)} collective-permute-done((bf16[4,264,128]{2,1,0:T(8,128)(2,1)S(1)}, bf16[4,264,128]{2,1,0:T(8,128)(2,1)S(1)}, u32[]{:S(2)}, u32[]{:S(2)}) %collective-permute-start.6) | collective-permute-done | bytes 270368 | tf_op jit(solution)/shard_map/ppermute | solution.py:35
  51.3 1.4 %base_products.6 = (f32[192,768]{1,0:T(8,128)S(1)}, f32[192,768]{1,0:T(8,128)S(1)}) custom-call(bf16[192,2176]{1,0:T(8,128)(2,1)S(1)} %collective-permute-done.8.x_ref.refs_1_, bf16[2048,768]{1,0:T(8,128)(2,1)S(1)} %bitcast.79, bf16[2048,768]{1,0:T(8,128)(2,1)S(1)} %bitcast.83), custom_call_target="tpu_custom_call" | custom-call | flops 1 | bytes 1 | tf_op jit(solution)/shard_map/base_products/pallas_call | solution.py:196
  52.7 1.2 %relayout_factors.1 = (bf16[2048,128]{1,0:T(8,128)(2,1)S(1)}, bf16[64,768]{1,0:T(8,128)(2,1)S(1)}, bf16[64,768]{1,0:T(8,128)(2,1)S(1)}, bf16[768,128]{1,0:T(8,128)(2,1)S(1)}, bf16[64,2048]{1,0:T(8,128)(2,1)S(1)}) custom-call(s32[1]{0:T(128)} %bitcast.place_ref, bf16[4,264,128]{2,1,0:T(8,128)(2,1)S(1)} %get-tuple-element.69.refs_0_, ...), custom_call_target="tpu_custom_call" | custom-call | flops 1 | bytes 1 | tf_op jit(solution)/shard_map/relayout_factors/pallas_call | solution.py:173
  54.0 1.4 %base_products.7 = (f32[192,768]{1,0:T(8,128)S(1)}, f32[192,768]{1,0:T(8,128)S(1)}) custom-call(bf16[192,2176]{1,0:T(8,128)(2,1)S(1)} %collective-permute-done.10.x_ref.refs_3_, bf16[2048,768]{1,0:T(8,128)(2,1)S(1)} %bitcast.80, bf16[2048,768]{1,0:T(8,128)(2,1)S(1)} %bitcast.84), custom_call_target="tpu_custom_call" | custom-call | flops 1 | bytes 1 | tf_op jit(solution)/shard_map/base_products/pallas_call | solution.py:196
  55.8 2.2 %finish_step.3 = (f32[128,2048]{1,0:T(8,128)S(1)}, bf16[128,2048]{1,0:T(8,128)(2,1)S(1)}) custom-call(s32[1]{0:T(128)} %bitcast.place_ref, bf16[192,2176]{1,0:T(8,128)(2,1)S(1)} %bitcast.88, bf16[192,2176]{1,0:T(8,128)(2,1)S(1)} %collective-permute-done.8.x_ref.refs_1_, bf16[192,2176]{1,0:T(8,128)(2,1)S(1)} %collective-permute-done.9.x_ref.refs_2_, ...), custom_call_target="tpu_custom_call" | custom-call | flops 8589934592 | bytes 1 | tf_op jit(solution)/shard_map/finish_step/pallas_call | solution.py:239
  58.0 0.6 collective-permute-start.11
  58.6 2.2 %finish_step.4 = (f32[128,2048]{1,0:T(8,128)S(1)}, bf16[128,2048]{1,0:T(8,128)(2,1)S(1)}) custom-call(s32[1]{0:T(128)} %bitcast.place_ref, bf16[192,2176]{1,0:T(8,128)(2,1)S(1)} %bitcast.89, bf16[192,2176]{1,0:T(8,128)(2,1)S(1)} %collective-permute-done.8.x_ref.refs_1_, bf16[192,2176]{1,0:T(8,128)(2,1)S(1)} %collective-permute-done.9.x_ref.refs_2_, ...), custom_call_target="tpu_custom_call" | custom-call | flops 8589934592 | bytes 1 | tf_op jit(solution)/shard_map/finish_step/pallas_call | solution.py:239
  60.8 2.2 %finish_step.5 = (f32[128,2048]{1,0:T(8,128)S(1)}, bf16[128,2048]{1,0:T(8,128)(2,1)S(1)}) custom-call(s32[1]{0:T(128)} %bitcast.place_ref, bf16[192,2176]{1,0:T(8,128)(2,1)S(1)} %bitcast.90, bf16[192,2176]{1,0:T(8,128)(2,1)S(1)} %collective-permute-done.8.x_ref.refs_1_, bf16[192,2176]{1,0:T(8,128)(2,1)S(1)} %collective-permute-done.9.x_ref.refs_2_, ...), custom_call_target="tpu_custom_call" | custom-call | flops 8589934592 | bytes 1 | tf_op jit(solution)/shard_map/finish_step/pallas_call | solution.py:239
  63.9 0.6 collective-permute-start.13
  65.3 2.5 %collective-permute-start.17 = (bf16[32,2048]{1,0:T(8,128)(2,1)S(1)}, bf16[32,2048]{1,0:T(8,128)(2,1)S(1)}, u32[]{:S(2)}, u32[]{:S(2)}) collective-permute-start(bf16[32,2048]{1,0:T(8,128)(2,1)S(1)} %bitcast.116), channel_id=1, source_target_pairs={{0,12},{1,13},{2,14},{3,15},{4,8},{5,9},{6,10},{7,11},{8,4},{9,5},... | collective-permute-start | bytes 393224 | tf_op jit(solution)/shard_map/ppermute | solution.py:35
  67.8 4.7 %collective-permute-start.16 = (bf16[32,2048]{1,0:T(8,128)(2,1)S(1)}, bf16[32,2048]{1,0:T(8,128)(2,1)S(1)}, u32[]{:S(2)}, u32[]{:S(2)}) collective-permute-start(bf16[32,2048]{1,0:T(8,128)(2,1)S(1)} %bitcast.115), channel_id=1, source_target_pairs={{0,8},{1,9},{2,10},{3,11},{4,12},{5,13},{6,14},{7,15},{8,0},{9,1},... | collective-permute-start | bytes 393224 | tf_op jit(solution)/shard_map/ppermute | solution.py:35
  72.9 8.8 %collective-permute-done.16 = bf16[32,2048]{1,0:T(8,128)(2,1)S(1)} collective-permute-done((bf16[32,2048]{1,0:T(8,128)(2,1)S(1)}, bf16[32,2048]{1,0:T(8,128)(2,1)S(1)}, u32[]{:S(2)}, u32[]{:S(2)}) %collective-permute-start.16) | collective-permute-done | bytes 131104 | tf_op jit(solution)/shard_map/ppermute | solution.py:35
  82.0 0.6 collective-permute-start.21
  82.8 2.4 %collective-permute-start.20 = (bf16[32,2048]{1,0:T(8,128)(2,1)S(1)}, bf16[32,2048]{1,0:T(8,128)(2,1)S(1)}, u32[]{:S(2)}, u32[]{:S(2)}) collective-permute-start(bf16[32,2048]{1,0:T(8,128)(2,1)S(1)} %bitcast.114), channel_id=1, source_target_pairs={{0,12},{1,13},{2,14},{3,15},{4,8},{5,9},{6,10},{7,11},{8,4},{9,5},... | collective-permute-start | bytes 393224 | tf_op jit(solution)/shard_map/ppermute | solution.py:35
  85.2 0.7 collective-permute-start.19
  85.9 1.4 %collective-permute-start.18 = (bf16[32,2048]{1,0:T(8,128)(2,1)S(1)}, bf16[32,2048]{1,0:T(8,128)(2,1)S(1)}, u32[]{:S(2)}, u32[]{:S(2)}) collective-permute-start(bf16[32,2048]{1,0:T(8,128)(2,1)S(1)} %bitcast.111), channel_id=1, source_target_pairs={{0,4},{1,5},{2,6},{3,7},{4,0},{5,1},{6,2},{7,3},{8,12},{9,13},{10,... | collective-permute-start | bytes 393224 | tf_op jit(solution)/shard_map/ppermute | solution.py:35
  87.3 3.8 %collective-permute-done.20 = bf16[32,2048]{1,0:T(8,128)(2,1)S(1)} collective-permute-done((bf16[32,2048]{1,0:T(8,128)(2,1)S(1)}, bf16[32,2048]{1,0:T(8,128)(2,1)S(1)}, u32[]{:S(2)}, u32[]{:S(2)}) %collective-permute-start.20) | collective-permute-done | bytes 131104 | tf_op jit(solution)/shard_map/ppermute | solution.py:35
  91.1 5.5 %collective-permute-done.19 = bf16[32,2048]{1,0:T(8,128)(2,1)S(1)} collective-permute-done((bf16[32,2048]{1,0:T(8,128)(2,1)S(1)}, bf16[32,2048]{1,0:T(8,128)(2,1)S(1)}, u32[]{:S(2)}, u32[]{:S(2)}) %collective-permute-start.19) | collective-permute-done | bytes 131104 | tf_op jit(solution)/shard_map/ppermute | solution.py:35
  96.7 0.7 pad_maximum_fusion.7
  (53 shorter events, 4.0 us)
Async XLA Ops:
  3.6 23.7 %copy-start.3 = (bf16[48,2176]{1,0:T(8,128)(2,1)S(1)}, bf16[48,2176]{1,0:T(8,128)(2,1)}, u32[]{:S(2)}) copy-start(bf16[48,2176]{1,0:T(8,128)(2,1)} %get-tuple-element.48) | copy-start | bytes 626692
  3.6 5.8 %collective-permute-start.3 = (bf16[2,4,264,128]{3,2,1,0:T(8,128)(2,1)}, bf16[2,4,264,128]{3,2,1,0:T(8,128)(2,1)S(1)}, u32[]{:S(2)}, u32[]{:S(2)}) collective-permute-start(bf16[2,4,264,128]{3,2,1,0:T(8,128)(2,1)} %get-tuple-element.50), channel_id=1, source_target_pairs={{0,1},{1,0},{2,3},{3,2},{4,5},{5,4},{6,7},{7,6},{8,9},{9,8},{10,11... | collective-permute-start | bytes 1622024 | tf_op jit(solution)/shard_map/ppermute | solution.py:35
  4.0 11.0 %collective-permute-start.2 = (bf16[48,2176]{1,0:T(8,128)(2,1)}, bf16[48,2176]{1,0:T(8,128)(2,1)S(1)}, u32[]{:S(2)}, u32[]{:S(2)}) collective-permute-start(bf16[48,2176]{1,0:T(8,128)(2,1)} %get-tuple-element.48), channel_id=1, source_target_pairs={{0,12},{1,13},{2,14},{3,15},{4,8},{5,9},{6,10},{7,11},{8,4},{9,5},... | collective-permute-start | bytes 626696 | tf_op jit(solution)/shard_map/ppermute | solution.py:35
  8.7 18.6 %collective-permute-start.1 = (bf16[48,2176]{1,0:T(8,128)(2,1)}, bf16[48,2176]{1,0:T(8,128)(2,1)S(1)}, u32[]{:S(2)}, u32[]{:S(2)}) collective-permute-start(bf16[48,2176]{1,0:T(8,128)(2,1)} %get-tuple-element.48), channel_id=1, source_target_pairs={{0,8},{1,9},{2,10},{3,11},{4,12},{5,13},{6,14},{7,15},{8,0},{9,1},... | collective-permute-start | bytes 626696 | tf_op jit(solution)/shard_map/ppermute | solution.py:35
  8.7 18.6 %collective-permute-start = (bf16[48,2176]{1,0:T(8,128)(2,1)}, bf16[48,2176]{1,0:T(8,128)(2,1)S(1)}, u32[]{:S(2)}, u32[]{:S(2)}) collective-permute-start(bf16[48,2176]{1,0:T(8,128)(2,1)} %get-tuple-element.48), channel_id=1, source_target_pairs={{0,4},{1,5},{2,6},{3,7},{4,0},{5,1},{6,2},{7,3},{8,12},{9,13},{10,... | collective-permute-start | bytes 626696 | tf_op jit(solution)/shard_map/ppermute | solution.py:35
  9.4 24.3 %copy-start.1 = (bf16[1,2048,768]{2,1,0:T(8,128)(2,1)S(1)}, bf16[1,2048,768]{2,1,0:T(8,128)(2,1)}, u32[]{:S(2)}) copy-start(bf16[1,2048,768]{2,1,0:T(8,128)(2,1)} %param.14) | copy-start | bytes 9437188
  10.7 16.8 %collective-permute-start.4 = (bf16[2,4,264,128]{3,2,0,1:T(8,128)(2,1)S(1)}, bf16[2,4,264,128]{3,2,0,1:T(8,128)(2,1)S(1)}, u32[]{:S(2)}, u32[]{:S(2)}) collective-permute-start(bf16[2,4,264,128]{3,2,0,1:T(8,128)(2,1)S(1)} %get-tuple-element.92), channel_id=1, source_target_pairs={{0,2},{1,3},{2,0},{3,1},{4,6},{5,7},{6,4},{7,5},{8,10},{9,11},{10,... | collective-permute-start | bytes 1622024 | tf_op jit(solution)/shard_map/ppermute | solution.py:35
  27.4 6.3 %copy-start = (bf16[1,2048,768]{2,1,0:T(8,128)(2,1)S(1)}, bf16[1,2048,768]{2,1,0:T(8,128)(2,1)}, u32[]{:S(2)}) copy-start(bf16[1,2048,768]{2,1,0:T(8,128)(2,1)} %param.13) | copy-start | bytes 9437188
  27.6 7.5 %collective-permute-start.9 = (bf16[192,2176]{1,0:T(8,128)(2,1)S(1)}, bf16[192,2176]{1,0:T(8,128)(2,1)S(1)}, u32[]{:S(2)}, u32[]{:S(2)}) collective-permute-start(bf16[192,2176]{1,0:T(8,128)(2,1)S(1)} %bitcast.85), channel_id=1, source_target_pairs={{0,1},{1,0},{2,3},{3,2},{4,5},{5,4},{6,7},{7,6},{8,9},{9,8},{10,11... | collective-permute-start | bytes 2506760 | tf_op jit(solution)/shard_map/ppermute | solution.py:35
  27.7 23.6 %collective-permute-start.8 = (bf16[192,2176]{1,0:T(8,128)(2,1)S(1)}, bf16[192,2176]{1,0:T(8,128)(2,1)S(1)}, u32[]{:S(2)}, u32[]{:S(2)}) collective-permute-start(bf16[192,2176]{1,0:T(8,128)(2,1)S(1)} %bitcast.86), channel_id=1, source_target_pairs={{0,2},{1,3},{2,0},{3,1},{4,6},{5,7},{6,4},{7,5},{8,10},{9,11},{10,... | collective-permute-start | bytes 2506760 | tf_op jit(solution)/shard_map/ppermute | solution.py:35
  29.3 13.8 %collective-permute-start.5 = (bf16[4,264,128]{2,1,0:T(8,128)(2,1)S(1)}, bf16[4,264,128]{2,1,0:T(8,128)(2,1)S(1)}, u32[]{:S(2)}, u32[]{:S(2)}) collective-permute-start(bf16[4,264,128]{2,1,0:T(8,128)(2,1)S(1)} %get-tuple-element.53), channel_id=1, source_target_pairs={{0,4},{1,5},{2,6},{3,7},{4,0},{5,1},{6,2},{7,3},{8,12},{9,13},{10,... | collective-permute-start | bytes 811016 | tf_op jit(solution)/shard_map/ppermute | solution.py:35
  29.3 22.0 %collective-permute-start.6 = (bf16[4,264,128]{2,1,0:T(8,128)(2,1)S(1)}, bf16[4,264,128]{2,1,0:T(8,128)(2,1)S(1)}, u32[]{:S(2)}, u32[]{:S(2)}) collective-permute-start(bf16[4,264,128]{2,1,0:T(8,128)(2,1)S(1)} %get-tuple-element.54), channel_id=1, source_target_pairs={{0,8},{1,9},{2,10},{3,11},{4,12},{5,13},{6,14},{7,15},{8,0},{9,1},... | collective-permute-start | bytes 811016 | tf_op jit(solution)/shard_map/ppermute | solution.py:35
  32.3 18.9 %collective-permute-start.7 = (bf16[4,264,128]{2,1,0:T(8,128)(2,1)S(1)}, bf16[4,264,128]{2,1,0:T(8,128)(2,1)S(1)}, u32[]{:S(2)}, u32[]{:S(2)}) collective-permute-start(bf16[4,264,128]{2,1,0:T(8,128)(2,1)S(1)} %get-tuple-element.55), channel_id=1, source_target_pairs={{0,12},{1,13},{2,14},{3,15},{4,8},{5,9},{6,10},{7,11},{8,4},{9,5},... | collective-permute-start | bytes 811016 | tf_op jit(solution)/shard_map/ppermute | solution.py:35
  51.3 2.7 %collective-permute-start.10 = (bf16[192,2176]{1,0:T(8,128)(2,1)S(1)}, bf16[192,2176]{1,0:T(8,128)(2,1)S(1)}, u32[]{:S(2)}, u32[]{:S(2)}) collective-permute-start(bf16[192,2176]{1,0:T(8,128)(2,1)S(1)} %collective-permute-done.8.x_ref.refs_1_), channel_id=1, source_target_pairs={{0,1},{1,0},{2,3},{3,2},{4,5},{5,4},{6,7},{7,6},{8,9},{9,8},{10,11... | collective-permute-start | bytes 2506760 | tf_op jit(solution)/shard_map/ppermute | solution.py:35
  53.9 1.9 %copy-start.2 = (bf16[1,768,2048]{2,1,0:T(8,128)(2,1)S(1)}, bf16[1,768,2048]{2,1,0:T(8,128)(2,1)}, u32[]{:S(2)}) copy-start(bf16[1,768,2048]{2,1,0:T(8,128)(2,1)} %param.15) | copy-start | bytes 9437188
  58.0 5.5 %collective-permute-start.11 = (bf16[128,2048]{1,0:T(8,128)(2,1)S(1)}, bf16[128,2048]{1,0:T(8,128)(2,1)S(1)}, u32[]{:S(2)}, u32[]{:S(2)}) collective-permute-start(bf16[128,2048]{1,0:T(8,128)(2,1)S(1)} %get-tuple-element.79), channel_id=1, source_target_pairs={{0,1},{1,0},{2,3},{3,2},{4,5},{5,4},{6,7},{7,6},{8,9},{9,8},{10,11... | collective-permute-start | bytes 1572872 | tf_op jit(solution)/shard_map/ppermute | solution.py:35
  60.7 3.0 %collective-permute-start.12 = (bf16[128,2048]{1,0:T(8,128)(2,1)S(1)}, bf16[128,2048]{1,0:T(8,128)(2,1)S(1)}, u32[]{:S(2)}, u32[]{:S(2)}) collective-permute-start(bf16[128,2048]{1,0:T(8,128)(2,1)S(1)} %get-tuple-element.82), channel_id=1, source_target_pairs={{0,1},{1,0},{2,3},{3,2},{4,5},{5,4},{6,7},{7,6},{8,9},{9,8},{10,11... | collective-permute-start | bytes 1572872 | tf_op jit(solution)/shard_map/ppermute | solution.py:35
  63.0 2.1 %collective-permute-start.14 = (bf16[128,2048]{1,0:T(8,128)(2,1)S(1)}, bf16[128,2048]{1,0:T(8,128)(2,1)S(1)}, u32[]{:S(2)}, u32[]{:S(2)}) collective-permute-start(bf16[128,2048]{1,0:T(8,128)(2,1)S(1)} %get-tuple-element.88), channel_id=1, source_target_pairs={{0,1},{1,0},{2,3},{3,2},{4,5},{5,4},{6,7},{7,6},{8,9},{9,8},{10,11... | collective-permute-start | bytes 1572872 | tf_op jit(solution)/shard_map/ppermute | solution.py:35
  63.9 17.9 %collective-permute-start.13 = (bf16[128,2048]{1,0:T(8,128)(2,1)S(1)}, bf16[128,2048]{1,0:T(8,128)(2,1)S(1)}, u32[]{:S(2)}, u32[]{:S(2)}) collective-permute-start(bf16[128,2048]{1,0:T(8,128)(2,1)S(1)} %bitcast.106), channel_id=1, source_target_pairs={{0,2},{1,3},{2,0},{3,1},{4,6},{5,7},{6,4},{7,5},{8,10},{9,11},{10,... | collective-permute-start | bytes 1572872 | tf_op jit(solution)/shard_map/ppermute | solution.py:35
  65.3 7.6 %collective-permute-start.17 = (bf16[32,2048]{1,0:T(8,128)(2,1)S(1)}, bf16[32,2048]{1,0:T(8,128)(2,1)S(1)}, u32[]{:S(2)}, u32[]{:S(2)}) collective-permute-start(bf16[32,2048]{1,0:T(8,128)(2,1)S(1)} %bitcast.116), channel_id=1, source_target_pairs={{0,12},{1,13},{2,14},{3,15},{4,8},{5,9},{6,10},{7,11},{8,4},{9,5},... | collective-permute-start | bytes 393224 | tf_op jit(solution)/shard_map/ppermute | solution.py:35
  67.8 14.0 %collective-permute-start.16 = (bf16[32,2048]{1,0:T(8,128)(2,1)S(1)}, bf16[32,2048]{1,0:T(8,128)(2,1)S(1)}, u32[]{:S(2)}, u32[]{:S(2)}) collective-permute-start(bf16[32,2048]{1,0:T(8,128)(2,1)S(1)} %bitcast.115), channel_id=1, source_target_pairs={{0,8},{1,9},{2,10},{3,11},{4,12},{5,13},{6,14},{7,15},{8,0},{9,1},... | collective-permute-start | bytes 393224 | tf_op jit(solution)/shard_map/ppermute | solution.py:35
  72.4 9.4 %collective-permute-start.15 = (bf16[32,2048]{1,0:T(8,128)(2,1)S(1)}, bf16[32,2048]{1,0:T(8,128)(2,1)S(1)}, u32[]{:S(2)}, u32[]{:S(2)}) collective-permute-start(bf16[32,2048]{1,0:T(8,128)(2,1)S(1)} %bitcast.113), channel_id=1, source_target_pairs={{0,4},{1,5},{2,6},{3,7},{4,0},{5,1},{6,2},{7,3},{8,12},{9,13},{10,... | collective-permute-start | bytes 393224 | tf_op jit(solution)/shard_map/ppermute | solution.py:35
  82.0 5.2 %collective-permute-start.21 = (bf16[16,2048]{1,0:T(8,128)(2,1)S(1)}, bf16[16,2048]{1,0:T(8,128)(2,1)S(1)}, u32[]{:S(2)}, u32[]{:S(2)}) collective-permute-start(bf16[16,2048]{1,0:T(8,128)(2,1)S(1)} %slice.160), channel_id=1, source_target_pairs={{0,2},{1,3},{2,0},{3,1},{4,6},{5,7},{6,4},{7,5},{8,10},{9,11},{10,... | collective-permute-start | bytes 196616 | tf_op jit(solution)/shard_map/ppermute | solution.py:35
  82.8 8.3 %collective-permute-start.20 = (bf16[32,2048]{1,0:T(8,128)(2,1)S(1)}, bf16[32,2048]{1,0:T(8,128)(2,1)S(1)}, u32[]{:S(2)}, u32[]{:S(2)}) collective-permute-start(bf16[32,2048]{1,0:T(8,128)(2,1)S(1)} %bitcast.114), channel_id=1, source_target_pairs={{0,12},{1,13},{2,14},{3,15},{4,8},{5,9},{6,10},{7,11},{8,4},{9,5},... | collective-permute-start | bytes 393224 | tf_op jit(solution)/shard_map/ppermute | solution.py:35
  85.2 11.4 %collective-permute-start.19 = (bf16[32,2048]{1,0:T(8,128)(2,1)S(1)}, bf16[32,2048]{1,0:T(8,128)(2,1)S(1)}, u32[]{:S(2)}, u32[]{:S(2)}) collective-permute-start(bf16[32,2048]{1,0:T(8,128)(2,1)S(1)} %bitcast.112), channel_id=1, source_target_pairs={{0,8},{1,9},{2,10},{3,11},{4,12},{5,13},{6,14},{7,15},{8,0},{9,1},... | collective-permute-start | bytes 393224 | tf_op jit(solution)/shard_map/ppermute | solution.py:35
  85.9 10.7 %collective-permute-start.18 = (bf16[32,2048]{1,0:T(8,128)(2,1)S(1)}, bf16[32,2048]{1,0:T(8,128)(2,1)S(1)}, u32[]{:S(2)}, u32[]{:S(2)}) collective-permute-start(bf16[32,2048]{1,0:T(8,128)(2,1)S(1)} %bitcast.111), channel_id=1, source_target_pairs={{0,4},{1,5},{2,6},{3,7},{4,0},{5,1},{6,2},{7,3},{8,12},{9,13},{10,... | collective-permute-start | bytes 393224 | tf_op jit(solution)/shard_map/ppermute | solution.py:35

commit v24 on v23

--- a/solution.py
+++ b/solution.py
@@ -285,7 +285,9 @@
     others = [swap(column, owners, 1, 1)]
     weights = (w_gate[0], w_up[0])
     base = [base_products(piece, *weights) for piece in (column, others[0])]
+    here = here[::-1]
     here, sheet[1:], base = lax.optimization_barrier((here, sheet[1:], base))
+    here = here[::-1]
     for r in range(1, middle):
         others.append(swap(sheet[r], owners, 1, 1))
         base.append(base_products(sheet[r], *weights))
@@ -306,7 +308,6 @@
     last = jnp.swapaxes(summed[-1], 0, 1).reshape(-1, width)
     first = scatter_along(first, owners, *along_middle)
     last = scatter_along(last, owners, *along_outer)
-    first, last = lax.optimization_barrier((first, last))
     first = jnp.swapaxes(first.reshape(steps - 1, outer, rows, width), 0, 1).reshape(-1, width)
     first = scatter_along(first, owners, *along_outer)
     last = scatter_along(last, owners, *along_middle)

time: 97.5 us -> 97.9 us (level)
  waiting for transfers between devices: 48.9 us -> 51.1 us
  starting transfers between devices: 27.5 us -> 25.6 us
    ppermute x22, waiting for transfers between devices: 48.9 us -> 51.1 us  [swap(): return lax.ppermute(x, 'expert', [(i, i ^ k * stride) for i in range(n)])]
    ppermute x22, starting transfers between devices: 27.5 us -> 25.6 us  [swap(): return lax.ppermute(x, 'expert', [(i, i ^ k * stride) for i in range(n)])]
  transfers between devices with their start and end apart: 22 -> 22, of which waited for: 9 -> 10; matrix products, arithmetic and copies ran while one was open for 2% -> 3% of each run, Pallas kernels for 10% -> 10%
where the time goes in v24:
time: 97.9 us; the launch traced here: 97.8 us
  waiting for transfers between devices  51.1 us (52%)
  starting transfers between devices  25.6 us (26%)
  Pallas kernels  16.9 us (17%)
  other arithmetic  3.04 us (3%)
    ppermute x22, waiting for transfers between devices, swap(): return lax.ppermute(x, 'expert', [(i, i ^ k * stride) for i in range(n)])  51.1 us
    ppermute x22, starting transfers between devices, swap(): return lax.ppermute(x, 'expert', [(i, i ^ k * stride) for i in range(n)])  25.6 us
    pallas_call x3, Pallas kernels, finish_step(): pl.pallas_call(functools.partial(finish_kernel, len(pieces), first, rows)...  6.48 us
    pallas_call x4, Pallas kernels, base_products(): pl.pallas_call(base_kernel, out_shape=[out, out], in_specs=[pl.BlockSpec(...  5.62 us
    pallas_call x1, Pallas kernels, lay_out(): pl.pallas_call(first_kernel, out_shape=[jax.ShapeDtypeStruct((steps * row...  3.59 us
  transfers between devices with their start and end apart: 22, of which 10 were waited for; matrix products, arithmetic and copies ran while one was open for 3% of the time, Pallas kernels for 10%

profile of v24, /device:TPU:0, one launch (start us, length us, event | category | flops | bytes accessed | tf_op | source)
XLA Modules:
  0.0 97.8 jit_solution(18211687065451704776)
XLA Ops:
  0.0 3.6 %lay_out.1 = (bf16[48,2176]{1,0:T(8,128)(2,1)}, bf16[2,4,264,128]{3,2,1,0:T(8,128)(2,1)}, bf16[2,4,264,128]{3,2,1,0:T(8,128)(2,1)}) custom-call(s32[1]{0:T(128)} %bitcast.place_ref, s32[16]{0:T(128)} %placement_ref.1, bf16[3,16,2048]{2,1,0:T(8,128)(2,1)} %hidden_ref.1, s32[3,8,16]{2,1,0:T(8,128)} %bitcast.117, f32[3,8,16]{2,1,0:T(8,128)} %bitcast.118, ...), custom_call_target="tpu_custom_call" | custom-call | flops 1 | bytes 1 | tf_op jit(solution)/shard_map/lay_out/pallas_call | solution.py:99
  4.0 4.7 %collective-permute-start.2 = (bf16[48,2176]{1,0:T(8,128)(2,1)}, bf16[48,2176]{1,0:T(8,128)(2,1)S(1)}, u32[]{:S(2)}, u32[]{:S(2)}) collective-permute-start(bf16[48,2176]{1,0:T(8,128)(2,1)} %get-tuple-element.46), channel_id=1, source_target_pairs={{0,12},{1,13},{2,14},{3,15},{4,8},{5,9},{6,10},{7,11},{8,4},{9,5},... | collective-permute-start | bytes 626696 | tf_op jit(solution)/shard_map/ppermute | solution.py:35
  8.7 0.7 collective-permute-start.1
  9.4 1.3 %fusion.3 = (bf16[2,4,264,128]{3,2,0,1:T(8,128)(2,1)S(1)}, bf16[2,4,264,128]{3,2,0,1:T(8,128)(2,1)S(1)}) fusion(bf16[1,2,4,264,128]{4,3,0,2,1:T(8,128)(2,1)} %bitcast.104, bf16[1,2,4,264,128]{4,3,0,2,1:T(8,128)(2,1)S(1)} %bitcast.105), kind=kLoop, calls=%fused_computation.14 | loop fusion | flops 540672 | bytes 2162688 | tf_op jit(solution)/shard_map/squeeze | solution.py:278
  10.7 1.7 %collective-permute-start.4 = (bf16[2,4,264,128]{3,2,0,1:T(8,128)(2,1)S(1)}, bf16[2,4,264,128]{3,2,0,1:T(8,128)(2,1)S(1)}, u32[]{:S(2)}, u32[]{:S(2)}) collective-permute-start(bf16[2,4,264,128]{3,2,0,1:T(8,128)(2,1)S(1)} %get-tuple-element.88), channel_id=1, source_target_pairs={{0,2},{1,3},{2,0},{3,1},{4,6},{5,7},{6,4},{7,5},{8,10},{9,11},{10,... | collective-permute-start | bytes 1622024 | tf_op jit(solution)/shard_map/ppermute | solution.py:35
  12.4 2.7 %collective-permute-done.2 = bf16[48,2176]{1,0:T(8,128)(2,1)S(1)} collective-permute-done((bf16[48,2176]{1,0:T(8,128)(2,1)}, bf16[48,2176]{1,0:T(8,128)(2,1)S(1)}, u32[]{:S(2)}, u32[]{:S(2)}) %collective-permute-start.2) | collective-permute-done | bytes 208928 | tf_op jit(solution)/shard_map/ppermute | solution.py:35
  15.0 5.3 %collective-permute-done = bf16[48,2176]{1,0:T(8,128)(2,1)S(1)} collective-permute-done((bf16[48,2176]{1,0:T(8,128)(2,1)}, bf16[48,2176]{1,0:T(8,128)(2,1)S(1)}, u32[]{:S(2)}, u32[]{:S(2)}) %collective-permute-start) | collective-permute-done | bytes 208928 | tf_op jit(solution)/shard_map/ppermute | solution.py:35
  20.3 7.0 %collective-permute-done.1 = bf16[48,2176]{1,0:T(8,128)(2,1)S(1)} collective-permute-done((bf16[48,2176]{1,0:T(8,128)(2,1)}, bf16[48,2176]{1,0:T(8,128)(2,1)S(1)}, u32[]{:S(2)}, u32[]{:S(2)}) %collective-permute-start.1) | collective-permute-done | bytes 208928 | tf_op jit(solution)/shard_map/ppermute | solution.py:35
  27.7 1.6 %collective-permute-start.8 = (bf16[192,2176]{1,0:T(8,128)(2,1)S(1)}, bf16[192,2176]{1,0:T(8,128)(2,1)S(1)}, u32[]{:S(2)}, u32[]{:S(2)}) collective-permute-start(bf16[192,2176]{1,0:T(8,128)(2,1)S(1)} %bitcast.86), channel_id=1, source_target_pairs={{0,2},{1,3},{2,0},{3,1},{4,6},{5,7},{6,4},{7,5},{8,10},{9,11},{10,... | collective-permute-start | bytes 2506760 | tf_op jit(solution)/shard_map/ppermute | solution.py:35
  29.3 2.5 %collective-permute-start.5 = (bf16[4,264,128]{2,1,0:T(8,128)(2,1)S(1)}, bf16[4,264,128]{2,1,0:T(8,128)(2,1)S(1)}, u32[]{:S(2)}, u32[]{:S(2)}) collective-permute-start(bf16[4,264,128]{2,1,0:T(8,128)(2,1)S(1)} %get-tuple-element.50), channel_id=1, source_target_pairs={{0,12},{1,13},{2,14},{3,15},{4,8},{5,9},{6,10},{7,11},{8,4},{9,5},... | collective-permute-start | bytes 811016 | tf_op jit(solution)/shard_map/ppermute | solution.py:35
  31.8 1.9 %collective-permute-start.7 = (bf16[4,264,128]{2,1,0:T(8,128)(2,1)S(1)}, bf16[4,264,128]{2,1,0:T(8,128)(2,1)S(1)}, u32[]{:S(2)}, u32[]{:S(2)}) collective-permute-start(bf16[4,264,128]{2,1,0:T(8,128)(2,1)S(1)} %get-tuple-element.52), channel_id=1, source_target_pairs={{0,4},{1,5},{2,6},{3,7},{4,0},{5,1},{6,2},{7,3},{8,12},{9,13},{10,... | collective-permute-start | bytes 811016 | tf_op jit(solution)/shard_map/ppermute | solution.py:35
  33.7 1.4 %base_products.4 = (f32[192,768]{1,0:T(8,128)S(1)}, f32[192,768]{1,0:T(8,128)S(1)}) custom-call(bf16[192,2176]{1,0:T(8,128)(2,1)S(1)} %bitcast.87, bf16[2048,768]{1,0:T(8,128)(2,1)S(1)} %bitcast.77, bf16[2048,768]{1,0:T(8,128)(2,1)S(1)} %bitcast.81), custom_call_target="tpu_custom_call" | custom-call | flops 1 | bytes 1 | tf_op jit(solution)/shard_map/base_products/pallas_call | solution.py:196
  35.1 1.4 %base_products.5 = (f32[192,768]{1,0:T(8,128)S(1)}, f32[192,768]{1,0:T(8,128)S(1)}) custom-call(bf16[192,2176]{1,0:T(8,128)(2,1)S(1)} %collective-permute-done.9.x_ref.refs_2_, bf16[2048,768]{1,0:T(8,128)(2,1)S(1)} %bitcast.78, bf16[2048,768]{1,0:T(8,128)(2,1)S(1)} %bitcast.82), custom_call_target="tpu_custom_call" | custom-call | flops 1 | bytes 1 | tf_op jit(solution)/shard_map/base_products/pallas_call | solution.py:196
  36.5 4.1 %collective-permute-done.5.refs_3_ = bf16[4,264,128]{2,1,0:T(8,128)(2,1)S(1)} collective-permute-done((bf16[4,264,128]{2,1,0:T(8,128)(2,1)S(1)}, bf16[4,264,128]{2,1,0:T(8,128)(2,1)S(1)}, u32[]{:S(2)}, u32[]{:S(2)}) %collective-permute-start.5) | collective-permute-done | bytes 270368 | tf_op jit(solution)/shard_map/ppermute | solution.py:35
  40.6 13.9 %collective-permute-done.6.refs_2_ = bf16[4,264,128]{2,1,0:T(8,128)(2,1)S(1)} collective-permute-done((bf16[4,264,128]{2,1,0:T(8,128)(2,1)S(1)}, bf16[4,264,128]{2,1,0:T(8,128)(2,1)S(1)}, u32[]{:S(2)}, u32[]{:S(2)}) %collective-permute-start.6) | collective-permute-done | bytes 270368 | tf_op jit(solution)/shard_map/ppermute | solution.py:35
  54.5 1.4 %base_products.6 = (f32[192,768]{1,0:T(8,128)S(1)}, f32[192,768]{1,0:T(8,128)S(1)}) custom-call(bf16[192,2176]{1,0:T(8,128)(2,1)S(1)} %collective-permute-done.8.x_ref.refs_1_, bf16[2048,768]{1,0:T(8,128)(2,1)S(1)} %bitcast.79, bf16[2048,768]{1,0:T(8,128)(2,1)S(1)} %bitcast.83), custom_call_target="tpu_custom_call" | custom-call | flops 1 | bytes 1 | tf_op jit(solution)/shard_map/base_products/pallas_call | solution.py:196
  55.9 1.2 %relayout_factors.1 = (bf16[2048,128]{1,0:T(8,128)(2,1)S(1)}, bf16[64,768]{1,0:T(8,128)(2,1)S(1)}, bf16[64,768]{1,0:T(8,128)(2,1)S(1)}, bf16[768,128]{1,0:T(8,128)(2,1)S(1)}, bf16[64,2048]{1,0:T(8,128)(2,1)S(1)}) custom-call(s32[1]{0:T(128)} %bitcast.place_ref, bf16[4,264,128]{2,1,0:T(8,128)(2,1)S(1)} %get-tuple-element.67.refs_0_, ...), custom_call_target="tpu_custom_call" | custom-call | flops 1 | bytes 1 | tf_op jit(solution)/shard_map/relayout_factors/pallas_call | solution.py:173
  57.2 1.4 %base_products.7 = (f32[192,768]{1,0:T(8,128)S(1)}, f32[192,768]{1,0:T(8,128)S(1)}) custom-call(bf16[192,2176]{1,0:T(8,128)(2,1)S(1)} %collective-permute-done.10.x_ref.refs_3_, bf16[2048,768]{1,0:T(8,128)(2,1)S(1)} %bitcast.80, bf16[2048,768]{1,0:T(8,128)(2,1)S(1)} %bitcast.84), custom_call_target="tpu_custom_call" | custom-call | flops 1 | bytes 1 | tf_op jit(solution)/shard_map/base_products/pallas_call | solution.py:196
  59.0 2.2 %finish_step.4 = (f32[128,2048]{1,0:T(8,128)S(1)}, bf16[128,2048]{1,0:T(8,128)(2,1)S(1)}) custom-call(s32[1]{0:T(128)} %bitcast.place_ref, bf16[192,2176]{1,0:T(8,128)(2,1)S(1)} %bitcast.88, bf16[192,2176]{1,0:T(8,128)(2,1)S(1)} %collective-permute-done.8.x_ref.refs_1_, bf16[192,2176]{1,0:T(8,128)(2,1)S(1)} %collective-permute-done.9.x_ref.refs_2_, ...), custom_call_target="tpu_custom_call" | custom-call | flops 8589934592 | bytes 1 | tf_op jit(solution)/shard_map/finish_step/pallas_call | solution.py:239
  61.8 2.2 %finish_step.3 = (f32[128,2048]{1,0:T(8,128)S(1)}, bf16[128,2048]{1,0:T(8,128)(2,1)S(1)}) custom-call(s32[1]{0:T(128)} %bitcast.place_ref, bf16[192,2176]{1,0:T(8,128)(2,1)S(1)} %bitcast.89, bf16[192,2176]{1,0:T(8,128)(2,1)S(1)} %collective-permute-done.8.x_ref.refs_1_, bf16[192,2176]{1,0:T(8,128)(2,1)S(1)} %collective-permute-done.9.x_ref.refs_2_, ...), custom_call_target="tpu_custom_call" | custom-call | flops 8589934592 | bytes 1 | tf_op jit(solution)/shard_map/finish_step/pallas_call | solution.py:239
  64.0 2.2 %finish_step.5 = (f32[128,2048]{1,0:T(8,128)S(1)}, bf16[128,2048]{1,0:T(8,128)(2,1)S(1)}) custom-call(s32[1]{0:T(128)} %bitcast.place_ref, bf16[192,2176]{1,0:T(8,128)(2,1)S(1)} %bitcast.90, bf16[192,2176]{1,0:T(8,128)(2,1)S(1)} %collective-permute-done.8.x_ref.refs_1_, bf16[192,2176]{1,0:T(8,128)(2,1)S(1)} %collective-permute-done.9.x_ref.refs_2_, ...), custom_call_target="tpu_custom_call" | custom-call | flops 8589934592 | bytes 1 | tf_op jit(solution)/shard_map/finish_step/pallas_call | solution.py:239
  67.7 0.6 collective-permute-done.17
  68.6 1.9 %collective-permute-start.19 = (bf16[32,2048]{1,0:T(8,128)(2,1)S(1)}, bf16[32,2048]{1,0:T(8,128)(2,1)S(1)}, u32[]{:S(2)}, u32[]{:S(2)}) collective-permute-start(bf16[32,2048]{1,0:T(8,128)(2,1)S(1)} %bitcast.115), channel_id=1, source_target_pairs={{0,8},{1,9},{2,10},{3,11},{4,12},{5,13},{6,14},{7,15},{8,0},{9,1},... | collective-permute-start | bytes 393224 | tf_op jit(solution)/shard_map/ppermute | solution.py:35
  70.5 2.5 %collective-permute-start.20 = (bf16[32,2048]{1,0:T(8,128)(2,1)S(1)}, bf16[32,2048]{1,0:T(8,128)(2,1)S(1)}, u32[]{:S(2)}, u32[]{:S(2)}) collective-permute-start(bf16[32,2048]{1,0:T(8,128)(2,1)S(1)} %bitcast.113), channel_id=1, source_target_pairs={{0,12},{1,13},{2,14},{3,15},{4,8},{5,9},{6,10},{7,11},{8,4},{9,5},... | collective-permute-start | bytes 393224 | tf_op jit(solution)/shard_map/ppermute | solution.py:35
  73.1 2.7 %collective-permute-done.18 = bf16[32,2048]{1,0:T(8,128)(2,1)S(1)} collective-permute-done((bf16[32,2048]{1,0:T(8,128)(2,1)S(1)}, bf16[32,2048]{1,0:T(8,128)(2,1)S(1)}, u32[]{:S(2)}, u32[]{:S(2)}) %collective-permute-start.18) | collective-permute-done | bytes 131104 | tf_op jit(solution)/shard_map/ppermute | solution.py:35
  75.8 5.8 %collective-permute-done.19 = bf16[32,2048]{1,0:T(8,128)(2,1)S(1)} collective-permute-done((bf16[32,2048]{1,0:T(8,128)(2,1)S(1)}, bf16[32,2048]{1,0:T(8,128)(2,1)S(1)}, u32[]{:S(2)}, u32[]{:S(2)}) %collective-permute-start.19) | collective-permute-done | bytes 131104 | tf_op jit(solution)/shard_map/ppermute | solution.py:35
  81.6 1.0 %collective-permute-start.21 = (bf16[16,2048]{1,0:T(8,128)(2,1)S(1)}, bf16[16,2048]{1,0:T(8,128)(2,1)S(1)}, u32[]{:S(2)}, u32[]{:S(2)}) collective-permute-start(bf16[16,2048]{1,0:T(8,128)(2,1)S(1)} %slice.163), channel_id=1, source_target_pairs={{0,2},{1,3},{2,0},{3,1},{4,6},{5,7},{6,4},{7,5},{8,10},{9,11},{10,... | collective-permute-start | bytes 196616 | tf_op jit(solution)/shard_map/ppermute | solution.py:35
  82.9 2.4 %collective-permute-start.14 = (bf16[32,2048]{1,0:T(8,128)(2,1)S(1)}, bf16[32,2048]{1,0:T(8,128)(2,1)S(1)}, u32[]{:S(2)}, u32[]{:S(2)}) collective-permute-start(bf16[32,2048]{1,0:T(8,128)(2,1)S(1)} %bitcast.114), channel_id=1, source_target_pairs={{0,4},{1,5},{2,6},{3,7},{4,0},{5,1},{6,2},{7,3},{8,12},{9,13},{10,... | collective-permute-start | bytes 393224 | tf_op jit(solution)/shard_map/ppermute | solution.py:35
  85.3 2.4 %collective-permute-start.16 = (bf16[32,2048]{1,0:T(8,128)(2,1)S(1)}, bf16[32,2048]{1,0:T(8,128)(2,1)S(1)}, u32[]{:S(2)}, u32[]{:S(2)}) collective-permute-start(bf16[32,2048]{1,0:T(8,128)(2,1)S(1)} %bitcast.111), channel_id=1, source_target_pairs={{0,12},{1,13},{2,14},{3,15},{4,8},{5,9},{6,10},{7,11},{8,4},{9,5},... | collective-permute-start | bytes 393224 | tf_op jit(solution)/shard_map/ppermute | solution.py:35
  87.9 1.4 %collective-permute-done.14 = bf16[32,2048]{1,0:T(8,128)(2,1)S(1)} collective-permute-done((bf16[32,2048]{1,0:T(8,128)(2,1)S(1)}, bf16[32,2048]{1,0:T(8,128)(2,1)S(1)}, u32[]{:S(2)}, u32[]{:S(2)}) %collective-permute-start.14) | collective-permute-done | bytes 131104 | tf_op jit(solution)/shard_map/ppermute | solution.py:35
  89.3 7.7 %collective-permute-done.15 = bf16[32,2048]{1,0:T(8,128)(2,1)S(1)} collective-permute-done((bf16[32,2048]{1,0:T(8,128)(2,1)S(1)}, bf16[32,2048]{1,0:T(8,128)(2,1)S(1)}, u32[]{:S(2)}, u32[]{:S(2)}) %collective-permute-start.15) | collective-permute-done | bytes 131104 | tf_op jit(solution)/shard_map/ppermute | solution.py:35
  97.1 0.7 pad_maximum_fusion.7
  (53 shorter events, 4.2 us)
Async XLA Ops:
  3.6 23.7 %copy-start.3 = (bf16[48,2176]{1,0:T(8,128)(2,1)S(1)}, bf16[48,2176]{1,0:T(8,128)(2,1)}, u32[]{:S(2)}) copy-start(bf16[48,2176]{1,0:T(8,128)(2,1)} %get-tuple-element.46) | copy-start | bytes 626692
  3.6 5.8 %collective-permute-start.3 = (bf16[2,4,264,128]{3,2,1,0:T(8,128)(2,1)}, bf16[2,4,264,128]{3,2,1,0:T(8,128)(2,1)S(1)}, u32[]{:S(2)}, u32[]{:S(2)}) collective-permute-start(bf16[2,4,264,128]{3,2,1,0:T(8,128)(2,1)} %get-tuple-element.48), channel_id=1, source_target_pairs={{0,1},{1,0},{2,3},{3,2},{4,5},{5,4},{6,7},{7,6},{8,9},{9,8},{10,11... | collective-permute-start | bytes 1622024 | tf_op jit(solution)/shard_map/ppermute | solution.py:35
  4.0 11.0 %collective-permute-start.2 = (bf16[48,2176]{1,0:T(8,128)(2,1)}, bf16[48,2176]{1,0:T(8,128)(2,1)S(1)}, u32[]{:S(2)}, u32[]{:S(2)}) collective-permute-start(bf16[48,2176]{1,0:T(8,128)(2,1)} %get-tuple-element.46), channel_id=1, source_target_pairs={{0,12},{1,13},{2,14},{3,15},{4,8},{5,9},{6,10},{7,11},{8,4},{9,5},... | collective-permute-start | bytes 626696 | tf_op jit(solution)/shard_map/ppermute | solution.py:35
  8.7 11.6 %collective-permute-start = (bf16[48,2176]{1,0:T(8,128)(2,1)}, bf16[48,2176]{1,0:T(8,128)(2,1)S(1)}, u32[]{:S(2)}, u32[]{:S(2)}) collective-permute-start(bf16[48,2176]{1,0:T(8,128)(2,1)} %get-tuple-element.46), channel_id=1, source_target_pairs={{0,4},{1,5},{2,6},{3,7},{4,0},{5,1},{6,2},{7,3},{8,12},{9,13},{10,... | collective-permute-start | bytes 626696 | tf_op jit(solution)/shard_map/ppermute | solution.py:35
  8.7 18.6 %collective-permute-start.1 = (bf16[48,2176]{1,0:T(8,128)(2,1)}, bf16[48,2176]{1,0:T(8,128)(2,1)S(1)}, u32[]{:S(2)}, u32[]{:S(2)}) collective-permute-start(bf16[48,2176]{1,0:T(8,128)(2,1)} %get-tuple-element.46), channel_id=1, source_target_pairs={{0,8},{1,9},{2,10},{3,11},{4,12},{5,13},{6,14},{7,15},{8,0},{9,1},... | collective-permute-start | bytes 626696 | tf_op jit(solution)/shard_map/ppermute | solution.py:35
  9.4 24.3 %copy-start.1 = (bf16[1,2048,768]{2,1,0:T(8,128)(2,1)S(1)}, bf16[1,2048,768]{2,1,0:T(8,128)(2,1)}, u32[]{:S(2)}) copy-start(bf16[1,2048,768]{2,1,0:T(8,128)(2,1)} %param.14) | copy-start | bytes 9437188
  10.7 16.8 %collective-permute-start.4 = (bf16[2,4,264,128]{3,2,0,1:T(8,128)(2,1)S(1)}, bf16[2,4,264,128]{3,2,0,1:T(8,128)(2,1)S(1)}, u32[]{:S(2)}, u32[]{:S(2)}) collective-permute-start(bf16[2,4,264,128]{3,2,0,1:T(8,128)(2,1)S(1)} %get-tuple-element.88), channel_id=1, source_target_pairs={{0,2},{1,3},{2,0},{3,1},{4,6},{5,7},{6,4},{7,5},{8,10},{9,11},{10,... | collective-permute-start | bytes 1622024 | tf_op jit(solution)/shard_map/ppermute | solution.py:35
  27.4 6.3 %copy-start = (bf16[1,2048,768]{2,1,0:T(8,128)(2,1)S(1)}, bf16[1,2048,768]{2,1,0:T(8,128)(2,1)}, u32[]{:S(2)}) copy-start(bf16[1,2048,768]{2,1,0:T(8,128)(2,1)} %param.13) | copy-start | bytes 9437188
  27.6 7.5 %collective-permute-start.9 = (bf16[192,2176]{1,0:T(8,128)(2,1)S(1)}, bf16[192,2176]{1,0:T(8,128)(2,1)S(1)}, u32[]{:S(2)}, u32[]{:S(2)}) collective-permute-start(bf16[192,2176]{1,0:T(8,128)(2,1)S(1)} %bitcast.85), channel_id=1, source_target_pairs={{0,1},{1,0},{2,3},{3,2},{4,5},{5,4},{6,7},{7,6},{8,9},{9,8},{10,11... | collective-permute-start | bytes 2506760 | tf_op jit(solution)/shard_map/ppermute | solution.py:35
  27.7 26.8 %collective-permute-start.8 = (bf16[192,2176]{1,0:T(8,128)(2,1)S(1)}, bf16[192,2176]{1,0:T(8,128)(2,1)S(1)}, u32[]{:S(2)}, u32[]{:S(2)}) collective-permute-start(bf16[192,2176]{1,0:T(8,128)(2,1)S(1)} %bitcast.86), channel_id=1, source_target_pairs={{0,2},{1,3},{2,0},{3,1},{4,6},{5,7},{6,4},{7,5},{8,10},{9,11},{10,... | collective-permute-start | bytes 2506760 | tf_op jit(solution)/shard_map/ppermute | solution.py:35
  29.3 11.3 %collective-permute-start.5 = (bf16[4,264,128]{2,1,0:T(8,128)(2,1)S(1)}, bf16[4,264,128]{2,1,0:T(8,128)(2,1)S(1)}, u32[]{:S(2)}, u32[]{:S(2)}) collective-permute-start(bf16[4,264,128]{2,1,0:T(8,128)(2,1)S(1)} %get-tuple-element.50), channel_id=1, source_target_pairs={{0,12},{1,13},{2,14},{3,15},{4,8},{5,9},{6,10},{7,11},{8,4},{9,5},... | collective-permute-start | bytes 811016 | tf_op jit(solution)/shard_map/ppermute | solution.py:35
  31.8 22.7 %collective-permute-start.6 = (bf16[4,264,128]{2,1,0:T(8,128)(2,1)S(1)}, bf16[4,264,128]{2,1,0:T(8,128)(2,1)S(1)}, u32[]{:S(2)}, u32[]{:S(2)}) collective-permute-start(bf16[4,264,128]{2,1,0:T(8,128)(2,1)S(1)} %get-tuple-element.51), channel_id=1, source_target_pairs={{0,8},{1,9},{2,10},{3,11},{4,12},{5,13},{6,14},{7,15},{8,0},{9,1},... | collective-permute-start | bytes 811016 | tf_op jit(solution)/shard_map/ppermute | solution.py:35
  31.8 22.7 %collective-permute-start.7 = (bf16[4,264,128]{2,1,0:T(8,128)(2,1)S(1)}, bf16[4,264,128]{2,1,0:T(8,128)(2,1)S(1)}, u32[]{:S(2)}, u32[]{:S(2)}) collective-permute-start(bf16[4,264,128]{2,1,0:T(8,128)(2,1)S(1)} %get-tuple-element.52), channel_id=1, source_target_pairs={{0,4},{1,5},{2,6},{3,7},{4,0},{5,1},{6,2},{7,3},{8,12},{9,13},{10,... | collective-permute-start | bytes 811016 | tf_op jit(solution)/shard_map/ppermute | solution.py:35
  54.5 2.7 %collective-permute-start.10 = (bf16[192,2176]{1,0:T(8,128)(2,1)S(1)}, bf16[192,2176]{1,0:T(8,128)(2,1)S(1)}, u32[]{:S(2)}, u32[]{:S(2)}) collective-permute-start(bf16[192,2176]{1,0:T(8,128)(2,1)S(1)} %collective-permute-done.8.x_ref.refs_1_), channel_id=1, source_target_pairs={{0,1},{1,0},{2,3},{3,2},{4,5},{5,4},{6,7},{7,6},{8,9},{9,8},{10,11... | collective-permute-start | bytes 2506760 | tf_op jit(solution)/shard_map/ppermute | solution.py:35
  57.1 1.9 %copy-start.2 = (bf16[1,768,2048]{2,1,0:T(8,128)(2,1)S(1)}, bf16[1,768,2048]{2,1,0:T(8,128)(2,1)}, u32[]{:S(2)}) copy-start(bf16[1,768,2048]{2,1,0:T(8,128)(2,1)} %param.15) | copy-start | bytes 9437188
  61.2 5.6 %collective-permute-start.12 = (bf16[128,2048]{1,0:T(8,128)(2,1)S(1)}, bf16[128,2048]{1,0:T(8,128)(2,1)S(1)}, u32[]{:S(2)}, u32[]{:S(2)}) collective-permute-start(bf16[128,2048]{1,0:T(8,128)(2,1)S(1)} %get-tuple-element.80), channel_id=1, source_target_pairs={{0,1},{1,0},{2,3},{3,2},{4,5},{5,4},{6,7},{7,6},{8,9},{9,8},{10,11... | collective-permute-start | bytes 1572872 | tf_op jit(solution)/shard_map/ppermute | solution.py:35
  63.9 3.0 %collective-permute-start.11 = (bf16[128,2048]{1,0:T(8,128)(2,1)S(1)}, bf16[128,2048]{1,0:T(8,128)(2,1)S(1)}, u32[]{:S(2)}, u32[]{:S(2)}) collective-permute-start(bf16[128,2048]{1,0:T(8,128)(2,1)S(1)} %get-tuple-element.77), channel_id=1, source_target_pairs={{0,1},{1,0},{2,3},{3,2},{4,5},{5,4},{6,7},{7,6},{8,9},{9,8},{10,11... | collective-permute-start | bytes 1572872 | tf_op jit(solution)/shard_map/ppermute | solution.py:35
  66.2 2.1 %collective-permute-start.17 = (bf16[128,2048]{1,0:T(8,128)(2,1)S(1)}, bf16[128,2048]{1,0:T(8,128)(2,1)S(1)}, u32[]{:S(2)}, u32[]{:S(2)}) collective-permute-start(bf16[128,2048]{1,0:T(8,128)(2,1)S(1)} %get-tuple-element.86), channel_id=1, source_target_pairs={{0,1},{1,0},{2,3},{3,2},{4,5},{5,4},{6,7},{7,6},{8,9},{9,8},{10,11... | collective-permute-start | bytes 1572872 | tf_op jit(solution)/shard_map/ppermute | solution.py:35
  67.1 15.5 %collective-permute-start.13 = (bf16[128,2048]{1,0:T(8,128)(2,1)S(1)}, bf16[128,2048]{1,0:T(8,128)(2,1)S(1)}, u32[]{:S(2)}, u32[]{:S(2)}) collective-permute-start(bf16[128,2048]{1,0:T(8,128)(2,1)S(1)} %bitcast.106), channel_id=1, source_target_pairs={{0,2},{1,3},{2,0},{3,1},{4,6},{5,7},{6,4},{7,5},{8,10},{9,11},{10,... | collective-permute-start | bytes 1572872 | tf_op jit(solution)/shard_map/ppermute | solution.py:35
  68.5 7.3 %collective-permute-start.18 = (bf16[32,2048]{1,0:T(8,128)(2,1)S(1)}, bf16[32,2048]{1,0:T(8,128)(2,1)S(1)}, u32[]{:S(2)}, u32[]{:S(2)}) collective-permute-start(bf16[32,2048]{1,0:T(8,128)(2,1)S(1)} %bitcast.116), channel_id=1, source_target_pairs={{0,4},{1,5},{2,6},{3,7},{4,0},{5,1},{6,2},{7,3},{8,12},{9,13},{10,... | collective-permute-start | bytes 393224 | tf_op jit(solution)/shard_map/ppermute | solution.py:35
  68.6 13.0 %collective-permute-start.19 = (bf16[32,2048]{1,0:T(8,128)(2,1)S(1)}, bf16[32,2048]{1,0:T(8,128)(2,1)S(1)}, u32[]{:S(2)}, u32[]{:S(2)}) collective-permute-start(bf16[32,2048]{1,0:T(8,128)(2,1)S(1)} %bitcast.115), channel_id=1, source_target_pairs={{0,8},{1,9},{2,10},{3,11},{4,12},{5,13},{6,14},{7,15},{8,0},{9,1},... | collective-permute-start | bytes 393224 | tf_op jit(solution)/shard_map/ppermute | solution.py:35
  70.5 11.1 %collective-permute-start.20 = (bf16[32,2048]{1,0:T(8,128)(2,1)S(1)}, bf16[32,2048]{1,0:T(8,128)(2,1)S(1)}, u32[]{:S(2)}, u32[]{:S(2)}) collective-permute-start(bf16[32,2048]{1,0:T(8,128)(2,1)S(1)} %bitcast.113), channel_id=1, source_target_pairs={{0,12},{1,13},{2,14},{3,15},{4,8},{5,9},{6,10},{7,11},{8,4},{9,5},... | collective-permute-start | bytes 393224 | tf_op jit(solution)/shard_map/ppermute | solution.py:35
  81.6 6.1 %collective-permute-start.21 = (bf16[16,2048]{1,0:T(8,128)(2,1)S(1)}, bf16[16,2048]{1,0:T(8,128)(2,1)S(1)}, u32[]{:S(2)}, u32[]{:S(2)}) collective-permute-start(bf16[16,2048]{1,0:T(8,128)(2,1)S(1)} %slice.163), channel_id=1, source_target_pairs={{0,2},{1,3},{2,0},{3,1},{4,6},{5,7},{6,4},{7,5},{8,10},{9,11},{10,... | collective-permute-start | bytes 196616 | tf_op jit(solution)/shard_map/ppermute | solution.py:35
  82.9 6.4 %collective-permute-start.14 = (bf16[32,2048]{1,0:T(8,128)(2,1)S(1)}, bf16[32,2048]{1,0:T(8,128)(2,1)S(1)}, u32[]{:S(2)}, u32[]{:S(2)}) collective-permute-start(bf16[32,2048]{1,0:T(8,128)(2,1)S(1)} %bitcast.114), channel_id=1, source_target_pairs={{0,4},{1,5},{2,6},{3,7},{4,0},{5,1},{6,2},{7,3},{8,12},{9,13},{10,... | collective-permute-start | bytes 393224 | tf_op jit(solution)/shard_map/ppermute | solution.py:35
  85.3 11.7 %collective-permute-start.15 = (bf16[32,2048]{1,0:T(8,128)(2,1)S(1)}, bf16[32,2048]{1,0:T(8,128)(2,1)S(1)}, u32[]{:S(2)}, u32[]{:S(2)}) collective-permute-start(bf16[32,2048]{1,0:T(8,128)(2,1)S(1)} %bitcast.112), channel_id=1, source_target_pairs={{0,8},{1,9},{2,10},{3,11},{4,12},{5,13},{6,14},{7,15},{8,0},{9,1},... | collective-permute-start | bytes 393224 | tf_op jit(solution)/shard_map/ppermute | solution.py:35
  85.3 11.7 %collective-permute-start.16 = (bf16[32,2048]{1,0:T(8,128)(2,1)S(1)}, bf16[32,2048]{1,0:T(8,128)(2,1)S(1)}, u32[]{:S(2)}, u32[]{:S(2)}) collective-permute-start(bf16[32,2048]{1,0:T(8,128)(2,1)S(1)} %bitcast.111), channel_id=1, source_target_pairs={{0,12},{1,13},{2,14},{3,15},{4,8},{5,9},{6,10},{7,11},{8,4},{9,5},... | collective-permute-start | bytes 393224 | tf_op jit(solution)/shard_map/ppermute | solution.py:35

commit v25 on v24

--- a/solution.py
+++ b/solution.py
@@ -308,6 +308,7 @@
     last = jnp.swapaxes(summed[-1], 0, 1).reshape(-1, width)
     first = scatter_along(first, owners, *along_middle)
     last = scatter_along(last, owners, *along_outer)
+    first, last = lax.optimization_barrier((first, last))
     first = jnp.swapaxes(first.reshape(steps - 1, outer, rows, width), 0, 1).reshape(-1, width)
     first = scatter_along(first, owners, *along_outer)
     last = scatter_along(last, owners, *along_middle)

time: 97.9 us -> 96.3 us (0.984)
  transfers between devices with their start and end apart: 22 -> 22, of which waited for: 10 -> 9; matrix products, arithmetic and copies ran while one was open for 3% -> 2% of each run, Pallas kernels for 10% -> 10%
where the time goes in v25:
time: 96.3 us; the launch traced here: 96.1 us
  waiting for transfers between devices  50.3 us (52%)
  starting transfers between devices  24.7 us (26%)
  Pallas kernels  16.9 us (18%)
  other arithmetic  3.03 us (3%)
    ppermute x22, waiting for transfers between devices, swap(): return lax.ppermute(x, 'expert', [(i, i ^ k * stride) for i in range(n)])  50.3 us
    ppermute x22, starting transfers between devices, swap(): return lax.ppermute(x, 'expert', [(i, i ^ k * stride) for i in range(n)])  24.7 us
    pallas_call x3, Pallas kernels, finish_step(): pl.pallas_call(functools.partial(finish_kernel, len(pieces), first, rows)...  6.49 us
    pallas_call x4, Pallas kernels, base_products(): pl.pallas_call(base_kernel, out_shape=[out, out], in_specs=[pl.BlockSpec(...  5.63 us
    pallas_call x1, Pallas kernels, lay_out(): pl.pallas_call(first_kernel, out_shape=[jax.ShapeDtypeStruct((steps * row...  3.59 us
  transfers between devices with their start and end apart: 22, of which 9 were waited for; matrix products, arithmetic and copies ran while one was open for 2% of the time, Pallas kernels for 10%

profile of v25, /device:TPU:0, one launch (start us, length us, event | category | flops | bytes accessed | tf_op | source)
XLA Modules:
  0.0 96.1 jit_solution(12878326537638090975)
XLA Ops:
  0.0 3.6 %lay_out.1 = (bf16[48,2176]{1,0:T(8,128)(2,1)}, bf16[2,4,264,128]{3,2,1,0:T(8,128)(2,1)}, bf16[2,4,264,128]{3,2,1,0:T(8,128)(2,1)}) custom-call(s32[1]{0:T(128)} %bitcast.place_ref, s32[16]{0:T(128)} %placement_ref.1, bf16[3,16,2048]{2,1,0:T(8,128)(2,1)} %hidden_ref.1, s32[3,8,16]{2,1,0:T(8,128)} %bitcast.117, f32[3,8,16]{2,1,0:T(8,128)} %bitcast.118, ...), custom_call_target="tpu_custom_call" | custom-call | flops 1 | bytes 1 | tf_op jit(solution)/shard_map/lay_out/pallas_call | solution.py:99
  4.0 4.7 %collective-permute-start.2 = (bf16[48,2176]{1,0:T(8,128)(2,1)}, bf16[48,2176]{1,0:T(8,128)(2,1)S(1)}, u32[]{:S(2)}, u32[]{:S(2)}) collective-permute-start(bf16[48,2176]{1,0:T(8,128)(2,1)} %get-tuple-element.48), channel_id=1, source_target_pairs={{0,12},{1,13},{2,14},{3,15},{4,8},{5,9},{6,10},{7,11},{8,4},{9,5},... | collective-permute-start | bytes 626696 | tf_op jit(solution)/shard_map/ppermute | solution.py:35
  8.7 0.7 collective-permute-start
  9.4 1.3 %fusion.3 = (bf16[2,4,264,128]{3,2,0,1:T(8,128)(2,1)S(1)}, bf16[2,4,264,128]{3,2,0,1:T(8,128)(2,1)S(1)}) fusion(bf16[1,2,4,264,128]{4,3,0,2,1:T(8,128)(2,1)} %bitcast.104, bf16[1,2,4,264,128]{4,3,0,2,1:T(8,128)(2,1)S(1)} %bitcast.105), kind=kLoop, calls=%fused_computation.14 | loop fusion | flops 540672 | bytes 2162688 | tf_op jit(solution)/shard_map/squeeze | solution.py:278
  10.7 1.7 %collective-permute-start.4 = (bf16[2,4,264,128]{3,2,0,1:T(8,128)(2,1)S(1)}, bf16[2,4,264,128]{3,2,0,1:T(8,128)(2,1)S(1)}, u32[]{:S(2)}, u32[]{:S(2)}) collective-permute-start(bf16[2,4,264,128]{3,2,0,1:T(8,128)(2,1)S(1)} %get-tuple-element.92), channel_id=1, source_target_pairs={{0,2},{1,3},{2,0},{3,1},{4,6},{5,7},{6,4},{7,5},{8,10},{9,11},{10,... | collective-permute-start | bytes 1622024 | tf_op jit(solution)/shard_map/ppermute | solution.py:35
  12.4 2.7 %collective-permute-done.2 = bf16[48,2176]{1,0:T(8,128)(2,1)S(1)} collective-permute-done((bf16[48,2176]{1,0:T(8,128)(2,1)}, bf16[48,2176]{1,0:T(8,128)(2,1)S(1)}, u32[]{:S(2)}, u32[]{:S(2)}) %collective-permute-start.2) | collective-permute-done | bytes 208928 | tf_op jit(solution)/shard_map/ppermute | solution.py:35
  15.1 12.2 %collective-permute-done.1 = bf16[48,2176]{1,0:T(8,128)(2,1)S(1)} collective-permute-done((bf16[48,2176]{1,0:T(8,128)(2,1)}, bf16[48,2176]{1,0:T(8,128)(2,1)S(1)}, u32[]{:S(2)}, u32[]{:S(2)}) %collective-permute-start.1) | collective-permute-done | bytes 208928 | tf_op jit(solution)/shard_map/ppermute | solution.py:35
  27.7 1.6 %collective-permute-start.8 = (bf16[192,2176]{1,0:T(8,128)(2,1)S(1)}, bf16[192,2176]{1,0:T(8,128)(2,1)S(1)}, u32[]{:S(2)}, u32[]{:S(2)}) collective-permute-start(bf16[192,2176]{1,0:T(8,128)(2,1)S(1)} %bitcast.86), channel_id=1, source_target_pairs={{0,2},{1,3},{2,0},{3,1},{4,6},{5,7},{6,4},{7,5},{8,10},{9,11},{10,... | collective-permute-start | bytes 2506760 | tf_op jit(solution)/shard_map/ppermute | solution.py:35
  29.3 2.5 %collective-permute-start.5 = (bf16[4,264,128]{2,1,0:T(8,128)(2,1)S(1)}, bf16[4,264,128]{2,1,0:T(8,128)(2,1)S(1)}, u32[]{:S(2)}, u32[]{:S(2)}) collective-permute-start(bf16[4,264,128]{2,1,0:T(8,128)(2,1)S(1)} %get-tuple-element.52), channel_id=1, source_target_pairs={{0,12},{1,13},{2,14},{3,15},{4,8},{5,9},{6,10},{7,11},{8,4},{9,5},... | collective-permute-start | bytes 811016 | tf_op jit(solution)/shard_map/ppermute | solution.py:35
  31.8 1.9 %collective-permute-start.7 = (bf16[4,264,128]{2,1,0:T(8,128)(2,1)S(1)}, bf16[4,264,128]{2,1,0:T(8,128)(2,1)S(1)}, u32[]{:S(2)}, u32[]{:S(2)}) collective-permute-start(bf16[4,264,128]{2,1,0:T(8,128)(2,1)S(1)} %get-tuple-element.54), channel_id=1, source_target_pairs={{0,4},{1,5},{2,6},{3,7},{4,0},{5,1},{6,2},{7,3},{8,12},{9,13},{10,... | collective-permute-start | bytes 811016 | tf_op jit(solution)/shard_map/ppermute | solution.py:35
  33.7 1.4 %base_products.4 = (f32[192,768]{1,0:T(8,128)S(1)}, f32[192,768]{1,0:T(8,128)S(1)}) custom-call(bf16[192,2176]{1,0:T(8,128)(2,1)S(1)} %bitcast.87, bf16[2048,768]{1,0:T(8,128)(2,1)S(1)} %bitcast.77, bf16[2048,768]{1,0:T(8,128)(2,1)S(1)} %bitcast.81), custom_call_target="tpu_custom_call" | custom-call | flops 1 | bytes 1 | tf_op jit(solution)/shard_map/base_products/pallas_call | solution.py:196
  35.1 1.4 %base_products.5 = (f32[192,768]{1,0:T(8,128)S(1)}, f32[192,768]{1,0:T(8,128)S(1)}) custom-call(bf16[192,2176]{1,0:T(8,128)(2,1)S(1)} %collective-permute-done.9.x_ref.refs_2_, bf16[2048,768]{1,0:T(8,128)(2,1)S(1)} %bitcast.78, bf16[2048,768]{1,0:T(8,128)(2,1)S(1)} %bitcast.82), custom_call_target="tpu_custom_call" | custom-call | flops 1 | bytes 1 | tf_op jit(solution)/shard_map/base_products/pallas_call | solution.py:196
  36.5 4.1 %collective-permute-done.5.refs_3_ = bf16[4,264,128]{2,1,0:T(8,128)(2,1)S(1)} collective-permute-done((bf16[4,264,128]{2,1,0:T(8,128)(2,1)S(1)}, bf16[4,264,128]{2,1,0:T(8,128)(2,1)S(1)}, u32[]{:S(2)}, u32[]{:S(2)}) %collective-permute-start.5) | collective-permute-done | bytes 270368 | tf_op jit(solution)/shard_map/ppermute | solution.py:35
  40.6 13.9 %collective-permute-done.6.refs_2_ = bf16[4,264,128]{2,1,0:T(8,128)(2,1)S(1)} collective-permute-done((bf16[4,264,128]{2,1,0:T(8,128)(2,1)S(1)}, bf16[4,264,128]{2,1,0:T(8,128)(2,1)S(1)}, u32[]{:S(2)}, u32[]{:S(2)}) %collective-permute-start.6) | collective-permute-done | bytes 270368 | tf_op jit(solution)/shard_map/ppermute | solution.py:35
  54.5 1.4 %base_products.6 = (f32[192,768]{1,0:T(8,128)S(1)}, f32[192,768]{1,0:T(8,128)S(1)}) custom-call(bf16[192,2176]{1,0:T(8,128)(2,1)S(1)} %collective-permute-done.8.x_ref.refs_1_, bf16[2048,768]{1,0:T(8,128)(2,1)S(1)} %bitcast.79, bf16[2048,768]{1,0:T(8,128)(2,1)S(1)} %bitcast.83), custom_call_target="tpu_custom_call" | custom-call | flops 1 | bytes 1 | tf_op jit(solution)/shard_map/base_products/pallas_call | solution.py:196
  55.9 1.2 %relayout_factors.1 = (bf16[2048,128]{1,0:T(8,128)(2,1)S(1)}, bf16[64,768]{1,0:T(8,128)(2,1)S(1)}, bf16[64,768]{1,0:T(8,128)(2,1)S(1)}, bf16[768,128]{1,0:T(8,128)(2,1)S(1)}, bf16[64,2048]{1,0:T(8,128)(2,1)S(1)}) custom-call(s32[1]{0:T(128)} %bitcast.place_ref, bf16[4,264,128]{2,1,0:T(8,128)(2,1)S(1)} %get-tuple-element.69.refs_0_, ...), custom_call_target="tpu_custom_call" | custom-call | flops 1 | bytes 1 | tf_op jit(solution)/shard_map/relayout_factors/pallas_call | solution.py:173
  57.1 1.4 %base_products.7 = (f32[192,768]{1,0:T(8,128)S(1)}, f32[192,768]{1,0:T(8,128)S(1)}) custom-call(bf16[192,2176]{1,0:T(8,128)(2,1)S(1)} %collective-permute-done.10.x_ref.refs_3_, bf16[2048,768]{1,0:T(8,128)(2,1)S(1)} %bitcast.80, bf16[2048,768]{1,0:T(8,128)(2,1)S(1)} %bitcast.84), custom_call_target="tpu_custom_call" | custom-call | flops 1 | bytes 1 | tf_op jit(solution)/shard_map/base_products/pallas_call | solution.py:196
  59.0 2.2 %finish_step.3 = (f32[128,2048]{1,0:T(8,128)S(1)}, bf16[128,2048]{1,0:T(8,128)(2,1)S(1)}) custom-call(s32[1]{0:T(128)} %bitcast.place_ref, bf16[192,2176]{1,0:T(8,128)(2,1)S(1)} %bitcast.88, bf16[192,2176]{1,0:T(8,128)(2,1)S(1)} %collective-permute-done.8.x_ref.refs_1_, bf16[192,2176]{1,0:T(8,128)(2,1)S(1)} %collective-permute-done.9.x_ref.refs_2_, ...), custom_call_target="tpu_custom_call" | custom-call | flops 8589934592 | bytes 1 | tf_op jit(solution)/shard_map/finish_step/pallas_call | solution.py:239
  61.2 0.6 collective-permute-start.11
  61.7 2.2 %finish_step.4 = (f32[128,2048]{1,0:T(8,128)S(1)}, bf16[128,2048]{1,0:T(8,128)(2,1)S(1)}) custom-call(s32[1]{0:T(128)} %bitcast.place_ref, bf16[192,2176]{1,0:T(8,128)(2,1)S(1)} %bitcast.89, bf16[192,2176]{1,0:T(8,128)(2,1)S(1)} %collective-permute-done.8.x_ref.refs_1_, bf16[192,2176]{1,0:T(8,128)(2,1)S(1)} %collective-permute-done.9.x_ref.refs_2_, ...), custom_call_target="tpu_custom_call" | custom-call | flops 8589934592 | bytes 1 | tf_op jit(solution)/shard_map/finish_step/pallas_call | solution.py:239
  64.0 2.2 %finish_step.5 = (f32[128,2048]{1,0:T(8,128)S(1)}, bf16[128,2048]{1,0:T(8,128)(2,1)S(1)}) custom-call(s32[1]{0:T(128)} %bitcast.place_ref, bf16[192,2176]{1,0:T(8,128)(2,1)S(1)} %bitcast.90, bf16[192,2176]{1,0:T(8,128)(2,1)S(1)} %collective-permute-done.8.x_ref.refs_1_, bf16[192,2176]{1,0:T(8,128)(2,1)S(1)} %collective-permute-done.9.x_ref.refs_2_, ...), custom_call_target="tpu_custom_call" | custom-call | flops 8589934592 | bytes 1 | tf_op jit(solution)/shard_map/finish_step/pallas_call | solution.py:239
  67.1 0.6 collective-permute-start.13
  67.7 0.6 collective-permute-done.14
  68.5 1.4 %collective-permute-start.17 = (bf16[32,2048]{1,0:T(8,128)(2,1)S(1)}, bf16[32,2048]{1,0:T(8,128)(2,1)S(1)}, u32[]{:S(2)}, u32[]{:S(2)}) collective-permute-start(bf16[32,2048]{1,0:T(8,128)(2,1)S(1)} %bitcast.116), channel_id=1, source_target_pairs={{0,12},{1,13},{2,14},{3,15},{4,8},{5,9},{6,10},{7,11},{8,4},{9,5},... | collective-permute-start | bytes 393224 | tf_op jit(solution)/shard_map/ppermute | solution.py:35
  69.9 3.0 %collective-permute-start.15 = (bf16[32,2048]{1,0:T(8,128)(2,1)S(1)}, bf16[32,2048]{1,0:T(8,128)(2,1)S(1)}, u32[]{:S(2)}, u32[]{:S(2)}) collective-permute-start(bf16[32,2048]{1,0:T(8,128)(2,1)S(1)} %bitcast.113), channel_id=1, source_target_pairs={{0,4},{1,5},{2,6},{3,7},{4,0},{5,1},{6,2},{7,3},{8,12},{9,13},{10,... | collective-permute-start | bytes 393224 | tf_op jit(solution)/shard_map/ppermute | solution.py:35
  73.0 3.8 %collective-permute-done.17 = bf16[32,2048]{1,0:T(8,128)(2,1)S(1)} collective-permute-done((bf16[32,2048]{1,0:T(8,128)(2,1)S(1)}, bf16[32,2048]{1,0:T(8,128)(2,1)S(1)}, u32[]{:S(2)}, u32[]{:S(2)}) %collective-permute-start.17) | collective-permute-done | bytes 131104 | tf_op jit(solution)/shard_map/ppermute | solution.py:35
  76.8 5.0 %collective-permute-done.16 = bf16[32,2048]{1,0:T(8,128)(2,1)S(1)} collective-permute-done((bf16[32,2048]{1,0:T(8,128)(2,1)S(1)}, bf16[32,2048]{1,0:T(8,128)(2,1)S(1)}, u32[]{:S(2)}, u32[]{:S(2)}) %collective-permute-start.16) | collective-permute-done | bytes 131104 | tf_op jit(solution)/shard_map/ppermute | solution.py:35
  82.7 1.5 %collective-permute-start.20 = (bf16[32,2048]{1,0:T(8,128)(2,1)S(1)}, bf16[32,2048]{1,0:T(8,128)(2,1)S(1)}, u32[]{:S(2)}, u32[]{:S(2)}) collective-permute-start(bf16[32,2048]{1,0:T(8,128)(2,1)S(1)} %bitcast.114), channel_id=1, source_target_pairs={{0,12},{1,13},{2,14},{3,15},{4,8},{5,9},{6,10},{7,11},{8,4},{9,5},... | collective-permute-start | bytes 393224 | tf_op jit(solution)/shard_map/ppermute | solution.py:35
  84.2 3.0 %collective-permute-start.18 = (bf16[32,2048]{1,0:T(8,128)(2,1)S(1)}, bf16[32,2048]{1,0:T(8,128)(2,1)S(1)}, u32[]{:S(2)}, u32[]{:S(2)}) collective-permute-start(bf16[32,2048]{1,0:T(8,128)(2,1)S(1)} %bitcast.111), channel_id=1, source_target_pairs={{0,4},{1,5},{2,6},{3,7},{4,0},{5,1},{6,2},{7,3},{8,12},{9,13},{10,... | collective-permute-start | bytes 393224 | tf_op jit(solution)/shard_map/ppermute | solution.py:35
  87.2 3.9 %collective-permute-done.20 = bf16[32,2048]{1,0:T(8,128)(2,1)S(1)} collective-permute-done((bf16[32,2048]{1,0:T(8,128)(2,1)S(1)}, bf16[32,2048]{1,0:T(8,128)(2,1)S(1)}, u32[]{:S(2)}, u32[]{:S(2)}) %collective-permute-start.20) | collective-permute-done | bytes 131104 | tf_op jit(solution)/shard_map/ppermute | solution.py:35
  91.1 4.3 %collective-permute-done.19 = bf16[32,2048]{1,0:T(8,128)(2,1)S(1)} collective-permute-done((bf16[32,2048]{1,0:T(8,128)(2,1)S(1)}, bf16[32,2048]{1,0:T(8,128)(2,1)S(1)}, u32[]{:S(2)}, u32[]{:S(2)}) %collective-permute-start.19) | collective-permute-done | bytes 131104 | tf_op jit(solution)/shard_map/ppermute | solution.py:35
  95.4 0.7 pad_maximum_fusion.7
  (53 shorter events, 3.6 us)
Async XLA Ops:
  3.6 23.7 %copy-start.3 = (bf16[48,2176]{1,0:T(8,128)(2,1)S(1)}, bf16[48,2176]{1,0:T(8,128)(2,1)}, u32[]{:S(2)}) copy-start(bf16[48,2176]{1,0:T(8,128)(2,1)} %get-tuple-element.48) | copy-start | bytes 626692
  3.6 5.8 %collective-permute-start.3 = (bf16[2,4,264,128]{3,2,1,0:T(8,128)(2,1)}, bf16[2,4,264,128]{3,2,1,0:T(8,128)(2,1)S(1)}, u32[]{:S(2)}, u32[]{:S(2)}) collective-permute-start(bf16[2,4,264,128]{3,2,1,0:T(8,128)(2,1)} %get-tuple-element.50), channel_id=1, source_target_pairs={{0,1},{1,0},{2,3},{3,2},{4,5},{5,4},{6,7},{7,6},{8,9},{9,8},{10,11... | collective-permute-start | bytes 1622024 | tf_op jit(solution)/shard_map/ppermute | solution.py:35
  4.0 11.0 %collective-permute-start.2 = (bf16[48,2176]{1,0:T(8,128)(2,1)}, bf16[48,2176]{1,0:T(8,128)(2,1)S(1)}, u32[]{:S(2)}, u32[]{:S(2)}) collective-permute-start(bf16[48,2176]{1,0:T(8,128)(2,1)} %get-tuple-element.48), channel_id=1, source_target_pairs={{0,12},{1,13},{2,14},{3,15},{4,8},{5,9},{6,10},{7,11},{8,4},{9,5},... | collective-permute-start | bytes 626696 | tf_op jit(solution)/shard_map/ppermute | solution.py:35
  8.7 18.6 %collective-permute-start.1 = (bf16[48,2176]{1,0:T(8,128)(2,1)}, bf16[48,2176]{1,0:T(8,128)(2,1)S(1)}, u32[]{:S(2)}, u32[]{:S(2)}) collective-permute-start(bf16[48,2176]{1,0:T(8,128)(2,1)} %get-tuple-element.48), channel_id=1, source_target_pairs={{0,8},{1,9},{2,10},{3,11},{4,12},{5,13},{6,14},{7,15},{8,0},{9,1},... | collective-permute-start | bytes 626696 | tf_op jit(solution)/shard_map/ppermute | solution.py:35
  8.7 18.6 %collective-permute-start = (bf16[48,2176]{1,0:T(8,128)(2,1)}, bf16[48,2176]{1,0:T(8,128)(2,1)S(1)}, u32[]{:S(2)}, u32[]{:S(2)}) collective-permute-start(bf16[48,2176]{1,0:T(8,128)(2,1)} %get-tuple-element.48), channel_id=1, source_target_pairs={{0,4},{1,5},{2,6},{3,7},{4,0},{5,1},{6,2},{7,3},{8,12},{9,13},{10,... | collective-permute-start | bytes 626696 | tf_op jit(solution)/shard_map/ppermute | solution.py:35
  9.4 24.3 %copy-start.1 = (bf16[1,2048,768]{2,1,0:T(8,128)(2,1)S(1)}, bf16[1,2048,768]{2,1,0:T(8,128)(2,1)}, u32[]{:S(2)}) copy-start(bf16[1,2048,768]{2,1,0:T(8,128)(2,1)} %param.14) | copy-start | bytes 9437188
  10.7 16.8 %collective-permute-start.4 = (bf16[2,4,264,128]{3,2,0,1:T(8,128)(2,1)S(1)}, bf16[2,4,264,128]{3,2,0,1:T(8,128)(2,1)S(1)}, u32[]{:S(2)}, u32[]{:S(2)}) collective-permute-start(bf16[2,4,264,128]{3,2,0,1:T(8,128)(2,1)S(1)} %get-tuple-element.92), channel_id=1, source_target_pairs={{0,2},{1,3},{2,0},{3,1},{4,6},{5,7},{6,4},{7,5},{8,10},{9,11},{10,... | collective-permute-start | bytes 1622024 | tf_op jit(solution)/shard_map/ppermute | solution.py:35
  27.4 6.3 %copy-start = (bf16[1,2048,768]{2,1,0:T(8,128)(2,1)S(1)}, bf16[1,2048,768]{2,1,0:T(8,128)(2,1)}, u32[]{:S(2)}) copy-start(bf16[1,2048,768]{2,1,0:T(8,128)(2,1)} %param.13) | copy-start | bytes 9437188
  27.6 7.5 %collective-permute-start.9 = (bf16[192,2176]{1,0:T(8,128)(2,1)S(1)}, bf16[192,2176]{1,0:T(8,128)(2,1)S(1)}, u32[]{:S(2)}, u32[]{:S(2)}) collective-permute-start(bf16[192,2176]{1,0:T(8,128)(2,1)S(1)} %bitcast.85), channel_id=1, source_target_pairs={{0,1},{1,0},{2,3},{3,2},{4,5},{5,4},{6,7},{7,6},{8,9},{9,8},{10,11... | collective-permute-start | bytes 2506760 | tf_op jit(solution)/shard_map/ppermute | solution.py:35
  27.7 26.7 %collective-permute-start.8 = (bf16[192,2176]{1,0:T(8,128)(2,1)S(1)}, bf16[192,2176]{1,0:T(8,128)(2,1)S(1)}, u32[]{:S(2)}, u32[]{:S(2)}) collective-permute-start(bf16[192,2176]{1,0:T(8,128)(2,1)S(1)} %bitcast.86), channel_id=1, source_target_pairs={{0,2},{1,3},{2,0},{3,1},{4,6},{5,7},{6,4},{7,5},{8,10},{9,11},{10,... | collective-permute-start | bytes 2506760 | tf_op jit(solution)/shard_map/ppermute | solution.py:35
  29.3 11.3 %collective-permute-start.5 = (bf16[4,264,128]{2,1,0:T(8,128)(2,1)S(1)}, bf16[4,264,128]{2,1,0:T(8,128)(2,1)S(1)}, u32[]{:S(2)}, u32[]{:S(2)}) collective-permute-start(bf16[4,264,128]{2,1,0:T(8,128)(2,1)S(1)} %get-tuple-element.52), channel_id=1, source_target_pairs={{0,12},{1,13},{2,14},{3,15},{4,8},{5,9},{6,10},{7,11},{8,4},{9,5},... | collective-permute-start | bytes 811016 | tf_op jit(solution)/shard_map/ppermute | solution.py:35
  31.8 22.7 %collective-permute-start.6 = (bf16[4,264,128]{2,1,0:T(8,128)(2,1)S(1)}, bf16[4,264,128]{2,1,0:T(8,128)(2,1)S(1)}, u32[]{:S(2)}, u32[]{:S(2)}) collective-permute-start(bf16[4,264,128]{2,1,0:T(8,128)(2,1)S(1)} %get-tuple-element.53), channel_id=1, source_target_pairs={{0,8},{1,9},{2,10},{3,11},{4,12},{5,13},{6,14},{7,15},{8,0},{9,1},... | collective-permute-start | bytes 811016 | tf_op jit(solution)/shard_map/ppermute | solution.py:35
  31.8 22.7 %collective-permute-start.7 = (bf16[4,264,128]{2,1,0:T(8,128)(2,1)S(1)}, bf16[4,264,128]{2,1,0:T(8,128)(2,1)S(1)}, u32[]{:S(2)}, u32[]{:S(2)}) collective-permute-start(bf16[4,264,128]{2,1,0:T(8,128)(2,1)S(1)} %get-tuple-element.54), channel_id=1, source_target_pairs={{0,4},{1,5},{2,6},{3,7},{4,0},{5,1},{6,2},{7,3},{8,12},{9,13},{10,... | collective-permute-start | bytes 811016 | tf_op jit(solution)/shard_map/ppermute | solution.py:35
  54.4 2.7 %collective-permute-start.10 = (bf16[192,2176]{1,0:T(8,128)(2,1)S(1)}, bf16[192,2176]{1,0:T(8,128)(2,1)S(1)}, u32[]{:S(2)}, u32[]{:S(2)}) collective-permute-start(bf16[192,2176]{1,0:T(8,128)(2,1)S(1)} %collective-permute-done.8.x_ref.refs_1_), channel_id=1, source_target_pairs={{0,1},{1,0},{2,3},{3,2},{4,5},{5,4},{6,7},{7,6},{8,9},{9,8},{10,11... | collective-permute-start | bytes 2506760 | tf_op jit(solution)/shard_map/ppermute | solution.py:35
  57.1 1.9 %copy-start.2 = (bf16[1,768,2048]{2,1,0:T(8,128)(2,1)S(1)}, bf16[1,768,2048]{2,1,0:T(8,128)(2,1)}, u32[]{:S(2)}) copy-start(bf16[1,768,2048]{2,1,0:T(8,128)(2,1)} %param.15) | copy-start | bytes 9437188
  61.2 5.5 %collective-permute-start.11 = (bf16[128,2048]{1,0:T(8,128)(2,1)S(1)}, bf16[128,2048]{1,0:T(8,128)(2,1)S(1)}, u32[]{:S(2)}, u32[]{:S(2)}) collective-permute-start(bf16[128,2048]{1,0:T(8,128)(2,1)S(1)} %get-tuple-element.79), channel_id=1, source_target_pairs={{0,1},{1,0},{2,3},{3,2},{4,5},{5,4},{6,7},{7,6},{8,9},{9,8},{10,11... | collective-permute-start | bytes 1572872 | tf_op jit(solution)/shard_map/ppermute | solution.py:35
  63.9 3.0 %collective-permute-start.12 = (bf16[128,2048]{1,0:T(8,128)(2,1)S(1)}, bf16[128,2048]{1,0:T(8,128)(2,1)S(1)}, u32[]{:S(2)}, u32[]{:S(2)}) collective-permute-start(bf16[128,2048]{1,0:T(8,128)(2,1)S(1)} %get-tuple-element.82), channel_id=1, source_target_pairs={{0,1},{1,0},{2,3},{3,2},{4,5},{5,4},{6,7},{7,6},{8,9},{9,8},{10,11... | collective-permute-start | bytes 1572872 | tf_op jit(solution)/shard_map/ppermute | solution.py:35
  66.2 2.1 %collective-permute-start.14 = (bf16[128,2048]{1,0:T(8,128)(2,1)S(1)}, bf16[128,2048]{1,0:T(8,128)(2,1)S(1)}, u32[]{:S(2)}, u32[]{:S(2)}) collective-permute-start(bf16[128,2048]{1,0:T(8,128)(2,1)S(1)} %get-tuple-element.88), channel_id=1, source_target_pairs={{0,1},{1,0},{2,3},{3,2},{4,5},{5,4},{6,7},{7,6},{8,9},{9,8},{10,11... | collective-permute-start | bytes 1572872 | tf_op jit(solution)/shard_map/ppermute | solution.py:35
  67.1 14.8 %collective-permute-start.13 = (bf16[128,2048]{1,0:T(8,128)(2,1)S(1)}, bf16[128,2048]{1,0:T(8,128)(2,1)S(1)}, u32[]{:S(2)}, u32[]{:S(2)}) collective-permute-start(bf16[128,2048]{1,0:T(8,128)(2,1)S(1)} %bitcast.106), channel_id=1, source_target_pairs={{0,2},{1,3},{2,0},{3,1},{4,6},{5,7},{6,4},{7,5},{8,10},{9,11},{10,... | collective-permute-start | bytes 1572872 | tf_op jit(solution)/shard_map/ppermute | solution.py:35
  68.5 8.3 %collective-permute-start.17 = (bf16[32,2048]{1,0:T(8,128)(2,1)S(1)}, bf16[32,2048]{1,0:T(8,128)(2,1)S(1)}, u32[]{:S(2)}, u32[]{:S(2)}) collective-permute-start(bf16[32,2048]{1,0:T(8,128)(2,1)S(1)} %bitcast.116), channel_id=1, source_target_pairs={{0,12},{1,13},{2,14},{3,15},{4,8},{5,9},{6,10},{7,11},{8,4},{9,5},... | collective-permute-start | bytes 393224 | tf_op jit(solution)/shard_map/ppermute | solution.py:35
  69.9 11.9 %collective-permute-start.16 = (bf16[32,2048]{1,0:T(8,128)(2,1)S(1)}, bf16[32,2048]{1,0:T(8,128)(2,1)S(1)}, u32[]{:S(2)}, u32[]{:S(2)}) collective-permute-start(bf16[32,2048]{1,0:T(8,128)(2,1)S(1)} %bitcast.115), channel_id=1, source_target_pairs={{0,8},{1,9},{2,10},{3,11},{4,12},{5,13},{6,14},{7,15},{8,0},{9,1},... | collective-permute-start | bytes 393224 | tf_op jit(solution)/shard_map/ppermute | solution.py:35
  69.9 11.9 %collective-permute-start.15 = (bf16[32,2048]{1,0:T(8,128)(2,1)S(1)}, bf16[32,2048]{1,0:T(8,128)(2,1)S(1)}, u32[]{:S(2)}, u32[]{:S(2)}) collective-permute-start(bf16[32,2048]{1,0:T(8,128)(2,1)S(1)} %bitcast.113), channel_id=1, source_target_pairs={{0,4},{1,5},{2,6},{3,7},{4,0},{5,1},{6,2},{7,3},{8,12},{9,13},{10,... | collective-permute-start | bytes 393224 | tf_op jit(solution)/shard_map/ppermute | solution.py:35
  82.0 5.2 %collective-permute-start.21 = (bf16[16,2048]{1,0:T(8,128)(2,1)S(1)}, bf16[16,2048]{1,0:T(8,128)(2,1)S(1)}, u32[]{:S(2)}, u32[]{:S(2)}) collective-permute-start(bf16[16,2048]{1,0:T(8,128)(2,1)S(1)} %slice.160), channel_id=1, source_target_pairs={{0,2},{1,3},{2,0},{3,1},{4,6},{5,7},{6,4},{7,5},{8,10},{9,11},{10,... | collective-permute-start | bytes 196616 | tf_op jit(solution)/shard_map/ppermute | solution.py:35
  82.7 8.4 %collective-permute-start.20 = (bf16[32,2048]{1,0:T(8,128)(2,1)S(1)}, bf16[32,2048]{1,0:T(8,128)(2,1)S(1)}, u32[]{:S(2)}, u32[]{:S(2)}) collective-permute-start(bf16[32,2048]{1,0:T(8,128)(2,1)S(1)} %bitcast.114), channel_id=1, source_target_pairs={{0,12},{1,13},{2,14},{3,15},{4,8},{5,9},{6,10},{7,11},{8,4},{9,5},... | collective-permute-start | bytes 393224 | tf_op jit(solution)/shard_map/ppermute | solution.py:35
  84.2 11.1 %collective-permute-start.19 = (bf16[32,2048]{1,0:T(8,128)(2,1)S(1)}, bf16[32,2048]{1,0:T(8,128)(2,1)S(1)}, u32[]{:S(2)}, u32[]{:S(2)}) collective-permute-start(bf16[32,2048]{1,0:T(8,128)(2,1)S(1)} %bitcast.112), channel_id=1, source_target_pairs={{0,8},{1,9},{2,10},{3,11},{4,12},{5,13},{6,14},{7,15},{8,0},{9,1},... | collective-permute-start | bytes 393224 | tf_op jit(solution)/shard_map/ppermute | solution.py:35
  84.2 11.1 %collective-permute-start.18 = (bf16[32,2048]{1,0:T(8,128)(2,1)S(1)}, bf16[32,2048]{1,0:T(8,128)(2,1)S(1)}, u32[]{:S(2)}, u32[]{:S(2)}) collective-permute-start(bf16[32,2048]{1,0:T(8,128)(2,1)S(1)} %bitcast.111), channel_id=1, source_target_pairs={{0,4},{1,5},{2,6},{3,7},{4,0},{5,1},{6,2},{7,3},{8,12},{9,13},{10,... | collective-permute-start | bytes 393224 | tf_op jit(solution)/shard_map/ppermute | solution.py:35

commit v26 on v25

--- a/solution.py
+++ b/solution.py
@@ -79,7 +79,7 @@
         wide_ref[pl.ds(t, slots, stride=length), :] = tile
         return carry
 
-    lax.fori_loop(0, length, cut, 0, unroll=8)
+    lax.fori_loop(0, length, cut, 0, unroll=24)
     for s in range(slots):
         slot_ref[placement_ref[s]] = s
     for core, out_ref in enumerate(out_refs):

time: 96.3 us -> 96.2 us (level)
  no operation moved by 1% of the time
where the time goes in v26:
time: 96.2 us; the launch traced here: 96 us
  waiting for transfers between devices  50.3 us (52%)
  starting transfers between devices  24.8 us (26%)
  Pallas kernels  16.8 us (17%)
  other arithmetic  3.03 us (3%)
    ppermute x22, waiting for transfers between devices, swap(): return lax.ppermute(x, 'expert', [(i, i ^ k * stride) for i in range(n)])  50.3 us
    ppermute x22, starting transfers between devices, swap(): return lax.ppermute(x, 'expert', [(i, i ^ k * stride) for i in range(n)])  24.8 us
    pallas_call x3, Pallas kernels, finish_step(): pl.pallas_call(functools.partial(finish_kernel, len(pieces), first, rows)...  6.49 us
    pallas_call x4, Pallas kernels, base_products(): pl.pallas_call(base_kernel, out_shape=[out, out], in_specs=[pl.BlockSpec(...  5.62 us
    pallas_call x1, Pallas kernels, lay_out(): pl.pallas_call(first_kernel, out_shape=[jax.ShapeDtypeStruct((steps * row...  3.5 us
  transfers between devices with their start and end apart: 22, of which 9 were waited for; matrix products, arithmetic and copies ran while one was open for 2% of the time, Pallas kernels for 10%

profile of v26, /device:TPU:0, one launch (start us, length us, event | category | flops | bytes accessed | tf_op | source)
XLA Modules:
  0.0 96.0 jit_solution(14623383764575850792)
XLA Ops:
  0.0 3.5 %lay_out.1 = (bf16[48,2176]{1,0:T(8,128)(2,1)}, bf16[2,4,264,128]{3,2,1,0:T(8,128)(2,1)}, bf16[2,4,264,128]{3,2,1,0:T(8,128)(2,1)}) custom-call(s32[1]{0:T(128)} %bitcast.place_ref, s32[16]{0:T(128)} %placement_ref.1, bf16[3,16,2048]{2,1,0:T(8,128)(2,1)} %hidden_ref.1, s32[3,8,16]{2,1,0:T(8,128)} %bitcast.117, f32[3,8,16]{2,1,0:T(8,128)} %bitcast.118, ...), custom_call_target="tpu_custom_call" | custom-call | flops 1 | bytes 1 | tf_op jit(solution)/shard_map/lay_out/pallas_call | solution.py:99
  4.0 4.7 %collective-permute-start.2 = (bf16[48,2176]{1,0:T(8,128)(2,1)}, bf16[48,2176]{1,0:T(8,128)(2,1)S(1)}, u32[]{:S(2)}, u32[]{:S(2)}) collective-permute-start(bf16[48,2176]{1,0:T(8,128)(2,1)} %get-tuple-element.48), channel_id=1, source_target_pairs={{0,12},{1,13},{2,14},{3,15},{4,8},{5,9},{6,10},{7,11},{8,4},{9,5},... | collective-permute-start | bytes 626696 | tf_op jit(solution)/shard_map/ppermute | solution.py:35
  8.6 0.7 collective-permute-start
  9.3 1.3 %fusion.3 = (bf16[2,4,264,128]{3,2,0,1:T(8,128)(2,1)S(1)}, bf16[2,4,264,128]{3,2,0,1:T(8,128)(2,1)S(1)}) fusion(bf16[1,2,4,264,128]{4,3,0,2,1:T(8,128)(2,1)} %bitcast.104, bf16[1,2,4,264,128]{4,3,0,2,1:T(8,128)(2,1)S(1)} %bitcast.105), kind=kLoop, calls=%fused_computation.14 | loop fusion | flops 540672 | bytes 2162688 | tf_op jit(solution)/shard_map/squeeze | solution.py:278
  10.6 1.7 %collective-permute-start.4 = (bf16[2,4,264,128]{3,2,0,1:T(8,128)(2,1)S(1)}, bf16[2,4,264,128]{3,2,0,1:T(8,128)(2,1)S(1)}, u32[]{:S(2)}, u32[]{:S(2)}) collective-permute-start(bf16[2,4,264,128]{3,2,0,1:T(8,128)(2,1)S(1)} %get-tuple-element.92), channel_id=1, source_target_pairs={{0,2},{1,3},{2,0},{3,1},{4,6},{5,7},{6,4},{7,5},{8,10},{9,11},{10,... | collective-permute-start | bytes 1622024 | tf_op jit(solution)/shard_map/ppermute | solution.py:35
  12.3 2.7 %collective-permute-done.2 = bf16[48,2176]{1,0:T(8,128)(2,1)S(1)} collective-permute-done((bf16[48,2176]{1,0:T(8,128)(2,1)}, bf16[48,2176]{1,0:T(8,128)(2,1)S(1)}, u32[]{:S(2)}, u32[]{:S(2)}) %collective-permute-start.2) | collective-permute-done | bytes 208928 | tf_op jit(solution)/shard_map/ppermute | solution.py:35
  15.0 12.2 %collective-permute-done.1 = bf16[48,2176]{1,0:T(8,128)(2,1)S(1)} collective-permute-done((bf16[48,2176]{1,0:T(8,128)(2,1)}, bf16[48,2176]{1,0:T(8,128)(2,1)S(1)}, u32[]{:S(2)}, u32[]{:S(2)}) %collective-permute-start.1) | collective-permute-done | bytes 208928 | tf_op jit(solution)/shard_map/ppermute | solution.py:35
  27.6 1.6 %collective-permute-start.8 = (bf16[192,2176]{1,0:T(8,128)(2,1)S(1)}, bf16[192,2176]{1,0:T(8,128)(2,1)S(1)}, u32[]{:S(2)}, u32[]{:S(2)}) collective-permute-start(bf16[192,2176]{1,0:T(8,128)(2,1)S(1)} %bitcast.86), channel_id=1, source_target_pairs={{0,2},{1,3},{2,0},{3,1},{4,6},{5,7},{6,4},{7,5},{8,10},{9,11},{10,... | collective-permute-start | bytes 2506760 | tf_op jit(solution)/shard_map/ppermute | solution.py:35
  29.2 2.5 %collective-permute-start.5 = (bf16[4,264,128]{2,1,0:T(8,128)(2,1)S(1)}, bf16[4,264,128]{2,1,0:T(8,128)(2,1)S(1)}, u32[]{:S(2)}, u32[]{:S(2)}) collective-permute-start(bf16[4,264,128]{2,1,0:T(8,128)(2,1)S(1)} %get-tuple-element.52), channel_id=1, source_target_pairs={{0,12},{1,13},{2,14},{3,15},{4,8},{5,9},{6,10},{7,11},{8,4},{9,5},... | collective-permute-start | bytes 811016 | tf_op jit(solution)/shard_map/ppermute | solution.py:35
  31.7 1.9 %collective-permute-start.7 = (bf16[4,264,128]{2,1,0:T(8,128)(2,1)S(1)}, bf16[4,264,128]{2,1,0:T(8,128)(2,1)S(1)}, u32[]{:S(2)}, u32[]{:S(2)}) collective-permute-start(bf16[4,264,128]{2,1,0:T(8,128)(2,1)S(1)} %get-tuple-element.54), channel_id=1, source_target_pairs={{0,4},{1,5},{2,6},{3,7},{4,0},{5,1},{6,2},{7,3},{8,12},{9,13},{10,... | collective-permute-start | bytes 811016 | tf_op jit(solution)/shard_map/ppermute | solution.py:35
  33.6 1.4 %base_products.4 = (f32[192,768]{1,0:T(8,128)S(1)}, f32[192,768]{1,0:T(8,128)S(1)}) custom-call(bf16[192,2176]{1,0:T(8,128)(2,1)S(1)} %bitcast.87, bf16[2048,768]{1,0:T(8,128)(2,1)S(1)} %bitcast.77, bf16[2048,768]{1,0:T(8,128)(2,1)S(1)} %bitcast.81), custom_call_target="tpu_custom_call" | custom-call | flops 1 | bytes 1 | tf_op jit(solution)/shard_map/base_products/pallas_call | solution.py:196
  35.0 1.4 %base_products.5 = (f32[192,768]{1,0:T(8,128)S(1)}, f32[192,768]{1,0:T(8,128)S(1)}) custom-call(bf16[192,2176]{1,0:T(8,128)(2,1)S(1)} %collective-permute-done.9.x_ref.refs_2_, bf16[2048,768]{1,0:T(8,128)(2,1)S(1)} %bitcast.78, bf16[2048,768]{1,0:T(8,128)(2,1)S(1)} %bitcast.82), custom_call_target="tpu_custom_call" | custom-call | flops 1 | bytes 1 | tf_op jit(solution)/shard_map/base_products/pallas_call | solution.py:196
  36.4 4.1 %collective-permute-done.5.refs_3_ = bf16[4,264,128]{2,1,0:T(8,128)(2,1)S(1)} collective-permute-done((bf16[4,264,128]{2,1,0:T(8,128)(2,1)S(1)}, bf16[4,264,128]{2,1,0:T(8,128)(2,1)S(1)}, u32[]{:S(2)}, u32[]{:S(2)}) %collective-permute-start.5) | collective-permute-done | bytes 270368 | tf_op jit(solution)/shard_map/ppermute | solution.py:35
  40.5 13.9 %collective-permute-done.6.refs_2_ = bf16[4,264,128]{2,1,0:T(8,128)(2,1)S(1)} collective-permute-done((bf16[4,264,128]{2,1,0:T(8,128)(2,1)S(1)}, bf16[4,264,128]{2,1,0:T(8,128)(2,1)S(1)}, u32[]{:S(2)}, u32[]{:S(2)}) %collective-permute-start.6) | collective-permute-done | bytes 270368 | tf_op jit(solution)/shard_map/ppermute | solution.py:35
  54.4 1.4 %base_products.6 = (f32[192,768]{1,0:T(8,128)S(1)}, f32[192,768]{1,0:T(8,128)S(1)}) custom-call(bf16[192,2176]{1,0:T(8,128)(2,1)S(1)} %collective-permute-done.8.x_ref.refs_1_, bf16[2048,768]{1,0:T(8,128)(2,1)S(1)} %bitcast.79, bf16[2048,768]{1,0:T(8,128)(2,1)S(1)} %bitcast.83), custom_call_target="tpu_custom_call" | custom-call | flops 1 | bytes 1 | tf_op jit(solution)/shard_map/base_products/pallas_call | solution.py:196
  55.8 1.2 %relayout_factors.1 = (bf16[2048,128]{1,0:T(8,128)(2,1)S(1)}, bf16[64,768]{1,0:T(8,128)(2,1)S(1)}, bf16[64,768]{1,0:T(8,128)(2,1)S(1)}, bf16[768,128]{1,0:T(8,128)(2,1)S(1)}, bf16[64,2048]{1,0:T(8,128)(2,1)S(1)}) custom-call(s32[1]{0:T(128)} %bitcast.place_ref, bf16[4,264,128]{2,1,0:T(8,128)(2,1)S(1)} %get-tuple-element.69.refs_0_, ...), custom_call_target="tpu_custom_call" | custom-call | flops 1 | bytes 1 | tf_op jit(solution)/shard_map/relayout_factors/pallas_call | solution.py:173
  57.0 1.4 %base_products.7 = (f32[192,768]{1,0:T(8,128)S(1)}, f32[192,768]{1,0:T(8,128)S(1)}) custom-call(bf16[192,2176]{1,0:T(8,128)(2,1)S(1)} %collective-permute-done.10.x_ref.refs_3_, bf16[2048,768]{1,0:T(8,128)(2,1)S(1)} %bitcast.80, bf16[2048,768]{1,0:T(8,128)(2,1)S(1)} %bitcast.84), custom_call_target="tpu_custom_call" | custom-call | flops 1 | bytes 1 | tf_op jit(solution)/shard_map/base_products/pallas_call | solution.py:196
  58.9 2.2 %finish_step.3 = (f32[128,2048]{1,0:T(8,128)S(1)}, bf16[128,2048]{1,0:T(8,128)(2,1)S(1)}) custom-call(s32[1]{0:T(128)} %bitcast.place_ref, bf16[192,2176]{1,0:T(8,128)(2,1)S(1)} %bitcast.88, bf16[192,2176]{1,0:T(8,128)(2,1)S(1)} %collective-permute-done.8.x_ref.refs_1_, bf16[192,2176]{1,0:T(8,128)(2,1)S(1)} %collective-permute-done.9.x_ref.refs_2_, ...), custom_call_target="tpu_custom_call" | custom-call | flops 8589934592 | bytes 1 | tf_op jit(solution)/shard_map/finish_step/pallas_call | solution.py:239
  61.1 0.6 collective-permute-start.11
  61.6 2.2 %finish_step.4 = (f32[128,2048]{1,0:T(8,128)S(1)}, bf16[128,2048]{1,0:T(8,128)(2,1)S(1)}) custom-call(s32[1]{0:T(128)} %bitcast.place_ref, bf16[192,2176]{1,0:T(8,128)(2,1)S(1)} %bitcast.89, bf16[192,2176]{1,0:T(8,128)(2,1)S(1)} %collective-permute-done.8.x_ref.refs_1_, bf16[192,2176]{1,0:T(8,128)(2,1)S(1)} %collective-permute-done.9.x_ref.refs_2_, ...), custom_call_target="tpu_custom_call" | custom-call | flops 8589934592 | bytes 1 | tf_op jit(solution)/shard_map/finish_step/pallas_call | solution.py:239
  63.9 2.2 %finish_step.5 = (f32[128,2048]{1,0:T(8,128)S(1)}, bf16[128,2048]{1,0:T(8,128)(2,1)S(1)}) custom-call(s32[1]{0:T(128)} %bitcast.place_ref, bf16[192,2176]{1,0:T(8,128)(2,1)S(1)} %bitcast.90, bf16[192,2176]{1,0:T(8,128)(2,1)S(1)} %collective-permute-done.8.x_ref.refs_1_, bf16[192,2176]{1,0:T(8,128)(2,1)S(1)} %collective-permute-done.9.x_ref.refs_2_, ...), custom_call_target="tpu_custom_call" | custom-call | flops 8589934592 | bytes 1 | tf_op jit(solution)/shard_map/finish_step/pallas_call | solution.py:239
  67.0 0.6 collective-permute-start.13
  67.6 0.6 collective-permute-done.14
  68.4 1.4 %collective-permute-start.17 = (bf16[32,2048]{1,0:T(8,128)(2,1)S(1)}, bf16[32,2048]{1,0:T(8,128)(2,1)S(1)}, u32[]{:S(2)}, u32[]{:S(2)}) collective-permute-start(bf16[32,2048]{1,0:T(8,128)(2,1)S(1)} %bitcast.116), channel_id=1, source_target_pairs={{0,12},{1,13},{2,14},{3,15},{4,8},{5,9},{6,10},{7,11},{8,4},{9,5},... | collective-permute-start | bytes 393224 | tf_op jit(solution)/shard_map/ppermute | solution.py:35
  69.8 3.0 %collective-permute-start.15 = (bf16[32,2048]{1,0:T(8,128)(2,1)S(1)}, bf16[32,2048]{1,0:T(8,128)(2,1)S(1)}, u32[]{:S(2)}, u32[]{:S(2)}) collective-permute-start(bf16[32,2048]{1,0:T(8,128)(2,1)S(1)} %bitcast.113), channel_id=1, source_target_pairs={{0,4},{1,5},{2,6},{3,7},{4,0},{5,1},{6,2},{7,3},{8,12},{9,13},{10,... | collective-permute-start | bytes 393224 | tf_op jit(solution)/shard_map/ppermute | solution.py:35
  73.0 3.8 %collective-permute-done.17 = bf16[32,2048]{1,0:T(8,128)(2,1)S(1)} collective-permute-done((bf16[32,2048]{1,0:T(8,128)(2,1)S(1)}, bf16[32,2048]{1,0:T(8,128)(2,1)S(1)}, u32[]{:S(2)}, u32[]{:S(2)}) %collective-permute-start.17) | collective-permute-done | bytes 131104 | tf_op jit(solution)/shard_map/ppermute | solution.py:35
  76.7 5.0 %collective-permute-done.16 = bf16[32,2048]{1,0:T(8,128)(2,1)S(1)} collective-permute-done((bf16[32,2048]{1,0:T(8,128)(2,1)S(1)}, bf16[32,2048]{1,0:T(8,128)(2,1)S(1)}, u32[]{:S(2)}, u32[]{:S(2)}) %collective-permute-start.16) | collective-permute-done | bytes 131104 | tf_op jit(solution)/shard_map/ppermute | solution.py:35
  82.7 1.5 %collective-permute-start.20 = (bf16[32,2048]{1,0:T(8,128)(2,1)S(1)}, bf16[32,2048]{1,0:T(8,128)(2,1)S(1)}, u32[]{:S(2)}, u32[]{:S(2)}) collective-permute-start(bf16[32,2048]{1,0:T(8,128)(2,1)S(1)} %bitcast.114), channel_id=1, source_target_pairs={{0,12},{1,13},{2,14},{3,15},{4,8},{5,9},{6,10},{7,11},{8,4},{9,5},... | collective-permute-start | bytes 393224 | tf_op jit(solution)/shard_map/ppermute | solution.py:35
  84.2 2.9 %collective-permute-start.18 = (bf16[32,2048]{1,0:T(8,128)(2,1)S(1)}, bf16[32,2048]{1,0:T(8,128)(2,1)S(1)}, u32[]{:S(2)}, u32[]{:S(2)}) collective-permute-start(bf16[32,2048]{1,0:T(8,128)(2,1)S(1)} %bitcast.111), channel_id=1, source_target_pairs={{0,4},{1,5},{2,6},{3,7},{4,0},{5,1},{6,2},{7,3},{8,12},{9,13},{10,... | collective-permute-start | bytes 393224 | tf_op jit(solution)/shard_map/ppermute | solution.py:35
  87.1 3.9 %collective-permute-done.20 = bf16[32,2048]{1,0:T(8,128)(2,1)S(1)} collective-permute-done((bf16[32,2048]{1,0:T(8,128)(2,1)S(1)}, bf16[32,2048]{1,0:T(8,128)(2,1)S(1)}, u32[]{:S(2)}, u32[]{:S(2)}) %collective-permute-start.20) | collective-permute-done | bytes 131104 | tf_op jit(solution)/shard_map/ppermute | solution.py:35
  91.0 4.3 %collective-permute-done.19 = bf16[32,2048]{1,0:T(8,128)(2,1)S(1)} collective-permute-done((bf16[32,2048]{1,0:T(8,128)(2,1)S(1)}, bf16[32,2048]{1,0:T(8,128)(2,1)S(1)}, u32[]{:S(2)}, u32[]{:S(2)}) %collective-permute-start.19) | collective-permute-done | bytes 131104 | tf_op jit(solution)/shard_map/ppermute | solution.py:35
  95.4 0.7 pad_maximum_fusion.7
  (53 shorter events, 3.6 us)
Async XLA Ops:
  3.5 23.7 %copy-start.3 = (bf16[48,2176]{1,0:T(8,128)(2,1)S(1)}, bf16[48,2176]{1,0:T(8,128)(2,1)}, u32[]{:S(2)}) copy-start(bf16[48,2176]{1,0:T(8,128)(2,1)} %get-tuple-element.48) | copy-start | bytes 626692
  3.5 5.8 %collective-permute-start.3 = (bf16[2,4,264,128]{3,2,1,0:T(8,128)(2,1)}, bf16[2,4,264,128]{3,2,1,0:T(8,128)(2,1)S(1)}, u32[]{:S(2)}, u32[]{:S(2)}) collective-permute-start(bf16[2,4,264,128]{3,2,1,0:T(8,128)(2,1)} %get-tuple-element.50), channel_id=1, source_target_pairs={{0,1},{1,0},{2,3},{3,2},{4,5},{5,4},{6,7},{7,6},{8,9},{9,8},{10,11... | collective-permute-start | bytes 1622024 | tf_op jit(solution)/shard_map/ppermute | solution.py:35
  4.0 11.0 %collective-permute-start.2 = (bf16[48,2176]{1,0:T(8,128)(2,1)}, bf16[48,2176]{1,0:T(8,128)(2,1)S(1)}, u32[]{:S(2)}, u32[]{:S(2)}) collective-permute-start(bf16[48,2176]{1,0:T(8,128)(2,1)} %get-tuple-element.48), channel_id=1, source_target_pairs={{0,12},{1,13},{2,14},{3,15},{4,8},{5,9},{6,10},{7,11},{8,4},{9,5},... | collective-permute-start | bytes 626696 | tf_op jit(solution)/shard_map/ppermute | solution.py:35
  8.6 18.6 %collective-permute-start.1 = (bf16[48,2176]{1,0:T(8,128)(2,1)}, bf16[48,2176]{1,0:T(8,128)(2,1)S(1)}, u32[]{:S(2)}, u32[]{:S(2)}) collective-permute-start(bf16[48,2176]{1,0:T(8,128)(2,1)} %get-tuple-element.48), channel_id=1, source_target_pairs={{0,8},{1,9},{2,10},{3,11},{4,12},{5,13},{6,14},{7,15},{8,0},{9,1},... | collective-permute-start | bytes 626696 | tf_op jit(solution)/shard_map/ppermute | solution.py:35
  8.6 18.6 %collective-permute-start = (bf16[48,2176]{1,0:T(8,128)(2,1)}, bf16[48,2176]{1,0:T(8,128)(2,1)S(1)}, u32[]{:S(2)}, u32[]{:S(2)}) collective-permute-start(bf16[48,2176]{1,0:T(8,128)(2,1)} %get-tuple-element.48), channel_id=1, source_target_pairs={{0,4},{1,5},{2,6},{3,7},{4,0},{5,1},{6,2},{7,3},{8,12},{9,13},{10,... | collective-permute-start | bytes 626696 | tf_op jit(solution)/shard_map/ppermute | solution.py:35
  9.3 24.3 %copy-start.1 = (bf16[1,2048,768]{2,1,0:T(8,128)(2,1)S(1)}, bf16[1,2048,768]{2,1,0:T(8,128)(2,1)}, u32[]{:S(2)}) copy-start(bf16[1,2048,768]{2,1,0:T(8,128)(2,1)} %param.14) | copy-start | bytes 9437188
  10.6 16.8 %collective-permute-start.4 = (bf16[2,4,264,128]{3,2,0,1:T(8,128)(2,1)S(1)}, bf16[2,4,264,128]{3,2,0,1:T(8,128)(2,1)S(1)}, u32[]{:S(2)}, u32[]{:S(2)}) collective-permute-start(bf16[2,4,264,128]{3,2,0,1:T(8,128)(2,1)S(1)} %get-tuple-element.92), channel_id=1, source_target_pairs={{0,2},{1,3},{2,0},{3,1},{4,6},{5,7},{6,4},{7,5},{8,10},{9,11},{10,... | collective-permute-start | bytes 1622024 | tf_op jit(solution)/shard_map/ppermute | solution.py:35
  27.3 6.3 %copy-start = (bf16[1,2048,768]{2,1,0:T(8,128)(2,1)S(1)}, bf16[1,2048,768]{2,1,0:T(8,128)(2,1)}, u32[]{:S(2)}) copy-start(bf16[1,2048,768]{2,1,0:T(8,128)(2,1)} %param.13) | copy-start | bytes 9437188
  27.6 7.5 %collective-permute-start.9 = (bf16[192,2176]{1,0:T(8,128)(2,1)S(1)}, bf16[192,2176]{1,0:T(8,128)(2,1)S(1)}, u32[]{:S(2)}, u32[]{:S(2)}) collective-permute-start(bf16[192,2176]{1,0:T(8,128)(2,1)S(1)} %bitcast.85), channel_id=1, source_target_pairs={{0,1},{1,0},{2,3},{3,2},{4,5},{5,4},{6,7},{7,6},{8,9},{9,8},{10,11... | collective-permute-start | bytes 2506760 | tf_op jit(solution)/shard_map/ppermute | solution.py:35
  27.6 26.7 %collective-permute-start.8 = (bf16[192,2176]{1,0:T(8,128)(2,1)S(1)}, bf16[192,2176]{1,0:T(8,128)(2,1)S(1)}, u32[]{:S(2)}, u32[]{:S(2)}) collective-permute-start(bf16[192,2176]{1,0:T(8,128)(2,1)S(1)} %bitcast.86), channel_id=1, source_target_pairs={{0,2},{1,3},{2,0},{3,1},{4,6},{5,7},{6,4},{7,5},{8,10},{9,11},{10,... | collective-permute-start | bytes 2506760 | tf_op jit(solution)/shard_map/ppermute | solution.py:35
  29.2 11.3 %collective-permute-start.5 = (bf16[4,264,128]{2,1,0:T(8,128)(2,1)S(1)}, bf16[4,264,128]{2,1,0:T(8,128)(2,1)S(1)}, u32[]{:S(2)}, u32[]{:S(2)}) collective-permute-start(bf16[4,264,128]{2,1,0:T(8,128)(2,1)S(1)} %get-tuple-element.52), channel_id=1, source_target_pairs={{0,12},{1,13},{2,14},{3,15},{4,8},{5,9},{6,10},{7,11},{8,4},{9,5},... | collective-permute-start | bytes 811016 | tf_op jit(solution)/shard_map/ppermute | solution.py:35
  31.7 22.7 %collective-permute-start.6 = (bf16[4,264,128]{2,1,0:T(8,128)(2,1)S(1)}, bf16[4,264,128]{2,1,0:T(8,128)(2,1)S(1)}, u32[]{:S(2)}, u32[]{:S(2)}) collective-permute-start(bf16[4,264,128]{2,1,0:T(8,128)(2,1)S(1)} %get-tuple-element.53), channel_id=1, source_target_pairs={{0,8},{1,9},{2,10},{3,11},{4,12},{5,13},{6,14},{7,15},{8,0},{9,1},... | collective-permute-start | bytes 811016 | tf_op jit(solution)/shard_map/ppermute | solution.py:35
  31.7 22.7 %collective-permute-start.7 = (bf16[4,264,128]{2,1,0:T(8,128)(2,1)S(1)}, bf16[4,264,128]{2,1,0:T(8,128)(2,1)S(1)}, u32[]{:S(2)}, u32[]{:S(2)}) collective-permute-start(bf16[4,264,128]{2,1,0:T(8,128)(2,1)S(1)} %get-tuple-element.54), channel_id=1, source_target_pairs={{0,4},{1,5},{2,6},{3,7},{4,0},{5,1},{6,2},{7,3},{8,12},{9,13},{10,... | collective-permute-start | bytes 811016 | tf_op jit(solution)/shard_map/ppermute | solution.py:35
  54.4 2.7 %collective-permute-start.10 = (bf16[192,2176]{1,0:T(8,128)(2,1)S(1)}, bf16[192,2176]{1,0:T(8,128)(2,1)S(1)}, u32[]{:S(2)}, u32[]{:S(2)}) collective-permute-start(bf16[192,2176]{1,0:T(8,128)(2,1)S(1)} %collective-permute-done.8.x_ref.refs_1_), channel_id=1, source_target_pairs={{0,1},{1,0},{2,3},{3,2},{4,5},{5,4},{6,7},{7,6},{8,9},{9,8},{10,11... | collective-permute-start | bytes 2506760 | tf_op jit(solution)/shard_map/ppermute | solution.py:35
  57.0 1.9 %copy-start.2 = (bf16[1,768,2048]{2,1,0:T(8,128)(2,1)S(1)}, bf16[1,768,2048]{2,1,0:T(8,128)(2,1)}, u32[]{:S(2)}) copy-start(bf16[1,768,2048]{2,1,0:T(8,128)(2,1)} %param.15) | copy-start | bytes 9437188
  61.1 5.6 %collective-permute-start.11 = (bf16[128,2048]{1,0:T(8,128)(2,1)S(1)}, bf16[128,2048]{1,0:T(8,128)(2,1)S(1)}, u32[]{:S(2)}, u32[]{:S(2)}) collective-permute-start(bf16[128,2048]{1,0:T(8,128)(2,1)S(1)} %get-tuple-element.79), channel_id=1, source_target_pairs={{0,1},{1,0},{2,3},{3,2},{4,5},{5,4},{6,7},{7,6},{8,9},{9,8},{10,11... | collective-permute-start | bytes 1572872 | tf_op jit(solution)/shard_map/ppermute | solution.py:35
  63.8 3.0 %collective-permute-start.12 = (bf16[128,2048]{1,0:T(8,128)(2,1)S(1)}, bf16[128,2048]{1,0:T(8,128)(2,1)S(1)}, u32[]{:S(2)}, u32[]{:S(2)}) collective-permute-start(bf16[128,2048]{1,0:T(8,128)(2,1)S(1)} %get-tuple-element.82), channel_id=1, source_target_pairs={{0,1},{1,0},{2,3},{3,2},{4,5},{5,4},{6,7},{7,6},{8,9},{9,8},{10,11... | collective-permute-start | bytes 1572872 | tf_op jit(solution)/shard_map/ppermute | solution.py:35
  66.1 2.1 %collective-permute-start.14 = (bf16[128,2048]{1,0:T(8,128)(2,1)S(1)}, bf16[128,2048]{1,0:T(8,128)(2,1)S(1)}, u32[]{:S(2)}, u32[]{:S(2)}) collective-permute-start(bf16[128,2048]{1,0:T(8,128)(2,1)S(1)} %get-tuple-element.88), channel_id=1, source_target_pairs={{0,1},{1,0},{2,3},{3,2},{4,5},{5,4},{6,7},{7,6},{8,9},{9,8},{10,11... | collective-permute-start | bytes 1572872 | tf_op jit(solution)/shard_map/ppermute | solution.py:35
  67.0 14.8 %collective-permute-start.13 = (bf16[128,2048]{1,0:T(8,128)(2,1)S(1)}, bf16[128,2048]{1,0:T(8,128)(2,1)S(1)}, u32[]{:S(2)}, u32[]{:S(2)}) collective-permute-start(bf16[128,2048]{1,0:T(8,128)(2,1)S(1)} %bitcast.106), channel_id=1, source_target_pairs={{0,2},{1,3},{2,0},{3,1},{4,6},{5,7},{6,4},{7,5},{8,10},{9,11},{10,... | collective-permute-start | bytes 1572872 | tf_op jit(solution)/shard_map/ppermute | solution.py:35
  68.4 8.3 %collective-permute-start.17 = (bf16[32,2048]{1,0:T(8,128)(2,1)S(1)}, bf16[32,2048]{1,0:T(8,128)(2,1)S(1)}, u32[]{:S(2)}, u32[]{:S(2)}) collective-permute-start(bf16[32,2048]{1,0:T(8,128)(2,1)S(1)} %bitcast.116), channel_id=1, source_target_pairs={{0,12},{1,13},{2,14},{3,15},{4,8},{5,9},{6,10},{7,11},{8,4},{9,5},... | collective-permute-start | bytes 393224 | tf_op jit(solution)/shard_map/ppermute | solution.py:35
  69.8 11.9 %collective-permute-start.16 = (bf16[32,2048]{1,0:T(8,128)(2,1)S(1)}, bf16[32,2048]{1,0:T(8,128)(2,1)S(1)}, u32[]{:S(2)}, u32[]{:S(2)}) collective-permute-start(bf16[32,2048]{1,0:T(8,128)(2,1)S(1)} %bitcast.115), channel_id=1, source_target_pairs={{0,8},{1,9},{2,10},{3,11},{4,12},{5,13},{6,14},{7,15},{8,0},{9,1},... | collective-permute-start | bytes 393224 | tf_op jit(solution)/shard_map/ppermute | solution.py:35
  69.8 11.9 %collective-permute-start.15 = (bf16[32,2048]{1,0:T(8,128)(2,1)S(1)}, bf16[32,2048]{1,0:T(8,128)(2,1)S(1)}, u32[]{:S(2)}, u32[]{:S(2)}) collective-permute-start(bf16[32,2048]{1,0:T(8,128)(2,1)S(1)} %bitcast.113), channel_id=1, source_target_pairs={{0,4},{1,5},{2,6},{3,7},{4,0},{5,1},{6,2},{7,3},{8,12},{9,13},{10,... | collective-permute-start | bytes 393224 | tf_op jit(solution)/shard_map/ppermute | solution.py:35
  81.9 5.2 %collective-permute-start.21 = (bf16[16,2048]{1,0:T(8,128)(2,1)S(1)}, bf16[16,2048]{1,0:T(8,128)(2,1)S(1)}, u32[]{:S(2)}, u32[]{:S(2)}) collective-permute-start(bf16[16,2048]{1,0:T(8,128)(2,1)S(1)} %slice.160), channel_id=1, source_target_pairs={{0,2},{1,3},{2,0},{3,1},{4,6},{5,7},{6,4},{7,5},{8,10},{9,11},{10,... | collective-permute-start | bytes 196616 | tf_op jit(solution)/shard_map/ppermute | solution.py:35
  82.7 8.4 %collective-permute-start.20 = (bf16[32,2048]{1,0:T(8,128)(2,1)S(1)}, bf16[32,2048]{1,0:T(8,128)(2,1)S(1)}, u32[]{:S(2)}, u32[]{:S(2)}) collective-permute-start(bf16[32,2048]{1,0:T(8,128)(2,1)S(1)} %bitcast.114), channel_id=1, source_target_pairs={{0,12},{1,13},{2,14},{3,15},{4,8},{5,9},{6,10},{7,11},{8,4},{9,5},... | collective-permute-start | bytes 393224 | tf_op jit(solution)/shard_map/ppermute | solution.py:35
  84.2 11.1 %collective-permute-start.19 = (bf16[32,2048]{1,0:T(8,128)(2,1)S(1)}, bf16[32,2048]{1,0:T(8,128)(2,1)S(1)}, u32[]{:S(2)}, u32[]{:S(2)}) collective-permute-start(bf16[32,2048]{1,0:T(8,128)(2,1)S(1)} %bitcast.112), channel_id=1, source_target_pairs={{0,8},{1,9},{2,10},{3,11},{4,12},{5,13},{6,14},{7,15},{8,0},{9,1},... | collective-permute-start | bytes 393224 | tf_op jit(solution)/shard_map/ppermute | solution.py:35
  84.2 11.1 %collective-permute-start.18 = (bf16[32,2048]{1,0:T(8,128)(2,1)S(1)}, bf16[32,2048]{1,0:T(8,128)(2,1)S(1)}, u32[]{:S(2)}, u32[]{:S(2)}) collective-permute-start(bf16[32,2048]{1,0:T(8,128)(2,1)S(1)} %bitcast.111), channel_id=1, source_target_pairs={{0,4},{1,5},{2,6},{3,7},{4,0},{5,1},{6,2},{7,3},{8,12},{9,13},{10,... | collective-permute-start | bytes 393224 | tf_op jit(solution)/shard_map/ppermute | solution.py:35
